TPU v7x, 32 devices: a whole 2x2x4 slice. The times are simulated.
32 devices in a mesh: sec: 8 (over y, x, core), term: 4 (over z).
Axes of the slice: x: 2, y: 2, z: 4, core: 2. Of those that a mesh axis runs over, the one named last changes fastest.
Arguments:
- vectors: bfloat16 [2, 8, 4, 256, 256], P(None, 'sec'), may hold values from -6 to 6
- left_ops: bfloat16 [12, 8, 256, 256], P('term', 'sec'), may hold values from -0.375 to 0.375
- right_ops: bfloat16 [12, 8, 256, 256], P('term', 'sec'), may hold values from -0.109375 to 0.109375
- offsets: int32 [12, 4], P('term'), may hold values from 0 to 7, as said below
Outputs:
- products: bfloat16 [2, 8, 4, 256, 256], P(None, 'sec', None, 'term')
- rayleigh: float32 [2, 2], replicated
Inputs may be any that keep to these rules, and one draw needn't show every extreme that they name: Each term's 4 offsets are distinct, and every shift from 0 to 7 occurs for some term and pair.
All inputs are finite; a program needn't handle non-finite values.
Results may differ from a plain program's by a relative error of at most 0.015.
Values may be sent and summed in bfloat16 or wider, within the bound.
No kernel may reach another device: no remote copies, remote signals or barrier semaphores. Data moves between devices by JAX's collectives and lax.ppermute only.
A program may use at most 64 MiB of HBM per device.

v0:
```python
import jax
import jax.numpy as jnp
from jax import lax
from jax.sharding import PartitionSpec as P


def pick_blocks(carried, piece, needed):
    piece_width = piece.shape[1]
    chosen_list = []
    for pair_index in range(needed.shape[1]):
        offset_in = needed[:, pair_index]
        inside = (offset_in >= 0) & (offset_in < piece_width)
        clipped = jnp.clip(offset_in, 0, piece_width - 1)
        candidate = jnp.take_along_axis(piece, clipped[:, None, None, None], axis=1)[:, 0]
        chosen_list.append(jnp.where(inside[:, None, None], candidate, carried[pair_index]))
    return jnp.stack(chosen_list)


def local(vectors, left_ops, right_ops, offsets):
    sectors = lax.axis_size("sec")
    my_sector = lax.axis_index("sec")
    needed = (my_sector + offsets) % sectors
    local_vectors = vectors[:, 0]
    inner_part = jnp.einsum(
        "tab,ipbc->tipac", left_ops[:, 0], local_vectors, preferred_element_type=jnp.float32
    ).astype(jnp.bfloat16)
    pair_count = offsets.shape[1]
    own_right = right_ops[:, 0]
    empty_blocks = jnp.zeros((pair_count,) + own_right.shape, jnp.bfloat16)
    picked = pick_blocks(empty_blocks, lax.all_gather(right_ops, "sec", axis=1, tiled=True), needed)
    partial_value = jnp.einsum(
        "tipac,ptcd->ipad", inner_part, picked, preferred_element_type=jnp.float32
    )
    rows_share = local_vectors.shape[2] // lax.axis_size("term")
    row_start = lax.axis_index("term") * rows_share
    vector_share = lax.dynamic_slice_in_dim(local_vectors, row_start, rows_share, 2).astype(
        jnp.float32
    )
    square_part = jnp.sum(vector_share * vector_share, axis=(1, 2, 3))
    shares = lax.psum_scatter(partial_value, "term", scatter_dimension=2, tiled=True)
    gram_part = jnp.einsum("ipab,jpab->ij", vector_share, shares)
    gram_matrix, squares = lax.psum((gram_part, square_part), ("sec", "term"))
    rayleigh = gram_matrix / jnp.sqrt(squares[:, None] * squares[None, :])
    return (shares.astype(jnp.bfloat16)[:, None], rayleigh)


def solution(mesh):
    in_specs = (
        P(None, "sec", None, None, None),
        P("term", "sec", None, None),
        P("term", "sec", None, None),
        P("term", None),
    )
    out_specs = (P(None, "sec", None, "term", None), P())
    return jax.shard_map(local, mesh=mesh, in_specs=in_specs, out_specs=out_specs, check_vma=False)
```

profile of v0, /device:TPU:0, one launch (start us, length us, event | category | flops | bytes accessed | tf_op | source)
XLA Modules:
  0.0 190.8 jit_solution(15732932617927107019)
XLA Ops:
  7.2 0.7 all-gather.2.cloned.1.call-update
  7.9 1.2 dynamic-slice.1
  9.8 0.7 add_select_fusion
  10.5 0.2 clamp_reduce_fusion.3
  10.8 0.2 and_reduce_fusion.3
  11.0 0.7 multiply_reduce_fusion
  11.8 33.2 %all-gather.2.cloned.1.call-done = bf16[3,8,256,256]{3,2,1,0:T(8,128)(2,1)} async-done(((bf16[3,1,256,256]{3,2,1,0:T(8,128)(2,1)}), bf16[3,8,256,256]{3,2,1,0:T(8,128)(2,1)}) %all-gather.2.cloned.1.call-update) | async-done | bytes 3145744 | tf_op jit(solution)/shard_map/all_gather | solution.py:30
  45.0 2.5 %gather_fusion.3 = bf16[3,256,256]{2,1,0:T(8,128)(2,1)S(1)} fusion(bf16[3,8,256,256]{3,2,1,0:T(8,128)(2,1)} %all-gather.2.cloned.1.call-done, s32[3]{0:T(128)S(1)} %or_bitcast_fusion), kind=kCustom, calls=%fused_computation.3.clone | custom fusion | bytes 786456 | tf_op jit(solution)/shard_map/jit(take_along_axis)/gather | solution.py:14
  47.4 0.2 copy.19
  47.6 2.5 %gather_fusion.2 = bf16[3,256,256]{2,1,0:T(8,128)(2,1)S(1)} fusion(bf16[3,8,256,256]{3,2,1,0:T(8,128)(2,1)} %all-gather.2.cloned.1.call-done, s32[3]{0:T(128)S(1)} %or_bitcast_fusion.1), kind=kCustom, calls=%fused_computation.2.clone | custom fusion | bytes 786456 | tf_op jit(solution)/shard_map/jit(take_along_axis)/gather | solution.py:14
  50.1 0.2 copy.18
  50.3 2.5 %gather_fusion.1 = bf16[3,256,256]{2,1,0:T(8,128)(2,1)S(1)} fusion(bf16[3,8,256,256]{3,2,1,0:T(8,128)(2,1)} %all-gather.2.cloned.1.call-done, s32[3]{0:T(128)S(1)} %or_bitcast_fusion.2), kind=kCustom, calls=%fused_computation.1.clone | custom fusion | bytes 786456 | tf_op jit(solution)/shard_map/jit(take_along_axis)/gather | solution.py:14
  52.7 0.2 copy.17
  52.9 2.5 %gather_fusion = bf16[3,256,256]{2,1,0:T(8,128)(2,1)S(1)} fusion(bf16[3,8,256,256]{3,2,1,0:T(8,128)(2,1)} %all-gather.2.cloned.1.call-done, s32[3]{0:T(128)S(1)} %or_bitcast_fusion.3), kind=kCustom, calls=%fused_computation.clone | custom fusion | bytes 786456 | tf_op jit(solution)/shard_map/jit(take_along_axis)/gather | solution.py:14
  55.4 0.2 copy.16
  56.0 4.2 %fusion.5 = f32[2,4,256,256]{2,3,0,1:T(8,128)} fusion(bf16[1,3,256,256]{2,3,1,0:T(8,128)(2,1)S(1)} %bitcast_select_fusion, bf16[1,3,256,256]{2,3,1,0:T(8,128)(2,1)S(1)} %bitcast_select_fusion.2, bf16[1,3,256,256]{2,3,1,0:T(8,128)(2,1)S(1)} %bitcast_select_fusion.4, bf16[1,3,256,256]{2,3,1,0:T(8,128)(2,1)S(1)} %bitcast_select_fusion.6, ...), kind=kOutput, calls=%fused_computation.8 | convolution fusion | flops 1618477056 | bytes 5111808 | tf_op jit(solution)/shard_map/tipac,ptcd->ipad/dot_general | solution.py:31
  60.3 2.2 %copy.22 = f32[2,4,256,256]{3,1,0,2:T(4,128)S(1)} copy(f32[2,4,256,256]{2,3,0,1:T(8,128)} %fusion.5) | data formatting | bytes 4194304 | tf_op jit(solution)/shard_map/tipac,ptcd->ipad/transpose | solution.py:31
  62.5 78.8 %all-reduce.3 = bf16[2,4,256,256]{3,1,0,2:T(4,128)(2,1)} all-reduce(f32[2,4,256,256]{3,1,0,2:T(4,128)S(1)} %copy.22), channel_id=2, replica_groups=mesh['sec'=8,'term'=4] {'term'}, use_global_device_ids=true, to_apply=%region_0.2.clone | all-reduce | flops 524288 | bytes 3145728
  141.3 1.0 fusion.29
  142.4 1.0 constant_dynamic-slice_fusion
  143.4 1.0 convolution_bitcast_fusion
  144.4 0.8 copy.25
  145.2 38.1 %all-reduce.1 = (f32[2,2]{1,0:T(2,128)S(1)}, f32[2]{0:T(128)S(1)}) all-reduce(f32[2,2]{1,0:T(2,128)S(1)} %convolution_bitcast_fusion, f32[2]{0:T(128)S(1)} %multiply_reduce_fusion), channel_id=1, replica_groups=mesh['sec'=8,'term'=4] {'sec','term'}, use_global_device_ids=true, to_apply=%region_1.3 | all-reduce | flops 6 | bytes 48 | tf_op jit(solution)/shard_map/psum | solution.py:42
  183.3 0.6 rsqrt_multiply_fusion
  (18 shorter events, 0.6 us)
Async XLA Ops:
  7.2 3.8 %copy-start = (bf16[2,1,4,256,256]{4,3,2,1,0:T(8,128)(2,1)S(1)}, bf16[2,1,4,256,256]{4,3,2,1,0:T(8,128)(2,1)}, u32[]{:S(2)}) copy-start(bf16[2,1,4,256,256]{4,3,2,1,0:T(8,128)(2,1)} %param.6) | copy-start | bytes 3145732
  7.2 37.8 %all-gather.2.cloned.1.call-start = ((), (), s32[]{:S(2)}) async-start(), calls=%async_computation | async-start | bytes 3538944 | tf_op jit(solution)/shard_map/all_gather | solution.py:30
Sparse Core Ops, SparseCore 0:
  9.9 35.0 all-gather.1
where the time goes:
time: 191 us
  blocking collectives  117 us (61%)
  waiting for transfers between devices  33.9 us (18%)
  local copies, waits for them, and re-layouts  16.9 us (9%)
  between operations  14.9 us (8%)
  matrix products  5.21 us (3%)
  other arithmetic  2.95 us (2%)
    unnamed x1, blocking collectives  78.8 us
    psum x1, blocking collectives, local(): gram_matrix, squares = lax.psum((gram_part, square_part), ('sec', 'term'))  38.1 us
    all_gather x1, waiting for transfers between devices, local(): lax.all_gather(right_ops, 'sec', axis=1, tiled=True)  33.2 us
    gather x8, local copies, waits for them, and re-layouts, pick_blocks(): jnp.take_along_axis(piece, clipped[:, None, None, None], axis=1)[:, 0]  10.5 us
    dot_general x1, matrix products, local(): jnp.einsum('tipac,ptcd->ipad', inner_part, picked, preferred_element_type...  4.23 us
  transfers between devices with their start and end apart: 1, of which 1 were waited for; matrix products, arithmetic and copies ran while one was open for 2% of the time, Pallas kernels for 0%

commit v1 on v0

v1 whole, which is shorter than its diff:
```python
import functools

import jax
import jax.numpy as jnp
from jax import lax
from jax.experimental import pallas as pl
from jax.experimental.pallas import tpu as pltpu
from jax.sharding import PartitionSpec as P

MIB = 1 << 20
TILE = (8, 128)


def swap(value, axis, mask):
    count = lax.axis_size(axis)
    return lax.ppermute(value, axis, [(place, place ^ mask) for place in range(count)])


def gather_by_mask(own, axis, high_last):
    held = [own]
    for mask in range(1, lax.axis_size(axis)):
        if mask & 1:
            step = 1
        elif high_last:
            step = 1 << (mask.bit_length() - 1)
        else:
            step = mask & -mask
        held.append(swap(held[mask ^ step], axis, step))
    return held


def place_rows(values):
    row = lax.broadcasted_iota(jnp.int32, TILE, 0)
    tile = jnp.zeros(TILE, jnp.float32)
    for position, value in values:
        tile = jnp.where(row == position, value, tile)
    return tile


def total(value):
    return jnp.sum(jnp.sum(value, axis=0, keepdims=True), axis=1, keepdims=True)


def inner_kernel(square_scale, vectors, left, inner, squares):
    terms, states = left.shape[0], left.shape[1]
    stacked = left[...].reshape(terms * states, states)
    sums = []
    for trial in range(vectors.shape[0]):
        square = jnp.zeros((8, states), jnp.float32)
        for pair in range(vectors.shape[1]):
            block = vectors[trial, pair]
            product = jnp.dot(stacked, block, preferred_element_type=jnp.float32)
            inner[:, trial, pair] = product.astype(jnp.bfloat16).reshape(terms, states, states)
            wide = block.astype(jnp.float32)
            square += jnp.sum((wide * wide).reshape(-1, 8, states), axis=0)
        sums.append(total(square) * square_scale)
    trials = len(sums)
    squares[...] = place_rows([(trials * trials + k, value) for k, value in enumerate(sums)])


def sum_kernel(sectors, shares, offsets, vectors, inner, squares, *rest):
    pieces = rest[: 2 * sectors]
    own, *others, tile, rights, partial, sems = rest[2 * sectors :]
    terms, trials, pairs, states, _ = inner.shape
    half = states // 2
    copies = []
    for mask in range(sectors):
        for part in range(2):
            copies.append(
                pltpu.make_async_copy(
                    pieces[2 * mask + part],
                    rights.at[mask, :, pl.ds(part * half, half)],
                    sems.at[2 * mask + part],
                )
            )
    for copy in copies:
        copy.start()
    for copy in copies:
        copy.wait()
    sector = lax.axis_index("sec")
    place = lax.axis_index("term")
    rows = states // shares
    grams = [jnp.zeros((8, states), jnp.float32) for _ in range(trials * trials)]
    for pair in range(pairs):
        result = None
        for term in range(terms):
            wanted = (sector + offsets[term, pair]) & (sectors - 1)
            added = jnp.dot(
                inner[term, :, pair].reshape(trials * states, states),
                rights[sector ^ wanted, term],
                preferred_element_type=jnp.float32,
            )
            result = added if result is None else result + added
        partial[...] = result.reshape(trials, states, states)
        for j in range(trials):
            product = partial[j]
            for i in range(trials):
                spread = vectors[i, pair].astype(jnp.float32) * product
                grams[i * trials + j] += jnp.sum(spread.reshape(-1, 8, states), axis=0)
        for mask in range(shares):
            start = pl.multiple_of((place ^ mask) * rows, rows)
            share = partial[:, pl.ds(start, rows)]
            if mask == 0:
                own[:, pair] = share
            else:
                others[mask - 1][:, pair] = share.astype(jnp.bfloat16)
    tile[...] = squares[...] + place_rows([(k, total(value)) for k, value in enumerate(grams)])


def in_vmem(count):
    return [pl.BlockSpec(memory_space=pltpu.VMEM)] * count


def local(vectors, left_ops, right_ops, offsets):
    sectors = lax.axis_size("sec")
    shares = lax.axis_size("term")
    trials, _, pairs, states, _ = vectors.shape
    terms = left_ops.shape[0]
    vectors, left, right = vectors[:, 0], left_ops[:, 0], right_ops[:, 0]
    half, rows = states // 2, states // shares

    first = gather_by_mask(right[:, :half], "sec", True)
    second = gather_by_mask(right[:, half:], "sec", False)
    pieces = [piece for both in zip(first, second) for piece in both]

    flops = 2 * terms * trials * pairs * states**3
    inner, squares = pl.pallas_call(
        functools.partial(inner_kernel, 1.0 / shares),
        out_shape=(
            jax.ShapeDtypeStruct((terms, trials, pairs, states, states), jnp.bfloat16),
            jax.ShapeDtypeStruct(TILE, jnp.float32),
        ),
        in_specs=in_vmem(2),
        out_specs=tuple(in_vmem(2)),
        compiler_params=pltpu.CompilerParams(vmem_limit_bytes=12 * MIB),
        cost_estimate=pl.CostEstimate(flops=flops, bytes_accessed=5 * MIB, transcendentals=0),
        name="inner_products",
    )(vectors, left)

    share_shape = (trials, pairs, rows, states)
    own, *others, tile = pl.pallas_call(
        functools.partial(sum_kernel, sectors, shares),
        out_shape=(
            jax.ShapeDtypeStruct(share_shape, jnp.float32),
            *[jax.ShapeDtypeStruct(share_shape, jnp.bfloat16)] * (shares - 1),
            jax.ShapeDtypeStruct(TILE, jnp.float32),
        ),
        in_specs=[pl.BlockSpec(memory_space=pltpu.SMEM)]
        + in_vmem(3)
        + [pl.BlockSpec(memory_space=pl.ANY)] * len(pieces),
        out_specs=tuple(in_vmem(shares + 1)),
        scratch_shapes=[
            pltpu.VMEM((sectors, terms, states, states), jnp.bfloat16),
            pltpu.VMEM((trials, states, states), jnp.float32),
            pltpu.SemaphoreType.DMA((2 * sectors,)),
        ],
        compiler_params=pltpu.CompilerParams(
            vmem_limit_bytes=sectors * terms * states * states * 2 + 12 * MIB
        ),
        cost_estimate=pl.CostEstimate(flops=flops, bytes_accessed=8 * MIB, transcendentals=0),
        name="sum_over_terms",
    )(offsets, vectors, inner, squares, *pieces)

    received = [swap(share, "term", mask + 1) for mask, share in enumerate(others)]
    for axis in ("sec", "term"):
        step = 1
        while step < lax.axis_size(axis):
            tile = tile + swap(tile, axis, step)
            step *= 2
    products = own
    for share in received:
        products = products + share.astype(jnp.float32)
    column = tile[:, 0]
    gram = column[: trials * trials].reshape(trials, trials)
    squares = column[trials * trials : trials * trials + trials]
    rayleigh = gram / jnp.sqrt(squares[:, None] * squares[None, :])
    return (products.astype(jnp.bfloat16)[:, None], rayleigh)


def solution(mesh):
    in_specs = (
        P(None, "sec", None, None, None),
        P("term", "sec", None, None),
        P("term", "sec", None, None),
        P("term", None),
    )
    out_specs = (P(None, "sec", None, "term", None), P())
    return jax.shard_map(local, mesh=mesh, in_specs=in_specs, out_specs=out_specs, check_vma=False)
```

time: 191 us -> 67.1 us (0.35)
  the two profiles are of different devices: /device:TPU:0 before, /device:TPU:8 now
where the time goes in v1:
time: 67.1 us; the launch traced here: 66.9 us
  waiting for transfers between devices  40.9 us (61%)
  starting transfers between devices  15.2 us (23%)
  Pallas kernels  4.74 us (7%)
  local copies, waits for them, and re-layouts  3.77 us (6%)
  other arithmetic  1.49 us (2%)
  between operations  0.75 us (1%)
    ppermute x22, waiting for transfers between devices, swap(): lax.ppermute(value, axis, [(place, place ^ mask) for place in range(count)])  40.9 us
    ppermute x22, starting transfers between devices, swap(): lax.ppermute(value, axis, [(place, place ^ mask) for place in range(count)])  15.2 us
    pallas_call x1, Pallas kernels, local(): pl.pallas_call(functools.partial(sum_kernel, sectors, shares), out_shape=...  3.76 us
    unnamed x8, local copies, waits for them, and re-layouts  2.4 us
  transfers between devices with their start and end apart: 22, of which 12 were waited for; matrix products, arithmetic and copies ran while one was open for 1% of the time, Pallas kernels for 1%

profile of v1, /device:TPU:8, one launch (start us, length us, event | category | flops | bytes accessed | tf_op | source)
XLA Modules:
  0.0 66.9 jit_solution(15995569399912507933)
XLA Ops:
  0.6 1.1 %fusion.1 = (bf16[3,128,256]{2,1,0:T(8,128)(2,1)S(1)}, bf16[3,128,256]{2,1,0:T(8,128)(2,1)S(1)}) fusion(bf16[3,256,256]{2,1,0:T(8,128)(2,1)} %bitcast.10), kind=kLoop, calls=%fused_computation.5 | loop fusion | bytes 786432 | tf_op jit(solution)/shard_map/slice | solution.py:123
  1.7 1.6 %collective-permute-start.7 = (bf16[3,128,256]{2,1,0:T(8,128)(2,1)S(1)}, bf16[3,128,256]{2,1,0:T(8,128)(2,1)S(1)}, u32[]{:S(2)}, u32[]{:S(2)}) collective-permute-start(bf16[3,128,256]{2,1,0:T(8,128)(2,1)S(1)} %get-tuple-element.20.rest_1_), channel_id=1, source_target_pairs={{0,16},{4,20},{8,24},{12,28},{16,0},{20,4},{24,8},{28,12},{1,17},{... | collective-permute-start | bytes 589832 | tf_op jit(solution)/shard_map/ppermute | solution.py:16
  3.3 1.5 %collective-permute-start.3 = (bf16[3,128,256]{2,1,0:T(8,128)(2,1)S(1)}, bf16[3,128,256]{2,1,0:T(8,128)(2,1)S(1)}, u32[]{:S(2)}, u32[]{:S(2)}) collective-permute-start(bf16[3,128,256]{2,1,0:T(8,128)(2,1)S(1)} %get-tuple-element.20.rest_1_), channel_id=1, source_target_pairs={{0,8},{4,12},{8,0},{12,4},{16,24},{20,28},{24,16},{28,20},{1,9},{5... | collective-permute-start | bytes 589832 | tf_op jit(solution)/shard_map/ppermute | solution.py:16
  5.8 2.8 %collective-permute-done.7.rest_9_ = bf16[3,128,256]{2,1,0:T(8,128)(2,1)S(1)} collective-permute-done((bf16[3,128,256]{2,1,0:T(8,128)(2,1)S(1)}, bf16[3,128,256]{2,1,0:T(8,128)(2,1)S(1)}, u32[]{:S(2)}, u32[]{:S(2)}) %collective-permute-start.7) | collective-permute-done | bytes 196640 | tf_op jit(solution)/shard_map/ppermute | solution.py:16
  8.6 2.5 %collective-permute-done.3.rest_5_ = bf16[3,128,256]{2,1,0:T(8,128)(2,1)S(1)} collective-permute-done((bf16[3,128,256]{2,1,0:T(8,128)(2,1)S(1)}, bf16[3,128,256]{2,1,0:T(8,128)(2,1)S(1)}, u32[]{:S(2)}, u32[]{:S(2)}) %collective-permute-start.3) | collective-permute-done | bytes 196640 | tf_op jit(solution)/shard_map/ppermute | solution.py:16
  11.1 1.5 %collective-permute-start.11 = (bf16[3,128,256]{2,1,0:T(8,128)(2,1)S(1)}, bf16[3,128,256]{2,1,0:T(8,128)(2,1)S(1)}, u32[]{:S(2)}, u32[]{:S(2)}) collective-permute-start(bf16[3,128,256]{2,1,0:T(8,128)(2,1)S(1)} %collective-permute-done.7.rest_9_), channel_id=1, source_target_pairs={{0,8},{4,12},{8,0},{12,4},{16,24},{20,28},{24,16},{28,20},{1,9},{5... | collective-permute-start | bytes 589832 | tf_op jit(solution)/shard_map/ppermute | solution.py:16
  12.6 2.7 %collective-permute-done.2.rest_4_ = bf16[3,128,256]{2,1,0:T(8,128)(2,1)S(1)} collective-permute-done((bf16[3,128,256]{2,1,0:T(8,128)(2,1)S(1)}, bf16[3,128,256]{2,1,0:T(8,128)(2,1)S(1)}, u32[]{:S(2)}, u32[]{:S(2)}) %collective-permute-start.2) | collective-permute-done | bytes 196640 | tf_op jit(solution)/shard_map/ppermute | solution.py:16
  15.8 2.2 %collective-permute-done.11.rest_13_ = bf16[3,128,256]{2,1,0:T(8,128)(2,1)S(1)} collective-permute-done((bf16[3,128,256]{2,1,0:T(8,128)(2,1)S(1)}, bf16[3,128,256]{2,1,0:T(8,128)(2,1)S(1)}, u32[]{:S(2)}, u32[]{:S(2)}) %collective-permute-start.11) | collective-permute-done | bytes 196640 | tf_op jit(solution)/shard_map/ppermute | solution.py:16
  18.6 2.4 %collective-permute-done.10.rest_12_ = bf16[3,128,256]{2,1,0:T(8,128)(2,1)S(1)} collective-permute-done((bf16[3,128,256]{2,1,0:T(8,128)(2,1)S(1)}, bf16[3,128,256]{2,1,0:T(8,128)(2,1)S(1)}, u32[]{:S(2)}, u32[]{:S(2)}) %collective-permute-start.10) | collective-permute-done | bytes 196640 | tf_op jit(solution)/shard_map/ppermute | solution.py:16
  21.0 1.2 %copy-done = bf16[2,1,4,256,256]{4,3,2,1,0:T(8,128)(2,1)S(1)} copy-done((bf16[2,1,4,256,256]{4,3,2,1,0:T(8,128)(2,1)S(1)}, bf16[2,1,4,256,256]{4,3,2,1,0:T(8,128)(2,1)}, u32[]{:S(2)}) %copy-start) | copy-done | bytes 1048600
  22.2 1.0 %copy-done.3 = bf16[3,1,256,256]{3,2,1,0:T(8,128)(2,1)S(1)} copy-done((bf16[3,1,256,256]{3,2,1,0:T(8,128)(2,1)S(1)}, bf16[3,1,256,256]{3,2,1,0:T(8,128)(2,1)}, u32[]{:S(2)}) %copy-start.3) | copy-done | bytes 393240
  23.2 1.0 %inner_products.1 = (bf16[3,2,4,256,256]{4,3,2,1,0:T(8,128)(2,1)S(1)}, f32[8,128]{1,0:T(8,128)S(1)}) custom-call(bf16[2,4,256,256]{3,2,1,0:T(8,128)(2,1)S(1)} %bitcast.7, bf16[3,256,256]{2,1,0:T(8,128)(2,1)S(1)} %bitcast.9), custom_call_target="tpu_custom_call" | custom-call | flops 805306368 | bytes 5242880 | tf_op jit(solution)/shard_map/inner_products/pallas_call | solution.py:127
  24.4 3.8 %sum_over_terms.1 = (f32[2,4,64,256]{3,2,1,0:T(8,128)S(1)}, bf16[2,4,64,256]{3,2,1,0:T(8,128)(2,1)S(1)}, bf16[2,4,64,256]{3,2,1,0:T(8,128)(2,1)S(1)}, bf16[2,4,64,256]{3,2,1,0:T(8,128)(2,1)S(1)}, f32[8,128]{1,0:T(8,128)S(1)}) custom-call(s32[3,4]{1,0:T(4,128)S(1)} %copy-done.2, bf16[2,4,256,256]{3,2,1,0:T(8,128)(2,1)S(1)} %bitcast.8, ...), custom_call_target="tpu_custom_call" | custom-call | flops 805306368 | bytes 8388608 | tf_op jit(solution)/shard_map/sum_over_terms/pallas_call | solution.py:141
  28.8 0.8 %collective-permute-done.17 = f32[8,128]{1,0:T(8,128)S(1)} collective-permute-done((f32[8,128]{1,0:T(8,128)S(1)}, f32[8,128]{1,0:T(8,128)S(1)}, u32[]{:S(2)}, u32[]{:S(2)}) %collective-permute-start.17) | collective-permute-done | bytes 4128 | tf_op jit(solution)/shard_map/ppermute | solution.py:16
  29.6 1.5 %collective-permute-start.18 = (f32[8,128]{1,0:T(8,128)S(1)}, f32[8,128]{1,0:T(8,128)S(1)}, u32[]{:S(2)}, u32[]{:S(2)}) collective-permute-start(f32[8,128]{1,0:T(8,128)S(1)} %add.27), channel_id=1, source_target_pairs={{0,8},{4,12},{8,0},{12,4},{16,24},{20,28},{24,16},{28,20},{1,9},{5... | collective-permute-start | bytes 12296 | tf_op jit(solution)/shard_map/ppermute | solution.py:16
  31.1 2.1 %collective-permute-done.18 = f32[8,128]{1,0:T(8,128)S(1)} collective-permute-done((f32[8,128]{1,0:T(8,128)S(1)}, f32[8,128]{1,0:T(8,128)S(1)}, u32[]{:S(2)}, u32[]{:S(2)}) %collective-permute-start.18) | collective-permute-done | bytes 4128 | tf_op jit(solution)/shard_map/ppermute | solution.py:16
  33.2 3.6 %collective-permute-done.19 = f32[8,128]{1,0:T(8,128)S(1)} collective-permute-done((f32[8,128]{1,0:T(8,128)S(1)}, f32[8,128]{1,0:T(8,128)S(1)}, u32[]{:S(2)}, u32[]{:S(2)}) %collective-permute-start.19) | collective-permute-done | bytes 4128 | tf_op jit(solution)/shard_map/ppermute | solution.py:16
  37.3 3.2 %collective-permute-done.20 = f32[8,128]{1,0:T(8,128)S(1)} collective-permute-done((f32[8,128]{1,0:T(8,128)S(1)}, f32[8,128]{1,0:T(8,128)S(1)}, u32[]{:S(2)}, u32[]{:S(2)}) %collective-permute-start.20) | collective-permute-done | bytes 4128 | tf_op jit(solution)/shard_map/ppermute | solution.py:16
  40.4 2.6 %collective-permute-start.21 = (f32[8,128]{1,0:T(8,128)S(1)}, f32[8,128]{1,0:T(8,128)S(1)}, u32[]{:S(2)}, u32[]{:S(2)}) collective-permute-start(f32[8,128]{1,0:T(8,128)S(1)} %add.30), channel_id=1, source_target_pairs={{0,2},{1,3},{2,0},{3,1},{4,6},{5,7},{6,4},{7,5},{8,10},{9,11},{10,... | collective-permute-start | bytes 12296 | tf_op jit(solution)/shard_map/ppermute | solution.py:16
  43.8 2.7 %collective-permute-start.16 = (bf16[2,4,64,256]{3,2,1,0:T(8,128)(2,1)S(1)}, bf16[2,4,64,256]{3,2,1,0:T(8,128)(2,1)S(1)}, u32[]{:S(2)}, u32[]{:S(2)}) collective-permute-start(bf16[2,4,64,256]{3,2,1,0:T(8,128)(2,1)S(1)} %get-tuple-element.14), channel_id=1, source_target_pairs={{0,3},{1,2},{2,1},{3,0},{4,7},{5,6},{6,5},{7,4},{8,11},{9,10},{10,... | collective-permute-start | bytes 786440 | tf_op jit(solution)/shard_map/ppermute | solution.py:16
  47.5 5.4 %collective-permute-done.14 = bf16[2,4,64,256]{3,2,1,0:T(8,128)(2,1)S(1)} collective-permute-done((bf16[2,4,64,256]{3,2,1,0:T(8,128)(2,1)S(1)}, bf16[2,4,64,256]{3,2,1,0:T(8,128)(2,1)S(1)}, u32[]{:S(2)}, u32[]{:S(2)}) %collective-permute-start.14) | collective-permute-done | bytes 262176 | tf_op jit(solution)/shard_map/ppermute | solution.py:16
  52.9 7.1 %collective-permute-done.15 = bf16[2,4,64,256]{3,2,1,0:T(8,128)(2,1)S(1)} collective-permute-done((bf16[2,4,64,256]{3,2,1,0:T(8,128)(2,1)S(1)}, bf16[2,4,64,256]{3,2,1,0:T(8,128)(2,1)S(1)}, u32[]{:S(2)}, u32[]{:S(2)}) %collective-permute-start.15) | collective-permute-done | bytes 262176 | tf_op jit(solution)/shard_map/ppermute | solution.py:16
  60.0 6.0 %collective-permute-done.16 = bf16[2,4,64,256]{3,2,1,0:T(8,128)(2,1)S(1)} collective-permute-done((bf16[2,4,64,256]{3,2,1,0:T(8,128)(2,1)S(1)}, bf16[2,4,64,256]{3,2,1,0:T(8,128)(2,1)S(1)}, u32[]{:S(2)}, u32[]{:S(2)}) %collective-permute-start.16) | collective-permute-done | bytes 262176 | tf_op jit(solution)/shard_map/ppermute | solution.py:16
  66.0 0.8 %fusion = bf16[2,1,4,64,256]{4,3,2,1,0:T(8,128)(2,1)} fusion(bf16[2,4,64,256]{3,2,1,0:T(8,128)(2,1)S(1)} %collective-permute-done.16, bf16[2,4,64,256]{3,2,1,0:T(8,128)(2,1)S(1)} %collective-permute-done.15, f32[2,4,64,256]{3,2,1,0:T(8,128)S(1)} %get-tuple-element.11, bf16[2,4,64,256]{3,2,1,0:T(8,128)(2,1)S(1)} %collective-permute-done.14), kind=kLoop, calls=%fused_computation.1 | loop fusion | flops 917504 | bytes 1572864
  (41 shorter events, 5.0 us)
Async XLA Ops:
  0.6 23.6 %copy-start.2 = (s32[3,4]{1,0:T(4,128)S(1)}, s32[3,4]{1,0:T(4,128)}, u32[]{:S(2)}) copy-start(s32[3,4]{1,0:T(4,128)} %offsets.1) | copy-start | bytes 148
  1.7 6.9 %collective-permute-start.7 = (bf16[3,128,256]{2,1,0:T(8,128)(2,1)S(1)}, bf16[3,128,256]{2,1,0:T(8,128)(2,1)S(1)}, u32[]{:S(2)}, u32[]{:S(2)}) collective-permute-start(bf16[3,128,256]{2,1,0:T(8,128)(2,1)S(1)} %get-tuple-element.20.rest_1_), channel_id=1, source_target_pairs={{0,16},{4,20},{8,24},{12,28},{16,0},{20,4},{24,8},{28,12},{1,17},{... | collective-permute-start | bytes 589832 | tf_op jit(solution)/shard_map/ppermute | solution.py:16
  3.3 7.8 %collective-permute-start.3 = (bf16[3,128,256]{2,1,0:T(8,128)(2,1)S(1)}, bf16[3,128,256]{2,1,0:T(8,128)(2,1)S(1)}, u32[]{:S(2)}, u32[]{:S(2)}) collective-permute-start(bf16[3,128,256]{2,1,0:T(8,128)(2,1)S(1)} %get-tuple-element.20.rest_1_), channel_id=1, source_target_pairs={{0,8},{4,12},{8,0},{12,4},{16,24},{20,28},{24,16},{28,20},{1,9},{5... | collective-permute-start | bytes 589832 | tf_op jit(solution)/shard_map/ppermute | solution.py:16
  4.8 7.8 %collective-permute-start.1 = (bf16[3,128,256]{2,1,0:T(8,128)(2,1)S(1)}, bf16[3,128,256]{2,1,0:T(8,128)(2,1)S(1)}, u32[]{:S(2)}, u32[]{:S(2)}) collective-permute-start(bf16[3,128,256]{2,1,0:T(8,128)(2,1)S(1)} %get-tuple-element.20.rest_1_), channel_id=1, source_target_pairs={{0,4},{4,0},{8,12},{12,8},{16,20},{20,16},{24,28},{28,24},{1,5},{5... | collective-permute-start | bytes 589832 | tf_op jit(solution)/shard_map/ppermute | solution.py:16
  4.8 10.5 %collective-permute-start.2 = (bf16[3,128,256]{2,1,0:T(8,128)(2,1)S(1)}, bf16[3,128,256]{2,1,0:T(8,128)(2,1)S(1)}, u32[]{:S(2)}, u32[]{:S(2)}) collective-permute-start(bf16[3,128,256]{2,1,0:T(8,128)(2,1)S(1)} %get-tuple-element.21.rest_0_), channel_id=1, source_target_pairs={{0,8},{4,12},{8,0},{12,4},{16,24},{20,28},{24,16},{28,20},{1,9},{5... | collective-permute-start | bytes 589832 | tf_op jit(solution)/shard_map/ppermute | solution.py:16
  5.3 10.0 %collective-permute-start.6 = (bf16[3,128,256]{2,1,0:T(8,128)(2,1)S(1)}, bf16[3,128,256]{2,1,0:T(8,128)(2,1)S(1)}, u32[]{:S(2)}, u32[]{:S(2)}) collective-permute-start(bf16[3,128,256]{2,1,0:T(8,128)(2,1)S(1)} %get-tuple-element.21.rest_0_), channel_id=1, source_target_pairs={{0,16},{4,20},{8,24},{12,28},{16,0},{20,4},{24,8},{28,12},{1,17},{... | collective-permute-start | bytes 589832 | tf_op jit(solution)/shard_map/ppermute | solution.py:16
  8.6 6.7 %collective-permute-start = (bf16[3,128,256]{2,1,0:T(8,128)(2,1)S(1)}, bf16[3,128,256]{2,1,0:T(8,128)(2,1)S(1)}, u32[]{:S(2)}, u32[]{:S(2)}) collective-permute-start(bf16[3,128,256]{2,1,0:T(8,128)(2,1)S(1)} %get-tuple-element.21.rest_0_), channel_id=1, source_target_pairs={{0,4},{4,0},{8,12},{12,8},{16,20},{20,16},{24,28},{28,24},{1,5},{5... | collective-permute-start | bytes 589832 | tf_op jit(solution)/shard_map/ppermute | solution.py:16
  11.1 7.0 %collective-permute-start.11 = (bf16[3,128,256]{2,1,0:T(8,128)(2,1)S(1)}, bf16[3,128,256]{2,1,0:T(8,128)(2,1)S(1)}, u32[]{:S(2)}, u32[]{:S(2)}) collective-permute-start(bf16[3,128,256]{2,1,0:T(8,128)(2,1)S(1)} %collective-permute-done.7.rest_9_), channel_id=1, source_target_pairs={{0,8},{4,12},{8,0},{12,4},{16,24},{20,28},{24,16},{28,20},{1,9},{5... | collective-permute-start | bytes 589832 | tf_op jit(solution)/shard_map/ppermute | solution.py:16
  12.6 5.5 %collective-permute-start.9 = (bf16[3,128,256]{2,1,0:T(8,128)(2,1)S(1)}, bf16[3,128,256]{2,1,0:T(8,128)(2,1)S(1)}, u32[]{:S(2)}, u32[]{:S(2)}) collective-permute-start(bf16[3,128,256]{2,1,0:T(8,128)(2,1)S(1)} %collective-permute-done.7.rest_9_), channel_id=1, source_target_pairs={{0,4},{4,0},{8,12},{12,8},{16,20},{20,16},{24,28},{28,24},{1,5},{5... | collective-permute-start | bytes 589832 | tf_op jit(solution)/shard_map/ppermute | solution.py:16
  15.3 5.7 %collective-permute-start.10 = (bf16[3,128,256]{2,1,0:T(8,128)(2,1)S(1)}, bf16[3,128,256]{2,1,0:T(8,128)(2,1)S(1)}, u32[]{:S(2)}, u32[]{:S(2)}) collective-permute-start(bf16[3,128,256]{2,1,0:T(8,128)(2,1)S(1)} %collective-permute-done.2.rest_4_), channel_id=1, source_target_pairs={{0,16},{4,20},{8,24},{12,28},{16,0},{20,4},{24,8},{28,12},{1,17},{... | collective-permute-start | bytes 589832 | tf_op jit(solution)/shard_map/ppermute | solution.py:16
  15.3 8.9 %collective-permute-start.4 = (bf16[3,128,256]{2,1,0:T(8,128)(2,1)S(1)}, bf16[3,128,256]{2,1,0:T(8,128)(2,1)S(1)}, u32[]{:S(2)}, u32[]{:S(2)}) collective-permute-start(bf16[3,128,256]{2,1,0:T(8,128)(2,1)S(1)} %collective-permute-done.2.rest_4_), channel_id=1, source_target_pairs={{0,4},{4,0},{8,12},{12,8},{16,20},{20,16},{24,28},{28,24},{1,5},{5... | collective-permute-start | bytes 589832 | tf_op jit(solution)/shard_map/ppermute | solution.py:16
  15.3 8.9 %collective-permute-start.5 = (bf16[3,128,256]{2,1,0:T(8,128)(2,1)S(1)}, bf16[3,128,256]{2,1,0:T(8,128)(2,1)S(1)}, u32[]{:S(2)}, u32[]{:S(2)}) collective-permute-start(bf16[3,128,256]{2,1,0:T(8,128)(2,1)S(1)} %collective-permute-done.3.rest_5_), channel_id=1, source_target_pairs={{0,4},{4,0},{8,12},{12,8},{16,20},{20,16},{24,28},{28,24},{1,5},{5... | collective-permute-start | bytes 589832 | tf_op jit(solution)/shard_map/ppermute | solution.py:16
  18.1 6.2 %collective-permute-start.8 = (bf16[3,128,256]{2,1,0:T(8,128)(2,1)S(1)}, bf16[3,128,256]{2,1,0:T(8,128)(2,1)S(1)}, u32[]{:S(2)}, u32[]{:S(2)}) collective-permute-start(bf16[3,128,256]{2,1,0:T(8,128)(2,1)S(1)} %collective-permute-done.6.rest_8_), channel_id=1, source_target_pairs={{0,4},{4,0},{8,12},{12,8},{16,20},{20,16},{24,28},{28,24},{1,5},{5... | collective-permute-start | bytes 589832 | tf_op jit(solution)/shard_map/ppermute | solution.py:16
  18.1 6.2 %collective-permute-start.13 = (bf16[3,128,256]{2,1,0:T(8,128)(2,1)S(1)}, bf16[3,128,256]{2,1,0:T(8,128)(2,1)S(1)}, u32[]{:S(2)}, u32[]{:S(2)}) collective-permute-start(bf16[3,128,256]{2,1,0:T(8,128)(2,1)S(1)} %collective-permute-done.11.rest_13_), channel_id=1, source_target_pairs={{0,4},{4,0},{8,12},{12,8},{16,20},{20,16},{24,28},{28,24},{1,5},{5... | collective-permute-start | bytes 589832 | tf_op jit(solution)/shard_map/ppermute | solution.py:16
  21.0 3.3 %collective-permute-start.12 = (bf16[3,128,256]{2,1,0:T(8,128)(2,1)S(1)}, bf16[3,128,256]{2,1,0:T(8,128)(2,1)S(1)}, u32[]{:S(2)}, u32[]{:S(2)}) collective-permute-start(bf16[3,128,256]{2,1,0:T(8,128)(2,1)S(1)} %collective-permute-done.10.rest_12_), channel_id=1, source_target_pairs={{0,4},{4,0},{8,12},{12,8},{16,20},{20,16},{24,28},{28,24},{1,5},{5... | collective-permute-start | bytes 589832 | tf_op jit(solution)/shard_map/ppermute | solution.py:16
  21.0 1.2 %copy-start = (bf16[2,1,4,256,256]{4,3,2,1,0:T(8,128)(2,1)S(1)}, bf16[2,1,4,256,256]{4,3,2,1,0:T(8,128)(2,1)}, u32[]{:S(2)}) copy-start(bf16[2,1,4,256,256]{4,3,2,1,0:T(8,128)(2,1)} %param.4) | copy-start | bytes 3145732
  28.2 1.4 %collective-permute-start.17 = (f32[8,128]{1,0:T(8,128)S(1)}, f32[8,128]{1,0:T(8,128)S(1)}, u32[]{:S(2)}, u32[]{:S(2)}) collective-permute-start(f32[8,128]{1,0:T(8,128)S(1)} %get-tuple-element.15), channel_id=1, source_target_pairs={{0,4},{4,0},{8,12},{12,8},{16,20},{20,16},{24,28},{28,24},{1,5},{5... | collective-permute-start | bytes 12296 | tf_op jit(solution)/shard_map/ppermute | solution.py:16
  29.6 3.6 %collective-permute-start.18 = (f32[8,128]{1,0:T(8,128)S(1)}, f32[8,128]{1,0:T(8,128)S(1)}, u32[]{:S(2)}, u32[]{:S(2)}) collective-permute-start(f32[8,128]{1,0:T(8,128)S(1)} %add.27), channel_id=1, source_target_pairs={{0,8},{4,12},{8,0},{12,4},{16,24},{20,28},{24,16},{28,20},{1,9},{5... | collective-permute-start | bytes 12296 | tf_op jit(solution)/shard_map/ppermute | solution.py:16
  33.2 3.6 %collective-permute-start.19 = (f32[8,128]{1,0:T(8,128)S(1)}, f32[8,128]{1,0:T(8,128)S(1)}, u32[]{:S(2)}, u32[]{:S(2)}) collective-permute-start(f32[8,128]{1,0:T(8,128)S(1)} %add.28), channel_id=1, source_target_pairs={{0,16},{4,20},{8,24},{12,28},{16,0},{20,4},{24,8},{28,12},{1,17},{... | collective-permute-start | bytes 12296 | tf_op jit(solution)/shard_map/ppermute | solution.py:16
  36.8 3.6 %collective-permute-start.20 = (f32[8,128]{1,0:T(8,128)S(1)}, f32[8,128]{1,0:T(8,128)S(1)}, u32[]{:S(2)}, u32[]{:S(2)}) collective-permute-start(f32[8,128]{1,0:T(8,128)S(1)} %add.29), channel_id=1, source_target_pairs={{0,1},{1,0},{2,3},{3,2},{4,5},{5,4},{6,7},{7,6},{8,9},{9,8},{10,11... | collective-permute-start | bytes 12296 | tf_op jit(solution)/shard_map/ppermute | solution.py:16
  40.4 6.1 %collective-permute-start.21 = (f32[8,128]{1,0:T(8,128)S(1)}, f32[8,128]{1,0:T(8,128)S(1)}, u32[]{:S(2)}, u32[]{:S(2)}) collective-permute-start(f32[8,128]{1,0:T(8,128)S(1)} %add.30), channel_id=1, source_target_pairs={{0,2},{1,3},{2,0},{3,1},{4,6},{5,7},{6,4},{7,5},{8,10},{9,11},{10,... | collective-permute-start | bytes 12296 | tf_op jit(solution)/shard_map/ppermute | solution.py:16
  43.0 9.9 %collective-permute-start.14 = (bf16[2,4,64,256]{3,2,1,0:T(8,128)(2,1)S(1)}, bf16[2,4,64,256]{3,2,1,0:T(8,128)(2,1)S(1)}, u32[]{:S(2)}, u32[]{:S(2)}) collective-permute-start(bf16[2,4,64,256]{3,2,1,0:T(8,128)(2,1)S(1)} %get-tuple-element.12), channel_id=1, source_target_pairs={{0,1},{1,0},{2,3},{3,2},{4,5},{5,4},{6,7},{7,6},{8,9},{9,8},{10,11... | collective-permute-start | bytes 786440 | tf_op jit(solution)/shard_map/ppermute | solution.py:16
  43.5 16.5 %collective-permute-start.15 = (bf16[2,4,64,256]{3,2,1,0:T(8,128)(2,1)S(1)}, bf16[2,4,64,256]{3,2,1,0:T(8,128)(2,1)S(1)}, u32[]{:S(2)}, u32[]{:S(2)}) collective-permute-start(bf16[2,4,64,256]{3,2,1,0:T(8,128)(2,1)S(1)} %get-tuple-element.13), channel_id=1, source_target_pairs={{0,2},{1,3},{2,0},{3,1},{4,6},{5,7},{6,4},{7,5},{8,10},{9,11},{10,... | collective-permute-start | bytes 786440 | tf_op jit(solution)/shard_map/ppermute | solution.py:16
  43.8 22.2 %collective-permute-start.16 = (bf16[2,4,64,256]{3,2,1,0:T(8,128)(2,1)S(1)}, bf16[2,4,64,256]{3,2,1,0:T(8,128)(2,1)S(1)}, u32[]{:S(2)}, u32[]{:S(2)}) collective-permute-start(bf16[2,4,64,256]{3,2,1,0:T(8,128)(2,1)S(1)} %get-tuple-element.14), channel_id=1, source_target_pairs={{0,3},{1,2},{2,1},{3,0},{4,7},{5,6},{6,5},{7,4},{8,11},{9,10},{10,... | collective-permute-start | bytes 786440 | tf_op jit(solution)/shard_map/ppermute | solution.py:16
  (2 other events, 2.2 us)

commit v2 on v1

v2 whole, which is shorter than its diff:
```python
import functools

import jax
import jax.numpy as jnp
from jax import lax
from jax.experimental import pallas as pl
from jax.experimental.pallas import tpu as pltpu
from jax.sharding import PartitionSpec as P

MIB = 1 << 20
TILE = (8, 128)
CHUNKS = 2
VMEM = pl.BlockSpec(memory_space=pltpu.VMEM)
SMEM = pl.BlockSpec(memory_space=pltpu.SMEM)
ANY = pl.BlockSpec(memory_space=pl.ANY)


def swap(value, axis, mask):
    count = lax.axis_size(axis)
    return lax.ppermute(value, axis, [(place, place ^ mask) for place in range(count)])


def place_rows(values):
    row = lax.broadcasted_iota(jnp.int32, TILE, 0)
    tile = jnp.zeros(TILE, jnp.float32)
    for position, value in values:
        tile = jnp.where(row == position, value, tile)
    return tile


def total(value):
    return jnp.sum(jnp.sum(value, axis=0, keepdims=True), axis=1, keepdims=True)


def inner_kernel(square_scale, vectors, left, inner, squares):
    terms, states = left.shape[0], left.shape[1]
    stacked = left[...].reshape(terms * states, states)
    sums = []
    for trial in range(vectors.shape[0]):
        square = jnp.zeros((8, states), jnp.float32)
        for pair in range(vectors.shape[1]):
            block = vectors[trial, pair]
            product = jnp.dot(stacked, block, preferred_element_type=jnp.float32)
            inner[:, trial, pair] = product.astype(jnp.bfloat16).reshape(terms, states, states)
            wide = block.astype(jnp.float32)
            square += jnp.sum((wide * wide).reshape(-1, 8, states), axis=0)
        sums.append(total(square) * square_scale)
    trials = len(sums)
    squares[...] = place_rows([(trials * trials + k, value) for k, value in enumerate(sums)])


def sum_kernel(sectors, chunk, offsets, vectors, inner, before, *rest):
    pieces = rest[:sectors]
    keep, send, tile, rights, partial = rest[-5:]
    terms, trials, pairs, states, _ = inner.shape
    width = partial.shape[2]
    shares = 2 * keep.shape[0]
    rows = states // shares
    for mask in range(sectors):
        rights[mask] = pieces[mask][...]
    sector = lax.axis_index("sec")
    place = lax.axis_index("term")
    columns = slice(chunk * width, (chunk + 1) * width)
    grams = [jnp.zeros((8, width), jnp.float32) for _ in range(trials * trials)]
    for pair in range(pairs):
        result = None
        for term in range(terms):
            wanted = (sector + offsets[term, pair]) & (sectors - 1)
            added = jnp.dot(
                inner[term, :, pair].reshape(trials * states, states),
                rights[sector ^ wanted, term],
                preferred_element_type=jnp.float32,
            )
            result = added if result is None else result + added
        partial[...] = result.reshape(trials, states, width)
        for j in range(trials):
            product = partial[j]
            for i in range(trials):
                spread = vectors[i, pair, :, columns].astype(jnp.float32) * product
                grams[i * trials + j] += jnp.sum(spread.reshape(-1, 8, width), axis=0)
        for mask in range(shares):
            start = pl.multiple_of((place ^ mask) * rows, rows)
            share = partial[:, pl.ds(start, rows)]
            if mask & 1:
                send[mask // 2, :, pair] = share.astype(jnp.bfloat16)
            else:
                keep[mask // 2, :, pair] = share
    tile[...] = before[...] + place_rows([(k, total(value)) for k, value in enumerate(grams)])


def halve_kernel(kept, received, keep, send):
    for k in range(kept.shape[0]):
        both = kept[k] + received[k].astype(jnp.float32)
        if k & 1:
            send[k // 2] = both.astype(jnp.bfloat16)
        else:
            keep[k // 2] = both


def finish_kernel(*refs):
    *parts, products = refs
    width = products.shape[-1] // (len(parts) // 2)
    for chunk in range(len(parts) // 2):
        kept, received = parts[2 * chunk : 2 * chunk + 2]
        both = kept[0] + received[0].astype(jnp.float32)
        products[:, :, :, chunk * width : (chunk + 1) * width] = both.astype(jnp.bfloat16)


def rayleigh_kernel(tiles, rayleigh):
    tile = jnp.sum(tiles[...], axis=0)
    trials = rayleigh.shape[0]
    row = lax.broadcasted_iota(jnp.int32, rayleigh.shape, 0)
    column = lax.broadcasted_iota(jnp.int32, rayleigh.shape, 1)

    def entry(position):
        return tile[position : position + 1, :trials]

    result = jnp.zeros(rayleigh.shape, jnp.float32)
    for i in range(trials):
        for j in range(trials):
            squares = entry(trials * trials + i) * entry(trials * trials + j)
            value = entry(i * trials + j) / jnp.sqrt(squares)
            result = jnp.where((row == i) & (column == j), value, result)
    rayleigh[...] = result


def call(kernel, name, flops, moved, limit, **kwargs):
    return pl.pallas_call(
        kernel,
        name=name,
        cost_estimate=pl.CostEstimate(flops=flops, bytes_accessed=moved, transcendentals=0),
        compiler_params=pltpu.CompilerParams(vmem_limit_bytes=limit),
        **kwargs,
    )


def local(vectors, left_ops, right_ops, offsets):
    sectors = lax.axis_size("sec")
    shares = lax.axis_size("term")
    trials, _, pairs, states, _ = vectors.shape
    terms = left_ops.shape[0]
    vectors, left, right = vectors[:, 0], left_ops[:, 0], right_ops[:, 0]
    width, rows = states // CHUNKS, states // shares

    inner, tile = call(
        functools.partial(inner_kernel, 1.0 / shares),
        "inner_products",
        2 * terms * trials * pairs * states**3,
        5 * MIB,
        12 * MIB,
        out_shape=(
            jax.ShapeDtypeStruct((terms, trials, pairs, states, states), jnp.bfloat16),
            jax.ShapeDtypeStruct(TILE, jnp.float32),
        ),
        in_specs=[VMEM, VMEM],
        out_specs=(VMEM, VMEM),
    )(vectors, left)

    gathered = []
    for chunk in range(CHUNKS):
        own = right[:, :, chunk * width : (chunk + 1) * width]
        held = [own] + [swap(own, "sec", mask) for mask in range(2, sectors, 2)]
        if chunk == 0:
            held[1], inner = lax.optimization_barrier((held[1], inner))
        both = []
        for block in held:
            both += [block, swap(block, "sec", 1)]
        gathered.append(both)

    def share_of(count, dtype):
        return jax.ShapeDtypeStruct((count, trials, pairs, rows, width), dtype)

    parts, waited = [], None
    for chunk in range(CHUNKS):
        after = [] if waited is None else [waited]
        keep, send, tile = call(
            functools.partial(sum_kernel, sectors, chunk),
            "sum_over_terms",
            2 * terms * trials * pairs * states * states * width,
            4 * MIB,
            sectors * terms * states * width * 2 + 12 * MIB,
            out_shape=(
                share_of(shares // 2, jnp.float32),
                share_of(shares // 2, jnp.bfloat16),
                jax.ShapeDtypeStruct(TILE, jnp.float32),
            ),
            in_specs=[SMEM, VMEM, VMEM, VMEM] + [VMEM] * sectors + [ANY] * len(after),
            out_specs=(VMEM, VMEM, VMEM),
            scratch_shapes=[
                pltpu.VMEM((sectors, terms, states, width), jnp.bfloat16),
                pltpu.VMEM((trials, states, width), jnp.float32),
            ],
        )(offsets, vectors, inner, tile, *gathered[chunk], *after)
        step = 1
        waited = received = swap(send, "term", step)
        while 2 * step < shares:
            step *= 2
            count = shares // (2 * step)
            keep, send = call(
                halve_kernel,
                "halve_rows",
                1,
                1,
                8 * MIB,
                out_shape=(share_of(count, jnp.float32), share_of(count, jnp.bfloat16)),
                in_specs=[VMEM, VMEM],
                out_specs=(VMEM, VMEM),
            )(keep, received)
            received = swap(send, "term", step)
        parts += [keep, received]

    tiles = jnp.broadcast_to(tile[None], (sectors * shares, *TILE))
    tiles = lax.all_to_all(tiles, ("sec", "term"), 0, 0, tiled=True)
    rayleigh = call(
        rayleigh_kernel,
        "rayleigh",
        1,
        1,
        8 * MIB,
        out_shape=jax.ShapeDtypeStruct((trials, trials), jnp.float32),
        in_specs=[VMEM],
        out_specs=VMEM,
    )(tiles)
    products = call(
        finish_kernel,
        "add_last_share",
        1,
        1,
        8 * MIB,
        out_shape=jax.ShapeDtypeStruct((trials, pairs, rows, states), jnp.bfloat16),
        in_specs=[VMEM] * len(parts),
        out_specs=VMEM,
    )(*parts)
    return (products[:, None], rayleigh)


def solution(mesh):
    in_specs = (
        P(None, "sec", None, None, None),
        P("term", "sec", None, None),
        P("term", "sec", None, None),
        P("term", None),
    )
    out_specs = (P(None, "sec", None, "term", None), P())
    return jax.shard_map(local, mesh=mesh, in_specs=in_specs, out_specs=out_specs, check_vma=False)
```

time: 67.1 us -> 56.7 us (0.85)
  the two profiles are of different devices: /device:TPU:8 before, /device:TPU:0 now
where the time goes in v2:
time: 56.7 us; the launch traced here: 56.4 us
  waiting for transfers between devices  25 us (44%)
  starting transfers between devices  20.5 us (36%)
  Pallas kernels  6.29 us (11%)
  local copies, waits for them, and re-layouts  3.94 us (7%)
  between operations  0.71 us (1%)
    ppermute x18, waiting for transfers between devices, swap(): lax.ppermute(value, axis, [(place, place ^ mask) for place in range(count)])  20.8 us
    ppermute x18, starting transfers between devices, swap(): lax.ppermute(value, axis, [(place, place ^ mask) for place in range(count)])  16 us
    all_to_all x1, starting transfers between devices, local(): tiles = lax.all_to_all(tiles, ('sec', 'term'), 0, 0, tiled=True)  4.43 us
    all_to_all x1, waiting for transfers between devices, local(): tiles = lax.all_to_all(tiles, ('sec', 'term'), 0, 0, tiled=True)  4.24 us
    pallas_call x2, Pallas kernels, local(): call(functools.partial(sum_kernel, sectors, chunk), 'sum_over_terms', 2 *...  3.85 us
    unnamed x8, local copies, waits for them, and re-layouts  2.23 us
  transfers between devices with their start and end apart: 19, of which 9 were waited for; matrix products, arithmetic and copies ran while one was open for 1% of the time, Pallas kernels for 6%

profile of v2, /device:TPU:0, one launch (start us, length us, event | category | flops | bytes accessed | tf_op | source)
XLA Modules:
  0.0 56.4 jit_solution(8302093980367555205)
XLA Ops:
  0.6 1.1 %fusion = (bf16[3,256,128]{2,1,0:T(8,128)(2,1)S(1)}, bf16[3,256,128]{2,1,0:T(8,128)(2,1)S(1)}) fusion(bf16[3,256,256]{2,1,0:T(8,128)(2,1)} %bitcast.10), kind=kLoop, calls=%fused_computation | loop fusion | bytes 786432 | tf_op jit(solution)/shard_map/slice | solution.py:161
  1.7 3.0 %collective-permute-start = (bf16[3,256,128]{2,1,0:T(8,128)(2,1)S(1)}, bf16[3,256,128]{2,1,0:T(8,128)(2,1)S(1)}, u32[]{:S(2)}, u32[]{:S(2)}) collective-permute-start(bf16[3,256,128]{2,1,0:T(8,128)(2,1)S(1)} %get-tuple-element.33.rest_0_), channel_id=1, source_target_pairs={{0,8},{4,12},{8,0},{12,4},{16,24},{20,28},{24,16},{28,20},{1,9},{5... | collective-permute-start | bytes 589832 | tf_op jit(solution)/shard_map/ppermute | solution.py:20
  4.7 1.5 %collective-permute-start.3 = (bf16[3,256,128]{2,1,0:T(8,128)(2,1)S(1)}, bf16[3,256,128]{2,1,0:T(8,128)(2,1)S(1)}, u32[]{:S(2)}, u32[]{:S(2)}) collective-permute-start(bf16[3,256,128]{2,1,0:T(8,128)(2,1)S(1)} %get-tuple-element.33.rest_0_), channel_id=1, source_target_pairs={{0,16},{4,20},{8,24},{12,28},{16,0},{20,4},{24,8},{28,12},{1,17},{... | collective-permute-start | bytes 589832 | tf_op jit(solution)/shard_map/ppermute | solution.py:20
  6.2 1.2 %copy-done = bf16[2,1,4,256,256]{4,3,2,1,0:T(8,128)(2,1)S(1)} copy-done((bf16[2,1,4,256,256]{4,3,2,1,0:T(8,128)(2,1)S(1)}, bf16[2,1,4,256,256]{4,3,2,1,0:T(8,128)(2,1)}, u32[]{:S(2)}) %copy-start) | copy-done | bytes 1048600
  7.5 1.0 %copy-done.3 = bf16[3,1,256,256]{3,2,1,0:T(8,128)(2,1)S(1)} copy-done((bf16[3,1,256,256]{3,2,1,0:T(8,128)(2,1)S(1)}, bf16[3,1,256,256]{3,2,1,0:T(8,128)(2,1)}, u32[]{:S(2)}) %copy-start.3) | copy-done | bytes 393240
  8.5 1.0 %inner_products.1 = (bf16[3,2,4,256,256]{4,3,2,1,0:T(8,128)(2,1)S(1)}, f32[8,128]{1,0:T(8,128)S(1)}) custom-call(bf16[2,4,256,256]{3,2,1,0:T(8,128)(2,1)S(1)} %bitcast.6, bf16[3,256,256]{2,1,0:T(8,128)(2,1)S(1)} %bitcast.9), custom_call_target="tpu_custom_call" | custom-call | flops 805306368 | bytes 5242880 | tf_op jit(solution)/shard_map/inner_products/pallas_call | solution.py:145
  9.5 1.0 %collective-permute-done.rest_2_ = bf16[3,256,128]{2,1,0:T(8,128)(2,1)S(1)} collective-permute-done((bf16[3,256,128]{2,1,0:T(8,128)(2,1)S(1)}, bf16[3,256,128]{2,1,0:T(8,128)(2,1)S(1)}, u32[]{:S(2)}, u32[]{:S(2)}) %collective-permute-start) | collective-permute-done | bytes 196640 | tf_op jit(solution)/shard_map/ppermute | solution.py:20
  10.4 4.8 %collective-permute-done.3.rest_4_ = bf16[3,256,128]{2,1,0:T(8,128)(2,1)S(1)} collective-permute-done((bf16[3,256,128]{2,1,0:T(8,128)(2,1)S(1)}, bf16[3,256,128]{2,1,0:T(8,128)(2,1)S(1)}, u32[]{:S(2)}, u32[]{:S(2)}) %collective-permute-start.3) | collective-permute-done | bytes 196640 | tf_op jit(solution)/shard_map/ppermute | solution.py:20
  16.5 1.3 %collective-permute-start.12 = (bf16[3,256,128]{2,1,0:T(8,128)(2,1)S(1)}, bf16[3,256,128]{2,1,0:T(8,128)(2,1)S(1)}, u32[]{:S(2)}, u32[]{:S(2)}) collective-permute-start(bf16[3,256,128]{2,1,0:T(8,128)(2,1)S(1)} %get-tuple-element.32.rest_0_), channel_id=1, source_target_pairs={{0,16},{4,20},{8,24},{12,28},{16,0},{20,4},{24,8},{28,12},{1,17},{... | collective-permute-start | bytes 589832 | tf_op jit(solution)/shard_map/ppermute | solution.py:20
  17.9 1.4 %collective-permute-start.14 = (bf16[3,256,128]{2,1,0:T(8,128)(2,1)S(1)}, bf16[3,256,128]{2,1,0:T(8,128)(2,1)S(1)}, u32[]{:S(2)}, u32[]{:S(2)}) collective-permute-start(bf16[3,256,128]{2,1,0:T(8,128)(2,1)S(1)} %get-tuple-element.32.rest_0_), channel_id=1, source_target_pairs={{0,24},{4,28},{8,16},{12,20},{16,8},{20,12},{24,0},{28,4},{1,25},{... | collective-permute-start | bytes 589832 | tf_op jit(solution)/shard_map/ppermute | solution.py:20
  19.3 1.9 %sum_over_terms.2 = (f32[2,2,4,64,128]{4,3,2,1,0:T(8,128)S(1)}, bf16[2,2,4,64,128]{4,3,2,1,0:T(8,128)(2,1)S(1)}, f32[8,128]{1,0:T(8,128)S(1)}) custom-call(s32[3,4]{1,0:T(4,128)S(1)} %copy-done.2, bf16[2,4,256,256]{3,2,1,0:T(8,128)(2,1)S(1)} %bitcast.7, bf16[3,2,4,256,256]{4,3,2,1,0:T(8,128)(2,1)S(1)} %get-tuple-element.17.inner, ...), custom_call_target="tpu_custom_call" | custom-call | flops 402653184 | bytes 4194304 | tf_op jit(solution)/shard_map/sum_over_terms/pallas_call | solution.py:176
  21.2 1.6 %collective-permute-start.7 = (bf16[2,2,4,64,128]{4,3,2,1,0:T(8,128)(2,1)S(1)}, bf16[2,2,4,64,128]{4,3,2,1,0:T(8,128)(2,1)S(1)}, u32[]{:S(2)}, u32[]{:S(2)}) collective-permute-start(bf16[2,2,4,64,128]{4,3,2,1,0:T(8,128)(2,1)S(1)} %get-tuple-element.21), channel_id=1, source_target_pairs={{0,1},{1,0},{2,3},{3,2},{4,5},{5,4},{6,7},{7,6},{8,9},{9,8},{10,11... | collective-permute-start | bytes 786440 | tf_op jit(solution)/shard_map/ppermute | solution.py:20
  23.6 2.6 %collective-permute-done.12.rest_4_ = bf16[3,256,128]{2,1,0:T(8,128)(2,1)S(1)} collective-permute-done((bf16[3,256,128]{2,1,0:T(8,128)(2,1)S(1)}, bf16[3,256,128]{2,1,0:T(8,128)(2,1)S(1)}, u32[]{:S(2)}, u32[]{:S(2)}) %collective-permute-start.12) | collective-permute-done | bytes 196640 | tf_op jit(solution)/shard_map/ppermute | solution.py:20
  26.1 1.6 %collective-permute-done.14.rest_6_ = bf16[3,256,128]{2,1,0:T(8,128)(2,1)S(1)} collective-permute-done((bf16[3,256,128]{2,1,0:T(8,128)(2,1)S(1)}, bf16[3,256,128]{2,1,0:T(8,128)(2,1)S(1)}, u32[]{:S(2)}, u32[]{:S(2)}) %collective-permute-start.14) | collective-permute-done | bytes 196640 | tf_op jit(solution)/shard_map/ppermute | solution.py:20
  27.8 1.4 %collective-permute-done.15.rest_7_ = bf16[3,256,128]{2,1,0:T(8,128)(2,1)S(1)} collective-permute-done((bf16[3,256,128]{2,1,0:T(8,128)(2,1)S(1)}, bf16[3,256,128]{2,1,0:T(8,128)(2,1)S(1)}, u32[]{:S(2)}, u32[]{:S(2)}) %collective-permute-start.15) | collective-permute-done | bytes 196640 | tf_op jit(solution)/shard_map/ppermute | solution.py:20
  29.2 1.9 %sum_over_terms.3 = (f32[2,2,4,64,128]{4,3,2,1,0:T(8,128)S(1)}, bf16[2,2,4,64,128]{4,3,2,1,0:T(8,128)(2,1)S(1)}, f32[8,128]{1,0:T(8,128)S(1)}) custom-call(s32[3,4]{1,0:T(4,128)S(1)} %copy-done.2, bf16[2,4,256,256]{3,2,1,0:T(8,128)(2,1)S(1)} %bitcast.8, bf16[3,2,4,256,256]{4,3,2,1,0:T(8,128)(2,1)S(1)} %get-tuple-element.17.inner, ...), custom_call_target="tpu_custom_call" | custom-call | flops 402653184 | bytes 4194304 | tf_op jit(solution)/shard_map/sum_over_terms/pallas_call | solution.py:176
  31.1 1.6 %collective-permute-start.16 = (bf16[2,2,4,64,128]{4,3,2,1,0:T(8,128)(2,1)S(1)}, bf16[2,2,4,64,128]{4,3,2,1,0:T(8,128)(2,1)S(1)}, u32[]{:S(2)}, u32[]{:S(2)}) collective-permute-start(bf16[2,2,4,64,128]{4,3,2,1,0:T(8,128)(2,1)S(1)} %get-tuple-element.26), channel_id=1, source_target_pairs={{0,1},{1,0},{2,3},{3,2},{4,5},{5,4},{6,7},{7,6},{8,9},{9,8},{10,11... | collective-permute-start | bytes 786440 | tf_op jit(solution)/shard_map/ppermute | solution.py:20
  33.4 4.4 %all-to-all-start = ((f32[32,8,128]{2,1,0:T(8,128)}), f32[32,8,128]{2,1,0:T(8,128)S(1)}, u32[]{:S(2)}, u32[]{:S(2)}) async-start(f32[32,8,128]{2,1,0:T(8,128)} %broadcast_in_dim.10), calls=%async_computation | async-start | bytes 262144 | tf_op jit(solution)/shard_map/all_to_all | solution.py:213
  37.9 2.7 %collective-permute-start.8 = (bf16[1,2,4,64,128]{4,3,2,1,0:T(8,128)(2,1)S(1)}, bf16[1,2,4,64,128]{4,3,2,1,0:T(8,128)(2,1)S(1)}, u32[]{:S(2)}, u32[]{:S(2)}) collective-permute-start(bf16[1,2,4,64,128]{4,3,2,1,0:T(8,128)(2,1)S(1)} %get-tuple-element.23), channel_id=1, source_target_pairs={{0,2},{1,3},{2,0},{3,1},{4,6},{5,7},{6,4},{7,5},{8,10},{9,11},{10,... | collective-permute-start | bytes 393224 | tf_op jit(solution)/shard_map/ppermute | solution.py:20
  40.7 1.5 %collective-permute-start.17 = (bf16[1,2,4,64,128]{4,3,2,1,0:T(8,128)(2,1)S(1)}, bf16[1,2,4,64,128]{4,3,2,1,0:T(8,128)(2,1)S(1)}, u32[]{:S(2)}, u32[]{:S(2)}) collective-permute-start(bf16[1,2,4,64,128]{4,3,2,1,0:T(8,128)(2,1)S(1)} %get-tuple-element.28), channel_id=1, source_target_pairs={{0,2},{1,3},{2,0},{3,1},{4,6},{5,7},{6,4},{7,5},{8,10},{9,11},{10,... | collective-permute-start | bytes 393224 | tf_op jit(solution)/shard_map/ppermute | solution.py:20
  42.2 4.2 %all-to-all-done.tiles = f32[32,8,128]{2,1,0:T(8,128)S(1)} async-done(((f32[32,8,128]{2,1,0:T(8,128)}), f32[32,8,128]{2,1,0:T(8,128)S(1)}, u32[]{:S(2)}, u32[]{:S(2)}) %all-to-all-start) | async-done | bytes 131104 | tf_op jit(solution)/shard_map/all_to_all | solution.py:213
  47.1 6.2 %collective-permute-done.8.refs_1_ = bf16[1,2,4,64,128]{4,3,2,1,0:T(8,128)(2,1)S(1)} collective-permute-done((bf16[1,2,4,64,128]{4,3,2,1,0:T(8,128)(2,1)S(1)}, bf16[1,2,4,64,128]{4,3,2,1,0:T(8,128)(2,1)S(1)}, u32[]{:S(2)}, u32[]{:S(2)}) %collective-permute-start.8) | collective-permute-done | bytes 131104 | tf_op jit(solution)/shard_map/ppermute | solution.py:20
  53.3 2.3 %collective-permute-done.17.refs_3_ = bf16[1,2,4,64,128]{4,3,2,1,0:T(8,128)(2,1)S(1)} collective-permute-done((bf16[1,2,4,64,128]{4,3,2,1,0:T(8,128)(2,1)S(1)}, bf16[1,2,4,64,128]{4,3,2,1,0:T(8,128)(2,1)S(1)}, u32[]{:S(2)}, u32[]{:S(2)}) %collective-permute-start.17) | collective-permute-done | bytes 131104 | tf_op jit(solution)/shard_map/ppermute | solution.py:20
  55.7 0.8 %add_last_share.1 = bf16[2,4,64,256]{3,2,1,0:T(8,128)(2,1)} custom-call(f32[1,2,4,64,128]{4,3,2,1,0:T(8,128)S(1)} %get-tuple-element.22.refs_0_, bf16[1,2,4,64,128]{4,3,2,1,0:T(8,128)(2,1)S(1)} %collective-permute-done.8.refs_1_, f32[1,2,4,64,128]{4,3,2,1,0:T(8,128)S(1)} %get-tuple-element.27.refs_2_, ...), custom_call_target="tpu_custom_call" | custom-call | flops 1 | bytes 1 | tf_op jit(solution)/shard_map/add_last_share/pallas_call | solution.py:224
  (31 shorter events, 3.4 us)
Async XLA Ops:
  0.6 18.7 %copy-start.2 = (s32[3,4]{1,0:T(4,128)S(1)}, s32[3,4]{1,0:T(4,128)}, u32[]{:S(2)}) copy-start(s32[3,4]{1,0:T(4,128)} %offsets.3) | copy-start | bytes 148
  1.7 8.7 %collective-permute-start = (bf16[3,256,128]{2,1,0:T(8,128)(2,1)S(1)}, bf16[3,256,128]{2,1,0:T(8,128)(2,1)S(1)}, u32[]{:S(2)}, u32[]{:S(2)}) collective-permute-start(bf16[3,256,128]{2,1,0:T(8,128)(2,1)S(1)} %get-tuple-element.33.rest_0_), channel_id=1, source_target_pairs={{0,8},{4,12},{8,0},{12,4},{16,24},{20,28},{24,16},{28,20},{1,9},{5... | collective-permute-start | bytes 589832 | tf_op jit(solution)/shard_map/ppermute | solution.py:20
  4.7 10.6 %collective-permute-start.3 = (bf16[3,256,128]{2,1,0:T(8,128)(2,1)S(1)}, bf16[3,256,128]{2,1,0:T(8,128)(2,1)S(1)}, u32[]{:S(2)}, u32[]{:S(2)}) collective-permute-start(bf16[3,256,128]{2,1,0:T(8,128)(2,1)S(1)} %get-tuple-element.33.rest_0_), channel_id=1, source_target_pairs={{0,16},{4,20},{8,24},{12,28},{16,0},{20,4},{24,8},{28,12},{1,17},{... | collective-permute-start | bytes 589832 | tf_op jit(solution)/shard_map/ppermute | solution.py:20
  6.2 9.1 %collective-permute-start.5 = (bf16[3,256,128]{2,1,0:T(8,128)(2,1)S(1)}, bf16[3,256,128]{2,1,0:T(8,128)(2,1)S(1)}, u32[]{:S(2)}, u32[]{:S(2)}) collective-permute-start(bf16[3,256,128]{2,1,0:T(8,128)(2,1)S(1)} %get-tuple-element.33.rest_0_), channel_id=1, source_target_pairs={{0,24},{4,28},{8,16},{12,20},{16,8},{20,12},{24,0},{28,4},{1,25},{... | collective-permute-start | bytes 589832 | tf_op jit(solution)/shard_map/ppermute | solution.py:20
  6.2 10.3 %collective-permute-start.1 = (bf16[3,256,128]{2,1,0:T(8,128)(2,1)S(1)}, bf16[3,256,128]{2,1,0:T(8,128)(2,1)S(1)}, u32[]{:S(2)}, u32[]{:S(2)}) collective-permute-start(bf16[3,256,128]{2,1,0:T(8,128)(2,1)S(1)} %get-tuple-element.33.rest_0_), channel_id=1, source_target_pairs={{0,4},{4,0},{8,12},{12,8},{16,20},{20,16},{24,28},{28,24},{1,5},{5... | collective-permute-start | bytes 589832 | tf_op jit(solution)/shard_map/ppermute | solution.py:20
  6.2 1.2 %copy-start = (bf16[2,1,4,256,256]{4,3,2,1,0:T(8,128)(2,1)S(1)}, bf16[2,1,4,256,256]{4,3,2,1,0:T(8,128)(2,1)}, u32[]{:S(2)}) copy-start(bf16[2,1,4,256,256]{4,3,2,1,0:T(8,128)(2,1)} %param.4) | copy-start | bytes 3145732
  7.5 1.0 %copy-start.3 = (bf16[3,1,256,256]{3,2,1,0:T(8,128)(2,1)S(1)}, bf16[3,1,256,256]{3,2,1,0:T(8,128)(2,1)}, u32[]{:S(2)}) copy-start(bf16[3,1,256,256]{3,2,1,0:T(8,128)(2,1)} %param.5) | copy-start | bytes 1179652
  8.5 10.8 %copy-start.1 = (bf16[2,1,4,256,256]{4,3,2,1,0:T(8,128)(2,1)S(1)}, bf16[2,1,4,256,256]{4,3,2,1,0:T(8,128)(2,1)}, u32[]{:S(2)}) copy-start(bf16[2,1,4,256,256]{4,3,2,1,0:T(8,128)(2,1)} %param.4) | copy-start | bytes 3145732
  10.4 7.4 %collective-permute-start.2 = (bf16[3,256,128]{2,1,0:T(8,128)(2,1)S(1)}, bf16[3,256,128]{2,1,0:T(8,128)(2,1)S(1)}, u32[]{:S(2)}, u32[]{:S(2)}) collective-permute-start(bf16[3,256,128]{2,1,0:T(8,128)(2,1)S(1)} %collective-permute-done.rest_2_), channel_id=1, source_target_pairs={{0,4},{4,0},{8,12},{12,8},{16,20},{20,16},{24,28},{28,24},{1,5},{5... | collective-permute-start | bytes 589832 | tf_op jit(solution)/shard_map/ppermute | solution.py:20
  15.3 4.0 %collective-permute-start.4 = (bf16[3,256,128]{2,1,0:T(8,128)(2,1)S(1)}, bf16[3,256,128]{2,1,0:T(8,128)(2,1)S(1)}, u32[]{:S(2)}, u32[]{:S(2)}) collective-permute-start(bf16[3,256,128]{2,1,0:T(8,128)(2,1)S(1)} %collective-permute-done.3.rest_4_), channel_id=1, source_target_pairs={{0,4},{4,0},{8,12},{12,8},{16,20},{20,16},{24,28},{28,24},{1,5},{5... | collective-permute-start | bytes 589832 | tf_op jit(solution)/shard_map/ppermute | solution.py:20
  15.3 4.0 %collective-permute-start.6 = (bf16[3,256,128]{2,1,0:T(8,128)(2,1)S(1)}, bf16[3,256,128]{2,1,0:T(8,128)(2,1)S(1)}, u32[]{:S(2)}, u32[]{:S(2)}) collective-permute-start(bf16[3,256,128]{2,1,0:T(8,128)(2,1)S(1)} %collective-permute-done.5.rest_6_), channel_id=1, source_target_pairs={{0,4},{4,0},{8,12},{12,8},{16,20},{20,16},{24,28},{28,24},{1,5},{5... | collective-permute-start | bytes 589832 | tf_op jit(solution)/shard_map/ppermute | solution.py:20
  15.8 7.8 %collective-permute-start.10 = (bf16[3,256,128]{2,1,0:T(8,128)(2,1)S(1)}, bf16[3,256,128]{2,1,0:T(8,128)(2,1)S(1)}, u32[]{:S(2)}, u32[]{:S(2)}) collective-permute-start(bf16[3,256,128]{2,1,0:T(8,128)(2,1)S(1)} %get-tuple-element.32.rest_0_), channel_id=1, source_target_pairs={{0,8},{4,12},{8,0},{12,4},{16,24},{20,28},{24,16},{28,20},{1,9},{5... | collective-permute-start | bytes 589832 | tf_op jit(solution)/shard_map/ppermute | solution.py:20
  16.5 9.6 %collective-permute-start.12 = (bf16[3,256,128]{2,1,0:T(8,128)(2,1)S(1)}, bf16[3,256,128]{2,1,0:T(8,128)(2,1)S(1)}, u32[]{:S(2)}, u32[]{:S(2)}) collective-permute-start(bf16[3,256,128]{2,1,0:T(8,128)(2,1)S(1)} %get-tuple-element.32.rest_0_), channel_id=1, source_target_pairs={{0,16},{4,20},{8,24},{12,28},{16,0},{20,4},{24,8},{28,12},{1,17},{... | collective-permute-start | bytes 589832 | tf_op jit(solution)/shard_map/ppermute | solution.py:20
  17.9 9.9 %collective-permute-start.14 = (bf16[3,256,128]{2,1,0:T(8,128)(2,1)S(1)}, bf16[3,256,128]{2,1,0:T(8,128)(2,1)S(1)}, u32[]{:S(2)}, u32[]{:S(2)}) collective-permute-start(bf16[3,256,128]{2,1,0:T(8,128)(2,1)S(1)} %get-tuple-element.32.rest_0_), channel_id=1, source_target_pairs={{0,24},{4,28},{8,16},{12,20},{16,8},{20,12},{24,0},{28,4},{1,25},{... | collective-permute-start | bytes 589832 | tf_op jit(solution)/shard_map/ppermute | solution.py:20
  21.2 8.0 %collective-permute-start.7 = (bf16[2,2,4,64,128]{4,3,2,1,0:T(8,128)(2,1)S(1)}, bf16[2,2,4,64,128]{4,3,2,1,0:T(8,128)(2,1)S(1)}, u32[]{:S(2)}, u32[]{:S(2)}) collective-permute-start(bf16[2,2,4,64,128]{4,3,2,1,0:T(8,128)(2,1)S(1)} %get-tuple-element.21), channel_id=1, source_target_pairs={{0,1},{1,0},{2,3},{3,2},{4,5},{5,4},{6,7},{7,6},{8,9},{9,8},{10,11... | collective-permute-start | bytes 786440 | tf_op jit(solution)/shard_map/ppermute | solution.py:20
  22.8 4.9 %collective-permute-start.9 = (bf16[3,256,128]{2,1,0:T(8,128)(2,1)S(1)}, bf16[3,256,128]{2,1,0:T(8,128)(2,1)S(1)}, u32[]{:S(2)}, u32[]{:S(2)}) collective-permute-start(bf16[3,256,128]{2,1,0:T(8,128)(2,1)S(1)} %get-tuple-element.32.rest_0_), channel_id=1, source_target_pairs={{0,4},{4,0},{8,12},{12,8},{16,20},{20,16},{24,28},{28,24},{1,5},{5... | collective-permute-start | bytes 589832 | tf_op jit(solution)/shard_map/ppermute | solution.py:20
  23.6 4.2 %collective-permute-start.11 = (bf16[3,256,128]{2,1,0:T(8,128)(2,1)S(1)}, bf16[3,256,128]{2,1,0:T(8,128)(2,1)S(1)}, u32[]{:S(2)}, u32[]{:S(2)}) collective-permute-start(bf16[3,256,128]{2,1,0:T(8,128)(2,1)S(1)} %collective-permute-done.10.rest_2_), channel_id=1, source_target_pairs={{0,4},{4,0},{8,12},{12,8},{16,20},{20,16},{24,28},{28,24},{1,5},{5... | collective-permute-start | bytes 589832 | tf_op jit(solution)/shard_map/ppermute | solution.py:20
  26.1 1.6 %collective-permute-start.13 = (bf16[3,256,128]{2,1,0:T(8,128)(2,1)S(1)}, bf16[3,256,128]{2,1,0:T(8,128)(2,1)S(1)}, u32[]{:S(2)}, u32[]{:S(2)}) collective-permute-start(bf16[3,256,128]{2,1,0:T(8,128)(2,1)S(1)} %collective-permute-done.12.rest_4_), channel_id=1, source_target_pairs={{0,4},{4,0},{8,12},{12,8},{16,20},{20,16},{24,28},{28,24},{1,5},{5... | collective-permute-start | bytes 589832 | tf_op jit(solution)/shard_map/ppermute | solution.py:20
  27.8 1.4 %collective-permute-start.15 = (bf16[3,256,128]{2,1,0:T(8,128)(2,1)S(1)}, bf16[3,256,128]{2,1,0:T(8,128)(2,1)S(1)}, u32[]{:S(2)}, u32[]{:S(2)}) collective-permute-start(bf16[3,256,128]{2,1,0:T(8,128)(2,1)S(1)} %collective-permute-done.14.rest_6_), channel_id=1, source_target_pairs={{0,4},{4,0},{8,12},{12,8},{16,20},{20,16},{24,28},{28,24},{1,5},{5... | collective-permute-start | bytes 589832 | tf_op jit(solution)/shard_map/ppermute | solution.py:20
  31.1 9.5 %collective-permute-start.16 = (bf16[2,2,4,64,128]{4,3,2,1,0:T(8,128)(2,1)S(1)}, bf16[2,2,4,64,128]{4,3,2,1,0:T(8,128)(2,1)S(1)}, u32[]{:S(2)}, u32[]{:S(2)}) collective-permute-start(bf16[2,2,4,64,128]{4,3,2,1,0:T(8,128)(2,1)S(1)} %get-tuple-element.26), channel_id=1, source_target_pairs={{0,1},{1,0},{2,3},{3,2},{4,5},{5,4},{6,7},{7,6},{8,9},{9,8},{10,11... | collective-permute-start | bytes 786440 | tf_op jit(solution)/shard_map/ppermute | solution.py:20
  33.4 13.1 %all-to-all-start = ((f32[32,8,128]{2,1,0:T(8,128)}), f32[32,8,128]{2,1,0:T(8,128)S(1)}, u32[]{:S(2)}, u32[]{:S(2)}) async-start(f32[32,8,128]{2,1,0:T(8,128)} %broadcast_in_dim.10), calls=%async_computation | async-start | bytes 262144 | tf_op jit(solution)/shard_map/all_to_all | solution.py:213
  37.9 15.4 %collective-permute-start.8 = (bf16[1,2,4,64,128]{4,3,2,1,0:T(8,128)(2,1)S(1)}, bf16[1,2,4,64,128]{4,3,2,1,0:T(8,128)(2,1)S(1)}, u32[]{:S(2)}, u32[]{:S(2)}) collective-permute-start(bf16[1,2,4,64,128]{4,3,2,1,0:T(8,128)(2,1)S(1)} %get-tuple-element.23), channel_id=1, source_target_pairs={{0,2},{1,3},{2,0},{3,1},{4,6},{5,7},{6,4},{7,5},{8,10},{9,11},{10,... | collective-permute-start | bytes 393224 | tf_op jit(solution)/shard_map/ppermute | solution.py:20
  40.7 15.0 %collective-permute-start.17 = (bf16[1,2,4,64,128]{4,3,2,1,0:T(8,128)(2,1)S(1)}, bf16[1,2,4,64,128]{4,3,2,1,0:T(8,128)(2,1)S(1)}, u32[]{:S(2)}, u32[]{:S(2)}) collective-permute-start(bf16[1,2,4,64,128]{4,3,2,1,0:T(8,128)(2,1)S(1)} %get-tuple-element.28), channel_id=1, source_target_pairs={{0,2},{1,3},{2,0},{3,1},{4,6},{5,7},{6,4},{7,5},{8,10},{9,11},{10,... | collective-permute-start | bytes 393224 | tf_op jit(solution)/shard_map/ppermute | solution.py:20

commit v3 on v2

--- a/solution.py
+++ b/solution.py
@@ -12,12 +12,34 @@
 CHUNKS = 2
 VMEM = pl.BlockSpec(memory_space=pltpu.VMEM)
 SMEM = pl.BlockSpec(memory_space=pltpu.SMEM)
-ANY = pl.BlockSpec(memory_space=pl.ANY)
-
-
-def swap(value, axis, mask):
-    count = lax.axis_size(axis)
-    return lax.ppermute(value, axis, [(place, place ^ mask) for place in range(count)])
+HBM = pl.BlockSpec(memory_space=pltpu.HBM)
+
+
+def swap(value, axis, mask, count=None):
+    masks = [mask, mask] if count is None else [turned(mask, parity, count) for parity in range(2)]
+    places = range(lax.axis_size(axis))
+    return lax.ppermute(value, axis, [(place, place ^ masks[place & 1]) for place in places])
+
+
+def turned(mask, parity, count):
+    bits = count.bit_length() - 1
+    if not parity:
+        return mask
+    return sum(1 << (bits - bit) for bit in range(1, bits) if mask >> bit & 1) | mask & 1
+
+
+def gather_sectors(own, sectors, after):
+    held = {0: own}
+    for mask in range(2, sectors, 2):
+        step = 1 << (mask.bit_length() - 1)
+        held[mask] = swap(held[mask ^ step], "sec", step, sectors)
+    blocks = []
+    for mask, block in held.items():
+        sent = block
+        if mask == 2:
+            sent = after(block)
+        blocks += [block, swap(sent, "sec", 1)]
+    return blocks
 
 
 def place_rows(values):
@@ -32,13 +54,26 @@
     return jnp.sum(jnp.sum(value, axis=0, keepdims=True), axis=1, keepdims=True)
 
 
-def inner_kernel(square_scale, vectors, left, inner, squares):
+def inner_kernel(square_scale, vectors_hbm, left_hbm, inner, squares, vectors, left, sems):
     terms, states = left.shape[0], left.shape[1]
+    pairs = vectors.shape[1]
+    fetch_left = pltpu.make_async_copy(left_hbm, left, sems.at[vectors.shape[0] * pairs])
+    fetch_left.start()
+    fetches = []
+    for trial in range(vectors.shape[0]):
+        for pair in range(pairs):
+            fetch = pltpu.make_async_copy(
+                vectors_hbm.at[trial, pair], vectors.at[trial, pair], sems.at[trial * pairs + pair]
+            )
+            fetch.start()
+            fetches.append(fetch)
+    fetch_left.wait()
     stacked = left[...].reshape(terms * states, states)
     sums = []
     for trial in range(vectors.shape[0]):
         square = jnp.zeros((8, states), jnp.float32)
         for pair in range(vectors.shape[1]):
+            fetches[trial * pairs + pair].wait()
             block = vectors[trial, pair]
             product = jnp.dot(stacked, block, preferred_element_type=jnp.float32)
             inner[:, trial, pair] = product.astype(jnp.bfloat16).reshape(terms, states, states)
@@ -51,14 +86,17 @@
 
 def sum_kernel(sectors, chunk, offsets, vectors, inner, before, *rest):
     pieces = rest[:sectors]
-    keep, send, tile, rights, partial = rest[-5:]
+    keep, send, tile, rights, partial = rest[sectors:]
     terms, trials, pairs, states, _ = inner.shape
     width = partial.shape[2]
     shares = 2 * keep.shape[0]
     rows = states // shares
-    for mask in range(sectors):
-        rights[mask] = pieces[mask][...]
     sector = lax.axis_index("sec")
+    odd = sector & 1
+    for mask in range(0, sectors, 2):
+        even_place, odd_place = turned(mask, 0, sectors), turned(mask, 1, sectors)
+        rights[jnp.where(odd == 1, odd_place, even_place)] = pieces[mask][...]
+        rights[jnp.where(odd == 1, even_place, odd_place) ^ 1] = pieces[mask + 1][...]
     place = lax.axis_index("term")
     columns = slice(chunk * width, (chunk + 1) * width)
     grams = [jnp.zeros((8, width), jnp.float32) for _ in range(trials * trials)]
@@ -106,8 +144,9 @@
         products[:, :, :, chunk * width : (chunk + 1) * width] = both.astype(jnp.bfloat16)
 
 
-def rayleigh_kernel(tiles, rayleigh):
-    tile = jnp.sum(tiles[...], axis=0)
+def rayleigh_kernel(*refs):
+    *tiles, rayleigh = refs
+    tile = sum(part[...] for part in tiles)
     trials = rayleigh.shape[0]
     row = lax.broadcasted_iota(jnp.int32, rayleigh.shape, 0)
     column = lax.broadcasted_iota(jnp.int32, rayleigh.shape, 1)
@@ -122,6 +161,19 @@
             value = entry(i * trials + j) / jnp.sqrt(squares)
             result = jnp.where((row == i) & (column == j), value, result)
     rayleigh[...] = result
+
+
+def in_hbm(value):
+    return pltpu.with_memory_space_constraint(value, pltpu.HBM)
+
+
+def add_places(tile, axis):
+    step, other = 1, None
+    while step < lax.axis_size(axis):
+        tile = tile if other is None else tile + other
+        other = swap(tile, axis, step)
+        step *= 2
+    return tile, other
 
 
 def call(kernel, name, flops, moved, limit, **kwargs):
@@ -152,27 +204,29 @@
             jax.ShapeDtypeStruct((terms, trials, pairs, states, states), jnp.bfloat16),
             jax.ShapeDtypeStruct(TILE, jnp.float32),
         ),
-        in_specs=[VMEM, VMEM],
+        in_specs=[HBM, HBM],
         out_specs=(VMEM, VMEM),
-    )(vectors, left)
+        scratch_shapes=[
+            pltpu.VMEM(vectors.shape, jnp.bfloat16),
+            pltpu.VMEM(left.shape, jnp.bfloat16),
+            pltpu.SemaphoreType.DMA((trials * pairs + 1,)),
+        ],
+    )(in_hbm(vectors), in_hbm(left))
+
+    def behind_inner(block):
+        return lax.optimization_barrier((block, inner))[0]
 
     gathered = []
     for chunk in range(CHUNKS):
         own = right[:, :, chunk * width : (chunk + 1) * width]
-        held = [own] + [swap(own, "sec", mask) for mask in range(2, sectors, 2)]
-        if chunk == 0:
-            held[1], inner = lax.optimization_barrier((held[1], inner))
-        both = []
-        for block in held:
-            both += [block, swap(block, "sec", 1)]
-        gathered.append(both)
+        after = behind_inner if chunk == 0 else lambda block: block
+        gathered.append(gather_sectors(own, sectors, after))
 
     def share_of(count, dtype):
         return jax.ShapeDtypeStruct((count, trials, pairs, rows, width), dtype)
 
-    parts, waited = [], None
+    parts, arrived = [], None
     for chunk in range(CHUNKS):
-        after = [] if waited is None else [waited]
         keep, send, tile = call(
             functools.partial(sum_kernel, sectors, chunk),
             "sum_over_terms",
@@ -184,15 +238,21 @@
                 share_of(shares // 2, jnp.bfloat16),
                 jax.ShapeDtypeStruct(TILE, jnp.float32),
             ),
-            in_specs=[SMEM, VMEM, VMEM, VMEM] + [VMEM] * sectors + [ANY] * len(after),
+            in_specs=[SMEM, VMEM, VMEM, VMEM] + [VMEM] * sectors,
             out_specs=(VMEM, VMEM, VMEM),
             scratch_shapes=[
                 pltpu.VMEM((sectors, terms, states, width), jnp.bfloat16),
                 pltpu.VMEM((trials, states, width), jnp.float32),
             ],
-        )(offsets, vectors, inner, tile, *gathered[chunk], *after)
+        )(offsets, vectors, inner, tile, *gathered[chunk])
+        if arrived is not None:
+            send, arrived = lax.optimization_barrier((send, arrived))
         step = 1
-        waited = received = swap(send, "term", step)
+        arrived = received = swap(send, "term", step)
+        if chunk == CHUNKS - 1:
+            tile, other = add_places(tile, "sec")
+            tile = tile + other
+            received, tile = lax.optimization_barrier((received, tile))
         while 2 * step < shares:
             step *= 2
             count = shares // (2 * step)
@@ -209,8 +269,7 @@
             received = swap(send, "term", step)
         parts += [keep, received]
 
-    tiles = jnp.broadcast_to(tile[None], (sectors * shares, *TILE))
-    tiles = lax.all_to_all(tiles, ("sec", "term"), 0, 0, tiled=True)
+    tiles = add_places(tile, "term")
     rayleigh = call(
         rayleigh_kernel,
         "rayleigh",
@@ -218,9 +277,9 @@
         1,
         8 * MIB,
         out_shape=jax.ShapeDtypeStruct((trials, trials), jnp.float32),
-        in_specs=[VMEM],
+        in_specs=[VMEM] * len(tiles),
         out_specs=VMEM,
-    )(tiles)
+    )(*tiles)
     products = call(
         finish_kernel,
         "add_last_share",

time: 56.7 us -> 55.3 us (0.975)
  waiting for transfers between devices: 25 us -> 21 us
  Pallas kernels: 6.29 us -> 9.2 us
  local copies, waits for them, and re-layouts: 3.94 us -> 1.15 us
  starting transfers between devices: 20.5 us -> 23 us
    ppermute x18 -> x23, starting transfers between devices: 16 us -> 23 us  [swap(): lax.ppermute(value, axis, [(place, place ^ masks[place & 1]) for place in...]
    all_to_all x1 -> x0, starting transfers between devices: 4.43 us -> none  [local(): tiles = lax.all_to_all(tiles, ('sec', 'term'), 0, 0, tiled=True)]
    all_to_all x1 -> x0, waiting for transfers between devices: 4.24 us -> none  [local(): tiles = lax.all_to_all(tiles, ('sec', 'term'), 0, 0, tiled=True)]
    pallas_call x1, Pallas kernels: 0.98 us -> 3.93 us  [local(): call(functools.partial(inner_kernel, 1.0 / shares), 'inner_products', 2 *...]
    unnamed x8 -> x4, local copies, waits for them, and re-layouts: 2.23 us -> 0.01 us
    broadcast_in_dim x1 -> x0, local copies, waits for them, and re-layouts: 0.66 us -> none  [local(): tiles = jnp.broadcast_to(tile[None], (sectors * shares, *TILE))]
    ppermute x18 -> x23, waiting for transfers between devices: 20.8 us -> 21 us  [swap(): lax.ppermute(value, axis, [(place, place ^ masks[place & 1]) for place in...]
  transfers between devices with their start and end apart: 19 -> 23, of which waited for: 9 -> 11; matrix products, arithmetic and copies ran while one was open for 1% -> 0% of each run, Pallas kernels for 6% -> 15%
where the time goes in v3:
time: 55.3 us; the launch traced here: 55.1 us
  starting transfers between devices  23 us (42%)
  waiting for transfers between devices  21 us (38%)
  Pallas kernels  9.2 us (17%)
  local copies, waits for them, and re-layouts  1.15 us (2%)
  between operations  0.73 us (1%)
    ppermute x23, starting transfers between devices, swap(): lax.ppermute(value, axis, [(place, place ^ masks[place & 1]) for place in...  23 us
    ppermute x23, waiting for transfers between devices, swap(): lax.ppermute(value, axis, [(place, place ^ masks[place & 1]) for place in...  21 us
    pallas_call x1, Pallas kernels, local(): call(functools.partial(inner_kernel, 1.0 / shares), 'inner_products', 2 *...  3.93 us
    pallas_call x2, Pallas kernels, local(): call(functools.partial(sum_kernel, sectors, chunk), 'sum_over_terms', 2 *...  3.81 us
    slice x1, local copies, waits for them, and re-layouts, local(): own = right[:, :, chunk * width:(chunk + 1) * width]  1.13 us
  transfers between devices with their start and end apart: 23, of which 11 were waited for; matrix products, arithmetic and copies ran while one was open for 0% of the time, Pallas kernels for 15%

profile of v3, /device:TPU:0, one launch (start us, length us, event | category | flops | bytes accessed | tf_op | source)
XLA Modules:
  0.0 55.1 jit_solution(5244761235180409037)
XLA Ops:
  0.7 1.1 %fusion = (bf16[3,256,128]{2,1,0:T(8,128)(2,1)S(1)}, bf16[3,256,128]{2,1,0:T(8,128)(2,1)S(1)}) fusion(bf16[3,256,256]{2,1,0:T(8,128)(2,1)} %bitcast.9), kind=kLoop, calls=%fused_computation | loop fusion | bytes 786432 | tf_op jit(solution)/shard_map/slice | solution.py:221
  1.8 3.0 %collective-permute-start.1 = (bf16[3,256,128]{2,1,0:T(8,128)(2,1)S(1)}, bf16[3,256,128]{2,1,0:T(8,128)(2,1)S(1)}, u32[]{:S(2)}, u32[]{:S(2)}) collective-permute-start(bf16[3,256,128]{2,1,0:T(8,128)(2,1)S(1)} %get-tuple-element.37.rest_0_), channel_id=1, source_target_pairs={{0,8},{4,20},{8,0},{12,28},{16,24},{20,4},{24,16},{28,12},{1,9},{5... | collective-permute-start | bytes 589832 | tf_op jit(solution)/shard_map/ppermute | solution.py:21
  4.8 1.5 %collective-permute-start.3 = (bf16[3,256,128]{2,1,0:T(8,128)(2,1)S(1)}, bf16[3,256,128]{2,1,0:T(8,128)(2,1)S(1)}, u32[]{:S(2)}, u32[]{:S(2)}) collective-permute-start(bf16[3,256,128]{2,1,0:T(8,128)(2,1)S(1)} %get-tuple-element.37.rest_0_), channel_id=1, source_target_pairs={{0,16},{4,12},{8,24},{12,4},{16,0},{20,28},{24,8},{28,20},{1,17},{... | collective-permute-start | bytes 589832 | tf_op jit(solution)/shard_map/ppermute | solution.py:21
  6.3 3.7 %collective-permute-done.1.rest_2_ = bf16[3,256,128]{2,1,0:T(8,128)(2,1)S(1)} collective-permute-done((bf16[3,256,128]{2,1,0:T(8,128)(2,1)S(1)}, bf16[3,256,128]{2,1,0:T(8,128)(2,1)S(1)}, u32[]{:S(2)}, u32[]{:S(2)}) %collective-permute-start.1) | collective-permute-done | bytes 196640 | tf_op jit(solution)/shard_map/ppermute | solution.py:21
  10.0 1.6 %collective-permute-start.5 = (bf16[3,256,128]{2,1,0:T(8,128)(2,1)S(1)}, bf16[3,256,128]{2,1,0:T(8,128)(2,1)S(1)}, u32[]{:S(2)}, u32[]{:S(2)}) collective-permute-start(bf16[3,256,128]{2,1,0:T(8,128)(2,1)S(1)} %collective-permute-done.1.rest_2_), channel_id=1, source_target_pairs={{0,16},{4,12},{8,24},{12,4},{16,0},{20,28},{24,8},{28,20},{1,17},{... | collective-permute-start | bytes 589832 | tf_op jit(solution)/shard_map/ppermute | solution.py:21
  11.5 1.6 %collective-permute-start.10 = (bf16[3,256,128]{2,1,0:T(8,128)(2,1)S(1)}, bf16[3,256,128]{2,1,0:T(8,128)(2,1)S(1)}, u32[]{:S(2)}, u32[]{:S(2)}) collective-permute-start(bf16[3,256,128]{2,1,0:T(8,128)(2,1)S(1)} %get-tuple-element.36.rest_0_), channel_id=1, source_target_pairs={{0,8},{4,20},{8,0},{12,28},{16,24},{20,4},{24,16},{28,12},{1,9},{5... | collective-permute-start | bytes 589832 | tf_op jit(solution)/shard_map/ppermute | solution.py:21
  13.2 3.9 %inner_products.1 = (bf16[3,2,4,256,256]{4,3,2,1,0:T(8,128)(2,1)S(1)}, f32[8,128]{1,0:T(8,128)S(1)}) custom-call(bf16[2,4,256,256]{3,2,1,0:T(8,128)(2,1)} %bitcast.6, bf16[3,256,256]{2,1,0:T(8,128)(2,1)} %bitcast.11), custom_call_target="tpu_custom_call" | custom-call | flops 805306368 | bytes 5242880 | tf_op jit(solution)/shard_map/inner_products/pallas_call | solution.py:197
  17.8 1.5 %collective-permute-start.12 = (bf16[3,256,128]{2,1,0:T(8,128)(2,1)S(1)}, bf16[3,256,128]{2,1,0:T(8,128)(2,1)S(1)}, u32[]{:S(2)}, u32[]{:S(2)}) collective-permute-start(bf16[3,256,128]{2,1,0:T(8,128)(2,1)S(1)} %get-tuple-element.36.rest_0_), channel_id=1, source_target_pairs={{0,16},{4,12},{8,24},{12,4},{16,0},{20,28},{24,8},{28,20},{1,17},{... | collective-permute-start | bytes 589832 | tf_op jit(solution)/shard_map/ppermute | solution.py:21
  19.9 1.9 %sum_over_terms.2 = (f32[2,2,4,64,128]{4,3,2,1,0:T(8,128)S(1)}, bf16[2,2,4,64,128]{4,3,2,1,0:T(8,128)(2,1)S(1)}, f32[8,128]{1,0:T(8,128)S(1)}) custom-call(s32[3,4]{1,0:T(4,128)S(1)} %copy-done.1, bf16[2,4,256,256]{3,2,1,0:T(8,128)(2,1)S(1)} %bitcast.7, bf16[3,2,4,256,256]{4,3,2,1,0:T(8,128)(2,1)S(1)} %get-tuple-element.18.inner, ...), custom_call_target="tpu_custom_call" | custom-call | flops 402653184 | bytes 4194304 | tf_op jit(solution)/shard_map/sum_over_terms/pallas_call | solution.py:230
  21.8 2.3 %collective-permute-start.7 = (bf16[2,2,4,64,128]{4,3,2,1,0:T(8,128)(2,1)S(1)}, bf16[2,2,4,64,128]{4,3,2,1,0:T(8,128)(2,1)S(1)}, u32[]{:S(2)}, u32[]{:S(2)}) collective-permute-start(bf16[2,2,4,64,128]{4,3,2,1,0:T(8,128)(2,1)S(1)} %get-tuple-element.22), channel_id=1, source_target_pairs={{0,1},{1,0},{2,3},{3,2},{4,5},{5,4},{6,7},{7,6},{8,9},{9,8},{10,11... | collective-permute-start | bytes 786440 | tf_op jit(solution)/shard_map/ppermute | solution.py:21
  24.6 1.0 %collective-permute-done.14.rest_6_ = bf16[3,256,128]{2,1,0:T(8,128)(2,1)S(1)} collective-permute-done((bf16[3,256,128]{2,1,0:T(8,128)(2,1)S(1)}, bf16[3,256,128]{2,1,0:T(8,128)(2,1)S(1)}, u32[]{:S(2)}, u32[]{:S(2)}) %collective-permute-start.14) | collective-permute-done | bytes 196640 | tf_op jit(solution)/shard_map/ppermute | solution.py:21
  26.1 0.9 %collective-permute-done.15.rest_7_ = bf16[3,256,128]{2,1,0:T(8,128)(2,1)S(1)} collective-permute-done((bf16[3,256,128]{2,1,0:T(8,128)(2,1)S(1)}, bf16[3,256,128]{2,1,0:T(8,128)(2,1)S(1)}, u32[]{:S(2)}, u32[]{:S(2)}) %collective-permute-start.15) | collective-permute-done | bytes 196640 | tf_op jit(solution)/shard_map/ppermute | solution.py:21
  27.0 1.9 %sum_over_terms.3 = (f32[2,2,4,64,128]{4,3,2,1,0:T(8,128)S(1)}, bf16[2,2,4,64,128]{4,3,2,1,0:T(8,128)(2,1)S(1)}, f32[8,128]{1,0:T(8,128)S(1)}) custom-call(s32[3,4]{1,0:T(4,128)S(1)} %copy-done.1, bf16[2,4,256,256]{3,2,1,0:T(8,128)(2,1)S(1)} %bitcast.8, bf16[3,2,4,256,256]{4,3,2,1,0:T(8,128)(2,1)S(1)} %get-tuple-element.18.inner, ...), custom_call_target="tpu_custom_call" | custom-call | flops 402653184 | bytes 4194304 | tf_op jit(solution)/shard_map/sum_over_terms/pallas_call | solution.py:230
  28.9 1.6 %collective-permute-done.7.received = bf16[2,2,4,64,128]{4,3,2,1,0:T(8,128)(2,1)S(1)} collective-permute-done((bf16[2,2,4,64,128]{4,3,2,1,0:T(8,128)(2,1)S(1)}, bf16[2,2,4,64,128]{4,3,2,1,0:T(8,128)(2,1)S(1)}, u32[]{:S(2)}, u32[]{:S(2)}) %collective-permute-start.7) | collective-permute-done | bytes 262176 | tf_op jit(solution)/shard_map/ppermute | solution.py:21
  30.5 1.7 %collective-permute-start.16 = (bf16[2,2,4,64,128]{4,3,2,1,0:T(8,128)(2,1)S(1)}, bf16[2,2,4,64,128]{4,3,2,1,0:T(8,128)(2,1)S(1)}, u32[]{:S(2)}, u32[]{:S(2)}) collective-permute-start(bf16[2,2,4,64,128]{4,3,2,1,0:T(8,128)(2,1)S(1)} %get-tuple-element.28), channel_id=1, source_target_pairs={{0,1},{1,0},{2,3},{3,2},{4,5},{5,4},{6,7},{7,6},{8,9},{9,8},{10,11... | collective-permute-start | bytes 786440 | tf_op jit(solution)/shard_map/ppermute | solution.py:21
  32.2 1.2 %collective-permute-done.17 = f32[8,128]{1,0:T(8,128)S(1)} collective-permute-done((f32[8,128]{1,0:T(8,128)S(1)}, f32[8,128]{1,0:T(8,128)S(1)}, u32[]{:S(2)}, u32[]{:S(2)}) %collective-permute-start.17) | collective-permute-done | bytes 4128 | tf_op jit(solution)/shard_map/ppermute | solution.py:21
  33.4 1.5 %collective-permute-start.18 = (f32[8,128]{1,0:T(8,128)S(1)}, f32[8,128]{1,0:T(8,128)S(1)}, u32[]{:S(2)}, u32[]{:S(2)}) collective-permute-start(f32[8,128]{1,0:T(8,128)S(1)} %add.12), channel_id=1, source_target_pairs={{0,8},{4,12},{8,0},{12,4},{16,24},{20,28},{24,16},{28,20},{1,9},{5... | collective-permute-start | bytes 12296 | tf_op jit(solution)/shard_map/ppermute | solution.py:21
  34.9 2.1 %collective-permute-done.18 = f32[8,128]{1,0:T(8,128)S(1)} collective-permute-done((f32[8,128]{1,0:T(8,128)S(1)}, f32[8,128]{1,0:T(8,128)S(1)}, u32[]{:S(2)}, u32[]{:S(2)}) %collective-permute-start.18) | collective-permute-done | bytes 4128 | tf_op jit(solution)/shard_map/ppermute | solution.py:21
  37.5 3.1 %collective-permute-done.19 = f32[8,128]{1,0:T(8,128)S(1)} collective-permute-done((f32[8,128]{1,0:T(8,128)S(1)}, f32[8,128]{1,0:T(8,128)S(1)}, u32[]{:S(2)}, u32[]{:S(2)}) %collective-permute-start.19) | collective-permute-done | bytes 4128 | tf_op jit(solution)/shard_map/ppermute | solution.py:21
  40.7 2.7 %collective-permute-start.8 = (bf16[1,2,4,64,128]{4,3,2,1,0:T(8,128)(2,1)S(1)}, bf16[1,2,4,64,128]{4,3,2,1,0:T(8,128)(2,1)S(1)}, u32[]{:S(2)}, u32[]{:S(2)}) collective-permute-start(bf16[1,2,4,64,128]{4,3,2,1,0:T(8,128)(2,1)S(1)} %get-tuple-element.24), channel_id=1, source_target_pairs={{0,2},{1,3},{2,0},{3,1},{4,6},{5,7},{6,4},{7,5},{8,10},{9,11},{10,... | collective-permute-start | bytes 393224 | tf_op jit(solution)/shard_map/ppermute | solution.py:21
  44.1 3.3 %collective-permute-done.21 = f32[8,128]{1,0:T(8,128)S(1)} collective-permute-done((f32[8,128]{1,0:T(8,128)S(1)}, f32[8,128]{1,0:T(8,128)S(1)}, u32[]{:S(2)}, u32[]{:S(2)}) %collective-permute-start.21) | collective-permute-done | bytes 4128 | tf_op jit(solution)/shard_map/ppermute | solution.py:21
  47.4 2.6 %collective-permute-start.22 = (f32[8,128]{1,0:T(8,128)S(1)}, f32[8,128]{1,0:T(8,128)S(1)}, u32[]{:S(2)}, u32[]{:S(2)}) collective-permute-start(f32[8,128]{1,0:T(8,128)S(1)} %add.15.refs_0_), channel_id=1, source_target_pairs={{0,2},{1,3},{2,0},{3,1},{4,6},{5,7},{6,4},{7,5},{8,10},{9,11},{10,... | collective-permute-start | bytes 12296 | tf_op jit(solution)/shard_map/ppermute | solution.py:21
  50.0 3.8 %collective-permute-done.22.refs_1_ = f32[8,128]{1,0:T(8,128)S(1)} collective-permute-done((f32[8,128]{1,0:T(8,128)S(1)}, f32[8,128]{1,0:T(8,128)S(1)}, u32[]{:S(2)}, u32[]{:S(2)}) %collective-permute-start.22) | collective-permute-done | bytes 4128 | tf_op jit(solution)/shard_map/ppermute | solution.py:21
  54.4 0.8 %add_last_share.1 = bf16[2,4,64,256]{3,2,1,0:T(8,128)(2,1)} custom-call(f32[1,2,4,64,128]{4,3,2,1,0:T(8,128)S(1)} %get-tuple-element.23.refs_0_, bf16[1,2,4,64,128]{4,3,2,1,0:T(8,128)(2,1)S(1)} %collective-permute-done.8.refs_1_, f32[1,2,4,64,128]{4,3,2,1,0:T(8,128)S(1)} %get-tuple-element.31.refs_2_, ...), custom_call_target="tpu_custom_call" | custom-call | flops 1 | bytes 1 | tf_op jit(solution)/shard_map/add_last_share/pallas_call | solution.py:283
  (38 shorter events, 4.1 us)
Async XLA Ops:
  0.6 19.2 %copy-start = (bf16[2,1,4,256,256]{4,3,2,1,0:T(8,128)(2,1)S(1)}, bf16[2,1,4,256,256]{4,3,2,1,0:T(8,128)(2,1)}, u32[]{:S(2)}) copy-start(bf16[2,1,4,256,256]{4,3,2,1,0:T(8,128)(2,1)} %param.4) | copy-start | bytes 3145732
  1.8 8.2 %collective-permute-start.1 = (bf16[3,256,128]{2,1,0:T(8,128)(2,1)S(1)}, bf16[3,256,128]{2,1,0:T(8,128)(2,1)S(1)}, u32[]{:S(2)}, u32[]{:S(2)}) collective-permute-start(bf16[3,256,128]{2,1,0:T(8,128)(2,1)S(1)} %get-tuple-element.37.rest_0_), channel_id=1, source_target_pairs={{0,8},{4,20},{8,0},{12,28},{16,24},{20,4},{24,16},{28,12},{1,9},{5... | collective-permute-start | bytes 589832 | tf_op jit(solution)/shard_map/ppermute | solution.py:21
  4.8 12.4 %collective-permute-start.3 = (bf16[3,256,128]{2,1,0:T(8,128)(2,1)S(1)}, bf16[3,256,128]{2,1,0:T(8,128)(2,1)S(1)}, u32[]{:S(2)}, u32[]{:S(2)}) collective-permute-start(bf16[3,256,128]{2,1,0:T(8,128)(2,1)S(1)} %get-tuple-element.37.rest_0_), channel_id=1, source_target_pairs={{0,16},{4,12},{8,24},{12,4},{16,0},{20,28},{24,8},{28,20},{1,17},{... | collective-permute-start | bytes 589832 | tf_op jit(solution)/shard_map/ppermute | solution.py:21
  10.0 7.7 %collective-permute-start.5 = (bf16[3,256,128]{2,1,0:T(8,128)(2,1)S(1)}, bf16[3,256,128]{2,1,0:T(8,128)(2,1)S(1)}, u32[]{:S(2)}, u32[]{:S(2)}) collective-permute-start(bf16[3,256,128]{2,1,0:T(8,128)(2,1)S(1)} %collective-permute-done.1.rest_2_), channel_id=1, source_target_pairs={{0,16},{4,12},{8,24},{12,4},{16,0},{20,28},{24,8},{28,20},{1,17},{... | collective-permute-start | bytes 589832 | tf_op jit(solution)/shard_map/ppermute | solution.py:21
  11.5 6.3 %collective-permute-start = (bf16[3,256,128]{2,1,0:T(8,128)(2,1)S(1)}, bf16[3,256,128]{2,1,0:T(8,128)(2,1)S(1)}, u32[]{:S(2)}, u32[]{:S(2)}) collective-permute-start(bf16[3,256,128]{2,1,0:T(8,128)(2,1)S(1)} %get-tuple-element.37.rest_0_), channel_id=1, source_target_pairs={{0,4},{4,0},{8,12},{12,8},{16,20},{20,16},{24,28},{28,24},{1,5},{5... | collective-permute-start | bytes 589832 | tf_op jit(solution)/shard_map/ppermute | solution.py:21
  11.5 7.8 %collective-permute-start.10 = (bf16[3,256,128]{2,1,0:T(8,128)(2,1)S(1)}, bf16[3,256,128]{2,1,0:T(8,128)(2,1)S(1)}, u32[]{:S(2)}, u32[]{:S(2)}) collective-permute-start(bf16[3,256,128]{2,1,0:T(8,128)(2,1)S(1)} %get-tuple-element.36.rest_0_), channel_id=1, source_target_pairs={{0,8},{4,20},{8,0},{12,28},{16,24},{20,4},{24,16},{28,12},{1,9},{5... | collective-permute-start | bytes 589832 | tf_op jit(solution)/shard_map/ppermute | solution.py:21
  17.1 2.7 %collective-permute-start.2 = (bf16[3,256,128]{2,1,0:T(8,128)(2,1)S(1)}, bf16[3,256,128]{2,1,0:T(8,128)(2,1)S(1)}, u32[]{:S(2)}, u32[]{:S(2)}) collective-permute-start(bf16[3,256,128]{2,1,0:T(8,128)(2,1)S(1)} %collective-permute-done.1.rest_2_), channel_id=1, source_target_pairs={{0,4},{4,0},{8,12},{12,8},{16,20},{20,16},{24,28},{28,24},{1,5},{5... | collective-permute-start | bytes 589832 | tf_op jit(solution)/shard_map/ppermute | solution.py:21
  17.2 2.6 %collective-permute-start.4 = (bf16[3,256,128]{2,1,0:T(8,128)(2,1)S(1)}, bf16[3,256,128]{2,1,0:T(8,128)(2,1)S(1)}, u32[]{:S(2)}, u32[]{:S(2)}) collective-permute-start(bf16[3,256,128]{2,1,0:T(8,128)(2,1)S(1)} %collective-permute-done.3.rest_4_), channel_id=1, source_target_pairs={{0,4},{4,0},{8,12},{12,8},{16,20},{20,16},{24,28},{28,24},{1,5},{5... | collective-permute-start | bytes 589832 | tf_op jit(solution)/shard_map/ppermute | solution.py:21
  17.7 2.1 %collective-permute-start.6 = (bf16[3,256,128]{2,1,0:T(8,128)(2,1)S(1)}, bf16[3,256,128]{2,1,0:T(8,128)(2,1)S(1)}, u32[]{:S(2)}, u32[]{:S(2)}) collective-permute-start(bf16[3,256,128]{2,1,0:T(8,128)(2,1)S(1)} %collective-permute-done.5.rest_6_), channel_id=1, source_target_pairs={{0,4},{4,0},{8,12},{12,8},{16,20},{20,16},{24,28},{28,24},{1,5},{5... | collective-permute-start | bytes 589832 | tf_op jit(solution)/shard_map/ppermute | solution.py:21
  17.8 6.8 %collective-permute-start.12 = (bf16[3,256,128]{2,1,0:T(8,128)(2,1)S(1)}, bf16[3,256,128]{2,1,0:T(8,128)(2,1)S(1)}, u32[]{:S(2)}, u32[]{:S(2)}) collective-permute-start(bf16[3,256,128]{2,1,0:T(8,128)(2,1)S(1)} %get-tuple-element.36.rest_0_), channel_id=1, source_target_pairs={{0,16},{4,12},{8,24},{12,4},{16,0},{20,28},{24,8},{28,20},{1,17},{... | collective-permute-start | bytes 589832 | tf_op jit(solution)/shard_map/ppermute | solution.py:21
  19.3 6.3 %collective-permute-start.14 = (bf16[3,256,128]{2,1,0:T(8,128)(2,1)S(1)}, bf16[3,256,128]{2,1,0:T(8,128)(2,1)S(1)}, u32[]{:S(2)}, u32[]{:S(2)}) collective-permute-start(bf16[3,256,128]{2,1,0:T(8,128)(2,1)S(1)} %collective-permute-done.10.rest_2_), channel_id=1, source_target_pairs={{0,16},{4,12},{8,24},{12,4},{16,0},{20,28},{24,8},{28,20},{1,17},{... | collective-permute-start | bytes 589832 | tf_op jit(solution)/shard_map/ppermute | solution.py:21
  21.8 8.7 %collective-permute-start.7 = (bf16[2,2,4,64,128]{4,3,2,1,0:T(8,128)(2,1)S(1)}, bf16[2,2,4,64,128]{4,3,2,1,0:T(8,128)(2,1)S(1)}, u32[]{:S(2)}, u32[]{:S(2)}) collective-permute-start(bf16[2,2,4,64,128]{4,3,2,1,0:T(8,128)(2,1)S(1)} %get-tuple-element.22), channel_id=1, source_target_pairs={{0,1},{1,0},{2,3},{3,2},{4,5},{5,4},{6,7},{7,6},{8,9},{9,8},{10,11... | collective-permute-start | bytes 786440 | tf_op jit(solution)/shard_map/ppermute | solution.py:21
  24.1 1.6 %collective-permute-start.9 = (bf16[3,256,128]{2,1,0:T(8,128)(2,1)S(1)}, bf16[3,256,128]{2,1,0:T(8,128)(2,1)S(1)}, u32[]{:S(2)}, u32[]{:S(2)}) collective-permute-start(bf16[3,256,128]{2,1,0:T(8,128)(2,1)S(1)} %get-tuple-element.36.rest_0_), channel_id=1, source_target_pairs={{0,4},{4,0},{8,12},{12,8},{16,20},{20,16},{24,28},{28,24},{1,5},{5... | collective-permute-start | bytes 589832 | tf_op jit(solution)/shard_map/ppermute | solution.py:21
  24.1 1.7 %collective-permute-start.11 = (bf16[3,256,128]{2,1,0:T(8,128)(2,1)S(1)}, bf16[3,256,128]{2,1,0:T(8,128)(2,1)S(1)}, u32[]{:S(2)}, u32[]{:S(2)}) collective-permute-start(bf16[3,256,128]{2,1,0:T(8,128)(2,1)S(1)} %collective-permute-done.10.rest_2_), channel_id=1, source_target_pairs={{0,4},{4,0},{8,12},{12,8},{16,20},{20,16},{24,28},{28,24},{1,5},{5... | collective-permute-start | bytes 589832 | tf_op jit(solution)/shard_map/ppermute | solution.py:21
  24.6 1.5 %collective-permute-start.13 = (bf16[3,256,128]{2,1,0:T(8,128)(2,1)S(1)}, bf16[3,256,128]{2,1,0:T(8,128)(2,1)S(1)}, u32[]{:S(2)}, u32[]{:S(2)}) collective-permute-start(bf16[3,256,128]{2,1,0:T(8,128)(2,1)S(1)} %collective-permute-done.12.rest_4_), channel_id=1, source_target_pairs={{0,4},{4,0},{8,12},{12,8},{16,20},{20,16},{24,28},{28,24},{1,5},{5... | collective-permute-start | bytes 589832 | tf_op jit(solution)/shard_map/ppermute | solution.py:21
  25.6 1.4 %collective-permute-start.15 = (bf16[3,256,128]{2,1,0:T(8,128)(2,1)S(1)}, bf16[3,256,128]{2,1,0:T(8,128)(2,1)S(1)}, u32[]{:S(2)}, u32[]{:S(2)}) collective-permute-start(bf16[3,256,128]{2,1,0:T(8,128)(2,1)S(1)} %collective-permute-done.14.rest_6_), channel_id=1, source_target_pairs={{0,4},{4,0},{8,12},{12,8},{16,20},{20,16},{24,28},{28,24},{1,5},{5... | collective-permute-start | bytes 589832 | tf_op jit(solution)/shard_map/ppermute | solution.py:21
  30.5 12.9 %collective-permute-start.16 = (bf16[2,2,4,64,128]{4,3,2,1,0:T(8,128)(2,1)S(1)}, bf16[2,2,4,64,128]{4,3,2,1,0:T(8,128)(2,1)S(1)}, u32[]{:S(2)}, u32[]{:S(2)}) collective-permute-start(bf16[2,2,4,64,128]{4,3,2,1,0:T(8,128)(2,1)S(1)} %get-tuple-element.28), channel_id=1, source_target_pairs={{0,1},{1,0},{2,3},{3,2},{4,5},{5,4},{6,7},{7,6},{8,9},{9,8},{10,11... | collective-permute-start | bytes 786440 | tf_op jit(solution)/shard_map/ppermute | solution.py:21
  32.2 1.2 %collective-permute-start.17 = (f32[8,128]{1,0:T(8,128)S(1)}, f32[8,128]{1,0:T(8,128)S(1)}, u32[]{:S(2)}, u32[]{:S(2)}) collective-permute-start(f32[8,128]{1,0:T(8,128)S(1)} %get-tuple-element.29), channel_id=1, source_target_pairs={{0,4},{4,0},{8,12},{12,8},{16,20},{20,16},{24,28},{28,24},{1,5},{5... | collective-permute-start | bytes 12296 | tf_op jit(solution)/shard_map/ppermute | solution.py:21
  33.4 3.6 %collective-permute-start.18 = (f32[8,128]{1,0:T(8,128)S(1)}, f32[8,128]{1,0:T(8,128)S(1)}, u32[]{:S(2)}, u32[]{:S(2)}) collective-permute-start(f32[8,128]{1,0:T(8,128)S(1)} %add.12), channel_id=1, source_target_pairs={{0,8},{4,12},{8,0},{12,4},{16,24},{20,28},{24,16},{28,20},{1,9},{5... | collective-permute-start | bytes 12296 | tf_op jit(solution)/shard_map/ppermute | solution.py:21
  37.0 3.6 %collective-permute-start.19 = (f32[8,128]{1,0:T(8,128)S(1)}, f32[8,128]{1,0:T(8,128)S(1)}, u32[]{:S(2)}, u32[]{:S(2)}) collective-permute-start(f32[8,128]{1,0:T(8,128)S(1)} %add.13), channel_id=1, source_target_pairs={{0,16},{4,20},{8,24},{12,28},{16,0},{20,4},{24,8},{28,12},{1,17},{... | collective-permute-start | bytes 12296 | tf_op jit(solution)/shard_map/ppermute | solution.py:21
  40.7 13.7 %collective-permute-start.8 = (bf16[1,2,4,64,128]{4,3,2,1,0:T(8,128)(2,1)S(1)}, bf16[1,2,4,64,128]{4,3,2,1,0:T(8,128)(2,1)S(1)}, u32[]{:S(2)}, u32[]{:S(2)}) collective-permute-start(bf16[1,2,4,64,128]{4,3,2,1,0:T(8,128)(2,1)S(1)} %get-tuple-element.24), channel_id=1, source_target_pairs={{0,2},{1,3},{2,0},{3,1},{4,6},{5,7},{6,4},{7,5},{8,10},{9,11},{10,... | collective-permute-start | bytes 393224 | tf_op jit(solution)/shard_map/ppermute | solution.py:21
  43.4 11.0 %collective-permute-start.20 = (bf16[1,2,4,64,128]{4,3,2,1,0:T(8,128)(2,1)S(1)}, bf16[1,2,4,64,128]{4,3,2,1,0:T(8,128)(2,1)S(1)}, u32[]{:S(2)}, u32[]{:S(2)}) collective-permute-start(bf16[1,2,4,64,128]{4,3,2,1,0:T(8,128)(2,1)S(1)} %get-tuple-element.32), channel_id=1, source_target_pairs={{0,2},{1,3},{2,0},{3,1},{4,6},{5,7},{6,4},{7,5},{8,10},{9,11},{10,... | collective-permute-start | bytes 393224 | tf_op jit(solution)/shard_map/ppermute | solution.py:21
  43.8 3.6 %collective-permute-start.21 = (f32[8,128]{1,0:T(8,128)S(1)}, f32[8,128]{1,0:T(8,128)S(1)}, u32[]{:S(2)}, u32[]{:S(2)}) collective-permute-start(f32[8,128]{1,0:T(8,128)S(1)} %add.14), channel_id=1, source_target_pairs={{0,1},{1,0},{2,3},{3,2},{4,5},{5,4},{6,7},{7,6},{8,9},{9,8},{10,11... | collective-permute-start | bytes 12296 | tf_op jit(solution)/shard_map/ppermute | solution.py:21
  47.4 6.4 %collective-permute-start.22 = (f32[8,128]{1,0:T(8,128)S(1)}, f32[8,128]{1,0:T(8,128)S(1)}, u32[]{:S(2)}, u32[]{:S(2)}) collective-permute-start(f32[8,128]{1,0:T(8,128)S(1)} %add.15.refs_0_), channel_id=1, source_target_pairs={{0,2},{1,3},{2,0},{3,1},{4,6},{5,7},{6,4},{7,5},{8,10},{9,11},{10,... | collective-permute-start | bytes 12296 | tf_op jit(solution)/shard_map/ppermute | solution.py:21
  (1 other events, 19.2 us)

commit v4 on v3

--- a/solution.py
+++ b/solution.py
@@ -33,13 +33,9 @@
     for mask in range(2, sectors, 2):
         step = 1 << (mask.bit_length() - 1)
         held[mask] = swap(held[mask ^ step], "sec", step, sectors)
-    blocks = []
-    for mask, block in held.items():
-        sent = block
         if mask == 2:
-            sent = after(block)
-        blocks += [block, swap(sent, "sec", 1)]
-    return blocks
+            held[mask] = after(held[mask])
+    return [block for mine in held.values() for block in (mine, swap(mine, "sec", 1))]
 
 
 def place_rows(values):
@@ -54,26 +50,26 @@
     return jnp.sum(jnp.sum(value, axis=0, keepdims=True), axis=1, keepdims=True)
 
 
-def inner_kernel(square_scale, vectors_hbm, left_hbm, inner, squares, vectors, left, sems):
+def split_kernel(right, *rest):
+    *chunks, sems = rest
+    width = chunks[0].shape[2]
+    copies = []
+    for place, chunk in enumerate(chunks):
+        columns = pl.ds(place * width, width)
+        copies.append(pltpu.make_async_copy(right.at[:, :, columns], chunk, sems.at[place]))
+    for copy in copies:
+        copy.start()
+    for copy in copies:
+        copy.wait()
+
+
+def inner_kernel(square_scale, vectors, left, inner, squares):
     terms, states = left.shape[0], left.shape[1]
-    pairs = vectors.shape[1]
-    fetch_left = pltpu.make_async_copy(left_hbm, left, sems.at[vectors.shape[0] * pairs])
-    fetch_left.start()
-    fetches = []
-    for trial in range(vectors.shape[0]):
-        for pair in range(pairs):
-            fetch = pltpu.make_async_copy(
-                vectors_hbm.at[trial, pair], vectors.at[trial, pair], sems.at[trial * pairs + pair]
-            )
-            fetch.start()
-            fetches.append(fetch)
-    fetch_left.wait()
     stacked = left[...].reshape(terms * states, states)
     sums = []
     for trial in range(vectors.shape[0]):
         square = jnp.zeros((8, states), jnp.float32)
         for pair in range(vectors.shape[1]):
-            fetches[trial * pairs + pair].wait()
             block = vectors[trial, pair]
             product = jnp.dot(stacked, block, preferred_element_type=jnp.float32)
             inner[:, trial, pair] = product.astype(jnp.bfloat16).reshape(terms, states, states)
@@ -167,13 +163,18 @@
     return pltpu.with_memory_space_constraint(value, pltpu.HBM)
 
 
-def add_places(tile, axis):
-    step, other = 1, None
-    while step < lax.axis_size(axis):
-        tile = tile if other is None else tile + other
-        other = swap(tile, axis, step)
-        step *= 2
-    return tile, other
+def add_places(tile, axis, masks):
+    parts = [tile] + [swap(tile, axis, mask) for mask in masks]
+    return sum(parts[1:], parts[0])
+
+
+def steps_of(count, low):
+    steps = []
+    while 1 << low < count:
+        unit = 1 << low
+        steps.append([unit, 2 * unit, 3 * unit] if 2 * unit < count else [unit])
+        low += 2
+    return steps
 
 
 def call(kernel, name, flops, moved, limit, **kwargs):
@@ -193,6 +194,18 @@
     terms = left_ops.shape[0]
     vectors, left, right = vectors[:, 0], left_ops[:, 0], right_ops[:, 0]
     width, rows = states // CHUNKS, states // shares
+
+    chunks = call(
+        split_kernel,
+        "split_columns",
+        2 * terms * trials * pairs * states**3,
+        2 * MIB,
+        4 * MIB,
+        out_shape=[jax.ShapeDtypeStruct((terms, states, width), jnp.bfloat16)] * CHUNKS,
+        in_specs=[HBM],
+        out_specs=[VMEM] * CHUNKS,
+        scratch_shapes=[pltpu.SemaphoreType.DMA((CHUNKS,))],
+    )(in_hbm(right))
 
     inner, tile = call(
         functools.partial(inner_kernel, 1.0 / shares),
@@ -204,23 +217,17 @@
             jax.ShapeDtypeStruct((terms, trials, pairs, states, states), jnp.bfloat16),
             jax.ShapeDtypeStruct(TILE, jnp.float32),
         ),
-        in_specs=[HBM, HBM],
+        in_specs=[VMEM, VMEM],
         out_specs=(VMEM, VMEM),
-        scratch_shapes=[
-            pltpu.VMEM(vectors.shape, jnp.bfloat16),
-            pltpu.VMEM(left.shape, jnp.bfloat16),
-            pltpu.SemaphoreType.DMA((trials * pairs + 1,)),
-        ],
-    )(in_hbm(vectors), in_hbm(left))
+    )(vectors, left)
 
     def behind_inner(block):
         return lax.optimization_barrier((block, inner))[0]
 
     gathered = []
     for chunk in range(CHUNKS):
-        own = right[:, :, chunk * width : (chunk + 1) * width]
         after = behind_inner if chunk == 0 else lambda block: block
-        gathered.append(gather_sectors(own, sectors, after))
+        gathered.append(gather_sectors(chunks[chunk], sectors, after))
 
     def share_of(count, dtype):
         return jax.ShapeDtypeStruct((count, trials, pairs, rows, width), dtype)
@@ -250,9 +257,11 @@
         step = 1
         arrived = received = swap(send, "term", step)
         if chunk == CHUNKS - 1:
-            tile, other = add_places(tile, "sec")
-            tile = tile + other
-            received, tile = lax.optimization_barrier((received, tile))
+            for masks in [[1]] + steps_of(sectors, 1):
+                tile = add_places(tile, "sec", masks)
+            others = tuple(parts[1::2])
+            received, tile, others = lax.optimization_barrier((received, tile, others))
+            parts[1::2] = others
         while 2 * step < shares:
             step *= 2
             count = shares // (2 * step)
@@ -269,7 +278,10 @@
             received = swap(send, "term", step)
         parts += [keep, received]
 
-    tiles = add_places(tile, "term")
+    *steps, last = steps_of(shares, 0)
+    for masks in steps:
+        tile = add_places(tile, "term", masks)
+    tiles = [tile] + [swap(tile, "term", mask) for mask in last]
     rayleigh = call(
         rayleigh_kernel,
         "rayleigh",

time: 55.3 us -> 55.7 us (level)
  starting transfers between devices: 23 us -> 27.8 us
  waiting for transfers between devices: 21 us -> 17.4 us
  Pallas kernels: 9.2 us -> 7.38 us
  local copies, waits for them, and re-layouts: 1.15 us -> 2.23 us
    ppermute x23 -> x25, starting transfers between devices: 23 us -> 27.8 us  [swap(): lax.ppermute(value, axis, [(place, place ^ masks[place & 1]) for place in...]
    ppermute x23 -> x25, waiting for transfers between devices: 21 us -> 17.4 us  [swap(): lax.ppermute(value, axis, [(place, place ^ masks[place & 1]) for place in...]
    pallas_call x1, Pallas kernels: 3.93 us -> 0.99 us  [local(): call(functools.partial(inner_kernel, 1.0 / shares), 'inner_products', 2 *...]
    unnamed x4 -> x8, local copies, waits for them, and re-layouts: 0.01 us -> 2.23 us
    slice x1 -> x0, local copies, waits for them, and re-layouts: 1.13 us -> none  [local(): own = right[:, :, chunk * width:(chunk + 1) * width]]
    pallas_call x0 -> x1, Pallas kernels: none -> 1.12 us  [local(): call(split_kernel, 'split_columns', 2 * terms * trials * pairs * states *...]
  transfers between devices with their start and end apart: 23 -> 25, of which waited for: 11 -> 13; matrix products, arithmetic and copies ran while one was open for 0% -> 0% of each run, Pallas kernels for 15% -> 10%
where the time goes in v4:
time: 55.7 us; the launch traced here: 55.4 us
  starting transfers between devices  27.8 us (50%)
  waiting for transfers between devices  17.4 us (31%)
  Pallas kernels  7.38 us (13%)
  local copies, waits for them, and re-layouts  2.23 us (4%)
  between operations  0.72 us (1%)
    ppermute x25, starting transfers between devices, swap(): lax.ppermute(value, axis, [(place, place ^ masks[place & 1]) for place in...  27.8 us
    ppermute x25, waiting for transfers between devices, swap(): lax.ppermute(value, axis, [(place, place ^ masks[place & 1]) for place in...  17.4 us
    pallas_call x2, Pallas kernels, local(): call(functools.partial(sum_kernel, sectors, chunk), 'sum_over_terms', 2 *...  3.81 us
    unnamed x8, local copies, waits for them, and re-layouts  2.23 us
    pallas_call x1, Pallas kernels, local(): call(split_kernel, 'split_columns', 2 * terms * trials * pairs * states *...  1.12 us
  transfers between devices with their start and end apart: 25, of which 13 were waited for; matrix products, arithmetic and copies ran while one was open for 0% of the time, Pallas kernels for 10%

profile of v4, /device:TPU:0, one launch (start us, length us, event | category | flops | bytes accessed | tf_op | source)
XLA Modules:
  0.0 55.4 jit_solution(15622685815561978261)
XLA Ops:
  0.7 1.1 %split_columns.1 = (bf16[3,256,128]{2,1,0:T(8,128)(2,1)S(1)}, bf16[3,256,128]{2,1,0:T(8,128)(2,1)S(1)}) custom-call(bf16[3,256,256]{2,1,0:T(8,128)(2,1)} %bitcast.11), custom_call_target="tpu_custom_call" | custom-call | flops 805306368 | bytes 2097152 | tf_op jit(solution)/shard_map/split_columns/pallas_call | solution.py:198
  1.8 3.0 %collective-permute-start.1 = (bf16[3,256,128]{2,1,0:T(8,128)(2,1)S(1)}, bf16[3,256,128]{2,1,0:T(8,128)(2,1)S(1)}, u32[]{:S(2)}, u32[]{:S(2)}) collective-permute-start(bf16[3,256,128]{2,1,0:T(8,128)(2,1)S(1)} %get-tuple-element.23.rest_0_), channel_id=1, source_target_pairs={{0,8},{4,20},{8,0},{12,28},{16,24},{20,4},{24,16},{28,12},{1,9},{5... | collective-permute-start | bytes 589832 | tf_op jit(solution)/shard_map/ppermute | solution.py:21
  4.8 1.5 %collective-permute-start.3 = (bf16[3,256,128]{2,1,0:T(8,128)(2,1)S(1)}, bf16[3,256,128]{2,1,0:T(8,128)(2,1)S(1)}, u32[]{:S(2)}, u32[]{:S(2)}) collective-permute-start(bf16[3,256,128]{2,1,0:T(8,128)(2,1)S(1)} %get-tuple-element.23.rest_0_), channel_id=1, source_target_pairs={{0,16},{4,12},{8,24},{12,4},{16,0},{20,28},{24,8},{28,20},{1,17},{... | collective-permute-start | bytes 589832 | tf_op jit(solution)/shard_map/ppermute | solution.py:21
  6.3 1.2 %copy-done = bf16[2,1,4,256,256]{4,3,2,1,0:T(8,128)(2,1)S(1)} copy-done((bf16[2,1,4,256,256]{4,3,2,1,0:T(8,128)(2,1)S(1)}, bf16[2,1,4,256,256]{4,3,2,1,0:T(8,128)(2,1)}, u32[]{:S(2)}) %copy-start) | copy-done | bytes 1048600
  7.5 1.0 %copy-done.3 = bf16[3,1,256,256]{3,2,1,0:T(8,128)(2,1)S(1)} copy-done((bf16[3,1,256,256]{3,2,1,0:T(8,128)(2,1)S(1)}, bf16[3,1,256,256]{3,2,1,0:T(8,128)(2,1)}, u32[]{:S(2)}) %copy-start.3) | copy-done | bytes 393240
  8.5 1.0 %inner_products.1 = (bf16[3,2,4,256,256]{4,3,2,1,0:T(8,128)(2,1)S(1)}, f32[8,128]{1,0:T(8,128)S(1)}) custom-call(bf16[2,4,256,256]{3,2,1,0:T(8,128)(2,1)S(1)} %bitcast.6, bf16[3,256,256]{2,1,0:T(8,128)(2,1)S(1)} %bitcast.9), custom_call_target="tpu_custom_call" | custom-call | flops 805306368 | bytes 5242880 | tf_op jit(solution)/shard_map/inner_products/pallas_call | solution.py:210
  10.0 1.6 %collective-permute-start.5 = (bf16[3,256,128]{2,1,0:T(8,128)(2,1)S(1)}, bf16[3,256,128]{2,1,0:T(8,128)(2,1)S(1)}, u32[]{:S(2)}, u32[]{:S(2)}) collective-permute-start(bf16[3,256,128]{2,1,0:T(8,128)(2,1)S(1)} %collective-permute-done.1.rest_2_), channel_id=1, source_target_pairs={{0,16},{4,12},{8,24},{12,4},{16,0},{20,28},{24,8},{28,20},{1,17},{... | collective-permute-start | bytes 589832 | tf_op jit(solution)/shard_map/ppermute | solution.py:21
  11.5 1.6 %collective-permute-start.9 = (bf16[3,256,128]{2,1,0:T(8,128)(2,1)S(1)}, bf16[3,256,128]{2,1,0:T(8,128)(2,1)S(1)}, u32[]{:S(2)}, u32[]{:S(2)}) collective-permute-start(bf16[3,256,128]{2,1,0:T(8,128)(2,1)S(1)} %get-tuple-element.29.rest_0_), channel_id=1, source_target_pairs={{0,8},{4,20},{8,0},{12,28},{16,24},{20,4},{24,16},{28,12},{1,9},{5... | collective-permute-start | bytes 589832 | tf_op jit(solution)/shard_map/ppermute | solution.py:21
  13.7 3.1 %collective-permute-done.5.rest_6_ = bf16[3,256,128]{2,1,0:T(8,128)(2,1)S(1)} collective-permute-done((bf16[3,256,128]{2,1,0:T(8,128)(2,1)S(1)}, bf16[3,256,128]{2,1,0:T(8,128)(2,1)S(1)}, u32[]{:S(2)}, u32[]{:S(2)}) %collective-permute-start.5) | collective-permute-done | bytes 196640 | tf_op jit(solution)/shard_map/ppermute | solution.py:21
  16.8 2.5 %collective-permute-start.11 = (bf16[3,256,128]{2,1,0:T(8,128)(2,1)S(1)}, bf16[3,256,128]{2,1,0:T(8,128)(2,1)S(1)}, u32[]{:S(2)}, u32[]{:S(2)}) collective-permute-start(bf16[3,256,128]{2,1,0:T(8,128)(2,1)S(1)} %get-tuple-element.29.rest_0_), channel_id=1, source_target_pairs={{0,16},{4,12},{8,24},{12,4},{16,0},{20,28},{24,8},{28,20},{1,17},{... | collective-permute-start | bytes 589832 | tf_op jit(solution)/shard_map/ppermute | solution.py:21
  19.4 1.9 %sum_over_terms.2 = (f32[2,2,4,64,128]{4,3,2,1,0:T(8,128)S(1)}, bf16[2,2,4,64,128]{4,3,2,1,0:T(8,128)(2,1)S(1)}, f32[8,128]{1,0:T(8,128)S(1)}) custom-call(s32[3,4]{1,0:T(4,128)S(1)} %copy-done.2, bf16[2,4,256,256]{3,2,1,0:T(8,128)(2,1)S(1)} %bitcast.7, bf16[3,2,4,256,256]{4,3,2,1,0:T(8,128)(2,1)S(1)} %get-tuple-element.21.inner, ...), custom_call_target="tpu_custom_call" | custom-call | flops 402653184 | bytes 4194304 | tf_op jit(solution)/shard_map/sum_over_terms/pallas_call | solution.py:237
  21.3 2.7 %collective-permute-start.7 = (bf16[2,2,4,64,128]{4,3,2,1,0:T(8,128)(2,1)S(1)}, bf16[2,2,4,64,128]{4,3,2,1,0:T(8,128)(2,1)S(1)}, u32[]{:S(2)}, u32[]{:S(2)}) collective-permute-start(bf16[2,2,4,64,128]{4,3,2,1,0:T(8,128)(2,1)S(1)} %get-tuple-element.26), channel_id=1, source_target_pairs={{0,1},{1,0},{2,3},{3,2},{4,5},{5,4},{6,7},{7,6},{8,9},{9,8},{10,11... | collective-permute-start | bytes 786440 | tf_op jit(solution)/shard_map/ppermute | solution.py:21
  26.5 1.9 %sum_over_terms.3 = (f32[2,2,4,64,128]{4,3,2,1,0:T(8,128)S(1)}, bf16[2,2,4,64,128]{4,3,2,1,0:T(8,128)(2,1)S(1)}, f32[8,128]{1,0:T(8,128)S(1)}) custom-call(s32[3,4]{1,0:T(4,128)S(1)} %copy-done.2, bf16[2,4,256,256]{3,2,1,0:T(8,128)(2,1)S(1)} %bitcast.8, bf16[3,2,4,256,256]{4,3,2,1,0:T(8,128)(2,1)S(1)} %get-tuple-element.21.inner, ...), custom_call_target="tpu_custom_call" | custom-call | flops 402653184 | bytes 4194304 | tf_op jit(solution)/shard_map/sum_over_terms/pallas_call | solution.py:237
  28.4 2.1 %collective-permute-done.7.received = bf16[2,2,4,64,128]{4,3,2,1,0:T(8,128)(2,1)S(1)} collective-permute-done((bf16[2,2,4,64,128]{4,3,2,1,0:T(8,128)(2,1)S(1)}, bf16[2,2,4,64,128]{4,3,2,1,0:T(8,128)(2,1)S(1)}, u32[]{:S(2)}, u32[]{:S(2)}) %collective-permute-start.7) | collective-permute-done | bytes 262176 | tf_op jit(solution)/shard_map/ppermute | solution.py:21
  30.5 1.7 %collective-permute-start.15 = (bf16[2,2,4,64,128]{4,3,2,1,0:T(8,128)(2,1)S(1)}, bf16[2,2,4,64,128]{4,3,2,1,0:T(8,128)(2,1)S(1)}, u32[]{:S(2)}, u32[]{:S(2)}) collective-permute-start(bf16[2,2,4,64,128]{4,3,2,1,0:T(8,128)(2,1)S(1)} %get-tuple-element.31), channel_id=1, source_target_pairs={{0,1},{1,0},{2,3},{3,2},{4,5},{5,4},{6,7},{7,6},{8,9},{9,8},{10,11... | collective-permute-start | bytes 786440 | tf_op jit(solution)/shard_map/ppermute | solution.py:21
  32.2 1.2 %collective-permute-done.16 = f32[8,128]{1,0:T(8,128)S(1)} collective-permute-done((f32[8,128]{1,0:T(8,128)S(1)}, f32[8,128]{1,0:T(8,128)S(1)}, u32[]{:S(2)}, u32[]{:S(2)}) %collective-permute-start.16) | collective-permute-done | bytes 4128 | tf_op jit(solution)/shard_map/ppermute | solution.py:21
  33.4 1.1 %collective-permute-start.19 = (f32[8,128]{1,0:T(8,128)S(1)}, f32[8,128]{1,0:T(8,128)S(1)}, u32[]{:S(2)}, u32[]{:S(2)}) collective-permute-start(f32[8,128]{1,0:T(8,128)S(1)} %add.12), channel_id=1, source_target_pairs={{0,24},{4,28},{8,16},{12,20},{16,8},{20,12},{24,0},{28,4},{1,25},{... | collective-permute-start | bytes 12296 | tf_op jit(solution)/shard_map/ppermute | solution.py:21
  34.5 1.9 %collective-permute-start.18 = (f32[8,128]{1,0:T(8,128)S(1)}, f32[8,128]{1,0:T(8,128)S(1)}, u32[]{:S(2)}, u32[]{:S(2)}) collective-permute-start(f32[8,128]{1,0:T(8,128)S(1)} %add.12), channel_id=1, source_target_pairs={{0,16},{4,20},{8,24},{12,28},{16,0},{20,4},{24,8},{28,12},{1,17},{... | collective-permute-start | bytes 12296 | tf_op jit(solution)/shard_map/ppermute | solution.py:21
  36.9 2.7 %collective-permute-start.20 = (bf16[1,2,4,64,128]{4,3,2,1,0:T(8,128)(2,1)S(1)}, bf16[1,2,4,64,128]{4,3,2,1,0:T(8,128)(2,1)S(1)}, u32[]{:S(2)}, u32[]{:S(2)}) collective-permute-start(bf16[1,2,4,64,128]{4,3,2,1,0:T(8,128)(2,1)S(1)} %get-tuple-element.33), channel_id=1, source_target_pairs={{0,2},{1,3},{2,0},{3,1},{4,6},{5,7},{6,4},{7,5},{8,10},{9,11},{10,... | collective-permute-start | bytes 393224 | tf_op jit(solution)/shard_map/ppermute | solution.py:21
  40.0 5.4 %collective-permute-done.20.refs_1_ = bf16[1,2,4,64,128]{4,3,2,1,0:T(8,128)(2,1)S(1)} collective-permute-done((bf16[1,2,4,64,128]{4,3,2,1,0:T(8,128)(2,1)S(1)}, bf16[1,2,4,64,128]{4,3,2,1,0:T(8,128)(2,1)S(1)}, u32[]{:S(2)}, u32[]{:S(2)}) %collective-permute-start.20) | collective-permute-done | bytes 131104 | tf_op jit(solution)/shard_map/ppermute | solution.py:21
  45.6 3.0 %collective-permute-start.22 = (f32[8,128]{1,0:T(8,128)S(1)}, f32[8,128]{1,0:T(8,128)S(1)}, u32[]{:S(2)}, u32[]{:S(2)}) collective-permute-start(f32[8,128]{1,0:T(8,128)S(1)} %add_add_fusion.refs_0_), channel_id=1, source_target_pairs={{0,1},{1,0},{2,3},{3,2},{4,5},{5,4},{6,7},{7,6},{8,9},{9,8},{10,11... | collective-permute-start | bytes 12296 | tf_op jit(solution)/shard_map/ppermute | solution.py:21
  48.7 2.3 %collective-permute-start.24 = (f32[8,128]{1,0:T(8,128)S(1)}, f32[8,128]{1,0:T(8,128)S(1)}, u32[]{:S(2)}, u32[]{:S(2)}) collective-permute-start(f32[8,128]{1,0:T(8,128)S(1)} %add_add_fusion.refs_0_), channel_id=1, source_target_pairs={{0,3},{1,2},{2,1},{3,0},{4,7},{5,6},{6,5},{7,4},{8,11},{9,10},{10,... | collective-permute-start | bytes 12296 | tf_op jit(solution)/shard_map/ppermute | solution.py:21
  51.0 2.7 %collective-permute-done.23.refs_2_ = f32[8,128]{1,0:T(8,128)S(1)} collective-permute-done((f32[8,128]{1,0:T(8,128)S(1)}, f32[8,128]{1,0:T(8,128)S(1)}, u32[]{:S(2)}, u32[]{:S(2)}) %collective-permute-start.23) | collective-permute-done | bytes 4128 | tf_op jit(solution)/shard_map/ppermute | solution.py:21
  54.7 0.8 %add_last_share.1 = bf16[2,4,64,256]{3,2,1,0:T(8,128)(2,1)} custom-call(f32[1,2,4,64,128]{4,3,2,1,0:T(8,128)S(1)} %get-tuple-element.27.refs_0_, bf16[1,2,4,64,128]{4,3,2,1,0:T(8,128)(2,1)S(1)} %collective-permute-done.20.refs_1_, f32[1,2,4,64,128]{4,3,2,1,0:T(8,128)S(1)} %get-tuple-element.37.refs_2_, ...), custom_call_target="tpu_custom_call" | custom-call | flops 1 | bytes 1 | tf_op jit(solution)/shard_map/add_last_share/pallas_call | solution.py:295
  (44 shorter events, 5.7 us)
Async XLA Ops:
  1.8 8.2 %collective-permute-start.1 = (bf16[3,256,128]{2,1,0:T(8,128)(2,1)S(1)}, bf16[3,256,128]{2,1,0:T(8,128)(2,1)S(1)}, u32[]{:S(2)}, u32[]{:S(2)}) collective-permute-start(bf16[3,256,128]{2,1,0:T(8,128)(2,1)S(1)} %get-tuple-element.23.rest_0_), channel_id=1, source_target_pairs={{0,8},{4,20},{8,0},{12,28},{16,24},{20,4},{24,16},{28,12},{1,9},{5... | collective-permute-start | bytes 589832 | tf_op jit(solution)/shard_map/ppermute | solution.py:21
  4.8 8.4 %collective-permute-start.3 = (bf16[3,256,128]{2,1,0:T(8,128)(2,1)S(1)}, bf16[3,256,128]{2,1,0:T(8,128)(2,1)S(1)}, u32[]{:S(2)}, u32[]{:S(2)}) collective-permute-start(bf16[3,256,128]{2,1,0:T(8,128)(2,1)S(1)} %get-tuple-element.23.rest_0_), channel_id=1, source_target_pairs={{0,16},{4,12},{8,24},{12,4},{16,0},{20,28},{24,8},{28,20},{1,17},{... | collective-permute-start | bytes 589832 | tf_op jit(solution)/shard_map/ppermute | solution.py:21
  10.0 6.9 %collective-permute-start.5 = (bf16[3,256,128]{2,1,0:T(8,128)(2,1)S(1)}, bf16[3,256,128]{2,1,0:T(8,128)(2,1)S(1)}, u32[]{:S(2)}, u32[]{:S(2)}) collective-permute-start(bf16[3,256,128]{2,1,0:T(8,128)(2,1)S(1)} %collective-permute-done.1.rest_2_), channel_id=1, source_target_pairs={{0,16},{4,12},{8,24},{12,4},{16,0},{20,28},{24,8},{28,20},{1,17},{... | collective-permute-start | bytes 589832 | tf_op jit(solution)/shard_map/ppermute | solution.py:21
  11.5 5.3 %collective-permute-start = (bf16[3,256,128]{2,1,0:T(8,128)(2,1)S(1)}, bf16[3,256,128]{2,1,0:T(8,128)(2,1)S(1)}, u32[]{:S(2)}, u32[]{:S(2)}) collective-permute-start(bf16[3,256,128]{2,1,0:T(8,128)(2,1)S(1)} %get-tuple-element.23.rest_0_), channel_id=1, source_target_pairs={{0,4},{4,0},{8,12},{12,8},{16,20},{20,16},{24,28},{28,24},{1,5},{5... | collective-permute-start | bytes 589832 | tf_op jit(solution)/shard_map/ppermute | solution.py:21
  11.5 7.8 %collective-permute-start.9 = (bf16[3,256,128]{2,1,0:T(8,128)(2,1)S(1)}, bf16[3,256,128]{2,1,0:T(8,128)(2,1)S(1)}, u32[]{:S(2)}, u32[]{:S(2)}) collective-permute-start(bf16[3,256,128]{2,1,0:T(8,128)(2,1)S(1)} %get-tuple-element.29.rest_0_), channel_id=1, source_target_pairs={{0,8},{4,20},{8,0},{12,28},{16,24},{20,4},{24,16},{28,12},{1,9},{5... | collective-permute-start | bytes 589832 | tf_op jit(solution)/shard_map/ppermute | solution.py:21
  13.2 6.2 %collective-permute-start.2 = (bf16[3,256,128]{2,1,0:T(8,128)(2,1)S(1)}, bf16[3,256,128]{2,1,0:T(8,128)(2,1)S(1)}, u32[]{:S(2)}, u32[]{:S(2)}) collective-permute-start(bf16[3,256,128]{2,1,0:T(8,128)(2,1)S(1)} %collective-permute-done.1.rest_2_), channel_id=1, source_target_pairs={{0,4},{4,0},{8,12},{12,8},{16,20},{20,16},{24,28},{28,24},{1,5},{5... | collective-permute-start | bytes 589832 | tf_op jit(solution)/shard_map/ppermute | solution.py:21
  13.2 6.2 %collective-permute-start.4 = (bf16[3,256,128]{2,1,0:T(8,128)(2,1)S(1)}, bf16[3,256,128]{2,1,0:T(8,128)(2,1)S(1)}, u32[]{:S(2)}, u32[]{:S(2)}) collective-permute-start(bf16[3,256,128]{2,1,0:T(8,128)(2,1)S(1)} %collective-permute-done.3.rest_4_), channel_id=1, source_target_pairs={{0,4},{4,0},{8,12},{12,8},{16,20},{20,16},{24,28},{28,24},{1,5},{5... | collective-permute-start | bytes 589832 | tf_op jit(solution)/shard_map/ppermute | solution.py:21
  16.8 2.6 %collective-permute-start.6 = (bf16[3,256,128]{2,1,0:T(8,128)(2,1)S(1)}, bf16[3,256,128]{2,1,0:T(8,128)(2,1)S(1)}, u32[]{:S(2)}, u32[]{:S(2)}) collective-permute-start(bf16[3,256,128]{2,1,0:T(8,128)(2,1)S(1)} %collective-permute-done.5.rest_6_), channel_id=1, source_target_pairs={{0,4},{4,0},{8,12},{12,8},{16,20},{20,16},{24,28},{28,24},{1,5},{5... | collective-permute-start | bytes 589832 | tf_op jit(solution)/shard_map/ppermute | solution.py:21
  16.8 7.7 %collective-permute-start.11 = (bf16[3,256,128]{2,1,0:T(8,128)(2,1)S(1)}, bf16[3,256,128]{2,1,0:T(8,128)(2,1)S(1)}, u32[]{:S(2)}, u32[]{:S(2)}) collective-permute-start(bf16[3,256,128]{2,1,0:T(8,128)(2,1)S(1)} %get-tuple-element.29.rest_0_), channel_id=1, source_target_pairs={{0,16},{4,12},{8,24},{12,4},{16,0},{20,28},{24,8},{28,20},{1,17},{... | collective-permute-start | bytes 589832 | tf_op jit(solution)/shard_map/ppermute | solution.py:21
  19.3 5.8 %collective-permute-start.13 = (bf16[3,256,128]{2,1,0:T(8,128)(2,1)S(1)}, bf16[3,256,128]{2,1,0:T(8,128)(2,1)S(1)}, u32[]{:S(2)}, u32[]{:S(2)}) collective-permute-start(bf16[3,256,128]{2,1,0:T(8,128)(2,1)S(1)} %collective-permute-done.9.rest_2_), channel_id=1, source_target_pairs={{0,16},{4,12},{8,24},{12,4},{16,0},{20,28},{24,8},{28,20},{1,17},{... | collective-permute-start | bytes 589832 | tf_op jit(solution)/shard_map/ppermute | solution.py:21
  21.3 9.1 %collective-permute-start.7 = (bf16[2,2,4,64,128]{4,3,2,1,0:T(8,128)(2,1)S(1)}, bf16[2,2,4,64,128]{4,3,2,1,0:T(8,128)(2,1)S(1)}, u32[]{:S(2)}, u32[]{:S(2)}) collective-permute-start(bf16[2,2,4,64,128]{4,3,2,1,0:T(8,128)(2,1)S(1)} %get-tuple-element.26), channel_id=1, source_target_pairs={{0,1},{1,0},{2,3},{3,2},{4,5},{5,4},{6,7},{7,6},{8,9},{9,8},{10,11... | collective-permute-start | bytes 786440 | tf_op jit(solution)/shard_map/ppermute | solution.py:21
  24.1 1.4 %collective-permute-start.8 = (bf16[3,256,128]{2,1,0:T(8,128)(2,1)S(1)}, bf16[3,256,128]{2,1,0:T(8,128)(2,1)S(1)}, u32[]{:S(2)}, u32[]{:S(2)}) collective-permute-start(bf16[3,256,128]{2,1,0:T(8,128)(2,1)S(1)} %get-tuple-element.29.rest_0_), channel_id=1, source_target_pairs={{0,4},{4,0},{8,12},{12,8},{16,20},{20,16},{24,28},{28,24},{1,5},{5... | collective-permute-start | bytes 589832 | tf_op jit(solution)/shard_map/ppermute | solution.py:21
  24.1 1.7 %collective-permute-start.10 = (bf16[3,256,128]{2,1,0:T(8,128)(2,1)S(1)}, bf16[3,256,128]{2,1,0:T(8,128)(2,1)S(1)}, u32[]{:S(2)}, u32[]{:S(2)}) collective-permute-start(bf16[3,256,128]{2,1,0:T(8,128)(2,1)S(1)} %collective-permute-done.9.rest_2_), channel_id=1, source_target_pairs={{0,4},{4,0},{8,12},{12,8},{16,20},{20,16},{24,28},{28,24},{1,5},{5... | collective-permute-start | bytes 589832 | tf_op jit(solution)/shard_map/ppermute | solution.py:21
  24.6 1.5 %collective-permute-start.12 = (bf16[3,256,128]{2,1,0:T(8,128)(2,1)S(1)}, bf16[3,256,128]{2,1,0:T(8,128)(2,1)S(1)}, u32[]{:S(2)}, u32[]{:S(2)}) collective-permute-start(bf16[3,256,128]{2,1,0:T(8,128)(2,1)S(1)} %collective-permute-done.11.rest_4_), channel_id=1, source_target_pairs={{0,4},{4,0},{8,12},{12,8},{16,20},{20,16},{24,28},{28,24},{1,5},{5... | collective-permute-start | bytes 589832 | tf_op jit(solution)/shard_map/ppermute | solution.py:21
  25.1 1.4 %collective-permute-start.14 = (bf16[3,256,128]{2,1,0:T(8,128)(2,1)S(1)}, bf16[3,256,128]{2,1,0:T(8,128)(2,1)S(1)}, u32[]{:S(2)}, u32[]{:S(2)}) collective-permute-start(bf16[3,256,128]{2,1,0:T(8,128)(2,1)S(1)} %collective-permute-done.13.rest_6_), channel_id=1, source_target_pairs={{0,4},{4,0},{8,12},{12,8},{16,20},{20,16},{24,28},{28,24},{1,5},{5... | collective-permute-start | bytes 589832 | tf_op jit(solution)/shard_map/ppermute | solution.py:21
  30.5 14.9 %collective-permute-start.15 = (bf16[2,2,4,64,128]{4,3,2,1,0:T(8,128)(2,1)S(1)}, bf16[2,2,4,64,128]{4,3,2,1,0:T(8,128)(2,1)S(1)}, u32[]{:S(2)}, u32[]{:S(2)}) collective-permute-start(bf16[2,2,4,64,128]{4,3,2,1,0:T(8,128)(2,1)S(1)} %get-tuple-element.31), channel_id=1, source_target_pairs={{0,1},{1,0},{2,3},{3,2},{4,5},{5,4},{6,7},{7,6},{8,9},{9,8},{10,11... | collective-permute-start | bytes 786440 | tf_op jit(solution)/shard_map/ppermute | solution.py:21
  33.4 6.2 %collective-permute-start.19 = (f32[8,128]{1,0:T(8,128)S(1)}, f32[8,128]{1,0:T(8,128)S(1)}, u32[]{:S(2)}, u32[]{:S(2)}) collective-permute-start(f32[8,128]{1,0:T(8,128)S(1)} %add.12), channel_id=1, source_target_pairs={{0,24},{4,28},{8,16},{12,20},{16,8},{20,12},{24,0},{28,4},{1,25},{... | collective-permute-start | bytes 12296 | tf_op jit(solution)/shard_map/ppermute | solution.py:21
  34.5 5.1 %collective-permute-start.18 = (f32[8,128]{1,0:T(8,128)S(1)}, f32[8,128]{1,0:T(8,128)S(1)}, u32[]{:S(2)}, u32[]{:S(2)}) collective-permute-start(f32[8,128]{1,0:T(8,128)S(1)} %add.12), channel_id=1, source_target_pairs={{0,16},{4,20},{8,24},{12,28},{16,0},{20,4},{24,8},{28,12},{1,17},{... | collective-permute-start | bytes 12296 | tf_op jit(solution)/shard_map/ppermute | solution.py:21
  36.3 3.6 %collective-permute-start.17 = (f32[8,128]{1,0:T(8,128)S(1)}, f32[8,128]{1,0:T(8,128)S(1)}, u32[]{:S(2)}, u32[]{:S(2)}) collective-permute-start(f32[8,128]{1,0:T(8,128)S(1)} %add.12), channel_id=1, source_target_pairs={{0,8},{4,12},{8,0},{12,4},{16,24},{20,28},{24,16},{28,20},{1,9},{5... | collective-permute-start | bytes 12296 | tf_op jit(solution)/shard_map/ppermute | solution.py:21
  36.9 8.5 %collective-permute-start.20 = (bf16[1,2,4,64,128]{4,3,2,1,0:T(8,128)(2,1)S(1)}, bf16[1,2,4,64,128]{4,3,2,1,0:T(8,128)(2,1)S(1)}, u32[]{:S(2)}, u32[]{:S(2)}) collective-permute-start(bf16[1,2,4,64,128]{4,3,2,1,0:T(8,128)(2,1)S(1)} %get-tuple-element.33), channel_id=1, source_target_pairs={{0,2},{1,3},{2,0},{3,1},{4,6},{5,7},{6,4},{7,5},{8,10},{9,11},{10,... | collective-permute-start | bytes 393224 | tf_op jit(solution)/shard_map/ppermute | solution.py:21
  45.4 9.2 %collective-permute-start.21 = (bf16[1,2,4,64,128]{4,3,2,1,0:T(8,128)(2,1)S(1)}, bf16[1,2,4,64,128]{4,3,2,1,0:T(8,128)(2,1)S(1)}, u32[]{:S(2)}, u32[]{:S(2)}) collective-permute-start(bf16[1,2,4,64,128]{4,3,2,1,0:T(8,128)(2,1)S(1)} %get-tuple-element.38), channel_id=1, source_target_pairs={{0,2},{1,3},{2,0},{3,1},{4,6},{5,7},{6,4},{7,5},{8,10},{9,11},{10,... | collective-permute-start | bytes 393224 | tf_op jit(solution)/shard_map/ppermute | solution.py:21
  45.6 5.4 %collective-permute-start.22 = (f32[8,128]{1,0:T(8,128)S(1)}, f32[8,128]{1,0:T(8,128)S(1)}, u32[]{:S(2)}, u32[]{:S(2)}) collective-permute-start(f32[8,128]{1,0:T(8,128)S(1)} %add_add_fusion.refs_0_), channel_id=1, source_target_pairs={{0,1},{1,0},{2,3},{3,2},{4,5},{5,4},{6,7},{7,6},{8,9},{9,8},{10,11... | collective-permute-start | bytes 12296 | tf_op jit(solution)/shard_map/ppermute | solution.py:21
  48.6 5.1 %collective-permute-start.23 = (f32[8,128]{1,0:T(8,128)S(1)}, f32[8,128]{1,0:T(8,128)S(1)}, u32[]{:S(2)}, u32[]{:S(2)}) collective-permute-start(f32[8,128]{1,0:T(8,128)S(1)} %add_add_fusion.refs_0_), channel_id=1, source_target_pairs={{0,2},{1,3},{2,0},{3,1},{4,6},{5,7},{6,4},{7,5},{8,10},{9,11},{10,... | collective-permute-start | bytes 12296 | tf_op jit(solution)/shard_map/ppermute | solution.py:21
  48.7 5.4 %collective-permute-start.24 = (f32[8,128]{1,0:T(8,128)S(1)}, f32[8,128]{1,0:T(8,128)S(1)}, u32[]{:S(2)}, u32[]{:S(2)}) collective-permute-start(f32[8,128]{1,0:T(8,128)S(1)} %add_add_fusion.refs_0_), channel_id=1, source_target_pairs={{0,3},{1,2},{2,1},{3,0},{4,7},{5,6},{6,5},{7,4},{8,11},{9,10},{10,... | collective-permute-start | bytes 12296 | tf_op jit(solution)/shard_map/ppermute | solution.py:21
  (5 other events, 41.0 us)

commit v5 on v4

--- a/solution.py
+++ b/solution.py
@@ -82,18 +82,16 @@
 
 def sum_kernel(sectors, chunk, offsets, vectors, inner, before, *rest):
     pieces = rest[:sectors]
-    keep, send, tile, rights, partial = rest[sectors:]
+    shares, tile, rights, partial = rest[sectors:]
     terms, trials, pairs, states, _ = inner.shape
     width = partial.shape[2]
-    shares = 2 * keep.shape[0]
-    rows = states // shares
+    rows = shares.shape[3]
     sector = lax.axis_index("sec")
     odd = sector & 1
     for mask in range(0, sectors, 2):
         even_place, odd_place = turned(mask, 0, sectors), turned(mask, 1, sectors)
         rights[jnp.where(odd == 1, odd_place, even_place)] = pieces[mask][...]
         rights[jnp.where(odd == 1, even_place, odd_place) ^ 1] = pieces[mask + 1][...]
-    place = lax.axis_index("term")
     columns = slice(chunk * width, (chunk + 1) * width)
     grams = [jnp.zeros((8, width), jnp.float32) for _ in range(trials * trials)]
     for pair in range(pairs):
@@ -112,31 +110,19 @@
             for i in range(trials):
                 spread = vectors[i, pair, :, columns].astype(jnp.float32) * product
                 grams[i * trials + j] += jnp.sum(spread.reshape(-1, 8, width), axis=0)
-        for mask in range(shares):
-            start = pl.multiple_of((place ^ mask) * rows, rows)
-            share = partial[:, pl.ds(start, rows)]
-            if mask & 1:
-                send[mask // 2, :, pair] = share.astype(jnp.bfloat16)
-            else:
-                keep[mask // 2, :, pair] = share
+        for place in range(shares.shape[0]):
+            share = partial[:, place * rows : (place + 1) * rows]
+            shares[place, :, pair] = share.astype(jnp.bfloat16)
     tile[...] = before[...] + place_rows([(k, total(value)) for k, value in enumerate(grams)])
 
 
-def halve_kernel(kept, received, keep, send):
-    for k in range(kept.shape[0]):
-        both = kept[k] + received[k].astype(jnp.float32)
-        if k & 1:
-            send[k // 2] = both.astype(jnp.bfloat16)
-        else:
-            keep[k // 2] = both
-
-
-def finish_kernel(*refs):
+def add_kernel(*refs):
     *parts, products = refs
-    width = products.shape[-1] // (len(parts) // 2)
-    for chunk in range(len(parts) // 2):
-        kept, received = parts[2 * chunk : 2 * chunk + 2]
-        both = kept[0] + received[0].astype(jnp.float32)
+    width = products.shape[-1] // len(parts)
+    for chunk, part in enumerate(parts):
+        both = part[0].astype(jnp.float32)
+        for place in range(1, part.shape[0]):
+            both = both + part[place].astype(jnp.float32)
         products[:, :, :, chunk * width : (chunk + 1) * width] = both.astype(jnp.bfloat16)
 
 
@@ -229,55 +215,29 @@
         after = behind_inner if chunk == 0 else lambda block: block
         gathered.append(gather_sectors(chunks[chunk], sectors, after))
 
-    def share_of(count, dtype):
-        return jax.ShapeDtypeStruct((count, trials, pairs, rows, width), dtype)
-
-    parts, arrived = [], None
+    parts = []
     for chunk in range(CHUNKS):
-        keep, send, tile = call(
+        sent, tile = call(
             functools.partial(sum_kernel, sectors, chunk),
             "sum_over_terms",
             2 * terms * trials * pairs * states * states * width,
             4 * MIB,
             sectors * terms * states * width * 2 + 12 * MIB,
             out_shape=(
-                share_of(shares // 2, jnp.float32),
-                share_of(shares // 2, jnp.bfloat16),
+                jax.ShapeDtypeStruct((shares, trials, pairs, rows, width), jnp.bfloat16),
                 jax.ShapeDtypeStruct(TILE, jnp.float32),
             ),
             in_specs=[SMEM, VMEM, VMEM, VMEM] + [VMEM] * sectors,
-            out_specs=(VMEM, VMEM, VMEM),
+            out_specs=(VMEM, VMEM),
             scratch_shapes=[
                 pltpu.VMEM((sectors, terms, states, width), jnp.bfloat16),
                 pltpu.VMEM((trials, states, width), jnp.float32),
             ],
         )(offsets, vectors, inner, tile, *gathered[chunk])
-        if arrived is not None:
-            send, arrived = lax.optimization_barrier((send, arrived))
-        step = 1
-        arrived = received = swap(send, "term", step)
-        if chunk == CHUNKS - 1:
-            for masks in [[1]] + steps_of(sectors, 1):
-                tile = add_places(tile, "sec", masks)
-            others = tuple(parts[1::2])
-            received, tile, others = lax.optimization_barrier((received, tile, others))
-            parts[1::2] = others
-        while 2 * step < shares:
-            step *= 2
-            count = shares // (2 * step)
-            keep, send = call(
-                halve_kernel,
-                "halve_rows",
-                1,
-                1,
-                8 * MIB,
-                out_shape=(share_of(count, jnp.float32), share_of(count, jnp.bfloat16)),
-                in_specs=[VMEM, VMEM],
-                out_specs=(VMEM, VMEM),
-            )(keep, received)
-            received = swap(send, "term", step)
-        parts += [keep, received]
-
+        parts.append(lax.all_to_all(sent, "term", 0, 0, tiled=True))
+
+    for masks in [[1]] + steps_of(sectors, 1):
+        tile = add_places(tile, "sec", masks)
     *steps, last = steps_of(shares, 0)
     for masks in steps:
         tile = add_places(tile, "term", masks)
@@ -293,8 +253,8 @@
         out_specs=VMEM,
     )(*tiles)
     products = call(
-        finish_kernel,
-        "add_last_share",
+        add_kernel,
+        "add_shares",
         1,
         1,
         8 * MIB,

time: 55.7 us -> 68.7 us (1.23)
  waiting for transfers between devices: 17.4 us -> 25.1 us
  local copies, waits for them, and re-layouts: 2.23 us -> 5.06 us
  starting transfers between devices: 27.8 us -> 29.3 us
    all_to_all x0 -> x2, starting transfers between devices: none -> 10.7 us  [local(): parts.append(lax.all_to_all(sent, 'term', 0, 0, tiled=True))]
    ppermute x25 -> x21, starting transfers between devices: 27.8 us -> 18.7 us  [swap(): lax.ppermute(value, axis, [(place, place ^ masks[place & 1]) for place in...]
    ppermute x25 -> x21, waiting for transfers between devices: 17.4 us -> 25.1 us  [swap(): lax.ppermute(value, axis, [(place, place ^ masks[place & 1]) for place in...]
    unnamed x8 -> x14, local copies, waits for them, and re-layouts: 2.23 us -> 5.06 us
    pallas_call x3 -> x1, Pallas kernels: 0.86 us -> 1.88 us  [local(): call(add_kernel, 'add_shares', 1, 1, 8 * MIB, out_shape=jax.ShapeDtypeStr...]
  transfers between devices with their start and end apart: 25 -> 23, of which waited for: 13 -> 12; matrix products, arithmetic and copies ran while one was open for 0% -> 0% of each run, Pallas kernels for 10% -> 5%
where the time goes in v5:
time: 68.7 us; the launch traced here: 68.3 us
  starting transfers between devices  29.3 us (43%)
  waiting for transfers between devices  25.1 us (37%)
  Pallas kernels  8.05 us (12%)
  local copies, waits for them, and re-layouts  5.06 us (7%)
  between operations  0.72 us (1%)
    ppermute x21, waiting for transfers between devices, swap(): lax.ppermute(value, axis, [(place, place ^ masks[place & 1]) for place in...  25.1 us
    ppermute x21, starting transfers between devices, swap(): lax.ppermute(value, axis, [(place, place ^ masks[place & 1]) for place in...  18.7 us
    all_to_all x2, starting transfers between devices, local(): parts.append(lax.all_to_all(sent, 'term', 0, 0, tiled=True))  10.7 us
    unnamed x14, local copies, waits for them, and re-layouts  5.06 us
    pallas_call x2, Pallas kernels, local(): call(functools.partial(sum_kernel, sectors, chunk), 'sum_over_terms', 2 *...  3.47 us
    pallas_call x1, Pallas kernels, local(): call(add_kernel, 'add_shares', 1, 1, 8 * MIB, out_shape=jax.ShapeDtypeStr...  1.88 us
  transfers between devices with their start and end apart: 23, of which 12 were waited for; matrix products, arithmetic and copies ran while one was open for 0% of the time, Pallas kernels for 5%

profile of v5, /device:TPU:0, one launch (start us, length us, event | category | flops | bytes accessed | tf_op | source)
XLA Modules:
  0.0 68.3 jit_solution(10641642157839607666)
XLA Ops:
  1.8 3.0 %collective-permute-start.1 = (bf16[3,256,128]{2,1,0:T(8,128)(2,1)S(1)}, bf16[3,256,128]{2,1,0:T(8,128)(2,1)S(1)}, u32[]{:S(2)}, u32[]{:S(2)}) collective-permute-start(bf16[3,256,128]{2,1,0:T(8,128)(2,1)S(1)} %get-tuple-element.13.rest_0_), channel_id=1, source_target_pairs={{0,8},{4,20},{8,0},{12,28},{16,24},{20,4},{24,16},{28,12},{1,9},{5... | collective-permute-start | bytes 589832 | tf_op jit(solution)/shard_map/ppermute | solution.py:21
  4.8 1.5 %collective-permute-start.3 = (bf16[3,256,128]{2,1,0:T(8,128)(2,1)S(1)}, bf16[3,256,128]{2,1,0:T(8,128)(2,1)S(1)}, u32[]{:S(2)}, u32[]{:S(2)}) collective-permute-start(bf16[3,256,128]{2,1,0:T(8,128)(2,1)S(1)} %get-tuple-element.13.rest_0_), channel_id=1, source_target_pairs={{0,16},{4,12},{8,24},{12,4},{16,0},{20,28},{24,8},{28,20},{1,17},{... | collective-permute-start | bytes 589832 | tf_op jit(solution)/shard_map/ppermute | solution.py:21
  6.3 1.2 %copy-done = bf16[2,1,4,256,256]{4,3,2,1,0:T(8,128)(2,1)S(1)} copy-done((bf16[2,1,4,256,256]{4,3,2,1,0:T(8,128)(2,1)S(1)}, bf16[2,1,4,256,256]{4,3,2,1,0:T(8,128)(2,1)}, u32[]{:S(2)}) %copy-start) | copy-done | bytes 1048600
  10.0 1.6 %collective-permute-start.5 = (bf16[3,256,128]{2,1,0:T(8,128)(2,1)S(1)}, bf16[3,256,128]{2,1,0:T(8,128)(2,1)S(1)}, u32[]{:S(2)}, u32[]{:S(2)}) collective-permute-start(bf16[3,256,128]{2,1,0:T(8,128)(2,1)S(1)} %collective-permute-done.1.rest_2_), channel_id=1, source_target_pairs={{0,16},{4,12},{8,24},{12,4},{16,0},{20,28},{24,8},{28,20},{1,17},{... | collective-permute-start | bytes 589832 | tf_op jit(solution)/shard_map/ppermute | solution.py:21
  12.1 3.6 %collective-permute-done.5.rest_6_ = bf16[3,256,128]{2,1,0:T(8,128)(2,1)S(1)} collective-permute-done((bf16[3,256,128]{2,1,0:T(8,128)(2,1)S(1)}, bf16[3,256,128]{2,1,0:T(8,128)(2,1)S(1)}, u32[]{:S(2)}, u32[]{:S(2)}) %collective-permute-start.5) | collective-permute-done | bytes 196640 | tf_op jit(solution)/shard_map/ppermute | solution.py:21
  15.7 1.4 %collective-permute-done.6.rest_7_ = bf16[3,256,128]{2,1,0:T(8,128)(2,1)S(1)} collective-permute-done((bf16[3,256,128]{2,1,0:T(8,128)(2,1)S(1)}, bf16[3,256,128]{2,1,0:T(8,128)(2,1)S(1)}, u32[]{:S(2)}, u32[]{:S(2)}) %collective-permute-start.6) | collective-permute-done | bytes 196640 | tf_op jit(solution)/shard_map/ppermute | solution.py:21
  17.1 1.7 %sum_over_terms.2 = (bf16[4,2,4,64,128]{4,3,2,1,0:T(8,128)(2,1)S(1)}, f32[8,128]{1,0:T(8,128)S(1)}) custom-call(s32[3,4]{1,0:T(4,128)S(1)} %copy-done.5, bf16[2,4,256,256]{3,2,1,0:T(8,128)(2,1)S(1)} %bitcast.7, bf16[3,2,4,256,256]{4,3,2,1,0:T(8,128)(2,1)S(1)} %get-tuple-element.11.inner, f32[8,128]{1,0:T(8,128)S(1)} %get-tuple-element.12.before, ...), custom_call_target="tpu_custom_call" | custom-call | flops 402653184 | bytes 4194304 | tf_op jit(solution)/shard_map/sum_over_terms/pallas_call | solution.py:220
  19.6 5.9 %all-to-all-start = ((bf16[4,2,4,64,128]{4,3,2,1,0:T(8,128)(2,1)}), bf16[4,2,4,64,128]{4,3,2,1,0:T(8,128)(2,1)}, u32[]{:S(2)}, u32[]{:S(2)}) async-start(bf16[4,2,4,64,128]{4,3,2,1,0:T(8,128)(2,1)} %copy-done.4), calls=%async_computation | async-start | bytes 1048576 | tf_op jit(solution)/shard_map/all_to_all | solution.py:237
  25.5 1.5 %collective-permute-start.8 = (bf16[3,256,128]{2,1,0:T(8,128)(2,1)S(1)}, bf16[3,256,128]{2,1,0:T(8,128)(2,1)S(1)}, u32[]{:S(2)}, u32[]{:S(2)}) collective-permute-start(bf16[3,256,128]{2,1,0:T(8,128)(2,1)S(1)} %get-tuple-element.17.rest_0_), channel_id=1, source_target_pairs={{0,8},{4,20},{8,0},{12,28},{16,24},{20,4},{24,16},{28,12},{1,9},{5... | collective-permute-start | bytes 589832 | tf_op jit(solution)/shard_map/ppermute | solution.py:21
  27.7 4.9 %collective-permute-done.8.rest_2_ = bf16[3,256,128]{2,1,0:T(8,128)(2,1)S(1)} collective-permute-done((bf16[3,256,128]{2,1,0:T(8,128)(2,1)S(1)}, bf16[3,256,128]{2,1,0:T(8,128)(2,1)S(1)}, u32[]{:S(2)}, u32[]{:S(2)}) %collective-permute-start.8) | collective-permute-done | bytes 196640 | tf_op jit(solution)/shard_map/ppermute | solution.py:21
  32.6 1.4 %collective-permute-start.12 = (bf16[3,256,128]{2,1,0:T(8,128)(2,1)S(1)}, bf16[3,256,128]{2,1,0:T(8,128)(2,1)S(1)}, u32[]{:S(2)}, u32[]{:S(2)}) collective-permute-start(bf16[3,256,128]{2,1,0:T(8,128)(2,1)S(1)} %collective-permute-done.8.rest_2_), channel_id=1, source_target_pairs={{0,16},{4,12},{8,24},{12,4},{16,0},{20,28},{24,8},{28,20},{1,17},{... | collective-permute-start | bytes 589832 | tf_op jit(solution)/shard_map/ppermute | solution.py:21
  34.5 3.8 %collective-permute-done.12.rest_6_ = bf16[3,256,128]{2,1,0:T(8,128)(2,1)S(1)} collective-permute-done((bf16[3,256,128]{2,1,0:T(8,128)(2,1)S(1)}, bf16[3,256,128]{2,1,0:T(8,128)(2,1)S(1)}, u32[]{:S(2)}, u32[]{:S(2)}) %collective-permute-start.12) | collective-permute-done | bytes 196640 | tf_op jit(solution)/shard_map/ppermute | solution.py:21
  38.3 1.4 %collective-permute-done.13.rest_7_ = bf16[3,256,128]{2,1,0:T(8,128)(2,1)S(1)} collective-permute-done((bf16[3,256,128]{2,1,0:T(8,128)(2,1)S(1)}, bf16[3,256,128]{2,1,0:T(8,128)(2,1)S(1)}, u32[]{:S(2)}, u32[]{:S(2)}) %collective-permute-start.13) | collective-permute-done | bytes 196640 | tf_op jit(solution)/shard_map/ppermute | solution.py:21
  39.7 1.2 %copy-done.2 = bf16[2,1,4,256,256]{4,3,2,1,0:T(8,128)(2,1)S(1)} copy-done((bf16[2,1,4,256,256]{4,3,2,1,0:T(8,128)(2,1)S(1)}, bf16[2,1,4,256,256]{4,3,2,1,0:T(8,128)(2,1)}, u32[]{:S(2)}) %copy-start.2) | copy-done | bytes 1048600
  40.9 1.7 %sum_over_terms.3 = (bf16[4,2,4,64,128]{4,3,2,1,0:T(8,128)(2,1)S(1)}, f32[8,128]{1,0:T(8,128)S(1)}) custom-call(s32[3,4]{1,0:T(4,128)S(1)} %copy-done.5, bf16[2,4,256,256]{3,2,1,0:T(8,128)(2,1)S(1)} %bitcast.8, bf16[3,2,4,256,256]{4,3,2,1,0:T(8,128)(2,1)S(1)} %get-tuple-element.11.inner, f32[8,128]{1,0:T(8,128)S(1)} %get-tuple-element.16.before, ...), custom_call_target="tpu_custom_call" | custom-call | flops 402653184 | bytes 4194304 | tf_op jit(solution)/shard_map/sum_over_terms/pallas_call | solution.py:220
  43.5 4.8 %all-to-all-start.1 = ((bf16[4,2,4,64,128]{4,3,2,1,0:T(8,128)(2,1)}), bf16[4,2,4,64,128]{4,3,2,1,0:T(8,128)(2,1)S(1)}, u32[]{:S(2)}, u32[]{:S(2)}) async-start(bf16[4,2,4,64,128]{4,3,2,1,0:T(8,128)(2,1)} %copy-done.3), calls=%async_computation.1 | async-start | bytes 1048576 | tf_op jit(solution)/shard_map/all_to_all | solution.py:237
  48.3 1.2 %collective-permute-done.14 = f32[8,128]{1,0:T(8,128)S(1)} collective-permute-done((f32[8,128]{1,0:T(8,128)S(1)}, f32[8,128]{1,0:T(8,128)S(1)}, u32[]{:S(2)}, u32[]{:S(2)}) %collective-permute-start.14) | collective-permute-done | bytes 4128 | tf_op jit(solution)/shard_map/ppermute | solution.py:21
  49.5 2.4 %collective-permute-start.17 = (f32[8,128]{1,0:T(8,128)S(1)}, f32[8,128]{1,0:T(8,128)S(1)}, u32[]{:S(2)}, u32[]{:S(2)}) collective-permute-start(f32[8,128]{1,0:T(8,128)S(1)} %add.12), channel_id=1, source_target_pairs={{0,24},{4,28},{8,16},{12,20},{16,8},{20,12},{24,0},{28,4},{1,25},{... | collective-permute-start | bytes 12296 | tf_op jit(solution)/shard_map/ppermute | solution.py:21
  54.0 1.5 %collective-permute-done.16 = f32[8,128]{1,0:T(8,128)S(1)} collective-permute-done((f32[8,128]{1,0:T(8,128)S(1)}, f32[8,128]{1,0:T(8,128)S(1)}, u32[]{:S(2)}, u32[]{:S(2)}) %collective-permute-start.16) | collective-permute-done | bytes 4128 | tf_op jit(solution)/shard_map/ppermute | solution.py:21
  56.0 2.0 %collective-permute-start.18 = (f32[8,128]{1,0:T(8,128)S(1)}, f32[8,128]{1,0:T(8,128)S(1)}, u32[]{:S(2)}, u32[]{:S(2)}) collective-permute-start(f32[8,128]{1,0:T(8,128)S(1)} %add_add_fusion.refs_0_), channel_id=1, source_target_pairs={{0,1},{1,0},{2,3},{3,2},{4,5},{5,4},{6,7},{7,6},{8,9},{9,8},{10,11... | collective-permute-start | bytes 12296 | tf_op jit(solution)/shard_map/ppermute | solution.py:21
  58.1 2.4 %collective-permute-start.19 = (f32[8,128]{1,0:T(8,128)S(1)}, f32[8,128]{1,0:T(8,128)S(1)}, u32[]{:S(2)}, u32[]{:S(2)}) collective-permute-start(f32[8,128]{1,0:T(8,128)S(1)} %add_add_fusion.refs_0_), channel_id=1, source_target_pairs={{0,2},{1,3},{2,0},{3,1},{4,6},{5,7},{6,4},{7,5},{8,10},{9,11},{10,... | collective-permute-start | bytes 12296 | tf_op jit(solution)/shard_map/ppermute | solution.py:21
  60.5 2.9 %collective-permute-done.19.refs_2_ = f32[8,128]{1,0:T(8,128)S(1)} collective-permute-done((f32[8,128]{1,0:T(8,128)S(1)}, f32[8,128]{1,0:T(8,128)S(1)}, u32[]{:S(2)}, u32[]{:S(2)}) %collective-permute-start.19) | collective-permute-done | bytes 4128 | tf_op jit(solution)/shard_map/ppermute | solution.py:21
  63.3 2.5 %collective-permute-done.20.refs_3_ = f32[8,128]{1,0:T(8,128)S(1)} collective-permute-done((f32[8,128]{1,0:T(8,128)S(1)}, f32[8,128]{1,0:T(8,128)S(1)}, u32[]{:S(2)}, u32[]{:S(2)}) %collective-permute-start.20) | collective-permute-done | bytes 4128 | tf_op jit(solution)/shard_map/ppermute | solution.py:21
  66.4 1.9 %add_shares.1 = bf16[2,4,64,256]{3,2,1,0:T(8,128)(2,1)} custom-call(bf16[4,2,4,64,128]{4,3,2,1,0:T(8,128)(2,1)} %all-to-all-done.refs_0_, bf16[4,2,4,64,128]{4,3,2,1,0:T(8,128)(2,1)S(1)} %all-to-all-done.1.refs_1_), custom_call_target="tpu_custom_call" | custom-call | flops 1 | bytes 1 | tf_op jit(solution)/shard_map/add_shares/pallas_call | solution.py:255
  (44 shorter events, 10.3 us)
Async XLA Ops:
  0.6 16.5 %copy-start.1 = (bf16[2,1,4,256,256]{4,3,2,1,0:T(8,128)(2,1)S(1)}, bf16[2,1,4,256,256]{4,3,2,1,0:T(8,128)(2,1)}, u32[]{:S(2)}) copy-start(bf16[2,1,4,256,256]{4,3,2,1,0:T(8,128)(2,1)} %param.4) | copy-start | bytes 3145732
  1.8 8.2 %collective-permute-start.1 = (bf16[3,256,128]{2,1,0:T(8,128)(2,1)S(1)}, bf16[3,256,128]{2,1,0:T(8,128)(2,1)S(1)}, u32[]{:S(2)}, u32[]{:S(2)}) collective-permute-start(bf16[3,256,128]{2,1,0:T(8,128)(2,1)S(1)} %get-tuple-element.13.rest_0_), channel_id=1, source_target_pairs={{0,8},{4,20},{8,0},{12,28},{16,24},{20,4},{24,16},{28,12},{1,9},{5... | collective-permute-start | bytes 589832 | tf_op jit(solution)/shard_map/ppermute | solution.py:21
  4.8 7.3 %collective-permute-start.3 = (bf16[3,256,128]{2,1,0:T(8,128)(2,1)S(1)}, bf16[3,256,128]{2,1,0:T(8,128)(2,1)S(1)}, u32[]{:S(2)}, u32[]{:S(2)}) collective-permute-start(bf16[3,256,128]{2,1,0:T(8,128)(2,1)S(1)} %get-tuple-element.13.rest_0_), channel_id=1, source_target_pairs={{0,16},{4,12},{8,24},{12,4},{16,0},{20,28},{24,8},{28,20},{1,17},{... | collective-permute-start | bytes 589832 | tf_op jit(solution)/shard_map/ppermute | solution.py:21
  10.0 5.7 %collective-permute-start.5 = (bf16[3,256,128]{2,1,0:T(8,128)(2,1)S(1)}, bf16[3,256,128]{2,1,0:T(8,128)(2,1)S(1)}, u32[]{:S(2)}, u32[]{:S(2)}) collective-permute-start(bf16[3,256,128]{2,1,0:T(8,128)(2,1)S(1)} %collective-permute-done.1.rest_2_), channel_id=1, source_target_pairs={{0,16},{4,12},{8,24},{12,4},{16,0},{20,28},{24,8},{28,20},{1,17},{... | collective-permute-start | bytes 589832 | tf_op jit(solution)/shard_map/ppermute | solution.py:21
  11.5 4.1 %collective-permute-start = (bf16[3,256,128]{2,1,0:T(8,128)(2,1)S(1)}, bf16[3,256,128]{2,1,0:T(8,128)(2,1)S(1)}, u32[]{:S(2)}, u32[]{:S(2)}) collective-permute-start(bf16[3,256,128]{2,1,0:T(8,128)(2,1)S(1)} %get-tuple-element.13.rest_0_), channel_id=1, source_target_pairs={{0,4},{4,0},{8,12},{12,8},{16,20},{20,16},{24,28},{28,24},{1,5},{5... | collective-permute-start | bytes 589832 | tf_op jit(solution)/shard_map/ppermute | solution.py:21
  11.5 4.1 %collective-permute-start.2 = (bf16[3,256,128]{2,1,0:T(8,128)(2,1)S(1)}, bf16[3,256,128]{2,1,0:T(8,128)(2,1)S(1)}, u32[]{:S(2)}, u32[]{:S(2)}) collective-permute-start(bf16[3,256,128]{2,1,0:T(8,128)(2,1)S(1)} %collective-permute-done.1.rest_2_), channel_id=1, source_target_pairs={{0,4},{4,0},{8,12},{12,8},{16,20},{20,16},{24,28},{28,24},{1,5},{5... | collective-permute-start | bytes 589832 | tf_op jit(solution)/shard_map/ppermute | solution.py:21
  12.1 3.6 %collective-permute-start.4 = (bf16[3,256,128]{2,1,0:T(8,128)(2,1)S(1)}, bf16[3,256,128]{2,1,0:T(8,128)(2,1)S(1)}, u32[]{:S(2)}, u32[]{:S(2)}) collective-permute-start(bf16[3,256,128]{2,1,0:T(8,128)(2,1)S(1)} %collective-permute-done.3.rest_4_), channel_id=1, source_target_pairs={{0,4},{4,0},{8,12},{12,8},{16,20},{20,16},{24,28},{28,24},{1,5},{5... | collective-permute-start | bytes 589832 | tf_op jit(solution)/shard_map/ppermute | solution.py:21
  15.6 1.4 %collective-permute-start.6 = (bf16[3,256,128]{2,1,0:T(8,128)(2,1)S(1)}, bf16[3,256,128]{2,1,0:T(8,128)(2,1)S(1)}, u32[]{:S(2)}, u32[]{:S(2)}) collective-permute-start(bf16[3,256,128]{2,1,0:T(8,128)(2,1)S(1)} %collective-permute-done.5.rest_6_), channel_id=1, source_target_pairs={{0,4},{4,0},{8,12},{12,8},{16,20},{20,16},{24,28},{28,24},{1,5},{5... | collective-permute-start | bytes 589832 | tf_op jit(solution)/shard_map/ppermute | solution.py:21
  19.6 23.8 %all-to-all-start = ((bf16[4,2,4,64,128]{4,3,2,1,0:T(8,128)(2,1)}), bf16[4,2,4,64,128]{4,3,2,1,0:T(8,128)(2,1)}, u32[]{:S(2)}, u32[]{:S(2)}) async-start(bf16[4,2,4,64,128]{4,3,2,1,0:T(8,128)(2,1)} %copy-done.4), calls=%async_computation | async-start | bytes 1048576 | tf_op jit(solution)/shard_map/all_to_all | solution.py:237
  25.5 7.1 %collective-permute-start.8 = (bf16[3,256,128]{2,1,0:T(8,128)(2,1)S(1)}, bf16[3,256,128]{2,1,0:T(8,128)(2,1)S(1)}, u32[]{:S(2)}, u32[]{:S(2)}) collective-permute-start(bf16[3,256,128]{2,1,0:T(8,128)(2,1)S(1)} %get-tuple-element.17.rest_0_), channel_id=1, source_target_pairs={{0,8},{4,20},{8,0},{12,28},{16,24},{20,4},{24,16},{28,12},{1,9},{5... | collective-permute-start | bytes 589832 | tf_op jit(solution)/shard_map/ppermute | solution.py:21
  27.0 7.5 %collective-permute-start.10 = (bf16[3,256,128]{2,1,0:T(8,128)(2,1)S(1)}, bf16[3,256,128]{2,1,0:T(8,128)(2,1)S(1)}, u32[]{:S(2)}, u32[]{:S(2)}) collective-permute-start(bf16[3,256,128]{2,1,0:T(8,128)(2,1)S(1)} %get-tuple-element.17.rest_0_), channel_id=1, source_target_pairs={{0,16},{4,12},{8,24},{12,4},{16,0},{20,28},{24,8},{28,20},{1,17},{... | collective-permute-start | bytes 589832 | tf_op jit(solution)/shard_map/ppermute | solution.py:21
  32.6 5.7 %collective-permute-start.12 = (bf16[3,256,128]{2,1,0:T(8,128)(2,1)S(1)}, bf16[3,256,128]{2,1,0:T(8,128)(2,1)S(1)}, u32[]{:S(2)}, u32[]{:S(2)}) collective-permute-start(bf16[3,256,128]{2,1,0:T(8,128)(2,1)S(1)} %collective-permute-done.8.rest_2_), channel_id=1, source_target_pairs={{0,16},{4,12},{8,24},{12,4},{16,0},{20,28},{24,8},{28,20},{1,17},{... | collective-permute-start | bytes 589832 | tf_op jit(solution)/shard_map/ppermute | solution.py:21
  34.0 4.3 %collective-permute-start.7 = (bf16[3,256,128]{2,1,0:T(8,128)(2,1)S(1)}, bf16[3,256,128]{2,1,0:T(8,128)(2,1)S(1)}, u32[]{:S(2)}, u32[]{:S(2)}) collective-permute-start(bf16[3,256,128]{2,1,0:T(8,128)(2,1)S(1)} %get-tuple-element.17.rest_0_), channel_id=1, source_target_pairs={{0,4},{4,0},{8,12},{12,8},{16,20},{20,16},{24,28},{28,24},{1,5},{5... | collective-permute-start | bytes 589832 | tf_op jit(solution)/shard_map/ppermute | solution.py:21
  34.0 4.3 %collective-permute-start.9 = (bf16[3,256,128]{2,1,0:T(8,128)(2,1)S(1)}, bf16[3,256,128]{2,1,0:T(8,128)(2,1)S(1)}, u32[]{:S(2)}, u32[]{:S(2)}) collective-permute-start(bf16[3,256,128]{2,1,0:T(8,128)(2,1)S(1)} %collective-permute-done.8.rest_2_), channel_id=1, source_target_pairs={{0,4},{4,0},{8,12},{12,8},{16,20},{20,16},{24,28},{28,24},{1,5},{5... | collective-permute-start | bytes 589832 | tf_op jit(solution)/shard_map/ppermute | solution.py:21
  34.5 3.8 %collective-permute-start.11 = (bf16[3,256,128]{2,1,0:T(8,128)(2,1)S(1)}, bf16[3,256,128]{2,1,0:T(8,128)(2,1)S(1)}, u32[]{:S(2)}, u32[]{:S(2)}) collective-permute-start(bf16[3,256,128]{2,1,0:T(8,128)(2,1)S(1)} %collective-permute-done.10.rest_4_), channel_id=1, source_target_pairs={{0,4},{4,0},{8,12},{12,8},{16,20},{20,16},{24,28},{28,24},{1,5},{5... | collective-permute-start | bytes 589832 | tf_op jit(solution)/shard_map/ppermute | solution.py:21
  38.3 1.4 %collective-permute-start.13 = (bf16[3,256,128]{2,1,0:T(8,128)(2,1)S(1)}, bf16[3,256,128]{2,1,0:T(8,128)(2,1)S(1)}, u32[]{:S(2)}, u32[]{:S(2)}) collective-permute-start(bf16[3,256,128]{2,1,0:T(8,128)(2,1)S(1)} %collective-permute-done.12.rest_6_), channel_id=1, source_target_pairs={{0,4},{4,0},{8,12},{12,8},{16,20},{20,16},{24,28},{28,24},{1,5},{5... | collective-permute-start | bytes 589832 | tf_op jit(solution)/shard_map/ppermute | solution.py:21
  43.5 22.9 %all-to-all-start.1 = ((bf16[4,2,4,64,128]{4,3,2,1,0:T(8,128)(2,1)}), bf16[4,2,4,64,128]{4,3,2,1,0:T(8,128)(2,1)S(1)}, u32[]{:S(2)}, u32[]{:S(2)}) async-start(bf16[4,2,4,64,128]{4,3,2,1,0:T(8,128)(2,1)} %copy-done.3), calls=%async_computation.1 | async-start | bytes 1048576 | tf_op jit(solution)/shard_map/all_to_all | solution.py:237
  48.3 1.2 %collective-permute-start.14 = (f32[8,128]{1,0:T(8,128)S(1)}, f32[8,128]{1,0:T(8,128)S(1)}, u32[]{:S(2)}, u32[]{:S(2)}) collective-permute-start(f32[8,128]{1,0:T(8,128)S(1)} %get-tuple-element.19), channel_id=1, source_target_pairs={{0,4},{4,0},{8,12},{12,8},{16,20},{20,16},{24,28},{28,24},{1,5},{5... | collective-permute-start | bytes 12296 | tf_op jit(solution)/shard_map/ppermute | solution.py:21
  49.5 4.5 %collective-permute-start.17 = (f32[8,128]{1,0:T(8,128)S(1)}, f32[8,128]{1,0:T(8,128)S(1)}, u32[]{:S(2)}, u32[]{:S(2)}) collective-permute-start(f32[8,128]{1,0:T(8,128)S(1)} %add.12), channel_id=1, source_target_pairs={{0,24},{4,28},{8,16},{12,20},{16,8},{20,12},{24,0},{28,4},{1,25},{... | collective-permute-start | bytes 12296 | tf_op jit(solution)/shard_map/ppermute | solution.py:21
  51.8 3.6 %collective-permute-start.16 = (f32[8,128]{1,0:T(8,128)S(1)}, f32[8,128]{1,0:T(8,128)S(1)}, u32[]{:S(2)}, u32[]{:S(2)}) collective-permute-start(f32[8,128]{1,0:T(8,128)S(1)} %add.12), channel_id=1, source_target_pairs={{0,16},{4,20},{8,24},{12,28},{16,0},{20,4},{24,8},{28,12},{1,17},{... | collective-permute-start | bytes 12296 | tf_op jit(solution)/shard_map/ppermute | solution.py:21
  52.4 3.6 %collective-permute-start.15 = (f32[8,128]{1,0:T(8,128)S(1)}, f32[8,128]{1,0:T(8,128)S(1)}, u32[]{:S(2)}, u32[]{:S(2)}) collective-permute-start(f32[8,128]{1,0:T(8,128)S(1)} %add.12), channel_id=1, source_target_pairs={{0,8},{4,12},{8,0},{12,4},{16,24},{20,28},{24,16},{28,20},{1,9},{5... | collective-permute-start | bytes 12296 | tf_op jit(solution)/shard_map/ppermute | solution.py:21
  56.0 4.5 %collective-permute-start.18 = (f32[8,128]{1,0:T(8,128)S(1)}, f32[8,128]{1,0:T(8,128)S(1)}, u32[]{:S(2)}, u32[]{:S(2)}) collective-permute-start(f32[8,128]{1,0:T(8,128)S(1)} %add_add_fusion.refs_0_), channel_id=1, source_target_pairs={{0,1},{1,0},{2,3},{3,2},{4,5},{5,4},{6,7},{7,6},{8,9},{9,8},{10,11... | collective-permute-start | bytes 12296 | tf_op jit(solution)/shard_map/ppermute | solution.py:21
  58.1 5.3 %collective-permute-start.19 = (f32[8,128]{1,0:T(8,128)S(1)}, f32[8,128]{1,0:T(8,128)S(1)}, u32[]{:S(2)}, u32[]{:S(2)}) collective-permute-start(f32[8,128]{1,0:T(8,128)S(1)} %add_add_fusion.refs_0_), channel_id=1, source_target_pairs={{0,2},{1,3},{2,0},{3,1},{4,6},{5,7},{6,4},{7,5},{8,10},{9,11},{10,... | collective-permute-start | bytes 12296 | tf_op jit(solution)/shard_map/ppermute | solution.py:21
  60.4 5.4 %collective-permute-start.20 = (f32[8,128]{1,0:T(8,128)S(1)}, f32[8,128]{1,0:T(8,128)S(1)}, u32[]{:S(2)}, u32[]{:S(2)}) collective-permute-start(f32[8,128]{1,0:T(8,128)S(1)} %add_add_fusion.refs_0_), channel_id=1, source_target_pairs={{0,3},{1,2},{2,1},{3,0},{4,7},{5,6},{6,5},{7,4},{8,11},{9,10},{10,... | collective-permute-start | bytes 12296 | tf_op jit(solution)/shard_map/ppermute | solution.py:21
  (6 other events, 21.5 us)

commit v6 on v4

--- a/solution.py
+++ b/solution.py
@@ -50,20 +50,9 @@
     return jnp.sum(jnp.sum(value, axis=0, keepdims=True), axis=1, keepdims=True)
 
 
-def split_kernel(right, *rest):
-    *chunks, sems = rest
-    width = chunks[0].shape[2]
-    copies = []
-    for place, chunk in enumerate(chunks):
-        columns = pl.ds(place * width, width)
-        copies.append(pltpu.make_async_copy(right.at[:, :, columns], chunk, sems.at[place]))
-    for copy in copies:
-        copy.start()
-    for copy in copies:
-        copy.wait()
-
-
-def inner_kernel(square_scale, vectors, left, inner, squares):
+def inner_kernel(square_scale, vectors, left, right_hbm, inner, squares, right, sem):
+    fetch = pltpu.make_async_copy(right_hbm, right, sem)
+    fetch.start()
     terms, states = left.shape[0], left.shape[1]
     stacked = left[...].reshape(terms * states, states)
     sums = []
@@ -78,6 +67,7 @@
         sums.append(total(square) * square_scale)
     trials = len(sums)
     squares[...] = place_rows([(trials * trials + k, value) for k, value in enumerate(sums)])
+    fetch.wait()
 
 
 def sum_kernel(sectors, chunk, offsets, vectors, inner, before, *rest):
@@ -89,12 +79,12 @@
     rows = states // shares
     sector = lax.axis_index("sec")
     odd = sector & 1
+    columns = slice(chunk * width, (chunk + 1) * width)
     for mask in range(0, sectors, 2):
         even_place, odd_place = turned(mask, 0, sectors), turned(mask, 1, sectors)
-        rights[jnp.where(odd == 1, odd_place, even_place)] = pieces[mask][...]
-        rights[jnp.where(odd == 1, even_place, odd_place) ^ 1] = pieces[mask + 1][...]
+        rights[jnp.where(odd == 1, odd_place, even_place)] = pieces[mask][:, :, columns]
+        rights[jnp.where(odd == 1, even_place, odd_place) ^ 1] = pieces[mask + 1][:, :, columns]
     place = lax.axis_index("term")
-    columns = slice(chunk * width, (chunk + 1) * width)
     grams = [jnp.zeros((8, width), jnp.float32) for _ in range(trials * trials)]
     for pair in range(pairs):
         result = None
@@ -195,19 +185,7 @@
     vectors, left, right = vectors[:, 0], left_ops[:, 0], right_ops[:, 0]
     width, rows = states // CHUNKS, states // shares
 
-    chunks = call(
-        split_kernel,
-        "split_columns",
-        2 * terms * trials * pairs * states**3,
-        2 * MIB,
-        4 * MIB,
-        out_shape=[jax.ShapeDtypeStruct((terms, states, width), jnp.bfloat16)] * CHUNKS,
-        in_specs=[HBM],
-        out_specs=[VMEM] * CHUNKS,
-        scratch_shapes=[pltpu.SemaphoreType.DMA((CHUNKS,))],
-    )(in_hbm(right))
-
-    inner, tile = call(
+    inner, tile, own = call(
         functools.partial(inner_kernel, 1.0 / shares),
         "inner_products",
         2 * terms * trials * pairs * states**3,
@@ -216,18 +194,18 @@
         out_shape=(
             jax.ShapeDtypeStruct((terms, trials, pairs, states, states), jnp.bfloat16),
             jax.ShapeDtypeStruct(TILE, jnp.float32),
+            jax.ShapeDtypeStruct(right.shape, jnp.bfloat16),
         ),
-        in_specs=[VMEM, VMEM],
-        out_specs=(VMEM, VMEM),
-    )(vectors, left)
+        in_specs=[VMEM, VMEM, HBM],
+        out_specs=(VMEM, VMEM, VMEM),
+        scratch_shapes=[pltpu.SemaphoreType.DMA],
+    )(vectors, left, in_hbm(right))
 
     def behind_inner(block):
         return lax.optimization_barrier((block, inner))[0]
 
-    gathered = []
-    for chunk in range(CHUNKS):
-        after = behind_inner if chunk == 0 else lambda block: block
-        gathered.append(gather_sectors(chunks[chunk], sectors, after))
+    gathered = gather_sectors(right, sectors, behind_inner)
+    gathered[0] = own
 
     def share_of(count, dtype):
         return jax.ShapeDtypeStruct((count, trials, pairs, rows, width), dtype)
@@ -251,16 +229,14 @@
                 pltpu.VMEM((sectors, terms, states, width), jnp.bfloat16),
                 pltpu.VMEM((trials, states, width), jnp.float32),
             ],
-        )(offsets, vectors, inner, tile, *gathered[chunk])
-        if arrived is not None:
-            send, arrived = lax.optimization_barrier((send, arrived))
+        )(in_hbm(offsets), vectors, inner, tile, *gathered)
         step = 1
         arrived = received = swap(send, "term", step)
         if chunk == CHUNKS - 1:
             for masks in [[1]] + steps_of(sectors, 1):
                 tile = add_places(tile, "sec", masks)
             others = tuple(parts[1::2])
-            received, tile, others = lax.optimization_barrier((received, tile, others))
+            tile, others = lax.optimization_barrier((tile, others))
             parts[1::2] = others
         while 2 * step < shares:
             step *= 2

time: 55.7 us -> 54 us (0.969)
  starting transfers between devices: 27.8 us -> 21.7 us
  waiting for transfers between devices: 17.4 us -> 22.1 us
    ppermute x25 -> x18, starting transfers between devices: 27.8 us -> 21.7 us  [swap(): lax.ppermute(value, axis, [(place, place ^ masks[place & 1]) for place in...]
    ppermute x25 -> x18, waiting for transfers between devices: 17.4 us -> 22.1 us  [swap(): lax.ppermute(value, axis, [(place, place ^ masks[place & 1]) for place in...]
    pallas_call x1 -> x0, Pallas kernels: 1.12 us -> none  [local(): call(split_kernel, 'split_columns', 2 * terms * trials * pairs * states *...]
    pallas_call x2, Pallas kernels: 3.81 us -> 4.43 us  [local(): call(functools.partial(sum_kernel, sectors, chunk), 'sum_over_terms', 2 *...]
    unnamed x8 -> x6, local copies, waits for them, and re-layouts: 2.23 us -> 2.22 us
  transfers between devices with their start and end apart: 25 -> 18, of which waited for: 13 -> 8; matrix products, arithmetic and copies ran while one was open for 0% -> 0% of each run, Pallas kernels for 10% -> 8%
where the time goes in v6:
time: 54 us; the launch traced here: 53.7 us
  waiting for transfers between devices  22.1 us (41%)
  starting transfers between devices  21.7 us (40%)
  Pallas kernels  6.97 us (13%)
  local copies, waits for them, and re-layouts  2.22 us (4%)
  between operations  0.7 us (1%)
    ppermute x18, waiting for transfers between devices, swap(): lax.ppermute(value, axis, [(place, place ^ masks[place & 1]) for place in...  22.1 us
    ppermute x18, starting transfers between devices, swap(): lax.ppermute(value, axis, [(place, place ^ masks[place & 1]) for place in...  21.7 us
    pallas_call x2, Pallas kernels, local(): call(functools.partial(sum_kernel, sectors, chunk), 'sum_over_terms', 2 *...  4.43 us
    unnamed x6, local copies, waits for them, and re-layouts  2.22 us
    pallas_call x1, Pallas kernels, local(): call(functools.partial(inner_kernel, 1.0 / shares), 'inner_products', 2 *...  1.09 us
  transfers between devices with their start and end apart: 18, of which 8 were waited for; matrix products, arithmetic and copies ran while one was open for 0% of the time, Pallas kernels for 8%

profile of v6, /device:TPU:0, one launch (start us, length us, event | category | flops | bytes accessed | tf_op | source)
XLA Modules:
  0.0 53.7 jit_solution(3385791551849121449)
XLA Ops:
  0.6 3.0 %collective-permute-start.1 = (bf16[3,256,256]{2,1,0:T(8,128)(2,1)}, bf16[3,256,256]{2,1,0:T(8,128)(2,1)S(1)}, u32[]{:S(2)}, u32[]{:S(2)}) collective-permute-start(bf16[3,256,256]{2,1,0:T(8,128)(2,1)} %bitcast.11), channel_id=1, source_target_pairs={{0,8},{4,20},{8,0},{12,28},{16,24},{20,4},{24,16},{28,12},{1,9},{5... | collective-permute-start | bytes 1179656 | tf_op jit(solution)/shard_map/ppermute | solution.py:21
  3.6 1.5 %collective-permute-start.3 = (bf16[3,256,256]{2,1,0:T(8,128)(2,1)}, bf16[3,256,256]{2,1,0:T(8,128)(2,1)S(1)}, u32[]{:S(2)}, u32[]{:S(2)}) collective-permute-start(bf16[3,256,256]{2,1,0:T(8,128)(2,1)} %bitcast.12), channel_id=1, source_target_pairs={{0,16},{4,12},{8,24},{12,4},{16,0},{20,28},{24,8},{28,20},{1,17},{... | collective-permute-start | bytes 1179656 | tf_op jit(solution)/shard_map/ppermute | solution.py:21
  5.2 1.2 %copy-done = bf16[2,1,4,256,256]{4,3,2,1,0:T(8,128)(2,1)S(1)} copy-done((bf16[2,1,4,256,256]{4,3,2,1,0:T(8,128)(2,1)S(1)}, bf16[2,1,4,256,256]{4,3,2,1,0:T(8,128)(2,1)}, u32[]{:S(2)}) %copy-start) | copy-done | bytes 1048600
  6.4 1.0 %copy-done.2 = bf16[3,1,256,256]{3,2,1,0:T(8,128)(2,1)S(1)} copy-done((bf16[3,1,256,256]{3,2,1,0:T(8,128)(2,1)S(1)}, bf16[3,1,256,256]{3,2,1,0:T(8,128)(2,1)}, u32[]{:S(2)}) %copy-start.2) | copy-done | bytes 393240
  7.4 1.1 %inner_products.1 = (bf16[3,2,4,256,256]{4,3,2,1,0:T(8,128)(2,1)S(1)}, f32[8,128]{1,0:T(8,128)S(1)}, bf16[3,256,256]{2,1,0:T(8,128)(2,1)S(1)}) custom-call(bf16[2,4,256,256]{3,2,1,0:T(8,128)(2,1)S(1)} %bitcast.6, bf16[3,256,256]{2,1,0:T(8,128)(2,1)S(1)} %bitcast.9, bf16[3,256,256]{2,1,0:T(8,128)(2,1)} %bitcast.13), custom_call_target="tpu_custom_call" | custom-call | flops 805306368 | bytes 5242880 | tf_op jit(solution)/shard_map/inner_products/pallas_call | solution.py:188
  8.5 4.9 %collective-permute-done.1.rest_2_ = bf16[3,256,256]{2,1,0:T(8,128)(2,1)S(1)} collective-permute-done((bf16[3,256,256]{2,1,0:T(8,128)(2,1)}, bf16[3,256,256]{2,1,0:T(8,128)(2,1)S(1)}, u32[]{:S(2)}, u32[]{:S(2)}) %collective-permute-start.1) | collective-permute-done | bytes 393248 | tf_op jit(solution)/shard_map/ppermute | solution.py:21
  13.3 1.5 %collective-permute-start.5 = (bf16[3,256,256]{2,1,0:T(8,128)(2,1)S(1)}, bf16[3,256,256]{2,1,0:T(8,128)(2,1)S(1)}, u32[]{:S(2)}, u32[]{:S(2)}) collective-permute-start(bf16[3,256,256]{2,1,0:T(8,128)(2,1)S(1)} %collective-permute-done.1.rest_2_), channel_id=1, source_target_pairs={{0,16},{4,12},{8,24},{12,4},{16,0},{20,28},{24,8},{28,20},{1,17},{... | collective-permute-start | bytes 1179656 | tf_op jit(solution)/shard_map/ppermute | solution.py:21
  15.3 5.8 %collective-permute-done.5.rest_6_ = bf16[3,256,256]{2,1,0:T(8,128)(2,1)S(1)} collective-permute-done((bf16[3,256,256]{2,1,0:T(8,128)(2,1)S(1)}, bf16[3,256,256]{2,1,0:T(8,128)(2,1)S(1)}, u32[]{:S(2)}, u32[]{:S(2)}) %collective-permute-start.5) | collective-permute-done | bytes 393248 | tf_op jit(solution)/shard_map/ppermute | solution.py:21
  21.1 1.7 %collective-permute-done.6.rest_7_ = bf16[3,256,256]{2,1,0:T(8,128)(2,1)S(1)} collective-permute-done((bf16[3,256,256]{2,1,0:T(8,128)(2,1)S(1)}, bf16[3,256,256]{2,1,0:T(8,128)(2,1)S(1)}, u32[]{:S(2)}, u32[]{:S(2)}) %collective-permute-start.6) | collective-permute-done | bytes 393248 | tf_op jit(solution)/shard_map/ppermute | solution.py:21
  22.9 2.2 %sum_over_terms.2 = (f32[2,2,4,64,128]{4,3,2,1,0:T(8,128)S(1)}, bf16[2,2,4,64,128]{4,3,2,1,0:T(8,128)(2,1)S(1)}, f32[8,128]{1,0:T(8,128)S(1)}) custom-call(s32[3,4]{1,0:T(4,128)} %offsets.3, bf16[2,4,256,256]{3,2,1,0:T(8,128)(2,1)S(1)} %bitcast.7, bf16[3,2,4,256,256]{4,3,2,1,0:T(8,128)(2,1)S(1)} %get-tuple-element.18.inner, ...), custom_call_target="tpu_custom_call" | custom-call | flops 402653184 | bytes 4194304 | tf_op jit(solution)/shard_map/sum_over_terms/pallas_call | solution.py:215
  25.1 2.5 %collective-permute-start.7 = (bf16[2,2,4,64,128]{4,3,2,1,0:T(8,128)(2,1)S(1)}, bf16[2,2,4,64,128]{4,3,2,1,0:T(8,128)(2,1)S(1)}, u32[]{:S(2)}, u32[]{:S(2)}) collective-permute-start(bf16[2,2,4,64,128]{4,3,2,1,0:T(8,128)(2,1)S(1)} %get-tuple-element.23), channel_id=1, source_target_pairs={{0,1},{1,0},{2,3},{3,2},{4,5},{5,4},{6,7},{7,6},{8,9},{9,8},{10,11... | collective-permute-start | bytes 786440 | tf_op jit(solution)/shard_map/ppermute | solution.py:21
  27.6 2.2 %sum_over_terms.3 = (f32[2,2,4,64,128]{4,3,2,1,0:T(8,128)S(1)}, bf16[2,2,4,64,128]{4,3,2,1,0:T(8,128)(2,1)S(1)}, f32[8,128]{1,0:T(8,128)S(1)}) custom-call(s32[3,4]{1,0:T(4,128)} %offsets.3, bf16[2,4,256,256]{3,2,1,0:T(8,128)(2,1)S(1)} %bitcast.8, bf16[3,2,4,256,256]{4,3,2,1,0:T(8,128)(2,1)S(1)} %get-tuple-element.18.inner, ...), custom_call_target="tpu_custom_call" | custom-call | flops 402653184 | bytes 4194304 | tf_op jit(solution)/shard_map/sum_over_terms/pallas_call | solution.py:215
  29.9 1.2 %collective-permute-done.8 = f32[8,128]{1,0:T(8,128)S(1)} collective-permute-done((f32[8,128]{1,0:T(8,128)S(1)}, f32[8,128]{1,0:T(8,128)S(1)}, u32[]{:S(2)}, u32[]{:S(2)}) %collective-permute-start.8) | collective-permute-done | bytes 4128 | tf_op jit(solution)/shard_map/ppermute | solution.py:21
  31.0 2.0 %collective-permute-start.11 = (f32[8,128]{1,0:T(8,128)S(1)}, f32[8,128]{1,0:T(8,128)S(1)}, u32[]{:S(2)}, u32[]{:S(2)}) collective-permute-start(f32[8,128]{1,0:T(8,128)S(1)} %add.12), channel_id=1, source_target_pairs={{0,24},{4,28},{8,16},{12,20},{16,8},{20,12},{24,0},{28,4},{1,25},{... | collective-permute-start | bytes 12296 | tf_op jit(solution)/shard_map/ppermute | solution.py:21
  33.1 1.3 %collective-permute-start.10 = (f32[8,128]{1,0:T(8,128)S(1)}, f32[8,128]{1,0:T(8,128)S(1)}, u32[]{:S(2)}, u32[]{:S(2)}) collective-permute-start(f32[8,128]{1,0:T(8,128)S(1)} %add.12), channel_id=1, source_target_pairs={{0,16},{4,20},{8,24},{12,28},{16,0},{20,4},{24,8},{28,12},{1,17},{... | collective-permute-start | bytes 12296 | tf_op jit(solution)/shard_map/ppermute | solution.py:21
  34.7 3.1 %collective-permute-start.12 = (bf16[1,2,4,64,128]{4,3,2,1,0:T(8,128)(2,1)S(1)}, bf16[1,2,4,64,128]{4,3,2,1,0:T(8,128)(2,1)S(1)}, u32[]{:S(2)}, u32[]{:S(2)}) collective-permute-start(bf16[1,2,4,64,128]{4,3,2,1,0:T(8,128)(2,1)S(1)} %get-tuple-element.27), channel_id=1, source_target_pairs={{0,2},{1,3},{2,0},{3,1},{4,6},{5,7},{6,4},{7,5},{8,10},{9,11},{10,... | collective-permute-start | bytes 393224 | tf_op jit(solution)/shard_map/ppermute | solution.py:21
  37.9 4.7 %collective-permute-done.13.received = bf16[2,2,4,64,128]{4,3,2,1,0:T(8,128)(2,1)S(1)} collective-permute-done((bf16[2,2,4,64,128]{4,3,2,1,0:T(8,128)(2,1)S(1)}, bf16[2,2,4,64,128]{4,3,2,1,0:T(8,128)(2,1)S(1)}, u32[]{:S(2)}, u32[]{:S(2)}) %collective-permute-start.13) | collective-permute-done | bytes 262176 | tf_op jit(solution)/shard_map/ppermute | solution.py:21
  42.6 1.0 %collective-permute-start.14 = (bf16[1,2,4,64,128]{4,3,2,1,0:T(8,128)(2,1)S(1)}, bf16[1,2,4,64,128]{4,3,2,1,0:T(8,128)(2,1)S(1)}, u32[]{:S(2)}, u32[]{:S(2)}) collective-permute-start(bf16[1,2,4,64,128]{4,3,2,1,0:T(8,128)(2,1)S(1)} %get-tuple-element.32), channel_id=1, source_target_pairs={{0,2},{1,3},{2,0},{3,1},{4,6},{5,7},{6,4},{7,5},{8,10},{9,11},{10,... | collective-permute-start | bytes 393224 | tf_op jit(solution)/shard_map/ppermute | solution.py:21
  43.7 2.5 %collective-permute-start.15 = (f32[8,128]{1,0:T(8,128)S(1)}, f32[8,128]{1,0:T(8,128)S(1)}, u32[]{:S(2)}, u32[]{:S(2)}) collective-permute-start(f32[8,128]{1,0:T(8,128)S(1)} %add_add_fusion.refs_0_), channel_id=1, source_target_pairs={{0,1},{1,0},{2,3},{3,2},{4,5},{5,4},{6,7},{7,6},{8,9},{9,8},{10,11... | collective-permute-start | bytes 12296 | tf_op jit(solution)/shard_map/ppermute | solution.py:21
  46.2 1.5 %collective-permute-start.16 = (f32[8,128]{1,0:T(8,128)S(1)}, f32[8,128]{1,0:T(8,128)S(1)}, u32[]{:S(2)}, u32[]{:S(2)}) collective-permute-start(f32[8,128]{1,0:T(8,128)S(1)} %add_add_fusion.refs_0_), channel_id=1, source_target_pairs={{0,2},{1,3},{2,0},{3,1},{4,6},{5,7},{6,4},{7,5},{8,10},{9,11},{10,... | collective-permute-start | bytes 12296 | tf_op jit(solution)/shard_map/ppermute | solution.py:21
  47.7 1.0 %collective-permute-start.17 = (f32[8,128]{1,0:T(8,128)S(1)}, f32[8,128]{1,0:T(8,128)S(1)}, u32[]{:S(2)}, u32[]{:S(2)}) collective-permute-start(f32[8,128]{1,0:T(8,128)S(1)} %add_add_fusion.refs_0_), channel_id=1, source_target_pairs={{0,3},{1,2},{2,1},{3,0},{4,7},{5,6},{6,5},{7,4},{8,11},{9,10},{10,... | collective-permute-start | bytes 12296 | tf_op jit(solution)/shard_map/ppermute | solution.py:21
  48.7 2.9 %collective-permute-done.14.refs_3_ = bf16[1,2,4,64,128]{4,3,2,1,0:T(8,128)(2,1)S(1)} collective-permute-done((bf16[1,2,4,64,128]{4,3,2,1,0:T(8,128)(2,1)S(1)}, bf16[1,2,4,64,128]{4,3,2,1,0:T(8,128)(2,1)S(1)}, u32[]{:S(2)}, u32[]{:S(2)}) %collective-permute-start.14) | collective-permute-done | bytes 131104 | tf_op jit(solution)/shard_map/ppermute | solution.py:21
  51.5 0.8 %add_last_share.1 = bf16[2,4,64,256]{3,2,1,0:T(8,128)(2,1)} custom-call(f32[1,2,4,64,128]{4,3,2,1,0:T(8,128)S(1)} %get-tuple-element.24.refs_0_, bf16[1,2,4,64,128]{4,3,2,1,0:T(8,128)(2,1)S(1)} %collective-permute-done.12.refs_1_, f32[1,2,4,64,128]{4,3,2,1,0:T(8,128)S(1)} %get-tuple-element.31.refs_2_, ...), custom_call_target="tpu_custom_call" | custom-call | flops 1 | bytes 1 | tf_op jit(solution)/shard_map/add_last_share/pallas_call | solution.py:271
  52.3 0.8 %collective-permute-done.17.refs_3_ = f32[8,128]{1,0:T(8,128)S(1)} collective-permute-done((f32[8,128]{1,0:T(8,128)S(1)}, f32[8,128]{1,0:T(8,128)S(1)}, u32[]{:S(2)}, u32[]{:S(2)}) %collective-permute-start.17) | collective-permute-done | bytes 4128 | tf_op jit(solution)/shard_map/ppermute | solution.py:21
  (27 shorter events, 1.6 us)
Async XLA Ops:
  0.6 12.7 %collective-permute-start.1 = (bf16[3,256,256]{2,1,0:T(8,128)(2,1)}, bf16[3,256,256]{2,1,0:T(8,128)(2,1)S(1)}, u32[]{:S(2)}, u32[]{:S(2)}) collective-permute-start(bf16[3,256,256]{2,1,0:T(8,128)(2,1)} %bitcast.11), channel_id=1, source_target_pairs={{0,8},{4,20},{8,0},{12,28},{16,24},{20,4},{24,16},{28,12},{1,9},{5... | collective-permute-start | bytes 1179656 | tf_op jit(solution)/shard_map/ppermute | solution.py:21
  3.6 11.7 %collective-permute-start.3 = (bf16[3,256,256]{2,1,0:T(8,128)(2,1)}, bf16[3,256,256]{2,1,0:T(8,128)(2,1)S(1)}, u32[]{:S(2)}, u32[]{:S(2)}) collective-permute-start(bf16[3,256,256]{2,1,0:T(8,128)(2,1)} %bitcast.12), channel_id=1, source_target_pairs={{0,16},{4,12},{8,24},{12,4},{16,0},{20,28},{24,8},{28,20},{1,17},{... | collective-permute-start | bytes 1179656 | tf_op jit(solution)/shard_map/ppermute | solution.py:21
  5.2 1.2 %copy-start = (bf16[2,1,4,256,256]{4,3,2,1,0:T(8,128)(2,1)S(1)}, bf16[2,1,4,256,256]{4,3,2,1,0:T(8,128)(2,1)}, u32[]{:S(2)}) copy-start(bf16[2,1,4,256,256]{4,3,2,1,0:T(8,128)(2,1)} %param.4) | copy-start | bytes 3145732
  6.4 1.0 %copy-start.2 = (bf16[3,1,256,256]{3,2,1,0:T(8,128)(2,1)S(1)}, bf16[3,1,256,256]{3,2,1,0:T(8,128)(2,1)}, u32[]{:S(2)}) copy-start(bf16[3,1,256,256]{3,2,1,0:T(8,128)(2,1)} %param.5) | copy-start | bytes 1179652
  7.4 15.5 %copy-start.1 = (bf16[2,1,4,256,256]{4,3,2,1,0:T(8,128)(2,1)S(1)}, bf16[2,1,4,256,256]{4,3,2,1,0:T(8,128)(2,1)}, u32[]{:S(2)}) copy-start(bf16[2,1,4,256,256]{4,3,2,1,0:T(8,128)(2,1)} %param.4) | copy-start | bytes 3145732
  13.3 7.8 %collective-permute-start.5 = (bf16[3,256,256]{2,1,0:T(8,128)(2,1)S(1)}, bf16[3,256,256]{2,1,0:T(8,128)(2,1)S(1)}, u32[]{:S(2)}, u32[]{:S(2)}) collective-permute-start(bf16[3,256,256]{2,1,0:T(8,128)(2,1)S(1)} %collective-permute-done.1.rest_2_), channel_id=1, source_target_pairs={{0,16},{4,12},{8,24},{12,4},{16,0},{20,28},{24,8},{28,20},{1,17},{... | collective-permute-start | bytes 1179656 | tf_op jit(solution)/shard_map/ppermute | solution.py:21
  14.8 6.3 %collective-permute-start = (bf16[3,256,256]{2,1,0:T(8,128)(2,1)}, bf16[3,256,256]{2,1,0:T(8,128)(2,1)S(1)}, u32[]{:S(2)}, u32[]{:S(2)}) collective-permute-start(bf16[3,256,256]{2,1,0:T(8,128)(2,1)} %bitcast.14), channel_id=1, source_target_pairs={{0,4},{4,0},{8,12},{12,8},{16,20},{20,16},{24,28},{28,24},{1,5},{5... | collective-permute-start | bytes 1179656 | tf_op jit(solution)/shard_map/ppermute | solution.py:21
  14.8 6.3 %collective-permute-start.2 = (bf16[3,256,256]{2,1,0:T(8,128)(2,1)S(1)}, bf16[3,256,256]{2,1,0:T(8,128)(2,1)S(1)}, u32[]{:S(2)}, u32[]{:S(2)}) collective-permute-start(bf16[3,256,256]{2,1,0:T(8,128)(2,1)S(1)} %collective-permute-done.1.rest_2_), channel_id=1, source_target_pairs={{0,4},{4,0},{8,12},{12,8},{16,20},{20,16},{24,28},{28,24},{1,5},{5... | collective-permute-start | bytes 1179656 | tf_op jit(solution)/shard_map/ppermute | solution.py:21
  15.3 5.8 %collective-permute-start.4 = (bf16[3,256,256]{2,1,0:T(8,128)(2,1)S(1)}, bf16[3,256,256]{2,1,0:T(8,128)(2,1)S(1)}, u32[]{:S(2)}, u32[]{:S(2)}) collective-permute-start(bf16[3,256,256]{2,1,0:T(8,128)(2,1)S(1)} %collective-permute-done.3.rest_4_), channel_id=1, source_target_pairs={{0,4},{4,0},{8,12},{12,8},{16,20},{20,16},{24,28},{28,24},{1,5},{5... | collective-permute-start | bytes 1179656 | tf_op jit(solution)/shard_map/ppermute | solution.py:21
  21.1 1.7 %collective-permute-start.6 = (bf16[3,256,256]{2,1,0:T(8,128)(2,1)S(1)}, bf16[3,256,256]{2,1,0:T(8,128)(2,1)S(1)}, u32[]{:S(2)}, u32[]{:S(2)}) collective-permute-start(bf16[3,256,256]{2,1,0:T(8,128)(2,1)S(1)} %collective-permute-done.5.rest_6_), channel_id=1, source_target_pairs={{0,4},{4,0},{8,12},{12,8},{16,20},{20,16},{24,28},{28,24},{1,5},{5... | collective-permute-start | bytes 1179656 | tf_op jit(solution)/shard_map/ppermute | solution.py:21
  25.1 9.6 %collective-permute-start.7 = (bf16[2,2,4,64,128]{4,3,2,1,0:T(8,128)(2,1)S(1)}, bf16[2,2,4,64,128]{4,3,2,1,0:T(8,128)(2,1)S(1)}, u32[]{:S(2)}, u32[]{:S(2)}) collective-permute-start(bf16[2,2,4,64,128]{4,3,2,1,0:T(8,128)(2,1)S(1)} %get-tuple-element.23), channel_id=1, source_target_pairs={{0,1},{1,0},{2,3},{3,2},{4,5},{5,4},{6,7},{7,6},{8,9},{9,8},{10,11... | collective-permute-start | bytes 786440 | tf_op jit(solution)/shard_map/ppermute | solution.py:21
  29.8 12.8 %collective-permute-start.13 = (bf16[2,2,4,64,128]{4,3,2,1,0:T(8,128)(2,1)S(1)}, bf16[2,2,4,64,128]{4,3,2,1,0:T(8,128)(2,1)S(1)}, u32[]{:S(2)}, u32[]{:S(2)}) collective-permute-start(bf16[2,2,4,64,128]{4,3,2,1,0:T(8,128)(2,1)S(1)} %get-tuple-element.30), channel_id=1, source_target_pairs={{0,1},{1,0},{2,3},{3,2},{4,5},{5,4},{6,7},{7,6},{8,9},{9,8},{10,11... | collective-permute-start | bytes 786440 | tf_op jit(solution)/shard_map/ppermute | solution.py:21
  29.8 1.2 %collective-permute-start.8 = (f32[8,128]{1,0:T(8,128)S(1)}, f32[8,128]{1,0:T(8,128)S(1)}, u32[]{:S(2)}, u32[]{:S(2)}) collective-permute-start(f32[8,128]{1,0:T(8,128)S(1)} %get-tuple-element.26), channel_id=1, source_target_pairs={{0,4},{4,0},{8,12},{12,8},{16,20},{20,16},{24,28},{28,24},{1,5},{5... | collective-permute-start | bytes 12296 | tf_op jit(solution)/shard_map/ppermute | solution.py:21
  31.0 12.6 %collective-permute-start.11 = (f32[8,128]{1,0:T(8,128)S(1)}, f32[8,128]{1,0:T(8,128)S(1)}, u32[]{:S(2)}, u32[]{:S(2)}) collective-permute-start(f32[8,128]{1,0:T(8,128)S(1)} %add.12), channel_id=1, source_target_pairs={{0,24},{4,28},{8,16},{12,20},{16,8},{20,12},{24,0},{28,4},{1,25},{... | collective-permute-start | bytes 12296 | tf_op jit(solution)/shard_map/ppermute | solution.py:21
  33.1 10.6 %collective-permute-start.10 = (f32[8,128]{1,0:T(8,128)S(1)}, f32[8,128]{1,0:T(8,128)S(1)}, u32[]{:S(2)}, u32[]{:S(2)}) collective-permute-start(f32[8,128]{1,0:T(8,128)S(1)} %add.12), channel_id=1, source_target_pairs={{0,16},{4,20},{8,24},{12,28},{16,0},{20,4},{24,8},{28,12},{1,17},{... | collective-permute-start | bytes 12296 | tf_op jit(solution)/shard_map/ppermute | solution.py:21
  34.4 9.3 %collective-permute-start.9 = (f32[8,128]{1,0:T(8,128)S(1)}, f32[8,128]{1,0:T(8,128)S(1)}, u32[]{:S(2)}, u32[]{:S(2)}) collective-permute-start(f32[8,128]{1,0:T(8,128)S(1)} %add.12), channel_id=1, source_target_pairs={{0,8},{4,12},{8,0},{12,4},{16,24},{20,28},{24,16},{28,20},{1,9},{5... | collective-permute-start | bytes 12296 | tf_op jit(solution)/shard_map/ppermute | solution.py:21
  34.7 9.0 %collective-permute-start.12 = (bf16[1,2,4,64,128]{4,3,2,1,0:T(8,128)(2,1)S(1)}, bf16[1,2,4,64,128]{4,3,2,1,0:T(8,128)(2,1)S(1)}, u32[]{:S(2)}, u32[]{:S(2)}) collective-permute-start(bf16[1,2,4,64,128]{4,3,2,1,0:T(8,128)(2,1)S(1)} %get-tuple-element.27), channel_id=1, source_target_pairs={{0,2},{1,3},{2,0},{3,1},{4,6},{5,7},{6,4},{7,5},{8,10},{9,11},{10,... | collective-permute-start | bytes 393224 | tf_op jit(solution)/shard_map/ppermute | solution.py:21
  42.6 8.9 %collective-permute-start.14 = (bf16[1,2,4,64,128]{4,3,2,1,0:T(8,128)(2,1)S(1)}, bf16[1,2,4,64,128]{4,3,2,1,0:T(8,128)(2,1)S(1)}, u32[]{:S(2)}, u32[]{:S(2)}) collective-permute-start(bf16[1,2,4,64,128]{4,3,2,1,0:T(8,128)(2,1)S(1)} %get-tuple-element.32), channel_id=1, source_target_pairs={{0,2},{1,3},{2,0},{3,1},{4,6},{5,7},{6,4},{7,5},{8,10},{9,11},{10,... | collective-permute-start | bytes 393224 | tf_op jit(solution)/shard_map/ppermute | solution.py:21
  43.7 8.6 %collective-permute-start.15 = (f32[8,128]{1,0:T(8,128)S(1)}, f32[8,128]{1,0:T(8,128)S(1)}, u32[]{:S(2)}, u32[]{:S(2)}) collective-permute-start(f32[8,128]{1,0:T(8,128)S(1)} %add_add_fusion.refs_0_), channel_id=1, source_target_pairs={{0,1},{1,0},{2,3},{3,2},{4,5},{5,4},{6,7},{7,6},{8,9},{9,8},{10,11... | collective-permute-start | bytes 12296 | tf_op jit(solution)/shard_map/ppermute | solution.py:21
  46.2 6.1 %collective-permute-start.16 = (f32[8,128]{1,0:T(8,128)S(1)}, f32[8,128]{1,0:T(8,128)S(1)}, u32[]{:S(2)}, u32[]{:S(2)}) collective-permute-start(f32[8,128]{1,0:T(8,128)S(1)} %add_add_fusion.refs_0_), channel_id=1, source_target_pairs={{0,2},{1,3},{2,0},{3,1},{4,6},{5,7},{6,4},{7,5},{8,10},{9,11},{10,... | collective-permute-start | bytes 12296 | tf_op jit(solution)/shard_map/ppermute | solution.py:21
  47.7 5.4 %collective-permute-start.17 = (f32[8,128]{1,0:T(8,128)S(1)}, f32[8,128]{1,0:T(8,128)S(1)}, u32[]{:S(2)}, u32[]{:S(2)}) collective-permute-start(f32[8,128]{1,0:T(8,128)S(1)} %add_add_fusion.refs_0_), channel_id=1, source_target_pairs={{0,3},{1,2},{2,1},{3,0},{4,7},{5,6},{6,5},{7,4},{8,11},{9,10},{10,... | collective-permute-start | bytes 12296 | tf_op jit(solution)/shard_map/ppermute | solution.py:21

commit v7 on v6

--- a/solution.py
+++ b/solution.py
@@ -9,7 +9,6 @@
 
 MIB = 1 << 20
 TILE = (8, 128)
-CHUNKS = 2
 VMEM = pl.BlockSpec(memory_space=pltpu.VMEM)
 SMEM = pl.BlockSpec(memory_space=pltpu.SMEM)
 HBM = pl.BlockSpec(memory_space=pltpu.HBM)
@@ -32,9 +31,8 @@
     held = {0: own}
     for mask in range(2, sectors, 2):
         step = 1 << (mask.bit_length() - 1)
-        held[mask] = swap(held[mask ^ step], "sec", step, sectors)
-        if mask == 2:
-            held[mask] = after(held[mask])
+        sent = after(own) if mask == 4 else held[mask ^ step]
+        held[mask] = swap(sent, "sec", step, sectors)
     return [block for mine in held.values() for block in (mine, swap(mine, "sec", 1))]
 
 
@@ -70,23 +68,28 @@
     fetch.wait()
 
 
-def sum_kernel(sectors, chunk, offsets, vectors, inner, before, *rest):
-    pieces = rest[:sectors]
-    keep, send, tile, rights, partial = rest[sectors:]
-    terms, trials, pairs, states, _ = inner.shape
-    width = partial.shape[2]
+def place_blocks(sectors, pieces, rights):
+    odd = lax.axis_index("sec") & 1
+    for mask in range(0, sectors, 2):
+        even_place, odd_place = turned(mask, 0, sectors), turned(mask, 1, sectors)
+        rights[jnp.where(odd == 1, odd_place, even_place)] = pieces[mask][...]
+        rights[jnp.where(odd == 1, even_place, odd_place) ^ 1] = pieces[mask + 1][...]
+
+
+def sum_kernel(sectors, first, offsets, vectors, inner, before, *rest):
+    if first == 0:
+        *pieces, keep, send, tile, rights, partial = rest
+        place_blocks(sectors, pieces, rights)
+    else:
+        rights, keep, send, tile, partial = rest
+    terms, trials, _, states, _ = inner.shape
     shares = 2 * keep.shape[0]
     rows = states // shares
     sector = lax.axis_index("sec")
-    odd = sector & 1
-    columns = slice(chunk * width, (chunk + 1) * width)
-    for mask in range(0, sectors, 2):
-        even_place, odd_place = turned(mask, 0, sectors), turned(mask, 1, sectors)
-        rights[jnp.where(odd == 1, odd_place, even_place)] = pieces[mask][:, :, columns]
-        rights[jnp.where(odd == 1, even_place, odd_place) ^ 1] = pieces[mask + 1][:, :, columns]
     place = lax.axis_index("term")
-    grams = [jnp.zeros((8, width), jnp.float32) for _ in range(trials * trials)]
-    for pair in range(pairs):
+    grams = [jnp.zeros((8, states), jnp.float32) for _ in range(trials * trials)]
+    for local_pair in range(keep.shape[2]):
+        pair = first + local_pair
         result = None
         for term in range(terms):
             wanted = (sector + offsets[term, pair]) & (sectors - 1)
@@ -96,19 +99,19 @@
                 preferred_element_type=jnp.float32,
             )
             result = added if result is None else result + added
-        partial[...] = result.reshape(trials, states, width)
+        partial[...] = result.reshape(trials, states, states)
         for j in range(trials):
             product = partial[j]
             for i in range(trials):
-                spread = vectors[i, pair, :, columns].astype(jnp.float32) * product
-                grams[i * trials + j] += jnp.sum(spread.reshape(-1, 8, width), axis=0)
+                spread = vectors[i, pair].astype(jnp.float32) * product
+                grams[i * trials + j] += jnp.sum(spread.reshape(-1, 8, states), axis=0)
         for mask in range(shares):
             start = pl.multiple_of((place ^ mask) * rows, rows)
             share = partial[:, pl.ds(start, rows)]
             if mask & 1:
-                send[mask // 2, :, pair] = share.astype(jnp.bfloat16)
+                send[mask // 2, :, local_pair] = share.astype(jnp.bfloat16)
             else:
-                keep[mask // 2, :, pair] = share
+                keep[mask // 2, :, local_pair] = share
     tile[...] = before[...] + place_rows([(k, total(value)) for k, value in enumerate(grams)])
 
 
@@ -123,11 +126,11 @@
 
 def finish_kernel(*refs):
     *parts, products = refs
-    width = products.shape[-1] // (len(parts) // 2)
-    for chunk in range(len(parts) // 2):
-        kept, received = parts[2 * chunk : 2 * chunk + 2]
+    first = 0
+    for kept, received in zip(parts[::2], parts[1::2]):
         both = kept[0] + received[0].astype(jnp.float32)
-        products[:, :, :, chunk * width : (chunk + 1) * width] = both.astype(jnp.bfloat16)
+        products[:, first : first + both.shape[1]] = both.astype(jnp.bfloat16)
+        first += both.shape[1]
 
 
 def rayleigh_kernel(*refs):
@@ -165,6 +168,10 @@
         steps.append([unit, 2 * unit, 3 * unit] if 2 * unit < count else [unit])
         low += 2
     return steps
+
+
+def chunk_sizes(pairs):
+    return [pairs // 2, pairs - pairs // 2]
 
 
 def call(kernel, name, flops, moved, limit, **kwargs):
@@ -183,7 +190,7 @@
     trials, _, pairs, states, _ = vectors.shape
     terms = left_ops.shape[0]
     vectors, left, right = vectors[:, 0], left_ops[:, 0], right_ops[:, 0]
-    width, rows = states // CHUNKS, states // shares
+    rows = states // shares
 
     inner, tile, own = call(
         functools.partial(inner_kernel, 1.0 / shares),
@@ -207,32 +214,37 @@
     gathered = gather_sectors(right, sectors, behind_inner)
     gathered[0] = own
 
-    def share_of(count, dtype):
-        return jax.ShapeDtypeStruct((count, trials, pairs, rows, width), dtype)
-
-    parts, arrived = [], None
-    for chunk in range(CHUNKS):
-        keep, send, tile = call(
-            functools.partial(sum_kernel, sectors, chunk),
+    def share_of(count, size, dtype):
+        return jax.ShapeDtypeStruct((count, trials, size, rows, states), dtype)
+
+    rights_shape = (sectors, terms, states, states)
+    sizes = chunk_sizes(pairs)
+    parts, rights, first = [], None, 0
+    for size in sizes:
+        outs = [
+            share_of(shares // 2, size, jnp.float32),
+            share_of(shares // 2, size, jnp.bfloat16),
+            jax.ShapeDtypeStruct(TILE, jnp.float32),
+        ]
+        blocks = gathered if first == 0 else [rights]
+        if first == 0:
+            outs.append(jax.ShapeDtypeStruct(rights_shape, jnp.bfloat16))
+        keep, send, tile, *placed = call(
+            functools.partial(sum_kernel, sectors, first),
             "sum_over_terms",
-            2 * terms * trials * pairs * states * states * width,
+            2 * terms * trials * size * states**3,
             4 * MIB,
-            sectors * terms * states * width * 2 + 12 * MIB,
-            out_shape=(
-                share_of(shares // 2, jnp.float32),
-                share_of(shares // 2, jnp.bfloat16),
-                jax.ShapeDtypeStruct(TILE, jnp.float32),
-            ),
-            in_specs=[SMEM, VMEM, VMEM, VMEM] + [VMEM] * sectors,
-            out_specs=(VMEM, VMEM, VMEM),
-            scratch_shapes=[
-                pltpu.VMEM((sectors, terms, states, width), jnp.bfloat16),
-                pltpu.VMEM((trials, states, width), jnp.float32),
-            ],
-        )(in_hbm(offsets), vectors, inner, tile, *gathered)
+            12 * MIB,
+            out_shape=outs,
+            in_specs=[SMEM, VMEM, VMEM, VMEM] + [VMEM] * len(blocks),
+            out_specs=[VMEM] * len(outs),
+            scratch_shapes=[pltpu.VMEM((trials, states, states), jnp.float32)],
+        )(in_hbm(offsets), vectors, inner, tile, *blocks)
+        rights = placed[0] if placed else rights
+        first += size
         step = 1
-        arrived = received = swap(send, "term", step)
-        if chunk == CHUNKS - 1:
+        received = swap(send, "term", step)
+        if first == pairs:
             for masks in [[1]] + steps_of(sectors, 1):
                 tile = add_places(tile, "sec", masks)
             others = tuple(parts[1::2])
@@ -247,7 +259,7 @@
                 1,
                 1,
                 8 * MIB,
-                out_shape=(share_of(count, jnp.float32), share_of(count, jnp.bfloat16)),
+                out_shape=(share_of(count, size, jnp.float32), share_of(count, size, jnp.bfloat16)),
                 in_specs=[VMEM, VMEM],
                 out_specs=(VMEM, VMEM),
             )(keep, received)

time: 54 us -> 50 us (0.926)
  waiting for transfers between devices: 22.1 us -> 19.1 us
  Pallas kernels: 6.97 us -> 5.79 us
    ppermute x18, waiting for transfers between devices: 22.1 us -> 19.1 us  [swap(): lax.ppermute(value, axis, [(place, place ^ masks[place & 1]) for place in...]
    pallas_call x2, Pallas kernels: 4.43 us -> 3.34 us  [local(): call(functools.partial(sum_kernel, sectors, first), 'sum_over_terms', 2 *...]
    unnamed x6 -> x4, local copies, waits for them, and re-layouts: 2.22 us -> 2.22 us
  transfers between devices with their start and end apart: 18 -> 18, of which waited for: 8 -> 8; matrix products, arithmetic and copies ran while one was open for 0% -> 0% of each run, Pallas kernels for 8% -> 7%
where the time goes in v7:
time: 50 us; the launch traced here: 49.7 us
  starting transfers between devices  21.8 us (44%)
  waiting for transfers between devices  19.1 us (38%)
  Pallas kernels  5.79 us (12%)
  local copies, waits for them, and re-layouts  2.22 us (4%)
  between operations  0.7 us (1%)
    ppermute x18, starting transfers between devices, swap(): lax.ppermute(value, axis, [(place, place ^ masks[place & 1]) for place in...  21.8 us
    ppermute x18, waiting for transfers between devices, swap(): lax.ppermute(value, axis, [(place, place ^ masks[place & 1]) for place in...  19.1 us
    pallas_call x2, Pallas kernels, local(): call(functools.partial(sum_kernel, sectors, first), 'sum_over_terms', 2 *...  3.34 us
    unnamed x4, local copies, waits for them, and re-layouts  2.22 us
    pallas_call x1, Pallas kernels, local(): call(functools.partial(inner_kernel, 1.0 / shares), 'inner_products', 2 *...  1 us
  transfers between devices with their start and end apart: 18, of which 8 were waited for; matrix products, arithmetic and copies ran while one was open for 0% of the time, Pallas kernels for 7%

profile of v7, /device:TPU:0, one launch (start us, length us, event | category | flops | bytes accessed | tf_op | source)
XLA Modules:
  0.0 49.7 jit_solution(17456455425140137620)
XLA Ops:
  0.6 3.0 %collective-permute-start.1 = (bf16[3,256,256]{2,1,0:T(8,128)(2,1)}, bf16[3,256,256]{2,1,0:T(8,128)(2,1)S(1)}, u32[]{:S(2)}, u32[]{:S(2)}) collective-permute-start(bf16[3,256,256]{2,1,0:T(8,128)(2,1)} %bitcast.11), channel_id=1, source_target_pairs={{0,8},{4,20},{8,0},{12,28},{16,24},{20,4},{24,16},{28,12},{1,9},{5... | collective-permute-start | bytes 1179656 | tf_op jit(solution)/shard_map/ppermute | solution.py:20
  3.6 1.2 %copy-done = bf16[2,1,4,256,256]{4,3,2,1,0:T(8,128)(2,1)S(1)} copy-done((bf16[2,1,4,256,256]{4,3,2,1,0:T(8,128)(2,1)S(1)}, bf16[2,1,4,256,256]{4,3,2,1,0:T(8,128)(2,1)}, u32[]{:S(2)}) %copy-start) | copy-done | bytes 1048600
  4.9 1.0 %copy-done.1 = bf16[3,1,256,256]{3,2,1,0:T(8,128)(2,1)S(1)} copy-done((bf16[3,1,256,256]{3,2,1,0:T(8,128)(2,1)S(1)}, bf16[3,1,256,256]{3,2,1,0:T(8,128)(2,1)}, u32[]{:S(2)}) %copy-start.1) | copy-done | bytes 393240
  5.9 1.0 %inner_products.1 = (bf16[3,2,4,256,256]{4,3,2,1,0:T(8,128)(2,1)S(1)}, f32[8,128]{1,0:T(8,128)S(1)}, bf16[3,256,256]{2,1,0:T(8,128)(2,1)S(1)}) custom-call(bf16[2,4,256,256]{3,2,1,0:T(8,128)(2,1)S(1)} %bitcast.6, bf16[3,256,256]{2,1,0:T(8,128)(2,1)S(1)} %bitcast.9, bf16[3,256,256]{2,1,0:T(8,128)(2,1)} %bitcast.12), custom_call_target="tpu_custom_call" | custom-call | flops 805306368 | bytes 5242880 | tf_op jit(solution)/shard_map/inner_products/pallas_call | solution.py:195
  6.9 1.6 %collective-permute-start.3 = (bf16[3,256,256]{2,1,0:T(8,128)(2,1)}, bf16[3,256,256]{2,1,0:T(8,128)(2,1)S(1)}, u32[]{:S(2)}, u32[]{:S(2)}) collective-permute-start(bf16[3,256,256]{2,1,0:T(8,128)(2,1)} %bitcast.13), channel_id=1, source_target_pairs={{0,16},{4,12},{8,24},{12,4},{16,0},{20,28},{24,8},{28,20},{1,17},{... | collective-permute-start | bytes 1179656 | tf_op jit(solution)/shard_map/ppermute | solution.py:20
  8.5 1.5 %collective-permute-done.1.rest_2_ = bf16[3,256,256]{2,1,0:T(8,128)(2,1)S(1)} collective-permute-done((bf16[3,256,256]{2,1,0:T(8,128)(2,1)}, bf16[3,256,256]{2,1,0:T(8,128)(2,1)S(1)}, u32[]{:S(2)}, u32[]{:S(2)}) %collective-permute-start.1) | collective-permute-done | bytes 393248 | tf_op jit(solution)/shard_map/ppermute | solution.py:20
  10.0 3.6 %collective-permute-start.5 = (bf16[3,256,256]{2,1,0:T(8,128)(2,1)S(1)}, bf16[3,256,256]{2,1,0:T(8,128)(2,1)S(1)}, u32[]{:S(2)}, u32[]{:S(2)}) collective-permute-start(bf16[3,256,256]{2,1,0:T(8,128)(2,1)S(1)} %collective-permute-done.1.rest_2_), channel_id=1, source_target_pairs={{0,16},{4,12},{8,24},{12,4},{16,0},{20,28},{24,8},{28,20},{1,17},{... | collective-permute-start | bytes 1179656 | tf_op jit(solution)/shard_map/ppermute | solution.py:20
  14.1 0.8 %collective-permute-done.3.rest_4_ = bf16[3,256,256]{2,1,0:T(8,128)(2,1)S(1)} collective-permute-done((bf16[3,256,256]{2,1,0:T(8,128)(2,1)}, bf16[3,256,256]{2,1,0:T(8,128)(2,1)S(1)}, u32[]{:S(2)}, u32[]{:S(2)}) %collective-permute-start.3) | collective-permute-done | bytes 393248 | tf_op jit(solution)/shard_map/ppermute | solution.py:20
  14.9 4.4 %collective-permute-done.5.rest_6_ = bf16[3,256,256]{2,1,0:T(8,128)(2,1)S(1)} collective-permute-done((bf16[3,256,256]{2,1,0:T(8,128)(2,1)S(1)}, bf16[3,256,256]{2,1,0:T(8,128)(2,1)S(1)}, u32[]{:S(2)}, u32[]{:S(2)}) %collective-permute-start.5) | collective-permute-done | bytes 393248 | tf_op jit(solution)/shard_map/ppermute | solution.py:20
  19.4 1.7 %collective-permute-done.6.rest_7_ = bf16[3,256,256]{2,1,0:T(8,128)(2,1)S(1)} collective-permute-done((bf16[3,256,256]{2,1,0:T(8,128)(2,1)S(1)}, bf16[3,256,256]{2,1,0:T(8,128)(2,1)S(1)}, u32[]{:S(2)}, u32[]{:S(2)}) %collective-permute-start.6) | collective-permute-done | bytes 393248 | tf_op jit(solution)/shard_map/ppermute | solution.py:20
  21.1 1.8 %sum_over_terms.2 = (f32[2,2,2,64,256]{4,3,2,1,0:T(8,128)S(1)}, bf16[2,2,2,64,256]{4,3,2,1,0:T(8,128)(2,1)S(1)}, f32[8,128]{1,0:T(8,128)S(1)}, bf16[8,3,256,256]{3,2,1,0:T(8,128)(2,1)S(1)}) custom-call(s32[3,4]{1,0:T(4,128)} %offsets.3, bf16[2,4,256,256]{3,2,1,0:T(8,128)(2,1)S(1)} %bitcast.7, bf16[3,2,4,256,256]{4,3,2,1,0:T(8,128)(2,1)S(1)} %get-tuple-element.19.inner, ...), custom_call_target="tpu_custom_call" | custom-call | flops 402653184 | bytes 4194304 | tf_op jit(solution)/shard_map/sum_over_terms/pallas_call | solution.py:232
  22.9 1.4 %collective-permute-start.7 = (bf16[2,2,2,64,256]{4,3,2,1,0:T(8,128)(2,1)S(1)}, bf16[2,2,2,64,256]{4,3,2,1,0:T(8,128)(2,1)S(1)}, u32[]{:S(2)}, u32[]{:S(2)}) collective-permute-start(bf16[2,2,2,64,256]{4,3,2,1,0:T(8,128)(2,1)S(1)} %get-tuple-element.24), channel_id=1, source_target_pairs={{0,1},{1,0},{2,3},{3,2},{4,5},{5,4},{6,7},{7,6},{8,9},{9,8},{10,11... | collective-permute-start | bytes 786440 | tf_op jit(solution)/shard_map/ppermute | solution.py:20
  24.3 1.6 %sum_over_terms.3 = (f32[2,2,2,64,256]{4,3,2,1,0:T(8,128)S(1)}, bf16[2,2,2,64,256]{4,3,2,1,0:T(8,128)(2,1)S(1)}, f32[8,128]{1,0:T(8,128)S(1)}) custom-call(s32[3,4]{1,0:T(4,128)} %offsets.3, bf16[2,4,256,256]{3,2,1,0:T(8,128)(2,1)S(1)} %bitcast.8, bf16[3,2,4,256,256]{4,3,2,1,0:T(8,128)(2,1)S(1)} %get-tuple-element.19.inner, ...), custom_call_target="tpu_custom_call" | custom-call | flops 402653184 | bytes 4194304 | tf_op jit(solution)/shard_map/sum_over_terms/pallas_call | solution.py:232
  25.8 0.7 %collective-permute-start.13 = (bf16[2,2,2,64,256]{4,3,2,1,0:T(8,128)(2,1)S(1)}, bf16[2,2,2,64,256]{4,3,2,1,0:T(8,128)(2,1)S(1)}, u32[]{:S(2)}, u32[]{:S(2)}) collective-permute-start(bf16[2,2,2,64,256]{4,3,2,1,0:T(8,128)(2,1)S(1)} %get-tuple-element.32), channel_id=1, source_target_pairs={{0,1},{1,0},{2,3},{3,2},{4,5},{5,4},{6,7},{7,6},{8,9},{9,8},{10,11... | collective-permute-start | bytes 786440 | tf_op jit(solution)/shard_map/ppermute | solution.py:20
  26.5 1.2 %collective-permute-done.8 = f32[8,128]{1,0:T(8,128)S(1)} collective-permute-done((f32[8,128]{1,0:T(8,128)S(1)}, f32[8,128]{1,0:T(8,128)S(1)}, u32[]{:S(2)}, u32[]{:S(2)}) %collective-permute-start.8) | collective-permute-done | bytes 4128 | tf_op jit(solution)/shard_map/ppermute | solution.py:20
  27.7 2.7 %collective-permute-start.11 = (f32[8,128]{1,0:T(8,128)S(1)}, f32[8,128]{1,0:T(8,128)S(1)}, u32[]{:S(2)}, u32[]{:S(2)}) collective-permute-start(f32[8,128]{1,0:T(8,128)S(1)} %add.12), channel_id=1, source_target_pairs={{0,24},{4,28},{8,16},{12,20},{16,8},{20,12},{24,0},{28,4},{1,25},{... | collective-permute-start | bytes 12296 | tf_op jit(solution)/shard_map/ppermute | solution.py:20
  30.4 0.7 %collective-permute-start.9 = (f32[8,128]{1,0:T(8,128)S(1)}, f32[8,128]{1,0:T(8,128)S(1)}, u32[]{:S(2)}, u32[]{:S(2)}) collective-permute-start(f32[8,128]{1,0:T(8,128)S(1)} %add.12), channel_id=1, source_target_pairs={{0,8},{4,12},{8,0},{12,4},{16,24},{20,28},{24,16},{28,20},{1,9},{5... | collective-permute-start | bytes 12296 | tf_op jit(solution)/shard_map/ppermute | solution.py:20
  31.2 0.9 %collective-permute-done.7.received = bf16[2,2,2,64,256]{4,3,2,1,0:T(8,128)(2,1)S(1)} collective-permute-done((bf16[2,2,2,64,256]{4,3,2,1,0:T(8,128)(2,1)S(1)}, bf16[2,2,2,64,256]{4,3,2,1,0:T(8,128)(2,1)S(1)}, u32[]{:S(2)}, u32[]{:S(2)}) %collective-permute-start.7) | collective-permute-done | bytes 262176 | tf_op jit(solution)/shard_map/ppermute | solution.py:20
  32.1 2.4 %collective-permute-start.12 = (bf16[1,2,2,64,256]{4,3,2,1,0:T(8,128)(2,1)S(1)}, bf16[1,2,2,64,256]{4,3,2,1,0:T(8,128)(2,1)S(1)}, u32[]{:S(2)}, u32[]{:S(2)}) collective-permute-start(bf16[1,2,2,64,256]{4,3,2,1,0:T(8,128)(2,1)S(1)} %get-tuple-element.29), channel_id=1, source_target_pairs={{0,2},{1,3},{2,0},{3,1},{4,6},{5,7},{6,4},{7,5},{8,10},{9,11},{10,... | collective-permute-start | bytes 393224 | tf_op jit(solution)/shard_map/ppermute | solution.py:20
  34.5 5.1 %collective-permute-done.13.received = bf16[2,2,2,64,256]{4,3,2,1,0:T(8,128)(2,1)S(1)} collective-permute-done((bf16[2,2,2,64,256]{4,3,2,1,0:T(8,128)(2,1)S(1)}, bf16[2,2,2,64,256]{4,3,2,1,0:T(8,128)(2,1)S(1)}, u32[]{:S(2)}, u32[]{:S(2)}) %collective-permute-start.13) | collective-permute-done | bytes 262176 | tf_op jit(solution)/shard_map/ppermute | solution.py:20
  39.7 0.6 %collective-permute-start.14 = (bf16[1,2,2,64,256]{4,3,2,1,0:T(8,128)(2,1)S(1)}, bf16[1,2,2,64,256]{4,3,2,1,0:T(8,128)(2,1)S(1)}, u32[]{:S(2)}, u32[]{:S(2)}) collective-permute-start(bf16[1,2,2,64,256]{4,3,2,1,0:T(8,128)(2,1)S(1)} %get-tuple-element.34), channel_id=1, source_target_pairs={{0,2},{1,3},{2,0},{3,1},{4,6},{5,7},{6,4},{7,5},{8,10},{9,11},{10,... | collective-permute-start | bytes 393224 | tf_op jit(solution)/shard_map/ppermute | solution.py:20
  40.4 3.4 %collective-permute-start.17 = (f32[8,128]{1,0:T(8,128)S(1)}, f32[8,128]{1,0:T(8,128)S(1)}, u32[]{:S(2)}, u32[]{:S(2)}) collective-permute-start(f32[8,128]{1,0:T(8,128)S(1)} %add_add_fusion.refs_0_), channel_id=1, source_target_pairs={{0,3},{1,2},{2,1},{3,0},{4,7},{5,6},{6,5},{7,4},{8,11},{9,10},{10,... | collective-permute-start | bytes 12296 | tf_op jit(solution)/shard_map/ppermute | solution.py:20
  44.9 3.5 %collective-permute-done.14.refs_3_ = bf16[1,2,2,64,256]{4,3,2,1,0:T(8,128)(2,1)S(1)} collective-permute-done((bf16[1,2,2,64,256]{4,3,2,1,0:T(8,128)(2,1)S(1)}, bf16[1,2,2,64,256]{4,3,2,1,0:T(8,128)(2,1)S(1)}, u32[]{:S(2)}, u32[]{:S(2)}) %collective-permute-start.14) | collective-permute-done | bytes 131104 | tf_op jit(solution)/shard_map/ppermute | solution.py:20
  48.3 0.7 %add_last_share.1 = bf16[2,4,64,256]{3,2,1,0:T(8,128)(2,1)} custom-call(f32[1,2,2,64,256]{4,3,2,1,0:T(8,128)S(1)} %get-tuple-element.25.refs_0_, bf16[1,2,2,64,256]{4,3,2,1,0:T(8,128)(2,1)S(1)} %collective-permute-done.12.refs_1_, f32[1,2,2,64,256]{4,3,2,1,0:T(8,128)S(1)} %get-tuple-element.33.refs_2_, ...), custom_call_target="tpu_custom_call" | custom-call | flops 1 | bytes 1 | tf_op jit(solution)/shard_map/add_last_share/pallas_call | solution.py:283
  (25 shorter events, 2.3 us)
Async XLA Ops:
  0.6 9.4 %collective-permute-start.1 = (bf16[3,256,256]{2,1,0:T(8,128)(2,1)}, bf16[3,256,256]{2,1,0:T(8,128)(2,1)S(1)}, u32[]{:S(2)}, u32[]{:S(2)}) collective-permute-start(bf16[3,256,256]{2,1,0:T(8,128)(2,1)} %bitcast.11), channel_id=1, source_target_pairs={{0,8},{4,20},{8,0},{12,28},{16,24},{20,4},{24,16},{28,12},{1,9},{5... | collective-permute-start | bytes 1179656 | tf_op jit(solution)/shard_map/ppermute | solution.py:20
  3.6 1.2 %copy-start = (bf16[2,1,4,256,256]{4,3,2,1,0:T(8,128)(2,1)S(1)}, bf16[2,1,4,256,256]{4,3,2,1,0:T(8,128)(2,1)}, u32[]{:S(2)}) copy-start(bf16[2,1,4,256,256]{4,3,2,1,0:T(8,128)(2,1)} %param.4) | copy-start | bytes 3145732
  4.9 1.0 %copy-start.1 = (bf16[3,1,256,256]{3,2,1,0:T(8,128)(2,1)S(1)}, bf16[3,1,256,256]{3,2,1,0:T(8,128)(2,1)}, u32[]{:S(2)}) copy-start(bf16[3,1,256,256]{3,2,1,0:T(8,128)(2,1)} %param.5) | copy-start | bytes 1179652
  6.9 8.1 %collective-permute-start.3 = (bf16[3,256,256]{2,1,0:T(8,128)(2,1)}, bf16[3,256,256]{2,1,0:T(8,128)(2,1)S(1)}, u32[]{:S(2)}, u32[]{:S(2)}) collective-permute-start(bf16[3,256,256]{2,1,0:T(8,128)(2,1)} %bitcast.13), channel_id=1, source_target_pairs={{0,16},{4,12},{8,24},{12,4},{16,0},{20,28},{24,8},{28,20},{1,17},{... | collective-permute-start | bytes 1179656 | tf_op jit(solution)/shard_map/ppermute | solution.py:20
  10.0 9.4 %collective-permute-start.5 = (bf16[3,256,256]{2,1,0:T(8,128)(2,1)S(1)}, bf16[3,256,256]{2,1,0:T(8,128)(2,1)S(1)}, u32[]{:S(2)}, u32[]{:S(2)}) collective-permute-start(bf16[3,256,256]{2,1,0:T(8,128)(2,1)S(1)} %collective-permute-done.1.rest_2_), channel_id=1, source_target_pairs={{0,16},{4,12},{8,24},{12,4},{16,0},{20,28},{24,8},{28,20},{1,17},{... | collective-permute-start | bytes 1179656 | tf_op jit(solution)/shard_map/ppermute | solution.py:20
  13.6 5.8 %collective-permute-start = (bf16[3,256,256]{2,1,0:T(8,128)(2,1)}, bf16[3,256,256]{2,1,0:T(8,128)(2,1)S(1)}, u32[]{:S(2)}, u32[]{:S(2)}) collective-permute-start(bf16[3,256,256]{2,1,0:T(8,128)(2,1)} %bitcast.14), channel_id=1, source_target_pairs={{0,4},{4,0},{8,12},{12,8},{16,20},{20,16},{24,28},{28,24},{1,5},{5... | collective-permute-start | bytes 1179656 | tf_op jit(solution)/shard_map/ppermute | solution.py:20
  13.6 5.8 %collective-permute-start.2 = (bf16[3,256,256]{2,1,0:T(8,128)(2,1)S(1)}, bf16[3,256,256]{2,1,0:T(8,128)(2,1)S(1)}, u32[]{:S(2)}, u32[]{:S(2)}) collective-permute-start(bf16[3,256,256]{2,1,0:T(8,128)(2,1)S(1)} %collective-permute-done.1.rest_2_), channel_id=1, source_target_pairs={{0,4},{4,0},{8,12},{12,8},{16,20},{20,16},{24,28},{28,24},{1,5},{5... | collective-permute-start | bytes 1179656 | tf_op jit(solution)/shard_map/ppermute | solution.py:20
  14.9 4.5 %collective-permute-start.4 = (bf16[3,256,256]{2,1,0:T(8,128)(2,1)S(1)}, bf16[3,256,256]{2,1,0:T(8,128)(2,1)S(1)}, u32[]{:S(2)}, u32[]{:S(2)}) collective-permute-start(bf16[3,256,256]{2,1,0:T(8,128)(2,1)S(1)} %collective-permute-done.3.rest_4_), channel_id=1, source_target_pairs={{0,4},{4,0},{8,12},{12,8},{16,20},{20,16},{24,28},{28,24},{1,5},{5... | collective-permute-start | bytes 1179656 | tf_op jit(solution)/shard_map/ppermute | solution.py:20
  19.4 1.7 %collective-permute-start.6 = (bf16[3,256,256]{2,1,0:T(8,128)(2,1)S(1)}, bf16[3,256,256]{2,1,0:T(8,128)(2,1)S(1)}, u32[]{:S(2)}, u32[]{:S(2)}) collective-permute-start(bf16[3,256,256]{2,1,0:T(8,128)(2,1)S(1)} %collective-permute-done.5.rest_6_), channel_id=1, source_target_pairs={{0,4},{4,0},{8,12},{12,8},{16,20},{20,16},{24,28},{28,24},{1,5},{5... | collective-permute-start | bytes 1179656 | tf_op jit(solution)/shard_map/ppermute | solution.py:20
  22.9 9.2 %collective-permute-start.7 = (bf16[2,2,2,64,256]{4,3,2,1,0:T(8,128)(2,1)S(1)}, bf16[2,2,2,64,256]{4,3,2,1,0:T(8,128)(2,1)S(1)}, u32[]{:S(2)}, u32[]{:S(2)}) collective-permute-start(bf16[2,2,2,64,256]{4,3,2,1,0:T(8,128)(2,1)S(1)} %get-tuple-element.24), channel_id=1, source_target_pairs={{0,1},{1,0},{2,3},{3,2},{4,5},{5,4},{6,7},{7,6},{8,9},{9,8},{10,11... | collective-permute-start | bytes 786440 | tf_op jit(solution)/shard_map/ppermute | solution.py:20
  25.8 13.8 %collective-permute-start.13 = (bf16[2,2,2,64,256]{4,3,2,1,0:T(8,128)(2,1)S(1)}, bf16[2,2,2,64,256]{4,3,2,1,0:T(8,128)(2,1)S(1)}, u32[]{:S(2)}, u32[]{:S(2)}) collective-permute-start(bf16[2,2,2,64,256]{4,3,2,1,0:T(8,128)(2,1)S(1)} %get-tuple-element.32), channel_id=1, source_target_pairs={{0,1},{1,0},{2,3},{3,2},{4,5},{5,4},{6,7},{7,6},{8,9},{9,8},{10,11... | collective-permute-start | bytes 786440 | tf_op jit(solution)/shard_map/ppermute | solution.py:20
  26.5 1.2 %collective-permute-start.8 = (f32[8,128]{1,0:T(8,128)S(1)}, f32[8,128]{1,0:T(8,128)S(1)}, u32[]{:S(2)}, u32[]{:S(2)}) collective-permute-start(f32[8,128]{1,0:T(8,128)S(1)} %get-tuple-element.28), channel_id=1, source_target_pairs={{0,4},{4,0},{8,12},{12,8},{16,20},{20,16},{24,28},{28,24},{1,5},{5... | collective-permute-start | bytes 12296 | tf_op jit(solution)/shard_map/ppermute | solution.py:20
  27.7 12.7 %collective-permute-start.11 = (f32[8,128]{1,0:T(8,128)S(1)}, f32[8,128]{1,0:T(8,128)S(1)}, u32[]{:S(2)}, u32[]{:S(2)}) collective-permute-start(f32[8,128]{1,0:T(8,128)S(1)} %add.12), channel_id=1, source_target_pairs={{0,24},{4,28},{8,16},{12,20},{16,8},{20,12},{24,0},{28,4},{1,25},{... | collective-permute-start | bytes 12296 | tf_op jit(solution)/shard_map/ppermute | solution.py:20
  30.4 10.0 %collective-permute-start.10 = (f32[8,128]{1,0:T(8,128)S(1)}, f32[8,128]{1,0:T(8,128)S(1)}, u32[]{:S(2)}, u32[]{:S(2)}) collective-permute-start(f32[8,128]{1,0:T(8,128)S(1)} %add.12), channel_id=1, source_target_pairs={{0,16},{4,20},{8,24},{12,28},{16,0},{20,4},{24,8},{28,12},{1,17},{... | collective-permute-start | bytes 12296 | tf_op jit(solution)/shard_map/ppermute | solution.py:20
  30.4 10.0 %collective-permute-start.9 = (f32[8,128]{1,0:T(8,128)S(1)}, f32[8,128]{1,0:T(8,128)S(1)}, u32[]{:S(2)}, u32[]{:S(2)}) collective-permute-start(f32[8,128]{1,0:T(8,128)S(1)} %add.12), channel_id=1, source_target_pairs={{0,8},{4,12},{8,0},{12,4},{16,24},{20,28},{24,16},{28,20},{1,9},{5... | collective-permute-start | bytes 12296 | tf_op jit(solution)/shard_map/ppermute | solution.py:20
  32.1 8.3 %collective-permute-start.12 = (bf16[1,2,2,64,256]{4,3,2,1,0:T(8,128)(2,1)S(1)}, bf16[1,2,2,64,256]{4,3,2,1,0:T(8,128)(2,1)S(1)}, u32[]{:S(2)}, u32[]{:S(2)}) collective-permute-start(bf16[1,2,2,64,256]{4,3,2,1,0:T(8,128)(2,1)S(1)} %get-tuple-element.29), channel_id=1, source_target_pairs={{0,2},{1,3},{2,0},{3,1},{4,6},{5,7},{6,4},{7,5},{8,10},{9,11},{10,... | collective-permute-start | bytes 393224 | tf_op jit(solution)/shard_map/ppermute | solution.py:20
  39.7 8.6 %collective-permute-start.14 = (bf16[1,2,2,64,256]{4,3,2,1,0:T(8,128)(2,1)S(1)}, bf16[1,2,2,64,256]{4,3,2,1,0:T(8,128)(2,1)S(1)}, u32[]{:S(2)}, u32[]{:S(2)}) collective-permute-start(bf16[1,2,2,64,256]{4,3,2,1,0:T(8,128)(2,1)S(1)} %get-tuple-element.34), channel_id=1, source_target_pairs={{0,2},{1,3},{2,0},{3,1},{4,6},{5,7},{6,4},{7,5},{8,10},{9,11},{10,... | collective-permute-start | bytes 393224 | tf_op jit(solution)/shard_map/ppermute | solution.py:20
  40.4 8.7 %collective-permute-start.17 = (f32[8,128]{1,0:T(8,128)S(1)}, f32[8,128]{1,0:T(8,128)S(1)}, u32[]{:S(2)}, u32[]{:S(2)}) collective-permute-start(f32[8,128]{1,0:T(8,128)S(1)} %add_add_fusion.refs_0_), channel_id=1, source_target_pairs={{0,3},{1,2},{2,1},{3,0},{4,7},{5,6},{6,5},{7,4},{8,11},{9,10},{10,... | collective-permute-start | bytes 12296 | tf_op jit(solution)/shard_map/ppermute | solution.py:20
  43.8 5.3 %collective-permute-start.16 = (f32[8,128]{1,0:T(8,128)S(1)}, f32[8,128]{1,0:T(8,128)S(1)}, u32[]{:S(2)}, u32[]{:S(2)}) collective-permute-start(f32[8,128]{1,0:T(8,128)S(1)} %add_add_fusion.refs_0_), channel_id=1, source_target_pairs={{0,2},{1,3},{2,0},{3,1},{4,6},{5,7},{6,4},{7,5},{8,10},{9,11},{10,... | collective-permute-start | bytes 12296 | tf_op jit(solution)/shard_map/ppermute | solution.py:20
  44.4 4.7 %collective-permute-start.15 = (f32[8,128]{1,0:T(8,128)S(1)}, f32[8,128]{1,0:T(8,128)S(1)}, u32[]{:S(2)}, u32[]{:S(2)}) collective-permute-start(f32[8,128]{1,0:T(8,128)S(1)} %add_add_fusion.refs_0_), channel_id=1, source_target_pairs={{0,1},{1,0},{2,3},{3,2},{4,5},{5,4},{6,7},{7,6},{8,9},{9,8},{10,11... | collective-permute-start | bytes 12296 | tf_op jit(solution)/shard_map/ppermute | solution.py:20

commit v8 on v7

--- a/solution.py
+++ b/solution.py
@@ -59,7 +59,9 @@
         for pair in range(vectors.shape[1]):
             block = vectors[trial, pair]
             product = jnp.dot(stacked, block, preferred_element_type=jnp.float32)
-            inner[:, trial, pair] = product.astype(jnp.bfloat16).reshape(terms, states, states)
+            for term in range(terms):
+                part = product[term * states : (term + 1) * states].astype(jnp.bfloat16)
+                inner[trial, pair, :, term * states : (term + 1) * states] = part
             wide = block.astype(jnp.float32)
             square += jnp.sum((wide * wide).reshape(-1, 8, states), axis=0)
         sums.append(total(square) * square_scale)
@@ -68,46 +70,58 @@
     fetch.wait()
 
 
-def place_blocks(sectors, pieces, rights):
+def place_kernel(sectors, *refs):
+    *pieces, rights = refs
     odd = lax.axis_index("sec") & 1
-    for mask in range(0, sectors, 2):
+    for mask in range(0, sectors - 2, 2):
         even_place, odd_place = turned(mask, 0, sectors), turned(mask, 1, sectors)
         rights[jnp.where(odd == 1, odd_place, even_place)] = pieces[mask][...]
         rights[jnp.where(odd == 1, even_place, odd_place) ^ 1] = pieces[mask + 1][...]
 
 
-def sum_kernel(sectors, first, offsets, vectors, inner, before, *rest):
-    if first == 0:
-        *pieces, keep, send, tile, rights, partial = rest
-        place_blocks(sectors, pieces, rights)
-    else:
-        rights, keep, send, tile, partial = rest
-    terms, trials, _, states, _ = inner.shape
+def sum_kernel(sectors, first, offsets, vectors, inner, before, early, mine, theirs, *rest):
+    keep, send, tile, blocks, partial = rest
+    trials, _, states, _ = inner.shape
+    terms = early.shape[1]
     shares = 2 * keep.shape[0]
     rows = states // shares
+    late = sectors - 2
     sector = lax.axis_index("sec")
     place = lax.axis_index("term")
     grams = [jnp.zeros((8, states), jnp.float32) for _ in range(trials * trials)]
     for local_pair in range(keep.shape[2]):
         pair = first + local_pair
-        result = None
+        slot = local_pair % 2
         for term in range(terms):
-            wanted = (sector + offsets[term, pair]) & (sectors - 1)
-            added = jnp.dot(
-                inner[term, :, pair].reshape(trials * states, states),
-                rights[sector ^ wanted, term],
-                preferred_element_type=jnp.float32,
-            )
-            result = added if result is None else result + added
-        partial[...] = result.reshape(trials, states, states)
+            mask = sector ^ ((sector + offsets[term, pair]) & (sectors - 1))
+            span = pl.ds(term * states, states)
+
+            @pl.when(mask < late)
+            def _():
+                blocks[slot, span] = early[mask, term]
+
+            @pl.when(mask == late)
+            def _():
+                blocks[slot, span] = mine[term]
+
+            @pl.when(mask == late + 1)
+            def _():
+                blocks[slot, span] = theirs[term]
+
+        result = jnp.dot(
+            inner[:, pair].reshape(trials * states, terms * states),
+            blocks[slot],
+            preferred_element_type=jnp.float32,
+        )
+        partial[slot] = result.reshape(trials, states, states)
         for j in range(trials):
-            product = partial[j]
+            product = partial[slot, j]
             for i in range(trials):
                 spread = vectors[i, pair].astype(jnp.float32) * product
                 grams[i * trials + j] += jnp.sum(spread.reshape(-1, 8, states), axis=0)
         for mask in range(shares):
             start = pl.multiple_of((place ^ mask) * rows, rows)
-            share = partial[:, pl.ds(start, rows)]
+            share = partial[slot, :, pl.ds(start, rows)]
             if mask & 1:
                 send[mask // 2, :, local_pair] = share.astype(jnp.bfloat16)
             else:
@@ -124,17 +138,15 @@
             keep[k // 2] = both
 
 
-def finish_kernel(*refs):
-    *parts, products = refs
+def finish_kernel(count, *refs):
+    *parts, products, rayleigh = refs
+    parts, tiles = parts[:count], parts[count:]
     first = 0
     for kept, received in zip(parts[::2], parts[1::2]):
         both = kept[0] + received[0].astype(jnp.float32)
         products[:, first : first + both.shape[1]] = both.astype(jnp.bfloat16)
         first += both.shape[1]
 
-
-def rayleigh_kernel(*refs):
-    *tiles, rayleigh = refs
     tile = sum(part[...] for part in tiles)
     trials = rayleigh.shape[0]
     row = lax.broadcasted_iota(jnp.int32, rayleigh.shape, 0)
@@ -168,10 +180,6 @@
         steps.append([unit, 2 * unit, 3 * unit] if 2 * unit < count else [unit])
         low += 2
     return steps
-
-
-def chunk_sizes(pairs):
-    return [pairs // 2, pairs - pairs // 2]
 
 
 def call(kernel, name, flops, moved, limit, **kwargs):
@@ -199,7 +207,7 @@
         5 * MIB,
         12 * MIB,
         out_shape=(
-            jax.ShapeDtypeStruct((terms, trials, pairs, states, states), jnp.bfloat16),
+            jax.ShapeDtypeStruct((trials, pairs, states, terms * states), jnp.bfloat16),
             jax.ShapeDtypeStruct(TILE, jnp.float32),
             jax.ShapeDtypeStruct(right.shape, jnp.bfloat16),
         ),
@@ -217,30 +225,38 @@
     def share_of(count, size, dtype):
         return jax.ShapeDtypeStruct((count, trials, size, rows, states), dtype)
 
-    rights_shape = (sectors, terms, states, states)
-    sizes = chunk_sizes(pairs)
-    parts, rights, first = [], None, 0
-    for size in sizes:
-        outs = [
-            share_of(shares // 2, size, jnp.float32),
-            share_of(shares // 2, size, jnp.bfloat16),
-            jax.ShapeDtypeStruct(TILE, jnp.float32),
-        ]
-        blocks = gathered if first == 0 else [rights]
-        if first == 0:
-            outs.append(jax.ShapeDtypeStruct(rights_shape, jnp.bfloat16))
-        keep, send, tile, *placed = call(
+    *early, mine, theirs = gathered
+    early = call(
+        functools.partial(place_kernel, sectors),
+        "place_blocks",
+        1,
+        1,
+        8 * MIB,
+        out_shape=jax.ShapeDtypeStruct((sectors - 2, terms, states, states), jnp.bfloat16),
+        in_specs=[VMEM] * len(early),
+        out_specs=VMEM,
+    )(*early)
+
+    parts, first = [], 0
+    for size in (pairs // 2, pairs - pairs // 2):
+        keep, send, tile = call(
             functools.partial(sum_kernel, sectors, first),
             "sum_over_terms",
             2 * terms * trials * size * states**3,
             4 * MIB,
             12 * MIB,
-            out_shape=outs,
-            in_specs=[SMEM, VMEM, VMEM, VMEM] + [VMEM] * len(blocks),
-            out_specs=[VMEM] * len(outs),
-            scratch_shapes=[pltpu.VMEM((trials, states, states), jnp.float32)],
-        )(in_hbm(offsets), vectors, inner, tile, *blocks)
-        rights = placed[0] if placed else rights
+            out_shape=(
+                share_of(shares // 2, size, jnp.float32),
+                share_of(shares // 2, size, jnp.bfloat16),
+                jax.ShapeDtypeStruct(TILE, jnp.float32),
+            ),
+            in_specs=[SMEM] + [VMEM] * 6,
+            out_specs=(VMEM, VMEM, VMEM),
+            scratch_shapes=[
+                pltpu.VMEM((2, terms * states, states), jnp.bfloat16),
+                pltpu.VMEM((2, trials, states, states), jnp.float32),
+            ],
+        )(in_hbm(offsets), vectors, inner, tile, early, mine, theirs)
         first += size
         step = 1
         received = swap(send, "term", step)
@@ -270,26 +286,19 @@
     for masks in steps:
         tile = add_places(tile, "term", masks)
     tiles = [tile] + [swap(tile, "term", mask) for mask in last]
-    rayleigh = call(
-        rayleigh_kernel,
-        "rayleigh",
+    products, rayleigh = call(
+        functools.partial(finish_kernel, len(parts)),
+        "finish",
         1,
         1,
         8 * MIB,
-        out_shape=jax.ShapeDtypeStruct((trials, trials), jnp.float32),
-        in_specs=[VMEM] * len(tiles),
-        out_specs=VMEM,
-    )(*tiles)
-    products = call(
-        finish_kernel,
-        "add_last_share",
-        1,
-        1,
-        8 * MIB,
-        out_shape=jax.ShapeDtypeStruct((trials, pairs, rows, states), jnp.bfloat16),
-        in_specs=[VMEM] * len(parts),
-        out_specs=VMEM,
-    )(*parts)
+        out_shape=(
+            jax.ShapeDtypeStruct((trials, pairs, rows, states), jnp.bfloat16),
+            jax.ShapeDtypeStruct((trials, trials), jnp.float32),
+        ),
+        in_specs=[VMEM] * (len(parts) + len(tiles)),
+        out_specs=(VMEM, VMEM),
+    )(*parts, *tiles)
     return (products[:, None], rayleigh)
 
 

time: 50 us -> 52.7 us (1.054)
  waiting for transfers between devices: 19.1 us -> 20.4 us
  starting transfers between devices: 21.8 us -> 22.9 us
    ppermute x18, waiting for transfers between devices: 19.1 us -> 20.4 us  [swap(): lax.ppermute(value, axis, [(place, place ^ masks[place & 1]) for place in...]
    ppermute x18, starting transfers between devices: 21.8 us -> 22.9 us  [swap(): lax.ppermute(value, axis, [(place, place ^ masks[place & 1]) for place in...]
    pallas_call x2, Pallas kernels: 3.34 us -> 4.2 us  [local(): call(functools.partial(sum_kernel, sectors, first), 'sum_over_terms', 2 *...]
  transfers between devices with their start and end apart: 18 -> 18, of which waited for: 8 -> 9; matrix products, arithmetic and copies ran while one was open for 0% -> 0% of each run, Pallas kernels for 7% -> 6%
where the time goes in v8:
time: 52.7 us; the launch traced here: 52.4 us
  starting transfers between devices  22.9 us (43%)
  waiting for transfers between devices  20.4 us (39%)
  Pallas kernels  6.2 us (12%)
  local copies, waits for them, and re-layouts  2.22 us (4%)
  between operations  0.7 us (1%)
    ppermute x18, starting transfers between devices, swap(): lax.ppermute(value, axis, [(place, place ^ masks[place & 1]) for place in...  22.9 us
    ppermute x18, waiting for transfers between devices, swap(): lax.ppermute(value, axis, [(place, place ^ masks[place & 1]) for place in...  20.4 us
    pallas_call x2, Pallas kernels, local(): call(functools.partial(sum_kernel, sectors, first), 'sum_over_terms', 2 *...  4.2 us
    unnamed x4, local copies, waits for them, and re-layouts  2.22 us
  transfers between devices with their start and end apart: 18, of which 9 were waited for; matrix products, arithmetic and copies ran while one was open for 0% of the time, Pallas kernels for 6%

profile of v8, /device:TPU:0, one launch (start us, length us, event | category | flops | bytes accessed | tf_op | source)
XLA Modules:
  0.0 52.4 jit_solution(17902615090439060664)
XLA Ops:
  0.6 3.0 %collective-permute-start.1 = (bf16[3,256,256]{2,1,0:T(8,128)(2,1)}, bf16[3,256,256]{2,1,0:T(8,128)(2,1)S(1)}, u32[]{:S(2)}, u32[]{:S(2)}) collective-permute-start(bf16[3,256,256]{2,1,0:T(8,128)(2,1)} %bitcast.10), channel_id=1, source_target_pairs={{0,8},{4,20},{8,0},{12,28},{16,24},{20,4},{24,16},{28,12},{1,9},{5... | collective-permute-start | bytes 1179656 | tf_op jit(solution)/shard_map/ppermute | solution.py:20
  3.6 1.2 %copy-done = bf16[2,1,4,256,256]{4,3,2,1,0:T(8,128)(2,1)S(1)} copy-done((bf16[2,1,4,256,256]{4,3,2,1,0:T(8,128)(2,1)S(1)}, bf16[2,1,4,256,256]{4,3,2,1,0:T(8,128)(2,1)}, u32[]{:S(2)}) %copy-start) | copy-done | bytes 1048600
  4.9 1.0 %copy-done.1 = bf16[3,1,256,256]{3,2,1,0:T(8,128)(2,1)S(1)} copy-done((bf16[3,1,256,256]{3,2,1,0:T(8,128)(2,1)S(1)}, bf16[3,1,256,256]{3,2,1,0:T(8,128)(2,1)}, u32[]{:S(2)}) %copy-start.1) | copy-done | bytes 393240
  5.9 1.0 %inner_products.1 = (bf16[2,4,256,768]{3,2,1,0:T(8,128)(2,1)S(1)}, f32[8,128]{1,0:T(8,128)S(1)}, bf16[3,256,256]{2,1,0:T(8,128)(2,1)S(1)}) custom-call(bf16[2,4,256,256]{3,2,1,0:T(8,128)(2,1)S(1)} %bitcast.6, bf16[3,256,256]{2,1,0:T(8,128)(2,1)S(1)} %bitcast.9, bf16[3,256,256]{2,1,0:T(8,128)(2,1)} %bitcast.11), custom_call_target="tpu_custom_call" | custom-call | flops 805306368 | bytes 5242880 | tf_op jit(solution)/shard_map/inner_products/pallas_call | solution.py:203
  6.9 1.6 %collective-permute-start.3 = (bf16[3,256,256]{2,1,0:T(8,128)(2,1)}, bf16[3,256,256]{2,1,0:T(8,128)(2,1)S(1)}, u32[]{:S(2)}, u32[]{:S(2)}) collective-permute-start(bf16[3,256,256]{2,1,0:T(8,128)(2,1)} %bitcast.12), channel_id=1, source_target_pairs={{0,16},{4,12},{8,24},{12,4},{16,0},{20,28},{24,8},{28,20},{1,17},{... | collective-permute-start | bytes 1179656 | tf_op jit(solution)/shard_map/ppermute | solution.py:20
  8.5 1.5 %collective-permute-done.1.refs_2_ = bf16[3,256,256]{2,1,0:T(8,128)(2,1)S(1)} collective-permute-done((bf16[3,256,256]{2,1,0:T(8,128)(2,1)}, bf16[3,256,256]{2,1,0:T(8,128)(2,1)S(1)}, u32[]{:S(2)}, u32[]{:S(2)}) %collective-permute-start.1) | collective-permute-done | bytes 393248 | tf_op jit(solution)/shard_map/ppermute | solution.py:20
  10.0 3.6 %collective-permute-start.5 = (bf16[3,256,256]{2,1,0:T(8,128)(2,1)S(1)}, bf16[3,256,256]{2,1,0:T(8,128)(2,1)S(1)}, u32[]{:S(2)}, u32[]{:S(2)}) collective-permute-start(bf16[3,256,256]{2,1,0:T(8,128)(2,1)S(1)} %collective-permute-done.1.refs_2_), channel_id=1, source_target_pairs={{0,16},{4,12},{8,24},{12,4},{16,0},{20,28},{24,8},{28,20},{1,17},{... | collective-permute-start | bytes 1179656 | tf_op jit(solution)/shard_map/ppermute | solution.py:20
  14.1 0.8 %collective-permute-done.3.refs_4_ = bf16[3,256,256]{2,1,0:T(8,128)(2,1)S(1)} collective-permute-done((bf16[3,256,256]{2,1,0:T(8,128)(2,1)}, bf16[3,256,256]{2,1,0:T(8,128)(2,1)S(1)}, u32[]{:S(2)}, u32[]{:S(2)}) %collective-permute-start.3) | collective-permute-done | bytes 393248 | tf_op jit(solution)/shard_map/ppermute | solution.py:20
  14.9 4.4 %collective-permute-done.5.mine = bf16[3,256,256]{2,1,0:T(8,128)(2,1)S(1)} collective-permute-done((bf16[3,256,256]{2,1,0:T(8,128)(2,1)S(1)}, bf16[3,256,256]{2,1,0:T(8,128)(2,1)S(1)}, u32[]{:S(2)}, u32[]{:S(2)}) %collective-permute-start.5) | collective-permute-done | bytes 393248 | tf_op jit(solution)/shard_map/ppermute | solution.py:20
  19.6 1.5 %collective-permute-done.6.theirs = bf16[3,256,256]{2,1,0:T(8,128)(2,1)S(1)} collective-permute-done((bf16[3,256,256]{2,1,0:T(8,128)(2,1)S(1)}, bf16[3,256,256]{2,1,0:T(8,128)(2,1)S(1)}, u32[]{:S(2)}, u32[]{:S(2)}) %collective-permute-start.6) | collective-permute-done | bytes 393248 | tf_op jit(solution)/shard_map/ppermute | solution.py:20
  21.1 2.1 %sum_over_terms.2 = (f32[2,2,2,64,256]{4,3,2,1,0:T(8,128)S(1)}, bf16[2,2,2,64,256]{4,3,2,1,0:T(8,128)(2,1)S(1)}, f32[8,128]{1,0:T(8,128)S(1)}) custom-call(s32[3,4]{1,0:T(4,128)} %offsets.3, bf16[2,4,256,256]{3,2,1,0:T(8,128)(2,1)S(1)} %bitcast.7, bf16[2,4,256,768]{3,2,1,0:T(8,128)(2,1)S(1)} %get-tuple-element.20.inner, ...), custom_call_target="tpu_custom_call" | custom-call | flops 402653184 | bytes 4194304 | tf_op jit(solution)/shard_map/sum_over_terms/pallas_call | solution.py:242
  23.2 1.4 %collective-permute-start.7 = (bf16[2,2,2,64,256]{4,3,2,1,0:T(8,128)(2,1)S(1)}, bf16[2,2,2,64,256]{4,3,2,1,0:T(8,128)(2,1)S(1)}, u32[]{:S(2)}, u32[]{:S(2)}) collective-permute-start(bf16[2,2,2,64,256]{4,3,2,1,0:T(8,128)(2,1)S(1)} %get-tuple-element.25), channel_id=1, source_target_pairs={{0,1},{1,0},{2,3},{3,2},{4,5},{5,4},{6,7},{7,6},{8,9},{9,8},{10,11... | collective-permute-start | bytes 786440 | tf_op jit(solution)/shard_map/ppermute | solution.py:20
  24.6 2.1 %sum_over_terms.3 = (f32[2,2,2,64,256]{4,3,2,1,0:T(8,128)S(1)}, bf16[2,2,2,64,256]{4,3,2,1,0:T(8,128)(2,1)S(1)}, f32[8,128]{1,0:T(8,128)S(1)}) custom-call(s32[3,4]{1,0:T(4,128)} %offsets.3, bf16[2,4,256,256]{3,2,1,0:T(8,128)(2,1)S(1)} %bitcast.8, bf16[2,4,256,768]{3,2,1,0:T(8,128)(2,1)S(1)} %get-tuple-element.20.inner, ...), custom_call_target="tpu_custom_call" | custom-call | flops 402653184 | bytes 4194304 | tf_op jit(solution)/shard_map/sum_over_terms/pallas_call | solution.py:242
  26.7 0.7 %collective-permute-start.13 = (bf16[2,2,2,64,256]{4,3,2,1,0:T(8,128)(2,1)S(1)}, bf16[2,2,2,64,256]{4,3,2,1,0:T(8,128)(2,1)S(1)}, u32[]{:S(2)}, u32[]{:S(2)}) collective-permute-start(bf16[2,2,2,64,256]{4,3,2,1,0:T(8,128)(2,1)S(1)} %get-tuple-element.32), channel_id=1, source_target_pairs={{0,1},{1,0},{2,3},{3,2},{4,5},{5,4},{6,7},{7,6},{8,9},{9,8},{10,11... | collective-permute-start | bytes 786440 | tf_op jit(solution)/shard_map/ppermute | solution.py:20
  27.4 1.2 %collective-permute-done.8 = f32[8,128]{1,0:T(8,128)S(1)} collective-permute-done((f32[8,128]{1,0:T(8,128)S(1)}, f32[8,128]{1,0:T(8,128)S(1)}, u32[]{:S(2)}, u32[]{:S(2)}) %collective-permute-start.8) | collective-permute-done | bytes 4128 | tf_op jit(solution)/shard_map/ppermute | solution.py:20
  28.5 2.7 %collective-permute-start.11 = (f32[8,128]{1,0:T(8,128)S(1)}, f32[8,128]{1,0:T(8,128)S(1)}, u32[]{:S(2)}, u32[]{:S(2)}) collective-permute-start(f32[8,128]{1,0:T(8,128)S(1)} %add.12), channel_id=1, source_target_pairs={{0,24},{4,28},{8,16},{12,20},{16,8},{20,12},{24,0},{28,4},{1,25},{... | collective-permute-start | bytes 12296 | tf_op jit(solution)/shard_map/ppermute | solution.py:20
  31.3 0.7 %collective-permute-start.9 = (f32[8,128]{1,0:T(8,128)S(1)}, f32[8,128]{1,0:T(8,128)S(1)}, u32[]{:S(2)}, u32[]{:S(2)}) collective-permute-start(f32[8,128]{1,0:T(8,128)S(1)} %add.12), channel_id=1, source_target_pairs={{0,8},{4,12},{8,0},{12,4},{16,24},{20,28},{24,16},{28,20},{1,9},{5... | collective-permute-start | bytes 12296 | tf_op jit(solution)/shard_map/ppermute | solution.py:20
  32.4 2.4 %collective-permute-start.12 = (bf16[1,2,2,64,256]{4,3,2,1,0:T(8,128)(2,1)S(1)}, bf16[1,2,2,64,256]{4,3,2,1,0:T(8,128)(2,1)S(1)}, u32[]{:S(2)}, u32[]{:S(2)}) collective-permute-start(bf16[1,2,2,64,256]{4,3,2,1,0:T(8,128)(2,1)S(1)} %get-tuple-element.29), channel_id=1, source_target_pairs={{0,2},{1,3},{2,0},{3,1},{4,6},{5,7},{6,4},{7,5},{8,10},{9,11},{10,... | collective-permute-start | bytes 393224 | tf_op jit(solution)/shard_map/ppermute | solution.py:20
  34.9 5.1 %collective-permute-done.13.received = bf16[2,2,2,64,256]{4,3,2,1,0:T(8,128)(2,1)S(1)} collective-permute-done((bf16[2,2,2,64,256]{4,3,2,1,0:T(8,128)(2,1)S(1)}, bf16[2,2,2,64,256]{4,3,2,1,0:T(8,128)(2,1)S(1)}, u32[]{:S(2)}, u32[]{:S(2)}) %collective-permute-start.13) | collective-permute-done | bytes 262176 | tf_op jit(solution)/shard_map/ppermute | solution.py:20
  40.6 2.5 %collective-permute-start.15 = (f32[8,128]{1,0:T(8,128)S(1)}, f32[8,128]{1,0:T(8,128)S(1)}, u32[]{:S(2)}, u32[]{:S(2)}) collective-permute-start(f32[8,128]{1,0:T(8,128)S(1)} %add_add_fusion.refs_4_), channel_id=1, source_target_pairs={{0,1},{1,0},{2,3},{3,2},{4,5},{5,4},{6,7},{7,6},{8,9},{9,8},{10,11... | collective-permute-start | bytes 12296 | tf_op jit(solution)/shard_map/ppermute | solution.py:20
  43.1 3.1 %collective-permute-start.16 = (f32[8,128]{1,0:T(8,128)S(1)}, f32[8,128]{1,0:T(8,128)S(1)}, u32[]{:S(2)}, u32[]{:S(2)}) collective-permute-start(f32[8,128]{1,0:T(8,128)S(1)} %add_add_fusion.refs_4_), channel_id=1, source_target_pairs={{0,2},{1,3},{2,0},{3,1},{4,6},{5,7},{6,4},{7,5},{8,10},{9,11},{10,... | collective-permute-start | bytes 12296 | tf_op jit(solution)/shard_map/ppermute | solution.py:20
  46.3 2.2 %collective-permute-done.14.refs_3_ = bf16[1,2,2,64,256]{4,3,2,1,0:T(8,128)(2,1)S(1)} collective-permute-done((bf16[1,2,2,64,256]{4,3,2,1,0:T(8,128)(2,1)S(1)}, bf16[1,2,2,64,256]{4,3,2,1,0:T(8,128)(2,1)S(1)}, u32[]{:S(2)}, u32[]{:S(2)}) %collective-permute-start.14) | collective-permute-done | bytes 131104 | tf_op jit(solution)/shard_map/ppermute | solution.py:20
  48.5 3.2 %collective-permute-done.17.refs_7_ = f32[8,128]{1,0:T(8,128)S(1)} collective-permute-done((f32[8,128]{1,0:T(8,128)S(1)}, f32[8,128]{1,0:T(8,128)S(1)}, u32[]{:S(2)}, u32[]{:S(2)}) %collective-permute-start.17) | collective-permute-done | bytes 4128 | tf_op jit(solution)/shard_map/ppermute | solution.py:20
  51.7 0.8 %finish.1 = (bf16[2,4,64,256]{3,2,1,0:T(8,128)(2,1)}, f32[2,2]{1,0:T(2,128)}) custom-call(f32[1,2,2,64,256]{4,3,2,1,0:T(8,128)S(1)} %get-tuple-element.26.refs_0_, bf16[1,2,2,64,256]{4,3,2,1,0:T(8,128)(2,1)S(1)} %collective-permute-done.12.refs_1_, f32[1,2,2,64,256]{4,3,2,1,0:T(8,128)S(1)} %get-tuple-element.33.refs_2_, ...), custom_call_target="tpu_custom_call" | custom-call | flops 1 | bytes 1 | tf_op jit(solution)/shard_map/finish/pallas_call | solution.py:289
  (25 shorter events, 1.7 us)
Async XLA Ops:
  0.6 9.4 %collective-permute-start.1 = (bf16[3,256,256]{2,1,0:T(8,128)(2,1)}, bf16[3,256,256]{2,1,0:T(8,128)(2,1)S(1)}, u32[]{:S(2)}, u32[]{:S(2)}) collective-permute-start(bf16[3,256,256]{2,1,0:T(8,128)(2,1)} %bitcast.10), channel_id=1, source_target_pairs={{0,8},{4,20},{8,0},{12,28},{16,24},{20,4},{24,16},{28,12},{1,9},{5... | collective-permute-start | bytes 1179656 | tf_op jit(solution)/shard_map/ppermute | solution.py:20
  3.6 1.2 %copy-start = (bf16[2,1,4,256,256]{4,3,2,1,0:T(8,128)(2,1)S(1)}, bf16[2,1,4,256,256]{4,3,2,1,0:T(8,128)(2,1)}, u32[]{:S(2)}) copy-start(bf16[2,1,4,256,256]{4,3,2,1,0:T(8,128)(2,1)} %param.4) | copy-start | bytes 3145732
  4.9 1.0 %copy-start.1 = (bf16[3,1,256,256]{3,2,1,0:T(8,128)(2,1)S(1)}, bf16[3,1,256,256]{3,2,1,0:T(8,128)(2,1)}, u32[]{:S(2)}) copy-start(bf16[3,1,256,256]{3,2,1,0:T(8,128)(2,1)} %param.5) | copy-start | bytes 1179652
  6.9 8.1 %collective-permute-start.3 = (bf16[3,256,256]{2,1,0:T(8,128)(2,1)}, bf16[3,256,256]{2,1,0:T(8,128)(2,1)S(1)}, u32[]{:S(2)}, u32[]{:S(2)}) collective-permute-start(bf16[3,256,256]{2,1,0:T(8,128)(2,1)} %bitcast.12), channel_id=1, source_target_pairs={{0,16},{4,12},{8,24},{12,4},{16,0},{20,28},{24,8},{28,20},{1,17},{... | collective-permute-start | bytes 1179656 | tf_op jit(solution)/shard_map/ppermute | solution.py:20
  10.0 9.4 %collective-permute-start.5 = (bf16[3,256,256]{2,1,0:T(8,128)(2,1)S(1)}, bf16[3,256,256]{2,1,0:T(8,128)(2,1)S(1)}, u32[]{:S(2)}, u32[]{:S(2)}) collective-permute-start(bf16[3,256,256]{2,1,0:T(8,128)(2,1)S(1)} %collective-permute-done.1.refs_2_), channel_id=1, source_target_pairs={{0,16},{4,12},{8,24},{12,4},{16,0},{20,28},{24,8},{28,20},{1,17},{... | collective-permute-start | bytes 1179656 | tf_op jit(solution)/shard_map/ppermute | solution.py:20
  13.6 5.8 %collective-permute-start = (bf16[3,256,256]{2,1,0:T(8,128)(2,1)}, bf16[3,256,256]{2,1,0:T(8,128)(2,1)S(1)}, u32[]{:S(2)}, u32[]{:S(2)}) collective-permute-start(bf16[3,256,256]{2,1,0:T(8,128)(2,1)} %bitcast.13), channel_id=1, source_target_pairs={{0,4},{4,0},{8,12},{12,8},{16,20},{20,16},{24,28},{28,24},{1,5},{5... | collective-permute-start | bytes 1179656 | tf_op jit(solution)/shard_map/ppermute | solution.py:20
  13.6 5.8 %collective-permute-start.2 = (bf16[3,256,256]{2,1,0:T(8,128)(2,1)S(1)}, bf16[3,256,256]{2,1,0:T(8,128)(2,1)S(1)}, u32[]{:S(2)}, u32[]{:S(2)}) collective-permute-start(bf16[3,256,256]{2,1,0:T(8,128)(2,1)S(1)} %collective-permute-done.1.refs_2_), channel_id=1, source_target_pairs={{0,4},{4,0},{8,12},{12,8},{16,20},{20,16},{24,28},{28,24},{1,5},{5... | collective-permute-start | bytes 1179656 | tf_op jit(solution)/shard_map/ppermute | solution.py:20
  14.9 4.5 %collective-permute-start.4 = (bf16[3,256,256]{2,1,0:T(8,128)(2,1)S(1)}, bf16[3,256,256]{2,1,0:T(8,128)(2,1)S(1)}, u32[]{:S(2)}, u32[]{:S(2)}) collective-permute-start(bf16[3,256,256]{2,1,0:T(8,128)(2,1)S(1)} %collective-permute-done.3.refs_4_), channel_id=1, source_target_pairs={{0,4},{4,0},{8,12},{12,8},{16,20},{20,16},{24,28},{28,24},{1,5},{5... | collective-permute-start | bytes 1179656 | tf_op jit(solution)/shard_map/ppermute | solution.py:20
  19.4 1.7 %collective-permute-start.6 = (bf16[3,256,256]{2,1,0:T(8,128)(2,1)S(1)}, bf16[3,256,256]{2,1,0:T(8,128)(2,1)S(1)}, u32[]{:S(2)}, u32[]{:S(2)}) collective-permute-start(bf16[3,256,256]{2,1,0:T(8,128)(2,1)S(1)} %collective-permute-done.5.mine), channel_id=1, source_target_pairs={{0,4},{4,0},{8,12},{12,8},{16,20},{20,16},{24,28},{28,24},{1,5},{5... | collective-permute-start | bytes 1179656 | tf_op jit(solution)/shard_map/ppermute | solution.py:20
  23.2 9.2 %collective-permute-start.7 = (bf16[2,2,2,64,256]{4,3,2,1,0:T(8,128)(2,1)S(1)}, bf16[2,2,2,64,256]{4,3,2,1,0:T(8,128)(2,1)S(1)}, u32[]{:S(2)}, u32[]{:S(2)}) collective-permute-start(bf16[2,2,2,64,256]{4,3,2,1,0:T(8,128)(2,1)S(1)} %get-tuple-element.25), channel_id=1, source_target_pairs={{0,1},{1,0},{2,3},{3,2},{4,5},{5,4},{6,7},{7,6},{8,9},{9,8},{10,11... | collective-permute-start | bytes 786440 | tf_op jit(solution)/shard_map/ppermute | solution.py:20
  26.7 13.3 %collective-permute-start.13 = (bf16[2,2,2,64,256]{4,3,2,1,0:T(8,128)(2,1)S(1)}, bf16[2,2,2,64,256]{4,3,2,1,0:T(8,128)(2,1)S(1)}, u32[]{:S(2)}, u32[]{:S(2)}) collective-permute-start(bf16[2,2,2,64,256]{4,3,2,1,0:T(8,128)(2,1)S(1)} %get-tuple-element.32), channel_id=1, source_target_pairs={{0,1},{1,0},{2,3},{3,2},{4,5},{5,4},{6,7},{7,6},{8,9},{9,8},{10,11... | collective-permute-start | bytes 786440 | tf_op jit(solution)/shard_map/ppermute | solution.py:20
  27.4 1.2 %collective-permute-start.8 = (f32[8,128]{1,0:T(8,128)S(1)}, f32[8,128]{1,0:T(8,128)S(1)}, u32[]{:S(2)}, u32[]{:S(2)}) collective-permute-start(f32[8,128]{1,0:T(8,128)S(1)} %get-tuple-element.28), channel_id=1, source_target_pairs={{0,4},{4,0},{8,12},{12,8},{16,20},{20,16},{24,28},{28,24},{1,5},{5... | collective-permute-start | bytes 12296 | tf_op jit(solution)/shard_map/ppermute | solution.py:20
  28.5 12.0 %collective-permute-start.11 = (f32[8,128]{1,0:T(8,128)S(1)}, f32[8,128]{1,0:T(8,128)S(1)}, u32[]{:S(2)}, u32[]{:S(2)}) collective-permute-start(f32[8,128]{1,0:T(8,128)S(1)} %add.12), channel_id=1, source_target_pairs={{0,24},{4,28},{8,16},{12,20},{16,8},{20,12},{24,0},{28,4},{1,25},{... | collective-permute-start | bytes 12296 | tf_op jit(solution)/shard_map/ppermute | solution.py:20
  31.3 9.3 %collective-permute-start.10 = (f32[8,128]{1,0:T(8,128)S(1)}, f32[8,128]{1,0:T(8,128)S(1)}, u32[]{:S(2)}, u32[]{:S(2)}) collective-permute-start(f32[8,128]{1,0:T(8,128)S(1)} %add.12), channel_id=1, source_target_pairs={{0,16},{4,20},{8,24},{12,28},{16,0},{20,4},{24,8},{28,12},{1,17},{... | collective-permute-start | bytes 12296 | tf_op jit(solution)/shard_map/ppermute | solution.py:20
  31.3 9.3 %collective-permute-start.9 = (f32[8,128]{1,0:T(8,128)S(1)}, f32[8,128]{1,0:T(8,128)S(1)}, u32[]{:S(2)}, u32[]{:S(2)}) collective-permute-start(f32[8,128]{1,0:T(8,128)S(1)} %add.12), channel_id=1, source_target_pairs={{0,8},{4,12},{8,0},{12,4},{16,24},{20,28},{24,16},{28,20},{1,9},{5... | collective-permute-start | bytes 12296 | tf_op jit(solution)/shard_map/ppermute | solution.py:20
  32.4 8.2 %collective-permute-start.12 = (bf16[1,2,2,64,256]{4,3,2,1,0:T(8,128)(2,1)S(1)}, bf16[1,2,2,64,256]{4,3,2,1,0:T(8,128)(2,1)S(1)}, u32[]{:S(2)}, u32[]{:S(2)}) collective-permute-start(bf16[1,2,2,64,256]{4,3,2,1,0:T(8,128)(2,1)S(1)} %get-tuple-element.29), channel_id=1, source_target_pairs={{0,2},{1,3},{2,0},{3,1},{4,6},{5,7},{6,4},{7,5},{8,10},{9,11},{10,... | collective-permute-start | bytes 393224 | tf_op jit(solution)/shard_map/ppermute | solution.py:20
  40.0 8.4 %collective-permute-start.14 = (bf16[1,2,2,64,256]{4,3,2,1,0:T(8,128)(2,1)S(1)}, bf16[1,2,2,64,256]{4,3,2,1,0:T(8,128)(2,1)S(1)}, u32[]{:S(2)}, u32[]{:S(2)}) collective-permute-start(bf16[1,2,2,64,256]{4,3,2,1,0:T(8,128)(2,1)S(1)} %get-tuple-element.34), channel_id=1, source_target_pairs={{0,2},{1,3},{2,0},{3,1},{4,6},{5,7},{6,4},{7,5},{8,10},{9,11},{10,... | collective-permute-start | bytes 393224 | tf_op jit(solution)/shard_map/ppermute | solution.py:20
  40.6 7.9 %collective-permute-start.15 = (f32[8,128]{1,0:T(8,128)S(1)}, f32[8,128]{1,0:T(8,128)S(1)}, u32[]{:S(2)}, u32[]{:S(2)}) collective-permute-start(f32[8,128]{1,0:T(8,128)S(1)} %add_add_fusion.refs_4_), channel_id=1, source_target_pairs={{0,1},{1,0},{2,3},{3,2},{4,5},{5,4},{6,7},{7,6},{8,9},{9,8},{10,11... | collective-permute-start | bytes 12296 | tf_op jit(solution)/shard_map/ppermute | solution.py:20
  43.1 5.4 %collective-permute-start.16 = (f32[8,128]{1,0:T(8,128)S(1)}, f32[8,128]{1,0:T(8,128)S(1)}, u32[]{:S(2)}, u32[]{:S(2)}) collective-permute-start(f32[8,128]{1,0:T(8,128)S(1)} %add_add_fusion.refs_4_), channel_id=1, source_target_pairs={{0,2},{1,3},{2,0},{3,1},{4,6},{5,7},{6,4},{7,5},{8,10},{9,11},{10,... | collective-permute-start | bytes 12296 | tf_op jit(solution)/shard_map/ppermute | solution.py:20
  46.3 5.4 %collective-permute-start.17 = (f32[8,128]{1,0:T(8,128)S(1)}, f32[8,128]{1,0:T(8,128)S(1)}, u32[]{:S(2)}, u32[]{:S(2)}) collective-permute-start(f32[8,128]{1,0:T(8,128)S(1)} %add_add_fusion.refs_4_), channel_id=1, source_target_pairs={{0,3},{1,2},{2,1},{3,0},{4,7},{5,6},{6,5},{7,4},{8,11},{9,10},{10,... | collective-permute-start | bytes 12296 | tf_op jit(solution)/shard_map/ppermute | solution.py:20

commit v9 on v7

--- a/solution.py
+++ b/solution.py
@@ -9,6 +9,7 @@
 
 MIB = 1 << 20
 TILE = (8, 128)
+TILE_ROWS = 16
 VMEM = pl.BlockSpec(memory_space=pltpu.VMEM)
 SMEM = pl.BlockSpec(memory_space=pltpu.SMEM)
 HBM = pl.BlockSpec(memory_space=pltpu.HBM)
@@ -59,7 +60,9 @@
         for pair in range(vectors.shape[1]):
             block = vectors[trial, pair]
             product = jnp.dot(stacked, block, preferred_element_type=jnp.float32)
-            inner[:, trial, pair] = product.astype(jnp.bfloat16).reshape(terms, states, states)
+            for term in range(terms):
+                part = product[term * states : (term + 1) * states].astype(jnp.bfloat16)
+                inner[trial, pair, :, term * states : (term + 1) * states] = part
             wide = block.astype(jnp.float32)
             square += jnp.sum((wide * wide).reshape(-1, 8, states), axis=0)
         sums.append(total(square) * square_scale)
@@ -82,7 +85,8 @@
         place_blocks(sectors, pieces, rights)
     else:
         rights, keep, send, tile, partial = rest
-    terms, trials, _, states, _ = inner.shape
+    trials, _, states, _ = inner.shape
+    terms = rights.shape[1]
     shares = 2 * keep.shape[0]
     rows = states // shares
     sector = lax.axis_index("sec")
@@ -90,15 +94,15 @@
     grams = [jnp.zeros((8, states), jnp.float32) for _ in range(trials * trials)]
     for local_pair in range(keep.shape[2]):
         pair = first + local_pair
-        result = None
+        blocks = []
         for term in range(terms):
             wanted = (sector + offsets[term, pair]) & (sectors - 1)
-            added = jnp.dot(
-                inner[term, :, pair].reshape(trials * states, states),
-                rights[sector ^ wanted, term],
-                preferred_element_type=jnp.float32,
-            )
-            result = added if result is None else result + added
+            blocks.append(rights[sector ^ wanted, term])
+        result = jnp.dot(
+            inner[:, pair].reshape(trials * states, terms * states),
+            jnp.concatenate(blocks, axis=0),
+            preferred_element_type=jnp.float32,
+        )
         partial[...] = result.reshape(trials, states, states)
         for j in range(trials):
             product = partial[j]
@@ -115,6 +119,20 @@
     tile[...] = before[...] + place_rows([(k, total(value)) for k, value in enumerate(grams)])
 
 
+def halve_last_kernel(kept, received, tile, keep, send):
+    keep[0] = kept[0] + received[0].astype(jnp.float32)
+    both = kept[1] + received[1].astype(jnp.float32)
+    lines = send.shape[0] - 3 * TILE_ROWS
+    send[:lines] = both.astype(jnp.bfloat16).reshape(lines, send.shape[1])
+    left = tile[...]
+    for part in range(3):
+        rounded = left.astype(jnp.bfloat16)
+        left = left - rounded.astype(jnp.float32)
+        block = jnp.concatenate([rounded, jnp.zeros_like(rounded)], axis=0)
+        start = lines + part * TILE_ROWS
+        send[start : start + TILE_ROWS] = jnp.concatenate([block, block], axis=1)
+
+
 def halve_kernel(kept, received, keep, send):
     for k in range(kept.shape[0]):
         both = kept[k] + received[k].astype(jnp.float32)
@@ -124,17 +142,28 @@
             keep[k // 2] = both
 
 
-def finish_kernel(*refs):
-    *parts, products = refs
-    first = 0
-    for kept, received in zip(parts[::2], parts[1::2]):
-        both = kept[0] + received[0].astype(jnp.float32)
-        products[:, first : first + both.shape[1]] = both.astype(jnp.bfloat16)
-        first += both.shape[1]
-
-
-def rayleigh_kernel(*refs):
-    *tiles, rayleigh = refs
+def ridden_tile(received):
+    lines = received.shape[0] - 3 * TILE_ROWS
+    parts = []
+    for part in range(3):
+        start = lines + part * TILE_ROWS
+        block = received[start : start + TILE_ROWS, : TILE[1]].astype(jnp.float32)
+        parts.append(block[: TILE[0]])
+    return parts[0] + parts[1] + parts[2]
+
+
+def add_ridden_kernel(tile, received, result):
+    result[...] = tile[...] + ridden_tile(received)
+
+
+def finish_kernel(first_kept, first_received, kept, received, *rest):
+    *tiles, products, rayleigh = rest
+    split = first_kept.shape[2]
+    lines = first_received.shape[0] - 3 * TILE_ROWS
+    both = first_received[:lines].astype(jnp.float32).reshape(first_kept.shape[1:])
+    products[:, :split] = (first_kept[0] + both).astype(jnp.bfloat16)
+    products[:, split:] = (kept[0] + received[0].astype(jnp.float32)).astype(jnp.bfloat16)
+
     tile = sum(part[...] for part in tiles)
     trials = rayleigh.shape[0]
     row = lax.broadcasted_iota(jnp.int32, rayleigh.shape, 0)
@@ -168,10 +197,6 @@
         steps.append([unit, 2 * unit, 3 * unit] if 2 * unit < count else [unit])
         low += 2
     return steps
-
-
-def chunk_sizes(pairs):
-    return [pairs // 2, pairs - pairs // 2]
 
 
 def call(kernel, name, flops, moved, limit, **kwargs):
@@ -199,7 +224,7 @@
         5 * MIB,
         12 * MIB,
         out_shape=(
-            jax.ShapeDtypeStruct((terms, trials, pairs, states, states), jnp.bfloat16),
+            jax.ShapeDtypeStruct((trials, pairs, states, terms * states), jnp.bfloat16),
             jax.ShapeDtypeStruct(TILE, jnp.float32),
             jax.ShapeDtypeStruct(right.shape, jnp.bfloat16),
         ),
@@ -218,8 +243,8 @@
         return jax.ShapeDtypeStruct((count, trials, size, rows, states), dtype)
 
     rights_shape = (sectors, terms, states, states)
-    sizes = chunk_sizes(pairs)
-    parts, rights, first = [], None, 0
+    sizes = [pairs // 2, pairs - pairs // 2]
+    sums, rights, first = [], None, 0
     for size in sizes:
         outs = [
             share_of(shares // 2, size, jnp.float32),
@@ -242,54 +267,67 @@
         )(in_hbm(offsets), vectors, inner, tile, *blocks)
         rights = placed[0] if placed else rights
         first += size
+        sums.append((keep, swap(send, "term", 1)))
+
+    for masks in [[1]] + steps_of(sectors, 1):
+        tile = add_places(tile, "sec", masks)
+
+    parts = []
+    for chunk, size in enumerate(sizes):
+        keep, received = sums[chunk]
         step = 1
-        received = swap(send, "term", step)
-        if first == pairs:
-            for masks in [[1]] + steps_of(sectors, 1):
-                tile = add_places(tile, "sec", masks)
-            others = tuple(parts[1::2])
-            tile, others = lax.optimization_barrier((tile, others))
-            parts[1::2] = others
         while 2 * step < shares:
             step *= 2
             count = shares // (2 * step)
+            last = count == 1 and chunk == 0
+            operands = (keep, received, tile) if last else (keep, received)
+            lines = trials * size * rows + 3 * TILE_ROWS
             keep, send = call(
-                halve_kernel,
+                halve_last_kernel if last else halve_kernel,
                 "halve_rows",
                 1,
                 1,
                 8 * MIB,
-                out_shape=(share_of(count, size, jnp.float32), share_of(count, size, jnp.bfloat16)),
-                in_specs=[VMEM, VMEM],
+                out_shape=(
+                    share_of(count, size, jnp.float32),
+                    jax.ShapeDtypeStruct((lines, states), jnp.bfloat16)
+                    if last
+                    else share_of(count, size, jnp.bfloat16),
+                ),
+                in_specs=[VMEM] * len(operands),
                 out_specs=(VMEM, VMEM),
-            )(keep, received)
+            )(*operands)
             received = swap(send, "term", step)
         parts += [keep, received]
 
-    *steps, last = steps_of(shares, 0)
-    for masks in steps:
-        tile = add_places(tile, "term", masks)
-    tiles = [tile] + [swap(tile, "term", mask) for mask in last]
-    rayleigh = call(
-        rayleigh_kernel,
-        "rayleigh",
+    tile = call(
+        add_ridden_kernel,
+        "add_ridden_tile",
         1,
         1,
         8 * MIB,
-        out_shape=jax.ShapeDtypeStruct((trials, trials), jnp.float32),
-        in_specs=[VMEM] * len(tiles),
+        out_shape=jax.ShapeDtypeStruct(TILE, jnp.float32),
+        in_specs=[VMEM, VMEM],
         out_specs=VMEM,
-    )(*tiles)
-    products = call(
+    )(tile, parts[1])
+    tiles, step = [tile], 1
+    while 2 * step < shares:
+        tile = tiles[0] if len(tiles) == 1 else tiles[0] + tiles[1]
+        tiles = [tile, swap(tile, "term", step)]
+        step *= 2
+    products, rayleigh = call(
         finish_kernel,
-        "add_last_share",
+        "finish",
         1,
         1,
         8 * MIB,
-        out_shape=jax.ShapeDtypeStruct((trials, pairs, rows, states), jnp.bfloat16),
-        in_specs=[VMEM] * len(parts),
-        out_specs=VMEM,
-    )(*parts)
+        out_shape=(
+            jax.ShapeDtypeStruct((trials, pairs, rows, states), jnp.bfloat16),
+            jax.ShapeDtypeStruct((trials, trials), jnp.float32),
+        ),
+        in_specs=[VMEM] * (len(parts) + len(tiles)),
+        out_specs=(VMEM, VMEM),
+    )(*parts, *tiles)
     return (products[:, None], rayleigh)
 
 

time: 50 us -> 52.2 us (1.044)
  waiting for transfers between devices: 19.1 us -> 24.8 us
  starting transfers between devices: 21.8 us -> 19 us
  Pallas kernels: 5.79 us -> 5.23 us
    ppermute x18 -> x16, waiting for transfers between devices: 19.1 us -> 24.8 us  [swap(): lax.ppermute(value, axis, [(place, place ^ masks[place & 1]) for place in...]
    ppermute x18 -> x16, starting transfers between devices: 21.8 us -> 19 us  [swap(): lax.ppermute(value, axis, [(place, place ^ masks[place & 1]) for place in...]
    pallas_call x4, Pallas kernels: 1.45 us -> 0.89 us  [the longest x1 0.76 us: local(): call(finish_kernel, 'finish', 1, 1, 8 * MIB, out_shape=(jax.ShapeDtypeStr...]
  transfers between devices with their start and end apart: 18 -> 16, of which waited for: 8 -> 11; matrix products, arithmetic and copies ran while one was open for 0% -> 0% of each run, Pallas kernels for 7% -> 5%
where the time goes in v9:
time: 52.2 us; the launch traced here: 51.9 us
  waiting for transfers between devices  24.8 us (48%)
  starting transfers between devices  19 us (36%)
  Pallas kernels  5.23 us (10%)
  local copies, waits for them, and re-layouts  2.22 us (4%)
  between operations  0.69 us (1%)
    ppermute x16, waiting for transfers between devices, swap(): lax.ppermute(value, axis, [(place, place ^ masks[place & 1]) for place in...  24.8 us
    ppermute x16, starting transfers between devices, swap(): lax.ppermute(value, axis, [(place, place ^ masks[place & 1]) for place in...  19 us
    pallas_call x2, Pallas kernels, local(): call(functools.partial(sum_kernel, sectors, first), 'sum_over_terms', 2 *...  3.34 us
    unnamed x4, local copies, waits for them, and re-layouts  2.22 us
  transfers between devices with their start and end apart: 16, of which 11 were waited for; matrix products, arithmetic and copies ran while one was open for 0% of the time, Pallas kernels for 5%

profile of v9, /device:TPU:0, one launch (start us, length us, event | category | flops | bytes accessed | tf_op | source)
XLA Modules:
  0.0 51.9 jit_solution(12931653453401239559)
XLA Ops:
  0.6 3.0 %collective-permute-start.1 = (bf16[3,256,256]{2,1,0:T(8,128)(2,1)}, bf16[3,256,256]{2,1,0:T(8,128)(2,1)S(1)}, u32[]{:S(2)}, u32[]{:S(2)}) collective-permute-start(bf16[3,256,256]{2,1,0:T(8,128)(2,1)} %bitcast.10), channel_id=1, source_target_pairs={{0,8},{4,20},{8,0},{12,28},{16,24},{20,4},{24,16},{28,12},{1,9},{5... | collective-permute-start | bytes 1179656 | tf_op jit(solution)/shard_map/ppermute | solution.py:21
  3.6 1.2 %copy-done = bf16[2,1,4,256,256]{4,3,2,1,0:T(8,128)(2,1)S(1)} copy-done((bf16[2,1,4,256,256]{4,3,2,1,0:T(8,128)(2,1)S(1)}, bf16[2,1,4,256,256]{4,3,2,1,0:T(8,128)(2,1)}, u32[]{:S(2)}) %copy-start) | copy-done | bytes 1048600
  4.9 1.0 %copy-done.1 = bf16[3,1,256,256]{3,2,1,0:T(8,128)(2,1)S(1)} copy-done((bf16[3,1,256,256]{3,2,1,0:T(8,128)(2,1)S(1)}, bf16[3,1,256,256]{3,2,1,0:T(8,128)(2,1)}, u32[]{:S(2)}) %copy-start.1) | copy-done | bytes 393240
  5.9 1.0 %inner_products.1 = (bf16[2,4,256,768]{3,2,1,0:T(8,128)(2,1)S(1)}, f32[8,128]{1,0:T(8,128)S(1)}, bf16[3,256,256]{2,1,0:T(8,128)(2,1)S(1)}) custom-call(bf16[2,4,256,256]{3,2,1,0:T(8,128)(2,1)S(1)} %bitcast.6, bf16[3,256,256]{2,1,0:T(8,128)(2,1)S(1)} %bitcast.9, bf16[3,256,256]{2,1,0:T(8,128)(2,1)} %bitcast.11), custom_call_target="tpu_custom_call" | custom-call | flops 805306368 | bytes 5242880 | tf_op jit(solution)/shard_map/inner_products/pallas_call | solution.py:220
  6.9 1.6 %collective-permute-start.3 = (bf16[3,256,256]{2,1,0:T(8,128)(2,1)}, bf16[3,256,256]{2,1,0:T(8,128)(2,1)S(1)}, u32[]{:S(2)}, u32[]{:S(2)}) collective-permute-start(bf16[3,256,256]{2,1,0:T(8,128)(2,1)} %bitcast.12), channel_id=1, source_target_pairs={{0,16},{4,12},{8,24},{12,4},{16,0},{20,28},{24,8},{28,20},{1,17},{... | collective-permute-start | bytes 1179656 | tf_op jit(solution)/shard_map/ppermute | solution.py:21
  8.5 1.5 %collective-permute-done.1.rest_2_ = bf16[3,256,256]{2,1,0:T(8,128)(2,1)S(1)} collective-permute-done((bf16[3,256,256]{2,1,0:T(8,128)(2,1)}, bf16[3,256,256]{2,1,0:T(8,128)(2,1)S(1)}, u32[]{:S(2)}, u32[]{:S(2)}) %collective-permute-start.1) | collective-permute-done | bytes 393248 | tf_op jit(solution)/shard_map/ppermute | solution.py:21
  10.0 3.6 %collective-permute-start.5 = (bf16[3,256,256]{2,1,0:T(8,128)(2,1)S(1)}, bf16[3,256,256]{2,1,0:T(8,128)(2,1)S(1)}, u32[]{:S(2)}, u32[]{:S(2)}) collective-permute-start(bf16[3,256,256]{2,1,0:T(8,128)(2,1)S(1)} %collective-permute-done.1.rest_2_), channel_id=1, source_target_pairs={{0,16},{4,12},{8,24},{12,4},{16,0},{20,28},{24,8},{28,20},{1,17},{... | collective-permute-start | bytes 1179656 | tf_op jit(solution)/shard_map/ppermute | solution.py:21
  14.1 0.8 %collective-permute-done.3.rest_4_ = bf16[3,256,256]{2,1,0:T(8,128)(2,1)S(1)} collective-permute-done((bf16[3,256,256]{2,1,0:T(8,128)(2,1)}, bf16[3,256,256]{2,1,0:T(8,128)(2,1)S(1)}, u32[]{:S(2)}, u32[]{:S(2)}) %collective-permute-start.3) | collective-permute-done | bytes 393248 | tf_op jit(solution)/shard_map/ppermute | solution.py:21
  14.9 4.4 %collective-permute-done.5.rest_6_ = bf16[3,256,256]{2,1,0:T(8,128)(2,1)S(1)} collective-permute-done((bf16[3,256,256]{2,1,0:T(8,128)(2,1)S(1)}, bf16[3,256,256]{2,1,0:T(8,128)(2,1)S(1)}, u32[]{:S(2)}, u32[]{:S(2)}) %collective-permute-start.5) | collective-permute-done | bytes 393248 | tf_op jit(solution)/shard_map/ppermute | solution.py:21
  19.4 1.7 %collective-permute-done.6.rest_7_ = bf16[3,256,256]{2,1,0:T(8,128)(2,1)S(1)} collective-permute-done((bf16[3,256,256]{2,1,0:T(8,128)(2,1)S(1)}, bf16[3,256,256]{2,1,0:T(8,128)(2,1)S(1)}, u32[]{:S(2)}, u32[]{:S(2)}) %collective-permute-start.6) | collective-permute-done | bytes 393248 | tf_op jit(solution)/shard_map/ppermute | solution.py:21
  21.1 1.8 %sum_over_terms.2 = (f32[2,2,2,64,256]{4,3,2,1,0:T(8,128)S(1)}, bf16[2,2,2,64,256]{4,3,2,1,0:T(8,128)(2,1)S(1)}, f32[8,128]{1,0:T(8,128)S(1)}, bf16[8,3,256,256]{3,2,1,0:T(8,128)(2,1)S(1)}) custom-call(s32[3,4]{1,0:T(4,128)} %offsets.3, bf16[2,4,256,256]{3,2,1,0:T(8,128)(2,1)S(1)} %bitcast.7, bf16[2,4,256,768]{3,2,1,0:T(8,128)(2,1)S(1)} %get-tuple-element.19.inner, ...), custom_call_target="tpu_custom_call" | custom-call | flops 402653184 | bytes 4194304 | tf_op jit(solution)/shard_map/sum_over_terms/pallas_call | solution.py:257
  22.9 1.4 %collective-permute-start.7 = (bf16[2,2,2,64,256]{4,3,2,1,0:T(8,128)(2,1)S(1)}, bf16[2,2,2,64,256]{4,3,2,1,0:T(8,128)(2,1)S(1)}, u32[]{:S(2)}, u32[]{:S(2)}) collective-permute-start(bf16[2,2,2,64,256]{4,3,2,1,0:T(8,128)(2,1)S(1)} %get-tuple-element.24), channel_id=1, source_target_pairs={{0,1},{1,0},{2,3},{3,2},{4,5},{5,4},{6,7},{7,6},{8,9},{9,8},{10,11... | collective-permute-start | bytes 786440 | tf_op jit(solution)/shard_map/ppermute | solution.py:21
  24.3 1.6 %sum_over_terms.3 = (f32[2,2,2,64,256]{4,3,2,1,0:T(8,128)S(1)}, bf16[2,2,2,64,256]{4,3,2,1,0:T(8,128)(2,1)S(1)}, f32[8,128]{1,0:T(8,128)S(1)}) custom-call(s32[3,4]{1,0:T(4,128)} %offsets.3, bf16[2,4,256,256]{3,2,1,0:T(8,128)(2,1)S(1)} %bitcast.8, bf16[2,4,256,768]{3,2,1,0:T(8,128)(2,1)S(1)} %get-tuple-element.19.inner, ...), custom_call_target="tpu_custom_call" | custom-call | flops 402653184 | bytes 4194304 | tf_op jit(solution)/shard_map/sum_over_terms/pallas_call | solution.py:257
  26.5 1.2 %collective-permute-done.8 = f32[8,128]{1,0:T(8,128)S(1)} collective-permute-done((f32[8,128]{1,0:T(8,128)S(1)}, f32[8,128]{1,0:T(8,128)S(1)}, u32[]{:S(2)}, u32[]{:S(2)}) %collective-permute-start.8) | collective-permute-done | bytes 4128 | tf_op jit(solution)/shard_map/ppermute | solution.py:21
  27.7 2.7 %collective-permute-start.11 = (f32[8,128]{1,0:T(8,128)S(1)}, f32[8,128]{1,0:T(8,128)S(1)}, u32[]{:S(2)}, u32[]{:S(2)}) collective-permute-start(f32[8,128]{1,0:T(8,128)S(1)} %add.12), channel_id=1, source_target_pairs={{0,24},{4,28},{8,16},{12,20},{16,8},{20,12},{24,0},{28,4},{1,25},{... | collective-permute-start | bytes 12296 | tf_op jit(solution)/shard_map/ppermute | solution.py:21
  31.2 1.0 %collective-permute-done.11 = f32[8,128]{1,0:T(8,128)S(1)} collective-permute-done((f32[8,128]{1,0:T(8,128)S(1)}, f32[8,128]{1,0:T(8,128)S(1)}, u32[]{:S(2)}, u32[]{:S(2)}) %collective-permute-start.11) | collective-permute-done | bytes 4128 | tf_op jit(solution)/shard_map/ppermute | solution.py:21
  32.2 1.8 %collective-permute-done.10 = f32[8,128]{1,0:T(8,128)S(1)} collective-permute-done((f32[8,128]{1,0:T(8,128)S(1)}, f32[8,128]{1,0:T(8,128)S(1)}, u32[]{:S(2)}, u32[]{:S(2)}) %collective-permute-start.10) | collective-permute-done | bytes 4128 | tf_op jit(solution)/shard_map/ppermute | solution.py:21
  34.1 2.7 %collective-permute-start.12 = (bf16[304,256]{1,0:T(8,128)(2,1)S(1)}, bf16[304,256]{1,0:T(8,128)(2,1)S(1)}, u32[]{:S(2)}, u32[]{:S(2)}) collective-permute-start(bf16[304,256]{1,0:T(8,128)(2,1)S(1)} %get-tuple-element.29), channel_id=1, source_target_pairs={{0,2},{1,3},{2,0},{3,1},{4,6},{5,7},{6,4},{7,5},{8,10},{9,11},{10,... | collective-permute-start | bytes 466952 | tf_op jit(solution)/shard_map/ppermute | solution.py:21
  36.8 1.3 %collective-permute-done.13.received = bf16[2,2,2,64,256]{4,3,2,1,0:T(8,128)(2,1)S(1)} collective-permute-done((bf16[2,2,2,64,256]{4,3,2,1,0:T(8,128)(2,1)S(1)}, bf16[2,2,2,64,256]{4,3,2,1,0:T(8,128)(2,1)S(1)}, u32[]{:S(2)}, u32[]{:S(2)}) %collective-permute-start.13) | collective-permute-done | bytes 262176 | tf_op jit(solution)/shard_map/ppermute | solution.py:21
  38.1 2.0 %collective-permute-start.14 = (bf16[1,2,2,64,256]{4,3,2,1,0:T(8,128)(2,1)S(1)}, bf16[1,2,2,64,256]{4,3,2,1,0:T(8,128)(2,1)S(1)}, u32[]{:S(2)}, u32[]{:S(2)}) collective-permute-start(bf16[1,2,2,64,256]{4,3,2,1,0:T(8,128)(2,1)S(1)} %get-tuple-element.33), channel_id=1, source_target_pairs={{0,2},{1,3},{2,0},{3,1},{4,6},{5,7},{6,4},{7,5},{8,10},{9,11},{10,... | collective-permute-start | bytes 393224 | tf_op jit(solution)/shard_map/ppermute | solution.py:21
  40.2 7.4 %collective-permute-done.12.received.first_received = bf16[304,256]{1,0:T(8,128)(2,1)S(1)} collective-permute-done((bf16[304,256]{1,0:T(8,128)(2,1)S(1)}, bf16[304,256]{1,0:T(8,128)(2,1)S(1)}, u32[]{:S(2)}, u32[]{:S(2)}) %collective-permute-start.12) | collective-permute-done | bytes 155680 | tf_op jit(solution)/shard_map/ppermute | solution.py:21
  47.5 1.5 %collective-permute-done.14.received = bf16[1,2,2,64,256]{4,3,2,1,0:T(8,128)(2,1)S(1)} collective-permute-done((bf16[1,2,2,64,256]{4,3,2,1,0:T(8,128)(2,1)S(1)}, bf16[1,2,2,64,256]{4,3,2,1,0:T(8,128)(2,1)S(1)}, u32[]{:S(2)}, u32[]{:S(2)}) %collective-permute-start.14) | collective-permute-done | bytes 131104 | tf_op jit(solution)/shard_map/ppermute | solution.py:21
  49.1 2.1 %collective-permute-done.15.rest_1_ = f32[8,128]{1,0:T(8,128)S(1)} collective-permute-done((f32[8,128]{1,0:T(8,128)S(1)}, f32[8,128]{1,0:T(8,128)S(1)}, u32[]{:S(2)}, u32[]{:S(2)}) %collective-permute-start.15) | collective-permute-done | bytes 4128 | tf_op jit(solution)/shard_map/ppermute | solution.py:21
  51.1 0.8 %finish.1 = (bf16[2,4,64,256]{3,2,1,0:T(8,128)(2,1)}, f32[2,2]{1,0:T(2,128)}) custom-call(f32[1,2,2,64,256]{4,3,2,1,0:T(8,128)S(1)} %get-tuple-element.28.first_kept, bf16[304,256]{1,0:T(8,128)(2,1)S(1)} %collective-permute-done.12.received.first_received, f32[1,2,2,64,256]{4,3,2,1,0:T(8,128)S(1)} %get-tuple-element.32.kept, ...), custom_call_target="tpu_custom_call" | custom-call | flops 1 | bytes 1 | tf_op jit(solution)/shard_map/finish/pallas_call | solution.py:318
  (21 shorter events, 2.1 us)
Async XLA Ops:
  0.6 9.4 %collective-permute-start.1 = (bf16[3,256,256]{2,1,0:T(8,128)(2,1)}, bf16[3,256,256]{2,1,0:T(8,128)(2,1)S(1)}, u32[]{:S(2)}, u32[]{:S(2)}) collective-permute-start(bf16[3,256,256]{2,1,0:T(8,128)(2,1)} %bitcast.10), channel_id=1, source_target_pairs={{0,8},{4,20},{8,0},{12,28},{16,24},{20,4},{24,16},{28,12},{1,9},{5... | collective-permute-start | bytes 1179656 | tf_op jit(solution)/shard_map/ppermute | solution.py:21
  3.6 1.2 %copy-start = (bf16[2,1,4,256,256]{4,3,2,1,0:T(8,128)(2,1)S(1)}, bf16[2,1,4,256,256]{4,3,2,1,0:T(8,128)(2,1)}, u32[]{:S(2)}) copy-start(bf16[2,1,4,256,256]{4,3,2,1,0:T(8,128)(2,1)} %param.4) | copy-start | bytes 3145732
  4.9 1.0 %copy-start.1 = (bf16[3,1,256,256]{3,2,1,0:T(8,128)(2,1)S(1)}, bf16[3,1,256,256]{3,2,1,0:T(8,128)(2,1)}, u32[]{:S(2)}) copy-start(bf16[3,1,256,256]{3,2,1,0:T(8,128)(2,1)} %param.5) | copy-start | bytes 1179652
  6.9 8.1 %collective-permute-start.3 = (bf16[3,256,256]{2,1,0:T(8,128)(2,1)}, bf16[3,256,256]{2,1,0:T(8,128)(2,1)S(1)}, u32[]{:S(2)}, u32[]{:S(2)}) collective-permute-start(bf16[3,256,256]{2,1,0:T(8,128)(2,1)} %bitcast.12), channel_id=1, source_target_pairs={{0,16},{4,12},{8,24},{12,4},{16,0},{20,28},{24,8},{28,20},{1,17},{... | collective-permute-start | bytes 1179656 | tf_op jit(solution)/shard_map/ppermute | solution.py:21
  10.0 9.4 %collective-permute-start.5 = (bf16[3,256,256]{2,1,0:T(8,128)(2,1)S(1)}, bf16[3,256,256]{2,1,0:T(8,128)(2,1)S(1)}, u32[]{:S(2)}, u32[]{:S(2)}) collective-permute-start(bf16[3,256,256]{2,1,0:T(8,128)(2,1)S(1)} %collective-permute-done.1.rest_2_), channel_id=1, source_target_pairs={{0,16},{4,12},{8,24},{12,4},{16,0},{20,28},{24,8},{28,20},{1,17},{... | collective-permute-start | bytes 1179656 | tf_op jit(solution)/shard_map/ppermute | solution.py:21
  13.6 5.8 %collective-permute-start = (bf16[3,256,256]{2,1,0:T(8,128)(2,1)}, bf16[3,256,256]{2,1,0:T(8,128)(2,1)S(1)}, u32[]{:S(2)}, u32[]{:S(2)}) collective-permute-start(bf16[3,256,256]{2,1,0:T(8,128)(2,1)} %bitcast.13), channel_id=1, source_target_pairs={{0,4},{4,0},{8,12},{12,8},{16,20},{20,16},{24,28},{28,24},{1,5},{5... | collective-permute-start | bytes 1179656 | tf_op jit(solution)/shard_map/ppermute | solution.py:21
  13.6 5.8 %collective-permute-start.2 = (bf16[3,256,256]{2,1,0:T(8,128)(2,1)S(1)}, bf16[3,256,256]{2,1,0:T(8,128)(2,1)S(1)}, u32[]{:S(2)}, u32[]{:S(2)}) collective-permute-start(bf16[3,256,256]{2,1,0:T(8,128)(2,1)S(1)} %collective-permute-done.1.rest_2_), channel_id=1, source_target_pairs={{0,4},{4,0},{8,12},{12,8},{16,20},{20,16},{24,28},{28,24},{1,5},{5... | collective-permute-start | bytes 1179656 | tf_op jit(solution)/shard_map/ppermute | solution.py:21
  14.9 4.5 %collective-permute-start.4 = (bf16[3,256,256]{2,1,0:T(8,128)(2,1)S(1)}, bf16[3,256,256]{2,1,0:T(8,128)(2,1)S(1)}, u32[]{:S(2)}, u32[]{:S(2)}) collective-permute-start(bf16[3,256,256]{2,1,0:T(8,128)(2,1)S(1)} %collective-permute-done.3.rest_4_), channel_id=1, source_target_pairs={{0,4},{4,0},{8,12},{12,8},{16,20},{20,16},{24,28},{28,24},{1,5},{5... | collective-permute-start | bytes 1179656 | tf_op jit(solution)/shard_map/ppermute | solution.py:21
  19.4 1.7 %collective-permute-start.6 = (bf16[3,256,256]{2,1,0:T(8,128)(2,1)S(1)}, bf16[3,256,256]{2,1,0:T(8,128)(2,1)S(1)}, u32[]{:S(2)}, u32[]{:S(2)}) collective-permute-start(bf16[3,256,256]{2,1,0:T(8,128)(2,1)S(1)} %collective-permute-done.5.rest_6_), channel_id=1, source_target_pairs={{0,4},{4,0},{8,12},{12,8},{16,20},{20,16},{24,28},{28,24},{1,5},{5... | collective-permute-start | bytes 1179656 | tf_op jit(solution)/shard_map/ppermute | solution.py:21
  22.9 11.2 %collective-permute-start.7 = (bf16[2,2,2,64,256]{4,3,2,1,0:T(8,128)(2,1)S(1)}, bf16[2,2,2,64,256]{4,3,2,1,0:T(8,128)(2,1)S(1)}, u32[]{:S(2)}, u32[]{:S(2)}) collective-permute-start(bf16[2,2,2,64,256]{4,3,2,1,0:T(8,128)(2,1)S(1)} %get-tuple-element.24), channel_id=1, source_target_pairs={{0,1},{1,0},{2,3},{3,2},{4,5},{5,4},{6,7},{7,6},{8,9},{9,8},{10,11... | collective-permute-start | bytes 786440 | tf_op jit(solution)/shard_map/ppermute | solution.py:21
  25.8 12.2 %collective-permute-start.13 = (bf16[2,2,2,64,256]{4,3,2,1,0:T(8,128)(2,1)S(1)}, bf16[2,2,2,64,256]{4,3,2,1,0:T(8,128)(2,1)S(1)}, u32[]{:S(2)}, u32[]{:S(2)}) collective-permute-start(bf16[2,2,2,64,256]{4,3,2,1,0:T(8,128)(2,1)S(1)} %get-tuple-element.31), channel_id=1, source_target_pairs={{0,1},{1,0},{2,3},{3,2},{4,5},{5,4},{6,7},{7,6},{8,9},{9,8},{10,11... | collective-permute-start | bytes 786440 | tf_op jit(solution)/shard_map/ppermute | solution.py:21
  26.5 1.2 %collective-permute-start.8 = (f32[8,128]{1,0:T(8,128)S(1)}, f32[8,128]{1,0:T(8,128)S(1)}, u32[]{:S(2)}, u32[]{:S(2)}) collective-permute-start(f32[8,128]{1,0:T(8,128)S(1)} %get-tuple-element.27), channel_id=1, source_target_pairs={{0,4},{4,0},{8,12},{12,8},{16,20},{20,16},{24,28},{28,24},{1,5},{5... | collective-permute-start | bytes 12296 | tf_op jit(solution)/shard_map/ppermute | solution.py:21
  27.7 4.5 %collective-permute-start.11 = (f32[8,128]{1,0:T(8,128)S(1)}, f32[8,128]{1,0:T(8,128)S(1)}, u32[]{:S(2)}, u32[]{:S(2)}) collective-permute-start(f32[8,128]{1,0:T(8,128)S(1)} %add.12), channel_id=1, source_target_pairs={{0,24},{4,28},{8,16},{12,20},{16,8},{20,12},{24,0},{28,4},{1,25},{... | collective-permute-start | bytes 12296 | tf_op jit(solution)/shard_map/ppermute | solution.py:21
  30.4 3.6 %collective-permute-start.10 = (f32[8,128]{1,0:T(8,128)S(1)}, f32[8,128]{1,0:T(8,128)S(1)}, u32[]{:S(2)}, u32[]{:S(2)}) collective-permute-start(f32[8,128]{1,0:T(8,128)S(1)} %add.12), channel_id=1, source_target_pairs={{0,16},{4,20},{8,24},{12,28},{16,0},{20,4},{24,8},{28,12},{1,17},{... | collective-permute-start | bytes 12296 | tf_op jit(solution)/shard_map/ppermute | solution.py:21
  30.4 3.6 %collective-permute-start.9 = (f32[8,128]{1,0:T(8,128)S(1)}, f32[8,128]{1,0:T(8,128)S(1)}, u32[]{:S(2)}, u32[]{:S(2)}) collective-permute-start(f32[8,128]{1,0:T(8,128)S(1)} %add.12), channel_id=1, source_target_pairs={{0,8},{4,12},{8,0},{12,4},{16,24},{20,28},{24,16},{28,20},{1,9},{5... | collective-permute-start | bytes 12296 | tf_op jit(solution)/shard_map/ppermute | solution.py:21
  34.1 13.4 %collective-permute-start.12 = (bf16[304,256]{1,0:T(8,128)(2,1)S(1)}, bf16[304,256]{1,0:T(8,128)(2,1)S(1)}, u32[]{:S(2)}, u32[]{:S(2)}) collective-permute-start(bf16[304,256]{1,0:T(8,128)(2,1)S(1)} %get-tuple-element.29), channel_id=1, source_target_pairs={{0,2},{1,3},{2,0},{3,1},{4,6},{5,7},{6,4},{7,5},{8,10},{9,11},{10,... | collective-permute-start | bytes 466952 | tf_op jit(solution)/shard_map/ppermute | solution.py:21
  38.1 10.9 %collective-permute-start.14 = (bf16[1,2,2,64,256]{4,3,2,1,0:T(8,128)(2,1)S(1)}, bf16[1,2,2,64,256]{4,3,2,1,0:T(8,128)(2,1)S(1)}, u32[]{:S(2)}, u32[]{:S(2)}) collective-permute-start(bf16[1,2,2,64,256]{4,3,2,1,0:T(8,128)(2,1)S(1)} %get-tuple-element.33), channel_id=1, source_target_pairs={{0,2},{1,3},{2,0},{3,1},{4,6},{5,7},{6,4},{7,5},{8,10},{9,11},{10,... | collective-permute-start | bytes 393224 | tf_op jit(solution)/shard_map/ppermute | solution.py:21
  47.5 3.6 %collective-permute-start.15 = (f32[8,128]{1,0:T(8,128)S(1)}, f32[8,128]{1,0:T(8,128)S(1)}, u32[]{:S(2)}, u32[]{:S(2)}) collective-permute-start(f32[8,128]{1,0:T(8,128)S(1)} %add_ridden_tile.1.rest_0_), channel_id=1, source_target_pairs={{0,1},{1,0},{2,3},{3,2},{4,5},{5,4},{6,7},{7,6},{8,9},{9,8},{10,11... | collective-permute-start | bytes 12296 | tf_op jit(solution)/shard_map/ppermute | solution.py:21

commit v10 on v9

--- a/solution.py
+++ b/solution.py
@@ -152,19 +152,18 @@
     return parts[0] + parts[1] + parts[2]
 
 
-def add_ridden_kernel(tile, received, result):
-    result[...] = tile[...] + ridden_tile(received)
-
-
-def finish_kernel(first_kept, first_received, kept, received, *rest):
-    *tiles, products, rayleigh = rest
-    split = first_kept.shape[2]
-    lines = first_received.shape[0] - 3 * TILE_ROWS
-    both = first_received[:lines].astype(jnp.float32).reshape(first_kept.shape[1:])
-    products[:, :split] = (first_kept[0] + both).astype(jnp.bfloat16)
-    products[:, split:] = (kept[0] + received[0].astype(jnp.float32)).astype(jnp.bfloat16)
-
-    tile = sum(part[...] for part in tiles)
+def add_last_kernel(kept, received, result):
+    result[...] = (kept[0] + received[0].astype(jnp.float32)).astype(jnp.bfloat16)
+
+
+def finish_kernel(done, kept, received, tile, products, rayleigh):
+    first = done.shape[1]
+    lines = received.shape[0] - 3 * TILE_ROWS
+    both = received[:lines].astype(jnp.float32).reshape(kept.shape[1:])
+    products[:, :first] = done[...]
+    products[:, first:] = (kept[0] + both).astype(jnp.bfloat16)
+
+    tile = tile[...] + ridden_tile(received)
     trials = rayleigh.shape[0]
     row = lax.broadcasted_iota(jnp.int32, rayleigh.shape, 0)
     column = lax.broadcasted_iota(jnp.int32, rayleigh.shape, 1)
@@ -272,6 +271,11 @@
     for masks in [[1]] + steps_of(sectors, 1):
         tile = add_places(tile, "sec", masks)
 
+    step = 1
+    while 2 * step < shares:
+        tile = add_places(tile, "term", [step])
+        step *= 2
+
     parts = []
     for chunk, size in enumerate(sizes):
         keep, received = sums[chunk]
@@ -279,7 +283,7 @@
         while 2 * step < shares:
             step *= 2
             count = shares // (2 * step)
-            last = count == 1 and chunk == 0
+            last = count == 1 and chunk == len(sizes) - 1
             operands = (keep, received, tile) if last else (keep, received)
             lines = trials * size * rows + 3 * TILE_ROWS
             keep, send = call(
@@ -300,21 +304,17 @@
             received = swap(send, "term", step)
         parts += [keep, received]
 
-    tile = call(
-        add_ridden_kernel,
-        "add_ridden_tile",
-        1,
+    kept, received, *second = parts
+    done = call(
+        add_last_kernel,
+        "add_last_share",
+        10**10,
         1,
         8 * MIB,
-        out_shape=jax.ShapeDtypeStruct(TILE, jnp.float32),
+        out_shape=jax.ShapeDtypeStruct((trials, sizes[0], rows, states), jnp.bfloat16),
         in_specs=[VMEM, VMEM],
         out_specs=VMEM,
-    )(tile, parts[1])
-    tiles, step = [tile], 1
-    while 2 * step < shares:
-        tile = tiles[0] if len(tiles) == 1 else tiles[0] + tiles[1]
-        tiles = [tile, swap(tile, "term", step)]
-        step *= 2
+    )(kept, received)
     products, rayleigh = call(
         finish_kernel,
         "finish",
@@ -325,9 +325,9 @@
             jax.ShapeDtypeStruct((trials, pairs, rows, states), jnp.bfloat16),
             jax.ShapeDtypeStruct((trials, trials), jnp.float32),
         ),
-        in_specs=[VMEM] * (len(parts) + len(tiles)),
+        in_specs=[VMEM] * 4,
         out_specs=(VMEM, VMEM),
-    )(*parts, *tiles)
+    )(done, *second, tile)
     return (products[:, None], rayleigh)
 
 

time: 52.2 us -> 50.4 us (0.966)
  waiting for transfers between devices: 24.8 us -> 21.1 us
  starting transfers between devices: 19 us -> 20.8 us
    ppermute x16, waiting for transfers between devices: 24.8 us -> 21.1 us  [swap(): lax.ppermute(value, axis, [(place, place ^ masks[place & 1]) for place in...]
    ppermute x16, starting transfers between devices: 19 us -> 20.8 us  [swap(): lax.ppermute(value, axis, [(place, place ^ masks[place & 1]) for place in...]
  transfers between devices with their start and end apart: 16 -> 16, of which waited for: 11 -> 8; matrix products, arithmetic and copies ran while one was open for 0% -> 0% of each run, Pallas kernels for 5% -> 5%
where the time goes in v10:
time: 50.4 us; the launch traced here: 50.1 us
  waiting for transfers between devices  21.1 us (42%)
  starting transfers between devices  20.8 us (41%)
  Pallas kernels  5.24 us (10%)
  local copies, waits for them, and re-layouts  2.22 us (4%)
  between operations  0.69 us (1%)
    ppermute x16, waiting for transfers between devices, swap(): lax.ppermute(value, axis, [(place, place ^ masks[place & 1]) for place in...  21.1 us
    ppermute x16, starting transfers between devices, swap(): lax.ppermute(value, axis, [(place, place ^ masks[place & 1]) for place in...  20.8 us
    pallas_call x2, Pallas kernels, local(): call(functools.partial(sum_kernel, sectors, first), 'sum_over_terms', 2 *...  3.34 us
    unnamed x4, local copies, waits for them, and re-layouts  2.22 us
  transfers between devices with their start and end apart: 16, of which 8 were waited for; matrix products, arithmetic and copies ran while one was open for 0% of the time, Pallas kernels for 5%

profile of v10, /device:TPU:0, one launch (start us, length us, event | category | flops | bytes accessed | tf_op | source)
XLA Modules:
  0.0 50.1 jit_solution(1666940117732785833)
XLA Ops:
  0.6 3.0 %collective-permute-start.1 = (bf16[3,256,256]{2,1,0:T(8,128)(2,1)}, bf16[3,256,256]{2,1,0:T(8,128)(2,1)S(1)}, u32[]{:S(2)}, u32[]{:S(2)}) collective-permute-start(bf16[3,256,256]{2,1,0:T(8,128)(2,1)} %bitcast.10), channel_id=1, source_target_pairs={{0,8},{4,20},{8,0},{12,28},{16,24},{20,4},{24,16},{28,12},{1,9},{5... | collective-permute-start | bytes 1179656 | tf_op jit(solution)/shard_map/ppermute | solution.py:21
  3.6 1.2 %copy-done = bf16[2,1,4,256,256]{4,3,2,1,0:T(8,128)(2,1)S(1)} copy-done((bf16[2,1,4,256,256]{4,3,2,1,0:T(8,128)(2,1)S(1)}, bf16[2,1,4,256,256]{4,3,2,1,0:T(8,128)(2,1)}, u32[]{:S(2)}) %copy-start) | copy-done | bytes 1048600
  4.9 1.0 %copy-done.1 = bf16[3,1,256,256]{3,2,1,0:T(8,128)(2,1)S(1)} copy-done((bf16[3,1,256,256]{3,2,1,0:T(8,128)(2,1)S(1)}, bf16[3,1,256,256]{3,2,1,0:T(8,128)(2,1)}, u32[]{:S(2)}) %copy-start.1) | copy-done | bytes 393240
  5.9 1.0 %inner_products.1 = (bf16[2,4,256,768]{3,2,1,0:T(8,128)(2,1)S(1)}, f32[8,128]{1,0:T(8,128)S(1)}, bf16[3,256,256]{2,1,0:T(8,128)(2,1)S(1)}) custom-call(bf16[2,4,256,256]{3,2,1,0:T(8,128)(2,1)S(1)} %bitcast.6, bf16[3,256,256]{2,1,0:T(8,128)(2,1)S(1)} %bitcast.9, bf16[3,256,256]{2,1,0:T(8,128)(2,1)} %bitcast.11), custom_call_target="tpu_custom_call" | custom-call | flops 805306368 | bytes 5242880 | tf_op jit(solution)/shard_map/inner_products/pallas_call | solution.py:219
  6.9 1.6 %collective-permute-start.3 = (bf16[3,256,256]{2,1,0:T(8,128)(2,1)}, bf16[3,256,256]{2,1,0:T(8,128)(2,1)S(1)}, u32[]{:S(2)}, u32[]{:S(2)}) collective-permute-start(bf16[3,256,256]{2,1,0:T(8,128)(2,1)} %bitcast.12), channel_id=1, source_target_pairs={{0,16},{4,12},{8,24},{12,4},{16,0},{20,28},{24,8},{28,20},{1,17},{... | collective-permute-start | bytes 1179656 | tf_op jit(solution)/shard_map/ppermute | solution.py:21
  8.5 1.5 %collective-permute-done.1.rest_2_ = bf16[3,256,256]{2,1,0:T(8,128)(2,1)S(1)} collective-permute-done((bf16[3,256,256]{2,1,0:T(8,128)(2,1)}, bf16[3,256,256]{2,1,0:T(8,128)(2,1)S(1)}, u32[]{:S(2)}, u32[]{:S(2)}) %collective-permute-start.1) | collective-permute-done | bytes 393248 | tf_op jit(solution)/shard_map/ppermute | solution.py:21
  10.0 3.6 %collective-permute-start.5 = (bf16[3,256,256]{2,1,0:T(8,128)(2,1)S(1)}, bf16[3,256,256]{2,1,0:T(8,128)(2,1)S(1)}, u32[]{:S(2)}, u32[]{:S(2)}) collective-permute-start(bf16[3,256,256]{2,1,0:T(8,128)(2,1)S(1)} %collective-permute-done.1.rest_2_), channel_id=1, source_target_pairs={{0,16},{4,12},{8,24},{12,4},{16,0},{20,28},{24,8},{28,20},{1,17},{... | collective-permute-start | bytes 1179656 | tf_op jit(solution)/shard_map/ppermute | solution.py:21
  14.1 0.8 %collective-permute-done.3.rest_4_ = bf16[3,256,256]{2,1,0:T(8,128)(2,1)S(1)} collective-permute-done((bf16[3,256,256]{2,1,0:T(8,128)(2,1)}, bf16[3,256,256]{2,1,0:T(8,128)(2,1)S(1)}, u32[]{:S(2)}, u32[]{:S(2)}) %collective-permute-start.3) | collective-permute-done | bytes 393248 | tf_op jit(solution)/shard_map/ppermute | solution.py:21
  14.9 4.4 %collective-permute-done.5.rest_6_ = bf16[3,256,256]{2,1,0:T(8,128)(2,1)S(1)} collective-permute-done((bf16[3,256,256]{2,1,0:T(8,128)(2,1)S(1)}, bf16[3,256,256]{2,1,0:T(8,128)(2,1)S(1)}, u32[]{:S(2)}, u32[]{:S(2)}) %collective-permute-start.5) | collective-permute-done | bytes 393248 | tf_op jit(solution)/shard_map/ppermute | solution.py:21
  19.4 1.7 %collective-permute-done.6.rest_7_ = bf16[3,256,256]{2,1,0:T(8,128)(2,1)S(1)} collective-permute-done((bf16[3,256,256]{2,1,0:T(8,128)(2,1)S(1)}, bf16[3,256,256]{2,1,0:T(8,128)(2,1)S(1)}, u32[]{:S(2)}, u32[]{:S(2)}) %collective-permute-start.6) | collective-permute-done | bytes 393248 | tf_op jit(solution)/shard_map/ppermute | solution.py:21
  21.1 1.8 %sum_over_terms.2 = (f32[2,2,2,64,256]{4,3,2,1,0:T(8,128)S(1)}, bf16[2,2,2,64,256]{4,3,2,1,0:T(8,128)(2,1)S(1)}, f32[8,128]{1,0:T(8,128)S(1)}, bf16[8,3,256,256]{3,2,1,0:T(8,128)(2,1)S(1)}) custom-call(s32[3,4]{1,0:T(4,128)} %offsets.3, bf16[2,4,256,256]{3,2,1,0:T(8,128)(2,1)S(1)} %bitcast.7, bf16[2,4,256,768]{3,2,1,0:T(8,128)(2,1)S(1)} %get-tuple-element.19.inner, ...), custom_call_target="tpu_custom_call" | custom-call | flops 402653184 | bytes 4194304 | tf_op jit(solution)/shard_map/sum_over_terms/pallas_call | solution.py:256
  22.9 1.4 %collective-permute-start.7 = (bf16[2,2,2,64,256]{4,3,2,1,0:T(8,128)(2,1)S(1)}, bf16[2,2,2,64,256]{4,3,2,1,0:T(8,128)(2,1)S(1)}, u32[]{:S(2)}, u32[]{:S(2)}) collective-permute-start(bf16[2,2,2,64,256]{4,3,2,1,0:T(8,128)(2,1)S(1)} %get-tuple-element.24), channel_id=1, source_target_pairs={{0,1},{1,0},{2,3},{3,2},{4,5},{5,4},{6,7},{7,6},{8,9},{9,8},{10,11... | collective-permute-start | bytes 786440 | tf_op jit(solution)/shard_map/ppermute | solution.py:21
  24.3 1.6 %sum_over_terms.3 = (f32[2,2,2,64,256]{4,3,2,1,0:T(8,128)S(1)}, bf16[2,2,2,64,256]{4,3,2,1,0:T(8,128)(2,1)S(1)}, f32[8,128]{1,0:T(8,128)S(1)}) custom-call(s32[3,4]{1,0:T(4,128)} %offsets.3, bf16[2,4,256,256]{3,2,1,0:T(8,128)(2,1)S(1)} %bitcast.8, bf16[2,4,256,768]{3,2,1,0:T(8,128)(2,1)S(1)} %get-tuple-element.19.inner, ...), custom_call_target="tpu_custom_call" | custom-call | flops 402653184 | bytes 4194304 | tf_op jit(solution)/shard_map/sum_over_terms/pallas_call | solution.py:256
  25.8 0.7 %collective-permute-start.9 = (bf16[2,2,2,64,256]{4,3,2,1,0:T(8,128)(2,1)S(1)}, bf16[2,2,2,64,256]{4,3,2,1,0:T(8,128)(2,1)S(1)}, u32[]{:S(2)}, u32[]{:S(2)}) collective-permute-start(bf16[2,2,2,64,256]{4,3,2,1,0:T(8,128)(2,1)S(1)} %get-tuple-element.30), channel_id=1, source_target_pairs={{0,1},{1,0},{2,3},{3,2},{4,5},{5,4},{6,7},{7,6},{8,9},{9,8},{10,11... | collective-permute-start | bytes 786440 | tf_op jit(solution)/shard_map/ppermute | solution.py:21
  26.5 1.2 %collective-permute-done.10 = f32[8,128]{1,0:T(8,128)S(1)} collective-permute-done((f32[8,128]{1,0:T(8,128)S(1)}, f32[8,128]{1,0:T(8,128)S(1)}, u32[]{:S(2)}, u32[]{:S(2)}) %collective-permute-start.10) | collective-permute-done | bytes 4128 | tf_op jit(solution)/shard_map/ppermute | solution.py:21
  27.7 2.7 %collective-permute-start.13 = (f32[8,128]{1,0:T(8,128)S(1)}, f32[8,128]{1,0:T(8,128)S(1)}, u32[]{:S(2)}, u32[]{:S(2)}) collective-permute-start(f32[8,128]{1,0:T(8,128)S(1)} %add.15), channel_id=1, source_target_pairs={{0,24},{4,28},{8,16},{12,20},{16,8},{20,12},{24,0},{28,4},{1,25},{... | collective-permute-start | bytes 12296 | tf_op jit(solution)/shard_map/ppermute | solution.py:21
  30.4 0.7 %collective-permute-start.11 = (f32[8,128]{1,0:T(8,128)S(1)}, f32[8,128]{1,0:T(8,128)S(1)}, u32[]{:S(2)}, u32[]{:S(2)}) collective-permute-start(f32[8,128]{1,0:T(8,128)S(1)} %add.15), channel_id=1, source_target_pairs={{0,8},{4,12},{8,0},{12,4},{16,24},{20,28},{24,16},{28,20},{1,9},{5... | collective-permute-start | bytes 12296 | tf_op jit(solution)/shard_map/ppermute | solution.py:21
  31.2 0.9 %collective-permute-done.7.received = bf16[2,2,2,64,256]{4,3,2,1,0:T(8,128)(2,1)S(1)} collective-permute-done((bf16[2,2,2,64,256]{4,3,2,1,0:T(8,128)(2,1)S(1)}, bf16[2,2,2,64,256]{4,3,2,1,0:T(8,128)(2,1)S(1)}, u32[]{:S(2)}, u32[]{:S(2)}) %collective-permute-start.7) | collective-permute-done | bytes 262176 | tf_op jit(solution)/shard_map/ppermute | solution.py:21
  32.1 2.4 %collective-permute-start.8 = (bf16[1,2,2,64,256]{4,3,2,1,0:T(8,128)(2,1)S(1)}, bf16[1,2,2,64,256]{4,3,2,1,0:T(8,128)(2,1)S(1)}, u32[]{:S(2)}, u32[]{:S(2)}) collective-permute-start(bf16[1,2,2,64,256]{4,3,2,1,0:T(8,128)(2,1)S(1)} %get-tuple-element.26), channel_id=1, source_target_pairs={{0,2},{1,3},{2,0},{3,1},{4,6},{5,7},{6,4},{7,5},{8,10},{9,11},{10,... | collective-permute-start | bytes 393224 | tf_op jit(solution)/shard_map/ppermute | solution.py:21
  34.6 1.6 %collective-permute-start.14 = (f32[8,128]{1,0:T(8,128)S(1)}, f32[8,128]{1,0:T(8,128)S(1)}, u32[]{:S(2)}, u32[]{:S(2)}) collective-permute-start(f32[8,128]{1,0:T(8,128)S(1)} %add_add_fusion), channel_id=1, source_target_pairs={{0,1},{1,0},{2,3},{3,2},{4,5},{5,4},{6,7},{7,6},{8,9},{9,8},{10,11... | collective-permute-start | bytes 12296 | tf_op jit(solution)/shard_map/ppermute | solution.py:21
  36.2 3.5 %collective-permute-done.14 = f32[8,128]{1,0:T(8,128)S(1)} collective-permute-done((f32[8,128]{1,0:T(8,128)S(1)}, f32[8,128]{1,0:T(8,128)S(1)}, u32[]{:S(2)}, u32[]{:S(2)}) %collective-permute-start.14) | collective-permute-done | bytes 4128 | tf_op jit(solution)/shard_map/ppermute | solution.py:21
  39.8 2.4 %collective-permute-start.15 = (bf16[304,256]{1,0:T(8,128)(2,1)S(1)}, bf16[304,256]{1,0:T(8,128)(2,1)S(1)}, u32[]{:S(2)}, u32[]{:S(2)}) collective-permute-start(bf16[304,256]{1,0:T(8,128)(2,1)S(1)} %get-tuple-element.33), channel_id=1, source_target_pairs={{0,2},{1,3},{2,0},{3,1},{4,6},{5,7},{6,4},{7,5},{8,10},{9,11},{10,... | collective-permute-start | bytes 466952 | tf_op jit(solution)/shard_map/ppermute | solution.py:21
  42.3 7.1 %collective-permute-done.15.received = bf16[304,256]{1,0:T(8,128)(2,1)S(1)} collective-permute-done((bf16[304,256]{1,0:T(8,128)(2,1)S(1)}, bf16[304,256]{1,0:T(8,128)(2,1)S(1)}, u32[]{:S(2)}, u32[]{:S(2)}) %collective-permute-start.15) | collective-permute-done | bytes 155680 | tf_op jit(solution)/shard_map/ppermute | solution.py:21
  49.4 0.7 %finish.1 = (bf16[2,4,64,256]{3,2,1,0:T(8,128)(2,1)}, f32[2,2]{1,0:T(2,128)}) custom-call(bf16[2,2,64,256]{3,2,1,0:T(8,128)(2,1)S(1)} %add_last_share.1.done, f32[1,2,2,64,256]{4,3,2,1,0:T(8,128)S(1)} %get-tuple-element.32.kept, bf16[304,256]{1,0:T(8,128)(2,1)S(1)} %collective-permute-done.15.received, f32[8,128]{1,0:T(8,128)S(1)} %add.19.tile), custom_call_target="tpu_custom_call" | custom-call | flops 1 | bytes 1 | tf_op jit(solution)/shard_map/finish/pallas_call | solution.py:318
  (22 shorter events, 0.7 us)
Async XLA Ops:
  0.6 9.4 %collective-permute-start.1 = (bf16[3,256,256]{2,1,0:T(8,128)(2,1)}, bf16[3,256,256]{2,1,0:T(8,128)(2,1)S(1)}, u32[]{:S(2)}, u32[]{:S(2)}) collective-permute-start(bf16[3,256,256]{2,1,0:T(8,128)(2,1)} %bitcast.10), channel_id=1, source_target_pairs={{0,8},{4,20},{8,0},{12,28},{16,24},{20,4},{24,16},{28,12},{1,9},{5... | collective-permute-start | bytes 1179656 | tf_op jit(solution)/shard_map/ppermute | solution.py:21
  3.6 1.2 %copy-start = (bf16[2,1,4,256,256]{4,3,2,1,0:T(8,128)(2,1)S(1)}, bf16[2,1,4,256,256]{4,3,2,1,0:T(8,128)(2,1)}, u32[]{:S(2)}) copy-start(bf16[2,1,4,256,256]{4,3,2,1,0:T(8,128)(2,1)} %param.4) | copy-start | bytes 3145732
  4.9 1.0 %copy-start.1 = (bf16[3,1,256,256]{3,2,1,0:T(8,128)(2,1)S(1)}, bf16[3,1,256,256]{3,2,1,0:T(8,128)(2,1)}, u32[]{:S(2)}) copy-start(bf16[3,1,256,256]{3,2,1,0:T(8,128)(2,1)} %param.5) | copy-start | bytes 1179652
  6.9 8.1 %collective-permute-start.3 = (bf16[3,256,256]{2,1,0:T(8,128)(2,1)}, bf16[3,256,256]{2,1,0:T(8,128)(2,1)S(1)}, u32[]{:S(2)}, u32[]{:S(2)}) collective-permute-start(bf16[3,256,256]{2,1,0:T(8,128)(2,1)} %bitcast.12), channel_id=1, source_target_pairs={{0,16},{4,12},{8,24},{12,4},{16,0},{20,28},{24,8},{28,20},{1,17},{... | collective-permute-start | bytes 1179656 | tf_op jit(solution)/shard_map/ppermute | solution.py:21
  10.0 9.4 %collective-permute-start.5 = (bf16[3,256,256]{2,1,0:T(8,128)(2,1)S(1)}, bf16[3,256,256]{2,1,0:T(8,128)(2,1)S(1)}, u32[]{:S(2)}, u32[]{:S(2)}) collective-permute-start(bf16[3,256,256]{2,1,0:T(8,128)(2,1)S(1)} %collective-permute-done.1.rest_2_), channel_id=1, source_target_pairs={{0,16},{4,12},{8,24},{12,4},{16,0},{20,28},{24,8},{28,20},{1,17},{... | collective-permute-start | bytes 1179656 | tf_op jit(solution)/shard_map/ppermute | solution.py:21
  13.6 5.8 %collective-permute-start = (bf16[3,256,256]{2,1,0:T(8,128)(2,1)}, bf16[3,256,256]{2,1,0:T(8,128)(2,1)S(1)}, u32[]{:S(2)}, u32[]{:S(2)}) collective-permute-start(bf16[3,256,256]{2,1,0:T(8,128)(2,1)} %bitcast.13), channel_id=1, source_target_pairs={{0,4},{4,0},{8,12},{12,8},{16,20},{20,16},{24,28},{28,24},{1,5},{5... | collective-permute-start | bytes 1179656 | tf_op jit(solution)/shard_map/ppermute | solution.py:21
  13.6 5.8 %collective-permute-start.2 = (bf16[3,256,256]{2,1,0:T(8,128)(2,1)S(1)}, bf16[3,256,256]{2,1,0:T(8,128)(2,1)S(1)}, u32[]{:S(2)}, u32[]{:S(2)}) collective-permute-start(bf16[3,256,256]{2,1,0:T(8,128)(2,1)S(1)} %collective-permute-done.1.rest_2_), channel_id=1, source_target_pairs={{0,4},{4,0},{8,12},{12,8},{16,20},{20,16},{24,28},{28,24},{1,5},{5... | collective-permute-start | bytes 1179656 | tf_op jit(solution)/shard_map/ppermute | solution.py:21
  14.9 4.5 %collective-permute-start.4 = (bf16[3,256,256]{2,1,0:T(8,128)(2,1)S(1)}, bf16[3,256,256]{2,1,0:T(8,128)(2,1)S(1)}, u32[]{:S(2)}, u32[]{:S(2)}) collective-permute-start(bf16[3,256,256]{2,1,0:T(8,128)(2,1)S(1)} %collective-permute-done.3.rest_4_), channel_id=1, source_target_pairs={{0,4},{4,0},{8,12},{12,8},{16,20},{20,16},{24,28},{28,24},{1,5},{5... | collective-permute-start | bytes 1179656 | tf_op jit(solution)/shard_map/ppermute | solution.py:21
  19.4 1.7 %collective-permute-start.6 = (bf16[3,256,256]{2,1,0:T(8,128)(2,1)S(1)}, bf16[3,256,256]{2,1,0:T(8,128)(2,1)S(1)}, u32[]{:S(2)}, u32[]{:S(2)}) collective-permute-start(bf16[3,256,256]{2,1,0:T(8,128)(2,1)S(1)} %collective-permute-done.5.rest_6_), channel_id=1, source_target_pairs={{0,4},{4,0},{8,12},{12,8},{16,20},{20,16},{24,28},{28,24},{1,5},{5... | collective-permute-start | bytes 1179656 | tf_op jit(solution)/shard_map/ppermute | solution.py:21
  22.9 9.2 %collective-permute-start.7 = (bf16[2,2,2,64,256]{4,3,2,1,0:T(8,128)(2,1)S(1)}, bf16[2,2,2,64,256]{4,3,2,1,0:T(8,128)(2,1)S(1)}, u32[]{:S(2)}, u32[]{:S(2)}) collective-permute-start(bf16[2,2,2,64,256]{4,3,2,1,0:T(8,128)(2,1)S(1)} %get-tuple-element.24), channel_id=1, source_target_pairs={{0,1},{1,0},{2,3},{3,2},{4,5},{5,4},{6,7},{7,6},{8,9},{9,8},{10,11... | collective-permute-start | bytes 786440 | tf_op jit(solution)/shard_map/ppermute | solution.py:21
  25.8 13.9 %collective-permute-start.9 = (bf16[2,2,2,64,256]{4,3,2,1,0:T(8,128)(2,1)S(1)}, bf16[2,2,2,64,256]{4,3,2,1,0:T(8,128)(2,1)S(1)}, u32[]{:S(2)}, u32[]{:S(2)}) collective-permute-start(bf16[2,2,2,64,256]{4,3,2,1,0:T(8,128)(2,1)S(1)} %get-tuple-element.30), channel_id=1, source_target_pairs={{0,1},{1,0},{2,3},{3,2},{4,5},{5,4},{6,7},{7,6},{8,9},{9,8},{10,11... | collective-permute-start | bytes 786440 | tf_op jit(solution)/shard_map/ppermute | solution.py:21
  26.5 1.2 %collective-permute-start.10 = (f32[8,128]{1,0:T(8,128)S(1)}, f32[8,128]{1,0:T(8,128)S(1)}, u32[]{:S(2)}, u32[]{:S(2)}) collective-permute-start(f32[8,128]{1,0:T(8,128)S(1)} %get-tuple-element.31), channel_id=1, source_target_pairs={{0,4},{4,0},{8,12},{12,8},{16,20},{20,16},{24,28},{28,24},{1,5},{5... | collective-permute-start | bytes 12296 | tf_op jit(solution)/shard_map/ppermute | solution.py:21
  27.7 6.9 %collective-permute-start.13 = (f32[8,128]{1,0:T(8,128)S(1)}, f32[8,128]{1,0:T(8,128)S(1)}, u32[]{:S(2)}, u32[]{:S(2)}) collective-permute-start(f32[8,128]{1,0:T(8,128)S(1)} %add.15), channel_id=1, source_target_pairs={{0,24},{4,28},{8,16},{12,20},{16,8},{20,12},{24,0},{28,4},{1,25},{... | collective-permute-start | bytes 12296 | tf_op jit(solution)/shard_map/ppermute | solution.py:21
  30.4 4.1 %collective-permute-start.12 = (f32[8,128]{1,0:T(8,128)S(1)}, f32[8,128]{1,0:T(8,128)S(1)}, u32[]{:S(2)}, u32[]{:S(2)}) collective-permute-start(f32[8,128]{1,0:T(8,128)S(1)} %add.15), channel_id=1, source_target_pairs={{0,16},{4,20},{8,24},{12,28},{16,0},{20,4},{24,8},{28,12},{1,17},{... | collective-permute-start | bytes 12296 | tf_op jit(solution)/shard_map/ppermute | solution.py:21
  30.4 4.1 %collective-permute-start.11 = (f32[8,128]{1,0:T(8,128)S(1)}, f32[8,128]{1,0:T(8,128)S(1)}, u32[]{:S(2)}, u32[]{:S(2)}) collective-permute-start(f32[8,128]{1,0:T(8,128)S(1)} %add.15), channel_id=1, source_target_pairs={{0,8},{4,12},{8,0},{12,4},{16,24},{20,28},{24,16},{28,20},{1,9},{5... | collective-permute-start | bytes 12296 | tf_op jit(solution)/shard_map/ppermute | solution.py:21
  32.1 10.2 %collective-permute-start.8 = (bf16[1,2,2,64,256]{4,3,2,1,0:T(8,128)(2,1)S(1)}, bf16[1,2,2,64,256]{4,3,2,1,0:T(8,128)(2,1)S(1)}, u32[]{:S(2)}, u32[]{:S(2)}) collective-permute-start(bf16[1,2,2,64,256]{4,3,2,1,0:T(8,128)(2,1)S(1)} %get-tuple-element.26), channel_id=1, source_target_pairs={{0,2},{1,3},{2,0},{3,1},{4,6},{5,7},{6,4},{7,5},{8,10},{9,11},{10,... | collective-permute-start | bytes 393224 | tf_op jit(solution)/shard_map/ppermute | solution.py:21
  34.6 5.2 %collective-permute-start.14 = (f32[8,128]{1,0:T(8,128)S(1)}, f32[8,128]{1,0:T(8,128)S(1)}, u32[]{:S(2)}, u32[]{:S(2)}) collective-permute-start(f32[8,128]{1,0:T(8,128)S(1)} %add_add_fusion), channel_id=1, source_target_pairs={{0,1},{1,0},{2,3},{3,2},{4,5},{5,4},{6,7},{7,6},{8,9},{9,8},{10,11... | collective-permute-start | bytes 12296 | tf_op jit(solution)/shard_map/ppermute | solution.py:21
  39.8 9.5 %collective-permute-start.15 = (bf16[304,256]{1,0:T(8,128)(2,1)S(1)}, bf16[304,256]{1,0:T(8,128)(2,1)S(1)}, u32[]{:S(2)}, u32[]{:S(2)}) collective-permute-start(bf16[304,256]{1,0:T(8,128)(2,1)S(1)} %get-tuple-element.33), channel_id=1, source_target_pairs={{0,2},{1,3},{2,0},{3,1},{4,6},{5,7},{6,4},{7,5},{8,10},{9,11},{10,... | collective-permute-start | bytes 466952 | tf_op jit(solution)/shard_map/ppermute | solution.py:21

commit v11 on v10

--- a/solution.py
+++ b/solution.py
@@ -9,7 +9,6 @@
 
 MIB = 1 << 20
 TILE = (8, 128)
-TILE_ROWS = 16
 VMEM = pl.BlockSpec(memory_space=pltpu.VMEM)
 SMEM = pl.BlockSpec(memory_space=pltpu.SMEM)
 HBM = pl.BlockSpec(memory_space=pltpu.HBM)
@@ -77,6 +76,13 @@
         even_place, odd_place = turned(mask, 0, sectors), turned(mask, 1, sectors)
         rights[jnp.where(odd == 1, odd_place, even_place)] = pieces[mask][...]
         rights[jnp.where(odd == 1, even_place, odd_place) ^ 1] = pieces[mask + 1][...]
+
+
+def share_masks(shares, backwards):
+    if not backwards:
+        return list(range(shares))
+    bits = shares.bit_length() - 1
+    return [sum(1 << (bits - 1 - bit) for bit in range(bits) if k >> bit & 1) for k in range(shares)]
 
 
 def sum_kernel(sectors, first, offsets, vectors, inner, before, *rest):
@@ -109,28 +115,33 @@
             for i in range(trials):
                 spread = vectors[i, pair].astype(jnp.float32) * product
                 grams[i * trials + j] += jnp.sum(spread.reshape(-1, 8, states), axis=0)
-        for mask in range(shares):
+        for k, mask in enumerate(share_masks(shares, first > 0)):
             start = pl.multiple_of((place ^ mask) * rows, rows)
             share = partial[:, pl.ds(start, rows)]
-            if mask & 1:
-                send[mask // 2, :, local_pair] = share.astype(jnp.bfloat16)
+            if k & 1:
+                send[k // 2, :, local_pair] = share.astype(jnp.bfloat16)
             else:
-                keep[mask // 2, :, local_pair] = share
+                keep[k // 2, :, local_pair] = share
     tile[...] = before[...] + place_rows([(k, total(value)) for k, value in enumerate(grams)])
 
 
 def halve_last_kernel(kept, received, tile, keep, send):
     keep[0] = kept[0] + received[0].astype(jnp.float32)
     both = kept[1] + received[1].astype(jnp.float32)
-    lines = send.shape[0] - 3 * TILE_ROWS
+    lines = send.shape[0] - 2 * TILE[0]
     send[:lines] = both.astype(jnp.bfloat16).reshape(lines, send.shape[1])
-    left = tile[...]
-    for part in range(3):
-        rounded = left.astype(jnp.bfloat16)
-        left = left - rounded.astype(jnp.float32)
-        block = jnp.concatenate([rounded, jnp.zeros_like(rounded)], axis=0)
-        start = lines + part * TILE_ROWS
-        send[start : start + TILE_ROWS] = jnp.concatenate([block, block], axis=1)
+    left, parts = tile[...], []
+    for _ in range(3):
+        parts.append(left.astype(jnp.bfloat16).astype(jnp.float32))
+        left = left - parts[-1]
+    block = jnp.concatenate(
+        [
+            jnp.concatenate([parts[0], parts[1]], axis=0),
+            jnp.concatenate([parts[2], jnp.zeros_like(left)], axis=0),
+        ],
+        axis=1,
+    )
+    send[lines:] = block.astype(jnp.bfloat16)
 
 
 def halve_kernel(kept, received, keep, send):
@@ -143,25 +154,26 @@
 
 
 def ridden_tile(received):
-    lines = received.shape[0] - 3 * TILE_ROWS
-    parts = []
-    for part in range(3):
-        start = lines + part * TILE_ROWS
-        block = received[start : start + TILE_ROWS, : TILE[1]].astype(jnp.float32)
-        parts.append(block[: TILE[0]])
-    return parts[0] + parts[1] + parts[2]
-
-
-def add_last_kernel(kept, received, result):
-    result[...] = (kept[0] + received[0].astype(jnp.float32)).astype(jnp.bfloat16)
-
-
-def finish_kernel(done, kept, received, tile, products, rayleigh):
+    height, width = TILE
+    block = received[received.shape[0] - 2 * height :].astype(jnp.float32)
+    return block[:height, :width] + block[height:, :width] + block[:height, width:]
+
+
+def last_rows(kept, received):
+    lines = received.shape[0] - 2 * TILE[0]
+    both = received[:lines].astype(jnp.float32).reshape(kept.shape[1:])
+    return (kept[0] + both).astype(jnp.bfloat16)
+
+
+def add_last_kernel(kept, received, tile, corner, rows, sums):
+    rows[...] = last_rows(kept, received)
+    sums[...] = tile[...] + ridden_tile(received) + corner[...]
+
+
+def finish_kernel(done, tile, kept, received, products, rayleigh):
     first = done.shape[1]
-    lines = received.shape[0] - 3 * TILE_ROWS
-    both = received[:lines].astype(jnp.float32).reshape(kept.shape[1:])
     products[:, :first] = done[...]
-    products[:, first:] = (kept[0] + both).astype(jnp.bfloat16)
+    products[:, first:] = last_rows(kept, received)
 
     tile = tile[...] + ridden_tile(received)
     trials = rayleigh.shape[0]
@@ -266,26 +278,24 @@
         )(in_hbm(offsets), vectors, inner, tile, *blocks)
         rights = placed[0] if placed else rights
         first += size
-        sums.append((keep, swap(send, "term", 1)))
-
+        sums.append((keep, send))
+
+    bits = [1 << bit for bit in range(shares.bit_length() - 1)]
+    orders = [bits, bits[::-1]]
+    arrived = [swap(send, "term", order[0]) for (_, send), order in zip(sums, orders)]
     for masks in [[1]] + steps_of(sectors, 1):
         tile = add_places(tile, "sec", masks)
-
-    step = 1
-    while 2 * step < shares:
-        tile = add_places(tile, "term", [step])
-        step *= 2
+    for bit in bits[1:-1]:
+        tile = add_places(tile, "term", [bit])
+    corner = swap(tile, "term", bits[0] | bits[-1])
 
     parts = []
-    for chunk, size in enumerate(sizes):
-        keep, received = sums[chunk]
-        step = 1
-        while 2 * step < shares:
-            step *= 2
-            count = shares // (2 * step)
-            last = count == 1 and chunk == len(sizes) - 1
+    for size, (keep, _), received, order in zip(sizes, sums, arrived, orders):
+        for step in order[1:]:
+            count = keep.shape[0] // 2
+            last = count == 1
             operands = (keep, received, tile) if last else (keep, received)
-            lines = trials * size * rows + 3 * TILE_ROWS
+            lines = trials * size * rows + 2 * TILE[0]
             keep, send = call(
                 halve_last_kernel if last else halve_kernel,
                 "halve_rows",
@@ -305,16 +315,19 @@
         parts += [keep, received]
 
     kept, received, *second = parts
-    done = call(
+    done, tile = call(
         add_last_kernel,
         "add_last_share",
-        10**10,
+        1,
         1,
         8 * MIB,
-        out_shape=jax.ShapeDtypeStruct((trials, sizes[0], rows, states), jnp.bfloat16),
-        in_specs=[VMEM, VMEM],
-        out_specs=VMEM,
-    )(kept, received)
+        out_shape=(
+            jax.ShapeDtypeStruct((trials, sizes[0], rows, states), jnp.bfloat16),
+            jax.ShapeDtypeStruct(TILE, jnp.float32),
+        ),
+        in_specs=[VMEM] * 4,
+        out_specs=(VMEM, VMEM),
+    )(kept, received, tile, corner)
     products, rayleigh = call(
         finish_kernel,
         "finish",
@@ -327,7 +340,7 @@
         ),
         in_specs=[VMEM] * 4,
         out_specs=(VMEM, VMEM),
-    )(done, *second, tile)
+    )(done, tile, *second)
     return (products[:, None], rayleigh)
 
 

time: 50.4 us -> 51.3 us (1.018)
  waiting for transfers between devices: 21.1 us -> 23.6 us
  starting transfers between devices: 20.8 us -> 19.3 us
    ppermute x16, waiting for transfers between devices: 21.1 us -> 23.6 us  [swap(): lax.ppermute(value, axis, [(place, place ^ masks[place & 1]) for place in...]
    ppermute x16, starting transfers between devices: 20.8 us -> 19.3 us  [swap(): lax.ppermute(value, axis, [(place, place ^ masks[place & 1]) for place in...]
  transfers between devices with their start and end apart: 16 -> 16, of which waited for: 8 -> 9; matrix products, arithmetic and copies ran while one was open for 0% -> 0% of each run, Pallas kernels for 5% -> 5%
where the time goes in v11:
time: 51.3 us; the launch traced here: 51 us
  waiting for transfers between devices  23.6 us (46%)
  starting transfers between devices  19.3 us (38%)
  Pallas kernels  5.24 us (10%)
  local copies, waits for them, and re-layouts  2.22 us (4%)
  between operations  0.7 us (1%)
    ppermute x16, waiting for transfers between devices, swap(): lax.ppermute(value, axis, [(place, place ^ masks[place & 1]) for place in...  23.6 us
    ppermute x16, starting transfers between devices, swap(): lax.ppermute(value, axis, [(place, place ^ masks[place & 1]) for place in...  19.3 us
    pallas_call x2, Pallas kernels, local(): call(functools.partial(sum_kernel, sectors, first), 'sum_over_terms', 2 *...  3.34 us
    unnamed x4, local copies, waits for them, and re-layouts  2.22 us
  transfers between devices with their start and end apart: 16, of which 9 were waited for; matrix products, arithmetic and copies ran while one was open for 0% of the time, Pallas kernels for 5%

profile of v11, /device:TPU:0, one launch (start us, length us, event | category | flops | bytes accessed | tf_op | source)
XLA Modules:
  0.0 51.0 jit_solution(1204644819200494084)
XLA Ops:
  0.6 3.0 %collective-permute-start.1 = (bf16[3,256,256]{2,1,0:T(8,128)(2,1)}, bf16[3,256,256]{2,1,0:T(8,128)(2,1)S(1)}, u32[]{:S(2)}, u32[]{:S(2)}) collective-permute-start(bf16[3,256,256]{2,1,0:T(8,128)(2,1)} %bitcast.10), channel_id=1, source_target_pairs={{0,8},{4,20},{8,0},{12,28},{16,24},{20,4},{24,16},{28,12},{1,9},{5... | collective-permute-start | bytes 1179656 | tf_op jit(solution)/shard_map/ppermute | solution.py:20
  3.6 1.2 %copy-done = bf16[2,1,4,256,256]{4,3,2,1,0:T(8,128)(2,1)S(1)} copy-done((bf16[2,1,4,256,256]{4,3,2,1,0:T(8,128)(2,1)S(1)}, bf16[2,1,4,256,256]{4,3,2,1,0:T(8,128)(2,1)}, u32[]{:S(2)}) %copy-start) | copy-done | bytes 1048600
  4.9 1.0 %copy-done.1 = bf16[3,1,256,256]{3,2,1,0:T(8,128)(2,1)S(1)} copy-done((bf16[3,1,256,256]{3,2,1,0:T(8,128)(2,1)S(1)}, bf16[3,1,256,256]{3,2,1,0:T(8,128)(2,1)}, u32[]{:S(2)}) %copy-start.1) | copy-done | bytes 393240
  5.9 1.0 %inner_products.1 = (bf16[2,4,256,768]{3,2,1,0:T(8,128)(2,1)S(1)}, f32[8,128]{1,0:T(8,128)S(1)}, bf16[3,256,256]{2,1,0:T(8,128)(2,1)S(1)}) custom-call(bf16[2,4,256,256]{3,2,1,0:T(8,128)(2,1)S(1)} %bitcast.6, bf16[3,256,256]{2,1,0:T(8,128)(2,1)S(1)} %bitcast.9, bf16[3,256,256]{2,1,0:T(8,128)(2,1)} %bitcast.11), custom_call_target="tpu_custom_call" | custom-call | flops 805306368 | bytes 5242880 | tf_op jit(solution)/shard_map/inner_products/pallas_call | solution.py:231
  6.9 1.6 %collective-permute-start.3 = (bf16[3,256,256]{2,1,0:T(8,128)(2,1)}, bf16[3,256,256]{2,1,0:T(8,128)(2,1)S(1)}, u32[]{:S(2)}, u32[]{:S(2)}) collective-permute-start(bf16[3,256,256]{2,1,0:T(8,128)(2,1)} %bitcast.12), channel_id=1, source_target_pairs={{0,16},{4,12},{8,24},{12,4},{16,0},{20,28},{24,8},{28,20},{1,17},{... | collective-permute-start | bytes 1179656 | tf_op jit(solution)/shard_map/ppermute | solution.py:20
  8.5 1.5 %collective-permute-done.1.rest_2_ = bf16[3,256,256]{2,1,0:T(8,128)(2,1)S(1)} collective-permute-done((bf16[3,256,256]{2,1,0:T(8,128)(2,1)}, bf16[3,256,256]{2,1,0:T(8,128)(2,1)S(1)}, u32[]{:S(2)}, u32[]{:S(2)}) %collective-permute-start.1) | collective-permute-done | bytes 393248 | tf_op jit(solution)/shard_map/ppermute | solution.py:20
  10.0 3.6 %collective-permute-start.5 = (bf16[3,256,256]{2,1,0:T(8,128)(2,1)S(1)}, bf16[3,256,256]{2,1,0:T(8,128)(2,1)S(1)}, u32[]{:S(2)}, u32[]{:S(2)}) collective-permute-start(bf16[3,256,256]{2,1,0:T(8,128)(2,1)S(1)} %collective-permute-done.1.rest_2_), channel_id=1, source_target_pairs={{0,16},{4,12},{8,24},{12,4},{16,0},{20,28},{24,8},{28,20},{1,17},{... | collective-permute-start | bytes 1179656 | tf_op jit(solution)/shard_map/ppermute | solution.py:20
  13.6 0.5 collective-permute-start.2
  14.1 0.8 %collective-permute-done.3.rest_4_ = bf16[3,256,256]{2,1,0:T(8,128)(2,1)S(1)} collective-permute-done((bf16[3,256,256]{2,1,0:T(8,128)(2,1)}, bf16[3,256,256]{2,1,0:T(8,128)(2,1)S(1)}, u32[]{:S(2)}, u32[]{:S(2)}) %collective-permute-start.3) | collective-permute-done | bytes 393248 | tf_op jit(solution)/shard_map/ppermute | solution.py:20
  14.9 4.4 %collective-permute-done.5.rest_6_ = bf16[3,256,256]{2,1,0:T(8,128)(2,1)S(1)} collective-permute-done((bf16[3,256,256]{2,1,0:T(8,128)(2,1)S(1)}, bf16[3,256,256]{2,1,0:T(8,128)(2,1)S(1)}, u32[]{:S(2)}, u32[]{:S(2)}) %collective-permute-start.5) | collective-permute-done | bytes 393248 | tf_op jit(solution)/shard_map/ppermute | solution.py:20
  19.4 1.7 %collective-permute-done.6.rest_7_ = bf16[3,256,256]{2,1,0:T(8,128)(2,1)S(1)} collective-permute-done((bf16[3,256,256]{2,1,0:T(8,128)(2,1)S(1)}, bf16[3,256,256]{2,1,0:T(8,128)(2,1)S(1)}, u32[]{:S(2)}, u32[]{:S(2)}) %collective-permute-start.6) | collective-permute-done | bytes 393248 | tf_op jit(solution)/shard_map/ppermute | solution.py:20
  21.1 1.8 %sum_over_terms.2 = (f32[2,2,2,64,256]{4,3,2,1,0:T(8,128)S(1)}, bf16[2,2,2,64,256]{4,3,2,1,0:T(8,128)(2,1)S(1)}, f32[8,128]{1,0:T(8,128)S(1)}, bf16[8,3,256,256]{3,2,1,0:T(8,128)(2,1)S(1)}) custom-call(s32[3,4]{1,0:T(4,128)} %offsets.3, bf16[2,4,256,256]{3,2,1,0:T(8,128)(2,1)S(1)} %bitcast.7, bf16[2,4,256,768]{3,2,1,0:T(8,128)(2,1)S(1)} %get-tuple-element.21.inner, ...), custom_call_target="tpu_custom_call" | custom-call | flops 402653184 | bytes 4194304 | tf_op jit(solution)/shard_map/sum_over_terms/pallas_call | solution.py:268
  22.9 1.4 %collective-permute-start.7 = (bf16[2,2,2,64,256]{4,3,2,1,0:T(8,128)(2,1)S(1)}, bf16[2,2,2,64,256]{4,3,2,1,0:T(8,128)(2,1)S(1)}, u32[]{:S(2)}, u32[]{:S(2)}) collective-permute-start(bf16[2,2,2,64,256]{4,3,2,1,0:T(8,128)(2,1)S(1)} %get-tuple-element.26), channel_id=1, source_target_pairs={{0,1},{1,0},{2,3},{3,2},{4,5},{5,4},{6,7},{7,6},{8,9},{9,8},{10,11... | collective-permute-start | bytes 786440 | tf_op jit(solution)/shard_map/ppermute | solution.py:20
  24.3 1.6 %sum_over_terms.3 = (f32[2,2,2,64,256]{4,3,2,1,0:T(8,128)S(1)}, bf16[2,2,2,64,256]{4,3,2,1,0:T(8,128)(2,1)S(1)}, f32[8,128]{1,0:T(8,128)S(1)}) custom-call(s32[3,4]{1,0:T(4,128)} %offsets.3, bf16[2,4,256,256]{3,2,1,0:T(8,128)(2,1)S(1)} %bitcast.8, bf16[2,4,256,768]{3,2,1,0:T(8,128)(2,1)S(1)} %get-tuple-element.21.inner, ...), custom_call_target="tpu_custom_call" | custom-call | flops 402653184 | bytes 4194304 | tf_op jit(solution)/shard_map/sum_over_terms/pallas_call | solution.py:268
  25.8 2.6 %collective-permute-start.14 = (bf16[2,2,2,64,256]{4,3,2,1,0:T(8,128)(2,1)S(1)}, bf16[2,2,2,64,256]{4,3,2,1,0:T(8,128)(2,1)S(1)}, u32[]{:S(2)}, u32[]{:S(2)}) collective-permute-start(bf16[2,2,2,64,256]{4,3,2,1,0:T(8,128)(2,1)S(1)} %get-tuple-element.35), channel_id=1, source_target_pairs={{0,2},{1,3},{2,0},{3,1},{4,6},{5,7},{6,4},{7,5},{8,10},{9,11},{10,... | collective-permute-start | bytes 786440 | tf_op jit(solution)/shard_map/ppermute | solution.py:20
  28.4 1.2 %collective-permute-done.8 = f32[8,128]{1,0:T(8,128)S(1)} collective-permute-done((f32[8,128]{1,0:T(8,128)S(1)}, f32[8,128]{1,0:T(8,128)S(1)}, u32[]{:S(2)}, u32[]{:S(2)}) %collective-permute-start.8) | collective-permute-done | bytes 4128 | tf_op jit(solution)/shard_map/ppermute | solution.py:20
  29.6 2.9 %collective-permute-start.11 = (f32[8,128]{1,0:T(8,128)S(1)}, f32[8,128]{1,0:T(8,128)S(1)}, u32[]{:S(2)}, u32[]{:S(2)}) collective-permute-start(f32[8,128]{1,0:T(8,128)S(1)} %add.12), channel_id=1, source_target_pairs={{0,24},{4,28},{8,16},{12,20},{16,8},{20,12},{24,0},{28,4},{1,25},{... | collective-permute-start | bytes 12296 | tf_op jit(solution)/shard_map/ppermute | solution.py:20
  32.6 0.6 %collective-permute-start.9 = (f32[8,128]{1,0:T(8,128)S(1)}, f32[8,128]{1,0:T(8,128)S(1)}, u32[]{:S(2)}, u32[]{:S(2)}) collective-permute-start(f32[8,128]{1,0:T(8,128)S(1)} %add.12), channel_id=1, source_target_pairs={{0,8},{4,12},{8,0},{12,4},{16,24},{20,28},{24,16},{28,20},{1,9},{5... | collective-permute-start | bytes 12296 | tf_op jit(solution)/shard_map/ppermute | solution.py:20
  33.1 1.0 %collective-permute-done.11 = f32[8,128]{1,0:T(8,128)S(1)} collective-permute-done((f32[8,128]{1,0:T(8,128)S(1)}, f32[8,128]{1,0:T(8,128)S(1)}, u32[]{:S(2)}, u32[]{:S(2)}) %collective-permute-start.11) | collective-permute-done | bytes 4128 | tf_op jit(solution)/shard_map/ppermute | solution.py:20
  34.1 2.0 %collective-permute-done.10 = f32[8,128]{1,0:T(8,128)S(1)} collective-permute-done((f32[8,128]{1,0:T(8,128)S(1)}, f32[8,128]{1,0:T(8,128)S(1)}, u32[]{:S(2)}, u32[]{:S(2)}) %collective-permute-start.10) | collective-permute-done | bytes 4128 | tf_op jit(solution)/shard_map/ppermute | solution.py:20
  36.6 7.9 %collective-permute-done.14.received = bf16[2,2,2,64,256]{4,3,2,1,0:T(8,128)(2,1)S(1)} collective-permute-done((bf16[2,2,2,64,256]{4,3,2,1,0:T(8,128)(2,1)S(1)}, bf16[2,2,2,64,256]{4,3,2,1,0:T(8,128)(2,1)S(1)}, u32[]{:S(2)}, u32[]{:S(2)}) %collective-permute-start.14) | collective-permute-done | bytes 262176 | tf_op jit(solution)/shard_map/ppermute | solution.py:20
  44.7 2.5 %collective-permute-start.13 = (f32[8,128]{1,0:T(8,128)S(1)}, f32[8,128]{1,0:T(8,128)S(1)}, u32[]{:S(2)}, u32[]{:S(2)}) collective-permute-start(f32[8,128]{1,0:T(8,128)S(1)} %add_add_fusion.tile), channel_id=1, source_target_pairs={{0,3},{1,2},{2,1},{3,0},{4,7},{5,6},{6,5},{7,4},{8,11},{9,10},{10,... | collective-permute-start | bytes 12296 | tf_op jit(solution)/shard_map/ppermute | solution.py:20
  47.2 3.0 %collective-permute-done.13.corner = f32[8,128]{1,0:T(8,128)S(1)} collective-permute-done((f32[8,128]{1,0:T(8,128)S(1)}, f32[8,128]{1,0:T(8,128)S(1)}, u32[]{:S(2)}, u32[]{:S(2)}) %collective-permute-start.13) | collective-permute-done | bytes 4128 | tf_op jit(solution)/shard_map/ppermute | solution.py:20
  50.3 0.7 %finish.1 = (bf16[2,4,64,256]{3,2,1,0:T(8,128)(2,1)}, f32[2,2]{1,0:T(2,128)}) custom-call(bf16[2,2,64,256]{3,2,1,0:T(8,128)(2,1)S(1)} %get-tuple-element.32.done, f32[8,128]{1,0:T(8,128)S(1)} %get-tuple-element.33.tile, f32[1,2,2,64,256]{4,3,2,1,0:T(8,128)S(1)} %get-tuple-element.36.kept, bf16[272,256]{1,0:T(8,128)(2,1)S(1)} %collective-permute-done.15.received), custom_call_target="tpu_custom_call" | custom-call | flops 1 | bytes 1 | tf_op jit(solution)/shard_map/finish/pallas_call | solution.py:331
  (21 shorter events, 0.7 us)
Async XLA Ops:
  0.6 9.4 %collective-permute-start.1 = (bf16[3,256,256]{2,1,0:T(8,128)(2,1)}, bf16[3,256,256]{2,1,0:T(8,128)(2,1)S(1)}, u32[]{:S(2)}, u32[]{:S(2)}) collective-permute-start(bf16[3,256,256]{2,1,0:T(8,128)(2,1)} %bitcast.10), channel_id=1, source_target_pairs={{0,8},{4,20},{8,0},{12,28},{16,24},{20,4},{24,16},{28,12},{1,9},{5... | collective-permute-start | bytes 1179656 | tf_op jit(solution)/shard_map/ppermute | solution.py:20
  3.6 1.2 %copy-start = (bf16[2,1,4,256,256]{4,3,2,1,0:T(8,128)(2,1)S(1)}, bf16[2,1,4,256,256]{4,3,2,1,0:T(8,128)(2,1)}, u32[]{:S(2)}) copy-start(bf16[2,1,4,256,256]{4,3,2,1,0:T(8,128)(2,1)} %param.4) | copy-start | bytes 3145732
  4.9 1.0 %copy-start.1 = (bf16[3,1,256,256]{3,2,1,0:T(8,128)(2,1)S(1)}, bf16[3,1,256,256]{3,2,1,0:T(8,128)(2,1)}, u32[]{:S(2)}) copy-start(bf16[3,1,256,256]{3,2,1,0:T(8,128)(2,1)} %param.5) | copy-start | bytes 1179652
  6.9 8.1 %collective-permute-start.3 = (bf16[3,256,256]{2,1,0:T(8,128)(2,1)}, bf16[3,256,256]{2,1,0:T(8,128)(2,1)S(1)}, u32[]{:S(2)}, u32[]{:S(2)}) collective-permute-start(bf16[3,256,256]{2,1,0:T(8,128)(2,1)} %bitcast.12), channel_id=1, source_target_pairs={{0,16},{4,12},{8,24},{12,4},{16,0},{20,28},{24,8},{28,20},{1,17},{... | collective-permute-start | bytes 1179656 | tf_op jit(solution)/shard_map/ppermute | solution.py:20
  10.0 9.4 %collective-permute-start.5 = (bf16[3,256,256]{2,1,0:T(8,128)(2,1)S(1)}, bf16[3,256,256]{2,1,0:T(8,128)(2,1)S(1)}, u32[]{:S(2)}, u32[]{:S(2)}) collective-permute-start(bf16[3,256,256]{2,1,0:T(8,128)(2,1)S(1)} %collective-permute-done.1.rest_2_), channel_id=1, source_target_pairs={{0,16},{4,12},{8,24},{12,4},{16,0},{20,28},{24,8},{28,20},{1,17},{... | collective-permute-start | bytes 1179656 | tf_op jit(solution)/shard_map/ppermute | solution.py:20
  13.6 5.8 %collective-permute-start = (bf16[3,256,256]{2,1,0:T(8,128)(2,1)}, bf16[3,256,256]{2,1,0:T(8,128)(2,1)S(1)}, u32[]{:S(2)}, u32[]{:S(2)}) collective-permute-start(bf16[3,256,256]{2,1,0:T(8,128)(2,1)} %bitcast.13), channel_id=1, source_target_pairs={{0,4},{4,0},{8,12},{12,8},{16,20},{20,16},{24,28},{28,24},{1,5},{5... | collective-permute-start | bytes 1179656 | tf_op jit(solution)/shard_map/ppermute | solution.py:20
  13.6 5.8 %collective-permute-start.2 = (bf16[3,256,256]{2,1,0:T(8,128)(2,1)S(1)}, bf16[3,256,256]{2,1,0:T(8,128)(2,1)S(1)}, u32[]{:S(2)}, u32[]{:S(2)}) collective-permute-start(bf16[3,256,256]{2,1,0:T(8,128)(2,1)S(1)} %collective-permute-done.1.rest_2_), channel_id=1, source_target_pairs={{0,4},{4,0},{8,12},{12,8},{16,20},{20,16},{24,28},{28,24},{1,5},{5... | collective-permute-start | bytes 1179656 | tf_op jit(solution)/shard_map/ppermute | solution.py:20
  14.9 4.5 %collective-permute-start.4 = (bf16[3,256,256]{2,1,0:T(8,128)(2,1)S(1)}, bf16[3,256,256]{2,1,0:T(8,128)(2,1)S(1)}, u32[]{:S(2)}, u32[]{:S(2)}) collective-permute-start(bf16[3,256,256]{2,1,0:T(8,128)(2,1)S(1)} %collective-permute-done.3.rest_4_), channel_id=1, source_target_pairs={{0,4},{4,0},{8,12},{12,8},{16,20},{20,16},{24,28},{28,24},{1,5},{5... | collective-permute-start | bytes 1179656 | tf_op jit(solution)/shard_map/ppermute | solution.py:20
  19.4 1.7 %collective-permute-start.6 = (bf16[3,256,256]{2,1,0:T(8,128)(2,1)S(1)}, bf16[3,256,256]{2,1,0:T(8,128)(2,1)S(1)}, u32[]{:S(2)}, u32[]{:S(2)}) collective-permute-start(bf16[3,256,256]{2,1,0:T(8,128)(2,1)S(1)} %collective-permute-done.5.rest_6_), channel_id=1, source_target_pairs={{0,4},{4,0},{8,12},{12,8},{16,20},{20,16},{24,28},{28,24},{1,5},{5... | collective-permute-start | bytes 1179656 | tf_op jit(solution)/shard_map/ppermute | solution.py:20
  22.9 13.3 %collective-permute-start.7 = (bf16[2,2,2,64,256]{4,3,2,1,0:T(8,128)(2,1)S(1)}, bf16[2,2,2,64,256]{4,3,2,1,0:T(8,128)(2,1)S(1)}, u32[]{:S(2)}, u32[]{:S(2)}) collective-permute-start(bf16[2,2,2,64,256]{4,3,2,1,0:T(8,128)(2,1)S(1)} %get-tuple-element.26), channel_id=1, source_target_pairs={{0,1},{1,0},{2,3},{3,2},{4,5},{5,4},{6,7},{7,6},{8,9},{9,8},{10,11... | collective-permute-start | bytes 786440 | tf_op jit(solution)/shard_map/ppermute | solution.py:20
  25.8 18.7 %collective-permute-start.14 = (bf16[2,2,2,64,256]{4,3,2,1,0:T(8,128)(2,1)S(1)}, bf16[2,2,2,64,256]{4,3,2,1,0:T(8,128)(2,1)S(1)}, u32[]{:S(2)}, u32[]{:S(2)}) collective-permute-start(bf16[2,2,2,64,256]{4,3,2,1,0:T(8,128)(2,1)S(1)} %get-tuple-element.35), channel_id=1, source_target_pairs={{0,2},{1,3},{2,0},{3,1},{4,6},{5,7},{6,4},{7,5},{8,10},{9,11},{10,... | collective-permute-start | bytes 786440 | tf_op jit(solution)/shard_map/ppermute | solution.py:20
  28.4 1.2 %collective-permute-start.8 = (f32[8,128]{1,0:T(8,128)S(1)}, f32[8,128]{1,0:T(8,128)S(1)}, u32[]{:S(2)}, u32[]{:S(2)}) collective-permute-start(f32[8,128]{1,0:T(8,128)S(1)} %get-tuple-element.29), channel_id=1, source_target_pairs={{0,4},{4,0},{8,12},{12,8},{16,20},{20,16},{24,28},{28,24},{1,5},{5... | collective-permute-start | bytes 12296 | tf_op jit(solution)/shard_map/ppermute | solution.py:20
  29.6 4.5 %collective-permute-start.11 = (f32[8,128]{1,0:T(8,128)S(1)}, f32[8,128]{1,0:T(8,128)S(1)}, u32[]{:S(2)}, u32[]{:S(2)}) collective-permute-start(f32[8,128]{1,0:T(8,128)S(1)} %add.12), channel_id=1, source_target_pairs={{0,24},{4,28},{8,16},{12,20},{16,8},{20,12},{24,0},{28,4},{1,25},{... | collective-permute-start | bytes 12296 | tf_op jit(solution)/shard_map/ppermute | solution.py:20
  32.6 3.6 %collective-permute-start.10 = (f32[8,128]{1,0:T(8,128)S(1)}, f32[8,128]{1,0:T(8,128)S(1)}, u32[]{:S(2)}, u32[]{:S(2)}) collective-permute-start(f32[8,128]{1,0:T(8,128)S(1)} %add.12), channel_id=1, source_target_pairs={{0,16},{4,20},{8,24},{12,28},{16,0},{20,4},{24,8},{28,12},{1,17},{... | collective-permute-start | bytes 12296 | tf_op jit(solution)/shard_map/ppermute | solution.py:20
  32.6 3.6 %collective-permute-start.9 = (f32[8,128]{1,0:T(8,128)S(1)}, f32[8,128]{1,0:T(8,128)S(1)}, u32[]{:S(2)}, u32[]{:S(2)}) collective-permute-start(f32[8,128]{1,0:T(8,128)S(1)} %add.12), channel_id=1, source_target_pairs={{0,8},{4,12},{8,0},{12,4},{16,24},{20,28},{24,16},{28,20},{1,9},{5... | collective-permute-start | bytes 12296 | tf_op jit(solution)/shard_map/ppermute | solution.py:20
  36.2 14.0 %collective-permute-start.12 = (bf16[272,256]{1,0:T(8,128)(2,1)S(1)}, bf16[272,256]{1,0:T(8,128)(2,1)S(1)}, u32[]{:S(2)}, u32[]{:S(2)}) collective-permute-start(bf16[272,256]{1,0:T(8,128)(2,1)S(1)} %get-tuple-element.31), channel_id=1, source_target_pairs={{0,2},{1,3},{2,0},{3,1},{4,6},{5,7},{6,4},{7,5},{8,10},{9,11},{10,... | collective-permute-start | bytes 417800 | tf_op jit(solution)/shard_map/ppermute | solution.py:20
  44.6 5.7 %collective-permute-start.15 = (bf16[272,256]{1,0:T(8,128)(2,1)S(1)}, bf16[272,256]{1,0:T(8,128)(2,1)S(1)}, u32[]{:S(2)}, u32[]{:S(2)}) collective-permute-start(bf16[272,256]{1,0:T(8,128)(2,1)S(1)} %get-tuple-element.37), channel_id=1, source_target_pairs={{0,1},{1,0},{2,3},{3,2},{4,5},{5,4},{6,7},{7,6},{8,9},{9,8},{10,11... | collective-permute-start | bytes 417800 | tf_op jit(solution)/shard_map/ppermute | solution.py:20
  44.7 5.5 %collective-permute-start.13 = (f32[8,128]{1,0:T(8,128)S(1)}, f32[8,128]{1,0:T(8,128)S(1)}, u32[]{:S(2)}, u32[]{:S(2)}) collective-permute-start(f32[8,128]{1,0:T(8,128)S(1)} %add_add_fusion.tile), channel_id=1, source_target_pairs={{0,3},{1,2},{2,1},{3,0},{4,7},{5,6},{6,5},{7,4},{8,11},{9,10},{10,... | collective-permute-start | bytes 12296 | tf_op jit(solution)/shard_map/ppermute | solution.py:20

commit v12 on v10

--- a/solution.py
+++ b/solution.py
@@ -9,7 +9,6 @@
 
 MIB = 1 << 20
 TILE = (8, 128)
-TILE_ROWS = 16
 VMEM = pl.BlockSpec(memory_space=pltpu.VMEM)
 SMEM = pl.BlockSpec(memory_space=pltpu.SMEM)
 HBM = pl.BlockSpec(memory_space=pltpu.HBM)
@@ -49,9 +48,22 @@
     return jnp.sum(jnp.sum(value, axis=0, keepdims=True), axis=1, keepdims=True)
 
 
-def inner_kernel(square_scale, vectors, left, right_hbm, inner, squares, right, sem):
-    fetch = pltpu.make_async_copy(right_hbm, right, sem)
-    fetch.start()
+def load_kernel(source, target, sems):
+    parts = sems.shape[0] // source.shape[0]
+    size = source.shape[1] // parts
+    copies = []
+    for term in range(source.shape[0]):
+        for part in range(parts):
+            rows = pl.ds(part * size, size)
+            sem = sems.at[term * parts + part]
+            copies.append(pltpu.make_async_copy(source.at[term, rows], target.at[term, rows], sem))
+    for copy in copies:
+        copy.start()
+    for copy in copies:
+        copy.wait()
+
+
+def inner_kernel(square_scale, vectors, left, inner, squares):
     terms, states = left.shape[0], left.shape[1]
     stacked = left[...].reshape(terms * states, states)
     sums = []
@@ -68,7 +80,6 @@
         sums.append(total(square) * square_scale)
     trials = len(sums)
     squares[...] = place_rows([(trials * trials + k, value) for k, value in enumerate(sums)])
-    fetch.wait()
 
 
 def place_blocks(sectors, pieces, rights):
@@ -122,15 +133,20 @@
 def halve_last_kernel(kept, received, tile, keep, send):
     keep[0] = kept[0] + received[0].astype(jnp.float32)
     both = kept[1] + received[1].astype(jnp.float32)
-    lines = send.shape[0] - 3 * TILE_ROWS
+    lines = send.shape[0] - 2 * TILE[0]
     send[:lines] = both.astype(jnp.bfloat16).reshape(lines, send.shape[1])
-    left = tile[...]
-    for part in range(3):
-        rounded = left.astype(jnp.bfloat16)
-        left = left - rounded.astype(jnp.float32)
-        block = jnp.concatenate([rounded, jnp.zeros_like(rounded)], axis=0)
-        start = lines + part * TILE_ROWS
-        send[start : start + TILE_ROWS] = jnp.concatenate([block, block], axis=1)
+    left, parts = tile[...], []
+    for _ in range(3):
+        parts.append(left.astype(jnp.bfloat16).astype(jnp.float32))
+        left = left - parts[-1]
+    block = jnp.concatenate(
+        [
+            jnp.concatenate([parts[0], parts[1]], axis=0),
+            jnp.concatenate([parts[2], jnp.zeros_like(left)], axis=0),
+        ],
+        axis=1,
+    )
+    send[lines:] = block.astype(jnp.bfloat16)
 
 
 def halve_kernel(kept, received, keep, send):
@@ -143,24 +159,23 @@
 
 
 def ridden_tile(received):
-    lines = received.shape[0] - 3 * TILE_ROWS
-    parts = []
-    for part in range(3):
-        start = lines + part * TILE_ROWS
-        block = received[start : start + TILE_ROWS, : TILE[1]].astype(jnp.float32)
-        parts.append(block[: TILE[0]])
-    return parts[0] + parts[1] + parts[2]
+    height, width = TILE
+    block = received[received.shape[0] - 2 * height :].astype(jnp.float32)
+    return block[:height, :width] + block[height:, :width] + block[:height, width:]
 
 
 def add_last_kernel(kept, received, result):
     result[...] = (kept[0] + received[0].astype(jnp.float32)).astype(jnp.bfloat16)
 
 
-def finish_kernel(done, kept, received, tile, products, rayleigh):
-    first = done.shape[1]
-    lines = received.shape[0] - 3 * TILE_ROWS
+def finish_kernel(*refs):
+    *done, kept, received, tile, products, rayleigh = refs
+    first = 0
+    for part in done:
+        products[:, first : first + part.shape[1]] = part[...]
+        first += part.shape[1]
+    lines = received.shape[0] - 2 * TILE[0]
     both = received[:lines].astype(jnp.float32).reshape(kept.shape[1:])
-    products[:, :first] = done[...]
     products[:, first:] = (kept[0] + both).astype(jnp.bfloat16)
 
     tile = tile[...] + ridden_tile(received)
@@ -216,7 +231,19 @@
     vectors, left, right = vectors[:, 0], left_ops[:, 0], right_ops[:, 0]
     rows = states // shares
 
-    inner, tile, own = call(
+    right = call(
+        load_kernel,
+        "load_right",
+        1,
+        1,
+        4 * MIB,
+        out_shape=jax.ShapeDtypeStruct(right.shape, jnp.bfloat16),
+        in_specs=[HBM],
+        out_specs=VMEM,
+        scratch_shapes=[pltpu.SemaphoreType.DMA((2 * terms,))],
+    )(in_hbm(right))
+
+    inner, tile = call(
         functools.partial(inner_kernel, 1.0 / shares),
         "inner_products",
         2 * terms * trials * pairs * states**3,
@@ -225,18 +252,15 @@
         out_shape=(
             jax.ShapeDtypeStruct((trials, pairs, states, terms * states), jnp.bfloat16),
             jax.ShapeDtypeStruct(TILE, jnp.float32),
-            jax.ShapeDtypeStruct(right.shape, jnp.bfloat16),
         ),
-        in_specs=[VMEM, VMEM, HBM],
-        out_specs=(VMEM, VMEM, VMEM),
-        scratch_shapes=[pltpu.SemaphoreType.DMA],
-    )(vectors, left, in_hbm(right))
+        in_specs=[VMEM, VMEM],
+        out_specs=(VMEM, VMEM),
+    )(vectors, left)
 
     def behind_inner(block):
         return lax.optimization_barrier((block, inner))[0]
 
     gathered = gather_sectors(right, sectors, behind_inner)
-    gathered[0] = own
 
     def share_of(count, size, dtype):
         return jax.ShapeDtypeStruct((count, trials, size, rows, states), dtype)
@@ -285,7 +309,7 @@
             count = shares // (2 * step)
             last = count == 1 and chunk == len(sizes) - 1
             operands = (keep, received, tile) if last else (keep, received)
-            lines = trials * size * rows + 3 * TILE_ROWS
+            lines = trials * size * rows + 2 * TILE[0]
             keep, send = call(
                 halve_last_kernel if last else halve_kernel,
                 "halve_rows",
@@ -304,17 +328,20 @@
             received = swap(send, "term", step)
         parts += [keep, received]
 
-    kept, received, *second = parts
-    done = call(
-        add_last_kernel,
-        "add_last_share",
-        10**10,
-        1,
-        8 * MIB,
-        out_shape=jax.ShapeDtypeStruct((trials, sizes[0], rows, states), jnp.bfloat16),
-        in_specs=[VMEM, VMEM],
-        out_specs=VMEM,
-    )(kept, received)
+    done = []
+    for chunk, size in enumerate(sizes[:-1]):
+        done.append(
+            call(
+                add_last_kernel,
+                "add_last_share",
+                10**10,
+                1,
+                8 * MIB,
+                out_shape=jax.ShapeDtypeStruct((trials, size, rows, states), jnp.bfloat16),
+                in_specs=[VMEM, VMEM],
+                out_specs=VMEM,
+            )(*parts[2 * chunk : 2 * chunk + 2])
+        )
     products, rayleigh = call(
         finish_kernel,
         "finish",
@@ -325,9 +352,9 @@
             jax.ShapeDtypeStruct((trials, pairs, rows, states), jnp.bfloat16),
             jax.ShapeDtypeStruct((trials, trials), jnp.float32),
         ),
-        in_specs=[VMEM] * 4,
+        in_specs=[VMEM] * (len(done) + 3),
         out_specs=(VMEM, VMEM),
-    )(done, *second, tile)
+    )(*done, *parts[-2:], tile)
     return (products[:, None], rayleigh)
 
 

time: 50.4 us -> 50.6 us (level)
  Pallas kernels: 5.24 us -> 6.27 us
  waiting for transfers between devices: 21.1 us -> 20.1 us
    pallas_call x0 -> x1, Pallas kernels: none -> 1.05 us  [local(): call(load_kernel, 'load_right', 1, 1, 4 * MIB, out_shape=jax.ShapeDtypeSt...]
    ppermute x16, waiting for transfers between devices: 21.1 us -> 20.1 us  [swap(): lax.ppermute(value, axis, [(place, place ^ masks[place & 1]) for place in...]
where the time goes in v12:
time: 50.6 us; the launch traced here: 50.3 us
  starting transfers between devices  20.9 us (41%)
  waiting for transfers between devices  20.1 us (40%)
  Pallas kernels  6.27 us (12%)
  local copies, waits for them, and re-layouts  2.22 us (4%)
  between operations  0.7 us (1%)
    ppermute x16, starting transfers between devices, swap(): lax.ppermute(value, axis, [(place, place ^ masks[place & 1]) for place in...  20.9 us
    ppermute x16, waiting for transfers between devices, swap(): lax.ppermute(value, axis, [(place, place ^ masks[place & 1]) for place in...  20.1 us
    pallas_call x2, Pallas kernels, local(): call(functools.partial(sum_kernel, sectors, first), 'sum_over_terms', 2 *...  3.33 us
    unnamed x4, local copies, waits for them, and re-layouts  2.22 us
    pallas_call x1, Pallas kernels, local(): call(load_kernel, 'load_right', 1, 1, 4 * MIB, out_shape=jax.ShapeDtypeSt...  1.05 us
  transfers between devices with their start and end apart: 16, of which 8 were waited for; matrix products, arithmetic and copies ran while one was open for 0% of the time, Pallas kernels for 5%

profile of v12, /device:TPU:0, one launch (start us, length us, event | category | flops | bytes accessed | tf_op | source)
XLA Modules:
  0.0 50.3 jit_solution(4353509440570043475)
XLA Ops:
  0.6 1.1 %load_right.1.rest_0_ = bf16[3,256,256]{2,1,0:T(8,128)(2,1)S(1)} custom-call(bf16[3,256,256]{2,1,0:T(8,128)(2,1)} %bitcast.10), custom_call_target="tpu_custom_call" | custom-call | flops 1 | bytes 1 | tf_op jit(solution)/shard_map/load_right/pallas_call | solution.py:234
  1.7 3.0 %collective-permute-start.1 = (bf16[3,256,256]{2,1,0:T(8,128)(2,1)S(1)}, bf16[3,256,256]{2,1,0:T(8,128)(2,1)S(1)}, u32[]{:S(2)}, u32[]{:S(2)}) collective-permute-start(bf16[3,256,256]{2,1,0:T(8,128)(2,1)S(1)} %load_right.1.rest_0_), channel_id=1, source_target_pairs={{0,8},{4,20},{8,0},{12,28},{16,24},{20,4},{24,16},{28,12},{1,9},{5... | collective-permute-start | bytes 1179656 | tf_op jit(solution)/shard_map/ppermute | solution.py:20
  4.7 1.2 %copy-done = bf16[2,1,4,256,256]{4,3,2,1,0:T(8,128)(2,1)S(1)} copy-done((bf16[2,1,4,256,256]{4,3,2,1,0:T(8,128)(2,1)S(1)}, bf16[2,1,4,256,256]{4,3,2,1,0:T(8,128)(2,1)}, u32[]{:S(2)}) %copy-start) | copy-done | bytes 1048600
  5.9 1.0 %copy-done.1 = bf16[3,1,256,256]{3,2,1,0:T(8,128)(2,1)S(1)} copy-done((bf16[3,1,256,256]{3,2,1,0:T(8,128)(2,1)S(1)}, bf16[3,1,256,256]{3,2,1,0:T(8,128)(2,1)}, u32[]{:S(2)}) %copy-start.1) | copy-done | bytes 393240
  6.9 1.0 %inner_products.1 = (bf16[2,4,256,768]{3,2,1,0:T(8,128)(2,1)S(1)}, f32[8,128]{1,0:T(8,128)S(1)}) custom-call(bf16[2,4,256,256]{3,2,1,0:T(8,128)(2,1)S(1)} %bitcast.6, bf16[3,256,256]{2,1,0:T(8,128)(2,1)S(1)} %bitcast.9), custom_call_target="tpu_custom_call" | custom-call | flops 805306368 | bytes 5242880 | tf_op jit(solution)/shard_map/inner_products/pallas_call | solution.py:246
  7.9 1.6 %collective-permute-start.3 = (bf16[3,256,256]{2,1,0:T(8,128)(2,1)S(1)}, bf16[3,256,256]{2,1,0:T(8,128)(2,1)S(1)}, u32[]{:S(2)}, u32[]{:S(2)}) collective-permute-start(bf16[3,256,256]{2,1,0:T(8,128)(2,1)S(1)} %load_right.1.rest_0_), channel_id=1, source_target_pairs={{0,16},{4,12},{8,24},{12,4},{16,0},{20,28},{24,8},{28,20},{1,17},{... | collective-permute-start | bytes 1179656 | tf_op jit(solution)/shard_map/ppermute | solution.py:20
  9.5 1.2 %collective-permute-done.1.rest_2_ = bf16[3,256,256]{2,1,0:T(8,128)(2,1)S(1)} collective-permute-done((bf16[3,256,256]{2,1,0:T(8,128)(2,1)S(1)}, bf16[3,256,256]{2,1,0:T(8,128)(2,1)S(1)}, u32[]{:S(2)}, u32[]{:S(2)}) %collective-permute-start.1) | collective-permute-done | bytes 393248 | tf_op jit(solution)/shard_map/ppermute | solution.py:20
  10.7 3.7 %collective-permute-start.5 = (bf16[3,256,256]{2,1,0:T(8,128)(2,1)S(1)}, bf16[3,256,256]{2,1,0:T(8,128)(2,1)S(1)}, u32[]{:S(2)}, u32[]{:S(2)}) collective-permute-start(bf16[3,256,256]{2,1,0:T(8,128)(2,1)S(1)} %collective-permute-done.1.rest_2_), channel_id=1, source_target_pairs={{0,16},{4,12},{8,24},{12,4},{16,0},{20,28},{24,8},{28,20},{1,17},{... | collective-permute-start | bytes 1179656 | tf_op jit(solution)/shard_map/ppermute | solution.py:20
  15.0 0.8 %collective-permute-done.3.rest_4_ = bf16[3,256,256]{2,1,0:T(8,128)(2,1)S(1)} collective-permute-done((bf16[3,256,256]{2,1,0:T(8,128)(2,1)S(1)}, bf16[3,256,256]{2,1,0:T(8,128)(2,1)S(1)}, u32[]{:S(2)}, u32[]{:S(2)}) %collective-permute-start.3) | collective-permute-done | bytes 393248 | tf_op jit(solution)/shard_map/ppermute | solution.py:20
  15.8 4.5 %collective-permute-done.5.rest_6_ = bf16[3,256,256]{2,1,0:T(8,128)(2,1)S(1)} collective-permute-done((bf16[3,256,256]{2,1,0:T(8,128)(2,1)S(1)}, bf16[3,256,256]{2,1,0:T(8,128)(2,1)S(1)}, u32[]{:S(2)}, u32[]{:S(2)}) %collective-permute-start.5) | collective-permute-done | bytes 393248 | tf_op jit(solution)/shard_map/ppermute | solution.py:20
  20.3 1.7 %collective-permute-done.6.rest_7_ = bf16[3,256,256]{2,1,0:T(8,128)(2,1)S(1)} collective-permute-done((bf16[3,256,256]{2,1,0:T(8,128)(2,1)S(1)}, bf16[3,256,256]{2,1,0:T(8,128)(2,1)S(1)}, u32[]{:S(2)}, u32[]{:S(2)}) %collective-permute-start.6) | collective-permute-done | bytes 393248 | tf_op jit(solution)/shard_map/ppermute | solution.py:20
  22.0 1.8 %sum_over_terms.2 = (f32[2,2,2,64,256]{4,3,2,1,0:T(8,128)S(1)}, bf16[2,2,2,64,256]{4,3,2,1,0:T(8,128)(2,1)S(1)}, f32[8,128]{1,0:T(8,128)S(1)}, bf16[8,3,256,256]{3,2,1,0:T(8,128)(2,1)S(1)}) custom-call(s32[3,4]{1,0:T(4,128)} %offsets.3, bf16[2,4,256,256]{3,2,1,0:T(8,128)(2,1)S(1)} %bitcast.7, bf16[2,4,256,768]{3,2,1,0:T(8,128)(2,1)S(1)} %get-tuple-element.18.inner, ...), custom_call_target="tpu_custom_call" | custom-call | flops 402653184 | bytes 4194304 | tf_op jit(solution)/shard_map/sum_over_terms/pallas_call | solution.py:280
  23.7 1.4 %collective-permute-start.7 = (bf16[2,2,2,64,256]{4,3,2,1,0:T(8,128)(2,1)S(1)}, bf16[2,2,2,64,256]{4,3,2,1,0:T(8,128)(2,1)S(1)}, u32[]{:S(2)}, u32[]{:S(2)}) collective-permute-start(bf16[2,2,2,64,256]{4,3,2,1,0:T(8,128)(2,1)S(1)} %get-tuple-element.22), channel_id=1, source_target_pairs={{0,1},{1,0},{2,3},{3,2},{4,5},{5,4},{6,7},{7,6},{8,9},{9,8},{10,11... | collective-permute-start | bytes 786440 | tf_op jit(solution)/shard_map/ppermute | solution.py:20
  25.1 1.6 %sum_over_terms.3 = (f32[2,2,2,64,256]{4,3,2,1,0:T(8,128)S(1)}, bf16[2,2,2,64,256]{4,3,2,1,0:T(8,128)(2,1)S(1)}, f32[8,128]{1,0:T(8,128)S(1)}) custom-call(s32[3,4]{1,0:T(4,128)} %offsets.3, bf16[2,4,256,256]{3,2,1,0:T(8,128)(2,1)S(1)} %bitcast.8, bf16[2,4,256,768]{3,2,1,0:T(8,128)(2,1)S(1)} %get-tuple-element.18.inner, ...), custom_call_target="tpu_custom_call" | custom-call | flops 402653184 | bytes 4194304 | tf_op jit(solution)/shard_map/sum_over_terms/pallas_call | solution.py:280
  27.4 1.2 %collective-permute-done.10 = f32[8,128]{1,0:T(8,128)S(1)} collective-permute-done((f32[8,128]{1,0:T(8,128)S(1)}, f32[8,128]{1,0:T(8,128)S(1)}, u32[]{:S(2)}, u32[]{:S(2)}) %collective-permute-start.10) | collective-permute-done | bytes 4128 | tf_op jit(solution)/shard_map/ppermute | solution.py:20
  28.5 2.7 %collective-permute-start.13 = (f32[8,128]{1,0:T(8,128)S(1)}, f32[8,128]{1,0:T(8,128)S(1)}, u32[]{:S(2)}, u32[]{:S(2)}) collective-permute-start(f32[8,128]{1,0:T(8,128)S(1)} %add.15), channel_id=1, source_target_pairs={{0,24},{4,28},{8,16},{12,20},{16,8},{20,12},{24,0},{28,4},{1,25},{... | collective-permute-start | bytes 12296 | tf_op jit(solution)/shard_map/ppermute | solution.py:20
  31.3 0.7 %collective-permute-start.11 = (f32[8,128]{1,0:T(8,128)S(1)}, f32[8,128]{1,0:T(8,128)S(1)}, u32[]{:S(2)}, u32[]{:S(2)}) collective-permute-start(f32[8,128]{1,0:T(8,128)S(1)} %add.15), channel_id=1, source_target_pairs={{0,8},{4,12},{8,0},{12,4},{16,24},{20,28},{24,16},{28,20},{1,9},{5... | collective-permute-start | bytes 12296 | tf_op jit(solution)/shard_map/ppermute | solution.py:20
  32.0 0.9 %collective-permute-done.7.received = bf16[2,2,2,64,256]{4,3,2,1,0:T(8,128)(2,1)S(1)} collective-permute-done((bf16[2,2,2,64,256]{4,3,2,1,0:T(8,128)(2,1)S(1)}, bf16[2,2,2,64,256]{4,3,2,1,0:T(8,128)(2,1)S(1)}, u32[]{:S(2)}, u32[]{:S(2)}) %collective-permute-start.7) | collective-permute-done | bytes 262176 | tf_op jit(solution)/shard_map/ppermute | solution.py:20
  33.0 2.4 %collective-permute-start.8 = (bf16[1,2,2,64,256]{4,3,2,1,0:T(8,128)(2,1)S(1)}, bf16[1,2,2,64,256]{4,3,2,1,0:T(8,128)(2,1)S(1)}, u32[]{:S(2)}, u32[]{:S(2)}) collective-permute-start(bf16[1,2,2,64,256]{4,3,2,1,0:T(8,128)(2,1)S(1)} %get-tuple-element.24), channel_id=1, source_target_pairs={{0,2},{1,3},{2,0},{3,1},{4,6},{5,7},{6,4},{7,5},{8,10},{9,11},{10,... | collective-permute-start | bytes 393224 | tf_op jit(solution)/shard_map/ppermute | solution.py:20
  35.4 1.6 %collective-permute-start.14 = (f32[8,128]{1,0:T(8,128)S(1)}, f32[8,128]{1,0:T(8,128)S(1)}, u32[]{:S(2)}, u32[]{:S(2)}) collective-permute-start(f32[8,128]{1,0:T(8,128)S(1)} %add_add_fusion), channel_id=1, source_target_pairs={{0,1},{1,0},{2,3},{3,2},{4,5},{5,4},{6,7},{7,6},{8,9},{9,8},{10,11... | collective-permute-start | bytes 12296 | tf_op jit(solution)/shard_map/ppermute | solution.py:20
  37.1 3.5 %collective-permute-done.14 = f32[8,128]{1,0:T(8,128)S(1)} collective-permute-done((f32[8,128]{1,0:T(8,128)S(1)}, f32[8,128]{1,0:T(8,128)S(1)}, u32[]{:S(2)}, u32[]{:S(2)}) %collective-permute-start.14) | collective-permute-done | bytes 4128 | tf_op jit(solution)/shard_map/ppermute | solution.py:20
  40.7 2.4 %collective-permute-start.15 = (bf16[272,256]{1,0:T(8,128)(2,1)S(1)}, bf16[272,256]{1,0:T(8,128)(2,1)S(1)}, u32[]{:S(2)}, u32[]{:S(2)}) collective-permute-start(bf16[272,256]{1,0:T(8,128)(2,1)S(1)} %get-tuple-element.31), channel_id=1, source_target_pairs={{0,2},{1,3},{2,0},{3,1},{4,6},{5,7},{6,4},{7,5},{8,10},{9,11},{10,... | collective-permute-start | bytes 417800 | tf_op jit(solution)/shard_map/ppermute | solution.py:20
  43.2 6.4 %collective-permute-done.15.refs_2_ = bf16[272,256]{1,0:T(8,128)(2,1)S(1)} collective-permute-done((bf16[272,256]{1,0:T(8,128)(2,1)S(1)}, bf16[272,256]{1,0:T(8,128)(2,1)S(1)}, u32[]{:S(2)}, u32[]{:S(2)}) %collective-permute-start.15) | collective-permute-done | bytes 139296 | tf_op jit(solution)/shard_map/ppermute | solution.py:20
  49.5 0.7 %finish.1 = (bf16[2,4,64,256]{3,2,1,0:T(8,128)(2,1)}, f32[2,2]{1,0:T(2,128)}) custom-call(bf16[2,2,64,256]{3,2,1,0:T(8,128)(2,1)S(1)} %add_last_share.1.refs_0_, f32[1,2,2,64,256]{4,3,2,1,0:T(8,128)S(1)} %get-tuple-element.30.refs_1_, bf16[272,256]{1,0:T(8,128)(2,1)S(1)} %collective-permute-done.15.refs_2_, f32[8,128]{1,0:T(8,128)S(1)} %add.19.tile.refs_3_), custom_call_target="tpu_custom_call" | custom-call | flops 1 | bytes 1 | tf_op jit(solution)/shard_map/finish/pallas_call | solution.py:345
  (23 shorter events, 1.4 us)
Async XLA Ops:
  1.7 9.1 %collective-permute-start.1 = (bf16[3,256,256]{2,1,0:T(8,128)(2,1)S(1)}, bf16[3,256,256]{2,1,0:T(8,128)(2,1)S(1)}, u32[]{:S(2)}, u32[]{:S(2)}) collective-permute-start(bf16[3,256,256]{2,1,0:T(8,128)(2,1)S(1)} %load_right.1.rest_0_), channel_id=1, source_target_pairs={{0,8},{4,20},{8,0},{12,28},{16,24},{20,4},{24,16},{28,12},{1,9},{5... | collective-permute-start | bytes 1179656 | tf_op jit(solution)/shard_map/ppermute | solution.py:20
  4.7 1.2 %copy-start = (bf16[2,1,4,256,256]{4,3,2,1,0:T(8,128)(2,1)S(1)}, bf16[2,1,4,256,256]{4,3,2,1,0:T(8,128)(2,1)}, u32[]{:S(2)}) copy-start(bf16[2,1,4,256,256]{4,3,2,1,0:T(8,128)(2,1)} %param.4) | copy-start | bytes 3145732
  5.9 1.0 %copy-start.1 = (bf16[3,1,256,256]{3,2,1,0:T(8,128)(2,1)S(1)}, bf16[3,1,256,256]{3,2,1,0:T(8,128)(2,1)}, u32[]{:S(2)}) copy-start(bf16[3,1,256,256]{3,2,1,0:T(8,128)(2,1)} %param.5) | copy-start | bytes 1179652
  7.9 7.8 %collective-permute-start.3 = (bf16[3,256,256]{2,1,0:T(8,128)(2,1)S(1)}, bf16[3,256,256]{2,1,0:T(8,128)(2,1)S(1)}, u32[]{:S(2)}, u32[]{:S(2)}) collective-permute-start(bf16[3,256,256]{2,1,0:T(8,128)(2,1)S(1)} %load_right.1.rest_0_), channel_id=1, source_target_pairs={{0,16},{4,12},{8,24},{12,4},{16,0},{20,28},{24,8},{28,20},{1,17},{... | collective-permute-start | bytes 1179656 | tf_op jit(solution)/shard_map/ppermute | solution.py:20
  10.7 9.5 %collective-permute-start.5 = (bf16[3,256,256]{2,1,0:T(8,128)(2,1)S(1)}, bf16[3,256,256]{2,1,0:T(8,128)(2,1)S(1)}, u32[]{:S(2)}, u32[]{:S(2)}) collective-permute-start(bf16[3,256,256]{2,1,0:T(8,128)(2,1)S(1)} %collective-permute-done.1.rest_2_), channel_id=1, source_target_pairs={{0,16},{4,12},{8,24},{12,4},{16,0},{20,28},{24,8},{28,20},{1,17},{... | collective-permute-start | bytes 1179656 | tf_op jit(solution)/shard_map/ppermute | solution.py:20
  14.5 5.8 %collective-permute-start = (bf16[3,256,256]{2,1,0:T(8,128)(2,1)S(1)}, bf16[3,256,256]{2,1,0:T(8,128)(2,1)S(1)}, u32[]{:S(2)}, u32[]{:S(2)}) collective-permute-start(bf16[3,256,256]{2,1,0:T(8,128)(2,1)S(1)} %load_right.1.rest_0_), channel_id=1, source_target_pairs={{0,4},{4,0},{8,12},{12,8},{16,20},{20,16},{24,28},{28,24},{1,5},{5... | collective-permute-start | bytes 1179656 | tf_op jit(solution)/shard_map/ppermute | solution.py:20
  14.5 5.8 %collective-permute-start.2 = (bf16[3,256,256]{2,1,0:T(8,128)(2,1)S(1)}, bf16[3,256,256]{2,1,0:T(8,128)(2,1)S(1)}, u32[]{:S(2)}, u32[]{:S(2)}) collective-permute-start(bf16[3,256,256]{2,1,0:T(8,128)(2,1)S(1)} %collective-permute-done.1.rest_2_), channel_id=1, source_target_pairs={{0,4},{4,0},{8,12},{12,8},{16,20},{20,16},{24,28},{28,24},{1,5},{5... | collective-permute-start | bytes 1179656 | tf_op jit(solution)/shard_map/ppermute | solution.py:20
  15.8 4.5 %collective-permute-start.4 = (bf16[3,256,256]{2,1,0:T(8,128)(2,1)S(1)}, bf16[3,256,256]{2,1,0:T(8,128)(2,1)S(1)}, u32[]{:S(2)}, u32[]{:S(2)}) collective-permute-start(bf16[3,256,256]{2,1,0:T(8,128)(2,1)S(1)} %collective-permute-done.3.rest_4_), channel_id=1, source_target_pairs={{0,4},{4,0},{8,12},{12,8},{16,20},{20,16},{24,28},{28,24},{1,5},{5... | collective-permute-start | bytes 1179656 | tf_op jit(solution)/shard_map/ppermute | solution.py:20
  20.2 1.7 %collective-permute-start.6 = (bf16[3,256,256]{2,1,0:T(8,128)(2,1)S(1)}, bf16[3,256,256]{2,1,0:T(8,128)(2,1)S(1)}, u32[]{:S(2)}, u32[]{:S(2)}) collective-permute-start(bf16[3,256,256]{2,1,0:T(8,128)(2,1)S(1)} %collective-permute-done.5.rest_6_), channel_id=1, source_target_pairs={{0,4},{4,0},{8,12},{12,8},{16,20},{20,16},{24,28},{28,24},{1,5},{5... | collective-permute-start | bytes 1179656 | tf_op jit(solution)/shard_map/ppermute | solution.py:20
  23.7 9.2 %collective-permute-start.7 = (bf16[2,2,2,64,256]{4,3,2,1,0:T(8,128)(2,1)S(1)}, bf16[2,2,2,64,256]{4,3,2,1,0:T(8,128)(2,1)S(1)}, u32[]{:S(2)}, u32[]{:S(2)}) collective-permute-start(bf16[2,2,2,64,256]{4,3,2,1,0:T(8,128)(2,1)S(1)} %get-tuple-element.22), channel_id=1, source_target_pairs={{0,1},{1,0},{2,3},{3,2},{4,5},{5,4},{6,7},{7,6},{8,9},{9,8},{10,11... | collective-permute-start | bytes 786440 | tf_op jit(solution)/shard_map/ppermute | solution.py:20
  26.7 13.9 %collective-permute-start.9 = (bf16[2,2,2,64,256]{4,3,2,1,0:T(8,128)(2,1)S(1)}, bf16[2,2,2,64,256]{4,3,2,1,0:T(8,128)(2,1)S(1)}, u32[]{:S(2)}, u32[]{:S(2)}) collective-permute-start(bf16[2,2,2,64,256]{4,3,2,1,0:T(8,128)(2,1)S(1)} %get-tuple-element.28), channel_id=1, source_target_pairs={{0,1},{1,0},{2,3},{3,2},{4,5},{5,4},{6,7},{7,6},{8,9},{9,8},{10,11... | collective-permute-start | bytes 786440 | tf_op jit(solution)/shard_map/ppermute | solution.py:20
  27.4 1.2 %collective-permute-start.10 = (f32[8,128]{1,0:T(8,128)S(1)}, f32[8,128]{1,0:T(8,128)S(1)}, u32[]{:S(2)}, u32[]{:S(2)}) collective-permute-start(f32[8,128]{1,0:T(8,128)S(1)} %get-tuple-element.29), channel_id=1, source_target_pairs={{0,4},{4,0},{8,12},{12,8},{16,20},{20,16},{24,28},{28,24},{1,5},{5... | collective-permute-start | bytes 12296 | tf_op jit(solution)/shard_map/ppermute | solution.py:20
  28.5 6.9 %collective-permute-start.13 = (f32[8,128]{1,0:T(8,128)S(1)}, f32[8,128]{1,0:T(8,128)S(1)}, u32[]{:S(2)}, u32[]{:S(2)}) collective-permute-start(f32[8,128]{1,0:T(8,128)S(1)} %add.15), channel_id=1, source_target_pairs={{0,24},{4,28},{8,16},{12,20},{16,8},{20,12},{24,0},{28,4},{1,25},{... | collective-permute-start | bytes 12296 | tf_op jit(solution)/shard_map/ppermute | solution.py:20
  31.3 4.1 %collective-permute-start.12 = (f32[8,128]{1,0:T(8,128)S(1)}, f32[8,128]{1,0:T(8,128)S(1)}, u32[]{:S(2)}, u32[]{:S(2)}) collective-permute-start(f32[8,128]{1,0:T(8,128)S(1)} %add.15), channel_id=1, source_target_pairs={{0,16},{4,20},{8,24},{12,28},{16,0},{20,4},{24,8},{28,12},{1,17},{... | collective-permute-start | bytes 12296 | tf_op jit(solution)/shard_map/ppermute | solution.py:20
  31.3 4.1 %collective-permute-start.11 = (f32[8,128]{1,0:T(8,128)S(1)}, f32[8,128]{1,0:T(8,128)S(1)}, u32[]{:S(2)}, u32[]{:S(2)}) collective-permute-start(f32[8,128]{1,0:T(8,128)S(1)} %add.15), channel_id=1, source_target_pairs={{0,8},{4,12},{8,0},{12,4},{16,24},{20,28},{24,16},{28,20},{1,9},{5... | collective-permute-start | bytes 12296 | tf_op jit(solution)/shard_map/ppermute | solution.py:20
  33.0 10.2 %collective-permute-start.8 = (bf16[1,2,2,64,256]{4,3,2,1,0:T(8,128)(2,1)S(1)}, bf16[1,2,2,64,256]{4,3,2,1,0:T(8,128)(2,1)S(1)}, u32[]{:S(2)}, u32[]{:S(2)}) collective-permute-start(bf16[1,2,2,64,256]{4,3,2,1,0:T(8,128)(2,1)S(1)} %get-tuple-element.24), channel_id=1, source_target_pairs={{0,2},{1,3},{2,0},{3,1},{4,6},{5,7},{6,4},{7,5},{8,10},{9,11},{10,... | collective-permute-start | bytes 393224 | tf_op jit(solution)/shard_map/ppermute | solution.py:20
  35.4 5.2 %collective-permute-start.14 = (f32[8,128]{1,0:T(8,128)S(1)}, f32[8,128]{1,0:T(8,128)S(1)}, u32[]{:S(2)}, u32[]{:S(2)}) collective-permute-start(f32[8,128]{1,0:T(8,128)S(1)} %add_add_fusion), channel_id=1, source_target_pairs={{0,1},{1,0},{2,3},{3,2},{4,5},{5,4},{6,7},{7,6},{8,9},{9,8},{10,11... | collective-permute-start | bytes 12296 | tf_op jit(solution)/shard_map/ppermute | solution.py:20
  40.7 8.8 %collective-permute-start.15 = (bf16[272,256]{1,0:T(8,128)(2,1)S(1)}, bf16[272,256]{1,0:T(8,128)(2,1)S(1)}, u32[]{:S(2)}, u32[]{:S(2)}) collective-permute-start(bf16[272,256]{1,0:T(8,128)(2,1)S(1)} %get-tuple-element.31), channel_id=1, source_target_pairs={{0,2},{1,3},{2,0},{3,1},{4,6},{5,7},{6,4},{7,5},{8,10},{9,11},{10,... | collective-permute-start | bytes 417800 | tf_op jit(solution)/shard_map/ppermute | solution.py:20

commit v13 on v12

--- a/solution.py
+++ b/solution.py
@@ -22,7 +22,7 @@
 
 def turned(mask, parity, count):
     bits = count.bit_length() - 1
-    if not parity:
+    if parity:
         return mask
     return sum(1 << (bits - bit) for bit in range(1, bits) if mask >> bit & 1) | mask & 1
 
@@ -48,22 +48,9 @@
     return jnp.sum(jnp.sum(value, axis=0, keepdims=True), axis=1, keepdims=True)
 
 
-def load_kernel(source, target, sems):
-    parts = sems.shape[0] // source.shape[0]
-    size = source.shape[1] // parts
-    copies = []
-    for term in range(source.shape[0]):
-        for part in range(parts):
-            rows = pl.ds(part * size, size)
-            sem = sems.at[term * parts + part]
-            copies.append(pltpu.make_async_copy(source.at[term, rows], target.at[term, rows], sem))
-    for copy in copies:
-        copy.start()
-    for copy in copies:
-        copy.wait()
-
-
-def inner_kernel(square_scale, vectors, left, inner, squares):
+def inner_kernel(square_scale, vectors, left, right_hbm, inner, squares, right, sem):
+    fetch = pltpu.make_async_copy(right_hbm, right, sem)
+    fetch.start()
     terms, states = left.shape[0], left.shape[1]
     stacked = left[...].reshape(terms * states, states)
     sums = []
@@ -80,6 +67,7 @@
         sums.append(total(square) * square_scale)
     trials = len(sums)
     squares[...] = place_rows([(trials * trials + k, value) for k, value in enumerate(sums)])
+    fetch.wait()
 
 
 def place_blocks(sectors, pieces, rights):
@@ -231,19 +219,7 @@
     vectors, left, right = vectors[:, 0], left_ops[:, 0], right_ops[:, 0]
     rows = states // shares
 
-    right = call(
-        load_kernel,
-        "load_right",
-        1,
-        1,
-        4 * MIB,
-        out_shape=jax.ShapeDtypeStruct(right.shape, jnp.bfloat16),
-        in_specs=[HBM],
-        out_specs=VMEM,
-        scratch_shapes=[pltpu.SemaphoreType.DMA((2 * terms,))],
-    )(in_hbm(right))
-
-    inner, tile = call(
+    inner, tile, own = call(
         functools.partial(inner_kernel, 1.0 / shares),
         "inner_products",
         2 * terms * trials * pairs * states**3,
@@ -252,15 +228,18 @@
         out_shape=(
             jax.ShapeDtypeStruct((trials, pairs, states, terms * states), jnp.bfloat16),
             jax.ShapeDtypeStruct(TILE, jnp.float32),
+            jax.ShapeDtypeStruct(right.shape, jnp.bfloat16),
         ),
-        in_specs=[VMEM, VMEM],
-        out_specs=(VMEM, VMEM),
-    )(vectors, left)
+        in_specs=[VMEM, VMEM, HBM],
+        out_specs=(VMEM, VMEM, VMEM),
+        scratch_shapes=[pltpu.SemaphoreType.DMA],
+    )(vectors, left, in_hbm(right))
 
     def behind_inner(block):
         return lax.optimization_barrier((block, inner))[0]
 
     gathered = gather_sectors(right, sectors, behind_inner)
+    gathered[0] = own
 
     def share_of(count, size, dtype):
         return jax.ShapeDtypeStruct((count, trials, size, rows, states), dtype)

time: 50.6 us -> 49.6 us (0.980)
  Pallas kernels: 6.27 us -> 5.24 us
    pallas_call x1 -> x0, Pallas kernels: 1.05 us -> none  [local(): call(load_kernel, 'load_right', 1, 1, 4 * MIB, out_shape=jax.ShapeDtypeSt...]
  transfers between devices with their start and end apart: 16 -> 16, of which waited for: 8 -> 9; matrix products, arithmetic and copies ran while one was open for 0% -> 0% of each run, Pallas kernels for 5% -> 6%
where the time goes in v13:
time: 49.6 us; the launch traced here: 49.4 us
  starting transfers between devices  20.7 us (42%)
  waiting for transfers between devices  20.5 us (41%)
  Pallas kernels  5.24 us (11%)
  local copies, waits for them, and re-layouts  2.22 us (4%)
  between operations  0.68 us (1%)
    ppermute x16, starting transfers between devices, swap(): lax.ppermute(value, axis, [(place, place ^ masks[place & 1]) for place in...  20.7 us
    ppermute x16, waiting for transfers between devices, swap(): lax.ppermute(value, axis, [(place, place ^ masks[place & 1]) for place in...  20.5 us
    pallas_call x2, Pallas kernels, local(): call(functools.partial(sum_kernel, sectors, first), 'sum_over_terms', 2 *...  3.34 us
    unnamed x4, local copies, waits for them, and re-layouts  2.22 us
    pallas_call x1, Pallas kernels, local(): call(functools.partial(inner_kernel, 1.0 / shares), 'inner_products', 2 *...  1 us
  transfers between devices with their start and end apart: 16, of which 9 were waited for; matrix products, arithmetic and copies ran while one was open for 0% of the time, Pallas kernels for 6%

profile of v13, /device:TPU:0, one launch (start us, length us, event | category | flops | bytes accessed | tf_op | source)
XLA Modules:
  0.0 49.4 jit_solution(2691041772392415422)
XLA Ops:
  0.6 3.0 %collective-permute-start.1 = (bf16[3,256,256]{2,1,0:T(8,128)(2,1)}, bf16[3,256,256]{2,1,0:T(8,128)(2,1)S(1)}, u32[]{:S(2)}, u32[]{:S(2)}) collective-permute-start(bf16[3,256,256]{2,1,0:T(8,128)(2,1)} %bitcast.10), channel_id=1, source_target_pairs={{0,16},{4,12},{8,24},{12,4},{16,0},{20,28},{24,8},{28,20},{1,17},{... | collective-permute-start | bytes 1179656 | tf_op jit(solution)/shard_map/ppermute | solution.py:20
  3.7 1.2 %copy-done = bf16[2,1,4,256,256]{4,3,2,1,0:T(8,128)(2,1)S(1)} copy-done((bf16[2,1,4,256,256]{4,3,2,1,0:T(8,128)(2,1)S(1)}, bf16[2,1,4,256,256]{4,3,2,1,0:T(8,128)(2,1)}, u32[]{:S(2)}) %copy-start) | copy-done | bytes 1048600
  4.9 1.0 %copy-done.1 = bf16[3,1,256,256]{3,2,1,0:T(8,128)(2,1)S(1)} copy-done((bf16[3,1,256,256]{3,2,1,0:T(8,128)(2,1)S(1)}, bf16[3,1,256,256]{3,2,1,0:T(8,128)(2,1)}, u32[]{:S(2)}) %copy-start.1) | copy-done | bytes 393240
  5.9 1.0 %inner_products.1 = (bf16[2,4,256,768]{3,2,1,0:T(8,128)(2,1)S(1)}, f32[8,128]{1,0:T(8,128)S(1)}, bf16[3,256,256]{2,1,0:T(8,128)(2,1)S(1)}) custom-call(bf16[2,4,256,256]{3,2,1,0:T(8,128)(2,1)S(1)} %bitcast.6, bf16[3,256,256]{2,1,0:T(8,128)(2,1)S(1)} %bitcast.9, bf16[3,256,256]{2,1,0:T(8,128)(2,1)} %bitcast.11), custom_call_target="tpu_custom_call" | custom-call | flops 805306368 | bytes 5242880 | tf_op jit(solution)/shard_map/inner_products/pallas_call | solution.py:222
  6.9 1.6 %collective-permute-start.3 = (bf16[3,256,256]{2,1,0:T(8,128)(2,1)}, bf16[3,256,256]{2,1,0:T(8,128)(2,1)S(1)}, u32[]{:S(2)}, u32[]{:S(2)}) collective-permute-start(bf16[3,256,256]{2,1,0:T(8,128)(2,1)} %bitcast.12), channel_id=1, source_target_pairs={{0,8},{4,20},{8,0},{12,28},{16,24},{20,4},{24,16},{28,12},{1,9},{5... | collective-permute-start | bytes 1179656 | tf_op jit(solution)/shard_map/ppermute | solution.py:20
  8.5 1.6 %collective-permute-done.1.rest_2_ = bf16[3,256,256]{2,1,0:T(8,128)(2,1)S(1)} collective-permute-done((bf16[3,256,256]{2,1,0:T(8,128)(2,1)}, bf16[3,256,256]{2,1,0:T(8,128)(2,1)S(1)}, u32[]{:S(2)}, u32[]{:S(2)}) %collective-permute-start.1) | collective-permute-done | bytes 393248 | tf_op jit(solution)/shard_map/ppermute | solution.py:20
  10.0 3.5 %collective-permute-start.5 = (bf16[3,256,256]{2,1,0:T(8,128)(2,1)S(1)}, bf16[3,256,256]{2,1,0:T(8,128)(2,1)S(1)}, u32[]{:S(2)}, u32[]{:S(2)}) collective-permute-start(bf16[3,256,256]{2,1,0:T(8,128)(2,1)S(1)} %collective-permute-done.1.rest_2_), channel_id=1, source_target_pairs={{0,8},{4,20},{8,0},{12,28},{16,24},{20,4},{24,16},{28,12},{1,9},{5... | collective-permute-start | bytes 1179656 | tf_op jit(solution)/shard_map/ppermute | solution.py:20
  14.1 0.9 %collective-permute-done.3.rest_4_ = bf16[3,256,256]{2,1,0:T(8,128)(2,1)S(1)} collective-permute-done((bf16[3,256,256]{2,1,0:T(8,128)(2,1)}, bf16[3,256,256]{2,1,0:T(8,128)(2,1)S(1)}, u32[]{:S(2)}, u32[]{:S(2)}) %collective-permute-start.3) | collective-permute-done | bytes 393248 | tf_op jit(solution)/shard_map/ppermute | solution.py:20
  15.0 4.4 %collective-permute-done.5.rest_6_ = bf16[3,256,256]{2,1,0:T(8,128)(2,1)S(1)} collective-permute-done((bf16[3,256,256]{2,1,0:T(8,128)(2,1)S(1)}, bf16[3,256,256]{2,1,0:T(8,128)(2,1)S(1)}, u32[]{:S(2)}, u32[]{:S(2)}) %collective-permute-start.5) | collective-permute-done | bytes 393248 | tf_op jit(solution)/shard_map/ppermute | solution.py:20
  19.3 1.7 %collective-permute-done.6.rest_7_ = bf16[3,256,256]{2,1,0:T(8,128)(2,1)S(1)} collective-permute-done((bf16[3,256,256]{2,1,0:T(8,128)(2,1)S(1)}, bf16[3,256,256]{2,1,0:T(8,128)(2,1)S(1)}, u32[]{:S(2)}, u32[]{:S(2)}) %collective-permute-start.6) | collective-permute-done | bytes 393248 | tf_op jit(solution)/shard_map/ppermute | solution.py:20
  21.0 1.8 %sum_over_terms.2 = (f32[2,2,2,64,256]{4,3,2,1,0:T(8,128)S(1)}, bf16[2,2,2,64,256]{4,3,2,1,0:T(8,128)(2,1)S(1)}, f32[8,128]{1,0:T(8,128)S(1)}, bf16[8,3,256,256]{3,2,1,0:T(8,128)(2,1)S(1)}) custom-call(s32[3,4]{1,0:T(4,128)} %offsets.3, bf16[2,4,256,256]{3,2,1,0:T(8,128)(2,1)S(1)} %bitcast.7, bf16[2,4,256,768]{3,2,1,0:T(8,128)(2,1)S(1)} %get-tuple-element.19.inner, ...), custom_call_target="tpu_custom_call" | custom-call | flops 402653184 | bytes 4194304 | tf_op jit(solution)/shard_map/sum_over_terms/pallas_call | solution.py:259
  22.8 1.5 %collective-permute-start.7 = (bf16[2,2,2,64,256]{4,3,2,1,0:T(8,128)(2,1)S(1)}, bf16[2,2,2,64,256]{4,3,2,1,0:T(8,128)(2,1)S(1)}, u32[]{:S(2)}, u32[]{:S(2)}) collective-permute-start(bf16[2,2,2,64,256]{4,3,2,1,0:T(8,128)(2,1)S(1)} %get-tuple-element.24), channel_id=1, source_target_pairs={{0,1},{1,0},{2,3},{3,2},{4,5},{5,4},{6,7},{7,6},{8,9},{9,8},{10,11... | collective-permute-start | bytes 786440 | tf_op jit(solution)/shard_map/ppermute | solution.py:20
  24.3 1.6 %sum_over_terms.3 = (f32[2,2,2,64,256]{4,3,2,1,0:T(8,128)S(1)}, bf16[2,2,2,64,256]{4,3,2,1,0:T(8,128)(2,1)S(1)}, f32[8,128]{1,0:T(8,128)S(1)}) custom-call(s32[3,4]{1,0:T(4,128)} %offsets.3, bf16[2,4,256,256]{3,2,1,0:T(8,128)(2,1)S(1)} %bitcast.8, bf16[2,4,256,768]{3,2,1,0:T(8,128)(2,1)S(1)} %get-tuple-element.19.inner, ...), custom_call_target="tpu_custom_call" | custom-call | flops 402653184 | bytes 4194304 | tf_op jit(solution)/shard_map/sum_over_terms/pallas_call | solution.py:259
  25.8 0.6 %collective-permute-start.9 = (bf16[2,2,2,64,256]{4,3,2,1,0:T(8,128)(2,1)S(1)}, bf16[2,2,2,64,256]{4,3,2,1,0:T(8,128)(2,1)S(1)}, u32[]{:S(2)}, u32[]{:S(2)}) collective-permute-start(bf16[2,2,2,64,256]{4,3,2,1,0:T(8,128)(2,1)S(1)} %get-tuple-element.30), channel_id=1, source_target_pairs={{0,1},{1,0},{2,3},{3,2},{4,5},{5,4},{6,7},{7,6},{8,9},{9,8},{10,11... | collective-permute-start | bytes 786440 | tf_op jit(solution)/shard_map/ppermute | solution.py:20
  26.5 1.2 %collective-permute-done.10 = f32[8,128]{1,0:T(8,128)S(1)} collective-permute-done((f32[8,128]{1,0:T(8,128)S(1)}, f32[8,128]{1,0:T(8,128)S(1)}, u32[]{:S(2)}, u32[]{:S(2)}) %collective-permute-start.10) | collective-permute-done | bytes 4128 | tf_op jit(solution)/shard_map/ppermute | solution.py:20
  27.6 2.8 %collective-permute-start.13 = (f32[8,128]{1,0:T(8,128)S(1)}, f32[8,128]{1,0:T(8,128)S(1)}, u32[]{:S(2)}, u32[]{:S(2)}) collective-permute-start(f32[8,128]{1,0:T(8,128)S(1)} %add.15), channel_id=1, source_target_pairs={{0,24},{4,28},{8,16},{12,20},{16,8},{20,12},{24,0},{28,4},{1,25},{... | collective-permute-start | bytes 12296 | tf_op jit(solution)/shard_map/ppermute | solution.py:20
  30.4 0.7 %collective-permute-start.12 = (f32[8,128]{1,0:T(8,128)S(1)}, f32[8,128]{1,0:T(8,128)S(1)}, u32[]{:S(2)}, u32[]{:S(2)}) collective-permute-start(f32[8,128]{1,0:T(8,128)S(1)} %add.15), channel_id=1, source_target_pairs={{0,16},{4,20},{8,24},{12,28},{16,0},{20,4},{24,8},{28,12},{1,17},{... | collective-permute-start | bytes 12296 | tf_op jit(solution)/shard_map/ppermute | solution.py:20
  31.1 0.9 %collective-permute-done.7.received = bf16[2,2,2,64,256]{4,3,2,1,0:T(8,128)(2,1)S(1)} collective-permute-done((bf16[2,2,2,64,256]{4,3,2,1,0:T(8,128)(2,1)S(1)}, bf16[2,2,2,64,256]{4,3,2,1,0:T(8,128)(2,1)S(1)}, u32[]{:S(2)}, u32[]{:S(2)}) %collective-permute-start.7) | collective-permute-done | bytes 262176 | tf_op jit(solution)/shard_map/ppermute | solution.py:20
  32.0 2.5 %collective-permute-start.8 = (bf16[1,2,2,64,256]{4,3,2,1,0:T(8,128)(2,1)S(1)}, bf16[1,2,2,64,256]{4,3,2,1,0:T(8,128)(2,1)S(1)}, u32[]{:S(2)}, u32[]{:S(2)}) collective-permute-start(bf16[1,2,2,64,256]{4,3,2,1,0:T(8,128)(2,1)S(1)} %get-tuple-element.26), channel_id=1, source_target_pairs={{0,2},{1,3},{2,0},{3,1},{4,6},{5,7},{6,4},{7,5},{8,10},{9,11},{10,... | collective-permute-start | bytes 393224 | tf_op jit(solution)/shard_map/ppermute | solution.py:20
  34.7 1.5 %collective-permute-start.14 = (f32[8,128]{1,0:T(8,128)S(1)}, f32[8,128]{1,0:T(8,128)S(1)}, u32[]{:S(2)}, u32[]{:S(2)}) collective-permute-start(f32[8,128]{1,0:T(8,128)S(1)} %add_add_fusion), channel_id=1, source_target_pairs={{0,1},{1,0},{2,3},{3,2},{4,5},{5,4},{6,7},{7,6},{8,9},{9,8},{10,11... | collective-permute-start | bytes 12296 | tf_op jit(solution)/shard_map/ppermute | solution.py:20
  36.2 3.5 %collective-permute-done.14 = f32[8,128]{1,0:T(8,128)S(1)} collective-permute-done((f32[8,128]{1,0:T(8,128)S(1)}, f32[8,128]{1,0:T(8,128)S(1)}, u32[]{:S(2)}, u32[]{:S(2)}) %collective-permute-start.14) | collective-permute-done | bytes 4128 | tf_op jit(solution)/shard_map/ppermute | solution.py:20
  39.8 2.5 %collective-permute-start.15 = (bf16[272,256]{1,0:T(8,128)(2,1)S(1)}, bf16[272,256]{1,0:T(8,128)(2,1)S(1)}, u32[]{:S(2)}, u32[]{:S(2)}) collective-permute-start(bf16[272,256]{1,0:T(8,128)(2,1)S(1)} %get-tuple-element.33), channel_id=1, source_target_pairs={{0,2},{1,3},{2,0},{3,1},{4,6},{5,7},{6,4},{7,5},{8,10},{9,11},{10,... | collective-permute-start | bytes 417800 | tf_op jit(solution)/shard_map/ppermute | solution.py:20
  42.3 6.3 %collective-permute-done.15.refs_2_ = bf16[272,256]{1,0:T(8,128)(2,1)S(1)} collective-permute-done((bf16[272,256]{1,0:T(8,128)(2,1)S(1)}, bf16[272,256]{1,0:T(8,128)(2,1)S(1)}, u32[]{:S(2)}, u32[]{:S(2)}) %collective-permute-start.15) | collective-permute-done | bytes 139296 | tf_op jit(solution)/shard_map/ppermute | solution.py:20
  48.6 0.7 %finish.1 = (bf16[2,4,64,256]{3,2,1,0:T(8,128)(2,1)}, f32[2,2]{1,0:T(2,128)}) custom-call(bf16[2,2,64,256]{3,2,1,0:T(8,128)(2,1)S(1)} %add_last_share.1.refs_0_, f32[1,2,2,64,256]{4,3,2,1,0:T(8,128)S(1)} %get-tuple-element.32.refs_1_, bf16[272,256]{1,0:T(8,128)(2,1)S(1)} %collective-permute-done.15.refs_2_, f32[8,128]{1,0:T(8,128)S(1)} %add.19.tile.refs_3_), custom_call_target="tpu_custom_call" | custom-call | flops 1 | bytes 1 | tf_op jit(solution)/shard_map/finish/pallas_call | solution.py:324
  (22 shorter events, 0.9 us)
Async XLA Ops:
  0.6 9.4 %collective-permute-start.1 = (bf16[3,256,256]{2,1,0:T(8,128)(2,1)}, bf16[3,256,256]{2,1,0:T(8,128)(2,1)S(1)}, u32[]{:S(2)}, u32[]{:S(2)}) collective-permute-start(bf16[3,256,256]{2,1,0:T(8,128)(2,1)} %bitcast.10), channel_id=1, source_target_pairs={{0,16},{4,12},{8,24},{12,4},{16,0},{20,28},{24,8},{28,20},{1,17},{... | collective-permute-start | bytes 1179656 | tf_op jit(solution)/shard_map/ppermute | solution.py:20
  3.7 1.2 %copy-start = (bf16[2,1,4,256,256]{4,3,2,1,0:T(8,128)(2,1)S(1)}, bf16[2,1,4,256,256]{4,3,2,1,0:T(8,128)(2,1)}, u32[]{:S(2)}) copy-start(bf16[2,1,4,256,256]{4,3,2,1,0:T(8,128)(2,1)} %param.4) | copy-start | bytes 3145732
  4.9 1.0 %copy-start.1 = (bf16[3,1,256,256]{3,2,1,0:T(8,128)(2,1)S(1)}, bf16[3,1,256,256]{3,2,1,0:T(8,128)(2,1)}, u32[]{:S(2)}) copy-start(bf16[3,1,256,256]{3,2,1,0:T(8,128)(2,1)} %param.5) | copy-start | bytes 1179652
  6.9 8.1 %collective-permute-start.3 = (bf16[3,256,256]{2,1,0:T(8,128)(2,1)}, bf16[3,256,256]{2,1,0:T(8,128)(2,1)S(1)}, u32[]{:S(2)}, u32[]{:S(2)}) collective-permute-start(bf16[3,256,256]{2,1,0:T(8,128)(2,1)} %bitcast.12), channel_id=1, source_target_pairs={{0,8},{4,20},{8,0},{12,28},{16,24},{20,4},{24,16},{28,12},{1,9},{5... | collective-permute-start | bytes 1179656 | tf_op jit(solution)/shard_map/ppermute | solution.py:20
  10.0 9.3 %collective-permute-start.5 = (bf16[3,256,256]{2,1,0:T(8,128)(2,1)S(1)}, bf16[3,256,256]{2,1,0:T(8,128)(2,1)S(1)}, u32[]{:S(2)}, u32[]{:S(2)}) collective-permute-start(bf16[3,256,256]{2,1,0:T(8,128)(2,1)S(1)} %collective-permute-done.1.rest_2_), channel_id=1, source_target_pairs={{0,8},{4,20},{8,0},{12,28},{16,24},{20,4},{24,16},{28,12},{1,9},{5... | collective-permute-start | bytes 1179656 | tf_op jit(solution)/shard_map/ppermute | solution.py:20
  13.6 5.8 %collective-permute-start = (bf16[3,256,256]{2,1,0:T(8,128)(2,1)}, bf16[3,256,256]{2,1,0:T(8,128)(2,1)S(1)}, u32[]{:S(2)}, u32[]{:S(2)}) collective-permute-start(bf16[3,256,256]{2,1,0:T(8,128)(2,1)} %bitcast.13), channel_id=1, source_target_pairs={{0,4},{4,0},{8,12},{12,8},{16,20},{20,16},{24,28},{28,24},{1,5},{5... | collective-permute-start | bytes 1179656 | tf_op jit(solution)/shard_map/ppermute | solution.py:20
  13.6 5.8 %collective-permute-start.2 = (bf16[3,256,256]{2,1,0:T(8,128)(2,1)S(1)}, bf16[3,256,256]{2,1,0:T(8,128)(2,1)S(1)}, u32[]{:S(2)}, u32[]{:S(2)}) collective-permute-start(bf16[3,256,256]{2,1,0:T(8,128)(2,1)S(1)} %collective-permute-done.1.rest_2_), channel_id=1, source_target_pairs={{0,4},{4,0},{8,12},{12,8},{16,20},{20,16},{24,28},{28,24},{1,5},{5... | collective-permute-start | bytes 1179656 | tf_op jit(solution)/shard_map/ppermute | solution.py:20
  14.9 4.4 %collective-permute-start.4 = (bf16[3,256,256]{2,1,0:T(8,128)(2,1)S(1)}, bf16[3,256,256]{2,1,0:T(8,128)(2,1)S(1)}, u32[]{:S(2)}, u32[]{:S(2)}) collective-permute-start(bf16[3,256,256]{2,1,0:T(8,128)(2,1)S(1)} %collective-permute-done.3.rest_4_), channel_id=1, source_target_pairs={{0,4},{4,0},{8,12},{12,8},{16,20},{20,16},{24,28},{28,24},{1,5},{5... | collective-permute-start | bytes 1179656 | tf_op jit(solution)/shard_map/ppermute | solution.py:20
  19.3 1.7 %collective-permute-start.6 = (bf16[3,256,256]{2,1,0:T(8,128)(2,1)S(1)}, bf16[3,256,256]{2,1,0:T(8,128)(2,1)S(1)}, u32[]{:S(2)}, u32[]{:S(2)}) collective-permute-start(bf16[3,256,256]{2,1,0:T(8,128)(2,1)S(1)} %collective-permute-done.5.rest_6_), channel_id=1, source_target_pairs={{0,4},{4,0},{8,12},{12,8},{16,20},{20,16},{24,28},{28,24},{1,5},{5... | collective-permute-start | bytes 1179656 | tf_op jit(solution)/shard_map/ppermute | solution.py:20
  22.8 9.2 %collective-permute-start.7 = (bf16[2,2,2,64,256]{4,3,2,1,0:T(8,128)(2,1)S(1)}, bf16[2,2,2,64,256]{4,3,2,1,0:T(8,128)(2,1)S(1)}, u32[]{:S(2)}, u32[]{:S(2)}) collective-permute-start(bf16[2,2,2,64,256]{4,3,2,1,0:T(8,128)(2,1)S(1)} %get-tuple-element.24), channel_id=1, source_target_pairs={{0,1},{1,0},{2,3},{3,2},{4,5},{5,4},{6,7},{7,6},{8,9},{9,8},{10,11... | collective-permute-start | bytes 786440 | tf_op jit(solution)/shard_map/ppermute | solution.py:20
  25.8 13.9 %collective-permute-start.9 = (bf16[2,2,2,64,256]{4,3,2,1,0:T(8,128)(2,1)S(1)}, bf16[2,2,2,64,256]{4,3,2,1,0:T(8,128)(2,1)S(1)}, u32[]{:S(2)}, u32[]{:S(2)}) collective-permute-start(bf16[2,2,2,64,256]{4,3,2,1,0:T(8,128)(2,1)S(1)} %get-tuple-element.30), channel_id=1, source_target_pairs={{0,1},{1,0},{2,3},{3,2},{4,5},{5,4},{6,7},{7,6},{8,9},{9,8},{10,11... | collective-permute-start | bytes 786440 | tf_op jit(solution)/shard_map/ppermute | solution.py:20
  26.5 1.2 %collective-permute-start.10 = (f32[8,128]{1,0:T(8,128)S(1)}, f32[8,128]{1,0:T(8,128)S(1)}, u32[]{:S(2)}, u32[]{:S(2)}) collective-permute-start(f32[8,128]{1,0:T(8,128)S(1)} %get-tuple-element.31), channel_id=1, source_target_pairs={{0,4},{4,0},{8,12},{12,8},{16,20},{20,16},{24,28},{28,24},{1,5},{5... | collective-permute-start | bytes 12296 | tf_op jit(solution)/shard_map/ppermute | solution.py:20
  27.6 6.9 %collective-permute-start.13 = (f32[8,128]{1,0:T(8,128)S(1)}, f32[8,128]{1,0:T(8,128)S(1)}, u32[]{:S(2)}, u32[]{:S(2)}) collective-permute-start(f32[8,128]{1,0:T(8,128)S(1)} %add.15), channel_id=1, source_target_pairs={{0,24},{4,28},{8,16},{12,20},{16,8},{20,12},{24,0},{28,4},{1,25},{... | collective-permute-start | bytes 12296 | tf_op jit(solution)/shard_map/ppermute | solution.py:20
  30.4 4.2 %collective-permute-start.12 = (f32[8,128]{1,0:T(8,128)S(1)}, f32[8,128]{1,0:T(8,128)S(1)}, u32[]{:S(2)}, u32[]{:S(2)}) collective-permute-start(f32[8,128]{1,0:T(8,128)S(1)} %add.15), channel_id=1, source_target_pairs={{0,16},{4,20},{8,24},{12,28},{16,0},{20,4},{24,8},{28,12},{1,17},{... | collective-permute-start | bytes 12296 | tf_op jit(solution)/shard_map/ppermute | solution.py:20
  31.1 3.6 %collective-permute-start.11 = (f32[8,128]{1,0:T(8,128)S(1)}, f32[8,128]{1,0:T(8,128)S(1)}, u32[]{:S(2)}, u32[]{:S(2)}) collective-permute-start(f32[8,128]{1,0:T(8,128)S(1)} %add.15), channel_id=1, source_target_pairs={{0,8},{4,12},{8,0},{12,4},{16,24},{20,28},{24,16},{28,20},{1,9},{5... | collective-permute-start | bytes 12296 | tf_op jit(solution)/shard_map/ppermute | solution.py:20
  32.0 10.2 %collective-permute-start.8 = (bf16[1,2,2,64,256]{4,3,2,1,0:T(8,128)(2,1)S(1)}, bf16[1,2,2,64,256]{4,3,2,1,0:T(8,128)(2,1)S(1)}, u32[]{:S(2)}, u32[]{:S(2)}) collective-permute-start(bf16[1,2,2,64,256]{4,3,2,1,0:T(8,128)(2,1)S(1)} %get-tuple-element.26), channel_id=1, source_target_pairs={{0,2},{1,3},{2,0},{3,1},{4,6},{5,7},{6,4},{7,5},{8,10},{9,11},{10,... | collective-permute-start | bytes 393224 | tf_op jit(solution)/shard_map/ppermute | solution.py:20
  34.7 5.0 %collective-permute-start.14 = (f32[8,128]{1,0:T(8,128)S(1)}, f32[8,128]{1,0:T(8,128)S(1)}, u32[]{:S(2)}, u32[]{:S(2)}) collective-permute-start(f32[8,128]{1,0:T(8,128)S(1)} %add_add_fusion), channel_id=1, source_target_pairs={{0,1},{1,0},{2,3},{3,2},{4,5},{5,4},{6,7},{7,6},{8,9},{9,8},{10,11... | collective-permute-start | bytes 12296 | tf_op jit(solution)/shard_map/ppermute | solution.py:20
  39.8 8.8 %collective-permute-start.15 = (bf16[272,256]{1,0:T(8,128)(2,1)S(1)}, bf16[272,256]{1,0:T(8,128)(2,1)S(1)}, u32[]{:S(2)}, u32[]{:S(2)}) collective-permute-start(bf16[272,256]{1,0:T(8,128)(2,1)S(1)} %get-tuple-element.33), channel_id=1, source_target_pairs={{0,2},{1,3},{2,0},{3,1},{4,6},{5,7},{6,4},{7,5},{8,10},{9,11},{10,... | collective-permute-start | bytes 417800 | tf_op jit(solution)/shard_map/ppermute | solution.py:20

commit v14 on v13

--- a/solution.py
+++ b/solution.py
@@ -75,47 +75,103 @@
     for mask in range(0, sectors, 2):
         even_place, odd_place = turned(mask, 0, sectors), turned(mask, 1, sectors)
         rights[jnp.where(odd == 1, odd_place, even_place)] = pieces[mask][...]
-        rights[jnp.where(odd == 1, even_place, odd_place) ^ 1] = pieces[mask + 1][...]
-
-
-def sum_kernel(sectors, first, offsets, vectors, inner, before, *rest):
-    if first == 0:
-        *pieces, keep, send, tile, rights, partial = rest
-        place_blocks(sectors, pieces, rights)
-    else:
-        rights, keep, send, tile, partial = rest
+        if mask + 1 < len(pieces):
+            rights[jnp.where(odd == 1, even_place, odd_place) ^ 1] = pieces[mask + 1][...]
+    rights[sectors - 1] = jnp.zeros(rights.shape[1:], rights.dtype)
+
+
+def needed_mask(sectors, offsets, term, pair):
+    sector = lax.axis_index("sec")
+    return sector ^ ((sector + offsets[term, pair]) & (sectors - 1))
+
+
+def times_right(inner, term, pair, block):
     trials, _, states, _ = inner.shape
-    terms = rights.shape[1]
+    lines = inner[:, pair, :, term * states : (term + 1) * states]
+    product = jnp.dot(
+        lines.reshape(trials * states, states), block, preferred_element_type=jnp.float32
+    )
+    return product.reshape(trials, states, states)
+
+
+def sum_terms(sectors, pair, offsets, inner, rights):
+    result = None
+    for term in range(rights.shape[1]):
+        mask = needed_mask(sectors, offsets, term, pair)
+        added = times_right(inner, term, pair, rights[mask, term])
+        result = added if result is None else result + added
+    return result
+
+
+def add_gram(vectors, pair, values, grams):
+    trials, states = vectors.shape[0], vectors.shape[-1]
+    for j in range(trials):
+        for i in range(trials):
+            spread = vectors[i, pair].astype(jnp.float32) * values[j]
+            grams[i * trials + j] += jnp.sum(spread.reshape(-1, 8, states), axis=0)
+
+
+def write_tile(before, grams, tile):
+    count = grams.shape[0]
+    tile[...] = before[...] + place_rows([(k, total(grams[k])) for k in range(count)])
+
+
+def write_shares(whole, slot, keep, send):
     shares = 2 * keep.shape[0]
-    rows = states // shares
-    sector = lax.axis_index("sec")
+    rows = whole.shape[1] // shares
     place = lax.axis_index("term")
-    grams = [jnp.zeros((8, states), jnp.float32) for _ in range(trials * trials)]
-    for local_pair in range(keep.shape[2]):
-        pair = first + local_pair
-        blocks = []
-        for term in range(terms):
-            wanted = (sector + offsets[term, pair]) & (sectors - 1)
-            blocks.append(rights[sector ^ wanted, term])
-        result = jnp.dot(
-            inner[:, pair].reshape(trials * states, terms * states),
-            jnp.concatenate(blocks, axis=0),
-            preferred_element_type=jnp.float32,
-        )
-        partial[...] = result.reshape(trials, states, states)
-        for j in range(trials):
-            product = partial[j]
-            for i in range(trials):
-                spread = vectors[i, pair].astype(jnp.float32) * product
-                grams[i * trials + j] += jnp.sum(spread.reshape(-1, 8, states), axis=0)
-        for mask in range(shares):
-            start = pl.multiple_of((place ^ mask) * rows, rows)
-            share = partial[:, pl.ds(start, rows)]
-            if mask & 1:
-                send[mask // 2, :, local_pair] = share.astype(jnp.bfloat16)
-            else:
-                keep[mask // 2, :, local_pair] = share
-    tile[...] = before[...] + place_rows([(k, total(value)) for k, value in enumerate(grams)])
+    for mask in range(shares):
+        start = pl.multiple_of((place ^ mask) * rows, rows)
+        share = whole[:, pl.ds(start, rows)]
+        if mask & 1:
+            send[mask // 2, :, slot] = share.astype(jnp.bfloat16)
+        else:
+            keep[mask // 2, :, slot] = share
+
+
+def early_kernel(sectors, offsets, vectors, inner, before, *rest):
+    *pieces, partial, tile, rights, grams = rest
+    place_blocks(sectors, pieces, rights)
+    grams[...] = jnp.zeros_like(grams)
+    for pair in range(partial.shape[0]):
+        partial[pair] = sum_terms(sectors, pair, offsets, inner, rights)
+        add_gram(vectors, pair, partial[pair], grams)
+    write_tile(before, grams, tile)
+
+
+def late_kernel(sectors, offsets, vectors, inner, before, partial, last, *rest):
+    keep, send, tile, whole, grams = rest
+    grams[...] = jnp.zeros_like(grams)
+    for pair in range(partial.shape[0]):
+        whole[...] = partial[pair]
+        for term in range(last.shape[0]):
+
+            @pl.when(needed_mask(sectors, offsets, term, pair) == sectors - 1)
+            def _():
+                added = times_right(inner, term, pair, last[term])
+                whole[...] += added
+                add_gram(vectors, pair, added, grams)
+
+        write_shares(whole, pair, keep, send)
+    write_tile(before, grams, tile)
+
+
+def second_kernel(sectors, first, offsets, vectors, inner, before, rights, last, *rest):
+    keep, send, tile, whole, grams = rest
+    grams[...] = jnp.zeros_like(grams)
+    for slot in range(keep.shape[2]):
+        pair = first + slot
+        whole[slot] = sum_terms(sectors, pair, offsets, inner, rights)
+        for term in range(last.shape[0]):
+
+            @pl.when(needed_mask(sectors, offsets, term, pair) == sectors - 1)
+            def _():
+                whole[slot] += times_right(inner, term, pair, last[term])
+
+    for slot in range(keep.shape[2]):
+        add_gram(vectors, first + slot, whole[slot], grams)
+        write_shares(whole.at[slot], slot, keep, send)
+    write_tile(before, grams, tile)
 
 
 def halve_last_kernel(kept, received, tile, keep, send):
@@ -244,32 +300,70 @@
     def share_of(count, size, dtype):
         return jax.ShapeDtypeStruct((count, trials, size, rows, states), dtype)
 
-    rights_shape = (sectors, terms, states, states)
+    tile_shape = jax.ShapeDtypeStruct(TILE, jnp.float32)
+    rights_shape = jax.ShapeDtypeStruct((sectors, terms, states, states), jnp.bfloat16)
     sizes = [pairs // 2, pairs - pairs // 2]
-    sums, rights, first = [], None, 0
-    for size in sizes:
-        outs = [
-            share_of(shares // 2, size, jnp.float32),
-            share_of(shares // 2, size, jnp.bfloat16),
-            jax.ShapeDtypeStruct(TILE, jnp.float32),
-        ]
-        blocks = gathered if first == 0 else [rights]
-        if first == 0:
-            outs.append(jax.ShapeDtypeStruct(rights_shape, jnp.bfloat16))
-        keep, send, tile, *placed = call(
-            functools.partial(sum_kernel, sectors, first),
-            "sum_over_terms",
-            2 * terms * trials * size * states**3,
-            4 * MIB,
+    grams = pltpu.VMEM((trials * trials, 8, states), jnp.float32)
+    *early, last = gathered
+    partial, tile, rights = call(
+        functools.partial(early_kernel, sectors),
+        "early_products",
+        2 * terms * trials * sizes[0] * states**3,
+        4 * MIB,
+        12 * MIB,
+        out_shape=(
+            jax.ShapeDtypeStruct((sizes[0], trials, states, states), jnp.float32),
+            tile_shape,
+            rights_shape,
+        ),
+        in_specs=[SMEM, VMEM, VMEM, VMEM] + [VMEM] * len(early),
+        out_specs=(VMEM, VMEM, VMEM),
+        scratch_shapes=[grams],
+    )(in_hbm(offsets), vectors, inner, tile, *early)
+
+    def sums_of(kernel, name, flops, size, scratch, *operands):
+        return call(
+            kernel,
+            name,
+            flops,
+            MIB,
             12 * MIB,
-            out_shape=outs,
-            in_specs=[SMEM, VMEM, VMEM, VMEM] + [VMEM] * len(blocks),
-            out_specs=[VMEM] * len(outs),
-            scratch_shapes=[pltpu.VMEM((trials, states, states), jnp.float32)],
-        )(in_hbm(offsets), vectors, inner, tile, *blocks)
-        rights = placed[0] if placed else rights
-        first += size
-        sums.append((keep, swap(send, "term", 1)))
+            out_shape=(
+                share_of(shares // 2, size, jnp.float32),
+                share_of(shares // 2, size, jnp.bfloat16),
+                tile_shape,
+            ),
+            in_specs=[SMEM] + [VMEM] * len(operands),
+            out_specs=(VMEM, VMEM, VMEM),
+            scratch_shapes=[pltpu.VMEM((*scratch, states, states), jnp.float32), grams],
+        )(in_hbm(offsets), *operands)
+
+    keep, send, tile = sums_of(
+        functools.partial(late_kernel, sectors),
+        "late_products",
+        terms * trials * sizes[0] * states**3 // 4,
+        sizes[0],
+        (trials,),
+        vectors,
+        inner,
+        tile,
+        partial,
+        last,
+    )
+    sums = [(keep, swap(send, "term", 1))]
+    keep, send, tile = sums_of(
+        functools.partial(second_kernel, sectors, sizes[0]),
+        "second_products",
+        2 * terms * trials * sizes[1] * states**3,
+        sizes[1],
+        (sizes[1], trials),
+        vectors,
+        inner,
+        tile,
+        rights,
+        last,
+    )
+    sums.append((keep, swap(send, "term", 1)))
 
     for masks in [[1]] + steps_of(sectors, 1):
         tile = add_places(tile, "sec", masks)

time: 49.6 us -> 49.9 us (level)
  Pallas kernels: 5.24 us -> 6.86 us
  waiting for transfers between devices: 20.5 us -> 19.5 us
    pallas_call x2 -> x3, Pallas kernels: 3.34 us -> 4.97 us  [the longest x2 3.36 us: sums_of(): call(kernel, name, flops, MIB, 12 * MIB, out_shape=(share_of(shares // 2,...]
    ppermute x16, waiting for transfers between devices: 20.5 us -> 19.5 us  [swap(): lax.ppermute(value, axis, [(place, place ^ masks[place & 1]) for place in...]
  transfers between devices with their start and end apart: 16 -> 16, of which waited for: 9 -> 8; matrix products, arithmetic and copies ran while one was open for 0% -> 0% of each run, Pallas kernels for 6% -> 10%
where the time goes in v14:
time: 49.9 us; the launch traced here: 50 us
  starting transfers between devices  20.7 us (41%)
  waiting for transfers between devices  19.5 us (39%)
  Pallas kernels  6.86 us (14%)
  local copies, waits for them, and re-layouts  2.22 us (4%)
  between operations  0.69 us (1%)
    ppermute x16, starting transfers between devices, swap(): lax.ppermute(value, axis, [(place, place ^ masks[place & 1]) for place in...  20.7 us
    ppermute x16, waiting for transfers between devices, swap(): lax.ppermute(value, axis, [(place, place ^ masks[place & 1]) for place in...  19.5 us
    pallas_call x2, Pallas kernels, sums_of(): call(kernel, name, flops, MIB, 12 * MIB, out_shape=(share_of(shares // 2,...  3.36 us
    unnamed x4, local copies, waits for them, and re-layouts  2.22 us
    pallas_call x1, Pallas kernels, local(): call(functools.partial(early_kernel, sectors), 'early_products', 2 * term...  1.62 us
    pallas_call x1, Pallas kernels, local(): call(functools.partial(inner_kernel, 1.0 / shares), 'inner_products', 2 *...  1 us
  transfers between devices with their start and end apart: 16, of which 8 were waited for; matrix products, arithmetic and copies ran while one was open for 0% of the time, Pallas kernels for 10%

profile of v14, /device:TPU:0, one launch (start us, length us, event | category | flops | bytes accessed | tf_op | source)
XLA Modules:
  0.0 50.0 jit_solution(1503499471860467724)
XLA Ops:
  0.6 3.0 %collective-permute-start.1 = (bf16[3,256,256]{2,1,0:T(8,128)(2,1)}, bf16[3,256,256]{2,1,0:T(8,128)(2,1)S(1)}, u32[]{:S(2)}, u32[]{:S(2)}) collective-permute-start(bf16[3,256,256]{2,1,0:T(8,128)(2,1)} %bitcast.11), channel_id=1, source_target_pairs={{0,16},{4,12},{8,24},{12,4},{16,0},{20,28},{24,8},{28,20},{1,17},{... | collective-permute-start | bytes 1179656 | tf_op jit(solution)/shard_map/ppermute | solution.py:20
  3.7 1.2 %copy-done = bf16[2,1,4,256,256]{4,3,2,1,0:T(8,128)(2,1)S(1)} copy-done((bf16[2,1,4,256,256]{4,3,2,1,0:T(8,128)(2,1)S(1)}, bf16[2,1,4,256,256]{4,3,2,1,0:T(8,128)(2,1)}, u32[]{:S(2)}) %copy-start) | copy-done | bytes 1048600
  4.9 1.0 %copy-done.1 = bf16[3,1,256,256]{3,2,1,0:T(8,128)(2,1)S(1)} copy-done((bf16[3,1,256,256]{3,2,1,0:T(8,128)(2,1)S(1)}, bf16[3,1,256,256]{3,2,1,0:T(8,128)(2,1)}, u32[]{:S(2)}) %copy-start.1) | copy-done | bytes 393240
  5.9 1.0 %inner_products.1 = (bf16[2,4,256,768]{3,2,1,0:T(8,128)(2,1)S(1)}, f32[8,128]{1,0:T(8,128)S(1)}, bf16[3,256,256]{2,1,0:T(8,128)(2,1)S(1)}) custom-call(bf16[2,4,256,256]{3,2,1,0:T(8,128)(2,1)S(1)} %bitcast.6, bf16[3,256,256]{2,1,0:T(8,128)(2,1)S(1)} %bitcast.10, bf16[3,256,256]{2,1,0:T(8,128)(2,1)} %bitcast.12), custom_call_target="tpu_custom_call" | custom-call | flops 805306368 | bytes 5242880 | tf_op jit(solution)/shard_map/inner_products/pallas_call | solution.py:278
  6.9 1.6 %collective-permute-start.3 = (bf16[3,256,256]{2,1,0:T(8,128)(2,1)}, bf16[3,256,256]{2,1,0:T(8,128)(2,1)S(1)}, u32[]{:S(2)}, u32[]{:S(2)}) collective-permute-start(bf16[3,256,256]{2,1,0:T(8,128)(2,1)} %bitcast.13), channel_id=1, source_target_pairs={{0,8},{4,20},{8,0},{12,28},{16,24},{20,4},{24,16},{28,12},{1,9},{5... | collective-permute-start | bytes 1179656 | tf_op jit(solution)/shard_map/ppermute | solution.py:20
  8.5 1.6 %collective-permute-done.1.rest_2_ = bf16[3,256,256]{2,1,0:T(8,128)(2,1)S(1)} collective-permute-done((bf16[3,256,256]{2,1,0:T(8,128)(2,1)}, bf16[3,256,256]{2,1,0:T(8,128)(2,1)S(1)}, u32[]{:S(2)}, u32[]{:S(2)}) %collective-permute-start.1) | collective-permute-done | bytes 393248 | tf_op jit(solution)/shard_map/ppermute | solution.py:20
  10.0 3.5 %collective-permute-start.5 = (bf16[3,256,256]{2,1,0:T(8,128)(2,1)S(1)}, bf16[3,256,256]{2,1,0:T(8,128)(2,1)S(1)}, u32[]{:S(2)}, u32[]{:S(2)}) collective-permute-start(bf16[3,256,256]{2,1,0:T(8,128)(2,1)S(1)} %collective-permute-done.1.rest_2_), channel_id=1, source_target_pairs={{0,8},{4,20},{8,0},{12,28},{16,24},{20,4},{24,16},{28,12},{1,9},{5... | collective-permute-start | bytes 1179656 | tf_op jit(solution)/shard_map/ppermute | solution.py:20
  13.6 1.4 %collective-permute-done.3.rest_4_ = bf16[3,256,256]{2,1,0:T(8,128)(2,1)S(1)} collective-permute-done((bf16[3,256,256]{2,1,0:T(8,128)(2,1)}, bf16[3,256,256]{2,1,0:T(8,128)(2,1)S(1)}, u32[]{:S(2)}, u32[]{:S(2)}) %collective-permute-start.3) | collective-permute-done | bytes 393248 | tf_op jit(solution)/shard_map/ppermute | solution.py:20
  15.0 0.5 %collective-permute-start.2 = (bf16[3,256,256]{2,1,0:T(8,128)(2,1)S(1)}, bf16[3,256,256]{2,1,0:T(8,128)(2,1)S(1)}, u32[]{:S(2)}, u32[]{:S(2)}) collective-permute-start(bf16[3,256,256]{2,1,0:T(8,128)(2,1)S(1)} %collective-permute-done.1.rest_2_), channel_id=1, source_target_pairs={{0,4},{4,0},{8,12},{12,8},{16,20},{20,16},{24,28},{28,24},{1,5},{5... | collective-permute-start | bytes 1179656 | tf_op jit(solution)/shard_map/ppermute | solution.py:20
  15.5 3.9 %collective-permute-done.5.rest_6_ = bf16[3,256,256]{2,1,0:T(8,128)(2,1)S(1)} collective-permute-done((bf16[3,256,256]{2,1,0:T(8,128)(2,1)S(1)}, bf16[3,256,256]{2,1,0:T(8,128)(2,1)S(1)}, u32[]{:S(2)}, u32[]{:S(2)}) %collective-permute-start.5) | collective-permute-done | bytes 393248 | tf_op jit(solution)/shard_map/ppermute | solution.py:20
  19.3 1.6 %early_products.1 = (f32[2,2,256,256]{3,2,1,0:T(8,128)S(1)}, f32[8,128]{1,0:T(8,128)S(1)}, bf16[8,3,256,256]{3,2,1,0:T(8,128)(2,1)S(1)}) custom-call(s32[3,4]{1,0:T(4,128)} %offsets.5, bf16[2,4,256,256]{3,2,1,0:T(8,128)(2,1)S(1)} %bitcast.7, bf16[2,4,256,768]{3,2,1,0:T(8,128)(2,1)S(1)} %get-tuple-element.21.inner, f32[8,128]{1,0:T(8,128)S(1)} %get-tuple-element.22.before, ...), custom_call_target="tpu_custom_call" | custom-call | flops 402653184 | bytes 4194304 | tf_op jit(solution)/shard_map/early_products/pallas_call | solution.py:308
  21.0 0.9 %late_products.1 = (f32[2,2,2,64,256]{4,3,2,1,0:T(8,128)S(1)}, bf16[2,2,2,64,256]{4,3,2,1,0:T(8,128)(2,1)S(1)}, f32[8,128]{1,0:T(8,128)S(1)}) custom-call(s32[3,4]{1,0:T(4,128)} %offsets.5, bf16[2,4,256,256]{3,2,1,0:T(8,128)(2,1)S(1)} %bitcast.8, bf16[2,4,256,768]{3,2,1,0:T(8,128)(2,1)S(1)} %get-tuple-element.21.inner, ...), custom_call_target="tpu_custom_call" | custom-call | flops 50331648 | bytes 1048576 | tf_op jit(solution)/shard_map/late_products/pallas_call | solution.py:325
  22.0 1.4 %collective-permute-start.7 = (bf16[2,2,2,64,256]{4,3,2,1,0:T(8,128)(2,1)S(1)}, bf16[2,2,2,64,256]{4,3,2,1,0:T(8,128)(2,1)S(1)}, u32[]{:S(2)}, u32[]{:S(2)}) collective-permute-start(bf16[2,2,2,64,256]{4,3,2,1,0:T(8,128)(2,1)S(1)} %get-tuple-element.28), channel_id=1, source_target_pairs={{0,1},{1,0},{2,3},{3,2},{4,5},{5,4},{6,7},{7,6},{8,9},{9,8},{10,11... | collective-permute-start | bytes 786440 | tf_op jit(solution)/shard_map/ppermute | solution.py:20
  23.4 2.4 %second_products.1 = (f32[2,2,2,64,256]{4,3,2,1,0:T(8,128)S(1)}, bf16[2,2,2,64,256]{4,3,2,1,0:T(8,128)(2,1)S(1)}, f32[8,128]{1,0:T(8,128)S(1)}) custom-call(s32[3,4]{1,0:T(4,128)} %offsets.5, bf16[2,4,256,256]{3,2,1,0:T(8,128)(2,1)S(1)} %bitcast.9, bf16[2,4,256,768]{3,2,1,0:T(8,128)(2,1)S(1)} %get-tuple-element.21.inner, ...), custom_call_target="tpu_custom_call" | custom-call | flops 402653184 | bytes 1048576 | tf_op jit(solution)/shard_map/second_products/pallas_call | solution.py:325
  26.3 0.9 %collective-permute-done.10 = f32[8,128]{1,0:T(8,128)S(1)} collective-permute-done((f32[8,128]{1,0:T(8,128)S(1)}, f32[8,128]{1,0:T(8,128)S(1)}, u32[]{:S(2)}, u32[]{:S(2)}) %collective-permute-start.10) | collective-permute-done | bytes 4128 | tf_op jit(solution)/shard_map/ppermute | solution.py:20
  27.1 2.7 %collective-permute-start.11 = (f32[8,128]{1,0:T(8,128)S(1)}, f32[8,128]{1,0:T(8,128)S(1)}, u32[]{:S(2)}, u32[]{:S(2)}) collective-permute-start(f32[8,128]{1,0:T(8,128)S(1)} %add.15), channel_id=1, source_target_pairs={{0,8},{4,12},{8,0},{12,4},{16,24},{20,28},{24,16},{28,20},{1,9},{5... | collective-permute-start | bytes 12296 | tf_op jit(solution)/shard_map/ppermute | solution.py:20
  29.8 1.3 %collective-permute-start.12 = (f32[8,128]{1,0:T(8,128)S(1)}, f32[8,128]{1,0:T(8,128)S(1)}, u32[]{:S(2)}, u32[]{:S(2)}) collective-permute-start(f32[8,128]{1,0:T(8,128)S(1)} %add.15), channel_id=1, source_target_pairs={{0,16},{4,20},{8,24},{12,28},{16,0},{20,4},{24,8},{28,12},{1,17},{... | collective-permute-start | bytes 12296 | tf_op jit(solution)/shard_map/ppermute | solution.py:20
  31.4 2.5 %collective-permute-start.8 = (bf16[1,2,2,64,256]{4,3,2,1,0:T(8,128)(2,1)S(1)}, bf16[1,2,2,64,256]{4,3,2,1,0:T(8,128)(2,1)S(1)}, u32[]{:S(2)}, u32[]{:S(2)}) collective-permute-start(bf16[1,2,2,64,256]{4,3,2,1,0:T(8,128)(2,1)S(1)} %get-tuple-element.30), channel_id=1, source_target_pairs={{0,2},{1,3},{2,0},{3,1},{4,6},{5,7},{6,4},{7,5},{8,10},{9,11},{10,... | collective-permute-start | bytes 393224 | tf_op jit(solution)/shard_map/ppermute | solution.py:20
  33.9 1.8 %collective-permute-done.13 = f32[8,128]{1,0:T(8,128)S(1)} collective-permute-done((f32[8,128]{1,0:T(8,128)S(1)}, f32[8,128]{1,0:T(8,128)S(1)}, u32[]{:S(2)}, u32[]{:S(2)}) %collective-permute-start.13) | collective-permute-done | bytes 4128 | tf_op jit(solution)/shard_map/ppermute | solution.py:20
  35.6 1.1 %collective-permute-start.14 = (f32[8,128]{1,0:T(8,128)S(1)}, f32[8,128]{1,0:T(8,128)S(1)}, u32[]{:S(2)}, u32[]{:S(2)}) collective-permute-start(f32[8,128]{1,0:T(8,128)S(1)} %add_add_fusion), channel_id=1, source_target_pairs={{0,1},{1,0},{2,3},{3,2},{4,5},{5,4},{6,7},{7,6},{8,9},{9,8},{10,11... | collective-permute-start | bytes 12296 | tf_op jit(solution)/shard_map/ppermute | solution.py:20
  36.8 2.9 %collective-permute-done.14 = f32[8,128]{1,0:T(8,128)S(1)} collective-permute-done((f32[8,128]{1,0:T(8,128)S(1)}, f32[8,128]{1,0:T(8,128)S(1)}, u32[]{:S(2)}, u32[]{:S(2)}) %collective-permute-start.14) | collective-permute-done | bytes 4128 | tf_op jit(solution)/shard_map/ppermute | solution.py:20
  39.7 2.4 %collective-permute-start.15 = (bf16[272,256]{1,0:T(8,128)(2,1)S(1)}, bf16[272,256]{1,0:T(8,128)(2,1)S(1)}, u32[]{:S(2)}, u32[]{:S(2)}) collective-permute-start(bf16[272,256]{1,0:T(8,128)(2,1)S(1)} %get-tuple-element.37), channel_id=1, source_target_pairs={{0,2},{1,3},{2,0},{3,1},{4,6},{5,7},{6,4},{7,5},{8,10},{9,11},{10,... | collective-permute-start | bytes 417800 | tf_op jit(solution)/shard_map/ppermute | solution.py:20
  42.2 7.1 %collective-permute-done.15.refs_2_ = bf16[272,256]{1,0:T(8,128)(2,1)S(1)} collective-permute-done((bf16[272,256]{1,0:T(8,128)(2,1)S(1)}, bf16[272,256]{1,0:T(8,128)(2,1)S(1)}, u32[]{:S(2)}, u32[]{:S(2)}) %collective-permute-start.15) | collective-permute-done | bytes 139296 | tf_op jit(solution)/shard_map/ppermute | solution.py:20
  49.3 0.7 %finish.1 = (bf16[2,4,64,256]{3,2,1,0:T(8,128)(2,1)}, f32[2,2]{1,0:T(2,128)}) custom-call(bf16[2,2,64,256]{3,2,1,0:T(8,128)(2,1)S(1)} %add_last_share.1.refs_0_, f32[1,2,2,64,256]{4,3,2,1,0:T(8,128)S(1)} %get-tuple-element.36.refs_1_, bf16[272,256]{1,0:T(8,128)(2,1)S(1)} %collective-permute-done.15.refs_2_, f32[8,128]{1,0:T(8,128)S(1)} %add.19.tile.refs_3_), custom_call_target="tpu_custom_call" | custom-call | flops 1 | bytes 1 | tf_op jit(solution)/shard_map/finish/pallas_call | solution.py:418
  (23 shorter events, 0.8 us)
Async XLA Ops:
  0.6 9.4 %collective-permute-start.1 = (bf16[3,256,256]{2,1,0:T(8,128)(2,1)}, bf16[3,256,256]{2,1,0:T(8,128)(2,1)S(1)}, u32[]{:S(2)}, u32[]{:S(2)}) collective-permute-start(bf16[3,256,256]{2,1,0:T(8,128)(2,1)} %bitcast.11), channel_id=1, source_target_pairs={{0,16},{4,12},{8,24},{12,4},{16,0},{20,28},{24,8},{28,20},{1,17},{... | collective-permute-start | bytes 1179656 | tf_op jit(solution)/shard_map/ppermute | solution.py:20
  3.7 1.2 %copy-start = (bf16[2,1,4,256,256]{4,3,2,1,0:T(8,128)(2,1)S(1)}, bf16[2,1,4,256,256]{4,3,2,1,0:T(8,128)(2,1)}, u32[]{:S(2)}) copy-start(bf16[2,1,4,256,256]{4,3,2,1,0:T(8,128)(2,1)} %param.4) | copy-start | bytes 3145732
  4.9 1.0 %copy-start.1 = (bf16[3,1,256,256]{3,2,1,0:T(8,128)(2,1)S(1)}, bf16[3,1,256,256]{3,2,1,0:T(8,128)(2,1)}, u32[]{:S(2)}) copy-start(bf16[3,1,256,256]{3,2,1,0:T(8,128)(2,1)} %param.5) | copy-start | bytes 1179652
  6.9 8.1 %collective-permute-start.3 = (bf16[3,256,256]{2,1,0:T(8,128)(2,1)}, bf16[3,256,256]{2,1,0:T(8,128)(2,1)S(1)}, u32[]{:S(2)}, u32[]{:S(2)}) collective-permute-start(bf16[3,256,256]{2,1,0:T(8,128)(2,1)} %bitcast.13), channel_id=1, source_target_pairs={{0,8},{4,20},{8,0},{12,28},{16,24},{20,4},{24,16},{28,12},{1,9},{5... | collective-permute-start | bytes 1179656 | tf_op jit(solution)/shard_map/ppermute | solution.py:20
  10.0 9.3 %collective-permute-start.5 = (bf16[3,256,256]{2,1,0:T(8,128)(2,1)S(1)}, bf16[3,256,256]{2,1,0:T(8,128)(2,1)S(1)}, u32[]{:S(2)}, u32[]{:S(2)}) collective-permute-start(bf16[3,256,256]{2,1,0:T(8,128)(2,1)S(1)} %collective-permute-done.1.rest_2_), channel_id=1, source_target_pairs={{0,8},{4,20},{8,0},{12,28},{16,24},{20,4},{24,16},{28,12},{1,9},{5... | collective-permute-start | bytes 1179656 | tf_op jit(solution)/shard_map/ppermute | solution.py:20
  13.6 5.8 %collective-permute-start = (bf16[3,256,256]{2,1,0:T(8,128)(2,1)}, bf16[3,256,256]{2,1,0:T(8,128)(2,1)S(1)}, u32[]{:S(2)}, u32[]{:S(2)}) collective-permute-start(bf16[3,256,256]{2,1,0:T(8,128)(2,1)} %bitcast.14), channel_id=1, source_target_pairs={{0,4},{4,0},{8,12},{12,8},{16,20},{20,16},{24,28},{28,24},{1,5},{5... | collective-permute-start | bytes 1179656 | tf_op jit(solution)/shard_map/ppermute | solution.py:20
  14.9 4.4 %collective-permute-start.4 = (bf16[3,256,256]{2,1,0:T(8,128)(2,1)S(1)}, bf16[3,256,256]{2,1,0:T(8,128)(2,1)S(1)}, u32[]{:S(2)}, u32[]{:S(2)}) collective-permute-start(bf16[3,256,256]{2,1,0:T(8,128)(2,1)S(1)} %collective-permute-done.3.rest_4_), channel_id=1, source_target_pairs={{0,4},{4,0},{8,12},{12,8},{16,20},{20,16},{24,28},{28,24},{1,5},{5... | collective-permute-start | bytes 1179656 | tf_op jit(solution)/shard_map/ppermute | solution.py:20
  15.0 4.4 %collective-permute-start.2 = (bf16[3,256,256]{2,1,0:T(8,128)(2,1)S(1)}, bf16[3,256,256]{2,1,0:T(8,128)(2,1)S(1)}, u32[]{:S(2)}, u32[]{:S(2)}) collective-permute-start(bf16[3,256,256]{2,1,0:T(8,128)(2,1)S(1)} %collective-permute-done.1.rest_2_), channel_id=1, source_target_pairs={{0,4},{4,0},{8,12},{12,8},{16,20},{20,16},{24,28},{28,24},{1,5},{5... | collective-permute-start | bytes 1179656 | tf_op jit(solution)/shard_map/ppermute | solution.py:20
  19.3 1.7 %collective-permute-start.6 = (bf16[3,256,256]{2,1,0:T(8,128)(2,1)S(1)}, bf16[3,256,256]{2,1,0:T(8,128)(2,1)S(1)}, u32[]{:S(2)}, u32[]{:S(2)}) collective-permute-start(bf16[3,256,256]{2,1,0:T(8,128)(2,1)S(1)} %collective-permute-done.5.rest_6_), channel_id=1, source_target_pairs={{0,4},{4,0},{8,12},{12,8},{16,20},{20,16},{24,28},{28,24},{1,5},{5... | collective-permute-start | bytes 1179656 | tf_op jit(solution)/shard_map/ppermute | solution.py:20
  22.0 9.3 %collective-permute-start.7 = (bf16[2,2,2,64,256]{4,3,2,1,0:T(8,128)(2,1)S(1)}, bf16[2,2,2,64,256]{4,3,2,1,0:T(8,128)(2,1)S(1)}, u32[]{:S(2)}, u32[]{:S(2)}) collective-permute-start(bf16[2,2,2,64,256]{4,3,2,1,0:T(8,128)(2,1)S(1)} %get-tuple-element.28), channel_id=1, source_target_pairs={{0,1},{1,0},{2,3},{3,2},{4,5},{5,4},{6,7},{7,6},{8,9},{9,8},{10,11... | collective-permute-start | bytes 786440 | tf_op jit(solution)/shard_map/ppermute | solution.py:20
  25.8 13.8 %collective-permute-start.9 = (bf16[2,2,2,64,256]{4,3,2,1,0:T(8,128)(2,1)S(1)}, bf16[2,2,2,64,256]{4,3,2,1,0:T(8,128)(2,1)S(1)}, u32[]{:S(2)}, u32[]{:S(2)}) collective-permute-start(bf16[2,2,2,64,256]{4,3,2,1,0:T(8,128)(2,1)S(1)} %get-tuple-element.34), channel_id=1, source_target_pairs={{0,1},{1,0},{2,3},{3,2},{4,5},{5,4},{6,7},{7,6},{8,9},{9,8},{10,11... | collective-permute-start | bytes 786440 | tf_op jit(solution)/shard_map/ppermute | solution.py:20
  25.9 1.2 %collective-permute-start.10 = (f32[8,128]{1,0:T(8,128)S(1)}, f32[8,128]{1,0:T(8,128)S(1)}, u32[]{:S(2)}, u32[]{:S(2)}) collective-permute-start(f32[8,128]{1,0:T(8,128)S(1)} %get-tuple-element.35), channel_id=1, source_target_pairs={{0,4},{4,0},{8,12},{12,8},{16,20},{20,16},{24,28},{28,24},{1,5},{5... | collective-permute-start | bytes 12296 | tf_op jit(solution)/shard_map/ppermute | solution.py:20
  27.1 6.7 %collective-permute-start.11 = (f32[8,128]{1,0:T(8,128)S(1)}, f32[8,128]{1,0:T(8,128)S(1)}, u32[]{:S(2)}, u32[]{:S(2)}) collective-permute-start(f32[8,128]{1,0:T(8,128)S(1)} %add.15), channel_id=1, source_target_pairs={{0,8},{4,12},{8,0},{12,4},{16,24},{20,28},{24,16},{28,20},{1,9},{5... | collective-permute-start | bytes 12296 | tf_op jit(solution)/shard_map/ppermute | solution.py:20
  29.8 4.0 %collective-permute-start.12 = (f32[8,128]{1,0:T(8,128)S(1)}, f32[8,128]{1,0:T(8,128)S(1)}, u32[]{:S(2)}, u32[]{:S(2)}) collective-permute-start(f32[8,128]{1,0:T(8,128)S(1)} %add.15), channel_id=1, source_target_pairs={{0,16},{4,20},{8,24},{12,28},{16,0},{20,4},{24,8},{28,12},{1,17},{... | collective-permute-start | bytes 12296 | tf_op jit(solution)/shard_map/ppermute | solution.py:20
  31.1 4.5 %collective-permute-start.13 = (f32[8,128]{1,0:T(8,128)S(1)}, f32[8,128]{1,0:T(8,128)S(1)}, u32[]{:S(2)}, u32[]{:S(2)}) collective-permute-start(f32[8,128]{1,0:T(8,128)S(1)} %add.15), channel_id=1, source_target_pairs={{0,24},{4,28},{8,16},{12,20},{16,8},{20,12},{24,0},{28,4},{1,25},{... | collective-permute-start | bytes 12296 | tf_op jit(solution)/shard_map/ppermute | solution.py:20
  31.4 10.8 %collective-permute-start.8 = (bf16[1,2,2,64,256]{4,3,2,1,0:T(8,128)(2,1)S(1)}, bf16[1,2,2,64,256]{4,3,2,1,0:T(8,128)(2,1)S(1)}, u32[]{:S(2)}, u32[]{:S(2)}) collective-permute-start(bf16[1,2,2,64,256]{4,3,2,1,0:T(8,128)(2,1)S(1)} %get-tuple-element.30), channel_id=1, source_target_pairs={{0,2},{1,3},{2,0},{3,1},{4,6},{5,7},{6,4},{7,5},{8,10},{9,11},{10,... | collective-permute-start | bytes 393224 | tf_op jit(solution)/shard_map/ppermute | solution.py:20
  35.6 4.0 %collective-permute-start.14 = (f32[8,128]{1,0:T(8,128)S(1)}, f32[8,128]{1,0:T(8,128)S(1)}, u32[]{:S(2)}, u32[]{:S(2)}) collective-permute-start(f32[8,128]{1,0:T(8,128)S(1)} %add_add_fusion), channel_id=1, source_target_pairs={{0,1},{1,0},{2,3},{3,2},{4,5},{5,4},{6,7},{7,6},{8,9},{9,8},{10,11... | collective-permute-start | bytes 12296 | tf_op jit(solution)/shard_map/ppermute | solution.py:20
  39.7 9.6 %collective-permute-start.15 = (bf16[272,256]{1,0:T(8,128)(2,1)S(1)}, bf16[272,256]{1,0:T(8,128)(2,1)S(1)}, u32[]{:S(2)}, u32[]{:S(2)}) collective-permute-start(bf16[272,256]{1,0:T(8,128)(2,1)S(1)} %get-tuple-element.37), channel_id=1, source_target_pairs={{0,2},{1,3},{2,0},{3,1},{4,6},{5,7},{6,4},{7,5},{8,10},{9,11},{10,... | collective-permute-start | bytes 417800 | tf_op jit(solution)/shard_map/ppermute | solution.py:20

commit v15 on v14

--- a/solution.py
+++ b/solution.py
@@ -116,17 +116,25 @@
     tile[...] = before[...] + place_rows([(k, total(grams[k])) for k in range(count)])
 
 
-def write_shares(whole, slot, keep, send):
+def share_masks(shares, backwards):
+    bits = shares.bit_length() - 1
+    places = range(bits)
+    if backwards:
+        return [sum((k >> bit & 1) << (bits - 1 - bit) for bit in places) for k in range(shares)]
+    return list(range(shares))
+
+
+def write_shares(whole, backwards, slot, keep, send):
     shares = 2 * keep.shape[0]
     rows = whole.shape[1] // shares
     place = lax.axis_index("term")
-    for mask in range(shares):
+    for k, mask in enumerate(share_masks(shares, backwards)):
         start = pl.multiple_of((place ^ mask) * rows, rows)
         share = whole[:, pl.ds(start, rows)]
-        if mask & 1:
-            send[mask // 2, :, slot] = share.astype(jnp.bfloat16)
+        if k & 1:
+            send[k // 2, :, slot] = share.astype(jnp.bfloat16)
         else:
-            keep[mask // 2, :, slot] = share
+            keep[k // 2, :, slot] = share
 
 
 def early_kernel(sectors, offsets, vectors, inner, before, *rest):
@@ -152,7 +160,7 @@
                 whole[...] += added
                 add_gram(vectors, pair, added, grams)
 
-        write_shares(whole, pair, keep, send)
+        write_shares(whole, False, pair, keep, send)
     write_tile(before, grams, tile)
 
 
@@ -170,7 +178,7 @@
 
     for slot in range(keep.shape[2]):
         add_gram(vectors, first + slot, whole[slot], grams)
-        write_shares(whole.at[slot], slot, keep, send)
+        write_shares(whole.at[slot], True, slot, keep, send)
     write_tile(before, grams, tile)
 
 
@@ -208,19 +216,21 @@
     return block[:height, :width] + block[height:, :width] + block[:height, width:]
 
 
-def add_last_kernel(kept, received, result):
-    result[...] = (kept[0] + received[0].astype(jnp.float32)).astype(jnp.bfloat16)
-
-
-def finish_kernel(*refs):
-    *done, kept, received, tile, products, rayleigh = refs
-    first = 0
-    for part in done:
-        products[:, first : first + part.shape[1]] = part[...]
-        first += part.shape[1]
+def last_rows(kept, received):
     lines = received.shape[0] - 2 * TILE[0]
     both = received[:lines].astype(jnp.float32).reshape(kept.shape[1:])
-    products[:, first:] = (kept[0] + both).astype(jnp.bfloat16)
+    return (kept[0] + both).astype(jnp.bfloat16)
+
+
+def add_last_kernel(kept, received, tile, corner, rows, sums):
+    rows[...] = last_rows(kept, received)
+    sums[...] = tile[...] + ridden_tile(received) + corner[...]
+
+
+def finish_kernel(kept, received, rows, tile, products, rayleigh):
+    first = kept.shape[2]
+    products[:, :first] = last_rows(kept, received)
+    products[:, first:] = rows[...]
 
     tile = tile[...] + ridden_tile(received)
     trials = rayleigh.shape[0]
@@ -302,7 +312,7 @@
 
     tile_shape = jax.ShapeDtypeStruct(TILE, jnp.float32)
     rights_shape = jax.ShapeDtypeStruct((sectors, terms, states, states), jnp.bfloat16)
-    sizes = [pairs // 2, pairs - pairs // 2]
+    sizes = [pairs - pairs // 4, pairs // 4]
     grams = pltpu.VMEM((trials * trials, 8, states), jnp.float32)
     *early, last = gathered
     partial, tile, rights = call(
@@ -350,7 +360,9 @@
         partial,
         last,
     )
-    sums = [(keep, swap(send, "term", 1))]
+    bits = [1 << bit for bit in range(shares.bit_length() - 1)]
+    orders = [bits, bits[::-1]]
+    sums = [(keep, swap(send, "term", bits[0]))]
     keep, send, tile = sums_of(
         functools.partial(second_kernel, sectors, sizes[0]),
         "second_products",
@@ -363,28 +375,24 @@
         rights,
         last,
     )
-    sums.append((keep, swap(send, "term", 1)))
+    sums.append((keep, swap(send, "term", bits[-1])))
 
     for masks in [[1]] + steps_of(sectors, 1):
         tile = add_places(tile, "sec", masks)
 
-    step = 1
-    while 2 * step < shares:
-        tile = add_places(tile, "term", [step])
-        step *= 2
+    for bit in bits[1:-1]:
+        tile = add_places(tile, "term", [bit])
+    corner = swap(tile, "term", bits[0] | bits[-1])
 
     parts = []
-    for chunk, size in enumerate(sizes):
-        keep, received = sums[chunk]
-        step = 1
-        while 2 * step < shares:
-            step *= 2
-            count = shares // (2 * step)
-            last = count == 1 and chunk == len(sizes) - 1
-            operands = (keep, received, tile) if last else (keep, received)
+    for size, (keep, received), order in zip(sizes, sums, orders):
+        for step in order[1:]:
+            count = keep.shape[0] // 2
+            last_step = count == 1
+            operands = (keep, received, tile) if last_step else (keep, received)
             lines = trials * size * rows + 2 * TILE[0]
             keep, send = call(
-                halve_last_kernel if last else halve_kernel,
+                halve_last_kernel if last_step else halve_kernel,
                 "halve_rows",
                 1,
                 1,
@@ -392,7 +400,7 @@
                 out_shape=(
                     share_of(count, size, jnp.float32),
                     jax.ShapeDtypeStruct((lines, states), jnp.bfloat16)
-                    if last
+                    if last_step
                     else share_of(count, size, jnp.bfloat16),
                 ),
                 in_specs=[VMEM] * len(operands),
@@ -401,20 +409,19 @@
             received = swap(send, "term", step)
         parts += [keep, received]
 
-    done = []
-    for chunk, size in enumerate(sizes[:-1]):
-        done.append(
-            call(
-                add_last_kernel,
-                "add_last_share",
-                10**10,
-                1,
-                8 * MIB,
-                out_shape=jax.ShapeDtypeStruct((trials, size, rows, states), jnp.bfloat16),
-                in_specs=[VMEM, VMEM],
-                out_specs=VMEM,
-            )(*parts[2 * chunk : 2 * chunk + 2])
-        )
+    rows_done, tile = call(
+        add_last_kernel,
+        "add_last_share",
+        1,
+        1,
+        8 * MIB,
+        out_shape=(
+            jax.ShapeDtypeStruct((trials, sizes[1], rows, states), jnp.bfloat16),
+            tile_shape,
+        ),
+        in_specs=[VMEM] * 4,
+        out_specs=(VMEM, VMEM),
+    )(*parts[2:], tile, corner)
     products, rayleigh = call(
         finish_kernel,
         "finish",
@@ -425,9 +432,9 @@
             jax.ShapeDtypeStruct((trials, pairs, rows, states), jnp.bfloat16),
             jax.ShapeDtypeStruct((trials, trials), jnp.float32),
         ),
-        in_specs=[VMEM] * (len(done) + 3),
+        in_specs=[VMEM] * 4,
         out_specs=(VMEM, VMEM),
-    )(*done, *parts[-2:], tile)
+    )(*parts[:2], rows_done, tile)
     return (products[:, None], rayleigh)
 
 

time: 49.9 us -> 49.4 us (0.990)
  starting transfers between devices: 20.7 us -> 20 us
  waiting for transfers between devices: 19.5 us -> 20.2 us
  Pallas kernels: 6.86 us -> 6.34 us
    pallas_call x2, Pallas kernels: 3.36 us -> 2.59 us  [sums_of(): call(kernel, name, flops, MIB, 12 * MIB, out_shape=(share_of(shares // 2,...]
    ppermute x16, starting transfers between devices: 20.7 us -> 20 us  [swap(): lax.ppermute(value, axis, [(place, place ^ masks[place & 1]) for place in...]
    ppermute x16, waiting for transfers between devices: 19.5 us -> 20.2 us  [swap(): lax.ppermute(value, axis, [(place, place ^ masks[place & 1]) for place in...]
  transfers between devices with their start and end apart: 16 -> 16, of which waited for: 8 -> 9; matrix products, arithmetic and copies ran while one was open for 0% -> 0% of each run, Pallas kernels for 10% -> 9%
where the time goes in v15:
time: 49.4 us
  waiting for transfers between devices  20.2 us (41%)
  starting transfers between devices  20 us (40%)
  Pallas kernels  6.34 us (13%)
  local copies, waits for them, and re-layouts  2.22 us (4%)
  between operations  0.68 us (1%)
    ppermute x16, waiting for transfers between devices, swap(): lax.ppermute(value, axis, [(place, place ^ masks[place & 1]) for place in...  20.2 us
    ppermute x16, starting transfers between devices, swap(): lax.ppermute(value, axis, [(place, place ^ masks[place & 1]) for place in...  20 us
    pallas_call x2, Pallas kernels, sums_of(): call(kernel, name, flops, MIB, 12 * MIB, out_shape=(share_of(shares // 2,...  2.59 us
    unnamed x4, local copies, waits for them, and re-layouts  2.22 us
    pallas_call x1, Pallas kernels, local(): call(functools.partial(early_kernel, sectors), 'early_products', 2 * term...  1.86 us
    pallas_call x1, Pallas kernels, local(): call(functools.partial(inner_kernel, 1.0 / shares), 'inner_products', 2 *...  1 us
  transfers between devices with their start and end apart: 16, of which 9 were waited for; matrix products, arithmetic and copies ran while one was open for 0% of the time, Pallas kernels for 9%

profile of v15, /device:TPU:0, one launch (start us, length us, event | category | flops | bytes accessed | tf_op | source)
XLA Modules:
  0.0 49.4 jit_solution(16468720693426229757)
XLA Ops:
  0.6 3.0 %collective-permute-start.1 = (bf16[3,256,256]{2,1,0:T(8,128)(2,1)}, bf16[3,256,256]{2,1,0:T(8,128)(2,1)S(1)}, u32[]{:S(2)}, u32[]{:S(2)}) collective-permute-start(bf16[3,256,256]{2,1,0:T(8,128)(2,1)} %bitcast.11), channel_id=1, source_target_pairs={{0,16},{4,12},{8,24},{12,4},{16,0},{20,28},{24,8},{28,20},{1,17},{... | collective-permute-start | bytes 1179656 | tf_op jit(solution)/shard_map/ppermute | solution.py:20
  3.7 1.2 %copy-done = bf16[2,1,4,256,256]{4,3,2,1,0:T(8,128)(2,1)S(1)} copy-done((bf16[2,1,4,256,256]{4,3,2,1,0:T(8,128)(2,1)S(1)}, bf16[2,1,4,256,256]{4,3,2,1,0:T(8,128)(2,1)}, u32[]{:S(2)}) %copy-start) | copy-done | bytes 1048600
  4.9 1.0 %copy-done.1 = bf16[3,1,256,256]{3,2,1,0:T(8,128)(2,1)S(1)} copy-done((bf16[3,1,256,256]{3,2,1,0:T(8,128)(2,1)S(1)}, bf16[3,1,256,256]{3,2,1,0:T(8,128)(2,1)}, u32[]{:S(2)}) %copy-start.1) | copy-done | bytes 393240
  5.9 1.0 %inner_products.1 = (bf16[2,4,256,768]{3,2,1,0:T(8,128)(2,1)S(1)}, f32[8,128]{1,0:T(8,128)S(1)}, bf16[3,256,256]{2,1,0:T(8,128)(2,1)S(1)}) custom-call(bf16[2,4,256,256]{3,2,1,0:T(8,128)(2,1)S(1)} %bitcast.6, bf16[3,256,256]{2,1,0:T(8,128)(2,1)S(1)} %bitcast.10, bf16[3,256,256]{2,1,0:T(8,128)(2,1)} %bitcast.12), custom_call_target="tpu_custom_call" | custom-call | flops 805306368 | bytes 5242880 | tf_op jit(solution)/shard_map/inner_products/pallas_call | solution.py:288
  6.9 1.6 %collective-permute-start.3 = (bf16[3,256,256]{2,1,0:T(8,128)(2,1)}, bf16[3,256,256]{2,1,0:T(8,128)(2,1)S(1)}, u32[]{:S(2)}, u32[]{:S(2)}) collective-permute-start(bf16[3,256,256]{2,1,0:T(8,128)(2,1)} %bitcast.13), channel_id=1, source_target_pairs={{0,8},{4,20},{8,0},{12,28},{16,24},{20,4},{24,16},{28,12},{1,9},{5... | collective-permute-start | bytes 1179656 | tf_op jit(solution)/shard_map/ppermute | solution.py:20
  8.5 1.6 %collective-permute-done.1.rest_2_ = bf16[3,256,256]{2,1,0:T(8,128)(2,1)S(1)} collective-permute-done((bf16[3,256,256]{2,1,0:T(8,128)(2,1)}, bf16[3,256,256]{2,1,0:T(8,128)(2,1)S(1)}, u32[]{:S(2)}, u32[]{:S(2)}) %collective-permute-start.1) | collective-permute-done | bytes 393248 | tf_op jit(solution)/shard_map/ppermute | solution.py:20
  10.0 3.5 %collective-permute-start.5 = (bf16[3,256,256]{2,1,0:T(8,128)(2,1)S(1)}, bf16[3,256,256]{2,1,0:T(8,128)(2,1)S(1)}, u32[]{:S(2)}, u32[]{:S(2)}) collective-permute-start(bf16[3,256,256]{2,1,0:T(8,128)(2,1)S(1)} %collective-permute-done.1.rest_2_), channel_id=1, source_target_pairs={{0,8},{4,20},{8,0},{12,28},{16,24},{20,4},{24,16},{28,12},{1,9},{5... | collective-permute-start | bytes 1179656 | tf_op jit(solution)/shard_map/ppermute | solution.py:20
  13.6 1.4 %collective-permute-done.3.rest_4_ = bf16[3,256,256]{2,1,0:T(8,128)(2,1)S(1)} collective-permute-done((bf16[3,256,256]{2,1,0:T(8,128)(2,1)}, bf16[3,256,256]{2,1,0:T(8,128)(2,1)S(1)}, u32[]{:S(2)}, u32[]{:S(2)}) %collective-permute-start.3) | collective-permute-done | bytes 393248 | tf_op jit(solution)/shard_map/ppermute | solution.py:20
  15.5 3.9 %collective-permute-done.5.rest_6_ = bf16[3,256,256]{2,1,0:T(8,128)(2,1)S(1)} collective-permute-done((bf16[3,256,256]{2,1,0:T(8,128)(2,1)S(1)}, bf16[3,256,256]{2,1,0:T(8,128)(2,1)S(1)}, u32[]{:S(2)}, u32[]{:S(2)}) %collective-permute-start.5) | collective-permute-done | bytes 393248 | tf_op jit(solution)/shard_map/ppermute | solution.py:20
  19.3 1.9 %early_products.1 = (f32[3,2,256,256]{3,2,1,0:T(8,128)S(1)}, f32[8,128]{1,0:T(8,128)S(1)}, bf16[8,3,256,256]{3,2,1,0:T(8,128)(2,1)S(1)}) custom-call(s32[3,4]{1,0:T(4,128)} %offsets.5, bf16[2,4,256,256]{3,2,1,0:T(8,128)(2,1)S(1)} %bitcast.7, bf16[2,4,256,768]{3,2,1,0:T(8,128)(2,1)S(1)} %get-tuple-element.23.inner, f32[8,128]{1,0:T(8,128)S(1)} %get-tuple-element.24.before, ...), custom_call_target="tpu_custom_call" | custom-call | flops 603979776 | bytes 4194304 | tf_op jit(solution)/shard_map/early_products/pallas_call | solution.py:318
  21.2 1.3 %late_products.1 = (f32[2,2,3,64,256]{4,3,2,1,0:T(8,128)S(1)}, bf16[2,2,3,64,256]{4,3,2,1,0:T(8,128)(2,1)S(1)}, f32[8,128]{1,0:T(8,128)S(1)}) custom-call(s32[3,4]{1,0:T(4,128)} %offsets.5, bf16[2,4,256,256]{3,2,1,0:T(8,128)(2,1)S(1)} %bitcast.8, bf16[2,4,256,768]{3,2,1,0:T(8,128)(2,1)S(1)} %get-tuple-element.23.inner, ...), custom_call_target="tpu_custom_call" | custom-call | flops 75497472 | bytes 1048576 | tf_op jit(solution)/shard_map/late_products/pallas_call | solution.py:335
  22.5 1.4 %collective-permute-start.7 = (bf16[2,2,3,64,256]{4,3,2,1,0:T(8,128)(2,1)S(1)}, bf16[2,2,3,64,256]{4,3,2,1,0:T(8,128)(2,1)S(1)}, u32[]{:S(2)}, u32[]{:S(2)}) collective-permute-start(bf16[2,2,3,64,256]{4,3,2,1,0:T(8,128)(2,1)S(1)} %get-tuple-element.30), channel_id=1, source_target_pairs={{0,1},{1,0},{2,3},{3,2},{4,5},{5,4},{6,7},{7,6},{8,9},{9,8},{10,11... | collective-permute-start | bytes 1179656 | tf_op jit(solution)/shard_map/ppermute | solution.py:20
  24.0 1.3 %second_products.1 = (f32[2,2,1,64,256]{4,3,2,1,0:T(8,128)S(1)}, bf16[2,2,1,64,256]{4,3,2,1,0:T(8,128)(2,1)S(1)}, f32[8,128]{1,0:T(8,128)S(1)}) custom-call(s32[3,4]{1,0:T(4,128)} %offsets.5, bf16[2,4,256,256]{3,2,1,0:T(8,128)(2,1)S(1)} %bitcast.9, bf16[2,4,256,768]{3,2,1,0:T(8,128)(2,1)S(1)} %get-tuple-element.23.inner, ...), custom_call_target="tpu_custom_call" | custom-call | flops 201326592 | bytes 1048576 | tf_op jit(solution)/shard_map/second_products/pallas_call | solution.py:335
  25.7 0.8 %collective-permute-done.8 = f32[8,128]{1,0:T(8,128)S(1)} collective-permute-done((f32[8,128]{1,0:T(8,128)S(1)}, f32[8,128]{1,0:T(8,128)S(1)}, u32[]{:S(2)}, u32[]{:S(2)}) %collective-permute-start.8) | collective-permute-done | bytes 4128 | tf_op jit(solution)/shard_map/ppermute | solution.py:20
  26.6 1.4 %collective-permute-start.10 = (f32[8,128]{1,0:T(8,128)S(1)}, f32[8,128]{1,0:T(8,128)S(1)}, u32[]{:S(2)}, u32[]{:S(2)}) collective-permute-start(f32[8,128]{1,0:T(8,128)S(1)} %add.12), channel_id=1, source_target_pairs={{0,16},{4,20},{8,24},{12,28},{16,0},{20,4},{24,8},{28,12},{1,17},{... | collective-permute-start | bytes 12296 | tf_op jit(solution)/shard_map/ppermute | solution.py:20
  28.0 1.8 %collective-permute-start.11 = (f32[8,128]{1,0:T(8,128)S(1)}, f32[8,128]{1,0:T(8,128)S(1)}, u32[]{:S(2)}, u32[]{:S(2)}) collective-permute-start(f32[8,128]{1,0:T(8,128)S(1)} %add.12), channel_id=1, source_target_pairs={{0,24},{4,28},{8,16},{12,20},{16,8},{20,12},{24,0},{28,4},{1,25},{... | collective-permute-start | bytes 12296 | tf_op jit(solution)/shard_map/ppermute | solution.py:20
  30.1 2.7 %collective-permute-start.13 = (bf16[2,2,1,64,256]{4,3,2,1,0:T(8,128)(2,1)S(1)}, bf16[2,2,1,64,256]{4,3,2,1,0:T(8,128)(2,1)S(1)}, u32[]{:S(2)}, u32[]{:S(2)}) collective-permute-start(bf16[2,2,1,64,256]{4,3,2,1,0:T(8,128)(2,1)S(1)} %get-tuple-element.37), channel_id=1, source_target_pairs={{0,2},{1,3},{2,0},{3,1},{4,6},{5,7},{6,4},{7,5},{8,10},{9,11},{10,... | collective-permute-start | bytes 393224 | tf_op jit(solution)/shard_map/ppermute | solution.py:20
  33.5 3.6 %collective-permute-done.7.received = bf16[2,2,3,64,256]{4,3,2,1,0:T(8,128)(2,1)S(1)} collective-permute-done((bf16[2,2,3,64,256]{4,3,2,1,0:T(8,128)(2,1)S(1)}, bf16[2,2,3,64,256]{4,3,2,1,0:T(8,128)(2,1)S(1)}, u32[]{:S(2)}, u32[]{:S(2)}) %collective-permute-start.7) | collective-permute-done | bytes 393248 | tf_op jit(solution)/shard_map/ppermute | solution.py:20
  37.6 1.3 %collective-permute-done.13.received = bf16[2,2,1,64,256]{4,3,2,1,0:T(8,128)(2,1)S(1)} collective-permute-done((bf16[2,2,1,64,256]{4,3,2,1,0:T(8,128)(2,1)S(1)}, bf16[2,2,1,64,256]{4,3,2,1,0:T(8,128)(2,1)S(1)}, u32[]{:S(2)}, u32[]{:S(2)}) %collective-permute-start.13) | collective-permute-done | bytes 131104 | tf_op jit(solution)/shard_map/ppermute | solution.py:20
  38.9 1.2 %collective-permute-start.14 = (bf16[144,256]{1,0:T(8,128)(2,1)S(1)}, bf16[144,256]{1,0:T(8,128)(2,1)S(1)}, u32[]{:S(2)}, u32[]{:S(2)}) collective-permute-start(bf16[144,256]{1,0:T(8,128)(2,1)S(1)} %get-tuple-element.39), channel_id=1, source_target_pairs={{0,1},{1,0},{2,3},{3,2},{4,5},{5,4},{6,7},{7,6},{8,9},{9,8},{10,11... | collective-permute-start | bytes 221192 | tf_op jit(solution)/shard_map/ppermute | solution.py:20
  40.2 1.5 %collective-permute-start.15 = (f32[8,128]{1,0:T(8,128)S(1)}, f32[8,128]{1,0:T(8,128)S(1)}, u32[]{:S(2)}, u32[]{:S(2)}) collective-permute-start(f32[8,128]{1,0:T(8,128)S(1)} %add_add_fusion.tile), channel_id=1, source_target_pairs={{0,3},{1,2},{2,1},{3,0},{4,7},{5,6},{6,5},{7,4},{8,11},{9,10},{10,... | collective-permute-start | bytes 12296 | tf_op jit(solution)/shard_map/ppermute | solution.py:20
  41.7 4.3 %collective-permute-done.15.corner = f32[8,128]{1,0:T(8,128)S(1)} collective-permute-done((f32[8,128]{1,0:T(8,128)S(1)}, f32[8,128]{1,0:T(8,128)S(1)}, u32[]{:S(2)}, u32[]{:S(2)}) %collective-permute-start.15) | collective-permute-done | bytes 4128 | tf_op jit(solution)/shard_map/ppermute | solution.py:20
  46.0 2.7 %collective-permute-done.12.received = bf16[400,256]{1,0:T(8,128)(2,1)S(1)} collective-permute-done((bf16[400,256]{1,0:T(8,128)(2,1)S(1)}, bf16[400,256]{1,0:T(8,128)(2,1)S(1)}, u32[]{:S(2)}, u32[]{:S(2)}) %collective-permute-start.12) | collective-permute-done | bytes 204832 | tf_op jit(solution)/shard_map/ppermute | solution.py:20
  48.7 0.8 %finish.1 = (bf16[2,4,64,256]{3,2,1,0:T(8,128)(2,1)}, f32[2,2]{1,0:T(2,128)}) custom-call(f32[1,2,3,64,256]{4,3,2,1,0:T(8,128)S(1)} %get-tuple-element.34.kept, bf16[400,256]{1,0:T(8,128)(2,1)S(1)} %collective-permute-done.12.received, bf16[2,1,64,256]{3,2,1,0:T(8,128)(2,1)S(1)} %get-tuple-element.40.rows, f32[8,128]{1,0:T(8,128)S(1)} %get-tuple-element.41.tile), custom_call_target="tpu_custom_call" | custom-call | flops 1 | bytes 1 | tf_op jit(solution)/shard_map/finish/pallas_call | solution.py:425
  (22 shorter events, 2.5 us)
Async XLA Ops:
  0.6 9.4 %collective-permute-start.1 = (bf16[3,256,256]{2,1,0:T(8,128)(2,1)}, bf16[3,256,256]{2,1,0:T(8,128)(2,1)S(1)}, u32[]{:S(2)}, u32[]{:S(2)}) collective-permute-start(bf16[3,256,256]{2,1,0:T(8,128)(2,1)} %bitcast.11), channel_id=1, source_target_pairs={{0,16},{4,12},{8,24},{12,4},{16,0},{20,28},{24,8},{28,20},{1,17},{... | collective-permute-start | bytes 1179656 | tf_op jit(solution)/shard_map/ppermute | solution.py:20
  3.7 1.2 %copy-start = (bf16[2,1,4,256,256]{4,3,2,1,0:T(8,128)(2,1)S(1)}, bf16[2,1,4,256,256]{4,3,2,1,0:T(8,128)(2,1)}, u32[]{:S(2)}) copy-start(bf16[2,1,4,256,256]{4,3,2,1,0:T(8,128)(2,1)} %param.4) | copy-start | bytes 3145732
  4.9 1.0 %copy-start.1 = (bf16[3,1,256,256]{3,2,1,0:T(8,128)(2,1)S(1)}, bf16[3,1,256,256]{3,2,1,0:T(8,128)(2,1)}, u32[]{:S(2)}) copy-start(bf16[3,1,256,256]{3,2,1,0:T(8,128)(2,1)} %param.5) | copy-start | bytes 1179652
  6.9 8.1 %collective-permute-start.3 = (bf16[3,256,256]{2,1,0:T(8,128)(2,1)}, bf16[3,256,256]{2,1,0:T(8,128)(2,1)S(1)}, u32[]{:S(2)}, u32[]{:S(2)}) collective-permute-start(bf16[3,256,256]{2,1,0:T(8,128)(2,1)} %bitcast.13), channel_id=1, source_target_pairs={{0,8},{4,20},{8,0},{12,28},{16,24},{20,4},{24,16},{28,12},{1,9},{5... | collective-permute-start | bytes 1179656 | tf_op jit(solution)/shard_map/ppermute | solution.py:20
  10.0 9.3 %collective-permute-start.5 = (bf16[3,256,256]{2,1,0:T(8,128)(2,1)S(1)}, bf16[3,256,256]{2,1,0:T(8,128)(2,1)S(1)}, u32[]{:S(2)}, u32[]{:S(2)}) collective-permute-start(bf16[3,256,256]{2,1,0:T(8,128)(2,1)S(1)} %collective-permute-done.1.rest_2_), channel_id=1, source_target_pairs={{0,8},{4,20},{8,0},{12,28},{16,24},{20,4},{24,16},{28,12},{1,9},{5... | collective-permute-start | bytes 1179656 | tf_op jit(solution)/shard_map/ppermute | solution.py:20
  13.6 5.8 %collective-permute-start = (bf16[3,256,256]{2,1,0:T(8,128)(2,1)}, bf16[3,256,256]{2,1,0:T(8,128)(2,1)S(1)}, u32[]{:S(2)}, u32[]{:S(2)}) collective-permute-start(bf16[3,256,256]{2,1,0:T(8,128)(2,1)} %bitcast.14), channel_id=1, source_target_pairs={{0,4},{4,0},{8,12},{12,8},{16,20},{20,16},{24,28},{28,24},{1,5},{5... | collective-permute-start | bytes 1179656 | tf_op jit(solution)/shard_map/ppermute | solution.py:20
  14.9 4.4 %collective-permute-start.4 = (bf16[3,256,256]{2,1,0:T(8,128)(2,1)S(1)}, bf16[3,256,256]{2,1,0:T(8,128)(2,1)S(1)}, u32[]{:S(2)}, u32[]{:S(2)}) collective-permute-start(bf16[3,256,256]{2,1,0:T(8,128)(2,1)S(1)} %collective-permute-done.3.rest_4_), channel_id=1, source_target_pairs={{0,4},{4,0},{8,12},{12,8},{16,20},{20,16},{24,28},{28,24},{1,5},{5... | collective-permute-start | bytes 1179656 | tf_op jit(solution)/shard_map/ppermute | solution.py:20
  15.0 4.4 %collective-permute-start.2 = (bf16[3,256,256]{2,1,0:T(8,128)(2,1)S(1)}, bf16[3,256,256]{2,1,0:T(8,128)(2,1)S(1)}, u32[]{:S(2)}, u32[]{:S(2)}) collective-permute-start(bf16[3,256,256]{2,1,0:T(8,128)(2,1)S(1)} %collective-permute-done.1.rest_2_), channel_id=1, source_target_pairs={{0,4},{4,0},{8,12},{12,8},{16,20},{20,16},{24,28},{28,24},{1,5},{5... | collective-permute-start | bytes 1179656 | tf_op jit(solution)/shard_map/ppermute | solution.py:20
  19.3 1.9 %collective-permute-start.6 = (bf16[3,256,256]{2,1,0:T(8,128)(2,1)S(1)}, bf16[3,256,256]{2,1,0:T(8,128)(2,1)S(1)}, u32[]{:S(2)}, u32[]{:S(2)}) collective-permute-start(bf16[3,256,256]{2,1,0:T(8,128)(2,1)S(1)} %collective-permute-done.5.rest_6_), channel_id=1, source_target_pairs={{0,4},{4,0},{8,12},{12,8},{16,20},{20,16},{24,28},{28,24},{1,5},{5... | collective-permute-start | bytes 1179656 | tf_op jit(solution)/shard_map/ppermute | solution.py:20
  22.5 14.5 %collective-permute-start.7 = (bf16[2,2,3,64,256]{4,3,2,1,0:T(8,128)(2,1)S(1)}, bf16[2,2,3,64,256]{4,3,2,1,0:T(8,128)(2,1)S(1)}, u32[]{:S(2)}, u32[]{:S(2)}) collective-permute-start(bf16[2,2,3,64,256]{4,3,2,1,0:T(8,128)(2,1)S(1)} %get-tuple-element.30), channel_id=1, source_target_pairs={{0,1},{1,0},{2,3},{3,2},{4,5},{5,4},{6,7},{7,6},{8,9},{9,8},{10,11... | collective-permute-start | bytes 1179656 | tf_op jit(solution)/shard_map/ppermute | solution.py:20
  25.2 1.3 %collective-permute-start.8 = (f32[8,128]{1,0:T(8,128)S(1)}, f32[8,128]{1,0:T(8,128)S(1)}, u32[]{:S(2)}, u32[]{:S(2)}) collective-permute-start(f32[8,128]{1,0:T(8,128)S(1)} %get-tuple-element.33), channel_id=1, source_target_pairs={{0,4},{4,0},{8,12},{12,8},{16,20},{20,16},{24,28},{28,24},{1,5},{5... | collective-permute-start | bytes 12296 | tf_op jit(solution)/shard_map/ppermute | solution.py:20
  26.6 6.2 %collective-permute-start.10 = (f32[8,128]{1,0:T(8,128)S(1)}, f32[8,128]{1,0:T(8,128)S(1)}, u32[]{:S(2)}, u32[]{:S(2)}) collective-permute-start(f32[8,128]{1,0:T(8,128)S(1)} %add.12), channel_id=1, source_target_pairs={{0,16},{4,20},{8,24},{12,28},{16,0},{20,4},{24,8},{28,12},{1,17},{... | collective-permute-start | bytes 12296 | tf_op jit(solution)/shard_map/ppermute | solution.py:20
  28.0 4.8 %collective-permute-start.11 = (f32[8,128]{1,0:T(8,128)S(1)}, f32[8,128]{1,0:T(8,128)S(1)}, u32[]{:S(2)}, u32[]{:S(2)}) collective-permute-start(f32[8,128]{1,0:T(8,128)S(1)} %add.12), channel_id=1, source_target_pairs={{0,24},{4,28},{8,16},{12,20},{16,8},{20,12},{24,0},{28,4},{1,25},{... | collective-permute-start | bytes 12296 | tf_op jit(solution)/shard_map/ppermute | solution.py:20
  29.8 3.6 %collective-permute-start.9 = (f32[8,128]{1,0:T(8,128)S(1)}, f32[8,128]{1,0:T(8,128)S(1)}, u32[]{:S(2)}, u32[]{:S(2)}) collective-permute-start(f32[8,128]{1,0:T(8,128)S(1)} %add.12), channel_id=1, source_target_pairs={{0,8},{4,12},{8,0},{12,4},{16,24},{20,28},{24,16},{28,20},{1,9},{5... | collective-permute-start | bytes 12296 | tf_op jit(solution)/shard_map/ppermute | solution.py:20
  30.1 8.8 %collective-permute-start.13 = (bf16[2,2,1,64,256]{4,3,2,1,0:T(8,128)(2,1)S(1)}, bf16[2,2,1,64,256]{4,3,2,1,0:T(8,128)(2,1)S(1)}, u32[]{:S(2)}, u32[]{:S(2)}) collective-permute-start(bf16[2,2,1,64,256]{4,3,2,1,0:T(8,128)(2,1)S(1)} %get-tuple-element.37), channel_id=1, source_target_pairs={{0,2},{1,3},{2,0},{3,1},{4,6},{5,7},{6,4},{7,5},{8,10},{9,11},{10,... | collective-permute-start | bytes 393224 | tf_op jit(solution)/shard_map/ppermute | solution.py:20
  37.1 11.5 %collective-permute-start.12 = (bf16[400,256]{1,0:T(8,128)(2,1)S(1)}, bf16[400,256]{1,0:T(8,128)(2,1)S(1)}, u32[]{:S(2)}, u32[]{:S(2)}) collective-permute-start(bf16[400,256]{1,0:T(8,128)(2,1)S(1)} %get-tuple-element.35), channel_id=1, source_target_pairs={{0,2},{1,3},{2,0},{3,1},{4,6},{5,7},{6,4},{7,5},{8,10},{9,11},{10,... | collective-permute-start | bytes 614408 | tf_op jit(solution)/shard_map/ppermute | solution.py:20
  38.9 7.1 %collective-permute-start.14 = (bf16[144,256]{1,0:T(8,128)(2,1)S(1)}, bf16[144,256]{1,0:T(8,128)(2,1)S(1)}, u32[]{:S(2)}, u32[]{:S(2)}) collective-permute-start(bf16[144,256]{1,0:T(8,128)(2,1)S(1)} %get-tuple-element.39), channel_id=1, source_target_pairs={{0,1},{1,0},{2,3},{3,2},{4,5},{5,4},{6,7},{7,6},{8,9},{9,8},{10,11... | collective-permute-start | bytes 221192 | tf_op jit(solution)/shard_map/ppermute | solution.py:20
  40.2 5.8 %collective-permute-start.15 = (f32[8,128]{1,0:T(8,128)S(1)}, f32[8,128]{1,0:T(8,128)S(1)}, u32[]{:S(2)}, u32[]{:S(2)}) collective-permute-start(f32[8,128]{1,0:T(8,128)S(1)} %add_add_fusion.tile), channel_id=1, source_target_pairs={{0,3},{1,2},{2,1},{3,0},{4,7},{5,6},{6,5},{7,4},{8,11},{9,10},{10,... | collective-permute-start | bytes 12296 | tf_op jit(solution)/shard_map/ppermute | solution.py:20

commit v16 on v14

--- a/solution.py
+++ b/solution.py
@@ -48,9 +48,15 @@
     return jnp.sum(jnp.sum(value, axis=0, keepdims=True), axis=1, keepdims=True)
 
 
-def inner_kernel(square_scale, vectors, left, right_hbm, inner, squares, right, sem):
-    fetch = pltpu.make_async_copy(right_hbm, right, sem)
-    fetch.start()
+def inner_kernel(
+    square_scale, vectors, left, right_hbm, offsets_hbm, inner, squares, right, offsets, sems
+):
+    fetches = [
+        pltpu.make_async_copy(offsets_hbm, offsets, sems.at[0]),
+        pltpu.make_async_copy(right_hbm, right, sems.at[1]),
+    ]
+    for fetch in fetches:
+        fetch.start()
     terms, states = left.shape[0], left.shape[1]
     stacked = left[...].reshape(terms * states, states)
     sums = []
@@ -67,7 +73,8 @@
         sums.append(total(square) * square_scale)
     trials = len(sums)
     squares[...] = place_rows([(trials * trials + k, value) for k, value in enumerate(sums)])
-    fetch.wait()
+    for fetch in fetches:
+        fetch.wait()
 
 
 def place_blocks(sectors, pieces, rights):
@@ -143,16 +150,26 @@
     keep, send, tile, whole, grams = rest
     grams[...] = jnp.zeros_like(grams)
     for pair in range(partial.shape[0]):
-        whole[...] = partial[pair]
-        for term in range(last.shape[0]):
-
-            @pl.when(needed_mask(sectors, offsets, term, pair) == sectors - 1)
-            def _():
-                added = times_right(inner, term, pair, last[term])
-                whole[...] += added
-                add_gram(vectors, pair, added, grams)
-
-        write_shares(whole, pair, keep, send)
+        lacks = [
+            needed_mask(sectors, offsets, term, pair) == sectors - 1
+            for term in range(last.shape[0])
+        ]
+        lacking = functools.reduce(jnp.logical_or, lacks)
+        write_shares(partial.at[pair], pair, keep, send)
+
+        @pl.when(lacking)
+        def _():
+            whole[...] = partial[pair]
+            for term, lack in enumerate(lacks):
+
+                @pl.when(lack)
+                def _():
+                    added = times_right(inner, term, pair, last[term])
+                    whole[...] += added
+                    add_gram(vectors, pair, added, grams)
+
+            write_shares(whole, pair, keep, send)
+
     write_tile(before, grams, tile)
 
 
@@ -275,7 +292,7 @@
     vectors, left, right = vectors[:, 0], left_ops[:, 0], right_ops[:, 0]
     rows = states // shares
 
-    inner, tile, own = call(
+    inner, tile, own, offsets = call(
         functools.partial(inner_kernel, 1.0 / shares),
         "inner_products",
         2 * terms * trials * pairs * states**3,
@@ -285,11 +302,12 @@
             jax.ShapeDtypeStruct((trials, pairs, states, terms * states), jnp.bfloat16),
             jax.ShapeDtypeStruct(TILE, jnp.float32),
             jax.ShapeDtypeStruct(right.shape, jnp.bfloat16),
+            jax.ShapeDtypeStruct(offsets.shape, offsets.dtype),
         ),
-        in_specs=[VMEM, VMEM, HBM],
-        out_specs=(VMEM, VMEM, VMEM),
-        scratch_shapes=[pltpu.SemaphoreType.DMA],
-    )(vectors, left, in_hbm(right))
+        in_specs=[VMEM, VMEM, HBM, HBM],
+        out_specs=(VMEM, VMEM, VMEM, VMEM),
+        scratch_shapes=[pltpu.SemaphoreType.DMA((2,))],
+    )(vectors, left, in_hbm(right), in_hbm(offsets))
 
     def behind_inner(block):
         return lax.optimization_barrier((block, inner))[0]
@@ -319,7 +337,7 @@
         in_specs=[SMEM, VMEM, VMEM, VMEM] + [VMEM] * len(early),
         out_specs=(VMEM, VMEM, VMEM),
         scratch_shapes=[grams],
-    )(in_hbm(offsets), vectors, inner, tile, *early)
+    )(offsets, vectors, inner, tile, *early)
 
     def sums_of(kernel, name, flops, size, scratch, *operands):
         return call(
@@ -336,7 +354,7 @@
             in_specs=[SMEM] + [VMEM] * len(operands),
             out_specs=(VMEM, VMEM, VMEM),
             scratch_shapes=[pltpu.VMEM((*scratch, states, states), jnp.float32), grams],
-        )(in_hbm(offsets), *operands)
+        )(offsets, *operands)
 
     keep, send, tile = sums_of(
         functools.partial(late_kernel, sectors),

time: 49.9 us -> 48.8 us (0.978); the launches traced: 50 us -> 48.3 us
  waiting for transfers between devices: 19.5 us -> 18.1 us
  Pallas kernels: 6.86 us -> 6.13 us
    ppermute x16, waiting for transfers between devices: 19.5 us -> 18.1 us  [swap(): lax.ppermute(value, axis, [(place, place ^ masks[place & 1]) for place in...]
    pallas_call x2, Pallas kernels: 3.36 us -> 2.72 us  [sums_of(): call(kernel, name, flops, MIB, 12 * MIB, out_shape=(share_of(shares // 2,...]
  transfers between devices with their start and end apart: 16 -> 16, of which waited for: 8 -> 9; matrix products, arithmetic and copies ran while one was open for 0% -> 0% of each run, Pallas kernels for 10% -> 9%
where the time goes in v16:
time: 48.8 us; the launch traced here: 48.3 us
  starting transfers between devices  21.1 us (43%)
  waiting for transfers between devices  18.1 us (37%)
  Pallas kernels  6.13 us (13%)
  local copies, waits for them, and re-layouts  2.22 us (5%)
  between operations  0.68 us (1%)
    ppermute x16, starting transfers between devices, swap(): lax.ppermute(value, axis, [(place, place ^ masks[place & 1]) for place in...  21.1 us
    ppermute x16, waiting for transfers between devices, swap(): lax.ppermute(value, axis, [(place, place ^ masks[place & 1]) for place in...  18.1 us
    pallas_call x2, Pallas kernels, sums_of(): call(kernel, name, flops, MIB, 12 * MIB, out_shape=(share_of(shares // 2,...  2.72 us
    unnamed x4, local copies, waits for them, and re-layouts  2.22 us
    pallas_call x1, Pallas kernels, local(): call(functools.partial(early_kernel, sectors), 'early_products', 2 * term...  1.49 us
    pallas_call x1, Pallas kernels, local(): call(functools.partial(inner_kernel, 1.0 / shares), 'inner_products', 2 *...  1.03 us
  transfers between devices with their start and end apart: 16, of which 9 were waited for; matrix products, arithmetic and copies ran while one was open for 0% of the time, Pallas kernels for 9%

profile of v16, /device:TPU:0, one launch (start us, length us, event | category | flops | bytes accessed | tf_op | source)
XLA Modules:
  0.0 48.3 jit_solution(8219524286761968756)
XLA Ops:
  0.6 3.0 %collective-permute-start.1 = (bf16[3,256,256]{2,1,0:T(8,128)(2,1)}, bf16[3,256,256]{2,1,0:T(8,128)(2,1)S(1)}, u32[]{:S(2)}, u32[]{:S(2)}) collective-permute-start(bf16[3,256,256]{2,1,0:T(8,128)(2,1)} %bitcast.11), channel_id=1, source_target_pairs={{0,16},{4,12},{8,24},{12,4},{16,0},{20,28},{24,8},{28,20},{1,17},{... | collective-permute-start | bytes 1179656 | tf_op jit(solution)/shard_map/ppermute | solution.py:20
  3.7 1.2 %copy-done = bf16[2,1,4,256,256]{4,3,2,1,0:T(8,128)(2,1)S(1)} copy-done((bf16[2,1,4,256,256]{4,3,2,1,0:T(8,128)(2,1)S(1)}, bf16[2,1,4,256,256]{4,3,2,1,0:T(8,128)(2,1)}, u32[]{:S(2)}) %copy-start) | copy-done | bytes 1048600
  4.9 1.0 %copy-done.1 = bf16[3,1,256,256]{3,2,1,0:T(8,128)(2,1)S(1)} copy-done((bf16[3,1,256,256]{3,2,1,0:T(8,128)(2,1)S(1)}, bf16[3,1,256,256]{3,2,1,0:T(8,128)(2,1)}, u32[]{:S(2)}) %copy-start.1) | copy-done | bytes 393240
  5.9 1.0 %inner_products.1 = (bf16[2,4,256,768]{3,2,1,0:T(8,128)(2,1)S(1)}, f32[8,128]{1,0:T(8,128)S(1)}, bf16[3,256,256]{2,1,0:T(8,128)(2,1)S(1)}, s32[3,4]{1,0:T(4,128)S(1)}) custom-call(bf16[2,4,256,256]{3,2,1,0:T(8,128)(2,1)S(1)} %bitcast.6, bf16[3,256,256]{2,1,0:T(8,128)(2,1)S(1)} %bitcast.10, bf16[3,256,256]{2,1,0:T(8,128)(2,1)} %bitcast.12, s32[3,4]{1,0:T(4,128)} %offsets_hbm.1), custom_call_target="tpu_custom_call" | custom-call | flops 805306368 | bytes 5242880 | tf_op jit(solution)/shard_map/inner_products/pallas_call | solution.py:295
  6.9 1.6 %collective-permute-start.3 = (bf16[3,256,256]{2,1,0:T(8,128)(2,1)}, bf16[3,256,256]{2,1,0:T(8,128)(2,1)S(1)}, u32[]{:S(2)}, u32[]{:S(2)}) collective-permute-start(bf16[3,256,256]{2,1,0:T(8,128)(2,1)} %bitcast.13), channel_id=1, source_target_pairs={{0,8},{4,20},{8,0},{12,28},{16,24},{20,4},{24,16},{28,12},{1,9},{5... | collective-permute-start | bytes 1179656 | tf_op jit(solution)/shard_map/ppermute | solution.py:20
  8.5 1.5 %collective-permute-done.1.rest_2_ = bf16[3,256,256]{2,1,0:T(8,128)(2,1)S(1)} collective-permute-done((bf16[3,256,256]{2,1,0:T(8,128)(2,1)}, bf16[3,256,256]{2,1,0:T(8,128)(2,1)S(1)}, u32[]{:S(2)}, u32[]{:S(2)}) %collective-permute-start.1) | collective-permute-done | bytes 393248 | tf_op jit(solution)/shard_map/ppermute | solution.py:20
  10.0 3.5 %collective-permute-start.5 = (bf16[3,256,256]{2,1,0:T(8,128)(2,1)S(1)}, bf16[3,256,256]{2,1,0:T(8,128)(2,1)S(1)}, u32[]{:S(2)}, u32[]{:S(2)}) collective-permute-start(bf16[3,256,256]{2,1,0:T(8,128)(2,1)S(1)} %collective-permute-done.1.rest_2_), channel_id=1, source_target_pairs={{0,8},{4,20},{8,0},{12,28},{16,24},{20,4},{24,16},{28,12},{1,9},{5... | collective-permute-start | bytes 1179656 | tf_op jit(solution)/shard_map/ppermute | solution.py:20
  13.5 1.4 %collective-permute-done.3.rest_4_ = bf16[3,256,256]{2,1,0:T(8,128)(2,1)S(1)} collective-permute-done((bf16[3,256,256]{2,1,0:T(8,128)(2,1)}, bf16[3,256,256]{2,1,0:T(8,128)(2,1)S(1)}, u32[]{:S(2)}, u32[]{:S(2)}) %collective-permute-start.3) | collective-permute-done | bytes 393248 | tf_op jit(solution)/shard_map/ppermute | solution.py:20
  15.5 3.8 %collective-permute-done.5.rest_6_ = bf16[3,256,256]{2,1,0:T(8,128)(2,1)S(1)} collective-permute-done((bf16[3,256,256]{2,1,0:T(8,128)(2,1)S(1)}, bf16[3,256,256]{2,1,0:T(8,128)(2,1)S(1)}, u32[]{:S(2)}, u32[]{:S(2)}) %collective-permute-start.5) | collective-permute-done | bytes 393248 | tf_op jit(solution)/shard_map/ppermute | solution.py:20
  19.3 1.5 %early_products.1 = (f32[2,2,256,256]{3,2,1,0:T(8,128)S(1)}, f32[8,128]{1,0:T(8,128)S(1)}, bf16[8,3,256,256]{3,2,1,0:T(8,128)(2,1)S(1)}) custom-call(s32[3,4]{1,0:T(4,128)S(1)} %get-tuple-element.22.offsets, bf16[2,4,256,256]{3,2,1,0:T(8,128)(2,1)S(1)} %bitcast.7, bf16[2,4,256,768]{3,2,1,0:T(8,128)(2,1)S(1)} %get-tuple-element.23.inner, ...), custom_call_target="tpu_custom_call" | custom-call | flops 402653184 | bytes 4194304 | tf_op jit(solution)/shard_map/early_products/pallas_call | solution.py:326
  21.0 1.1 %late_products.1 = (f32[2,2,2,64,256]{4,3,2,1,0:T(8,128)S(1)}, bf16[2,2,2,64,256]{4,3,2,1,0:T(8,128)(2,1)S(1)}, f32[8,128]{1,0:T(8,128)S(1)}) custom-call(s32[3,4]{1,0:T(4,128)S(1)} %get-tuple-element.22.offsets, bf16[2,4,256,256]{3,2,1,0:T(8,128)(2,1)S(1)} %bitcast.8, bf16[2,4,256,768]{3,2,1,0:T(8,128)(2,1)S(1)} %get-tuple-element.23.inner, ...), custom_call_target="tpu_custom_call" | custom-call | flops 50331648 | bytes 1048576 | tf_op jit(solution)/shard_map/late_products/pallas_call | solution.py:343
  22.1 1.7 %collective-permute-start.7 = (bf16[2,2,2,64,256]{4,3,2,1,0:T(8,128)(2,1)S(1)}, bf16[2,2,2,64,256]{4,3,2,1,0:T(8,128)(2,1)S(1)}, u32[]{:S(2)}, u32[]{:S(2)}) collective-permute-start(bf16[2,2,2,64,256]{4,3,2,1,0:T(8,128)(2,1)S(1)} %get-tuple-element.30), channel_id=1, source_target_pairs={{0,1},{1,0},{2,3},{3,2},{4,5},{5,4},{6,7},{7,6},{8,9},{9,8},{10,11... | collective-permute-start | bytes 786440 | tf_op jit(solution)/shard_map/ppermute | solution.py:20
  23.8 1.7 %second_products.1 = (f32[2,2,2,64,256]{4,3,2,1,0:T(8,128)S(1)}, bf16[2,2,2,64,256]{4,3,2,1,0:T(8,128)(2,1)S(1)}, f32[8,128]{1,0:T(8,128)S(1)}) custom-call(s32[3,4]{1,0:T(4,128)S(1)} %get-tuple-element.22.offsets, bf16[2,4,256,256]{3,2,1,0:T(8,128)(2,1)S(1)} %bitcast.9, bf16[2,4,256,768]{3,2,1,0:T(8,128)(2,1)S(1)} %get-tuple-element.23.inner, ...), custom_call_target="tpu_custom_call" | custom-call | flops 402653184 | bytes 1048576 | tf_op jit(solution)/shard_map/second_products/pallas_call | solution.py:343
  25.8 1.2 %collective-permute-done.10 = f32[8,128]{1,0:T(8,128)S(1)} collective-permute-done((f32[8,128]{1,0:T(8,128)S(1)}, f32[8,128]{1,0:T(8,128)S(1)}, u32[]{:S(2)}, u32[]{:S(2)}) %collective-permute-start.10) | collective-permute-done | bytes 4128 | tf_op jit(solution)/shard_map/ppermute | solution.py:20
  27.0 1.9 %collective-permute-start.11 = (f32[8,128]{1,0:T(8,128)S(1)}, f32[8,128]{1,0:T(8,128)S(1)}, u32[]{:S(2)}, u32[]{:S(2)}) collective-permute-start(f32[8,128]{1,0:T(8,128)S(1)} %add.15), channel_id=1, source_target_pairs={{0,8},{4,12},{8,0},{12,4},{16,24},{20,28},{24,16},{28,20},{1,9},{5... | collective-permute-start | bytes 12296 | tf_op jit(solution)/shard_map/ppermute | solution.py:20
  28.9 1.3 %collective-permute-start.12 = (f32[8,128]{1,0:T(8,128)S(1)}, f32[8,128]{1,0:T(8,128)S(1)}, u32[]{:S(2)}, u32[]{:S(2)}) collective-permute-start(f32[8,128]{1,0:T(8,128)S(1)} %add.15), channel_id=1, source_target_pairs={{0,16},{4,20},{8,24},{12,28},{16,0},{20,4},{24,8},{28,12},{1,17},{... | collective-permute-start | bytes 12296 | tf_op jit(solution)/shard_map/ppermute | solution.py:20
  30.5 0.8 %collective-permute-done.7.received = bf16[2,2,2,64,256]{4,3,2,1,0:T(8,128)(2,1)S(1)} collective-permute-done((bf16[2,2,2,64,256]{4,3,2,1,0:T(8,128)(2,1)S(1)}, bf16[2,2,2,64,256]{4,3,2,1,0:T(8,128)(2,1)S(1)}, u32[]{:S(2)}, u32[]{:S(2)}) %collective-permute-start.7) | collective-permute-done | bytes 262176 | tf_op jit(solution)/shard_map/ppermute | solution.py:20
  31.3 2.6 %collective-permute-start.8 = (bf16[1,2,2,64,256]{4,3,2,1,0:T(8,128)(2,1)S(1)}, bf16[1,2,2,64,256]{4,3,2,1,0:T(8,128)(2,1)S(1)}, u32[]{:S(2)}, u32[]{:S(2)}) collective-permute-start(bf16[1,2,2,64,256]{4,3,2,1,0:T(8,128)(2,1)S(1)} %get-tuple-element.32), channel_id=1, source_target_pairs={{0,2},{1,3},{2,0},{3,1},{4,6},{5,7},{6,4},{7,5},{8,10},{9,11},{10,... | collective-permute-start | bytes 393224 | tf_op jit(solution)/shard_map/ppermute | solution.py:20
  33.9 0.8 %collective-permute-done.13 = f32[8,128]{1,0:T(8,128)S(1)} collective-permute-done((f32[8,128]{1,0:T(8,128)S(1)}, f32[8,128]{1,0:T(8,128)S(1)}, u32[]{:S(2)}, u32[]{:S(2)}) %collective-permute-start.13) | collective-permute-done | bytes 4128 | tf_op jit(solution)/shard_map/ppermute | solution.py:20
  34.7 1.8 %collective-permute-start.14 = (f32[8,128]{1,0:T(8,128)S(1)}, f32[8,128]{1,0:T(8,128)S(1)}, u32[]{:S(2)}, u32[]{:S(2)}) collective-permute-start(f32[8,128]{1,0:T(8,128)S(1)} %add_add_fusion), channel_id=1, source_target_pairs={{0,1},{1,0},{2,3},{3,2},{4,5},{5,4},{6,7},{7,6},{8,9},{9,8},{10,11... | collective-permute-start | bytes 12296 | tf_op jit(solution)/shard_map/ppermute | solution.py:20
  36.5 2.3 %collective-permute-done.14 = f32[8,128]{1,0:T(8,128)S(1)} collective-permute-done((f32[8,128]{1,0:T(8,128)S(1)}, f32[8,128]{1,0:T(8,128)S(1)}, u32[]{:S(2)}, u32[]{:S(2)}) %collective-permute-start.14) | collective-permute-done | bytes 4128 | tf_op jit(solution)/shard_map/ppermute | solution.py:20
  38.9 2.5 %collective-permute-start.15 = (bf16[272,256]{1,0:T(8,128)(2,1)S(1)}, bf16[272,256]{1,0:T(8,128)(2,1)S(1)}, u32[]{:S(2)}, u32[]{:S(2)}) collective-permute-start(bf16[272,256]{1,0:T(8,128)(2,1)S(1)} %get-tuple-element.39), channel_id=1, source_target_pairs={{0,2},{1,3},{2,0},{3,1},{4,6},{5,7},{6,4},{7,5},{8,10},{9,11},{10,... | collective-permute-start | bytes 417800 | tf_op jit(solution)/shard_map/ppermute | solution.py:20
  41.4 6.1 %collective-permute-done.15.refs_2_ = bf16[272,256]{1,0:T(8,128)(2,1)S(1)} collective-permute-done((bf16[272,256]{1,0:T(8,128)(2,1)S(1)}, bf16[272,256]{1,0:T(8,128)(2,1)S(1)}, u32[]{:S(2)}, u32[]{:S(2)}) %collective-permute-start.15) | collective-permute-done | bytes 139296 | tf_op jit(solution)/shard_map/ppermute | solution.py:20
  47.5 0.7 %finish.1 = (bf16[2,4,64,256]{3,2,1,0:T(8,128)(2,1)}, f32[2,2]{1,0:T(2,128)}) custom-call(bf16[2,2,64,256]{3,2,1,0:T(8,128)(2,1)S(1)} %add_last_share.1.refs_0_, f32[1,2,2,64,256]{4,3,2,1,0:T(8,128)S(1)} %get-tuple-element.38.refs_1_, bf16[272,256]{1,0:T(8,128)(2,1)S(1)} %collective-permute-done.15.refs_2_, f32[8,128]{1,0:T(8,128)S(1)} %add.19.tile.refs_3_), custom_call_target="tpu_custom_call" | custom-call | flops 1 | bytes 1 | tf_op jit(solution)/shard_map/finish/pallas_call | solution.py:436
  (23 shorter events, 1.5 us)
Async XLA Ops:
  0.6 9.4 %collective-permute-start.1 = (bf16[3,256,256]{2,1,0:T(8,128)(2,1)}, bf16[3,256,256]{2,1,0:T(8,128)(2,1)S(1)}, u32[]{:S(2)}, u32[]{:S(2)}) collective-permute-start(bf16[3,256,256]{2,1,0:T(8,128)(2,1)} %bitcast.11), channel_id=1, source_target_pairs={{0,16},{4,12},{8,24},{12,4},{16,0},{20,28},{24,8},{28,20},{1,17},{... | collective-permute-start | bytes 1179656 | tf_op jit(solution)/shard_map/ppermute | solution.py:20
  3.7 1.2 %copy-start = (bf16[2,1,4,256,256]{4,3,2,1,0:T(8,128)(2,1)S(1)}, bf16[2,1,4,256,256]{4,3,2,1,0:T(8,128)(2,1)}, u32[]{:S(2)}) copy-start(bf16[2,1,4,256,256]{4,3,2,1,0:T(8,128)(2,1)} %param.4) | copy-start | bytes 3145732
  4.9 1.0 %copy-start.1 = (bf16[3,1,256,256]{3,2,1,0:T(8,128)(2,1)S(1)}, bf16[3,1,256,256]{3,2,1,0:T(8,128)(2,1)}, u32[]{:S(2)}) copy-start(bf16[3,1,256,256]{3,2,1,0:T(8,128)(2,1)} %param.5) | copy-start | bytes 1179652
  6.9 8.1 %collective-permute-start.3 = (bf16[3,256,256]{2,1,0:T(8,128)(2,1)}, bf16[3,256,256]{2,1,0:T(8,128)(2,1)S(1)}, u32[]{:S(2)}, u32[]{:S(2)}) collective-permute-start(bf16[3,256,256]{2,1,0:T(8,128)(2,1)} %bitcast.13), channel_id=1, source_target_pairs={{0,8},{4,20},{8,0},{12,28},{16,24},{20,4},{24,16},{28,12},{1,9},{5... | collective-permute-start | bytes 1179656 | tf_op jit(solution)/shard_map/ppermute | solution.py:20
  10.0 9.3 %collective-permute-start.5 = (bf16[3,256,256]{2,1,0:T(8,128)(2,1)S(1)}, bf16[3,256,256]{2,1,0:T(8,128)(2,1)S(1)}, u32[]{:S(2)}, u32[]{:S(2)}) collective-permute-start(bf16[3,256,256]{2,1,0:T(8,128)(2,1)S(1)} %collective-permute-done.1.rest_2_), channel_id=1, source_target_pairs={{0,8},{4,20},{8,0},{12,28},{16,24},{20,4},{24,16},{28,12},{1,9},{5... | collective-permute-start | bytes 1179656 | tf_op jit(solution)/shard_map/ppermute | solution.py:20
  13.5 5.8 %collective-permute-start = (bf16[3,256,256]{2,1,0:T(8,128)(2,1)}, bf16[3,256,256]{2,1,0:T(8,128)(2,1)S(1)}, u32[]{:S(2)}, u32[]{:S(2)}) collective-permute-start(bf16[3,256,256]{2,1,0:T(8,128)(2,1)} %bitcast.14), channel_id=1, source_target_pairs={{0,4},{4,0},{8,12},{12,8},{16,20},{20,16},{24,28},{28,24},{1,5},{5... | collective-permute-start | bytes 1179656 | tf_op jit(solution)/shard_map/ppermute | solution.py:20
  15.0 4.3 %collective-permute-start.4 = (bf16[3,256,256]{2,1,0:T(8,128)(2,1)S(1)}, bf16[3,256,256]{2,1,0:T(8,128)(2,1)S(1)}, u32[]{:S(2)}, u32[]{:S(2)}) collective-permute-start(bf16[3,256,256]{2,1,0:T(8,128)(2,1)S(1)} %collective-permute-done.3.rest_4_), channel_id=1, source_target_pairs={{0,4},{4,0},{8,12},{12,8},{16,20},{20,16},{24,28},{28,24},{1,5},{5... | collective-permute-start | bytes 1179656 | tf_op jit(solution)/shard_map/ppermute | solution.py:20
  15.0 4.3 %collective-permute-start.2 = (bf16[3,256,256]{2,1,0:T(8,128)(2,1)S(1)}, bf16[3,256,256]{2,1,0:T(8,128)(2,1)S(1)}, u32[]{:S(2)}, u32[]{:S(2)}) collective-permute-start(bf16[3,256,256]{2,1,0:T(8,128)(2,1)S(1)} %collective-permute-done.1.rest_2_), channel_id=1, source_target_pairs={{0,4},{4,0},{8,12},{12,8},{16,20},{20,16},{24,28},{28,24},{1,5},{5... | collective-permute-start | bytes 1179656 | tf_op jit(solution)/shard_map/ppermute | solution.py:20
  19.3 1.7 %collective-permute-start.6 = (bf16[3,256,256]{2,1,0:T(8,128)(2,1)S(1)}, bf16[3,256,256]{2,1,0:T(8,128)(2,1)S(1)}, u32[]{:S(2)}, u32[]{:S(2)}) collective-permute-start(bf16[3,256,256]{2,1,0:T(8,128)(2,1)S(1)} %collective-permute-done.5.rest_6_), channel_id=1, source_target_pairs={{0,4},{4,0},{8,12},{12,8},{16,20},{20,16},{24,28},{28,24},{1,5},{5... | collective-permute-start | bytes 1179656 | tf_op jit(solution)/shard_map/ppermute | solution.py:20
  22.1 9.2 %collective-permute-start.7 = (bf16[2,2,2,64,256]{4,3,2,1,0:T(8,128)(2,1)S(1)}, bf16[2,2,2,64,256]{4,3,2,1,0:T(8,128)(2,1)S(1)}, u32[]{:S(2)}, u32[]{:S(2)}) collective-permute-start(bf16[2,2,2,64,256]{4,3,2,1,0:T(8,128)(2,1)S(1)} %get-tuple-element.30), channel_id=1, source_target_pairs={{0,1},{1,0},{2,3},{3,2},{4,5},{5,4},{6,7},{7,6},{8,9},{9,8},{10,11... | collective-permute-start | bytes 786440 | tf_op jit(solution)/shard_map/ppermute | solution.py:20
  25.5 13.3 %collective-permute-start.9 = (bf16[2,2,2,64,256]{4,3,2,1,0:T(8,128)(2,1)S(1)}, bf16[2,2,2,64,256]{4,3,2,1,0:T(8,128)(2,1)S(1)}, u32[]{:S(2)}, u32[]{:S(2)}) collective-permute-start(bf16[2,2,2,64,256]{4,3,2,1,0:T(8,128)(2,1)S(1)} %get-tuple-element.36), channel_id=1, source_target_pairs={{0,1},{1,0},{2,3},{3,2},{4,5},{5,4},{6,7},{7,6},{8,9},{9,8},{10,11... | collective-permute-start | bytes 786440 | tf_op jit(solution)/shard_map/ppermute | solution.py:20
  25.8 1.2 %collective-permute-start.10 = (f32[8,128]{1,0:T(8,128)S(1)}, f32[8,128]{1,0:T(8,128)S(1)}, u32[]{:S(2)}, u32[]{:S(2)}) collective-permute-start(f32[8,128]{1,0:T(8,128)S(1)} %get-tuple-element.37), channel_id=1, source_target_pairs={{0,4},{4,0},{8,12},{12,8},{16,20},{20,16},{24,28},{28,24},{1,5},{5... | collective-permute-start | bytes 12296 | tf_op jit(solution)/shard_map/ppermute | solution.py:20
  27.0 6.9 %collective-permute-start.11 = (f32[8,128]{1,0:T(8,128)S(1)}, f32[8,128]{1,0:T(8,128)S(1)}, u32[]{:S(2)}, u32[]{:S(2)}) collective-permute-start(f32[8,128]{1,0:T(8,128)S(1)} %add.15), channel_id=1, source_target_pairs={{0,8},{4,12},{8,0},{12,4},{16,24},{20,28},{24,16},{28,20},{1,9},{5... | collective-permute-start | bytes 12296 | tf_op jit(solution)/shard_map/ppermute | solution.py:20
  28.9 5.0 %collective-permute-start.12 = (f32[8,128]{1,0:T(8,128)S(1)}, f32[8,128]{1,0:T(8,128)S(1)}, u32[]{:S(2)}, u32[]{:S(2)}) collective-permute-start(f32[8,128]{1,0:T(8,128)S(1)} %add.15), channel_id=1, source_target_pairs={{0,16},{4,20},{8,24},{12,28},{16,0},{20,4},{24,8},{28,12},{1,17},{... | collective-permute-start | bytes 12296 | tf_op jit(solution)/shard_map/ppermute | solution.py:20
  30.2 4.5 %collective-permute-start.13 = (f32[8,128]{1,0:T(8,128)S(1)}, f32[8,128]{1,0:T(8,128)S(1)}, u32[]{:S(2)}, u32[]{:S(2)}) collective-permute-start(f32[8,128]{1,0:T(8,128)S(1)} %add.15), channel_id=1, source_target_pairs={{0,24},{4,28},{8,16},{12,20},{16,8},{20,12},{24,0},{28,4},{1,25},{... | collective-permute-start | bytes 12296 | tf_op jit(solution)/shard_map/ppermute | solution.py:20
  31.3 10.1 %collective-permute-start.8 = (bf16[1,2,2,64,256]{4,3,2,1,0:T(8,128)(2,1)S(1)}, bf16[1,2,2,64,256]{4,3,2,1,0:T(8,128)(2,1)S(1)}, u32[]{:S(2)}, u32[]{:S(2)}) collective-permute-start(bf16[1,2,2,64,256]{4,3,2,1,0:T(8,128)(2,1)S(1)} %get-tuple-element.32), channel_id=1, source_target_pairs={{0,2},{1,3},{2,0},{3,1},{4,6},{5,7},{6,4},{7,5},{8,10},{9,11},{10,... | collective-permute-start | bytes 393224 | tf_op jit(solution)/shard_map/ppermute | solution.py:20
  34.7 4.1 %collective-permute-start.14 = (f32[8,128]{1,0:T(8,128)S(1)}, f32[8,128]{1,0:T(8,128)S(1)}, u32[]{:S(2)}, u32[]{:S(2)}) collective-permute-start(f32[8,128]{1,0:T(8,128)S(1)} %add_add_fusion), channel_id=1, source_target_pairs={{0,1},{1,0},{2,3},{3,2},{4,5},{5,4},{6,7},{7,6},{8,9},{9,8},{10,11... | collective-permute-start | bytes 12296 | tf_op jit(solution)/shard_map/ppermute | solution.py:20
  38.9 8.7 %collective-permute-start.15 = (bf16[272,256]{1,0:T(8,128)(2,1)S(1)}, bf16[272,256]{1,0:T(8,128)(2,1)S(1)}, u32[]{:S(2)}, u32[]{:S(2)}) collective-permute-start(bf16[272,256]{1,0:T(8,128)(2,1)S(1)} %get-tuple-element.39), channel_id=1, source_target_pairs={{0,2},{1,3},{2,0},{3,1},{4,6},{5,7},{6,4},{7,5},{8,10},{9,11},{10,... | collective-permute-start | bytes 417800 | tf_op jit(solution)/shard_map/ppermute | solution.py:20

commit v17 on v16

--- a/solution.py
+++ b/solution.py
@@ -123,17 +123,25 @@
     tile[...] = before[...] + place_rows([(k, total(grams[k])) for k in range(count)])
 
 
-def write_shares(whole, slot, keep, send):
+def share_masks(shares, backwards):
+    bits = shares.bit_length() - 1
+    places = range(bits)
+    if backwards:
+        return [sum((k >> bit & 1) << (bits - 1 - bit) for bit in places) for k in range(shares)]
+    return list(range(shares))
+
+
+def write_shares(whole, backwards, slot, keep, send):
     shares = 2 * keep.shape[0]
     rows = whole.shape[1] // shares
     place = lax.axis_index("term")
-    for mask in range(shares):
+    for k, mask in enumerate(share_masks(shares, backwards)):
         start = pl.multiple_of((place ^ mask) * rows, rows)
         share = whole[:, pl.ds(start, rows)]
-        if mask & 1:
-            send[mask // 2, :, slot] = share.astype(jnp.bfloat16)
+        if k & 1:
+            send[k // 2, :, slot] = share.astype(jnp.bfloat16)
         else:
-            keep[mask // 2, :, slot] = share
+            keep[k // 2, :, slot] = share
 
 
 def early_kernel(sectors, offsets, vectors, inner, before, *rest):
@@ -155,7 +163,7 @@
             for term in range(last.shape[0])
         ]
         lacking = functools.reduce(jnp.logical_or, lacks)
-        write_shares(partial.at[pair], pair, keep, send)
+        write_shares(partial.at[pair], False, pair, keep, send)
 
         @pl.when(lacking)
         def _():
@@ -168,7 +176,7 @@
                     whole[...] += added
                     add_gram(vectors, pair, added, grams)
 
-            write_shares(whole, pair, keep, send)
+            write_shares(whole, False, pair, keep, send)
 
     write_tile(before, grams, tile)
 
@@ -187,7 +195,7 @@
 
     for slot in range(keep.shape[2]):
         add_gram(vectors, first + slot, whole[slot], grams)
-        write_shares(whole.at[slot], slot, keep, send)
+        write_shares(whole.at[slot], True, slot, keep, send)
     write_tile(before, grams, tile)
 
 
@@ -368,7 +376,9 @@
         partial,
         last,
     )
-    sums = [(keep, swap(send, "term", 1))]
+    bits = [1 << bit for bit in range(shares.bit_length() - 1)]
+    orders = [bits, bits[::-1]]
+    sums = [(keep, swap(send, "term", bits[0]))]
     keep, send, tile = sums_of(
         functools.partial(second_kernel, sectors, sizes[0]),
         "second_products",
@@ -381,28 +391,26 @@
         rights,
         last,
     )
-    sums.append((keep, swap(send, "term", 1)))
+    sums.append((keep, swap(send, "term", bits[-1])))
 
     for masks in [[1]] + steps_of(sectors, 1):
         tile = add_places(tile, "sec", masks)
 
-    step = 1
-    while 2 * step < shares:
-        tile = add_places(tile, "term", [step])
-        step *= 2
+    keep, received = sums[0]
+    received, tile = lax.optimization_barrier((received, tile))
+    sums[0] = (keep, received)
+    for bit in bits[1:]:
+        tile = add_places(tile, "term", [bit])
 
     parts = []
-    for chunk, size in enumerate(sizes):
-        keep, received = sums[chunk]
-        step = 1
-        while 2 * step < shares:
-            step *= 2
-            count = shares // (2 * step)
-            last = count == 1 and chunk == len(sizes) - 1
-            operands = (keep, received, tile) if last else (keep, received)
+    for chunk, (size, (keep, received), order) in enumerate(zip(sizes, sums, orders)):
+        for step in order[1:]:
+            count = keep.shape[0] // 2
+            rides = count == 1 and chunk == len(sizes) - 1
+            operands = (keep, received, tile) if rides else (keep, received)
             lines = trials * size * rows + 2 * TILE[0]
             keep, send = call(
-                halve_last_kernel if last else halve_kernel,
+                halve_last_kernel if rides else halve_kernel,
                 "halve_rows",
                 1,
                 1,
@@ -410,7 +418,7 @@
                 out_shape=(
                     share_of(count, size, jnp.float32),
                     jax.ShapeDtypeStruct((lines, states), jnp.bfloat16)
-                    if last
+                    if rides
                     else share_of(count, size, jnp.bfloat16),
                 ),
                 in_specs=[VMEM] * len(operands),
@@ -425,7 +433,7 @@
             call(
                 add_last_kernel,
                 "add_last_share",
-                10**10,
+                10**8,
                 1,
                 8 * MIB,
                 out_shape=jax.ShapeDtypeStruct((trials, size, rows, states), jnp.bfloat16),

time: 48.8 us -> 50.2 us (1.029)
  waiting for transfers between devices: 18.1 us -> 21.2 us
  starting transfers between devices: 21.1 us -> 19.9 us
    ppermute x16, waiting for transfers between devices: 18.1 us -> 21.2 us  [swap(): lax.ppermute(value, axis, [(place, place ^ masks[place & 1]) for place in...]
    ppermute x16, starting transfers between devices: 21.1 us -> 19.9 us  [swap(): lax.ppermute(value, axis, [(place, place ^ masks[place & 1]) for place in...]
  transfers between devices with their start and end apart: 16 -> 16, of which waited for: 9 -> 11; matrix products, arithmetic and copies ran while one was open for 0% -> 0% of each run, Pallas kernels for 9% -> 9%
where the time goes in v17:
time: 50.2 us; the launch traced here: 50.1 us
  waiting for transfers between devices  21.2 us (42%)
  starting transfers between devices  19.9 us (40%)
  Pallas kernels  6.12 us (12%)
  local copies, waits for them, and re-layouts  2.22 us (4%)
  between operations  0.69 us (1%)
    ppermute x16, waiting for transfers between devices, swap(): lax.ppermute(value, axis, [(place, place ^ masks[place & 1]) for place in...  21.2 us
    ppermute x16, starting transfers between devices, swap(): lax.ppermute(value, axis, [(place, place ^ masks[place & 1]) for place in...  19.9 us
    pallas_call x2, Pallas kernels, sums_of(): call(kernel, name, flops, MIB, 12 * MIB, out_shape=(share_of(shares // 2,...  2.72 us
    unnamed x4, local copies, waits for them, and re-layouts  2.22 us
    pallas_call x1, Pallas kernels, local(): call(functools.partial(early_kernel, sectors), 'early_products', 2 * term...  1.49 us
    pallas_call x1, Pallas kernels, local(): call(functools.partial(inner_kernel, 1.0 / shares), 'inner_products', 2 *...  1.03 us
  transfers between devices with their start and end apart: 16, of which 11 were waited for; matrix products, arithmetic and copies ran while one was open for 0% of the time, Pallas kernels for 9%

profile of v17, /device:TPU:0, one launch (start us, length us, event | category | flops | bytes accessed | tf_op | source)
XLA Modules:
  0.0 50.1 jit_solution(15565381630148415579)
XLA Ops:
  0.6 3.0 %collective-permute-start.1 = (bf16[3,256,256]{2,1,0:T(8,128)(2,1)}, bf16[3,256,256]{2,1,0:T(8,128)(2,1)S(1)}, u32[]{:S(2)}, u32[]{:S(2)}) collective-permute-start(bf16[3,256,256]{2,1,0:T(8,128)(2,1)} %bitcast.11), channel_id=1, source_target_pairs={{0,16},{4,12},{8,24},{12,4},{16,0},{20,28},{24,8},{28,20},{1,17},{... | collective-permute-start | bytes 1179656 | tf_op jit(solution)/shard_map/ppermute | solution.py:20
  3.7 1.2 %copy-done = bf16[2,1,4,256,256]{4,3,2,1,0:T(8,128)(2,1)S(1)} copy-done((bf16[2,1,4,256,256]{4,3,2,1,0:T(8,128)(2,1)S(1)}, bf16[2,1,4,256,256]{4,3,2,1,0:T(8,128)(2,1)}, u32[]{:S(2)}) %copy-start) | copy-done | bytes 1048600
  4.9 1.0 %copy-done.1 = bf16[3,1,256,256]{3,2,1,0:T(8,128)(2,1)S(1)} copy-done((bf16[3,1,256,256]{3,2,1,0:T(8,128)(2,1)S(1)}, bf16[3,1,256,256]{3,2,1,0:T(8,128)(2,1)}, u32[]{:S(2)}) %copy-start.1) | copy-done | bytes 393240
  5.9 1.0 %inner_products.1 = (bf16[2,4,256,768]{3,2,1,0:T(8,128)(2,1)S(1)}, f32[8,128]{1,0:T(8,128)S(1)}, bf16[3,256,256]{2,1,0:T(8,128)(2,1)S(1)}, s32[3,4]{1,0:T(4,128)S(1)}) custom-call(bf16[2,4,256,256]{3,2,1,0:T(8,128)(2,1)S(1)} %bitcast.6, bf16[3,256,256]{2,1,0:T(8,128)(2,1)S(1)} %bitcast.10, bf16[3,256,256]{2,1,0:T(8,128)(2,1)} %bitcast.12, s32[3,4]{1,0:T(4,128)} %offsets_hbm.1), custom_call_target="tpu_custom_call" | custom-call | flops 805306368 | bytes 5242880 | tf_op jit(solution)/shard_map/inner_products/pallas_call | solution.py:303
  6.9 1.6 %collective-permute-start.3 = (bf16[3,256,256]{2,1,0:T(8,128)(2,1)}, bf16[3,256,256]{2,1,0:T(8,128)(2,1)S(1)}, u32[]{:S(2)}, u32[]{:S(2)}) collective-permute-start(bf16[3,256,256]{2,1,0:T(8,128)(2,1)} %bitcast.13), channel_id=1, source_target_pairs={{0,8},{4,20},{8,0},{12,28},{16,24},{20,4},{24,16},{28,12},{1,9},{5... | collective-permute-start | bytes 1179656 | tf_op jit(solution)/shard_map/ppermute | solution.py:20
  8.5 1.5 %collective-permute-done.1.rest_2_ = bf16[3,256,256]{2,1,0:T(8,128)(2,1)S(1)} collective-permute-done((bf16[3,256,256]{2,1,0:T(8,128)(2,1)}, bf16[3,256,256]{2,1,0:T(8,128)(2,1)S(1)}, u32[]{:S(2)}, u32[]{:S(2)}) %collective-permute-start.1) | collective-permute-done | bytes 393248 | tf_op jit(solution)/shard_map/ppermute | solution.py:20
  10.0 3.5 %collective-permute-start.5 = (bf16[3,256,256]{2,1,0:T(8,128)(2,1)S(1)}, bf16[3,256,256]{2,1,0:T(8,128)(2,1)S(1)}, u32[]{:S(2)}, u32[]{:S(2)}) collective-permute-start(bf16[3,256,256]{2,1,0:T(8,128)(2,1)S(1)} %collective-permute-done.1.rest_2_), channel_id=1, source_target_pairs={{0,8},{4,20},{8,0},{12,28},{16,24},{20,4},{24,16},{28,12},{1,9},{5... | collective-permute-start | bytes 1179656 | tf_op jit(solution)/shard_map/ppermute | solution.py:20
  13.5 1.4 %collective-permute-done.3.rest_4_ = bf16[3,256,256]{2,1,0:T(8,128)(2,1)S(1)} collective-permute-done((bf16[3,256,256]{2,1,0:T(8,128)(2,1)}, bf16[3,256,256]{2,1,0:T(8,128)(2,1)S(1)}, u32[]{:S(2)}, u32[]{:S(2)}) %collective-permute-start.3) | collective-permute-done | bytes 393248 | tf_op jit(solution)/shard_map/ppermute | solution.py:20
  15.5 3.8 %collective-permute-done.5.rest_6_ = bf16[3,256,256]{2,1,0:T(8,128)(2,1)S(1)} collective-permute-done((bf16[3,256,256]{2,1,0:T(8,128)(2,1)S(1)}, bf16[3,256,256]{2,1,0:T(8,128)(2,1)S(1)}, u32[]{:S(2)}, u32[]{:S(2)}) %collective-permute-start.5) | collective-permute-done | bytes 393248 | tf_op jit(solution)/shard_map/ppermute | solution.py:20
  19.3 1.5 %early_products.1 = (f32[2,2,256,256]{3,2,1,0:T(8,128)S(1)}, f32[8,128]{1,0:T(8,128)S(1)}, bf16[8,3,256,256]{3,2,1,0:T(8,128)(2,1)S(1)}) custom-call(s32[3,4]{1,0:T(4,128)S(1)} %get-tuple-element.24.offsets, bf16[2,4,256,256]{3,2,1,0:T(8,128)(2,1)S(1)} %bitcast.7, bf16[2,4,256,768]{3,2,1,0:T(8,128)(2,1)S(1)} %get-tuple-element.25.inner, ...), custom_call_target="tpu_custom_call" | custom-call | flops 402653184 | bytes 4194304 | tf_op jit(solution)/shard_map/early_products/pallas_call | solution.py:334
  21.0 1.1 %late_products.1 = (f32[2,2,2,64,256]{4,3,2,1,0:T(8,128)S(1)}, bf16[2,2,2,64,256]{4,3,2,1,0:T(8,128)(2,1)S(1)}, f32[8,128]{1,0:T(8,128)S(1)}) custom-call(s32[3,4]{1,0:T(4,128)S(1)} %get-tuple-element.24.offsets, bf16[2,4,256,256]{3,2,1,0:T(8,128)(2,1)S(1)} %bitcast.8, bf16[2,4,256,768]{3,2,1,0:T(8,128)(2,1)S(1)} %get-tuple-element.25.inner, ...), custom_call_target="tpu_custom_call" | custom-call | flops 50331648 | bytes 1048576 | tf_op jit(solution)/shard_map/late_products/pallas_call | solution.py:351
  22.1 1.5 %collective-permute-start.7 = (bf16[2,2,2,64,256]{4,3,2,1,0:T(8,128)(2,1)S(1)}, bf16[2,2,2,64,256]{4,3,2,1,0:T(8,128)(2,1)S(1)}, u32[]{:S(2)}, u32[]{:S(2)}) collective-permute-start(bf16[2,2,2,64,256]{4,3,2,1,0:T(8,128)(2,1)S(1)} %get-tuple-element.32), channel_id=1, source_target_pairs={{0,1},{1,0},{2,3},{3,2},{4,5},{5,4},{6,7},{7,6},{8,9},{9,8},{10,11... | collective-permute-start | bytes 786440 | tf_op jit(solution)/shard_map/ppermute | solution.py:20
  23.6 1.7 %second_products.1 = (f32[2,2,2,64,256]{4,3,2,1,0:T(8,128)S(1)}, bf16[2,2,2,64,256]{4,3,2,1,0:T(8,128)(2,1)S(1)}, f32[8,128]{1,0:T(8,128)S(1)}) custom-call(s32[3,4]{1,0:T(4,128)S(1)} %get-tuple-element.24.offsets, bf16[2,4,256,256]{3,2,1,0:T(8,128)(2,1)S(1)} %bitcast.9, bf16[2,4,256,768]{3,2,1,0:T(8,128)(2,1)S(1)} %get-tuple-element.25.inner, ...), custom_call_target="tpu_custom_call" | custom-call | flops 402653184 | bytes 1048576 | tf_op jit(solution)/shard_map/second_products/pallas_call | solution.py:351
  25.2 3.2 %collective-permute-start.13 = (bf16[2,2,2,64,256]{4,3,2,1,0:T(8,128)(2,1)S(1)}, bf16[2,2,2,64,256]{4,3,2,1,0:T(8,128)(2,1)S(1)}, u32[]{:S(2)}, u32[]{:S(2)}) collective-permute-start(bf16[2,2,2,64,256]{4,3,2,1,0:T(8,128)(2,1)S(1)} %get-tuple-element.40), channel_id=1, source_target_pairs={{0,2},{1,3},{2,0},{3,1},{4,6},{5,7},{6,4},{7,5},{8,10},{9,11},{10,... | collective-permute-start | bytes 786440 | tf_op jit(solution)/shard_map/ppermute | solution.py:20
  28.4 1.2 %collective-permute-done.8 = f32[8,128]{1,0:T(8,128)S(1)} collective-permute-done((f32[8,128]{1,0:T(8,128)S(1)}, f32[8,128]{1,0:T(8,128)S(1)}, u32[]{:S(2)}, u32[]{:S(2)}) %collective-permute-start.8) | collective-permute-done | bytes 4128 | tf_op jit(solution)/shard_map/ppermute | solution.py:20
  29.5 1.4 %collective-permute-start.10 = (f32[8,128]{1,0:T(8,128)S(1)}, f32[8,128]{1,0:T(8,128)S(1)}, u32[]{:S(2)}, u32[]{:S(2)}) collective-permute-start(f32[8,128]{1,0:T(8,128)S(1)} %add.15), channel_id=1, source_target_pairs={{0,16},{4,20},{8,24},{12,28},{16,0},{20,4},{24,8},{28,12},{1,17},{... | collective-permute-start | bytes 12296 | tf_op jit(solution)/shard_map/ppermute | solution.py:20
  31.0 1.5 %collective-permute-start.11 = (f32[8,128]{1,0:T(8,128)S(1)}, f32[8,128]{1,0:T(8,128)S(1)}, u32[]{:S(2)}, u32[]{:S(2)}) collective-permute-start(f32[8,128]{1,0:T(8,128)S(1)} %add.15), channel_id=1, source_target_pairs={{0,24},{4,28},{8,16},{12,20},{16,8},{20,12},{24,0},{28,4},{1,25},{... | collective-permute-start | bytes 12296 | tf_op jit(solution)/shard_map/ppermute | solution.py:20
  33.2 2.3 %collective-permute-done.11 = f32[8,128]{1,0:T(8,128)S(1)} collective-permute-done((f32[8,128]{1,0:T(8,128)S(1)}, f32[8,128]{1,0:T(8,128)S(1)}, u32[]{:S(2)}, u32[]{:S(2)}) %collective-permute-start.11) | collective-permute-done | bytes 4128 | tf_op jit(solution)/shard_map/ppermute | solution.py:20
  35.5 0.6 %collective-permute-done.9 = f32[8,128]{1,0:T(8,128)S(1)} collective-permute-done((f32[8,128]{1,0:T(8,128)S(1)}, f32[8,128]{1,0:T(8,128)S(1)}, u32[]{:S(2)}, u32[]{:S(2)}) %collective-permute-start.9) | collective-permute-done | bytes 4128 | tf_op jit(solution)/shard_map/ppermute | solution.py:20
  36.6 2.7 %collective-permute-start.12 = (bf16[1,2,2,64,256]{4,3,2,1,0:T(8,128)(2,1)S(1)}, bf16[1,2,2,64,256]{4,3,2,1,0:T(8,128)(2,1)S(1)}, u32[]{:S(2)}, u32[]{:S(2)}) collective-permute-start(bf16[1,2,2,64,256]{4,3,2,1,0:T(8,128)(2,1)S(1)} %get-tuple-element.38), channel_id=1, source_target_pairs={{0,2},{1,3},{2,0},{3,1},{4,6},{5,7},{6,4},{7,5},{8,10},{9,11},{10,... | collective-permute-start | bytes 393224 | tf_op jit(solution)/shard_map/ppermute | solution.py:20
  39.2 5.0 %collective-permute-done.14 = f32[8,128]{1,0:T(8,128)S(1)} collective-permute-done((f32[8,128]{1,0:T(8,128)S(1)}, f32[8,128]{1,0:T(8,128)S(1)}, u32[]{:S(2)}, u32[]{:S(2)}) %collective-permute-start.14) | collective-permute-done | bytes 4128 | tf_op jit(solution)/shard_map/ppermute | solution.py:20
  44.3 1.9 %collective-permute-done.12.received = bf16[1,2,2,64,256]{4,3,2,1,0:T(8,128)(2,1)S(1)} collective-permute-done((bf16[1,2,2,64,256]{4,3,2,1,0:T(8,128)(2,1)S(1)}, bf16[1,2,2,64,256]{4,3,2,1,0:T(8,128)(2,1)S(1)}, u32[]{:S(2)}, u32[]{:S(2)}) %collective-permute-start.12) | collective-permute-done | bytes 131104 | tf_op jit(solution)/shard_map/ppermute | solution.py:20
  46.3 3.1 %collective-permute-done.15.refs_2_ = bf16[272,256]{1,0:T(8,128)(2,1)S(1)} collective-permute-done((bf16[272,256]{1,0:T(8,128)(2,1)S(1)}, bf16[272,256]{1,0:T(8,128)(2,1)S(1)}, u32[]{:S(2)}, u32[]{:S(2)}) %collective-permute-start.15) | collective-permute-done | bytes 139296 | tf_op jit(solution)/shard_map/ppermute | solution.py:20
  49.4 0.7 %finish.1 = (bf16[2,4,64,256]{3,2,1,0:T(8,128)(2,1)}, f32[2,2]{1,0:T(2,128)}) custom-call(bf16[2,2,64,256]{3,2,1,0:T(8,128)(2,1)S(1)} %add_last_share.1.refs_0_, f32[1,2,2,64,256]{4,3,2,1,0:T(8,128)S(1)} %get-tuple-element.42.refs_1_, bf16[272,256]{1,0:T(8,128)(2,1)S(1)} %collective-permute-done.15.refs_2_, f32[8,128]{1,0:T(8,128)S(1)} %add.19.tile.refs_3_), custom_call_target="tpu_custom_call" | custom-call | flops 1 | bytes 1 | tf_op jit(solution)/shard_map/finish/pallas_call | solution.py:444
  (23 shorter events, 2.0 us)
Async XLA Ops:
  0.6 9.4 %collective-permute-start.1 = (bf16[3,256,256]{2,1,0:T(8,128)(2,1)}, bf16[3,256,256]{2,1,0:T(8,128)(2,1)S(1)}, u32[]{:S(2)}, u32[]{:S(2)}) collective-permute-start(bf16[3,256,256]{2,1,0:T(8,128)(2,1)} %bitcast.11), channel_id=1, source_target_pairs={{0,16},{4,12},{8,24},{12,4},{16,0},{20,28},{24,8},{28,20},{1,17},{... | collective-permute-start | bytes 1179656 | tf_op jit(solution)/shard_map/ppermute | solution.py:20
  3.7 1.2 %copy-start = (bf16[2,1,4,256,256]{4,3,2,1,0:T(8,128)(2,1)S(1)}, bf16[2,1,4,256,256]{4,3,2,1,0:T(8,128)(2,1)}, u32[]{:S(2)}) copy-start(bf16[2,1,4,256,256]{4,3,2,1,0:T(8,128)(2,1)} %param.4) | copy-start | bytes 3145732
  4.9 1.0 %copy-start.1 = (bf16[3,1,256,256]{3,2,1,0:T(8,128)(2,1)S(1)}, bf16[3,1,256,256]{3,2,1,0:T(8,128)(2,1)}, u32[]{:S(2)}) copy-start(bf16[3,1,256,256]{3,2,1,0:T(8,128)(2,1)} %param.5) | copy-start | bytes 1179652
  6.9 8.1 %collective-permute-start.3 = (bf16[3,256,256]{2,1,0:T(8,128)(2,1)}, bf16[3,256,256]{2,1,0:T(8,128)(2,1)S(1)}, u32[]{:S(2)}, u32[]{:S(2)}) collective-permute-start(bf16[3,256,256]{2,1,0:T(8,128)(2,1)} %bitcast.13), channel_id=1, source_target_pairs={{0,8},{4,20},{8,0},{12,28},{16,24},{20,4},{24,16},{28,12},{1,9},{5... | collective-permute-start | bytes 1179656 | tf_op jit(solution)/shard_map/ppermute | solution.py:20
  10.0 9.3 %collective-permute-start.5 = (bf16[3,256,256]{2,1,0:T(8,128)(2,1)S(1)}, bf16[3,256,256]{2,1,0:T(8,128)(2,1)S(1)}, u32[]{:S(2)}, u32[]{:S(2)}) collective-permute-start(bf16[3,256,256]{2,1,0:T(8,128)(2,1)S(1)} %collective-permute-done.1.rest_2_), channel_id=1, source_target_pairs={{0,8},{4,20},{8,0},{12,28},{16,24},{20,4},{24,16},{28,12},{1,9},{5... | collective-permute-start | bytes 1179656 | tf_op jit(solution)/shard_map/ppermute | solution.py:20
  13.5 5.8 %collective-permute-start = (bf16[3,256,256]{2,1,0:T(8,128)(2,1)}, bf16[3,256,256]{2,1,0:T(8,128)(2,1)S(1)}, u32[]{:S(2)}, u32[]{:S(2)}) collective-permute-start(bf16[3,256,256]{2,1,0:T(8,128)(2,1)} %bitcast.14), channel_id=1, source_target_pairs={{0,4},{4,0},{8,12},{12,8},{16,20},{20,16},{24,28},{28,24},{1,5},{5... | collective-permute-start | bytes 1179656 | tf_op jit(solution)/shard_map/ppermute | solution.py:20
  15.0 4.3 %collective-permute-start.4 = (bf16[3,256,256]{2,1,0:T(8,128)(2,1)S(1)}, bf16[3,256,256]{2,1,0:T(8,128)(2,1)S(1)}, u32[]{:S(2)}, u32[]{:S(2)}) collective-permute-start(bf16[3,256,256]{2,1,0:T(8,128)(2,1)S(1)} %collective-permute-done.3.rest_4_), channel_id=1, source_target_pairs={{0,4},{4,0},{8,12},{12,8},{16,20},{20,16},{24,28},{28,24},{1,5},{5... | collective-permute-start | bytes 1179656 | tf_op jit(solution)/shard_map/ppermute | solution.py:20
  15.0 4.3 %collective-permute-start.2 = (bf16[3,256,256]{2,1,0:T(8,128)(2,1)S(1)}, bf16[3,256,256]{2,1,0:T(8,128)(2,1)S(1)}, u32[]{:S(2)}, u32[]{:S(2)}) collective-permute-start(bf16[3,256,256]{2,1,0:T(8,128)(2,1)S(1)} %collective-permute-done.1.rest_2_), channel_id=1, source_target_pairs={{0,4},{4,0},{8,12},{12,8},{16,20},{20,16},{24,28},{28,24},{1,5},{5... | collective-permute-start | bytes 1179656 | tf_op jit(solution)/shard_map/ppermute | solution.py:20
  19.3 1.7 %collective-permute-start.6 = (bf16[3,256,256]{2,1,0:T(8,128)(2,1)S(1)}, bf16[3,256,256]{2,1,0:T(8,128)(2,1)S(1)}, u32[]{:S(2)}, u32[]{:S(2)}) collective-permute-start(bf16[3,256,256]{2,1,0:T(8,128)(2,1)S(1)} %collective-permute-done.5.rest_6_), channel_id=1, source_target_pairs={{0,4},{4,0},{8,12},{12,8},{16,20},{20,16},{24,28},{28,24},{1,5},{5... | collective-permute-start | bytes 1179656 | tf_op jit(solution)/shard_map/ppermute | solution.py:20
  22.1 14.0 %collective-permute-start.7 = (bf16[2,2,2,64,256]{4,3,2,1,0:T(8,128)(2,1)S(1)}, bf16[2,2,2,64,256]{4,3,2,1,0:T(8,128)(2,1)S(1)}, u32[]{:S(2)}, u32[]{:S(2)}) collective-permute-start(bf16[2,2,2,64,256]{4,3,2,1,0:T(8,128)(2,1)S(1)} %get-tuple-element.32), channel_id=1, source_target_pairs={{0,1},{1,0},{2,3},{3,2},{4,5},{5,4},{6,7},{7,6},{8,9},{9,8},{10,11... | collective-permute-start | bytes 786440 | tf_op jit(solution)/shard_map/ppermute | solution.py:20
  25.2 19.0 %collective-permute-start.13 = (bf16[2,2,2,64,256]{4,3,2,1,0:T(8,128)(2,1)S(1)}, bf16[2,2,2,64,256]{4,3,2,1,0:T(8,128)(2,1)S(1)}, u32[]{:S(2)}, u32[]{:S(2)}) collective-permute-start(bf16[2,2,2,64,256]{4,3,2,1,0:T(8,128)(2,1)S(1)} %get-tuple-element.40), channel_id=1, source_target_pairs={{0,2},{1,3},{2,0},{3,1},{4,6},{5,7},{6,4},{7,5},{8,10},{9,11},{10,... | collective-permute-start | bytes 786440 | tf_op jit(solution)/shard_map/ppermute | solution.py:20
  28.4 1.2 %collective-permute-start.8 = (f32[8,128]{1,0:T(8,128)S(1)}, f32[8,128]{1,0:T(8,128)S(1)}, u32[]{:S(2)}, u32[]{:S(2)}) collective-permute-start(f32[8,128]{1,0:T(8,128)S(1)} %get-tuple-element.35), channel_id=1, source_target_pairs={{0,4},{4,0},{8,12},{12,8},{16,20},{20,16},{24,28},{28,24},{1,5},{5... | collective-permute-start | bytes 12296 | tf_op jit(solution)/shard_map/ppermute | solution.py:20
  29.5 3.6 %collective-permute-start.10 = (f32[8,128]{1,0:T(8,128)S(1)}, f32[8,128]{1,0:T(8,128)S(1)}, u32[]{:S(2)}, u32[]{:S(2)}) collective-permute-start(f32[8,128]{1,0:T(8,128)S(1)} %add.15), channel_id=1, source_target_pairs={{0,16},{4,20},{8,24},{12,28},{16,0},{20,4},{24,8},{28,12},{1,17},{... | collective-permute-start | bytes 12296 | tf_op jit(solution)/shard_map/ppermute | solution.py:20
  31.0 4.5 %collective-permute-start.11 = (f32[8,128]{1,0:T(8,128)S(1)}, f32[8,128]{1,0:T(8,128)S(1)}, u32[]{:S(2)}, u32[]{:S(2)}) collective-permute-start(f32[8,128]{1,0:T(8,128)S(1)} %add.15), channel_id=1, source_target_pairs={{0,24},{4,28},{8,16},{12,20},{16,8},{20,12},{24,0},{28,4},{1,25},{... | collective-permute-start | bytes 12296 | tf_op jit(solution)/shard_map/ppermute | solution.py:20
  32.5 3.6 %collective-permute-start.9 = (f32[8,128]{1,0:T(8,128)S(1)}, f32[8,128]{1,0:T(8,128)S(1)}, u32[]{:S(2)}, u32[]{:S(2)}) collective-permute-start(f32[8,128]{1,0:T(8,128)S(1)} %add.15), channel_id=1, source_target_pairs={{0,8},{4,12},{8,0},{12,4},{16,24},{20,28},{24,16},{28,20},{1,9},{5... | collective-permute-start | bytes 12296 | tf_op jit(solution)/shard_map/ppermute | solution.py:20
  36.1 8.1 %collective-permute-start.14 = (f32[8,128]{1,0:T(8,128)S(1)}, f32[8,128]{1,0:T(8,128)S(1)}, u32[]{:S(2)}, u32[]{:S(2)}) collective-permute-start(f32[8,128]{1,0:T(8,128)S(1)} %add_add_fusion), channel_id=1, source_target_pairs={{0,2},{1,3},{2,0},{3,1},{4,6},{5,7},{6,4},{7,5},{8,10},{9,11},{10,... | collective-permute-start | bytes 12296 | tf_op jit(solution)/shard_map/ppermute | solution.py:20
  36.6 9.7 %collective-permute-start.12 = (bf16[1,2,2,64,256]{4,3,2,1,0:T(8,128)(2,1)S(1)}, bf16[1,2,2,64,256]{4,3,2,1,0:T(8,128)(2,1)S(1)}, u32[]{:S(2)}, u32[]{:S(2)}) collective-permute-start(bf16[1,2,2,64,256]{4,3,2,1,0:T(8,128)(2,1)S(1)} %get-tuple-element.38), channel_id=1, source_target_pairs={{0,2},{1,3},{2,0},{3,1},{4,6},{5,7},{6,4},{7,5},{8,10},{9,11},{10,... | collective-permute-start | bytes 393224 | tf_op jit(solution)/shard_map/ppermute | solution.py:20
  44.2 5.1 %collective-permute-start.15 = (bf16[272,256]{1,0:T(8,128)(2,1)S(1)}, bf16[272,256]{1,0:T(8,128)(2,1)S(1)}, u32[]{:S(2)}, u32[]{:S(2)}) collective-permute-start(bf16[272,256]{1,0:T(8,128)(2,1)S(1)} %get-tuple-element.43), channel_id=1, source_target_pairs={{0,1},{1,0},{2,3},{3,2},{4,5},{5,4},{6,7},{7,6},{8,9},{9,8},{10,11... | collective-permute-start | bytes 417800 | tf_op jit(solution)/shard_map/ppermute | solution.py:20

commit v18 on v16

--- a/solution.py
+++ b/solution.py
@@ -49,20 +49,46 @@
 
 
 def inner_kernel(
-    square_scale, vectors, left, right_hbm, offsets_hbm, inner, squares, right, offsets, sems
+    square_scale,
+    vectors_hbm,
+    left_hbm,
+    right_hbm,
+    offsets_hbm,
+    inner,
+    squares,
+    right,
+    offsets,
+    vectors,
+    left,
+    sems,
+    block_sems,
 ):
+    fetch_left = pltpu.make_async_copy(left_hbm, left, sems.at[2])
+    fetch_left.start()
+    pairs = vectors.shape[1]
+    fetch_blocks = []
+    for trial in range(vectors.shape[0]):
+        for pair in range(pairs):
+            place = trial * pairs + pair
+            fetch = pltpu.make_async_copy(
+                vectors_hbm.at[trial, pair], vectors.at[trial, pair], block_sems.at[place]
+            )
+            fetch.start()
+            fetch_blocks.append(fetch)
     fetches = [
         pltpu.make_async_copy(offsets_hbm, offsets, sems.at[0]),
         pltpu.make_async_copy(right_hbm, right, sems.at[1]),
     ]
     for fetch in fetches:
         fetch.start()
+    fetch_left.wait()
     terms, states = left.shape[0], left.shape[1]
     stacked = left[...].reshape(terms * states, states)
     sums = []
     for trial in range(vectors.shape[0]):
         square = jnp.zeros((8, states), jnp.float32)
         for pair in range(vectors.shape[1]):
+            fetch_blocks[trial * pairs + pair].wait()
             block = vectors[trial, pair]
             product = jnp.dot(stacked, block, preferred_element_type=jnp.float32)
             for term in range(terms):
@@ -304,10 +330,15 @@
             jax.ShapeDtypeStruct(right.shape, jnp.bfloat16),
             jax.ShapeDtypeStruct(offsets.shape, offsets.dtype),
         ),
-        in_specs=[VMEM, VMEM, HBM, HBM],
+        in_specs=[HBM, HBM, HBM, HBM],
         out_specs=(VMEM, VMEM, VMEM, VMEM),
-        scratch_shapes=[pltpu.SemaphoreType.DMA((2,))],
-    )(vectors, left, in_hbm(right), in_hbm(offsets))
+        scratch_shapes=[
+            pltpu.VMEM(vectors.shape, jnp.bfloat16),
+            pltpu.VMEM(left.shape, jnp.bfloat16),
+            pltpu.SemaphoreType.DMA((3,)),
+            pltpu.SemaphoreType.DMA((trials * pairs,)),
+        ],
+    )(in_hbm(vectors), in_hbm(left), in_hbm(right), in_hbm(offsets))
 
     def behind_inner(block):
         return lax.optimization_barrier((block, inner))[0]

time: 48.8 us -> 50.1 us (1.027)
  Pallas kernels: 6.13 us -> 9 us
  local copies, waits for them, and re-layouts: 2.22 us -> 0.01 us
  starting transfers between devices: 21.1 us -> 22 us
  waiting for transfers between devices: 18.1 us -> 17.4 us
    pallas_call x1, Pallas kernels: 1.03 us -> 4.25 us  [local(): call(functools.partial(inner_kernel, 1.0 / shares), 'inner_products', 2 *...]
    unnamed x4 -> x2, local copies, waits for them, and re-layouts: 2.22 us -> 0.01 us
    ppermute x16, starting transfers between devices: 21.1 us -> 22 us  [swap(): lax.ppermute(value, axis, [(place, place ^ masks[place & 1]) for place in...]
    ppermute x16, waiting for transfers between devices: 18.1 us -> 17.4 us  [swap(): lax.ppermute(value, axis, [(place, place ^ masks[place & 1]) for place in...]
  transfers between devices with their start and end apart: 16 -> 16, of which waited for: 9 -> 8; matrix products, arithmetic and copies ran while one was open for 0% -> 0% of each run, Pallas kernels for 9% -> 15%
where the time goes in v18:
time: 50.1 us; the launch traced here: 49.1 us
  starting transfers between devices  22 us (44%)
  waiting for transfers between devices  17.4 us (35%)
  Pallas kernels  9 us (18%)
  between operations  0.7 us (1%)
    ppermute x16, starting transfers between devices, swap(): lax.ppermute(value, axis, [(place, place ^ masks[place & 1]) for place in...  22 us
    ppermute x16, waiting for transfers between devices, swap(): lax.ppermute(value, axis, [(place, place ^ masks[place & 1]) for place in...  17.4 us
    pallas_call x1, Pallas kernels, local(): call(functools.partial(inner_kernel, 1.0 / shares), 'inner_products', 2 *...  4.25 us
    pallas_call x2, Pallas kernels, sums_of(): call(kernel, name, flops, MIB, 12 * MIB, out_shape=(share_of(shares // 2,...  2.38 us
    pallas_call x1, Pallas kernels, local(): call(functools.partial(early_kernel, sectors), 'early_products', 2 * term...  1.49 us
  transfers between devices with their start and end apart: 16, of which 8 were waited for; matrix products, arithmetic and copies ran while one was open for 0% of the time, Pallas kernels for 15%

profile of v18, /device:TPU:0, one launch (start us, length us, event | category | flops | bytes accessed | tf_op | source)
XLA Modules:
  0.0 49.1 jit_solution(3835038819452246889)
XLA Ops:
  0.6 3.0 %collective-permute-start.1 = (bf16[3,256,256]{2,1,0:T(8,128)(2,1)}, bf16[3,256,256]{2,1,0:T(8,128)(2,1)S(1)}, u32[]{:S(2)}, u32[]{:S(2)}) collective-permute-start(bf16[3,256,256]{2,1,0:T(8,128)(2,1)} %bitcast.11), channel_id=1, source_target_pairs={{0,16},{4,12},{8,24},{12,4},{16,0},{20,28},{24,8},{28,20},{1,17},{... | collective-permute-start | bytes 1179656 | tf_op jit(solution)/shard_map/ppermute | solution.py:20
  3.7 4.2 %inner_products.1 = (bf16[2,4,256,768]{3,2,1,0:T(8,128)(2,1)S(1)}, f32[8,128]{1,0:T(8,128)S(1)}, bf16[3,256,256]{2,1,0:T(8,128)(2,1)S(1)}, s32[3,4]{1,0:T(4,128)S(1)}) custom-call(bf16[2,4,256,256]{3,2,1,0:T(8,128)(2,1)} %bitcast.6, bf16[3,256,256]{2,1,0:T(8,128)(2,1)} %bitcast.10, bf16[3,256,256]{2,1,0:T(8,128)(2,1)} %bitcast.12, s32[3,4]{1,0:T(4,128)} %offsets_hbm.1), custom_call_target="tpu_custom_call" | custom-call | flops 805306368 | bytes 5242880 | tf_op jit(solution)/shard_map/inner_products/pallas_call | solution.py:321
  7.9 1.6 %collective-permute-start.3 = (bf16[3,256,256]{2,1,0:T(8,128)(2,1)}, bf16[3,256,256]{2,1,0:T(8,128)(2,1)S(1)}, u32[]{:S(2)}, u32[]{:S(2)}) collective-permute-start(bf16[3,256,256]{2,1,0:T(8,128)(2,1)} %bitcast.13), channel_id=1, source_target_pairs={{0,8},{4,20},{8,0},{12,28},{16,24},{20,4},{24,16},{28,12},{1,9},{5... | collective-permute-start | bytes 1179656 | tf_op jit(solution)/shard_map/ppermute | solution.py:20
  9.6 2.9 %collective-permute-start.5 = (bf16[3,256,256]{2,1,0:T(8,128)(2,1)S(1)}, bf16[3,256,256]{2,1,0:T(8,128)(2,1)S(1)}, u32[]{:S(2)}, u32[]{:S(2)}) collective-permute-start(bf16[3,256,256]{2,1,0:T(8,128)(2,1)S(1)} %collective-permute-done.1.rest_2_), channel_id=1, source_target_pairs={{0,8},{4,20},{8,0},{12,28},{16,24},{20,4},{24,16},{28,12},{1,9},{5... | collective-permute-start | bytes 1179656 | tf_op jit(solution)/shard_map/ppermute | solution.py:20
  12.5 3.5 %collective-permute-done.3.rest_4_ = bf16[3,256,256]{2,1,0:T(8,128)(2,1)S(1)} collective-permute-done((bf16[3,256,256]{2,1,0:T(8,128)(2,1)}, bf16[3,256,256]{2,1,0:T(8,128)(2,1)S(1)}, u32[]{:S(2)}, u32[]{:S(2)}) %collective-permute-start.3) | collective-permute-done | bytes 393248 | tf_op jit(solution)/shard_map/ppermute | solution.py:20
  16.0 0.5 %collective-permute-start.2 = (bf16[3,256,256]{2,1,0:T(8,128)(2,1)S(1)}, bf16[3,256,256]{2,1,0:T(8,128)(2,1)S(1)}, u32[]{:S(2)}, u32[]{:S(2)}) collective-permute-start(bf16[3,256,256]{2,1,0:T(8,128)(2,1)S(1)} %collective-permute-done.1.rest_2_), channel_id=1, source_target_pairs={{0,4},{4,0},{8,12},{12,8},{16,20},{20,16},{24,28},{28,24},{1,5},{5... | collective-permute-start | bytes 1179656 | tf_op jit(solution)/shard_map/ppermute | solution.py:20
  16.5 3.7 %collective-permute-done.5.rest_6_ = bf16[3,256,256]{2,1,0:T(8,128)(2,1)S(1)} collective-permute-done((bf16[3,256,256]{2,1,0:T(8,128)(2,1)S(1)}, bf16[3,256,256]{2,1,0:T(8,128)(2,1)S(1)}, u32[]{:S(2)}, u32[]{:S(2)}) %collective-permute-start.5) | collective-permute-done | bytes 393248 | tf_op jit(solution)/shard_map/ppermute | solution.py:20
  20.2 1.5 %early_products.1 = (f32[2,2,256,256]{3,2,1,0:T(8,128)S(1)}, f32[8,128]{1,0:T(8,128)S(1)}, bf16[8,3,256,256]{3,2,1,0:T(8,128)(2,1)S(1)}) custom-call(s32[3,4]{1,0:T(4,128)S(1)} %get-tuple-element.22.offsets, bf16[2,4,256,256]{3,2,1,0:T(8,128)(2,1)S(1)} %bitcast.7, bf16[2,4,256,768]{3,2,1,0:T(8,128)(2,1)S(1)} %get-tuple-element.23.inner, ...), custom_call_target="tpu_custom_call" | custom-call | flops 402653184 | bytes 4194304 | tf_op jit(solution)/shard_map/early_products/pallas_call | solution.py:357
  21.9 0.7 %late_products.1 = (f32[2,2,2,64,256]{4,3,2,1,0:T(8,128)S(1)}, bf16[2,2,2,64,256]{4,3,2,1,0:T(8,128)(2,1)S(1)}, f32[8,128]{1,0:T(8,128)S(1)}) custom-call(s32[3,4]{1,0:T(4,128)S(1)} %get-tuple-element.22.offsets, bf16[2,4,256,256]{3,2,1,0:T(8,128)(2,1)S(1)} %bitcast.8, bf16[2,4,256,768]{3,2,1,0:T(8,128)(2,1)S(1)} %get-tuple-element.23.inner, ...), custom_call_target="tpu_custom_call" | custom-call | flops 50331648 | bytes 1048576 | tf_op jit(solution)/shard_map/late_products/pallas_call | solution.py:374
  22.6 1.6 %collective-permute-start.7 = (bf16[2,2,2,64,256]{4,3,2,1,0:T(8,128)(2,1)S(1)}, bf16[2,2,2,64,256]{4,3,2,1,0:T(8,128)(2,1)S(1)}, u32[]{:S(2)}, u32[]{:S(2)}) collective-permute-start(bf16[2,2,2,64,256]{4,3,2,1,0:T(8,128)(2,1)S(1)} %get-tuple-element.30), channel_id=1, source_target_pairs={{0,1},{1,0},{2,3},{3,2},{4,5},{5,4},{6,7},{7,6},{8,9},{9,8},{10,11... | collective-permute-start | bytes 786440 | tf_op jit(solution)/shard_map/ppermute | solution.py:20
  24.2 1.7 %second_products.1 = (f32[2,2,2,64,256]{4,3,2,1,0:T(8,128)S(1)}, bf16[2,2,2,64,256]{4,3,2,1,0:T(8,128)(2,1)S(1)}, f32[8,128]{1,0:T(8,128)S(1)}) custom-call(s32[3,4]{1,0:T(4,128)S(1)} %get-tuple-element.22.offsets, bf16[2,4,256,256]{3,2,1,0:T(8,128)(2,1)S(1)} %bitcast.9, bf16[2,4,256,768]{3,2,1,0:T(8,128)(2,1)S(1)} %get-tuple-element.23.inner, ...), custom_call_target="tpu_custom_call" | custom-call | flops 402653184 | bytes 1048576 | tf_op jit(solution)/shard_map/second_products/pallas_call | solution.py:374
  25.9 0.5 %collective-permute-start.9 = (bf16[2,2,2,64,256]{4,3,2,1,0:T(8,128)(2,1)S(1)}, bf16[2,2,2,64,256]{4,3,2,1,0:T(8,128)(2,1)S(1)}, u32[]{:S(2)}, u32[]{:S(2)}) collective-permute-start(bf16[2,2,2,64,256]{4,3,2,1,0:T(8,128)(2,1)S(1)} %get-tuple-element.36), channel_id=1, source_target_pairs={{0,1},{1,0},{2,3},{3,2},{4,5},{5,4},{6,7},{7,6},{8,9},{9,8},{10,11... | collective-permute-start | bytes 786440 | tf_op jit(solution)/shard_map/ppermute | solution.py:20
  26.4 0.4 collective-permute-start.10
  26.8 0.8 %collective-permute-done.10 = f32[8,128]{1,0:T(8,128)S(1)} collective-permute-done((f32[8,128]{1,0:T(8,128)S(1)}, f32[8,128]{1,0:T(8,128)S(1)}, u32[]{:S(2)}, u32[]{:S(2)}) %collective-permute-start.10) | collective-permute-done | bytes 4128 | tf_op jit(solution)/shard_map/ppermute | solution.py:20
  27.6 2.1 %collective-permute-start.11 = (f32[8,128]{1,0:T(8,128)S(1)}, f32[8,128]{1,0:T(8,128)S(1)}, u32[]{:S(2)}, u32[]{:S(2)}) collective-permute-start(f32[8,128]{1,0:T(8,128)S(1)} %add.15), channel_id=1, source_target_pairs={{0,8},{4,12},{8,0},{12,4},{16,24},{20,28},{24,16},{28,20},{1,9},{5... | collective-permute-start | bytes 12296 | tf_op jit(solution)/shard_map/ppermute | solution.py:20
  29.7 0.5 %collective-permute-start.12 = (f32[8,128]{1,0:T(8,128)S(1)}, f32[8,128]{1,0:T(8,128)S(1)}, u32[]{:S(2)}, u32[]{:S(2)}) collective-permute-start(f32[8,128]{1,0:T(8,128)S(1)} %add.15), channel_id=1, source_target_pairs={{0,16},{4,20},{8,24},{12,28},{16,0},{20,4},{24,8},{28,12},{1,17},{... | collective-permute-start | bytes 12296 | tf_op jit(solution)/shard_map/ppermute | solution.py:20
  30.2 1.0 %collective-permute-start.13 = (f32[8,128]{1,0:T(8,128)S(1)}, f32[8,128]{1,0:T(8,128)S(1)}, u32[]{:S(2)}, u32[]{:S(2)}) collective-permute-start(f32[8,128]{1,0:T(8,128)S(1)} %add.15), channel_id=1, source_target_pairs={{0,24},{4,28},{8,16},{12,20},{16,8},{20,12},{24,0},{28,4},{1,25},{... | collective-permute-start | bytes 12296 | tf_op jit(solution)/shard_map/ppermute | solution.py:20
  31.2 0.6 %collective-permute-done.7.received = bf16[2,2,2,64,256]{4,3,2,1,0:T(8,128)(2,1)S(1)} collective-permute-done((bf16[2,2,2,64,256]{4,3,2,1,0:T(8,128)(2,1)S(1)}, bf16[2,2,2,64,256]{4,3,2,1,0:T(8,128)(2,1)S(1)}, u32[]{:S(2)}, u32[]{:S(2)}) %collective-permute-start.7) | collective-permute-done | bytes 262176 | tf_op jit(solution)/shard_map/ppermute | solution.py:20
  31.8 3.7 %collective-permute-start.8 = (bf16[1,2,2,64,256]{4,3,2,1,0:T(8,128)(2,1)S(1)}, bf16[1,2,2,64,256]{4,3,2,1,0:T(8,128)(2,1)S(1)}, u32[]{:S(2)}, u32[]{:S(2)}) collective-permute-start(bf16[1,2,2,64,256]{4,3,2,1,0:T(8,128)(2,1)S(1)} %get-tuple-element.32), channel_id=1, source_target_pairs={{0,2},{1,3},{2,0},{3,1},{4,6},{5,7},{6,4},{7,5},{8,10},{9,11},{10,... | collective-permute-start | bytes 393224 | tf_op jit(solution)/shard_map/ppermute | solution.py:20
  35.5 1.6 %collective-permute-start.14 = (f32[8,128]{1,0:T(8,128)S(1)}, f32[8,128]{1,0:T(8,128)S(1)}, u32[]{:S(2)}, u32[]{:S(2)}) collective-permute-start(f32[8,128]{1,0:T(8,128)S(1)} %add_add_fusion), channel_id=1, source_target_pairs={{0,1},{1,0},{2,3},{3,2},{4,5},{5,4},{6,7},{7,6},{8,9},{9,8},{10,11... | collective-permute-start | bytes 12296 | tf_op jit(solution)/shard_map/ppermute | solution.py:20
  37.1 2.6 %collective-permute-done.14 = f32[8,128]{1,0:T(8,128)S(1)} collective-permute-done((f32[8,128]{1,0:T(8,128)S(1)}, f32[8,128]{1,0:T(8,128)S(1)}, u32[]{:S(2)}, u32[]{:S(2)}) %collective-permute-start.14) | collective-permute-done | bytes 4128 | tf_op jit(solution)/shard_map/ppermute | solution.py:20
  39.8 2.7 %collective-permute-start.15 = (bf16[272,256]{1,0:T(8,128)(2,1)S(1)}, bf16[272,256]{1,0:T(8,128)(2,1)S(1)}, u32[]{:S(2)}, u32[]{:S(2)}) collective-permute-start(bf16[272,256]{1,0:T(8,128)(2,1)S(1)} %get-tuple-element.39), channel_id=1, source_target_pairs={{0,2},{1,3},{2,0},{3,1},{4,6},{5,7},{6,4},{7,5},{8,10},{9,11},{10,... | collective-permute-start | bytes 417800 | tf_op jit(solution)/shard_map/ppermute | solution.py:20
  42.5 5.9 %collective-permute-done.15.refs_2_ = bf16[272,256]{1,0:T(8,128)(2,1)S(1)} collective-permute-done((bf16[272,256]{1,0:T(8,128)(2,1)S(1)}, bf16[272,256]{1,0:T(8,128)(2,1)S(1)}, u32[]{:S(2)}, u32[]{:S(2)}) %collective-permute-start.15) | collective-permute-done | bytes 139296 | tf_op jit(solution)/shard_map/ppermute | solution.py:20
  48.3 0.7 %finish.1 = (bf16[2,4,64,256]{3,2,1,0:T(8,128)(2,1)}, f32[2,2]{1,0:T(2,128)}) custom-call(bf16[2,2,64,256]{3,2,1,0:T(8,128)(2,1)S(1)} %add_last_share.1.refs_0_, f32[1,2,2,64,256]{4,3,2,1,0:T(8,128)S(1)} %get-tuple-element.38.refs_1_, bf16[272,256]{1,0:T(8,128)(2,1)S(1)} %collective-permute-done.15.refs_2_, f32[8,128]{1,0:T(8,128)S(1)} %add.19.tile.refs_3_), custom_call_target="tpu_custom_call" | custom-call | flops 1 | bytes 1 | tf_op jit(solution)/shard_map/finish/pallas_call | solution.py:467
  (21 shorter events, 0.5 us)
Async XLA Ops:
  0.6 19.6 %copy-start = (bf16[2,1,4,256,256]{4,3,2,1,0:T(8,128)(2,1)S(1)}, bf16[2,1,4,256,256]{4,3,2,1,0:T(8,128)(2,1)}, u32[]{:S(2)}) copy-start(bf16[2,1,4,256,256]{4,3,2,1,0:T(8,128)(2,1)} %param.4) | copy-start | bytes 3145732
  0.6 9.0 %collective-permute-start.1 = (bf16[3,256,256]{2,1,0:T(8,128)(2,1)}, bf16[3,256,256]{2,1,0:T(8,128)(2,1)S(1)}, u32[]{:S(2)}, u32[]{:S(2)}) collective-permute-start(bf16[3,256,256]{2,1,0:T(8,128)(2,1)} %bitcast.11), channel_id=1, source_target_pairs={{0,16},{4,12},{8,24},{12,4},{16,0},{20,28},{24,8},{28,20},{1,17},{... | collective-permute-start | bytes 1179656 | tf_op jit(solution)/shard_map/ppermute | solution.py:20
  7.9 8.1 %collective-permute-start.3 = (bf16[3,256,256]{2,1,0:T(8,128)(2,1)}, bf16[3,256,256]{2,1,0:T(8,128)(2,1)S(1)}, u32[]{:S(2)}, u32[]{:S(2)}) collective-permute-start(bf16[3,256,256]{2,1,0:T(8,128)(2,1)} %bitcast.13), channel_id=1, source_target_pairs={{0,8},{4,20},{8,0},{12,28},{16,24},{20,4},{24,16},{28,12},{1,9},{5... | collective-permute-start | bytes 1179656 | tf_op jit(solution)/shard_map/ppermute | solution.py:20
  9.6 10.6 %collective-permute-start.5 = (bf16[3,256,256]{2,1,0:T(8,128)(2,1)S(1)}, bf16[3,256,256]{2,1,0:T(8,128)(2,1)S(1)}, u32[]{:S(2)}, u32[]{:S(2)}) collective-permute-start(bf16[3,256,256]{2,1,0:T(8,128)(2,1)S(1)} %collective-permute-done.1.rest_2_), channel_id=1, source_target_pairs={{0,8},{4,20},{8,0},{12,28},{16,24},{20,4},{24,16},{28,12},{1,9},{5... | collective-permute-start | bytes 1179656 | tf_op jit(solution)/shard_map/ppermute | solution.py:20
  12.5 7.7 %collective-permute-start = (bf16[3,256,256]{2,1,0:T(8,128)(2,1)}, bf16[3,256,256]{2,1,0:T(8,128)(2,1)S(1)}, u32[]{:S(2)}, u32[]{:S(2)}) collective-permute-start(bf16[3,256,256]{2,1,0:T(8,128)(2,1)} %bitcast.14), channel_id=1, source_target_pairs={{0,4},{4,0},{8,12},{12,8},{16,20},{20,16},{24,28},{28,24},{1,5},{5... | collective-permute-start | bytes 1179656 | tf_op jit(solution)/shard_map/ppermute | solution.py:20
  16.0 4.2 %collective-permute-start.4 = (bf16[3,256,256]{2,1,0:T(8,128)(2,1)S(1)}, bf16[3,256,256]{2,1,0:T(8,128)(2,1)S(1)}, u32[]{:S(2)}, u32[]{:S(2)}) collective-permute-start(bf16[3,256,256]{2,1,0:T(8,128)(2,1)S(1)} %collective-permute-done.3.rest_4_), channel_id=1, source_target_pairs={{0,4},{4,0},{8,12},{12,8},{16,20},{20,16},{24,28},{28,24},{1,5},{5... | collective-permute-start | bytes 1179656 | tf_op jit(solution)/shard_map/ppermute | solution.py:20
  16.0 4.2 %collective-permute-start.2 = (bf16[3,256,256]{2,1,0:T(8,128)(2,1)S(1)}, bf16[3,256,256]{2,1,0:T(8,128)(2,1)S(1)}, u32[]{:S(2)}, u32[]{:S(2)}) collective-permute-start(bf16[3,256,256]{2,1,0:T(8,128)(2,1)S(1)} %collective-permute-done.1.rest_2_), channel_id=1, source_target_pairs={{0,4},{4,0},{8,12},{12,8},{16,20},{20,16},{24,28},{28,24},{1,5},{5... | collective-permute-start | bytes 1179656 | tf_op jit(solution)/shard_map/ppermute | solution.py:20
  20.2 1.7 %collective-permute-start.6 = (bf16[3,256,256]{2,1,0:T(8,128)(2,1)S(1)}, bf16[3,256,256]{2,1,0:T(8,128)(2,1)S(1)}, u32[]{:S(2)}, u32[]{:S(2)}) collective-permute-start(bf16[3,256,256]{2,1,0:T(8,128)(2,1)S(1)} %collective-permute-done.5.rest_6_), channel_id=1, source_target_pairs={{0,4},{4,0},{8,12},{12,8},{16,20},{20,16},{24,28},{28,24},{1,5},{5... | collective-permute-start | bytes 1179656 | tf_op jit(solution)/shard_map/ppermute | solution.py:20
  22.6 9.1 %collective-permute-start.7 = (bf16[2,2,2,64,256]{4,3,2,1,0:T(8,128)(2,1)S(1)}, bf16[2,2,2,64,256]{4,3,2,1,0:T(8,128)(2,1)S(1)}, u32[]{:S(2)}, u32[]{:S(2)}) collective-permute-start(bf16[2,2,2,64,256]{4,3,2,1,0:T(8,128)(2,1)S(1)} %get-tuple-element.30), channel_id=1, source_target_pairs={{0,1},{1,0},{2,3},{3,2},{4,5},{5,4},{6,7},{7,6},{8,9},{9,8},{10,11... | collective-permute-start | bytes 786440 | tf_op jit(solution)/shard_map/ppermute | solution.py:20
  25.9 13.8 %collective-permute-start.9 = (bf16[2,2,2,64,256]{4,3,2,1,0:T(8,128)(2,1)S(1)}, bf16[2,2,2,64,256]{4,3,2,1,0:T(8,128)(2,1)S(1)}, u32[]{:S(2)}, u32[]{:S(2)}) collective-permute-start(bf16[2,2,2,64,256]{4,3,2,1,0:T(8,128)(2,1)S(1)} %get-tuple-element.36), channel_id=1, source_target_pairs={{0,1},{1,0},{2,3},{3,2},{4,5},{5,4},{6,7},{7,6},{8,9},{9,8},{10,11... | collective-permute-start | bytes 786440 | tf_op jit(solution)/shard_map/ppermute | solution.py:20
  26.4 1.2 %collective-permute-start.10 = (f32[8,128]{1,0:T(8,128)S(1)}, f32[8,128]{1,0:T(8,128)S(1)}, u32[]{:S(2)}, u32[]{:S(2)}) collective-permute-start(f32[8,128]{1,0:T(8,128)S(1)} %get-tuple-element.37), channel_id=1, source_target_pairs={{0,4},{4,0},{8,12},{12,8},{16,20},{20,16},{24,28},{28,24},{1,5},{5... | collective-permute-start | bytes 12296 | tf_op jit(solution)/shard_map/ppermute | solution.py:20
  27.6 7.9 %collective-permute-start.11 = (f32[8,128]{1,0:T(8,128)S(1)}, f32[8,128]{1,0:T(8,128)S(1)}, u32[]{:S(2)}, u32[]{:S(2)}) collective-permute-start(f32[8,128]{1,0:T(8,128)S(1)} %add.15), channel_id=1, source_target_pairs={{0,8},{4,12},{8,0},{12,4},{16,24},{20,28},{24,16},{28,20},{1,9},{5... | collective-permute-start | bytes 12296 | tf_op jit(solution)/shard_map/ppermute | solution.py:20
  29.7 5.8 %collective-permute-start.12 = (f32[8,128]{1,0:T(8,128)S(1)}, f32[8,128]{1,0:T(8,128)S(1)}, u32[]{:S(2)}, u32[]{:S(2)}) collective-permute-start(f32[8,128]{1,0:T(8,128)S(1)} %add.15), channel_id=1, source_target_pairs={{0,16},{4,20},{8,24},{12,28},{16,0},{20,4},{24,8},{28,12},{1,17},{... | collective-permute-start | bytes 12296 | tf_op jit(solution)/shard_map/ppermute | solution.py:20
  30.2 5.3 %collective-permute-start.13 = (f32[8,128]{1,0:T(8,128)S(1)}, f32[8,128]{1,0:T(8,128)S(1)}, u32[]{:S(2)}, u32[]{:S(2)}) collective-permute-start(f32[8,128]{1,0:T(8,128)S(1)} %add.15), channel_id=1, source_target_pairs={{0,24},{4,28},{8,16},{12,20},{16,8},{20,12},{24,0},{28,4},{1,25},{... | collective-permute-start | bytes 12296 | tf_op jit(solution)/shard_map/ppermute | solution.py:20
  31.8 10.6 %collective-permute-start.8 = (bf16[1,2,2,64,256]{4,3,2,1,0:T(8,128)(2,1)S(1)}, bf16[1,2,2,64,256]{4,3,2,1,0:T(8,128)(2,1)S(1)}, u32[]{:S(2)}, u32[]{:S(2)}) collective-permute-start(bf16[1,2,2,64,256]{4,3,2,1,0:T(8,128)(2,1)S(1)} %get-tuple-element.32), channel_id=1, source_target_pairs={{0,2},{1,3},{2,0},{3,1},{4,6},{5,7},{6,4},{7,5},{8,10},{9,11},{10,... | collective-permute-start | bytes 393224 | tf_op jit(solution)/shard_map/ppermute | solution.py:20
  35.5 4.2 %collective-permute-start.14 = (f32[8,128]{1,0:T(8,128)S(1)}, f32[8,128]{1,0:T(8,128)S(1)}, u32[]{:S(2)}, u32[]{:S(2)}) collective-permute-start(f32[8,128]{1,0:T(8,128)S(1)} %add_add_fusion), channel_id=1, source_target_pairs={{0,1},{1,0},{2,3},{3,2},{4,5},{5,4},{6,7},{7,6},{8,9},{9,8},{10,11... | collective-permute-start | bytes 12296 | tf_op jit(solution)/shard_map/ppermute | solution.py:20
  39.8 8.6 %collective-permute-start.15 = (bf16[272,256]{1,0:T(8,128)(2,1)S(1)}, bf16[272,256]{1,0:T(8,128)(2,1)S(1)}, u32[]{:S(2)}, u32[]{:S(2)}) collective-permute-start(bf16[272,256]{1,0:T(8,128)(2,1)S(1)} %get-tuple-element.39), channel_id=1, source_target_pairs={{0,2},{1,3},{2,0},{3,1},{4,6},{5,7},{6,4},{7,5},{8,10},{9,11},{10,... | collective-permute-start | bytes 417800 | tf_op jit(solution)/shard_map/ppermute | solution.py:20

commit v19 on v16

--- a/solution.py
+++ b/solution.py
@@ -230,14 +230,18 @@
 
 
 def finish_kernel(*refs):
-    *done, kept, received, tile, products, rayleigh = refs
-    first = 0
-    for part in done:
-        products[:, first : first + part.shape[1]] = part[...]
+    *done, kept, received, tile, products, rayleigh_hbm, rows, rayleigh, sems = refs
+    copies, first = [], 0
+    for part in [*done, rows]:
+        target = products.at[:, pl.ds(first, part.shape[1])]
+        copies.append(pltpu.make_async_copy(part, target, sems.at[len(copies)]))
         first += part.shape[1]
+    for copy in copies[:-1]:
+        copy.start()
     lines = received.shape[0] - 2 * TILE[0]
     both = received[:lines].astype(jnp.float32).reshape(kept.shape[1:])
-    products[:, first:] = (kept[0] + both).astype(jnp.bfloat16)
+    rows[...] = (kept[0] + both).astype(jnp.bfloat16)
+    copies[-1].start()
 
     tile = tile[...] + ridden_tile(received)
     trials = rayleigh.shape[0]
@@ -254,6 +258,10 @@
             value = entry(i * trials + j) / jnp.sqrt(squares)
             result = jnp.where((row == i) & (column == j), value, result)
     rayleigh[...] = result
+    last = pltpu.make_async_copy(rayleigh, rayleigh_hbm, sems.at[len(copies)])
+    last.start()
+    for copy in [*copies, last]:
+        copy.wait()
 
 
 def in_hbm(value):
@@ -444,7 +452,12 @@
             jax.ShapeDtypeStruct((trials, trials), jnp.float32),
         ),
         in_specs=[VMEM] * (len(done) + 3),
-        out_specs=(VMEM, VMEM),
+        out_specs=(HBM, HBM),
+        scratch_shapes=[
+            pltpu.VMEM((trials, sizes[-1], rows, states), jnp.bfloat16),
+            pltpu.VMEM((trials, trials), jnp.float32),
+            pltpu.SemaphoreType.DMA((len(sizes) + 1,)),
+        ],
     )(*done, *parts[-2:], tile)
     return (products[:, None], rayleigh)
 

time: 48.8 us -> 49.5 us (1.014); the launches traced: 48.3 us -> 49.8 us
  waiting for transfers between devices: 18.1 us -> 19.5 us
    ppermute x16, waiting for transfers between devices: 18.1 us -> 19.5 us  [swap(): lax.ppermute(value, axis, [(place, place ^ masks[place & 1]) for place in...]
where the time goes in v19:
time: 49.5 us; the launch traced here: 49.8 us
  starting transfers between devices  21.3 us (43%)
  waiting for transfers between devices  19.5 us (39%)
  Pallas kernels  5.99 us (12%)
  local copies, waits for them, and re-layouts  2.22 us (4%)
  between operations  0.68 us (1%)
    ppermute x16, starting transfers between devices, swap(): lax.ppermute(value, axis, [(place, place ^ masks[place & 1]) for place in...  21.3 us
    ppermute x16, waiting for transfers between devices, swap(): lax.ppermute(value, axis, [(place, place ^ masks[place & 1]) for place in...  19.5 us
    pallas_call x2, Pallas kernels, sums_of(): call(kernel, name, flops, MIB, 12 * MIB, out_shape=(share_of(shares // 2,...  2.6 us
    unnamed x4, local copies, waits for them, and re-layouts  2.22 us
    pallas_call x1, Pallas kernels, local(): call(functools.partial(early_kernel, sectors), 'early_products', 2 * term...  1.49 us
    pallas_call x1, Pallas kernels, local(): call(functools.partial(inner_kernel, 1.0 / shares), 'inner_products', 2 *...  1.03 us
  transfers between devices with their start and end apart: 16, of which 9 were waited for; matrix products, arithmetic and copies ran while one was open for 0% of the time, Pallas kernels for 9%

profile of v19, /device:TPU:0, one launch (start us, length us, event | category | flops | bytes accessed | tf_op | source)
XLA Modules:
  0.0 49.8 jit_solution(2649584004399359663)
XLA Ops:
  0.6 3.0 %collective-permute-start.1 = (bf16[3,256,256]{2,1,0:T(8,128)(2,1)}, bf16[3,256,256]{2,1,0:T(8,128)(2,1)S(1)}, u32[]{:S(2)}, u32[]{:S(2)}) collective-permute-start(bf16[3,256,256]{2,1,0:T(8,128)(2,1)} %bitcast.11), channel_id=1, source_target_pairs={{0,16},{4,12},{8,24},{12,4},{16,0},{20,28},{24,8},{28,20},{1,17},{... | collective-permute-start | bytes 1179656 | tf_op jit(solution)/shard_map/ppermute | solution.py:20
  3.7 1.2 %copy-done = bf16[2,1,4,256,256]{4,3,2,1,0:T(8,128)(2,1)S(1)} copy-done((bf16[2,1,4,256,256]{4,3,2,1,0:T(8,128)(2,1)S(1)}, bf16[2,1,4,256,256]{4,3,2,1,0:T(8,128)(2,1)}, u32[]{:S(2)}) %copy-start) | copy-done | bytes 1048600
  4.9 1.0 %copy-done.1 = bf16[3,1,256,256]{3,2,1,0:T(8,128)(2,1)S(1)} copy-done((bf16[3,1,256,256]{3,2,1,0:T(8,128)(2,1)S(1)}, bf16[3,1,256,256]{3,2,1,0:T(8,128)(2,1)}, u32[]{:S(2)}) %copy-start.1) | copy-done | bytes 393240
  5.9 1.0 %inner_products.1 = (bf16[2,4,256,768]{3,2,1,0:T(8,128)(2,1)S(1)}, f32[8,128]{1,0:T(8,128)S(1)}, bf16[3,256,256]{2,1,0:T(8,128)(2,1)S(1)}, s32[3,4]{1,0:T(4,128)S(1)}) custom-call(bf16[2,4,256,256]{3,2,1,0:T(8,128)(2,1)S(1)} %bitcast.6, bf16[3,256,256]{2,1,0:T(8,128)(2,1)S(1)} %bitcast.10, bf16[3,256,256]{2,1,0:T(8,128)(2,1)} %bitcast.12, s32[3,4]{1,0:T(4,128)} %offsets_hbm.1), custom_call_target="tpu_custom_call" | custom-call | flops 805306368 | bytes 5242880 | tf_op jit(solution)/shard_map/inner_products/pallas_call | solution.py:303
  6.9 1.6 %collective-permute-start.3 = (bf16[3,256,256]{2,1,0:T(8,128)(2,1)}, bf16[3,256,256]{2,1,0:T(8,128)(2,1)S(1)}, u32[]{:S(2)}, u32[]{:S(2)}) collective-permute-start(bf16[3,256,256]{2,1,0:T(8,128)(2,1)} %bitcast.13), channel_id=1, source_target_pairs={{0,8},{4,20},{8,0},{12,28},{16,24},{20,4},{24,16},{28,12},{1,9},{5... | collective-permute-start | bytes 1179656 | tf_op jit(solution)/shard_map/ppermute | solution.py:20
  8.5 1.5 %collective-permute-done.1.rest_2_ = bf16[3,256,256]{2,1,0:T(8,128)(2,1)S(1)} collective-permute-done((bf16[3,256,256]{2,1,0:T(8,128)(2,1)}, bf16[3,256,256]{2,1,0:T(8,128)(2,1)S(1)}, u32[]{:S(2)}, u32[]{:S(2)}) %collective-permute-start.1) | collective-permute-done | bytes 393248 | tf_op jit(solution)/shard_map/ppermute | solution.py:20
  10.0 3.5 %collective-permute-start.5 = (bf16[3,256,256]{2,1,0:T(8,128)(2,1)S(1)}, bf16[3,256,256]{2,1,0:T(8,128)(2,1)S(1)}, u32[]{:S(2)}, u32[]{:S(2)}) collective-permute-start(bf16[3,256,256]{2,1,0:T(8,128)(2,1)S(1)} %collective-permute-done.1.rest_2_), channel_id=1, source_target_pairs={{0,8},{4,20},{8,0},{12,28},{16,24},{20,4},{24,16},{28,12},{1,9},{5... | collective-permute-start | bytes 1179656 | tf_op jit(solution)/shard_map/ppermute | solution.py:20
  13.5 1.4 %collective-permute-done.3.rest_4_ = bf16[3,256,256]{2,1,0:T(8,128)(2,1)S(1)} collective-permute-done((bf16[3,256,256]{2,1,0:T(8,128)(2,1)}, bf16[3,256,256]{2,1,0:T(8,128)(2,1)S(1)}, u32[]{:S(2)}, u32[]{:S(2)}) %collective-permute-start.3) | collective-permute-done | bytes 393248 | tf_op jit(solution)/shard_map/ppermute | solution.py:20
  15.5 3.8 %collective-permute-done.5.rest_6_ = bf16[3,256,256]{2,1,0:T(8,128)(2,1)S(1)} collective-permute-done((bf16[3,256,256]{2,1,0:T(8,128)(2,1)S(1)}, bf16[3,256,256]{2,1,0:T(8,128)(2,1)S(1)}, u32[]{:S(2)}, u32[]{:S(2)}) %collective-permute-start.5) | collective-permute-done | bytes 393248 | tf_op jit(solution)/shard_map/ppermute | solution.py:20
  19.3 1.5 %early_products.1 = (f32[2,2,256,256]{3,2,1,0:T(8,128)S(1)}, f32[8,128]{1,0:T(8,128)S(1)}, bf16[8,3,256,256]{3,2,1,0:T(8,128)(2,1)S(1)}) custom-call(s32[3,4]{1,0:T(4,128)S(1)} %get-tuple-element.22.offsets, bf16[2,4,256,256]{3,2,1,0:T(8,128)(2,1)S(1)} %bitcast.7, bf16[2,4,256,768]{3,2,1,0:T(8,128)(2,1)S(1)} %get-tuple-element.23.inner, ...), custom_call_target="tpu_custom_call" | custom-call | flops 402653184 | bytes 4194304 | tf_op jit(solution)/shard_map/early_products/pallas_call | solution.py:334
  21.0 0.7 %late_products.1 = (f32[2,2,2,64,256]{4,3,2,1,0:T(8,128)S(1)}, bf16[2,2,2,64,256]{4,3,2,1,0:T(8,128)(2,1)S(1)}, f32[8,128]{1,0:T(8,128)S(1)}) custom-call(s32[3,4]{1,0:T(4,128)S(1)} %get-tuple-element.22.offsets, bf16[2,4,256,256]{3,2,1,0:T(8,128)(2,1)S(1)} %bitcast.8, bf16[2,4,256,768]{3,2,1,0:T(8,128)(2,1)S(1)} %get-tuple-element.23.inner, ...), custom_call_target="tpu_custom_call" | custom-call | flops 50331648 | bytes 1048576 | tf_op jit(solution)/shard_map/late_products/pallas_call | solution.py:351
  21.7 1.5 %collective-permute-start.7 = (bf16[2,2,2,64,256]{4,3,2,1,0:T(8,128)(2,1)S(1)}, bf16[2,2,2,64,256]{4,3,2,1,0:T(8,128)(2,1)S(1)}, u32[]{:S(2)}, u32[]{:S(2)}) collective-permute-start(bf16[2,2,2,64,256]{4,3,2,1,0:T(8,128)(2,1)S(1)} %get-tuple-element.30), channel_id=1, source_target_pairs={{0,1},{1,0},{2,3},{3,2},{4,5},{5,4},{6,7},{7,6},{8,9},{9,8},{10,11... | collective-permute-start | bytes 786440 | tf_op jit(solution)/shard_map/ppermute | solution.py:20
  23.2 1.9 %second_products.1 = (f32[2,2,2,64,256]{4,3,2,1,0:T(8,128)S(1)}, bf16[2,2,2,64,256]{4,3,2,1,0:T(8,128)(2,1)S(1)}, f32[8,128]{1,0:T(8,128)S(1)}) custom-call(s32[3,4]{1,0:T(4,128)S(1)} %get-tuple-element.22.offsets, bf16[2,4,256,256]{3,2,1,0:T(8,128)(2,1)S(1)} %bitcast.9, bf16[2,4,256,768]{3,2,1,0:T(8,128)(2,1)S(1)} %get-tuple-element.23.inner, ...), custom_call_target="tpu_custom_call" | custom-call | flops 402653184 | bytes 1048576 | tf_op jit(solution)/shard_map/second_products/pallas_call | solution.py:351
  25.1 0.8 %collective-permute-start.9 = (bf16[2,2,2,64,256]{4,3,2,1,0:T(8,128)(2,1)S(1)}, bf16[2,2,2,64,256]{4,3,2,1,0:T(8,128)(2,1)S(1)}, u32[]{:S(2)}, u32[]{:S(2)}) collective-permute-start(bf16[2,2,2,64,256]{4,3,2,1,0:T(8,128)(2,1)S(1)} %get-tuple-element.36), channel_id=1, source_target_pairs={{0,1},{1,0},{2,3},{3,2},{4,5},{5,4},{6,7},{7,6},{8,9},{9,8},{10,11... | collective-permute-start | bytes 786440 | tf_op jit(solution)/shard_map/ppermute | solution.py:20
  25.9 1.2 %collective-permute-done.10 = f32[8,128]{1,0:T(8,128)S(1)} collective-permute-done((f32[8,128]{1,0:T(8,128)S(1)}, f32[8,128]{1,0:T(8,128)S(1)}, u32[]{:S(2)}, u32[]{:S(2)}) %collective-permute-start.10) | collective-permute-done | bytes 4128 | tf_op jit(solution)/shard_map/ppermute | solution.py:20
  27.1 1.9 %collective-permute-start.11 = (f32[8,128]{1,0:T(8,128)S(1)}, f32[8,128]{1,0:T(8,128)S(1)}, u32[]{:S(2)}, u32[]{:S(2)}) collective-permute-start(f32[8,128]{1,0:T(8,128)S(1)} %add.15), channel_id=1, source_target_pairs={{0,8},{4,12},{8,0},{12,4},{16,24},{20,28},{24,16},{28,20},{1,9},{5... | collective-permute-start | bytes 12296 | tf_op jit(solution)/shard_map/ppermute | solution.py:20
  29.0 1.3 %collective-permute-start.12 = (f32[8,128]{1,0:T(8,128)S(1)}, f32[8,128]{1,0:T(8,128)S(1)}, u32[]{:S(2)}, u32[]{:S(2)}) collective-permute-start(f32[8,128]{1,0:T(8,128)S(1)} %add.15), channel_id=1, source_target_pairs={{0,16},{4,20},{8,24},{12,28},{16,0},{20,4},{24,8},{28,12},{1,17},{... | collective-permute-start | bytes 12296 | tf_op jit(solution)/shard_map/ppermute | solution.py:20
  31.0 2.5 %collective-permute-start.8 = (bf16[1,2,2,64,256]{4,3,2,1,0:T(8,128)(2,1)S(1)}, bf16[1,2,2,64,256]{4,3,2,1,0:T(8,128)(2,1)S(1)}, u32[]{:S(2)}, u32[]{:S(2)}) collective-permute-start(bf16[1,2,2,64,256]{4,3,2,1,0:T(8,128)(2,1)S(1)} %get-tuple-element.32), channel_id=1, source_target_pairs={{0,2},{1,3},{2,0},{3,1},{4,6},{5,7},{6,4},{7,5},{8,10},{9,11},{10,... | collective-permute-start | bytes 393224 | tf_op jit(solution)/shard_map/ppermute | solution.py:20
  33.5 1.3 %collective-permute-done.13 = f32[8,128]{1,0:T(8,128)S(1)} collective-permute-done((f32[8,128]{1,0:T(8,128)S(1)}, f32[8,128]{1,0:T(8,128)S(1)}, u32[]{:S(2)}, u32[]{:S(2)}) %collective-permute-start.13) | collective-permute-done | bytes 4128 | tf_op jit(solution)/shard_map/ppermute | solution.py:20
  34.8 1.8 %collective-permute-start.14 = (f32[8,128]{1,0:T(8,128)S(1)}, f32[8,128]{1,0:T(8,128)S(1)}, u32[]{:S(2)}, u32[]{:S(2)}) collective-permute-start(f32[8,128]{1,0:T(8,128)S(1)} %add_add_fusion), channel_id=1, source_target_pairs={{0,1},{1,0},{2,3},{3,2},{4,5},{5,4},{6,7},{7,6},{8,9},{9,8},{10,11... | collective-permute-start | bytes 12296 | tf_op jit(solution)/shard_map/ppermute | solution.py:20
  36.7 2.7 %collective-permute-done.14 = f32[8,128]{1,0:T(8,128)S(1)} collective-permute-done((f32[8,128]{1,0:T(8,128)S(1)}, f32[8,128]{1,0:T(8,128)S(1)}, u32[]{:S(2)}, u32[]{:S(2)}) %collective-permute-start.14) | collective-permute-done | bytes 4128 | tf_op jit(solution)/shard_map/ppermute | solution.py:20
  39.5 2.5 %collective-permute-start.15 = (bf16[272,256]{1,0:T(8,128)(2,1)S(1)}, bf16[272,256]{1,0:T(8,128)(2,1)S(1)}, u32[]{:S(2)}, u32[]{:S(2)}) collective-permute-start(bf16[272,256]{1,0:T(8,128)(2,1)S(1)} %get-tuple-element.39), channel_id=1, source_target_pairs={{0,2},{1,3},{2,0},{3,1},{4,6},{5,7},{6,4},{7,5},{8,10},{9,11},{10,... | collective-permute-start | bytes 417800 | tf_op jit(solution)/shard_map/ppermute | solution.py:20
  42.0 7.0 %collective-permute-done.15.refs_2_ = bf16[272,256]{1,0:T(8,128)(2,1)S(1)} collective-permute-done((bf16[272,256]{1,0:T(8,128)(2,1)S(1)}, bf16[272,256]{1,0:T(8,128)(2,1)S(1)}, u32[]{:S(2)}, u32[]{:S(2)}) %collective-permute-start.15) | collective-permute-done | bytes 139296 | tf_op jit(solution)/shard_map/ppermute | solution.py:20
  49.1 0.7 %finish.1 = (bf16[2,4,64,256]{3,2,1,0:T(8,128)(2,1)}, f32[2,2]{1,0:T(2,128)}) custom-call(bf16[2,2,64,256]{3,2,1,0:T(8,128)(2,1)S(1)} %add_last_share.1.refs_0_, f32[1,2,2,64,256]{4,3,2,1,0:T(8,128)S(1)} %get-tuple-element.38.refs_1_, bf16[272,256]{1,0:T(8,128)(2,1)S(1)} %collective-permute-done.15.refs_2_, f32[8,128]{1,0:T(8,128)S(1)} %add.19.tile.refs_3_), custom_call_target="tpu_custom_call" | custom-call | flops 1 | bytes 1 | tf_op jit(solution)/shard_map/finish/pallas_call | solution.py:444
  (23 shorter events, 1.5 us)
Async XLA Ops:
  0.6 9.4 %collective-permute-start.1 = (bf16[3,256,256]{2,1,0:T(8,128)(2,1)}, bf16[3,256,256]{2,1,0:T(8,128)(2,1)S(1)}, u32[]{:S(2)}, u32[]{:S(2)}) collective-permute-start(bf16[3,256,256]{2,1,0:T(8,128)(2,1)} %bitcast.11), channel_id=1, source_target_pairs={{0,16},{4,12},{8,24},{12,4},{16,0},{20,28},{24,8},{28,20},{1,17},{... | collective-permute-start | bytes 1179656 | tf_op jit(solution)/shard_map/ppermute | solution.py:20
  3.7 1.2 %copy-start = (bf16[2,1,4,256,256]{4,3,2,1,0:T(8,128)(2,1)S(1)}, bf16[2,1,4,256,256]{4,3,2,1,0:T(8,128)(2,1)}, u32[]{:S(2)}) copy-start(bf16[2,1,4,256,256]{4,3,2,1,0:T(8,128)(2,1)} %param.4) | copy-start | bytes 3145732
  4.9 1.0 %copy-start.1 = (bf16[3,1,256,256]{3,2,1,0:T(8,128)(2,1)S(1)}, bf16[3,1,256,256]{3,2,1,0:T(8,128)(2,1)}, u32[]{:S(2)}) copy-start(bf16[3,1,256,256]{3,2,1,0:T(8,128)(2,1)} %param.5) | copy-start | bytes 1179652
  6.9 8.1 %collective-permute-start.3 = (bf16[3,256,256]{2,1,0:T(8,128)(2,1)}, bf16[3,256,256]{2,1,0:T(8,128)(2,1)S(1)}, u32[]{:S(2)}, u32[]{:S(2)}) collective-permute-start(bf16[3,256,256]{2,1,0:T(8,128)(2,1)} %bitcast.13), channel_id=1, source_target_pairs={{0,8},{4,20},{8,0},{12,28},{16,24},{20,4},{24,16},{28,12},{1,9},{5... | collective-permute-start | bytes 1179656 | tf_op jit(solution)/shard_map/ppermute | solution.py:20
  10.0 9.3 %collective-permute-start.5 = (bf16[3,256,256]{2,1,0:T(8,128)(2,1)S(1)}, bf16[3,256,256]{2,1,0:T(8,128)(2,1)S(1)}, u32[]{:S(2)}, u32[]{:S(2)}) collective-permute-start(bf16[3,256,256]{2,1,0:T(8,128)(2,1)S(1)} %collective-permute-done.1.rest_2_), channel_id=1, source_target_pairs={{0,8},{4,20},{8,0},{12,28},{16,24},{20,4},{24,16},{28,12},{1,9},{5... | collective-permute-start | bytes 1179656 | tf_op jit(solution)/shard_map/ppermute | solution.py:20
  13.5 5.8 %collective-permute-start = (bf16[3,256,256]{2,1,0:T(8,128)(2,1)}, bf16[3,256,256]{2,1,0:T(8,128)(2,1)S(1)}, u32[]{:S(2)}, u32[]{:S(2)}) collective-permute-start(bf16[3,256,256]{2,1,0:T(8,128)(2,1)} %bitcast.14), channel_id=1, source_target_pairs={{0,4},{4,0},{8,12},{12,8},{16,20},{20,16},{24,28},{28,24},{1,5},{5... | collective-permute-start | bytes 1179656 | tf_op jit(solution)/shard_map/ppermute | solution.py:20
  15.0 4.3 %collective-permute-start.4 = (bf16[3,256,256]{2,1,0:T(8,128)(2,1)S(1)}, bf16[3,256,256]{2,1,0:T(8,128)(2,1)S(1)}, u32[]{:S(2)}, u32[]{:S(2)}) collective-permute-start(bf16[3,256,256]{2,1,0:T(8,128)(2,1)S(1)} %collective-permute-done.3.rest_4_), channel_id=1, source_target_pairs={{0,4},{4,0},{8,12},{12,8},{16,20},{20,16},{24,28},{28,24},{1,5},{5... | collective-permute-start | bytes 1179656 | tf_op jit(solution)/shard_map/ppermute | solution.py:20
  15.0 4.3 %collective-permute-start.2 = (bf16[3,256,256]{2,1,0:T(8,128)(2,1)S(1)}, bf16[3,256,256]{2,1,0:T(8,128)(2,1)S(1)}, u32[]{:S(2)}, u32[]{:S(2)}) collective-permute-start(bf16[3,256,256]{2,1,0:T(8,128)(2,1)S(1)} %collective-permute-done.1.rest_2_), channel_id=1, source_target_pairs={{0,4},{4,0},{8,12},{12,8},{16,20},{20,16},{24,28},{28,24},{1,5},{5... | collective-permute-start | bytes 1179656 | tf_op jit(solution)/shard_map/ppermute | solution.py:20
  19.3 1.7 %collective-permute-start.6 = (bf16[3,256,256]{2,1,0:T(8,128)(2,1)S(1)}, bf16[3,256,256]{2,1,0:T(8,128)(2,1)S(1)}, u32[]{:S(2)}, u32[]{:S(2)}) collective-permute-start(bf16[3,256,256]{2,1,0:T(8,128)(2,1)S(1)} %collective-permute-done.5.rest_6_), channel_id=1, source_target_pairs={{0,4},{4,0},{8,12},{12,8},{16,20},{20,16},{24,28},{28,24},{1,5},{5... | collective-permute-start | bytes 1179656 | tf_op jit(solution)/shard_map/ppermute | solution.py:20
  21.7 9.2 %collective-permute-start.7 = (bf16[2,2,2,64,256]{4,3,2,1,0:T(8,128)(2,1)S(1)}, bf16[2,2,2,64,256]{4,3,2,1,0:T(8,128)(2,1)S(1)}, u32[]{:S(2)}, u32[]{:S(2)}) collective-permute-start(bf16[2,2,2,64,256]{4,3,2,1,0:T(8,128)(2,1)S(1)} %get-tuple-element.30), channel_id=1, source_target_pairs={{0,1},{1,0},{2,3},{3,2},{4,5},{5,4},{6,7},{7,6},{8,9},{9,8},{10,11... | collective-permute-start | bytes 786440 | tf_op jit(solution)/shard_map/ppermute | solution.py:20
  25.1 14.3 %collective-permute-start.9 = (bf16[2,2,2,64,256]{4,3,2,1,0:T(8,128)(2,1)S(1)}, bf16[2,2,2,64,256]{4,3,2,1,0:T(8,128)(2,1)S(1)}, u32[]{:S(2)}, u32[]{:S(2)}) collective-permute-start(bf16[2,2,2,64,256]{4,3,2,1,0:T(8,128)(2,1)S(1)} %get-tuple-element.36), channel_id=1, source_target_pairs={{0,1},{1,0},{2,3},{3,2},{4,5},{5,4},{6,7},{7,6},{8,9},{9,8},{10,11... | collective-permute-start | bytes 786440 | tf_op jit(solution)/shard_map/ppermute | solution.py:20
  25.9 1.2 %collective-permute-start.10 = (f32[8,128]{1,0:T(8,128)S(1)}, f32[8,128]{1,0:T(8,128)S(1)}, u32[]{:S(2)}, u32[]{:S(2)}) collective-permute-start(f32[8,128]{1,0:T(8,128)S(1)} %get-tuple-element.37), channel_id=1, source_target_pairs={{0,4},{4,0},{8,12},{12,8},{16,20},{20,16},{24,28},{28,24},{1,5},{5... | collective-permute-start | bytes 12296 | tf_op jit(solution)/shard_map/ppermute | solution.py:20
  27.1 6.5 %collective-permute-start.11 = (f32[8,128]{1,0:T(8,128)S(1)}, f32[8,128]{1,0:T(8,128)S(1)}, u32[]{:S(2)}, u32[]{:S(2)}) collective-permute-start(f32[8,128]{1,0:T(8,128)S(1)} %add.15), channel_id=1, source_target_pairs={{0,8},{4,12},{8,0},{12,4},{16,24},{20,28},{24,16},{28,20},{1,9},{5... | collective-permute-start | bytes 12296 | tf_op jit(solution)/shard_map/ppermute | solution.py:20
  29.0 4.5 %collective-permute-start.12 = (f32[8,128]{1,0:T(8,128)S(1)}, f32[8,128]{1,0:T(8,128)S(1)}, u32[]{:S(2)}, u32[]{:S(2)}) collective-permute-start(f32[8,128]{1,0:T(8,128)S(1)} %add.15), channel_id=1, source_target_pairs={{0,16},{4,20},{8,24},{12,28},{16,0},{20,4},{24,8},{28,12},{1,17},{... | collective-permute-start | bytes 12296 | tf_op jit(solution)/shard_map/ppermute | solution.py:20
  30.3 4.5 %collective-permute-start.13 = (f32[8,128]{1,0:T(8,128)S(1)}, f32[8,128]{1,0:T(8,128)S(1)}, u32[]{:S(2)}, u32[]{:S(2)}) collective-permute-start(f32[8,128]{1,0:T(8,128)S(1)} %add.15), channel_id=1, source_target_pairs={{0,24},{4,28},{8,16},{12,20},{16,8},{20,12},{24,0},{28,4},{1,25},{... | collective-permute-start | bytes 12296 | tf_op jit(solution)/shard_map/ppermute | solution.py:20
  31.0 11.0 %collective-permute-start.8 = (bf16[1,2,2,64,256]{4,3,2,1,0:T(8,128)(2,1)S(1)}, bf16[1,2,2,64,256]{4,3,2,1,0:T(8,128)(2,1)S(1)}, u32[]{:S(2)}, u32[]{:S(2)}) collective-permute-start(bf16[1,2,2,64,256]{4,3,2,1,0:T(8,128)(2,1)S(1)} %get-tuple-element.32), channel_id=1, source_target_pairs={{0,2},{1,3},{2,0},{3,1},{4,6},{5,7},{6,4},{7,5},{8,10},{9,11},{10,... | collective-permute-start | bytes 393224 | tf_op jit(solution)/shard_map/ppermute | solution.py:20
  34.8 4.6 %collective-permute-start.14 = (f32[8,128]{1,0:T(8,128)S(1)}, f32[8,128]{1,0:T(8,128)S(1)}, u32[]{:S(2)}, u32[]{:S(2)}) collective-permute-start(f32[8,128]{1,0:T(8,128)S(1)} %add_add_fusion), channel_id=1, source_target_pairs={{0,1},{1,0},{2,3},{3,2},{4,5},{5,4},{6,7},{7,6},{8,9},{9,8},{10,11... | collective-permute-start | bytes 12296 | tf_op jit(solution)/shard_map/ppermute | solution.py:20
  39.5 9.6 %collective-permute-start.15 = (bf16[272,256]{1,0:T(8,128)(2,1)S(1)}, bf16[272,256]{1,0:T(8,128)(2,1)S(1)}, u32[]{:S(2)}, u32[]{:S(2)}) collective-permute-start(bf16[272,256]{1,0:T(8,128)(2,1)S(1)} %get-tuple-element.39), channel_id=1, source_target_pairs={{0,2},{1,3},{2,0},{3,1},{4,6},{5,7},{6,4},{7,5},{8,10},{9,11},{10,... | collective-permute-start | bytes 417800 | tf_op jit(solution)/shard_map/ppermute | solution.py:20

commit v20 on v19

--- a/solution.py
+++ b/solution.py
@@ -155,7 +155,10 @@
             for term in range(last.shape[0])
         ]
         lacking = functools.reduce(jnp.logical_or, lacks)
-        write_shares(partial.at[pair], pair, keep, send)
+
+        @pl.when(jnp.logical_not(lacking))
+        def _():
+            write_shares(partial.at[pair], pair, keep, send)
 
         @pl.when(lacking)
         def _():

time: 49.5 us -> 48.8 us (0.986); the launches traced: 49.8 us -> 47.8 us
  waiting for transfers between devices: 19.5 us -> 18 us
  starting transfers between devices: 21.3 us -> 20.6 us
    ppermute x16, waiting for transfers between devices: 19.5 us -> 18 us  [swap(): lax.ppermute(value, axis, [(place, place ^ masks[place & 1]) for place in...]
    ppermute x16, starting transfers between devices: 21.3 us -> 20.6 us  [swap(): lax.ppermute(value, axis, [(place, place ^ masks[place & 1]) for place in...]
where the time goes in v20:
time: 48.8 us; the launch traced here: 47.8 us
  starting transfers between devices  20.6 us (42%)
  waiting for transfers between devices  18 us (37%)
  Pallas kernels  6.37 us (13%)
  local copies, waits for them, and re-layouts  2.22 us (5%)
  between operations  0.68 us (1%)
    ppermute x16, starting transfers between devices, swap(): lax.ppermute(value, axis, [(place, place ^ masks[place & 1]) for place in...  20.6 us
    ppermute x16, waiting for transfers between devices, swap(): lax.ppermute(value, axis, [(place, place ^ masks[place & 1]) for place in...  18 us
    pallas_call x2, Pallas kernels, sums_of(): call(kernel, name, flops, MIB, 12 * MIB, out_shape=(share_of(shares // 2,...  2.99 us
    unnamed x4, local copies, waits for them, and re-layouts  2.22 us
    pallas_call x1, Pallas kernels, local(): call(functools.partial(early_kernel, sectors), 'early_products', 2 * term...  1.49 us
    pallas_call x1, Pallas kernels, local(): call(functools.partial(inner_kernel, 1.0 / shares), 'inner_products', 2 *...  1.03 us
  transfers between devices with their start and end apart: 16, of which 9 were waited for; matrix products, arithmetic and copies ran while one was open for 0% of the time, Pallas kernels for 9%

profile of v20, /device:TPU:0, one launch (start us, length us, event | category | flops | bytes accessed | tf_op | source)
XLA Modules:
  0.0 47.8 jit_solution(4262520500589302379)
XLA Ops:
  0.6 3.0 %collective-permute-start.1 = (bf16[3,256,256]{2,1,0:T(8,128)(2,1)}, bf16[3,256,256]{2,1,0:T(8,128)(2,1)S(1)}, u32[]{:S(2)}, u32[]{:S(2)}) collective-permute-start(bf16[3,256,256]{2,1,0:T(8,128)(2,1)} %bitcast.11), channel_id=1, source_target_pairs={{0,16},{4,12},{8,24},{12,4},{16,0},{20,28},{24,8},{28,20},{1,17},{... | collective-permute-start | bytes 1179656 | tf_op jit(solution)/shard_map/ppermute | solution.py:20
  3.7 1.2 %copy-done = bf16[2,1,4,256,256]{4,3,2,1,0:T(8,128)(2,1)S(1)} copy-done((bf16[2,1,4,256,256]{4,3,2,1,0:T(8,128)(2,1)S(1)}, bf16[2,1,4,256,256]{4,3,2,1,0:T(8,128)(2,1)}, u32[]{:S(2)}) %copy-start) | copy-done | bytes 1048600
  4.9 1.0 %copy-done.1 = bf16[3,1,256,256]{3,2,1,0:T(8,128)(2,1)S(1)} copy-done((bf16[3,1,256,256]{3,2,1,0:T(8,128)(2,1)S(1)}, bf16[3,1,256,256]{3,2,1,0:T(8,128)(2,1)}, u32[]{:S(2)}) %copy-start.1) | copy-done | bytes 393240
  5.9 1.0 %inner_products.1 = (bf16[2,4,256,768]{3,2,1,0:T(8,128)(2,1)S(1)}, f32[8,128]{1,0:T(8,128)S(1)}, bf16[3,256,256]{2,1,0:T(8,128)(2,1)S(1)}, s32[3,4]{1,0:T(4,128)S(1)}) custom-call(bf16[2,4,256,256]{3,2,1,0:T(8,128)(2,1)S(1)} %bitcast.6, bf16[3,256,256]{2,1,0:T(8,128)(2,1)S(1)} %bitcast.10, bf16[3,256,256]{2,1,0:T(8,128)(2,1)} %bitcast.12, s32[3,4]{1,0:T(4,128)} %offsets_hbm.1), custom_call_target="tpu_custom_call" | custom-call | flops 805306368 | bytes 5242880 | tf_op jit(solution)/shard_map/inner_products/pallas_call | solution.py:306
  6.9 1.6 %collective-permute-start.3 = (bf16[3,256,256]{2,1,0:T(8,128)(2,1)}, bf16[3,256,256]{2,1,0:T(8,128)(2,1)S(1)}, u32[]{:S(2)}, u32[]{:S(2)}) collective-permute-start(bf16[3,256,256]{2,1,0:T(8,128)(2,1)} %bitcast.13), channel_id=1, source_target_pairs={{0,8},{4,20},{8,0},{12,28},{16,24},{20,4},{24,16},{28,12},{1,9},{5... | collective-permute-start | bytes 1179656 | tf_op jit(solution)/shard_map/ppermute | solution.py:20
  8.5 1.5 %collective-permute-done.1.rest_2_ = bf16[3,256,256]{2,1,0:T(8,128)(2,1)S(1)} collective-permute-done((bf16[3,256,256]{2,1,0:T(8,128)(2,1)}, bf16[3,256,256]{2,1,0:T(8,128)(2,1)S(1)}, u32[]{:S(2)}, u32[]{:S(2)}) %collective-permute-start.1) | collective-permute-done | bytes 393248 | tf_op jit(solution)/shard_map/ppermute | solution.py:20
  10.0 3.5 %collective-permute-start.5 = (bf16[3,256,256]{2,1,0:T(8,128)(2,1)S(1)}, bf16[3,256,256]{2,1,0:T(8,128)(2,1)S(1)}, u32[]{:S(2)}, u32[]{:S(2)}) collective-permute-start(bf16[3,256,256]{2,1,0:T(8,128)(2,1)S(1)} %collective-permute-done.1.rest_2_), channel_id=1, source_target_pairs={{0,8},{4,20},{8,0},{12,28},{16,24},{20,4},{24,16},{28,12},{1,9},{5... | collective-permute-start | bytes 1179656 | tf_op jit(solution)/shard_map/ppermute | solution.py:20
  13.5 1.4 %collective-permute-done.3.rest_4_ = bf16[3,256,256]{2,1,0:T(8,128)(2,1)S(1)} collective-permute-done((bf16[3,256,256]{2,1,0:T(8,128)(2,1)}, bf16[3,256,256]{2,1,0:T(8,128)(2,1)S(1)}, u32[]{:S(2)}, u32[]{:S(2)}) %collective-permute-start.3) | collective-permute-done | bytes 393248 | tf_op jit(solution)/shard_map/ppermute | solution.py:20
  15.5 3.8 %collective-permute-done.5.rest_6_ = bf16[3,256,256]{2,1,0:T(8,128)(2,1)S(1)} collective-permute-done((bf16[3,256,256]{2,1,0:T(8,128)(2,1)S(1)}, bf16[3,256,256]{2,1,0:T(8,128)(2,1)S(1)}, u32[]{:S(2)}, u32[]{:S(2)}) %collective-permute-start.5) | collective-permute-done | bytes 393248 | tf_op jit(solution)/shard_map/ppermute | solution.py:20
  19.3 1.5 %early_products.1 = (f32[2,2,256,256]{3,2,1,0:T(8,128)S(1)}, f32[8,128]{1,0:T(8,128)S(1)}, bf16[8,3,256,256]{3,2,1,0:T(8,128)(2,1)S(1)}) custom-call(s32[3,4]{1,0:T(4,128)S(1)} %get-tuple-element.22.offsets, bf16[2,4,256,256]{3,2,1,0:T(8,128)(2,1)S(1)} %bitcast.7, bf16[2,4,256,768]{3,2,1,0:T(8,128)(2,1)S(1)} %get-tuple-element.23.inner, ...), custom_call_target="tpu_custom_call" | custom-call | flops 402653184 | bytes 4194304 | tf_op jit(solution)/shard_map/early_products/pallas_call | solution.py:337
  21.0 1.3 %late_products.1 = (f32[2,2,2,64,256]{4,3,2,1,0:T(8,128)S(1)}, bf16[2,2,2,64,256]{4,3,2,1,0:T(8,128)(2,1)S(1)}, f32[8,128]{1,0:T(8,128)S(1)}) custom-call(s32[3,4]{1,0:T(4,128)S(1)} %get-tuple-element.22.offsets, bf16[2,4,256,256]{3,2,1,0:T(8,128)(2,1)S(1)} %bitcast.8, bf16[2,4,256,768]{3,2,1,0:T(8,128)(2,1)S(1)} %get-tuple-element.23.inner, ...), custom_call_target="tpu_custom_call" | custom-call | flops 50331648 | bytes 1048576 | tf_op jit(solution)/shard_map/late_products/pallas_call | solution.py:354
  22.3 1.2 %collective-permute-start.7 = (bf16[2,2,2,64,256]{4,3,2,1,0:T(8,128)(2,1)S(1)}, bf16[2,2,2,64,256]{4,3,2,1,0:T(8,128)(2,1)S(1)}, u32[]{:S(2)}, u32[]{:S(2)}) collective-permute-start(bf16[2,2,2,64,256]{4,3,2,1,0:T(8,128)(2,1)S(1)} %get-tuple-element.30), channel_id=1, source_target_pairs={{0,1},{1,0},{2,3},{3,2},{4,5},{5,4},{6,7},{7,6},{8,9},{9,8},{10,11... | collective-permute-start | bytes 786440 | tf_op jit(solution)/shard_map/ppermute | solution.py:20
  23.5 1.7 %second_products.1 = (f32[2,2,2,64,256]{4,3,2,1,0:T(8,128)S(1)}, bf16[2,2,2,64,256]{4,3,2,1,0:T(8,128)(2,1)S(1)}, f32[8,128]{1,0:T(8,128)S(1)}) custom-call(s32[3,4]{1,0:T(4,128)S(1)} %get-tuple-element.22.offsets, bf16[2,4,256,256]{3,2,1,0:T(8,128)(2,1)S(1)} %bitcast.9, bf16[2,4,256,768]{3,2,1,0:T(8,128)(2,1)S(1)} %get-tuple-element.23.inner, ...), custom_call_target="tpu_custom_call" | custom-call | flops 402653184 | bytes 1048576 | tf_op jit(solution)/shard_map/second_products/pallas_call | solution.py:354
  25.2 0.9 %collective-permute-start.9 = (bf16[2,2,2,64,256]{4,3,2,1,0:T(8,128)(2,1)S(1)}, bf16[2,2,2,64,256]{4,3,2,1,0:T(8,128)(2,1)S(1)}, u32[]{:S(2)}, u32[]{:S(2)}) collective-permute-start(bf16[2,2,2,64,256]{4,3,2,1,0:T(8,128)(2,1)S(1)} %get-tuple-element.36), channel_id=1, source_target_pairs={{0,1},{1,0},{2,3},{3,2},{4,5},{5,4},{6,7},{7,6},{8,9},{9,8},{10,11... | collective-permute-start | bytes 786440 | tf_op jit(solution)/shard_map/ppermute | solution.py:20
  26.1 1.2 %collective-permute-done.10 = f32[8,128]{1,0:T(8,128)S(1)} collective-permute-done((f32[8,128]{1,0:T(8,128)S(1)}, f32[8,128]{1,0:T(8,128)S(1)}, u32[]{:S(2)}, u32[]{:S(2)}) %collective-permute-start.10) | collective-permute-done | bytes 4128 | tf_op jit(solution)/shard_map/ppermute | solution.py:20
  27.2 2.0 %collective-permute-start.11 = (f32[8,128]{1,0:T(8,128)S(1)}, f32[8,128]{1,0:T(8,128)S(1)}, u32[]{:S(2)}, u32[]{:S(2)}) collective-permute-start(f32[8,128]{1,0:T(8,128)S(1)} %add.15), channel_id=1, source_target_pairs={{0,8},{4,12},{8,0},{12,4},{16,24},{20,28},{24,16},{28,20},{1,9},{5... | collective-permute-start | bytes 12296 | tf_op jit(solution)/shard_map/ppermute | solution.py:20
  29.3 1.3 %collective-permute-start.12 = (f32[8,128]{1,0:T(8,128)S(1)}, f32[8,128]{1,0:T(8,128)S(1)}, u32[]{:S(2)}, u32[]{:S(2)}) collective-permute-start(f32[8,128]{1,0:T(8,128)S(1)} %add.15), channel_id=1, source_target_pairs={{0,16},{4,20},{8,24},{12,28},{16,0},{20,4},{24,8},{28,12},{1,17},{... | collective-permute-start | bytes 12296 | tf_op jit(solution)/shard_map/ppermute | solution.py:20
  30.7 0.8 %collective-permute-done.7.received = bf16[2,2,2,64,256]{4,3,2,1,0:T(8,128)(2,1)S(1)} collective-permute-done((bf16[2,2,2,64,256]{4,3,2,1,0:T(8,128)(2,1)S(1)}, bf16[2,2,2,64,256]{4,3,2,1,0:T(8,128)(2,1)S(1)}, u32[]{:S(2)}, u32[]{:S(2)}) %collective-permute-start.7) | collective-permute-done | bytes 262176 | tf_op jit(solution)/shard_map/ppermute | solution.py:20
  31.6 2.5 %collective-permute-start.8 = (bf16[1,2,2,64,256]{4,3,2,1,0:T(8,128)(2,1)S(1)}, bf16[1,2,2,64,256]{4,3,2,1,0:T(8,128)(2,1)S(1)}, u32[]{:S(2)}, u32[]{:S(2)}) collective-permute-start(bf16[1,2,2,64,256]{4,3,2,1,0:T(8,128)(2,1)S(1)} %get-tuple-element.32), channel_id=1, source_target_pairs={{0,2},{1,3},{2,0},{3,1},{4,6},{5,7},{6,4},{7,5},{8,10},{9,11},{10,... | collective-permute-start | bytes 393224 | tf_op jit(solution)/shard_map/ppermute | solution.py:20
  34.2 0.9 %collective-permute-done.13 = f32[8,128]{1,0:T(8,128)S(1)} collective-permute-done((f32[8,128]{1,0:T(8,128)S(1)}, f32[8,128]{1,0:T(8,128)S(1)}, u32[]{:S(2)}, u32[]{:S(2)}) %collective-permute-start.13) | collective-permute-done | bytes 4128 | tf_op jit(solution)/shard_map/ppermute | solution.py:20
  35.1 1.3 %collective-permute-start.14 = (f32[8,128]{1,0:T(8,128)S(1)}, f32[8,128]{1,0:T(8,128)S(1)}, u32[]{:S(2)}, u32[]{:S(2)}) collective-permute-start(f32[8,128]{1,0:T(8,128)S(1)} %add_add_fusion), channel_id=1, source_target_pairs={{0,1},{1,0},{2,3},{3,2},{4,5},{5,4},{6,7},{7,6},{8,9},{9,8},{10,11... | collective-permute-start | bytes 12296 | tf_op jit(solution)/shard_map/ppermute | solution.py:20
  36.4 2.4 %collective-permute-done.14 = f32[8,128]{1,0:T(8,128)S(1)} collective-permute-done((f32[8,128]{1,0:T(8,128)S(1)}, f32[8,128]{1,0:T(8,128)S(1)}, u32[]{:S(2)}, u32[]{:S(2)}) %collective-permute-start.14) | collective-permute-done | bytes 4128 | tf_op jit(solution)/shard_map/ppermute | solution.py:20
  38.9 2.5 %collective-permute-start.15 = (bf16[272,256]{1,0:T(8,128)(2,1)S(1)}, bf16[272,256]{1,0:T(8,128)(2,1)S(1)}, u32[]{:S(2)}, u32[]{:S(2)}) collective-permute-start(bf16[272,256]{1,0:T(8,128)(2,1)S(1)} %get-tuple-element.39), channel_id=1, source_target_pairs={{0,2},{1,3},{2,0},{3,1},{4,6},{5,7},{6,4},{7,5},{8,10},{9,11},{10,... | collective-permute-start | bytes 417800 | tf_op jit(solution)/shard_map/ppermute | solution.py:20
  41.5 5.7 %collective-permute-done.15.refs_2_ = bf16[272,256]{1,0:T(8,128)(2,1)S(1)} collective-permute-done((bf16[272,256]{1,0:T(8,128)(2,1)S(1)}, bf16[272,256]{1,0:T(8,128)(2,1)S(1)}, u32[]{:S(2)}, u32[]{:S(2)}) %collective-permute-start.15) | collective-permute-done | bytes 139296 | tf_op jit(solution)/shard_map/ppermute | solution.py:20
  (23 shorter events, 1.8 us)
Async XLA Ops:
  0.6 9.4 %collective-permute-start.1 = (bf16[3,256,256]{2,1,0:T(8,128)(2,1)}, bf16[3,256,256]{2,1,0:T(8,128)(2,1)S(1)}, u32[]{:S(2)}, u32[]{:S(2)}) collective-permute-start(bf16[3,256,256]{2,1,0:T(8,128)(2,1)} %bitcast.11), channel_id=1, source_target_pairs={{0,16},{4,12},{8,24},{12,4},{16,0},{20,28},{24,8},{28,20},{1,17},{... | collective-permute-start | bytes 1179656 | tf_op jit(solution)/shard_map/ppermute | solution.py:20
  3.7 1.2 %copy-start = (bf16[2,1,4,256,256]{4,3,2,1,0:T(8,128)(2,1)S(1)}, bf16[2,1,4,256,256]{4,3,2,1,0:T(8,128)(2,1)}, u32[]{:S(2)}) copy-start(bf16[2,1,4,256,256]{4,3,2,1,0:T(8,128)(2,1)} %param.4) | copy-start | bytes 3145732
  4.9 1.0 %copy-start.1 = (bf16[3,1,256,256]{3,2,1,0:T(8,128)(2,1)S(1)}, bf16[3,1,256,256]{3,2,1,0:T(8,128)(2,1)}, u32[]{:S(2)}) copy-start(bf16[3,1,256,256]{3,2,1,0:T(8,128)(2,1)} %param.5) | copy-start | bytes 1179652
  6.9 8.1 %collective-permute-start.3 = (bf16[3,256,256]{2,1,0:T(8,128)(2,1)}, bf16[3,256,256]{2,1,0:T(8,128)(2,1)S(1)}, u32[]{:S(2)}, u32[]{:S(2)}) collective-permute-start(bf16[3,256,256]{2,1,0:T(8,128)(2,1)} %bitcast.13), channel_id=1, source_target_pairs={{0,8},{4,20},{8,0},{12,28},{16,24},{20,4},{24,16},{28,12},{1,9},{5... | collective-permute-start | bytes 1179656 | tf_op jit(solution)/shard_map/ppermute | solution.py:20
  10.0 9.3 %collective-permute-start.5 = (bf16[3,256,256]{2,1,0:T(8,128)(2,1)S(1)}, bf16[3,256,256]{2,1,0:T(8,128)(2,1)S(1)}, u32[]{:S(2)}, u32[]{:S(2)}) collective-permute-start(bf16[3,256,256]{2,1,0:T(8,128)(2,1)S(1)} %collective-permute-done.1.rest_2_), channel_id=1, source_target_pairs={{0,8},{4,20},{8,0},{12,28},{16,24},{20,4},{24,16},{28,12},{1,9},{5... | collective-permute-start | bytes 1179656 | tf_op jit(solution)/shard_map/ppermute | solution.py:20
  13.5 5.8 %collective-permute-start = (bf16[3,256,256]{2,1,0:T(8,128)(2,1)}, bf16[3,256,256]{2,1,0:T(8,128)(2,1)S(1)}, u32[]{:S(2)}, u32[]{:S(2)}) collective-permute-start(bf16[3,256,256]{2,1,0:T(8,128)(2,1)} %bitcast.14), channel_id=1, source_target_pairs={{0,4},{4,0},{8,12},{12,8},{16,20},{20,16},{24,28},{28,24},{1,5},{5... | collective-permute-start | bytes 1179656 | tf_op jit(solution)/shard_map/ppermute | solution.py:20
  15.0 4.3 %collective-permute-start.4 = (bf16[3,256,256]{2,1,0:T(8,128)(2,1)S(1)}, bf16[3,256,256]{2,1,0:T(8,128)(2,1)S(1)}, u32[]{:S(2)}, u32[]{:S(2)}) collective-permute-start(bf16[3,256,256]{2,1,0:T(8,128)(2,1)S(1)} %collective-permute-done.3.rest_4_), channel_id=1, source_target_pairs={{0,4},{4,0},{8,12},{12,8},{16,20},{20,16},{24,28},{28,24},{1,5},{5... | collective-permute-start | bytes 1179656 | tf_op jit(solution)/shard_map/ppermute | solution.py:20
  15.0 4.3 %collective-permute-start.2 = (bf16[3,256,256]{2,1,0:T(8,128)(2,1)S(1)}, bf16[3,256,256]{2,1,0:T(8,128)(2,1)S(1)}, u32[]{:S(2)}, u32[]{:S(2)}) collective-permute-start(bf16[3,256,256]{2,1,0:T(8,128)(2,1)S(1)} %collective-permute-done.1.rest_2_), channel_id=1, source_target_pairs={{0,4},{4,0},{8,12},{12,8},{16,20},{20,16},{24,28},{28,24},{1,5},{5... | collective-permute-start | bytes 1179656 | tf_op jit(solution)/shard_map/ppermute | solution.py:20
  19.3 1.7 %collective-permute-start.6 = (bf16[3,256,256]{2,1,0:T(8,128)(2,1)S(1)}, bf16[3,256,256]{2,1,0:T(8,128)(2,1)S(1)}, u32[]{:S(2)}, u32[]{:S(2)}) collective-permute-start(bf16[3,256,256]{2,1,0:T(8,128)(2,1)S(1)} %collective-permute-done.5.rest_6_), channel_id=1, source_target_pairs={{0,4},{4,0},{8,12},{12,8},{16,20},{20,16},{24,28},{28,24},{1,5},{5... | collective-permute-start | bytes 1179656 | tf_op jit(solution)/shard_map/ppermute | solution.py:20
  22.3 9.2 %collective-permute-start.7 = (bf16[2,2,2,64,256]{4,3,2,1,0:T(8,128)(2,1)S(1)}, bf16[2,2,2,64,256]{4,3,2,1,0:T(8,128)(2,1)S(1)}, u32[]{:S(2)}, u32[]{:S(2)}) collective-permute-start(bf16[2,2,2,64,256]{4,3,2,1,0:T(8,128)(2,1)S(1)} %get-tuple-element.30), channel_id=1, source_target_pairs={{0,1},{1,0},{2,3},{3,2},{4,5},{5,4},{6,7},{7,6},{8,9},{9,8},{10,11... | collective-permute-start | bytes 786440 | tf_op jit(solution)/shard_map/ppermute | solution.py:20
  25.2 13.6 %collective-permute-start.9 = (bf16[2,2,2,64,256]{4,3,2,1,0:T(8,128)(2,1)S(1)}, bf16[2,2,2,64,256]{4,3,2,1,0:T(8,128)(2,1)S(1)}, u32[]{:S(2)}, u32[]{:S(2)}) collective-permute-start(bf16[2,2,2,64,256]{4,3,2,1,0:T(8,128)(2,1)S(1)} %get-tuple-element.36), channel_id=1, source_target_pairs={{0,1},{1,0},{2,3},{3,2},{4,5},{5,4},{6,7},{7,6},{8,9},{9,8},{10,11... | collective-permute-start | bytes 786440 | tf_op jit(solution)/shard_map/ppermute | solution.py:20
  26.1 1.2 %collective-permute-start.10 = (f32[8,128]{1,0:T(8,128)S(1)}, f32[8,128]{1,0:T(8,128)S(1)}, u32[]{:S(2)}, u32[]{:S(2)}) collective-permute-start(f32[8,128]{1,0:T(8,128)S(1)} %get-tuple-element.37), channel_id=1, source_target_pairs={{0,4},{4,0},{8,12},{12,8},{16,20},{20,16},{24,28},{28,24},{1,5},{5... | collective-permute-start | bytes 12296 | tf_op jit(solution)/shard_map/ppermute | solution.py:20
  27.2 6.9 %collective-permute-start.11 = (f32[8,128]{1,0:T(8,128)S(1)}, f32[8,128]{1,0:T(8,128)S(1)}, u32[]{:S(2)}, u32[]{:S(2)}) collective-permute-start(f32[8,128]{1,0:T(8,128)S(1)} %add.15), channel_id=1, source_target_pairs={{0,8},{4,12},{8,0},{12,4},{16,24},{20,28},{24,16},{28,20},{1,9},{5... | collective-permute-start | bytes 12296 | tf_op jit(solution)/shard_map/ppermute | solution.py:20
  29.3 4.9 %collective-permute-start.12 = (f32[8,128]{1,0:T(8,128)S(1)}, f32[8,128]{1,0:T(8,128)S(1)}, u32[]{:S(2)}, u32[]{:S(2)}) collective-permute-start(f32[8,128]{1,0:T(8,128)S(1)} %add.15), channel_id=1, source_target_pairs={{0,16},{4,20},{8,24},{12,28},{16,0},{20,4},{24,8},{28,12},{1,17},{... | collective-permute-start | bytes 12296 | tf_op jit(solution)/shard_map/ppermute | solution.py:20
  30.6 4.5 %collective-permute-start.13 = (f32[8,128]{1,0:T(8,128)S(1)}, f32[8,128]{1,0:T(8,128)S(1)}, u32[]{:S(2)}, u32[]{:S(2)}) collective-permute-start(f32[8,128]{1,0:T(8,128)S(1)} %add.15), channel_id=1, source_target_pairs={{0,24},{4,28},{8,16},{12,20},{16,8},{20,12},{24,0},{28,4},{1,25},{... | collective-permute-start | bytes 12296 | tf_op jit(solution)/shard_map/ppermute | solution.py:20
  31.6 9.8 %collective-permute-start.8 = (bf16[1,2,2,64,256]{4,3,2,1,0:T(8,128)(2,1)S(1)}, bf16[1,2,2,64,256]{4,3,2,1,0:T(8,128)(2,1)S(1)}, u32[]{:S(2)}, u32[]{:S(2)}) collective-permute-start(bf16[1,2,2,64,256]{4,3,2,1,0:T(8,128)(2,1)S(1)} %get-tuple-element.32), channel_id=1, source_target_pairs={{0,2},{1,3},{2,0},{3,1},{4,6},{5,7},{6,4},{7,5},{8,10},{9,11},{10,... | collective-permute-start | bytes 393224 | tf_op jit(solution)/shard_map/ppermute | solution.py:20
  35.1 3.7 %collective-permute-start.14 = (f32[8,128]{1,0:T(8,128)S(1)}, f32[8,128]{1,0:T(8,128)S(1)}, u32[]{:S(2)}, u32[]{:S(2)}) collective-permute-start(f32[8,128]{1,0:T(8,128)S(1)} %add_add_fusion), channel_id=1, source_target_pairs={{0,1},{1,0},{2,3},{3,2},{4,5},{5,4},{6,7},{7,6},{8,9},{9,8},{10,11... | collective-permute-start | bytes 12296 | tf_op jit(solution)/shard_map/ppermute | solution.py:20
  38.9 8.2 %collective-permute-start.15 = (bf16[272,256]{1,0:T(8,128)(2,1)S(1)}, bf16[272,256]{1,0:T(8,128)(2,1)S(1)}, u32[]{:S(2)}, u32[]{:S(2)}) collective-permute-start(bf16[272,256]{1,0:T(8,128)(2,1)S(1)} %get-tuple-element.39), channel_id=1, source_target_pairs={{0,2},{1,3},{2,0},{3,1},{4,6},{5,7},{6,4},{7,5},{8,10},{9,11},{10,... | collective-permute-start | bytes 417800 | tf_op jit(solution)/shard_map/ppermute | solution.py:20

commit v21 on v20

--- a/solution.py
+++ b/solution.py
@@ -233,7 +233,7 @@
 
 
 def finish_kernel(*refs):
-    *done, kept, received, tile, products, rayleigh_hbm, rows, rayleigh, sems = refs
+    *done, kept, received, tile, near, far, products, rayleigh_hbm, rows, rayleigh, sems = refs
     copies, first = [], 0
     for part in [*done, rows]:
         target = products.at[:, pl.ds(first, part.shape[1])]
@@ -246,7 +246,7 @@
     rows[...] = (kept[0] + both).astype(jnp.bfloat16)
     copies[-1].start()
 
-    tile = tile[...] + ridden_tile(received)
+    tile = tile[...] + near[...] + far[...] + ridden_tile(received)
     trials = rayleigh.shape[0]
     row = lax.broadcasted_iota(jnp.int32, rayleigh.shape, 0)
     column = lax.broadcasted_iota(jnp.int32, rayleigh.shape, 1)
@@ -397,10 +397,11 @@
     for masks in [[1]] + steps_of(sectors, 1):
         tile = add_places(tile, "sec", masks)
 
-    step = 1
+    step = 2
     while 2 * step < shares:
         tile = add_places(tile, "term", [step])
         step *= 2
+    nearby = [swap(tile, "term", 1), swap(tile, "term", 1 | step)]
 
     parts = []
     for chunk, size in enumerate(sizes):
@@ -436,7 +437,7 @@
             call(
                 add_last_kernel,
                 "add_last_share",
-                10**10,
+                10**8,
                 1,
                 8 * MIB,
                 out_shape=jax.ShapeDtypeStruct((trials, size, rows, states), jnp.bfloat16),
@@ -454,14 +455,14 @@
             jax.ShapeDtypeStruct((trials, pairs, rows, states), jnp.bfloat16),
             jax.ShapeDtypeStruct((trials, trials), jnp.float32),
         ),
-        in_specs=[VMEM] * (len(done) + 3),
+        in_specs=[VMEM] * (len(done) + 5),
         out_specs=(HBM, HBM),
         scratch_shapes=[
             pltpu.VMEM((trials, sizes[-1], rows, states), jnp.bfloat16),
             pltpu.VMEM((trials, trials), jnp.float32),
             pltpu.SemaphoreType.DMA((len(sizes) + 1,)),
         ],
-    )(*done, *parts[-2:], tile)
+    )(*done, *parts[-2:], tile, *nearby)
     return (products[:, None], rayleigh)
 
 

time: 48.8 us -> 49.6 us (1.016); the launches traced: 47.8 us -> 49.5 us
  waiting for transfers between devices: 18 us -> 19.2 us
  starting transfers between devices: 20.6 us -> 21.2 us
    ppermute x16 -> x17, waiting for transfers between devices: 18 us -> 19.2 us  [swap(): lax.ppermute(value, axis, [(place, place ^ masks[place & 1]) for place in...]
    ppermute x16 -> x17, starting transfers between devices: 20.6 us -> 21.2 us  [swap(): lax.ppermute(value, axis, [(place, place ^ masks[place & 1]) for place in...]
  transfers between devices with their start and end apart: 16 -> 17, of which waited for: 9 -> 11; matrix products, arithmetic and copies ran while one was open for 0% -> 0% of each run, Pallas kernels for 9% -> 10%
where the time goes in v21:
time: 49.6 us; the launch traced here: 49.5 us
  starting transfers between devices  21.2 us (43%)
  waiting for transfers between devices  19.2 us (39%)
  Pallas kernels  6.23 us (13%)
  local copies, waits for them, and re-layouts  2.22 us (4%)
  between operations  0.68 us (1%)
    ppermute x17, starting transfers between devices, swap(): lax.ppermute(value, axis, [(place, place ^ masks[place & 1]) for place in...  21.2 us
    ppermute x17, waiting for transfers between devices, swap(): lax.ppermute(value, axis, [(place, place ^ masks[place & 1]) for place in...  19.2 us
    pallas_call x2, Pallas kernels, sums_of(): call(kernel, name, flops, MIB, 12 * MIB, out_shape=(share_of(shares // 2,...  2.85 us
    unnamed x4, local copies, waits for them, and re-layouts  2.22 us
    pallas_call x1, Pallas kernels, local(): call(functools.partial(early_kernel, sectors), 'early_products', 2 * term...  1.49 us
    pallas_call x1, Pallas kernels, local(): call(functools.partial(inner_kernel, 1.0 / shares), 'inner_products', 2 *...  1.03 us
  transfers between devices with their start and end apart: 17, of which 11 were waited for; matrix products, arithmetic and copies ran while one was open for 0% of the time, Pallas kernels for 10%

profile of v21, /device:TPU:0, one launch (start us, length us, event | category | flops | bytes accessed | tf_op | source)
XLA Modules:
  0.0 49.5 jit_solution(3570245444398223185)
XLA Ops:
  0.6 3.0 %collective-permute-start.1 = (bf16[3,256,256]{2,1,0:T(8,128)(2,1)}, bf16[3,256,256]{2,1,0:T(8,128)(2,1)S(1)}, u32[]{:S(2)}, u32[]{:S(2)}) collective-permute-start(bf16[3,256,256]{2,1,0:T(8,128)(2,1)} %bitcast.11), channel_id=1, source_target_pairs={{0,16},{4,12},{8,24},{12,4},{16,0},{20,28},{24,8},{28,20},{1,17},{... | collective-permute-start | bytes 1179656 | tf_op jit(solution)/shard_map/ppermute | solution.py:20
  3.7 1.2 %copy-done = bf16[2,1,4,256,256]{4,3,2,1,0:T(8,128)(2,1)S(1)} copy-done((bf16[2,1,4,256,256]{4,3,2,1,0:T(8,128)(2,1)S(1)}, bf16[2,1,4,256,256]{4,3,2,1,0:T(8,128)(2,1)}, u32[]{:S(2)}) %copy-start) | copy-done | bytes 1048600
  4.9 1.0 %copy-done.1 = bf16[3,1,256,256]{3,2,1,0:T(8,128)(2,1)S(1)} copy-done((bf16[3,1,256,256]{3,2,1,0:T(8,128)(2,1)S(1)}, bf16[3,1,256,256]{3,2,1,0:T(8,128)(2,1)}, u32[]{:S(2)}) %copy-start.1) | copy-done | bytes 393240
  5.9 1.0 %inner_products.1 = (bf16[2,4,256,768]{3,2,1,0:T(8,128)(2,1)S(1)}, f32[8,128]{1,0:T(8,128)S(1)}, bf16[3,256,256]{2,1,0:T(8,128)(2,1)S(1)}, s32[3,4]{1,0:T(4,128)S(1)}) custom-call(bf16[2,4,256,256]{3,2,1,0:T(8,128)(2,1)S(1)} %bitcast.6, bf16[3,256,256]{2,1,0:T(8,128)(2,1)S(1)} %bitcast.10, bf16[3,256,256]{2,1,0:T(8,128)(2,1)} %bitcast.12, s32[3,4]{1,0:T(4,128)} %offsets_hbm.1), custom_call_target="tpu_custom_call" | custom-call | flops 805306368 | bytes 5242880 | tf_op jit(solution)/shard_map/inner_products/pallas_call | solution.py:306
  6.9 1.6 %collective-permute-start.3 = (bf16[3,256,256]{2,1,0:T(8,128)(2,1)}, bf16[3,256,256]{2,1,0:T(8,128)(2,1)S(1)}, u32[]{:S(2)}, u32[]{:S(2)}) collective-permute-start(bf16[3,256,256]{2,1,0:T(8,128)(2,1)} %bitcast.13), channel_id=1, source_target_pairs={{0,8},{4,20},{8,0},{12,28},{16,24},{20,4},{24,16},{28,12},{1,9},{5... | collective-permute-start | bytes 1179656 | tf_op jit(solution)/shard_map/ppermute | solution.py:20
  8.5 1.5 %collective-permute-done.1.rest_2_ = bf16[3,256,256]{2,1,0:T(8,128)(2,1)S(1)} collective-permute-done((bf16[3,256,256]{2,1,0:T(8,128)(2,1)}, bf16[3,256,256]{2,1,0:T(8,128)(2,1)S(1)}, u32[]{:S(2)}, u32[]{:S(2)}) %collective-permute-start.1) | collective-permute-done | bytes 393248 | tf_op jit(solution)/shard_map/ppermute | solution.py:20
  10.0 3.5 %collective-permute-start.5 = (bf16[3,256,256]{2,1,0:T(8,128)(2,1)S(1)}, bf16[3,256,256]{2,1,0:T(8,128)(2,1)S(1)}, u32[]{:S(2)}, u32[]{:S(2)}) collective-permute-start(bf16[3,256,256]{2,1,0:T(8,128)(2,1)S(1)} %collective-permute-done.1.rest_2_), channel_id=1, source_target_pairs={{0,8},{4,20},{8,0},{12,28},{16,24},{20,4},{24,16},{28,12},{1,9},{5... | collective-permute-start | bytes 1179656 | tf_op jit(solution)/shard_map/ppermute | solution.py:20
  13.5 1.4 %collective-permute-done.3.rest_4_ = bf16[3,256,256]{2,1,0:T(8,128)(2,1)S(1)} collective-permute-done((bf16[3,256,256]{2,1,0:T(8,128)(2,1)}, bf16[3,256,256]{2,1,0:T(8,128)(2,1)S(1)}, u32[]{:S(2)}, u32[]{:S(2)}) %collective-permute-start.3) | collective-permute-done | bytes 393248 | tf_op jit(solution)/shard_map/ppermute | solution.py:20
  15.5 3.8 %collective-permute-done.5.rest_6_ = bf16[3,256,256]{2,1,0:T(8,128)(2,1)S(1)} collective-permute-done((bf16[3,256,256]{2,1,0:T(8,128)(2,1)S(1)}, bf16[3,256,256]{2,1,0:T(8,128)(2,1)S(1)}, u32[]{:S(2)}, u32[]{:S(2)}) %collective-permute-start.5) | collective-permute-done | bytes 393248 | tf_op jit(solution)/shard_map/ppermute | solution.py:20
  19.3 1.5 %early_products.1 = (f32[2,2,256,256]{3,2,1,0:T(8,128)S(1)}, f32[8,128]{1,0:T(8,128)S(1)}, bf16[8,3,256,256]{3,2,1,0:T(8,128)(2,1)S(1)}) custom-call(s32[3,4]{1,0:T(4,128)S(1)} %get-tuple-element.22.offsets, bf16[2,4,256,256]{3,2,1,0:T(8,128)(2,1)S(1)} %bitcast.7, bf16[2,4,256,768]{3,2,1,0:T(8,128)(2,1)S(1)} %get-tuple-element.23.inner, ...), custom_call_target="tpu_custom_call" | custom-call | flops 402653184 | bytes 4194304 | tf_op jit(solution)/shard_map/early_products/pallas_call | solution.py:337
  21.0 0.8 %late_products.1 = (f32[2,2,2,64,256]{4,3,2,1,0:T(8,128)S(1)}, bf16[2,2,2,64,256]{4,3,2,1,0:T(8,128)(2,1)S(1)}, f32[8,128]{1,0:T(8,128)S(1)}) custom-call(s32[3,4]{1,0:T(4,128)S(1)} %get-tuple-element.22.offsets, bf16[2,4,256,256]{3,2,1,0:T(8,128)(2,1)S(1)} %bitcast.8, bf16[2,4,256,768]{3,2,1,0:T(8,128)(2,1)S(1)} %get-tuple-element.23.inner, ...), custom_call_target="tpu_custom_call" | custom-call | flops 50331648 | bytes 1048576 | tf_op jit(solution)/shard_map/late_products/pallas_call | solution.py:354
  21.8 1.5 %collective-permute-start.7 = (bf16[2,2,2,64,256]{4,3,2,1,0:T(8,128)(2,1)S(1)}, bf16[2,2,2,64,256]{4,3,2,1,0:T(8,128)(2,1)S(1)}, u32[]{:S(2)}, u32[]{:S(2)}) collective-permute-start(bf16[2,2,2,64,256]{4,3,2,1,0:T(8,128)(2,1)S(1)} %get-tuple-element.30), channel_id=1, source_target_pairs={{0,1},{1,0},{2,3},{3,2},{4,5},{5,4},{6,7},{7,6},{8,9},{9,8},{10,11... | collective-permute-start | bytes 786440 | tf_op jit(solution)/shard_map/ppermute | solution.py:20
  23.2 2.1 %second_products.1 = (f32[2,2,2,64,256]{4,3,2,1,0:T(8,128)S(1)}, bf16[2,2,2,64,256]{4,3,2,1,0:T(8,128)(2,1)S(1)}, f32[8,128]{1,0:T(8,128)S(1)}) custom-call(s32[3,4]{1,0:T(4,128)S(1)} %get-tuple-element.22.offsets, bf16[2,4,256,256]{3,2,1,0:T(8,128)(2,1)S(1)} %bitcast.9, bf16[2,4,256,768]{3,2,1,0:T(8,128)(2,1)S(1)} %get-tuple-element.23.inner, ...), custom_call_target="tpu_custom_call" | custom-call | flops 402653184 | bytes 1048576 | tf_op jit(solution)/shard_map/second_products/pallas_call | solution.py:354
  25.9 1.2 %collective-permute-done.10 = f32[8,128]{1,0:T(8,128)S(1)} collective-permute-done((f32[8,128]{1,0:T(8,128)S(1)}, f32[8,128]{1,0:T(8,128)S(1)}, u32[]{:S(2)}, u32[]{:S(2)}) %collective-permute-start.10) | collective-permute-done | bytes 4128 | tf_op jit(solution)/shard_map/ppermute | solution.py:20
  27.1 1.8 %collective-permute-start.11 = (f32[8,128]{1,0:T(8,128)S(1)}, f32[8,128]{1,0:T(8,128)S(1)}, u32[]{:S(2)}, u32[]{:S(2)}) collective-permute-start(f32[8,128]{1,0:T(8,128)S(1)} %add.12), channel_id=1, source_target_pairs={{0,8},{4,12},{8,0},{12,4},{16,24},{20,28},{24,16},{28,20},{1,9},{5... | collective-permute-start | bytes 12296 | tf_op jit(solution)/shard_map/ppermute | solution.py:20
  28.9 1.3 %collective-permute-start.12 = (f32[8,128]{1,0:T(8,128)S(1)}, f32[8,128]{1,0:T(8,128)S(1)}, u32[]{:S(2)}, u32[]{:S(2)}) collective-permute-start(f32[8,128]{1,0:T(8,128)S(1)} %add.12), channel_id=1, source_target_pairs={{0,16},{4,20},{8,24},{12,28},{16,0},{20,4},{24,8},{28,12},{1,17},{... | collective-permute-start | bytes 12296 | tf_op jit(solution)/shard_map/ppermute | solution.py:20
  31.0 2.5 %collective-permute-start.8 = (bf16[1,2,2,64,256]{4,3,2,1,0:T(8,128)(2,1)S(1)}, bf16[1,2,2,64,256]{4,3,2,1,0:T(8,128)(2,1)S(1)}, u32[]{:S(2)}, u32[]{:S(2)}) collective-permute-start(bf16[1,2,2,64,256]{4,3,2,1,0:T(8,128)(2,1)S(1)} %get-tuple-element.32), channel_id=1, source_target_pairs={{0,2},{1,3},{2,0},{3,1},{4,6},{5,7},{6,4},{7,5},{8,10},{9,11},{10,... | collective-permute-start | bytes 393224 | tf_op jit(solution)/shard_map/ppermute | solution.py:20
  33.6 1.1 %collective-permute-done.13 = f32[8,128]{1,0:T(8,128)S(1)} collective-permute-done((f32[8,128]{1,0:T(8,128)S(1)}, f32[8,128]{1,0:T(8,128)S(1)}, u32[]{:S(2)}, u32[]{:S(2)}) %collective-permute-start.13) | collective-permute-done | bytes 4128 | tf_op jit(solution)/shard_map/ppermute | solution.py:20
  34.7 4.6 %collective-permute-done.9.received = bf16[2,2,2,64,256]{4,3,2,1,0:T(8,128)(2,1)S(1)} collective-permute-done((bf16[2,2,2,64,256]{4,3,2,1,0:T(8,128)(2,1)S(1)}, bf16[2,2,2,64,256]{4,3,2,1,0:T(8,128)(2,1)S(1)}, u32[]{:S(2)}, u32[]{:S(2)}) %collective-permute-start.9) | collective-permute-done | bytes 262176 | tf_op jit(solution)/shard_map/ppermute | solution.py:20
  39.4 0.8 %collective-permute-start.14 = (bf16[272,256]{1,0:T(8,128)(2,1)S(1)}, bf16[272,256]{1,0:T(8,128)(2,1)S(1)}, u32[]{:S(2)}, u32[]{:S(2)}) collective-permute-start(bf16[272,256]{1,0:T(8,128)(2,1)S(1)} %get-tuple-element.39), channel_id=1, source_target_pairs={{0,2},{1,3},{2,0},{3,1},{4,6},{5,7},{6,4},{7,5},{8,10},{9,11},{10,... | collective-permute-start | bytes 417800 | tf_op jit(solution)/shard_map/ppermute | solution.py:20
  40.2 2.5 %collective-permute-start.15 = (f32[8,128]{1,0:T(8,128)S(1)}, f32[8,128]{1,0:T(8,128)S(1)}, u32[]{:S(2)}, u32[]{:S(2)}) collective-permute-start(f32[8,128]{1,0:T(8,128)S(1)} %add_add_fusion.tile.refs_3_), channel_id=1, source_target_pairs={{0,1},{1,0},{2,3},{3,2},{4,5},{5,4},{6,7},{7,6},{8,9},{9,8},{10,11... | collective-permute-start | bytes 12296 | tf_op jit(solution)/shard_map/ppermute | solution.py:20
  42.6 1.2 %collective-permute-start.16 = (f32[8,128]{1,0:T(8,128)S(1)}, f32[8,128]{1,0:T(8,128)S(1)}, u32[]{:S(2)}, u32[]{:S(2)}) collective-permute-start(f32[8,128]{1,0:T(8,128)S(1)} %add_add_fusion.tile.refs_3_), channel_id=1, source_target_pairs={{0,3},{1,2},{2,1},{3,0},{4,7},{5,6},{6,5},{7,4},{8,11},{9,10},{10,... | collective-permute-start | bytes 12296 | tf_op jit(solution)/shard_map/ppermute | solution.py:20
  44.2 3.9 %collective-permute-done.16.refs_5_ = f32[8,128]{1,0:T(8,128)S(1)} collective-permute-done((f32[8,128]{1,0:T(8,128)S(1)}, f32[8,128]{1,0:T(8,128)S(1)}, u32[]{:S(2)}, u32[]{:S(2)}) %collective-permute-start.16) | collective-permute-done | bytes 4128 | tf_op jit(solution)/shard_map/ppermute | solution.py:20
  48.8 0.7 %finish.1 = (bf16[2,4,64,256]{3,2,1,0:T(8,128)(2,1)}, f32[2,2]{1,0:T(2,128)}) custom-call(bf16[2,2,64,256]{3,2,1,0:T(8,128)(2,1)S(1)} %add_last_share.1.refs_0_, f32[1,2,2,64,256]{4,3,2,1,0:T(8,128)S(1)} %get-tuple-element.38.refs_1_, bf16[272,256]{1,0:T(8,128)(2,1)S(1)} %collective-permute-done.14.refs_2_, f32[8,128]{1,0:T(8,128)S(1)} %add_add_fusion.tile.refs_3_, ...), custom_call_target="tpu_custom_call" | custom-call | flops 1 | bytes 1 | tf_op jit(solution)/shard_map/finish/pallas_call | solution.py:448
  (24 shorter events, 3.3 us)
Async XLA Ops:
  0.6 9.4 %collective-permute-start.1 = (bf16[3,256,256]{2,1,0:T(8,128)(2,1)}, bf16[3,256,256]{2,1,0:T(8,128)(2,1)S(1)}, u32[]{:S(2)}, u32[]{:S(2)}) collective-permute-start(bf16[3,256,256]{2,1,0:T(8,128)(2,1)} %bitcast.11), channel_id=1, source_target_pairs={{0,16},{4,12},{8,24},{12,4},{16,0},{20,28},{24,8},{28,20},{1,17},{... | collective-permute-start | bytes 1179656 | tf_op jit(solution)/shard_map/ppermute | solution.py:20
  3.7 1.2 %copy-start = (bf16[2,1,4,256,256]{4,3,2,1,0:T(8,128)(2,1)S(1)}, bf16[2,1,4,256,256]{4,3,2,1,0:T(8,128)(2,1)}, u32[]{:S(2)}) copy-start(bf16[2,1,4,256,256]{4,3,2,1,0:T(8,128)(2,1)} %param.4) | copy-start | bytes 3145732
  4.9 1.0 %copy-start.1 = (bf16[3,1,256,256]{3,2,1,0:T(8,128)(2,1)S(1)}, bf16[3,1,256,256]{3,2,1,0:T(8,128)(2,1)}, u32[]{:S(2)}) copy-start(bf16[3,1,256,256]{3,2,1,0:T(8,128)(2,1)} %param.5) | copy-start | bytes 1179652
  6.9 8.1 %collective-permute-start.3 = (bf16[3,256,256]{2,1,0:T(8,128)(2,1)}, bf16[3,256,256]{2,1,0:T(8,128)(2,1)S(1)}, u32[]{:S(2)}, u32[]{:S(2)}) collective-permute-start(bf16[3,256,256]{2,1,0:T(8,128)(2,1)} %bitcast.13), channel_id=1, source_target_pairs={{0,8},{4,20},{8,0},{12,28},{16,24},{20,4},{24,16},{28,12},{1,9},{5... | collective-permute-start | bytes 1179656 | tf_op jit(solution)/shard_map/ppermute | solution.py:20
  10.0 9.3 %collective-permute-start.5 = (bf16[3,256,256]{2,1,0:T(8,128)(2,1)S(1)}, bf16[3,256,256]{2,1,0:T(8,128)(2,1)S(1)}, u32[]{:S(2)}, u32[]{:S(2)}) collective-permute-start(bf16[3,256,256]{2,1,0:T(8,128)(2,1)S(1)} %collective-permute-done.1.rest_2_), channel_id=1, source_target_pairs={{0,8},{4,20},{8,0},{12,28},{16,24},{20,4},{24,16},{28,12},{1,9},{5... | collective-permute-start | bytes 1179656 | tf_op jit(solution)/shard_map/ppermute | solution.py:20
  13.5 5.8 %collective-permute-start = (bf16[3,256,256]{2,1,0:T(8,128)(2,1)}, bf16[3,256,256]{2,1,0:T(8,128)(2,1)S(1)}, u32[]{:S(2)}, u32[]{:S(2)}) collective-permute-start(bf16[3,256,256]{2,1,0:T(8,128)(2,1)} %bitcast.14), channel_id=1, source_target_pairs={{0,4},{4,0},{8,12},{12,8},{16,20},{20,16},{24,28},{28,24},{1,5},{5... | collective-permute-start | bytes 1179656 | tf_op jit(solution)/shard_map/ppermute | solution.py:20
  15.0 4.3 %collective-permute-start.4 = (bf16[3,256,256]{2,1,0:T(8,128)(2,1)S(1)}, bf16[3,256,256]{2,1,0:T(8,128)(2,1)S(1)}, u32[]{:S(2)}, u32[]{:S(2)}) collective-permute-start(bf16[3,256,256]{2,1,0:T(8,128)(2,1)S(1)} %collective-permute-done.3.rest_4_), channel_id=1, source_target_pairs={{0,4},{4,0},{8,12},{12,8},{16,20},{20,16},{24,28},{28,24},{1,5},{5... | collective-permute-start | bytes 1179656 | tf_op jit(solution)/shard_map/ppermute | solution.py:20
  15.0 4.3 %collective-permute-start.2 = (bf16[3,256,256]{2,1,0:T(8,128)(2,1)S(1)}, bf16[3,256,256]{2,1,0:T(8,128)(2,1)S(1)}, u32[]{:S(2)}, u32[]{:S(2)}) collective-permute-start(bf16[3,256,256]{2,1,0:T(8,128)(2,1)S(1)} %collective-permute-done.1.rest_2_), channel_id=1, source_target_pairs={{0,4},{4,0},{8,12},{12,8},{16,20},{20,16},{24,28},{28,24},{1,5},{5... | collective-permute-start | bytes 1179656 | tf_op jit(solution)/shard_map/ppermute | solution.py:20
  19.3 1.7 %collective-permute-start.6 = (bf16[3,256,256]{2,1,0:T(8,128)(2,1)S(1)}, bf16[3,256,256]{2,1,0:T(8,128)(2,1)S(1)}, u32[]{:S(2)}, u32[]{:S(2)}) collective-permute-start(bf16[3,256,256]{2,1,0:T(8,128)(2,1)S(1)} %collective-permute-done.5.rest_6_), channel_id=1, source_target_pairs={{0,4},{4,0},{8,12},{12,8},{16,20},{20,16},{24,28},{28,24},{1,5},{5... | collective-permute-start | bytes 1179656 | tf_op jit(solution)/shard_map/ppermute | solution.py:20
  21.8 9.2 %collective-permute-start.7 = (bf16[2,2,2,64,256]{4,3,2,1,0:T(8,128)(2,1)S(1)}, bf16[2,2,2,64,256]{4,3,2,1,0:T(8,128)(2,1)S(1)}, u32[]{:S(2)}, u32[]{:S(2)}) collective-permute-start(bf16[2,2,2,64,256]{4,3,2,1,0:T(8,128)(2,1)S(1)} %get-tuple-element.30), channel_id=1, source_target_pairs={{0,1},{1,0},{2,3},{3,2},{4,5},{5,4},{6,7},{7,6},{8,9},{9,8},{10,11... | collective-permute-start | bytes 786440 | tf_op jit(solution)/shard_map/ppermute | solution.py:20
  25.3 14.0 %collective-permute-start.9 = (bf16[2,2,2,64,256]{4,3,2,1,0:T(8,128)(2,1)S(1)}, bf16[2,2,2,64,256]{4,3,2,1,0:T(8,128)(2,1)S(1)}, u32[]{:S(2)}, u32[]{:S(2)}) collective-permute-start(bf16[2,2,2,64,256]{4,3,2,1,0:T(8,128)(2,1)S(1)} %get-tuple-element.36), channel_id=1, source_target_pairs={{0,1},{1,0},{2,3},{3,2},{4,5},{5,4},{6,7},{7,6},{8,9},{9,8},{10,11... | collective-permute-start | bytes 786440 | tf_op jit(solution)/shard_map/ppermute | solution.py:20
  25.9 1.2 %collective-permute-start.10 = (f32[8,128]{1,0:T(8,128)S(1)}, f32[8,128]{1,0:T(8,128)S(1)}, u32[]{:S(2)}, u32[]{:S(2)}) collective-permute-start(f32[8,128]{1,0:T(8,128)S(1)} %get-tuple-element.37), channel_id=1, source_target_pairs={{0,4},{4,0},{8,12},{12,8},{16,20},{20,16},{24,28},{28,24},{1,5},{5... | collective-permute-start | bytes 12296 | tf_op jit(solution)/shard_map/ppermute | solution.py:20
  27.1 6.5 %collective-permute-start.11 = (f32[8,128]{1,0:T(8,128)S(1)}, f32[8,128]{1,0:T(8,128)S(1)}, u32[]{:S(2)}, u32[]{:S(2)}) collective-permute-start(f32[8,128]{1,0:T(8,128)S(1)} %add.12), channel_id=1, source_target_pairs={{0,8},{4,12},{8,0},{12,4},{16,24},{20,28},{24,16},{28,20},{1,9},{5... | collective-permute-start | bytes 12296 | tf_op jit(solution)/shard_map/ppermute | solution.py:20
  28.9 4.7 %collective-permute-start.12 = (f32[8,128]{1,0:T(8,128)S(1)}, f32[8,128]{1,0:T(8,128)S(1)}, u32[]{:S(2)}, u32[]{:S(2)}) collective-permute-start(f32[8,128]{1,0:T(8,128)S(1)} %add.12), channel_id=1, source_target_pairs={{0,16},{4,20},{8,24},{12,28},{16,0},{20,4},{24,8},{28,12},{1,17},{... | collective-permute-start | bytes 12296 | tf_op jit(solution)/shard_map/ppermute | solution.py:20
  30.2 4.5 %collective-permute-start.13 = (f32[8,128]{1,0:T(8,128)S(1)}, f32[8,128]{1,0:T(8,128)S(1)}, u32[]{:S(2)}, u32[]{:S(2)}) collective-permute-start(f32[8,128]{1,0:T(8,128)S(1)} %add.12), channel_id=1, source_target_pairs={{0,24},{4,28},{8,16},{12,20},{16,8},{20,12},{24,0},{28,4},{1,25},{... | collective-permute-start | bytes 12296 | tf_op jit(solution)/shard_map/ppermute | solution.py:20
  31.0 12.8 %collective-permute-start.8 = (bf16[1,2,2,64,256]{4,3,2,1,0:T(8,128)(2,1)S(1)}, bf16[1,2,2,64,256]{4,3,2,1,0:T(8,128)(2,1)S(1)}, u32[]{:S(2)}, u32[]{:S(2)}) collective-permute-start(bf16[1,2,2,64,256]{4,3,2,1,0:T(8,128)(2,1)S(1)} %get-tuple-element.32), channel_id=1, source_target_pairs={{0,2},{1,3},{2,0},{3,1},{4,6},{5,7},{6,4},{7,5},{8,10},{9,11},{10,... | collective-permute-start | bytes 393224 | tf_op jit(solution)/shard_map/ppermute | solution.py:20
  39.4 9.4 %collective-permute-start.14 = (bf16[272,256]{1,0:T(8,128)(2,1)S(1)}, bf16[272,256]{1,0:T(8,128)(2,1)S(1)}, u32[]{:S(2)}, u32[]{:S(2)}) collective-permute-start(bf16[272,256]{1,0:T(8,128)(2,1)S(1)} %get-tuple-element.39), channel_id=1, source_target_pairs={{0,2},{1,3},{2,0},{3,1},{4,6},{5,7},{6,4},{7,5},{8,10},{9,11},{10,... | collective-permute-start | bytes 417800 | tf_op jit(solution)/shard_map/ppermute | solution.py:20
  40.2 4.1 %collective-permute-start.15 = (f32[8,128]{1,0:T(8,128)S(1)}, f32[8,128]{1,0:T(8,128)S(1)}, u32[]{:S(2)}, u32[]{:S(2)}) collective-permute-start(f32[8,128]{1,0:T(8,128)S(1)} %add_add_fusion.tile.refs_3_), channel_id=1, source_target_pairs={{0,1},{1,0},{2,3},{3,2},{4,5},{5,4},{6,7},{7,6},{8,9},{9,8},{10,11... | collective-permute-start | bytes 12296 | tf_op jit(solution)/shard_map/ppermute | solution.py:20
  42.6 5.5 %collective-permute-start.16 = (f32[8,128]{1,0:T(8,128)S(1)}, f32[8,128]{1,0:T(8,128)S(1)}, u32[]{:S(2)}, u32[]{:S(2)}) collective-permute-start(f32[8,128]{1,0:T(8,128)S(1)} %add_add_fusion.tile.refs_3_), channel_id=1, source_target_pairs={{0,3},{1,2},{2,1},{3,0},{4,7},{5,6},{6,5},{7,4},{8,11},{9,10},{10,... | collective-permute-start | bytes 12296 | tf_op jit(solution)/shard_map/ppermute | solution.py:20

commit v22 on v21

--- a/solution.py
+++ b/solution.py
@@ -176,7 +176,7 @@
     write_tile(before, grams, tile)
 
 
-def second_kernel(sectors, first, offsets, vectors, inner, before, rights, last, *rest):
+def other_kernel(sectors, first, offsets, vectors, inner, before, rights, last, *rest):
     keep, send, tile, whole, grams = rest
     grams[...] = jnp.zeros_like(grams)
     for slot in range(keep.shape[2]):
@@ -331,7 +331,7 @@
 
     tile_shape = jax.ShapeDtypeStruct(TILE, jnp.float32)
     rights_shape = jax.ShapeDtypeStruct((sectors, terms, states, states), jnp.bfloat16)
-    sizes = [pairs // 2, pairs - pairs // 2]
+    sizes = [pairs - 2 * (pairs // 4), pairs // 4, pairs // 4]
     grams = pltpu.VMEM((trials * trials, 8, states), jnp.float32)
     *early, last = gathered
     partial, tile, rights = call(
@@ -380,19 +380,22 @@
         last,
     )
     sums = [(keep, swap(send, "term", 1))]
-    keep, send, tile = sums_of(
-        functools.partial(second_kernel, sectors, sizes[0]),
-        "second_products",
-        2 * terms * trials * sizes[1] * states**3,
-        sizes[1],
-        (sizes[1], trials),
-        vectors,
-        inner,
-        tile,
-        rights,
-        last,
-    )
-    sums.append((keep, swap(send, "term", 1)))
+    first = sizes[0]
+    for size in sizes[1:]:
+        keep, send, tile = sums_of(
+            functools.partial(other_kernel, sectors, first),
+            "other_products",
+            2 * terms * trials * size * states**3,
+            size,
+            (size, trials),
+            vectors,
+            inner,
+            tile,
+            rights,
+            last,
+        )
+        sums.append((keep, swap(send, "term", 1)))
+        first += size
 
     for masks in [[1]] + steps_of(sectors, 1):
         tile = add_places(tile, "sec", masks)
@@ -406,6 +409,8 @@
     parts = []
     for chunk, size in enumerate(sizes):
         keep, received = sums[chunk]
+        if chunk:
+            received, send = lax.optimization_barrier((received, send))
         step = 1
         while 2 * step < shares:
             step *= 2

time: 49.6 us -> 49.3 us (level); the launches traced: 49.5 us -> 48.6 us
  waiting for transfers between devices: 19.2 us -> 14.8 us
  starting transfers between devices: 21.2 us -> 23.9 us
  Pallas kernels: 6.23 us -> 6.93 us
    ppermute x17 -> x19, waiting for transfers between devices: 19.2 us -> 14.8 us  [swap(): lax.ppermute(value, axis, [(place, place ^ masks[place & 1]) for place in...]
    ppermute x17 -> x19, starting transfers between devices: 21.2 us -> 23.9 us  [swap(): lax.ppermute(value, axis, [(place, place ^ masks[place & 1]) for place in...]
    pallas_call x2 -> x3, Pallas kernels: 2.85 us -> 3.51 us  [sums_of(): call(kernel, name, flops, MIB, 12 * MIB, out_shape=(share_of(shares // 2,...]
  transfers between devices with their start and end apart: 17 -> 19, of which waited for: 11 -> 8; matrix products, arithmetic and copies ran while one was open for 0% -> 0% of each run, Pallas kernels for 10% -> 11%
where the time goes in v22:
time: 49.3 us; the launch traced here: 48.6 us
  starting transfers between devices  23.9 us (48%)
  waiting for transfers between devices  14.8 us (30%)
  Pallas kernels  6.93 us (14%)
  local copies, waits for them, and re-layouts  2.22 us (5%)
  between operations  0.74 us (2%)
    ppermute x19, starting transfers between devices, swap(): lax.ppermute(value, axis, [(place, place ^ masks[place & 1]) for place in...  23.9 us
    ppermute x19, waiting for transfers between devices, swap(): lax.ppermute(value, axis, [(place, place ^ masks[place & 1]) for place in...  14.8 us
    pallas_call x3, Pallas kernels, sums_of(): call(kernel, name, flops, MIB, 12 * MIB, out_shape=(share_of(shares // 2,...  3.51 us
    unnamed x4, local copies, waits for them, and re-layouts  2.22 us
    pallas_call x1, Pallas kernels, local(): call(functools.partial(early_kernel, sectors), 'early_products', 2 * term...  1.49 us
    pallas_call x1, Pallas kernels, local(): call(functools.partial(inner_kernel, 1.0 / shares), 'inner_products', 2 *...  1.03 us
  transfers between devices with their start and end apart: 19, of which 8 were waited for; matrix products, arithmetic and copies ran while one was open for 0% of the time, Pallas kernels for 11%

profile of v22, /device:TPU:0, one launch (start us, length us, event | category | flops | bytes accessed | tf_op | source)
XLA Modules:
  0.0 48.6 jit_solution(9832463736959076563)
XLA Ops:
  0.6 3.0 %collective-permute-start.1 = (bf16[3,256,256]{2,1,0:T(8,128)(2,1)}, bf16[3,256,256]{2,1,0:T(8,128)(2,1)S(1)}, u32[]{:S(2)}, u32[]{:S(2)}) collective-permute-start(bf16[3,256,256]{2,1,0:T(8,128)(2,1)} %bitcast.12), channel_id=1, source_target_pairs={{0,16},{4,12},{8,24},{12,4},{16,0},{20,28},{24,8},{28,20},{1,17},{... | collective-permute-start | bytes 1179656 | tf_op jit(solution)/shard_map/ppermute | solution.py:20
  3.7 1.2 %copy-done = bf16[2,1,4,256,256]{4,3,2,1,0:T(8,128)(2,1)S(1)} copy-done((bf16[2,1,4,256,256]{4,3,2,1,0:T(8,128)(2,1)S(1)}, bf16[2,1,4,256,256]{4,3,2,1,0:T(8,128)(2,1)}, u32[]{:S(2)}) %copy-start) | copy-done | bytes 1048600
  4.9 1.0 %copy-done.1 = bf16[3,1,256,256]{3,2,1,0:T(8,128)(2,1)S(1)} copy-done((bf16[3,1,256,256]{3,2,1,0:T(8,128)(2,1)S(1)}, bf16[3,1,256,256]{3,2,1,0:T(8,128)(2,1)}, u32[]{:S(2)}) %copy-start.1) | copy-done | bytes 393240
  5.9 1.0 %inner_products.1 = (bf16[2,4,256,768]{3,2,1,0:T(8,128)(2,1)S(1)}, f32[8,128]{1,0:T(8,128)S(1)}, bf16[3,256,256]{2,1,0:T(8,128)(2,1)S(1)}, s32[3,4]{1,0:T(4,128)S(1)}) custom-call(bf16[2,4,256,256]{3,2,1,0:T(8,128)(2,1)S(1)} %bitcast.6, bf16[3,256,256]{2,1,0:T(8,128)(2,1)S(1)} %bitcast.11, bf16[3,256,256]{2,1,0:T(8,128)(2,1)} %bitcast.13, s32[3,4]{1,0:T(4,128)} %offsets_hbm.1), custom_call_target="tpu_custom_call" | custom-call | flops 805306368 | bytes 5242880 | tf_op jit(solution)/shard_map/inner_products/pallas_call | solution.py:306
  6.9 1.6 %collective-permute-start.3 = (bf16[3,256,256]{2,1,0:T(8,128)(2,1)}, bf16[3,256,256]{2,1,0:T(8,128)(2,1)S(1)}, u32[]{:S(2)}, u32[]{:S(2)}) collective-permute-start(bf16[3,256,256]{2,1,0:T(8,128)(2,1)} %bitcast.14), channel_id=1, source_target_pairs={{0,8},{4,20},{8,0},{12,28},{16,24},{20,4},{24,16},{28,12},{1,9},{5... | collective-permute-start | bytes 1179656 | tf_op jit(solution)/shard_map/ppermute | solution.py:20
  8.5 1.5 %collective-permute-done.1.rest_2_ = bf16[3,256,256]{2,1,0:T(8,128)(2,1)S(1)} collective-permute-done((bf16[3,256,256]{2,1,0:T(8,128)(2,1)}, bf16[3,256,256]{2,1,0:T(8,128)(2,1)S(1)}, u32[]{:S(2)}, u32[]{:S(2)}) %collective-permute-start.1) | collective-permute-done | bytes 393248 | tf_op jit(solution)/shard_map/ppermute | solution.py:20
  10.0 3.5 %collective-permute-start.5 = (bf16[3,256,256]{2,1,0:T(8,128)(2,1)S(1)}, bf16[3,256,256]{2,1,0:T(8,128)(2,1)S(1)}, u32[]{:S(2)}, u32[]{:S(2)}) collective-permute-start(bf16[3,256,256]{2,1,0:T(8,128)(2,1)S(1)} %collective-permute-done.1.rest_2_), channel_id=1, source_target_pairs={{0,8},{4,20},{8,0},{12,28},{16,24},{20,4},{24,16},{28,12},{1,9},{5... | collective-permute-start | bytes 1179656 | tf_op jit(solution)/shard_map/ppermute | solution.py:20
  13.5 1.4 %collective-permute-done.3.rest_4_ = bf16[3,256,256]{2,1,0:T(8,128)(2,1)S(1)} collective-permute-done((bf16[3,256,256]{2,1,0:T(8,128)(2,1)}, bf16[3,256,256]{2,1,0:T(8,128)(2,1)S(1)}, u32[]{:S(2)}, u32[]{:S(2)}) %collective-permute-start.3) | collective-permute-done | bytes 393248 | tf_op jit(solution)/shard_map/ppermute | solution.py:20
  15.5 3.8 %collective-permute-done.5.rest_6_ = bf16[3,256,256]{2,1,0:T(8,128)(2,1)S(1)} collective-permute-done((bf16[3,256,256]{2,1,0:T(8,128)(2,1)S(1)}, bf16[3,256,256]{2,1,0:T(8,128)(2,1)S(1)}, u32[]{:S(2)}, u32[]{:S(2)}) %collective-permute-start.5) | collective-permute-done | bytes 393248 | tf_op jit(solution)/shard_map/ppermute | solution.py:20
  19.3 1.5 %early_products.1 = (f32[2,2,256,256]{3,2,1,0:T(8,128)S(1)}, f32[8,128]{1,0:T(8,128)S(1)}, bf16[8,3,256,256]{3,2,1,0:T(8,128)(2,1)S(1)}) custom-call(s32[3,4]{1,0:T(4,128)S(1)} %get-tuple-element.29.offsets, bf16[2,4,256,256]{3,2,1,0:T(8,128)(2,1)S(1)} %bitcast.7, bf16[2,4,256,768]{3,2,1,0:T(8,128)(2,1)S(1)} %get-tuple-element.30.inner, ...), custom_call_target="tpu_custom_call" | custom-call | flops 402653184 | bytes 4194304 | tf_op jit(solution)/shard_map/early_products/pallas_call | solution.py:337
  21.0 0.8 %late_products.1 = (f32[2,2,2,64,256]{4,3,2,1,0:T(8,128)S(1)}, bf16[2,2,2,64,256]{4,3,2,1,0:T(8,128)(2,1)S(1)}, f32[8,128]{1,0:T(8,128)S(1)}) custom-call(s32[3,4]{1,0:T(4,128)S(1)} %get-tuple-element.29.offsets, bf16[2,4,256,256]{3,2,1,0:T(8,128)(2,1)S(1)} %bitcast.8, bf16[2,4,256,768]{3,2,1,0:T(8,128)(2,1)S(1)} %get-tuple-element.30.inner, ...), custom_call_target="tpu_custom_call" | custom-call | flops 50331648 | bytes 1048576 | tf_op jit(solution)/shard_map/late_products/pallas_call | solution.py:354
  21.8 1.5 %collective-permute-start.7 = (bf16[2,2,2,64,256]{4,3,2,1,0:T(8,128)(2,1)S(1)}, bf16[2,2,2,64,256]{4,3,2,1,0:T(8,128)(2,1)S(1)}, u32[]{:S(2)}, u32[]{:S(2)}) collective-permute-start(bf16[2,2,2,64,256]{4,3,2,1,0:T(8,128)(2,1)S(1)} %get-tuple-element.37), channel_id=1, source_target_pairs={{0,1},{1,0},{2,3},{3,2},{4,5},{5,4},{6,7},{7,6},{8,9},{9,8},{10,11... | collective-permute-start | bytes 786440 | tf_op jit(solution)/shard_map/ppermute | solution.py:20
  23.2 1.6 %other_products.2 = (f32[2,2,1,64,256]{4,3,2,1,0:T(8,128)S(1)}, bf16[2,2,1,64,256]{4,3,2,1,0:T(8,128)(2,1)S(1)}, f32[8,128]{1,0:T(8,128)S(1)}) custom-call(s32[3,4]{1,0:T(4,128)S(1)} %get-tuple-element.29.offsets, bf16[2,4,256,256]{3,2,1,0:T(8,128)(2,1)S(1)} %bitcast.9, bf16[2,4,256,768]{3,2,1,0:T(8,128)(2,1)S(1)} %get-tuple-element.30.inner, ...), custom_call_target="tpu_custom_call" | custom-call | flops 201326592 | bytes 1048576 | tf_op jit(solution)/shard_map/other_products/pallas_call | solution.py:354
  25.2 1.2 %other_products.3 = (f32[2,2,1,64,256]{4,3,2,1,0:T(8,128)S(1)}, bf16[2,2,1,64,256]{4,3,2,1,0:T(8,128)(2,1)S(1)}, f32[8,128]{1,0:T(8,128)S(1)}) custom-call(s32[3,4]{1,0:T(4,128)S(1)} %get-tuple-element.29.offsets, bf16[2,4,256,256]{3,2,1,0:T(8,128)(2,1)S(1)} %bitcast.10, bf16[2,4,256,768]{3,2,1,0:T(8,128)(2,1)S(1)} %get-tuple-element.30.inner, ...), custom_call_target="tpu_custom_call" | custom-call | flops 201326592 | bytes 1048576 | tf_op jit(solution)/shard_map/other_products/pallas_call | solution.py:354
  26.4 1.2 %collective-permute-done.12 = f32[8,128]{1,0:T(8,128)S(1)} collective-permute-done((f32[8,128]{1,0:T(8,128)S(1)}, f32[8,128]{1,0:T(8,128)S(1)}, u32[]{:S(2)}, u32[]{:S(2)}) %collective-permute-start.12) | collective-permute-done | bytes 4128 | tf_op jit(solution)/shard_map/ppermute | solution.py:20
  27.6 2.1 %collective-permute-start.13 = (f32[8,128]{1,0:T(8,128)S(1)}, f32[8,128]{1,0:T(8,128)S(1)}, u32[]{:S(2)}, u32[]{:S(2)}) collective-permute-start(f32[8,128]{1,0:T(8,128)S(1)} %add.12), channel_id=1, source_target_pairs={{0,8},{4,12},{8,0},{12,4},{16,24},{20,28},{24,16},{28,20},{1,9},{5... | collective-permute-start | bytes 12296 | tf_op jit(solution)/shard_map/ppermute | solution.py:20
  29.7 1.3 %collective-permute-start.14 = (f32[8,128]{1,0:T(8,128)S(1)}, f32[8,128]{1,0:T(8,128)S(1)}, u32[]{:S(2)}, u32[]{:S(2)}) collective-permute-start(f32[8,128]{1,0:T(8,128)S(1)} %add.12), channel_id=1, source_target_pairs={{0,16},{4,20},{8,24},{12,28},{16,0},{20,4},{24,8},{28,12},{1,17},{... | collective-permute-start | bytes 12296 | tf_op jit(solution)/shard_map/ppermute | solution.py:20
  31.1 1.7 %collective-permute-start.11 = (bf16[2,2,1,64,256]{4,3,2,1,0:T(8,128)(2,1)S(1)}, bf16[2,2,1,64,256]{4,3,2,1,0:T(8,128)(2,1)S(1)}, u32[]{:S(2)}, u32[]{:S(2)}) collective-permute-start(bf16[2,2,1,64,256]{4,3,2,1,0:T(8,128)(2,1)S(1)} %get-tuple-element.49), channel_id=1, source_target_pairs={{0,1},{1,0},{2,3},{3,2},{4,5},{5,4},{6,7},{7,6},{8,9},{9,8},{10,11... | collective-permute-start | bytes 393224 | tf_op jit(solution)/shard_map/ppermute | solution.py:20
  33.1 2.5 %collective-permute-start.8 = (bf16[1,2,2,64,256]{4,3,2,1,0:T(8,128)(2,1)S(1)}, bf16[1,2,2,64,256]{4,3,2,1,0:T(8,128)(2,1)S(1)}, u32[]{:S(2)}, u32[]{:S(2)}) collective-permute-start(bf16[1,2,2,64,256]{4,3,2,1,0:T(8,128)(2,1)S(1)} %get-tuple-element.39), channel_id=1, source_target_pairs={{0,2},{1,3},{2,0},{3,1},{4,6},{5,7},{6,4},{7,5},{8,10},{9,11},{10,... | collective-permute-start | bytes 393224 | tf_op jit(solution)/shard_map/ppermute | solution.py:20
  36.2 3.6 %collective-permute-start.16 = (bf16[144,256]{1,0:T(8,128)(2,1)S(1)}, bf16[144,256]{1,0:T(8,128)(2,1)S(1)}, u32[]{:S(2)}, u32[]{:S(2)}) collective-permute-start(bf16[144,256]{1,0:T(8,128)(2,1)S(1)} %get-tuple-element.53), channel_id=1, source_target_pairs={{0,2},{1,3},{2,0},{3,1},{4,6},{5,7},{6,4},{7,5},{8,10},{9,11},{10,... | collective-permute-start | bytes 221192 | tf_op jit(solution)/shard_map/ppermute | solution.py:20
  39.8 0.8 %collective-permute-start.17 = (f32[8,128]{1,0:T(8,128)S(1)}, f32[8,128]{1,0:T(8,128)S(1)}, u32[]{:S(2)}, u32[]{:S(2)}) collective-permute-start(f32[8,128]{1,0:T(8,128)S(1)} %add_add_fusion.tile.refs_4_), channel_id=1, source_target_pairs={{0,1},{1,0},{2,3},{3,2},{4,5},{5,4},{6,7},{7,6},{8,9},{9,8},{10,11... | collective-permute-start | bytes 12296 | tf_op jit(solution)/shard_map/ppermute | solution.py:20
  40.6 0.7 %collective-permute-start.18 = (f32[8,128]{1,0:T(8,128)S(1)}, f32[8,128]{1,0:T(8,128)S(1)}, u32[]{:S(2)}, u32[]{:S(2)}) collective-permute-start(f32[8,128]{1,0:T(8,128)S(1)} %add_add_fusion.tile.refs_4_), channel_id=1, source_target_pairs={{0,3},{1,2},{2,1},{3,0},{4,7},{5,6},{6,5},{7,4},{8,11},{9,10},{10,... | collective-permute-start | bytes 12296 | tf_op jit(solution)/shard_map/ppermute | solution.py:20
  41.4 5.7 %collective-permute-done.10.received = bf16[1,2,1,64,256]{4,3,2,1,0:T(8,128)(2,1)S(1)} collective-permute-done((bf16[1,2,1,64,256]{4,3,2,1,0:T(8,128)(2,1)S(1)}, bf16[1,2,1,64,256]{4,3,2,1,0:T(8,128)(2,1)S(1)}, u32[]{:S(2)}, u32[]{:S(2)}) %collective-permute-start.10) | collective-permute-done | bytes 65568 | tf_op jit(solution)/shard_map/ppermute | solution.py:20
  47.8 0.7 %finish.1 = (bf16[2,4,64,256]{3,2,1,0:T(8,128)(2,1)}, f32[2,2]{1,0:T(2,128)}) custom-call(bf16[2,2,64,256]{3,2,1,0:T(8,128)(2,1)S(1)} %add_last_share.2.refs_0_, bf16[2,1,64,256]{3,2,1,0:T(8,128)(2,1)S(1)} %add_last_share.3.refs_1_, f32[1,2,1,64,256]{4,3,2,1,0:T(8,128)S(1)} %get-tuple-element.52.refs_2_, ...), custom_call_target="tpu_custom_call" | custom-call | flops 1 | bytes 1 | tf_op jit(solution)/shard_map/finish/pallas_call | solution.py:453
  (31 shorter events, 2.9 us)
Async XLA Ops:
  0.6 9.4 %collective-permute-start.1 = (bf16[3,256,256]{2,1,0:T(8,128)(2,1)}, bf16[3,256,256]{2,1,0:T(8,128)(2,1)S(1)}, u32[]{:S(2)}, u32[]{:S(2)}) collective-permute-start(bf16[3,256,256]{2,1,0:T(8,128)(2,1)} %bitcast.12), channel_id=1, source_target_pairs={{0,16},{4,12},{8,24},{12,4},{16,0},{20,28},{24,8},{28,20},{1,17},{... | collective-permute-start | bytes 1179656 | tf_op jit(solution)/shard_map/ppermute | solution.py:20
  3.7 1.2 %copy-start = (bf16[2,1,4,256,256]{4,3,2,1,0:T(8,128)(2,1)S(1)}, bf16[2,1,4,256,256]{4,3,2,1,0:T(8,128)(2,1)}, u32[]{:S(2)}) copy-start(bf16[2,1,4,256,256]{4,3,2,1,0:T(8,128)(2,1)} %param.4) | copy-start | bytes 3145732
  4.9 1.0 %copy-start.1 = (bf16[3,1,256,256]{3,2,1,0:T(8,128)(2,1)S(1)}, bf16[3,1,256,256]{3,2,1,0:T(8,128)(2,1)}, u32[]{:S(2)}) copy-start(bf16[3,1,256,256]{3,2,1,0:T(8,128)(2,1)} %param.5) | copy-start | bytes 1179652
  6.9 8.1 %collective-permute-start.3 = (bf16[3,256,256]{2,1,0:T(8,128)(2,1)}, bf16[3,256,256]{2,1,0:T(8,128)(2,1)S(1)}, u32[]{:S(2)}, u32[]{:S(2)}) collective-permute-start(bf16[3,256,256]{2,1,0:T(8,128)(2,1)} %bitcast.14), channel_id=1, source_target_pairs={{0,8},{4,20},{8,0},{12,28},{16,24},{20,4},{24,16},{28,12},{1,9},{5... | collective-permute-start | bytes 1179656 | tf_op jit(solution)/shard_map/ppermute | solution.py:20
  10.0 9.3 %collective-permute-start.5 = (bf16[3,256,256]{2,1,0:T(8,128)(2,1)S(1)}, bf16[3,256,256]{2,1,0:T(8,128)(2,1)S(1)}, u32[]{:S(2)}, u32[]{:S(2)}) collective-permute-start(bf16[3,256,256]{2,1,0:T(8,128)(2,1)S(1)} %collective-permute-done.1.rest_2_), channel_id=1, source_target_pairs={{0,8},{4,20},{8,0},{12,28},{16,24},{20,4},{24,16},{28,12},{1,9},{5... | collective-permute-start | bytes 1179656 | tf_op jit(solution)/shard_map/ppermute | solution.py:20
  13.5 5.8 %collective-permute-start = (bf16[3,256,256]{2,1,0:T(8,128)(2,1)}, bf16[3,256,256]{2,1,0:T(8,128)(2,1)S(1)}, u32[]{:S(2)}, u32[]{:S(2)}) collective-permute-start(bf16[3,256,256]{2,1,0:T(8,128)(2,1)} %bitcast.15), channel_id=1, source_target_pairs={{0,4},{4,0},{8,12},{12,8},{16,20},{20,16},{24,28},{28,24},{1,5},{5... | collective-permute-start | bytes 1179656 | tf_op jit(solution)/shard_map/ppermute | solution.py:20
  15.0 4.3 %collective-permute-start.4 = (bf16[3,256,256]{2,1,0:T(8,128)(2,1)S(1)}, bf16[3,256,256]{2,1,0:T(8,128)(2,1)S(1)}, u32[]{:S(2)}, u32[]{:S(2)}) collective-permute-start(bf16[3,256,256]{2,1,0:T(8,128)(2,1)S(1)} %collective-permute-done.3.rest_4_), channel_id=1, source_target_pairs={{0,4},{4,0},{8,12},{12,8},{16,20},{20,16},{24,28},{28,24},{1,5},{5... | collective-permute-start | bytes 1179656 | tf_op jit(solution)/shard_map/ppermute | solution.py:20
  15.0 4.3 %collective-permute-start.2 = (bf16[3,256,256]{2,1,0:T(8,128)(2,1)S(1)}, bf16[3,256,256]{2,1,0:T(8,128)(2,1)S(1)}, u32[]{:S(2)}, u32[]{:S(2)}) collective-permute-start(bf16[3,256,256]{2,1,0:T(8,128)(2,1)S(1)} %collective-permute-done.1.rest_2_), channel_id=1, source_target_pairs={{0,4},{4,0},{8,12},{12,8},{16,20},{20,16},{24,28},{28,24},{1,5},{5... | collective-permute-start | bytes 1179656 | tf_op jit(solution)/shard_map/ppermute | solution.py:20
  19.3 1.7 %collective-permute-start.6 = (bf16[3,256,256]{2,1,0:T(8,128)(2,1)S(1)}, bf16[3,256,256]{2,1,0:T(8,128)(2,1)S(1)}, u32[]{:S(2)}, u32[]{:S(2)}) collective-permute-start(bf16[3,256,256]{2,1,0:T(8,128)(2,1)S(1)} %collective-permute-done.5.rest_6_), channel_id=1, source_target_pairs={{0,4},{4,0},{8,12},{12,8},{16,20},{20,16},{24,28},{28,24},{1,5},{5... | collective-permute-start | bytes 1179656 | tf_op jit(solution)/shard_map/ppermute | solution.py:20
  21.8 9.4 %collective-permute-start.7 = (bf16[2,2,2,64,256]{4,3,2,1,0:T(8,128)(2,1)S(1)}, bf16[2,2,2,64,256]{4,3,2,1,0:T(8,128)(2,1)S(1)}, u32[]{:S(2)}, u32[]{:S(2)}) collective-permute-start(bf16[2,2,2,64,256]{4,3,2,1,0:T(8,128)(2,1)S(1)} %get-tuple-element.37), channel_id=1, source_target_pairs={{0,1},{1,0},{2,3},{3,2},{4,5},{5,4},{6,7},{7,6},{8,9},{9,8},{10,11... | collective-permute-start | bytes 786440 | tf_op jit(solution)/shard_map/ppermute | solution.py:20
  24.8 8.3 %collective-permute-start.9 = (bf16[2,2,1,64,256]{4,3,2,1,0:T(8,128)(2,1)S(1)}, bf16[2,2,1,64,256]{4,3,2,1,0:T(8,128)(2,1)S(1)}, u32[]{:S(2)}, u32[]{:S(2)}) collective-permute-start(bf16[2,2,1,64,256]{4,3,2,1,0:T(8,128)(2,1)S(1)} %get-tuple-element.43), channel_id=1, source_target_pairs={{0,1},{1,0},{2,3},{3,2},{4,5},{5,4},{6,7},{7,6},{8,9},{9,8},{10,11... | collective-permute-start | bytes 393224 | tf_op jit(solution)/shard_map/ppermute | solution.py:20
  26.4 1.2 %collective-permute-start.12 = (f32[8,128]{1,0:T(8,128)S(1)}, f32[8,128]{1,0:T(8,128)S(1)}, u32[]{:S(2)}, u32[]{:S(2)}) collective-permute-start(f32[8,128]{1,0:T(8,128)S(1)} %get-tuple-element.51), channel_id=1, source_target_pairs={{0,4},{4,0},{8,12},{12,8},{16,20},{20,16},{24,28},{28,24},{1,5},{5... | collective-permute-start | bytes 12296 | tf_op jit(solution)/shard_map/ppermute | solution.py:20
  27.6 8.1 %collective-permute-start.13 = (f32[8,128]{1,0:T(8,128)S(1)}, f32[8,128]{1,0:T(8,128)S(1)}, u32[]{:S(2)}, u32[]{:S(2)}) collective-permute-start(f32[8,128]{1,0:T(8,128)S(1)} %add.12), channel_id=1, source_target_pairs={{0,8},{4,12},{8,0},{12,4},{16,24},{20,28},{24,16},{28,20},{1,9},{5... | collective-permute-start | bytes 12296 | tf_op jit(solution)/shard_map/ppermute | solution.py:20
  29.7 6.5 %collective-permute-start.14 = (f32[8,128]{1,0:T(8,128)S(1)}, f32[8,128]{1,0:T(8,128)S(1)}, u32[]{:S(2)}, u32[]{:S(2)}) collective-permute-start(f32[8,128]{1,0:T(8,128)S(1)} %add.12), channel_id=1, source_target_pairs={{0,16},{4,20},{8,24},{12,28},{16,0},{20,4},{24,8},{28,12},{1,17},{... | collective-permute-start | bytes 12296 | tf_op jit(solution)/shard_map/ppermute | solution.py:20
  31.0 5.2 %collective-permute-start.15 = (f32[8,128]{1,0:T(8,128)S(1)}, f32[8,128]{1,0:T(8,128)S(1)}, u32[]{:S(2)}, u32[]{:S(2)}) collective-permute-start(f32[8,128]{1,0:T(8,128)S(1)} %add.12), channel_id=1, source_target_pairs={{0,24},{4,28},{8,16},{12,20},{16,8},{20,12},{24,0},{28,4},{1,25},{... | collective-permute-start | bytes 12296 | tf_op jit(solution)/shard_map/ppermute | solution.py:20
  31.1 5.0 %collective-permute-start.11 = (bf16[2,2,1,64,256]{4,3,2,1,0:T(8,128)(2,1)S(1)}, bf16[2,2,1,64,256]{4,3,2,1,0:T(8,128)(2,1)S(1)}, u32[]{:S(2)}, u32[]{:S(2)}) collective-permute-start(bf16[2,2,1,64,256]{4,3,2,1,0:T(8,128)(2,1)S(1)} %get-tuple-element.49), channel_id=1, source_target_pairs={{0,1},{1,0},{2,3},{3,2},{4,5},{5,4},{6,7},{7,6},{8,9},{9,8},{10,11... | collective-permute-start | bytes 393224 | tf_op jit(solution)/shard_map/ppermute | solution.py:20
  33.1 14.0 %collective-permute-start.8 = (bf16[1,2,2,64,256]{4,3,2,1,0:T(8,128)(2,1)S(1)}, bf16[1,2,2,64,256]{4,3,2,1,0:T(8,128)(2,1)S(1)}, u32[]{:S(2)}, u32[]{:S(2)}) collective-permute-start(bf16[1,2,2,64,256]{4,3,2,1,0:T(8,128)(2,1)S(1)} %get-tuple-element.39), channel_id=1, source_target_pairs={{0,2},{1,3},{2,0},{3,1},{4,6},{5,7},{6,4},{7,5},{8,10},{9,11},{10,... | collective-permute-start | bytes 393224 | tf_op jit(solution)/shard_map/ppermute | solution.py:20
  35.6 11.4 %collective-permute-start.10 = (bf16[1,2,1,64,256]{4,3,2,1,0:T(8,128)(2,1)S(1)}, bf16[1,2,1,64,256]{4,3,2,1,0:T(8,128)(2,1)S(1)}, u32[]{:S(2)}, u32[]{:S(2)}) collective-permute-start(bf16[1,2,1,64,256]{4,3,2,1,0:T(8,128)(2,1)S(1)} %get-tuple-element.46), channel_id=1, source_target_pairs={{0,2},{1,3},{2,0},{3,1},{4,6},{5,7},{6,4},{7,5},{8,10},{9,11},{10,... | collective-permute-start | bytes 196616 | tf_op jit(solution)/shard_map/ppermute | solution.py:20
  36.2 11.6 %collective-permute-start.16 = (bf16[144,256]{1,0:T(8,128)(2,1)S(1)}, bf16[144,256]{1,0:T(8,128)(2,1)S(1)}, u32[]{:S(2)}, u32[]{:S(2)}) collective-permute-start(bf16[144,256]{1,0:T(8,128)(2,1)S(1)} %get-tuple-element.53), channel_id=1, source_target_pairs={{0,2},{1,3},{2,0},{3,1},{4,6},{5,7},{6,4},{7,5},{8,10},{9,11},{10,... | collective-permute-start | bytes 221192 | tf_op jit(solution)/shard_map/ppermute | solution.py:20
  39.8 7.3 %collective-permute-start.17 = (f32[8,128]{1,0:T(8,128)S(1)}, f32[8,128]{1,0:T(8,128)S(1)}, u32[]{:S(2)}, u32[]{:S(2)}) collective-permute-start(f32[8,128]{1,0:T(8,128)S(1)} %add_add_fusion.tile.refs_4_), channel_id=1, source_target_pairs={{0,1},{1,0},{2,3},{3,2},{4,5},{5,4},{6,7},{7,6},{8,9},{9,8},{10,11... | collective-permute-start | bytes 12296 | tf_op jit(solution)/shard_map/ppermute | solution.py:20
  40.6 6.5 %collective-permute-start.18 = (f32[8,128]{1,0:T(8,128)S(1)}, f32[8,128]{1,0:T(8,128)S(1)}, u32[]{:S(2)}, u32[]{:S(2)}) collective-permute-start(f32[8,128]{1,0:T(8,128)S(1)} %add_add_fusion.tile.refs_4_), channel_id=1, source_target_pairs={{0,3},{1,2},{2,1},{3,0},{4,7},{5,6},{6,5},{7,4},{8,11},{9,10},{10,... | collective-permute-start | bytes 12296 | tf_op jit(solution)/shard_map/ppermute | solution.py:20

commit v23 on v22

--- a/solution.py
+++ b/solution.py
@@ -274,15 +274,6 @@
 def add_places(tile, axis, masks):
     parts = [tile] + [swap(tile, axis, mask) for mask in masks]
     return sum(parts[1:], parts[0])
-
-
-def steps_of(count, low):
-    steps = []
-    while 1 << low < count:
-        unit = 1 << low
-        steps.append([unit, 2 * unit, 3 * unit] if 2 * unit < count else [unit])
-        low += 2
-    return steps
 
 
 def call(kernel, name, flops, moved, limit, **kwargs):
@@ -397,9 +388,14 @@
         sums.append((keep, swap(send, "term", 1)))
         first += size
 
-    for masks in [[1]] + steps_of(sectors, 1):
-        tile = add_places(tile, "sec", masks)
-
+    step = 1
+    while step < sectors:
+        tile = add_places(tile, "sec", [step])
+        if step == 2:
+            keep, received = sums[0]
+            received, tile = lax.optimization_barrier((received, tile))
+            sums[0] = (keep, received)
+        step *= 2
     step = 2
     while 2 * step < shares:
         tile = add_places(tile, "term", [step])

time: 49.3 us -> 49 us (level); the launches traced: 48.6 us -> 48.9 us
  waiting for transfers between devices: 14.8 us -> 15.8 us
    ppermute x19 -> x18, waiting for transfers between devices: 14.8 us -> 15.8 us  [swap(): lax.ppermute(value, axis, [(place, place ^ masks[place & 1]) for place in...]
    ppermute x19 -> x18, starting transfers between devices: 23.9 us -> 23.5 us  [swap(): lax.ppermute(value, axis, [(place, place ^ masks[place & 1]) for place in...]
  transfers between devices with their start and end apart: 19 -> 18, of which waited for: 8 -> 9; matrix products, arithmetic and copies ran while one was open for 0% -> 0% of each run, Pallas kernels for 11% -> 11%
where the time goes in v23:
time: 49 us; the launch traced here: 48.9 us
  starting transfers between devices  23.5 us (48%)
  waiting for transfers between devices  15.8 us (32%)
  Pallas kernels  6.71 us (14%)
  local copies, waits for them, and re-layouts  2.22 us (5%)
  between operations  0.71 us (1%)
    ppermute x18, starting transfers between devices, swap(): lax.ppermute(value, axis, [(place, place ^ masks[place & 1]) for place in...  23.5 us
    ppermute x18, waiting for transfers between devices, swap(): lax.ppermute(value, axis, [(place, place ^ masks[place & 1]) for place in...  15.8 us
    pallas_call x3, Pallas kernels, sums_of(): call(kernel, name, flops, MIB, 12 * MIB, out_shape=(share_of(shares // 2,...  3.29 us
    unnamed x4, local copies, waits for them, and re-layouts  2.22 us
    pallas_call x1, Pallas kernels, local(): call(functools.partial(early_kernel, sectors), 'early_products', 2 * term...  1.49 us
    pallas_call x1, Pallas kernels, local(): call(functools.partial(inner_kernel, 1.0 / shares), 'inner_products', 2 *...  1.03 us
  transfers between devices with their start and end apart: 18, of which 9 were waited for; matrix products, arithmetic and copies ran while one was open for 0% of the time, Pallas kernels for 11%

profile of v23, /device:TPU:0, one launch (start us, length us, event | category | flops | bytes accessed | tf_op | source)
XLA Modules:
  0.0 48.9 jit_solution(6162260334200208681)
XLA Ops:
  0.6 3.0 %collective-permute-start.1 = (bf16[3,256,256]{2,1,0:T(8,128)(2,1)}, bf16[3,256,256]{2,1,0:T(8,128)(2,1)S(1)}, u32[]{:S(2)}, u32[]{:S(2)}) collective-permute-start(bf16[3,256,256]{2,1,0:T(8,128)(2,1)} %bitcast.12), channel_id=1, source_target_pairs={{0,16},{4,12},{8,24},{12,4},{16,0},{20,28},{24,8},{28,20},{1,17},{... | collective-permute-start | bytes 1179656 | tf_op jit(solution)/shard_map/ppermute | solution.py:20
  3.7 1.2 %copy-done = bf16[2,1,4,256,256]{4,3,2,1,0:T(8,128)(2,1)S(1)} copy-done((bf16[2,1,4,256,256]{4,3,2,1,0:T(8,128)(2,1)S(1)}, bf16[2,1,4,256,256]{4,3,2,1,0:T(8,128)(2,1)}, u32[]{:S(2)}) %copy-start) | copy-done | bytes 1048600
  4.9 1.0 %copy-done.1 = bf16[3,1,256,256]{3,2,1,0:T(8,128)(2,1)S(1)} copy-done((bf16[3,1,256,256]{3,2,1,0:T(8,128)(2,1)S(1)}, bf16[3,1,256,256]{3,2,1,0:T(8,128)(2,1)}, u32[]{:S(2)}) %copy-start.1) | copy-done | bytes 393240
  5.9 1.0 %inner_products.1 = (bf16[2,4,256,768]{3,2,1,0:T(8,128)(2,1)S(1)}, f32[8,128]{1,0:T(8,128)S(1)}, bf16[3,256,256]{2,1,0:T(8,128)(2,1)S(1)}, s32[3,4]{1,0:T(4,128)S(1)}) custom-call(bf16[2,4,256,256]{3,2,1,0:T(8,128)(2,1)S(1)} %bitcast.6, bf16[3,256,256]{2,1,0:T(8,128)(2,1)S(1)} %bitcast.11, bf16[3,256,256]{2,1,0:T(8,128)(2,1)} %bitcast.13, s32[3,4]{1,0:T(4,128)} %offsets_hbm.1), custom_call_target="tpu_custom_call" | custom-call | flops 805306368 | bytes 5242880 | tf_op jit(solution)/shard_map/inner_products/pallas_call | solution.py:297
  6.9 1.6 %collective-permute-start.3 = (bf16[3,256,256]{2,1,0:T(8,128)(2,1)}, bf16[3,256,256]{2,1,0:T(8,128)(2,1)S(1)}, u32[]{:S(2)}, u32[]{:S(2)}) collective-permute-start(bf16[3,256,256]{2,1,0:T(8,128)(2,1)} %bitcast.14), channel_id=1, source_target_pairs={{0,8},{4,20},{8,0},{12,28},{16,24},{20,4},{24,16},{28,12},{1,9},{5... | collective-permute-start | bytes 1179656 | tf_op jit(solution)/shard_map/ppermute | solution.py:20
  8.5 1.5 %collective-permute-done.1.rest_2_ = bf16[3,256,256]{2,1,0:T(8,128)(2,1)S(1)} collective-permute-done((bf16[3,256,256]{2,1,0:T(8,128)(2,1)}, bf16[3,256,256]{2,1,0:T(8,128)(2,1)S(1)}, u32[]{:S(2)}, u32[]{:S(2)}) %collective-permute-start.1) | collective-permute-done | bytes 393248 | tf_op jit(solution)/shard_map/ppermute | solution.py:20
  10.0 3.5 %collective-permute-start.5 = (bf16[3,256,256]{2,1,0:T(8,128)(2,1)S(1)}, bf16[3,256,256]{2,1,0:T(8,128)(2,1)S(1)}, u32[]{:S(2)}, u32[]{:S(2)}) collective-permute-start(bf16[3,256,256]{2,1,0:T(8,128)(2,1)S(1)} %collective-permute-done.1.rest_2_), channel_id=1, source_target_pairs={{0,8},{4,20},{8,0},{12,28},{16,24},{20,4},{24,16},{28,12},{1,9},{5... | collective-permute-start | bytes 1179656 | tf_op jit(solution)/shard_map/ppermute | solution.py:20
  13.5 1.4 %collective-permute-done.3.rest_4_ = bf16[3,256,256]{2,1,0:T(8,128)(2,1)S(1)} collective-permute-done((bf16[3,256,256]{2,1,0:T(8,128)(2,1)}, bf16[3,256,256]{2,1,0:T(8,128)(2,1)S(1)}, u32[]{:S(2)}, u32[]{:S(2)}) %collective-permute-start.3) | collective-permute-done | bytes 393248 | tf_op jit(solution)/shard_map/ppermute | solution.py:20
  15.5 3.8 %collective-permute-done.5.rest_6_ = bf16[3,256,256]{2,1,0:T(8,128)(2,1)S(1)} collective-permute-done((bf16[3,256,256]{2,1,0:T(8,128)(2,1)S(1)}, bf16[3,256,256]{2,1,0:T(8,128)(2,1)S(1)}, u32[]{:S(2)}, u32[]{:S(2)}) %collective-permute-start.5) | collective-permute-done | bytes 393248 | tf_op jit(solution)/shard_map/ppermute | solution.py:20
  19.3 1.5 %early_products.1 = (f32[2,2,256,256]{3,2,1,0:T(8,128)S(1)}, f32[8,128]{1,0:T(8,128)S(1)}, bf16[8,3,256,256]{3,2,1,0:T(8,128)(2,1)S(1)}) custom-call(s32[3,4]{1,0:T(4,128)S(1)} %get-tuple-element.31.offsets, bf16[2,4,256,256]{3,2,1,0:T(8,128)(2,1)S(1)} %bitcast.7, bf16[2,4,256,768]{3,2,1,0:T(8,128)(2,1)S(1)} %get-tuple-element.32.inner, ...), custom_call_target="tpu_custom_call" | custom-call | flops 402653184 | bytes 4194304 | tf_op jit(solution)/shard_map/early_products/pallas_call | solution.py:328
  21.8 1.5 %collective-permute-start.7 = (bf16[2,2,2,64,256]{4,3,2,1,0:T(8,128)(2,1)S(1)}, bf16[2,2,2,64,256]{4,3,2,1,0:T(8,128)(2,1)S(1)}, u32[]{:S(2)}, u32[]{:S(2)}) collective-permute-start(bf16[2,2,2,64,256]{4,3,2,1,0:T(8,128)(2,1)S(1)} %get-tuple-element.39), channel_id=1, source_target_pairs={{0,1},{1,0},{2,3},{3,2},{4,5},{5,4},{6,7},{7,6},{8,9},{9,8},{10,11... | collective-permute-start | bytes 786440 | tf_op jit(solution)/shard_map/ppermute | solution.py:20
  23.2 1.4 %other_products.2 = (f32[2,2,1,64,256]{4,3,2,1,0:T(8,128)S(1)}, bf16[2,2,1,64,256]{4,3,2,1,0:T(8,128)(2,1)S(1)}, f32[8,128]{1,0:T(8,128)S(1)}) custom-call(s32[3,4]{1,0:T(4,128)S(1)} %get-tuple-element.31.offsets, bf16[2,4,256,256]{3,2,1,0:T(8,128)(2,1)S(1)} %bitcast.9, bf16[2,4,256,768]{3,2,1,0:T(8,128)(2,1)S(1)} %get-tuple-element.32.inner, ...), custom_call_target="tpu_custom_call" | custom-call | flops 201326592 | bytes 1048576 | tf_op jit(solution)/shard_map/other_products/pallas_call | solution.py:345
  25.2 1.2 %other_products.3 = (f32[2,2,1,64,256]{4,3,2,1,0:T(8,128)S(1)}, bf16[2,2,1,64,256]{4,3,2,1,0:T(8,128)(2,1)S(1)}, f32[8,128]{1,0:T(8,128)S(1)}) custom-call(s32[3,4]{1,0:T(4,128)S(1)} %get-tuple-element.31.offsets, bf16[2,4,256,256]{3,2,1,0:T(8,128)(2,1)S(1)} %bitcast.10, bf16[2,4,256,768]{3,2,1,0:T(8,128)(2,1)S(1)} %get-tuple-element.32.inner, ...), custom_call_target="tpu_custom_call" | custom-call | flops 201326592 | bytes 1048576 | tf_op jit(solution)/shard_map/other_products/pallas_call | solution.py:345
  26.4 1.5 %collective-permute-start.13 = (bf16[2,2,1,64,256]{4,3,2,1,0:T(8,128)(2,1)S(1)}, bf16[2,2,1,64,256]{4,3,2,1,0:T(8,128)(2,1)S(1)}, u32[]{:S(2)}, u32[]{:S(2)}) collective-permute-start(bf16[2,2,1,64,256]{4,3,2,1,0:T(8,128)(2,1)S(1)} %get-tuple-element.53), channel_id=1, source_target_pairs={{0,1},{1,0},{2,3},{3,2},{4,5},{5,4},{6,7},{7,6},{8,9},{9,8},{10,11... | collective-permute-start | bytes 393224 | tf_op jit(solution)/shard_map/ppermute | solution.py:20
  27.9 1.2 %collective-permute-done.8 = f32[8,128]{1,0:T(8,128)S(1)} collective-permute-done((f32[8,128]{1,0:T(8,128)S(1)}, f32[8,128]{1,0:T(8,128)S(1)}, u32[]{:S(2)}, u32[]{:S(2)}) %collective-permute-start.8) | collective-permute-done | bytes 4128 | tf_op jit(solution)/shard_map/ppermute | solution.py:20
  29.0 1.9 %collective-permute-start.9 = (f32[8,128]{1,0:T(8,128)S(1)}, f32[8,128]{1,0:T(8,128)S(1)}, u32[]{:S(2)}, u32[]{:S(2)}) collective-permute-start(f32[8,128]{1,0:T(8,128)S(1)} %add.9), channel_id=1, source_target_pairs={{0,8},{4,12},{8,0},{12,4},{16,24},{20,28},{24,16},{28,20},{1,9},{5... | collective-permute-start | bytes 12296 | tf_op jit(solution)/shard_map/ppermute | solution.py:20
  30.9 1.7 %collective-permute-done.9 = f32[8,128]{1,0:T(8,128)S(1)} collective-permute-done((f32[8,128]{1,0:T(8,128)S(1)}, f32[8,128]{1,0:T(8,128)S(1)}, u32[]{:S(2)}, u32[]{:S(2)}) %collective-permute-start.9) | collective-permute-done | bytes 4128 | tf_op jit(solution)/shard_map/ppermute | solution.py:20
  32.7 2.9 %collective-permute-start.10 = (bf16[1,2,2,64,256]{4,3,2,1,0:T(8,128)(2,1)S(1)}, bf16[1,2,2,64,256]{4,3,2,1,0:T(8,128)(2,1)S(1)}, u32[]{:S(2)}, u32[]{:S(2)}) collective-permute-start(bf16[1,2,2,64,256]{4,3,2,1,0:T(8,128)(2,1)S(1)} %get-tuple-element.46), channel_id=1, source_target_pairs={{0,2},{1,3},{2,0},{3,1},{4,6},{5,7},{6,4},{7,5},{8,10},{9,11},{10,... | collective-permute-start | bytes 393224 | tf_op jit(solution)/shard_map/ppermute | solution.py:20
  36.3 1.4 %collective-permute-start.14 = (f32[8,128]{1,0:T(8,128)S(1)}, f32[8,128]{1,0:T(8,128)S(1)}, u32[]{:S(2)}, u32[]{:S(2)}) collective-permute-start(f32[8,128]{1,0:T(8,128)S(1)} %add.10), channel_id=1, source_target_pairs={{0,16},{4,20},{8,24},{12,28},{16,0},{20,4},{24,8},{28,12},{1,17},{... | collective-permute-start | bytes 12296 | tf_op jit(solution)/shard_map/ppermute | solution.py:20
  37.7 2.2 %collective-permute-done.14 = f32[8,128]{1,0:T(8,128)S(1)} collective-permute-done((f32[8,128]{1,0:T(8,128)S(1)}, f32[8,128]{1,0:T(8,128)S(1)}, u32[]{:S(2)}, u32[]{:S(2)}) %collective-permute-start.14) | collective-permute-done | bytes 4128 | tf_op jit(solution)/shard_map/ppermute | solution.py:20
  39.9 2.4 %collective-permute-start.15 = (bf16[144,256]{1,0:T(8,128)(2,1)S(1)}, bf16[144,256]{1,0:T(8,128)(2,1)S(1)}, u32[]{:S(2)}, u32[]{:S(2)}) collective-permute-start(bf16[144,256]{1,0:T(8,128)(2,1)S(1)} %get-tuple-element.57), channel_id=1, source_target_pairs={{0,2},{1,3},{2,0},{3,1},{4,6},{5,7},{6,4},{7,5},{8,10},{9,11},{10,... | collective-permute-start | bytes 221192 | tf_op jit(solution)/shard_map/ppermute | solution.py:20
  42.7 1.6 %collective-permute-start.17 = (f32[8,128]{1,0:T(8,128)S(1)}, f32[8,128]{1,0:T(8,128)S(1)}, u32[]{:S(2)}, u32[]{:S(2)}) collective-permute-start(f32[8,128]{1,0:T(8,128)S(1)} %add.11.tile.refs_4_), channel_id=1, source_target_pairs={{0,3},{1,2},{2,1},{3,0},{4,7},{5,6},{6,5},{7,4},{8,11},{9,10},{10,... | collective-permute-start | bytes 12296 | tf_op jit(solution)/shard_map/ppermute | solution.py:20
  44.4 2.4 %collective-permute-done.12.received = bf16[1,2,1,64,256]{4,3,2,1,0:T(8,128)(2,1)S(1)} collective-permute-done((bf16[1,2,1,64,256]{4,3,2,1,0:T(8,128)(2,1)S(1)}, bf16[1,2,1,64,256]{4,3,2,1,0:T(8,128)(2,1)S(1)}, u32[]{:S(2)}, u32[]{:S(2)}) %collective-permute-start.12) | collective-permute-done | bytes 65568 | tf_op jit(solution)/shard_map/ppermute | solution.py:20
  46.9 1.3 %collective-permute-done.17.refs_6_ = f32[8,128]{1,0:T(8,128)S(1)} collective-permute-done((f32[8,128]{1,0:T(8,128)S(1)}, f32[8,128]{1,0:T(8,128)S(1)}, u32[]{:S(2)}, u32[]{:S(2)}) %collective-permute-start.17) | collective-permute-done | bytes 4128 | tf_op jit(solution)/shard_map/ppermute | solution.py:20
  (30 shorter events, 4.1 us)
Async XLA Ops:
  0.6 9.4 %collective-permute-start.1 = (bf16[3,256,256]{2,1,0:T(8,128)(2,1)}, bf16[3,256,256]{2,1,0:T(8,128)(2,1)S(1)}, u32[]{:S(2)}, u32[]{:S(2)}) collective-permute-start(bf16[3,256,256]{2,1,0:T(8,128)(2,1)} %bitcast.12), channel_id=1, source_target_pairs={{0,16},{4,12},{8,24},{12,4},{16,0},{20,28},{24,8},{28,20},{1,17},{... | collective-permute-start | bytes 1179656 | tf_op jit(solution)/shard_map/ppermute | solution.py:20
  3.7 1.2 %copy-start = (bf16[2,1,4,256,256]{4,3,2,1,0:T(8,128)(2,1)S(1)}, bf16[2,1,4,256,256]{4,3,2,1,0:T(8,128)(2,1)}, u32[]{:S(2)}) copy-start(bf16[2,1,4,256,256]{4,3,2,1,0:T(8,128)(2,1)} %param.4) | copy-start | bytes 3145732
  4.9 1.0 %copy-start.1 = (bf16[3,1,256,256]{3,2,1,0:T(8,128)(2,1)S(1)}, bf16[3,1,256,256]{3,2,1,0:T(8,128)(2,1)}, u32[]{:S(2)}) copy-start(bf16[3,1,256,256]{3,2,1,0:T(8,128)(2,1)} %param.5) | copy-start | bytes 1179652
  6.9 8.1 %collective-permute-start.3 = (bf16[3,256,256]{2,1,0:T(8,128)(2,1)}, bf16[3,256,256]{2,1,0:T(8,128)(2,1)S(1)}, u32[]{:S(2)}, u32[]{:S(2)}) collective-permute-start(bf16[3,256,256]{2,1,0:T(8,128)(2,1)} %bitcast.14), channel_id=1, source_target_pairs={{0,8},{4,20},{8,0},{12,28},{16,24},{20,4},{24,16},{28,12},{1,9},{5... | collective-permute-start | bytes 1179656 | tf_op jit(solution)/shard_map/ppermute | solution.py:20
  10.0 9.3 %collective-permute-start.5 = (bf16[3,256,256]{2,1,0:T(8,128)(2,1)S(1)}, bf16[3,256,256]{2,1,0:T(8,128)(2,1)S(1)}, u32[]{:S(2)}, u32[]{:S(2)}) collective-permute-start(bf16[3,256,256]{2,1,0:T(8,128)(2,1)S(1)} %collective-permute-done.1.rest_2_), channel_id=1, source_target_pairs={{0,8},{4,20},{8,0},{12,28},{16,24},{20,4},{24,16},{28,12},{1,9},{5... | collective-permute-start | bytes 1179656 | tf_op jit(solution)/shard_map/ppermute | solution.py:20
  13.5 5.8 %collective-permute-start = (bf16[3,256,256]{2,1,0:T(8,128)(2,1)}, bf16[3,256,256]{2,1,0:T(8,128)(2,1)S(1)}, u32[]{:S(2)}, u32[]{:S(2)}) collective-permute-start(bf16[3,256,256]{2,1,0:T(8,128)(2,1)} %bitcast.15), channel_id=1, source_target_pairs={{0,4},{4,0},{8,12},{12,8},{16,20},{20,16},{24,28},{28,24},{1,5},{5... | collective-permute-start | bytes 1179656 | tf_op jit(solution)/shard_map/ppermute | solution.py:20
  15.0 4.3 %collective-permute-start.4 = (bf16[3,256,256]{2,1,0:T(8,128)(2,1)S(1)}, bf16[3,256,256]{2,1,0:T(8,128)(2,1)S(1)}, u32[]{:S(2)}, u32[]{:S(2)}) collective-permute-start(bf16[3,256,256]{2,1,0:T(8,128)(2,1)S(1)} %collective-permute-done.3.rest_4_), channel_id=1, source_target_pairs={{0,4},{4,0},{8,12},{12,8},{16,20},{20,16},{24,28},{28,24},{1,5},{5... | collective-permute-start | bytes 1179656 | tf_op jit(solution)/shard_map/ppermute | solution.py:20
  15.0 4.3 %collective-permute-start.2 = (bf16[3,256,256]{2,1,0:T(8,128)(2,1)S(1)}, bf16[3,256,256]{2,1,0:T(8,128)(2,1)S(1)}, u32[]{:S(2)}, u32[]{:S(2)}) collective-permute-start(bf16[3,256,256]{2,1,0:T(8,128)(2,1)S(1)} %collective-permute-done.1.rest_2_), channel_id=1, source_target_pairs={{0,4},{4,0},{8,12},{12,8},{16,20},{20,16},{24,28},{28,24},{1,5},{5... | collective-permute-start | bytes 1179656 | tf_op jit(solution)/shard_map/ppermute | solution.py:20
  19.3 1.7 %collective-permute-start.6 = (bf16[3,256,256]{2,1,0:T(8,128)(2,1)S(1)}, bf16[3,256,256]{2,1,0:T(8,128)(2,1)S(1)}, u32[]{:S(2)}, u32[]{:S(2)}) collective-permute-start(bf16[3,256,256]{2,1,0:T(8,128)(2,1)S(1)} %collective-permute-done.5.rest_6_), channel_id=1, source_target_pairs={{0,4},{4,0},{8,12},{12,8},{16,20},{20,16},{24,28},{28,24},{1,5},{5... | collective-permute-start | bytes 1179656 | tf_op jit(solution)/shard_map/ppermute | solution.py:20
  21.8 10.9 %collective-permute-start.7 = (bf16[2,2,2,64,256]{4,3,2,1,0:T(8,128)(2,1)S(1)}, bf16[2,2,2,64,256]{4,3,2,1,0:T(8,128)(2,1)S(1)}, u32[]{:S(2)}, u32[]{:S(2)}) collective-permute-start(bf16[2,2,2,64,256]{4,3,2,1,0:T(8,128)(2,1)S(1)} %get-tuple-element.39), channel_id=1, source_target_pairs={{0,1},{1,0},{2,3},{3,2},{4,5},{5,4},{6,7},{7,6},{8,9},{9,8},{10,11... | collective-permute-start | bytes 786440 | tf_op jit(solution)/shard_map/ppermute | solution.py:20
  24.6 10.9 %collective-permute-start.11 = (bf16[2,2,1,64,256]{4,3,2,1,0:T(8,128)(2,1)S(1)}, bf16[2,2,1,64,256]{4,3,2,1,0:T(8,128)(2,1)S(1)}, u32[]{:S(2)}, u32[]{:S(2)}) collective-permute-start(bf16[2,2,1,64,256]{4,3,2,1,0:T(8,128)(2,1)S(1)} %get-tuple-element.48), channel_id=1, source_target_pairs={{0,1},{1,0},{2,3},{3,2},{4,5},{5,4},{6,7},{7,6},{8,9},{9,8},{10,11... | collective-permute-start | bytes 393224 | tf_op jit(solution)/shard_map/ppermute | solution.py:20
  26.4 11.3 %collective-permute-start.13 = (bf16[2,2,1,64,256]{4,3,2,1,0:T(8,128)(2,1)S(1)}, bf16[2,2,1,64,256]{4,3,2,1,0:T(8,128)(2,1)S(1)}, u32[]{:S(2)}, u32[]{:S(2)}) collective-permute-start(bf16[2,2,1,64,256]{4,3,2,1,0:T(8,128)(2,1)S(1)} %get-tuple-element.53), channel_id=1, source_target_pairs={{0,1},{1,0},{2,3},{3,2},{4,5},{5,4},{6,7},{7,6},{8,9},{9,8},{10,11... | collective-permute-start | bytes 393224 | tf_op jit(solution)/shard_map/ppermute | solution.py:20
  27.8 1.2 %collective-permute-start.8 = (f32[8,128]{1,0:T(8,128)S(1)}, f32[8,128]{1,0:T(8,128)S(1)}, u32[]{:S(2)}, u32[]{:S(2)}) collective-permute-start(f32[8,128]{1,0:T(8,128)S(1)} %get-tuple-element.43), channel_id=1, source_target_pairs={{0,4},{4,0},{8,12},{12,8},{16,20},{20,16},{24,28},{28,24},{1,5},{5... | collective-permute-start | bytes 12296 | tf_op jit(solution)/shard_map/ppermute | solution.py:20
  29.0 3.6 %collective-permute-start.9 = (f32[8,128]{1,0:T(8,128)S(1)}, f32[8,128]{1,0:T(8,128)S(1)}, u32[]{:S(2)}, u32[]{:S(2)}) collective-permute-start(f32[8,128]{1,0:T(8,128)S(1)} %add.9), channel_id=1, source_target_pairs={{0,8},{4,12},{8,0},{12,4},{16,24},{20,28},{24,16},{28,20},{1,9},{5... | collective-permute-start | bytes 12296 | tf_op jit(solution)/shard_map/ppermute | solution.py:20
  32.7 14.1 %collective-permute-start.10 = (bf16[1,2,2,64,256]{4,3,2,1,0:T(8,128)(2,1)S(1)}, bf16[1,2,2,64,256]{4,3,2,1,0:T(8,128)(2,1)S(1)}, u32[]{:S(2)}, u32[]{:S(2)}) collective-permute-start(bf16[1,2,2,64,256]{4,3,2,1,0:T(8,128)(2,1)S(1)} %get-tuple-element.46), channel_id=1, source_target_pairs={{0,2},{1,3},{2,0},{3,1},{4,6},{5,7},{6,4},{7,5},{8,10},{9,11},{10,... | collective-permute-start | bytes 393224 | tf_op jit(solution)/shard_map/ppermute | solution.py:20
  35.6 11.2 %collective-permute-start.12 = (bf16[1,2,1,64,256]{4,3,2,1,0:T(8,128)(2,1)S(1)}, bf16[1,2,1,64,256]{4,3,2,1,0:T(8,128)(2,1)S(1)}, u32[]{:S(2)}, u32[]{:S(2)}) collective-permute-start(bf16[1,2,1,64,256]{4,3,2,1,0:T(8,128)(2,1)S(1)} %get-tuple-element.51), channel_id=1, source_target_pairs={{0,2},{1,3},{2,0},{3,1},{4,6},{5,7},{6,4},{7,5},{8,10},{9,11},{10,... | collective-permute-start | bytes 196616 | tf_op jit(solution)/shard_map/ppermute | solution.py:20
  36.3 3.6 %collective-permute-start.14 = (f32[8,128]{1,0:T(8,128)S(1)}, f32[8,128]{1,0:T(8,128)S(1)}, u32[]{:S(2)}, u32[]{:S(2)}) collective-permute-start(f32[8,128]{1,0:T(8,128)S(1)} %add.10), channel_id=1, source_target_pairs={{0,16},{4,20},{8,24},{12,28},{16,0},{20,4},{24,8},{28,12},{1,17},{... | collective-permute-start | bytes 12296 | tf_op jit(solution)/shard_map/ppermute | solution.py:20
  39.9 8.2 %collective-permute-start.15 = (bf16[144,256]{1,0:T(8,128)(2,1)S(1)}, bf16[144,256]{1,0:T(8,128)(2,1)S(1)}, u32[]{:S(2)}, u32[]{:S(2)}) collective-permute-start(bf16[144,256]{1,0:T(8,128)(2,1)S(1)} %get-tuple-element.57), channel_id=1, source_target_pairs={{0,2},{1,3},{2,0},{3,1},{4,6},{5,7},{6,4},{7,5},{8,10},{9,11},{10,... | collective-permute-start | bytes 221192 | tf_op jit(solution)/shard_map/ppermute | solution.py:20
  42.3 4.5 %collective-permute-start.16 = (f32[8,128]{1,0:T(8,128)S(1)}, f32[8,128]{1,0:T(8,128)S(1)}, u32[]{:S(2)}, u32[]{:S(2)}) collective-permute-start(f32[8,128]{1,0:T(8,128)S(1)} %add.11.tile.refs_4_), channel_id=1, source_target_pairs={{0,1},{1,0},{2,3},{3,2},{4,5},{5,4},{6,7},{7,6},{8,9},{9,8},{10,11... | collective-permute-start | bytes 12296 | tf_op jit(solution)/shard_map/ppermute | solution.py:20
  42.7 5.4 %collective-permute-start.17 = (f32[8,128]{1,0:T(8,128)S(1)}, f32[8,128]{1,0:T(8,128)S(1)}, u32[]{:S(2)}, u32[]{:S(2)}) collective-permute-start(f32[8,128]{1,0:T(8,128)S(1)} %add.11.tile.refs_4_), channel_id=1, source_target_pairs={{0,3},{1,2},{2,1},{3,0},{4,7},{5,6},{6,5},{7,4},{8,11},{9,10},{10,... | collective-permute-start | bytes 12296 | tf_op jit(solution)/shard_map/ppermute | solution.py:20

commit v24 on v23

--- a/solution.py
+++ b/solution.py
@@ -438,7 +438,7 @@
             call(
                 add_last_kernel,
                 "add_last_share",
-                10**8,
+                [10**10,1][chunk],
                 1,
                 8 * MIB,
                 out_shape=jax.ShapeDtypeStruct((trials, size, rows, states), jnp.bfloat16),

time: 49 us -> 49.4 us (level)
  starting transfers between devices: 23.5 us -> 24.3 us
  waiting for transfers between devices: 15.8 us -> 15.1 us
    ppermute x18, starting transfers between devices: 23.5 us -> 24.3 us  [swap(): lax.ppermute(value, axis, [(place, place ^ masks[place & 1]) for place in...]
    ppermute x18, waiting for transfers between devices: 15.8 us -> 15.1 us  [swap(): lax.ppermute(value, axis, [(place, place ^ masks[place & 1]) for place in...]
where the time goes in v24:
time: 49.4 us; the launch traced here: 49 us
  starting transfers between devices  24.3 us (49%)
  waiting for transfers between devices  15.1 us (31%)
  Pallas kernels  6.7 us (14%)
  local copies, waits for them, and re-layouts  2.22 us (4%)
  between operations  0.72 us (1%)
    ppermute x18, starting transfers between devices, swap(): lax.ppermute(value, axis, [(place, place ^ masks[place & 1]) for place in...  24.3 us
    ppermute x18, waiting for transfers between devices, swap(): lax.ppermute(value, axis, [(place, place ^ masks[place & 1]) for place in...  15.1 us
    pallas_call x3, Pallas kernels, sums_of(): call(kernel, name, flops, MIB, 12 * MIB, out_shape=(share_of(shares // 2,...  3.28 us
    unnamed x4, local copies, waits for them, and re-layouts  2.22 us
    pallas_call x1, Pallas kernels, local(): call(functools.partial(early_kernel, sectors), 'early_products', 2 * term...  1.49 us
    pallas_call x1, Pallas kernels, local(): call(functools.partial(inner_kernel, 1.0 / shares), 'inner_products', 2 *...  1.03 us
  transfers between devices with their start and end apart: 18, of which 9 were waited for; matrix products, arithmetic and copies ran while one was open for 0% of the time, Pallas kernels for 11%

profile of v24, /device:TPU:0, one launch (start us, length us, event | category | flops | bytes accessed | tf_op | source)
XLA Modules:
  0.0 49.0 jit_solution(18238276220014074163)
XLA Ops:
  0.6 3.0 %collective-permute-start.1 = (bf16[3,256,256]{2,1,0:T(8,128)(2,1)}, bf16[3,256,256]{2,1,0:T(8,128)(2,1)S(1)}, u32[]{:S(2)}, u32[]{:S(2)}) collective-permute-start(bf16[3,256,256]{2,1,0:T(8,128)(2,1)} %bitcast.12), channel_id=1, source_target_pairs={{0,16},{4,12},{8,24},{12,4},{16,0},{20,28},{24,8},{28,20},{1,17},{... | collective-permute-start | bytes 1179656 | tf_op jit(solution)/shard_map/ppermute | solution.py:20
  3.7 1.2 %copy-done = bf16[2,1,4,256,256]{4,3,2,1,0:T(8,128)(2,1)S(1)} copy-done((bf16[2,1,4,256,256]{4,3,2,1,0:T(8,128)(2,1)S(1)}, bf16[2,1,4,256,256]{4,3,2,1,0:T(8,128)(2,1)}, u32[]{:S(2)}) %copy-start) | copy-done | bytes 1048600
  5.9 1.0 %inner_products.1 = (bf16[2,4,256,768]{3,2,1,0:T(8,128)(2,1)S(1)}, f32[8,128]{1,0:T(8,128)S(1)}, bf16[3,256,256]{2,1,0:T(8,128)(2,1)S(1)}, s32[3,4]{1,0:T(4,128)S(1)}) custom-call(bf16[2,4,256,256]{3,2,1,0:T(8,128)(2,1)S(1)} %bitcast.6, bf16[3,256,256]{2,1,0:T(8,128)(2,1)S(1)} %bitcast.11, bf16[3,256,256]{2,1,0:T(8,128)(2,1)} %bitcast.13, s32[3,4]{1,0:T(4,128)} %offsets_hbm.1), custom_call_target="tpu_custom_call" | custom-call | flops 805306368 | bytes 5242880 | tf_op jit(solution)/shard_map/inner_products/pallas_call | solution.py:297
  6.9 1.6 %collective-permute-start.3 = (bf16[3,256,256]{2,1,0:T(8,128)(2,1)}, bf16[3,256,256]{2,1,0:T(8,128)(2,1)S(1)}, u32[]{:S(2)}, u32[]{:S(2)}) collective-permute-start(bf16[3,256,256]{2,1,0:T(8,128)(2,1)} %bitcast.14), channel_id=1, source_target_pairs={{0,8},{4,20},{8,0},{12,28},{16,24},{20,4},{24,16},{28,12},{1,9},{5... | collective-permute-start | bytes 1179656 | tf_op jit(solution)/shard_map/ppermute | solution.py:20
  8.5 1.5 %collective-permute-done.1.rest_2_ = bf16[3,256,256]{2,1,0:T(8,128)(2,1)S(1)} collective-permute-done((bf16[3,256,256]{2,1,0:T(8,128)(2,1)}, bf16[3,256,256]{2,1,0:T(8,128)(2,1)S(1)}, u32[]{:S(2)}, u32[]{:S(2)}) %collective-permute-start.1) | collective-permute-done | bytes 393248 | tf_op jit(solution)/shard_map/ppermute | solution.py:20
  10.0 3.5 %collective-permute-start.5 = (bf16[3,256,256]{2,1,0:T(8,128)(2,1)S(1)}, bf16[3,256,256]{2,1,0:T(8,128)(2,1)S(1)}, u32[]{:S(2)}, u32[]{:S(2)}) collective-permute-start(bf16[3,256,256]{2,1,0:T(8,128)(2,1)S(1)} %collective-permute-done.1.rest_2_), channel_id=1, source_target_pairs={{0,8},{4,20},{8,0},{12,28},{16,24},{20,4},{24,16},{28,12},{1,9},{5... | collective-permute-start | bytes 1179656 | tf_op jit(solution)/shard_map/ppermute | solution.py:20
  13.5 1.4 %collective-permute-done.3.rest_4_ = bf16[3,256,256]{2,1,0:T(8,128)(2,1)S(1)} collective-permute-done((bf16[3,256,256]{2,1,0:T(8,128)(2,1)}, bf16[3,256,256]{2,1,0:T(8,128)(2,1)S(1)}, u32[]{:S(2)}, u32[]{:S(2)}) %collective-permute-start.3) | collective-permute-done | bytes 393248 | tf_op jit(solution)/shard_map/ppermute | solution.py:20
  15.5 3.8 %collective-permute-done.5.rest_6_ = bf16[3,256,256]{2,1,0:T(8,128)(2,1)S(1)} collective-permute-done((bf16[3,256,256]{2,1,0:T(8,128)(2,1)S(1)}, bf16[3,256,256]{2,1,0:T(8,128)(2,1)S(1)}, u32[]{:S(2)}, u32[]{:S(2)}) %collective-permute-start.5) | collective-permute-done | bytes 393248 | tf_op jit(solution)/shard_map/ppermute | solution.py:20
  19.3 1.5 %early_products.1 = (f32[2,2,256,256]{3,2,1,0:T(8,128)S(1)}, f32[8,128]{1,0:T(8,128)S(1)}, bf16[8,3,256,256]{3,2,1,0:T(8,128)(2,1)S(1)}) custom-call(s32[3,4]{1,0:T(4,128)S(1)} %get-tuple-element.31.offsets, bf16[2,4,256,256]{3,2,1,0:T(8,128)(2,1)S(1)} %bitcast.7, bf16[2,4,256,768]{3,2,1,0:T(8,128)(2,1)S(1)} %get-tuple-element.32.inner, ...), custom_call_target="tpu_custom_call" | custom-call | flops 402653184 | bytes 4194304 | tf_op jit(solution)/shard_map/early_products/pallas_call | solution.py:328
  21.8 1.5 %collective-permute-start.7 = (bf16[2,2,2,64,256]{4,3,2,1,0:T(8,128)(2,1)S(1)}, bf16[2,2,2,64,256]{4,3,2,1,0:T(8,128)(2,1)S(1)}, u32[]{:S(2)}, u32[]{:S(2)}) collective-permute-start(bf16[2,2,2,64,256]{4,3,2,1,0:T(8,128)(2,1)S(1)} %get-tuple-element.39), channel_id=1, source_target_pairs={{0,1},{1,0},{2,3},{3,2},{4,5},{5,4},{6,7},{7,6},{8,9},{9,8},{10,11... | collective-permute-start | bytes 786440 | tf_op jit(solution)/shard_map/ppermute | solution.py:20
  23.2 1.4 %other_products.2 = (f32[2,2,1,64,256]{4,3,2,1,0:T(8,128)S(1)}, bf16[2,2,1,64,256]{4,3,2,1,0:T(8,128)(2,1)S(1)}, f32[8,128]{1,0:T(8,128)S(1)}) custom-call(s32[3,4]{1,0:T(4,128)S(1)} %get-tuple-element.31.offsets, bf16[2,4,256,256]{3,2,1,0:T(8,128)(2,1)S(1)} %bitcast.9, bf16[2,4,256,768]{3,2,1,0:T(8,128)(2,1)S(1)} %get-tuple-element.32.inner, ...), custom_call_target="tpu_custom_call" | custom-call | flops 201326592 | bytes 1048576 | tf_op jit(solution)/shard_map/other_products/pallas_call | solution.py:345
  24.6 1.0 %collective-permute-start.11 = (bf16[2,2,1,64,256]{4,3,2,1,0:T(8,128)(2,1)S(1)}, bf16[2,2,1,64,256]{4,3,2,1,0:T(8,128)(2,1)S(1)}, u32[]{:S(2)}, u32[]{:S(2)}) collective-permute-start(bf16[2,2,1,64,256]{4,3,2,1,0:T(8,128)(2,1)S(1)} %get-tuple-element.48), channel_id=1, source_target_pairs={{0,1},{1,0},{2,3},{3,2},{4,5},{5,4},{6,7},{7,6},{8,9},{9,8},{10,11... | collective-permute-start | bytes 393224 | tf_op jit(solution)/shard_map/ppermute | solution.py:20
  25.6 1.2 %other_products.3 = (f32[2,2,1,64,256]{4,3,2,1,0:T(8,128)S(1)}, bf16[2,2,1,64,256]{4,3,2,1,0:T(8,128)(2,1)S(1)}, f32[8,128]{1,0:T(8,128)S(1)}) custom-call(s32[3,4]{1,0:T(4,128)S(1)} %get-tuple-element.31.offsets, bf16[2,4,256,256]{3,2,1,0:T(8,128)(2,1)S(1)} %bitcast.10, bf16[2,4,256,768]{3,2,1,0:T(8,128)(2,1)S(1)} %get-tuple-element.32.inner, ...), custom_call_target="tpu_custom_call" | custom-call | flops 201326592 | bytes 1048576 | tf_op jit(solution)/shard_map/other_products/pallas_call | solution.py:345
  26.8 1.2 %collective-permute-done.8 = f32[8,128]{1,0:T(8,128)S(1)} collective-permute-done((f32[8,128]{1,0:T(8,128)S(1)}, f32[8,128]{1,0:T(8,128)S(1)}, u32[]{:S(2)}, u32[]{:S(2)}) %collective-permute-start.8) | collective-permute-done | bytes 4128 | tf_op jit(solution)/shard_map/ppermute | solution.py:20
  28.0 1.7 %collective-permute-start.9 = (f32[8,128]{1,0:T(8,128)S(1)}, f32[8,128]{1,0:T(8,128)S(1)}, u32[]{:S(2)}, u32[]{:S(2)}) collective-permute-start(f32[8,128]{1,0:T(8,128)S(1)} %add.9), channel_id=1, source_target_pairs={{0,8},{4,12},{8,0},{12,4},{16,24},{20,28},{24,16},{28,20},{1,9},{5... | collective-permute-start | bytes 12296 | tf_op jit(solution)/shard_map/ppermute | solution.py:20
  29.7 1.9 %collective-permute-start.13 = (bf16[2,2,1,64,256]{4,3,2,1,0:T(8,128)(2,1)S(1)}, bf16[2,2,1,64,256]{4,3,2,1,0:T(8,128)(2,1)S(1)}, u32[]{:S(2)}, u32[]{:S(2)}) collective-permute-start(bf16[2,2,1,64,256]{4,3,2,1,0:T(8,128)(2,1)S(1)} %get-tuple-element.53), channel_id=1, source_target_pairs={{0,1},{1,0},{2,3},{3,2},{4,5},{5,4},{6,7},{7,6},{8,9},{9,8},{10,11... | collective-permute-start | bytes 393224 | tf_op jit(solution)/shard_map/ppermute | solution.py:20
  31.7 2.4 %collective-permute-start.10 = (bf16[1,2,2,64,256]{4,3,2,1,0:T(8,128)(2,1)S(1)}, bf16[1,2,2,64,256]{4,3,2,1,0:T(8,128)(2,1)S(1)}, u32[]{:S(2)}, u32[]{:S(2)}) collective-permute-start(bf16[1,2,2,64,256]{4,3,2,1,0:T(8,128)(2,1)S(1)} %get-tuple-element.46), channel_id=1, source_target_pairs={{0,2},{1,3},{2,0},{3,1},{4,6},{5,7},{6,4},{7,5},{8,10},{9,11},{10,... | collective-permute-start | bytes 393224 | tf_op jit(solution)/shard_map/ppermute | solution.py:20
  34.1 2.2 %collective-permute-start.12 = (bf16[1,2,1,64,256]{4,3,2,1,0:T(8,128)(2,1)S(1)}, bf16[1,2,1,64,256]{4,3,2,1,0:T(8,128)(2,1)S(1)}, u32[]{:S(2)}, u32[]{:S(2)}) collective-permute-start(bf16[1,2,1,64,256]{4,3,2,1,0:T(8,128)(2,1)S(1)} %get-tuple-element.51), channel_id=1, source_target_pairs={{0,2},{1,3},{2,0},{3,1},{4,6},{5,7},{6,4},{7,5},{8,10},{9,11},{10,... | collective-permute-start | bytes 196616 | tf_op jit(solution)/shard_map/ppermute | solution.py:20
  36.3 1.4 %collective-permute-start.14 = (f32[8,128]{1,0:T(8,128)S(1)}, f32[8,128]{1,0:T(8,128)S(1)}, u32[]{:S(2)}, u32[]{:S(2)}) collective-permute-start(f32[8,128]{1,0:T(8,128)S(1)} %add.10), channel_id=1, source_target_pairs={{0,16},{4,20},{8,24},{12,28},{16,0},{20,4},{24,8},{28,12},{1,17},{... | collective-permute-start | bytes 12296 | tf_op jit(solution)/shard_map/ppermute | solution.py:20
  37.7 1.3 %collective-permute-done.13.received = bf16[2,2,1,64,256]{4,3,2,1,0:T(8,128)(2,1)S(1)} collective-permute-done((bf16[2,2,1,64,256]{4,3,2,1,0:T(8,128)(2,1)S(1)}, bf16[2,2,1,64,256]{4,3,2,1,0:T(8,128)(2,1)S(1)}, u32[]{:S(2)}, u32[]{:S(2)}) %collective-permute-start.13) | collective-permute-done | bytes 131104 | tf_op jit(solution)/shard_map/ppermute | solution.py:20
  39.9 1.6 %collective-permute-start.16 = (f32[8,128]{1,0:T(8,128)S(1)}, f32[8,128]{1,0:T(8,128)S(1)}, u32[]{:S(2)}, u32[]{:S(2)}) collective-permute-start(f32[8,128]{1,0:T(8,128)S(1)} %add.11.tile.refs_4_), channel_id=1, source_target_pairs={{0,1},{1,0},{2,3},{3,2},{4,5},{5,4},{6,7},{7,6},{8,9},{9,8},{10,11... | collective-permute-start | bytes 12296 | tf_op jit(solution)/shard_map/ppermute | solution.py:20
  42.2 1.3 %collective-permute-start.15 = (bf16[144,256]{1,0:T(8,128)(2,1)S(1)}, bf16[144,256]{1,0:T(8,128)(2,1)S(1)}, u32[]{:S(2)}, u32[]{:S(2)}) collective-permute-start(bf16[144,256]{1,0:T(8,128)(2,1)S(1)} %get-tuple-element.57), channel_id=1, source_target_pairs={{0,2},{1,3},{2,0},{3,1},{4,6},{5,7},{6,4},{7,5},{8,10},{9,11},{10,... | collective-permute-start | bytes 221192 | tf_op jit(solution)/shard_map/ppermute | solution.py:20
  43.6 3.4 %collective-permute-done.17.refs_6_ = f32[8,128]{1,0:T(8,128)S(1)} collective-permute-done((f32[8,128]{1,0:T(8,128)S(1)}, f32[8,128]{1,0:T(8,128)S(1)}, u32[]{:S(2)}, u32[]{:S(2)}) %collective-permute-start.17) | collective-permute-done | bytes 4128 | tf_op jit(solution)/shard_map/ppermute | solution.py:20
  47.0 1.3 %collective-permute-done.15.refs_3_ = bf16[144,256]{1,0:T(8,128)(2,1)S(1)} collective-permute-done((bf16[144,256]{1,0:T(8,128)(2,1)S(1)}, bf16[144,256]{1,0:T(8,128)(2,1)S(1)}, u32[]{:S(2)}, u32[]{:S(2)}) %collective-permute-start.15) | collective-permute-done | bytes 73760 | tf_op jit(solution)/shard_map/ppermute | solution.py:20
  (30 shorter events, 5.0 us)
Async XLA Ops:
  0.6 9.4 %collective-permute-start.1 = (bf16[3,256,256]{2,1,0:T(8,128)(2,1)}, bf16[3,256,256]{2,1,0:T(8,128)(2,1)S(1)}, u32[]{:S(2)}, u32[]{:S(2)}) collective-permute-start(bf16[3,256,256]{2,1,0:T(8,128)(2,1)} %bitcast.12), channel_id=1, source_target_pairs={{0,16},{4,12},{8,24},{12,4},{16,0},{20,28},{24,8},{28,20},{1,17},{... | collective-permute-start | bytes 1179656 | tf_op jit(solution)/shard_map/ppermute | solution.py:20
  3.7 1.2 %copy-start = (bf16[2,1,4,256,256]{4,3,2,1,0:T(8,128)(2,1)S(1)}, bf16[2,1,4,256,256]{4,3,2,1,0:T(8,128)(2,1)}, u32[]{:S(2)}) copy-start(bf16[2,1,4,256,256]{4,3,2,1,0:T(8,128)(2,1)} %param.4) | copy-start | bytes 3145732
  4.9 1.0 %copy-start.1 = (bf16[3,1,256,256]{3,2,1,0:T(8,128)(2,1)S(1)}, bf16[3,1,256,256]{3,2,1,0:T(8,128)(2,1)}, u32[]{:S(2)}) copy-start(bf16[3,1,256,256]{3,2,1,0:T(8,128)(2,1)} %param.5) | copy-start | bytes 1179652
  6.9 8.1 %collective-permute-start.3 = (bf16[3,256,256]{2,1,0:T(8,128)(2,1)}, bf16[3,256,256]{2,1,0:T(8,128)(2,1)S(1)}, u32[]{:S(2)}, u32[]{:S(2)}) collective-permute-start(bf16[3,256,256]{2,1,0:T(8,128)(2,1)} %bitcast.14), channel_id=1, source_target_pairs={{0,8},{4,20},{8,0},{12,28},{16,24},{20,4},{24,16},{28,12},{1,9},{5... | collective-permute-start | bytes 1179656 | tf_op jit(solution)/shard_map/ppermute | solution.py:20
  10.0 9.3 %collective-permute-start.5 = (bf16[3,256,256]{2,1,0:T(8,128)(2,1)S(1)}, bf16[3,256,256]{2,1,0:T(8,128)(2,1)S(1)}, u32[]{:S(2)}, u32[]{:S(2)}) collective-permute-start(bf16[3,256,256]{2,1,0:T(8,128)(2,1)S(1)} %collective-permute-done.1.rest_2_), channel_id=1, source_target_pairs={{0,8},{4,20},{8,0},{12,28},{16,24},{20,4},{24,16},{28,12},{1,9},{5... | collective-permute-start | bytes 1179656 | tf_op jit(solution)/shard_map/ppermute | solution.py:20
  13.5 5.8 %collective-permute-start = (bf16[3,256,256]{2,1,0:T(8,128)(2,1)}, bf16[3,256,256]{2,1,0:T(8,128)(2,1)S(1)}, u32[]{:S(2)}, u32[]{:S(2)}) collective-permute-start(bf16[3,256,256]{2,1,0:T(8,128)(2,1)} %bitcast.15), channel_id=1, source_target_pairs={{0,4},{4,0},{8,12},{12,8},{16,20},{20,16},{24,28},{28,24},{1,5},{5... | collective-permute-start | bytes 1179656 | tf_op jit(solution)/shard_map/ppermute | solution.py:20
  15.0 4.3 %collective-permute-start.4 = (bf16[3,256,256]{2,1,0:T(8,128)(2,1)S(1)}, bf16[3,256,256]{2,1,0:T(8,128)(2,1)S(1)}, u32[]{:S(2)}, u32[]{:S(2)}) collective-permute-start(bf16[3,256,256]{2,1,0:T(8,128)(2,1)S(1)} %collective-permute-done.3.rest_4_), channel_id=1, source_target_pairs={{0,4},{4,0},{8,12},{12,8},{16,20},{20,16},{24,28},{28,24},{1,5},{5... | collective-permute-start | bytes 1179656 | tf_op jit(solution)/shard_map/ppermute | solution.py:20
  15.0 4.3 %collective-permute-start.2 = (bf16[3,256,256]{2,1,0:T(8,128)(2,1)S(1)}, bf16[3,256,256]{2,1,0:T(8,128)(2,1)S(1)}, u32[]{:S(2)}, u32[]{:S(2)}) collective-permute-start(bf16[3,256,256]{2,1,0:T(8,128)(2,1)S(1)} %collective-permute-done.1.rest_2_), channel_id=1, source_target_pairs={{0,4},{4,0},{8,12},{12,8},{16,20},{20,16},{24,28},{28,24},{1,5},{5... | collective-permute-start | bytes 1179656 | tf_op jit(solution)/shard_map/ppermute | solution.py:20
  19.3 1.7 %collective-permute-start.6 = (bf16[3,256,256]{2,1,0:T(8,128)(2,1)S(1)}, bf16[3,256,256]{2,1,0:T(8,128)(2,1)S(1)}, u32[]{:S(2)}, u32[]{:S(2)}) collective-permute-start(bf16[3,256,256]{2,1,0:T(8,128)(2,1)S(1)} %collective-permute-done.5.rest_6_), channel_id=1, source_target_pairs={{0,4},{4,0},{8,12},{12,8},{16,20},{20,16},{24,28},{28,24},{1,5},{5... | collective-permute-start | bytes 1179656 | tf_op jit(solution)/shard_map/ppermute | solution.py:20
  21.8 9.8 %collective-permute-start.7 = (bf16[2,2,2,64,256]{4,3,2,1,0:T(8,128)(2,1)S(1)}, bf16[2,2,2,64,256]{4,3,2,1,0:T(8,128)(2,1)S(1)}, u32[]{:S(2)}, u32[]{:S(2)}) collective-permute-start(bf16[2,2,2,64,256]{4,3,2,1,0:T(8,128)(2,1)S(1)} %get-tuple-element.39), channel_id=1, source_target_pairs={{0,1},{1,0},{2,3},{3,2},{4,5},{5,4},{6,7},{7,6},{8,9},{9,8},{10,11... | collective-permute-start | bytes 786440 | tf_op jit(solution)/shard_map/ppermute | solution.py:20
  24.6 9.4 %collective-permute-start.11 = (bf16[2,2,1,64,256]{4,3,2,1,0:T(8,128)(2,1)S(1)}, bf16[2,2,1,64,256]{4,3,2,1,0:T(8,128)(2,1)S(1)}, u32[]{:S(2)}, u32[]{:S(2)}) collective-permute-start(bf16[2,2,1,64,256]{4,3,2,1,0:T(8,128)(2,1)S(1)} %get-tuple-element.48), channel_id=1, source_target_pairs={{0,1},{1,0},{2,3},{3,2},{4,5},{5,4},{6,7},{7,6},{8,9},{9,8},{10,11... | collective-permute-start | bytes 393224 | tf_op jit(solution)/shard_map/ppermute | solution.py:20
  26.8 1.2 %collective-permute-start.8 = (f32[8,128]{1,0:T(8,128)S(1)}, f32[8,128]{1,0:T(8,128)S(1)}, u32[]{:S(2)}, u32[]{:S(2)}) collective-permute-start(f32[8,128]{1,0:T(8,128)S(1)} %get-tuple-element.43), channel_id=1, source_target_pairs={{0,4},{4,0},{8,12},{12,8},{16,20},{20,16},{24,28},{28,24},{1,5},{5... | collective-permute-start | bytes 12296 | tf_op jit(solution)/shard_map/ppermute | solution.py:20
  28.0 3.6 %collective-permute-start.9 = (f32[8,128]{1,0:T(8,128)S(1)}, f32[8,128]{1,0:T(8,128)S(1)}, u32[]{:S(2)}, u32[]{:S(2)}) collective-permute-start(f32[8,128]{1,0:T(8,128)S(1)} %add.9), channel_id=1, source_target_pairs={{0,8},{4,12},{8,0},{12,4},{16,24},{20,28},{24,16},{28,20},{1,9},{5... | collective-permute-start | bytes 12296 | tf_op jit(solution)/shard_map/ppermute | solution.py:20
  29.7 9.4 %collective-permute-start.13 = (bf16[2,2,1,64,256]{4,3,2,1,0:T(8,128)(2,1)S(1)}, bf16[2,2,1,64,256]{4,3,2,1,0:T(8,128)(2,1)S(1)}, u32[]{:S(2)}, u32[]{:S(2)}) collective-permute-start(bf16[2,2,1,64,256]{4,3,2,1,0:T(8,128)(2,1)S(1)} %get-tuple-element.53), channel_id=1, source_target_pairs={{0,1},{1,0},{2,3},{3,2},{4,5},{5,4},{6,7},{7,6},{8,9},{9,8},{10,11... | collective-permute-start | bytes 393224 | tf_op jit(solution)/shard_map/ppermute | solution.py:20
  31.7 11.9 %collective-permute-start.10 = (bf16[1,2,2,64,256]{4,3,2,1,0:T(8,128)(2,1)S(1)}, bf16[1,2,2,64,256]{4,3,2,1,0:T(8,128)(2,1)S(1)}, u32[]{:S(2)}, u32[]{:S(2)}) collective-permute-start(bf16[1,2,2,64,256]{4,3,2,1,0:T(8,128)(2,1)S(1)} %get-tuple-element.46), channel_id=1, source_target_pairs={{0,2},{1,3},{2,0},{3,1},{4,6},{5,7},{6,4},{7,5},{8,10},{9,11},{10,... | collective-permute-start | bytes 393224 | tf_op jit(solution)/shard_map/ppermute | solution.py:20
  34.1 9.4 %collective-permute-start.12 = (bf16[1,2,1,64,256]{4,3,2,1,0:T(8,128)(2,1)S(1)}, bf16[1,2,1,64,256]{4,3,2,1,0:T(8,128)(2,1)S(1)}, u32[]{:S(2)}, u32[]{:S(2)}) collective-permute-start(bf16[1,2,1,64,256]{4,3,2,1,0:T(8,128)(2,1)S(1)} %get-tuple-element.51), channel_id=1, source_target_pairs={{0,2},{1,3},{2,0},{3,1},{4,6},{5,7},{6,4},{7,5},{8,10},{9,11},{10,... | collective-permute-start | bytes 196616 | tf_op jit(solution)/shard_map/ppermute | solution.py:20
  36.3 3.6 %collective-permute-start.14 = (f32[8,128]{1,0:T(8,128)S(1)}, f32[8,128]{1,0:T(8,128)S(1)}, u32[]{:S(2)}, u32[]{:S(2)}) collective-permute-start(f32[8,128]{1,0:T(8,128)S(1)} %add.10), channel_id=1, source_target_pairs={{0,16},{4,20},{8,24},{12,28},{16,0},{20,4},{24,8},{28,12},{1,17},{... | collective-permute-start | bytes 12296 | tf_op jit(solution)/shard_map/ppermute | solution.py:20
  39.9 3.7 %collective-permute-start.16 = (f32[8,128]{1,0:T(8,128)S(1)}, f32[8,128]{1,0:T(8,128)S(1)}, u32[]{:S(2)}, u32[]{:S(2)}) collective-permute-start(f32[8,128]{1,0:T(8,128)S(1)} %add.11.tile.refs_4_), channel_id=1, source_target_pairs={{0,1},{1,0},{2,3},{3,2},{4,5},{5,4},{6,7},{7,6},{8,9},{9,8},{10,11... | collective-permute-start | bytes 12296 | tf_op jit(solution)/shard_map/ppermute | solution.py:20
  41.5 5.5 %collective-permute-start.17 = (f32[8,128]{1,0:T(8,128)S(1)}, f32[8,128]{1,0:T(8,128)S(1)}, u32[]{:S(2)}, u32[]{:S(2)}) collective-permute-start(f32[8,128]{1,0:T(8,128)S(1)} %add.11.tile.refs_4_), channel_id=1, source_target_pairs={{0,3},{1,2},{2,1},{3,0},{4,7},{5,6},{6,5},{7,4},{8,11},{9,10},{10,... | collective-permute-start | bytes 12296 | tf_op jit(solution)/shard_map/ppermute | solution.py:20
  42.2 6.2 %collective-permute-start.15 = (bf16[144,256]{1,0:T(8,128)(2,1)S(1)}, bf16[144,256]{1,0:T(8,128)(2,1)S(1)}, u32[]{:S(2)}, u32[]{:S(2)}) collective-permute-start(bf16[144,256]{1,0:T(8,128)(2,1)S(1)} %get-tuple-element.57), channel_id=1, source_target_pairs={{0,2},{1,3},{2,0},{3,1},{4,6},{5,7},{6,4},{7,5},{8,10},{9,11},{10,... | collective-permute-start | bytes 221192 | tf_op jit(solution)/shard_map/ppermute | solution.py:20
